TPU v7x, 32 devices: a whole 2x2x4 slice. The times are simulated.
32 devices in a mesh: seq: 8 (over z, y), head: 4 (over x, core).
Axes of the slice: x: 2, y: 2, z: 4, core: 2. Of those that a mesh axis runs over, the one named last changes fastest.
Arguments:
- queries_first: bfloat16 [4096, 1024], P('seq', 'head'), may hold values from -4.4 to 4.4
- keys_first: bfloat16 [4096, 1024], P('seq', 'head'), may hold values from -4.4 to 4.4
- values_first: bfloat16 [4096, 1024], P('seq', 'head'), may hold values from -6 to 6
- input_map: bfloat16 [4, 256, 512], P('head'), may hold values from -0.375 to 0.375
- fast_keys: bfloat16 [4096, 2048], P('seq', 'head'), may hold values from -6 to 6
- fast_values: bfloat16 [4096, 2048], P('seq', 'head'), may hold values from -6 to 6
- step_rates: float32 [4096, 4], P('seq', 'head'), may hold values from 0.1 to 1
- fast_weights: bfloat16 [4, 512, 3, 512], P('head'), may hold values from -6 to 6
- output_map: bfloat16 [2048, 1024], P('head'), may hold values from -0.25 to 0.25
- queries_second: bfloat16 [4096, 1024], P('seq', 'head'), may hold values from -4.4 to 4.4
- keys_second: bfloat16 [4096, 1024], P('seq', 'head'), may hold values from -4.4 to 4.4
- values_second: bfloat16 [4096, 1024], P('seq', 'head'), may hold values from -6 to 6
Outputs:
- block_output: bfloat16 [4096, 1024], P('seq', 'head')
- new_weights: bfloat16 [4, 512, 3, 512], P('head', 'seq')
All inputs are finite; a program needn't handle non-finite values.
Results may differ from a plain program's by a relative error of at most 0.034.
Values may be sent and summed in bfloat16 or wider, within the bound.
No kernel may reach another device: no remote copies, remote signals or barrier semaphores. Data moves between devices by JAX's collectives and lax.ppermute only.
A program may use at most 64 MiB of HBM per device.

v0:
```python
import math

import jax
import jax.numpy as jnp
from jax import lax
from jax.sharding import PartitionSpec as P

HALF_WIN = 512
HEAD_DIM = 128
HEADS_GRP = 2
FAST_DIM = 512
FAST_HIDDEN = 512


def padded(value, sides, width):
    for axis, dim in sides:
        peers, length = (lax.axis_size(axis), value.shape[dim])
        up = [(i, (i + 1) % peers) for i in range(peers - 1)]
        down = [(j, i) for i, j in up]
        last = lax.slice_in_dim(value, length - width, length, axis=dim)
        first = lax.slice_in_dim(value, 0, width, axis=dim)
        before = lax.ppermute(last, axis, up)
        after = lax.ppermute(first, axis, down)
        value = jnp.concatenate([before, value, after], axis=dim)
    return value


def rms_round(matrix):
    return (matrix * lax.rsqrt(jnp.mean(matrix * matrix, axis=-1, keepdims=True) + 1e-05)).astype(
        jnp.bfloat16
    )


def window_attend(queries, keys_ext, values_ext, anchor, token_total):
    local_rows = queries.shape[0]
    reach = (keys_ext.shape[0] - local_rows) // 2
    block_rows = min(512, local_rows)
    span_rows = block_rows + 2 * reach
    inverse_root = 1.0 / math.sqrt(HEAD_DIM)

    def attend_block(block_index):
        start_row = block_index * block_rows
        query_block = queries.reshape(block_rows, HEADS_GRP, HEAD_DIM)
        key_block = keys_ext.reshape(span_rows, HEADS_GRP, HEAD_DIM)
        value_block = values_ext.reshape(span_rows, HEADS_GRP, HEAD_DIM)
        scores = (
            jnp.einsum("qhd,khd->hqk", query_block, key_block, preferred_element_type=jnp.float32)
            * inverse_root
        )
        query_pos = jnp.arange(block_rows, dtype=jnp.int32)[:, None]
        key_pos = jnp.arange(span_rows, dtype=jnp.int32)[None, :]
        global_pos = anchor + start_row + key_pos - reach
        allowed = (
            (key_pos >= query_pos)
            & (key_pos <= query_pos + 2 * reach)
            & (global_pos >= 0)
            & (global_pos < token_total)
        )
        scores = jnp.where(allowed[None], scores, -jnp.inf)
        highest = jnp.max(scores, axis=-1, keepdims=True)
        weights_exp = jnp.exp(scores - highest)
        weights_bf = (weights_exp / jnp.sum(weights_exp, axis=-1, keepdims=True)).astype(
            jnp.bfloat16
        )
        attended = jnp.einsum(
            "hqk,khd->qhd", weights_bf, value_block, preferred_element_type=jnp.float32
        )
        return rms_round(attended.reshape(block_rows, HEADS_GRP * HEAD_DIM))

    outputs = lax.map(attend_block, jnp.arange(local_rows // block_rows, dtype=jnp.int32))
    return outputs.reshape(local_rows, HEADS_GRP * HEAD_DIM)


def swiglu_apply(fast_query, weights_rows):
    inverse = 1.0 / math.sqrt(FAST_DIM)
    gate_part = (
        jnp.einsum(
            "td,ud->tu", fast_query, weights_rows[:, 0, :], preferred_element_type=jnp.float32
        )
        * inverse
    )
    up_part = (
        jnp.einsum(
            "td,ud->tu", fast_query, weights_rows[:, 1, :], preferred_element_type=jnp.float32
        )
        * inverse
    )
    hidden_query = (jax.nn.silu(gate_part) * up_part).astype(jnp.bfloat16)
    return jnp.einsum(
        "tu,ud->td", hidden_query, weights_rows[:, 2, :], preferred_element_type=jnp.float32
    )


def renormalize(old_rows, gradient_rows, factor):
    old_float = old_rows.astype(jnp.float32)
    stepped = old_float + factor * gradient_rows
    old_norm = jnp.sqrt(jnp.sum(old_float * old_float, axis=-1, keepdims=True))
    return (
        stepped * old_norm * lax.rsqrt(jnp.sum(stepped * stepped, axis=-1, keepdims=True) + 1e-06)
    ).astype(jnp.bfloat16)


def local(
    queries_first,
    keys_first,
    values_first,
    input_map,
    fast_keys,
    fast_values,
    step_rates,
    fast_weights,
    output_map,
    queries_second,
    keys_second,
    values_second,
):
    local_rows = queries_first.shape[0]
    seq_count = lax.axis_size("seq")
    seq_place = lax.axis_index("seq")
    anchor = seq_place * local_rows
    token_total = local_rows * seq_count
    stacked = jnp.stack([keys_first, values_first, keys_second, values_second])
    extended = padded(stacked, (("seq", 1),), HALF_WIN)
    normed_first = window_attend(queries_first, extended[0], extended[1], anchor, token_total)
    fast_query = jnp.dot(normed_first, input_map[0], preferred_element_type=jnp.float32).astype(
        jnp.bfloat16
    )
    weights_local = fast_weights[0]
    hidden_size = weights_local.shape[0]
    inverse = 1.0 / math.sqrt(FAST_DIM)
    gate_keys = (
        jnp.einsum(
            "td,ud->tu", fast_keys, weights_local[:, 0, :], preferred_element_type=jnp.float32
        )
        * inverse
    )
    up_keys = (
        jnp.einsum(
            "td,ud->tu", fast_keys, weights_local[:, 1, :], preferred_element_type=jnp.float32
        )
        * inverse
    )
    sigmoid_gate = jax.nn.sigmoid(gate_keys)
    silu_gate = gate_keys * sigmoid_gate
    hidden_keys = (step_rates * silu_gate * up_keys).astype(jnp.bfloat16)
    backward = step_rates * jnp.einsum(
        "td,ud->tu", fast_values, weights_local[:, 2, :], preferred_element_type=jnp.float32
    )
    d_gate = (
        backward * up_keys * sigmoid_gate * (1.0 + gate_keys * (1.0 - sigmoid_gate)) * inverse
    ).astype(jnp.bfloat16)
    d_up = (backward * silu_gate * inverse).astype(jnp.bfloat16)

    def gradient_rows(start_row, row_count):
        return jnp.stack(
            [
                jnp.einsum("tu,td->ud", d_gate, fast_keys, preferred_element_type=jnp.float32),
                jnp.einsum("tu,td->ud", d_up, fast_keys, preferred_element_type=jnp.float32),
                jnp.einsum(
                    "tu,td->ud", hidden_keys, fast_values, preferred_element_type=jnp.float32
                ),
            ],
            axis=1,
        )

    limit_norm = math.sqrt(FAST_HIDDEN * FAST_DIM) / 2.0
    share_rows = hidden_size // seq_count
    gradient = lax.psum(gradient_rows(0, hidden_size), "seq")
    factor = jnp.minimum(1.0, limit_norm * lax.rsqrt(jnp.sum(gradient * gradient) + 1e-06))
    updated = renormalize(weights_local, gradient, factor)
    own_new = lax.dynamic_slice_in_dim(updated, seq_place * share_rows, share_rows, 0)
    fast_raw = swiglu_apply(fast_query, updated)
    fast_out = rms_round(fast_raw)
    group_count = lax.axis_size("head")
    group_width = queries_second.shape[1]
    output_split = output_map.reshape(FAST_DIM, group_count, group_width)
    mixed = lax.psum_scatter(
        jnp.einsum(
            "td,dgc->gtc", fast_out, output_split, preferred_element_type=jnp.float32
        ).astype(jnp.bfloat16),
        "head",
        scatter_dimension=0,
        tiled=True,
    ).astype(jnp.float32)[0]
    query_two = (queries_second.astype(jnp.float32) + mixed).astype(jnp.bfloat16)
    normed_second = window_attend(query_two, extended[2], extended[3], anchor, token_total)
    return (normed_second, own_new[None])


def solution(mesh):
    return jax.shard_map(
        local,
        mesh=mesh,
        in_specs=(
            P("seq", "head"),
            P("seq", "head"),
            P("seq", "head"),
            P("head", None, None),
            P("seq", "head"),
            P("seq", "head"),
            P("seq", "head"),
            P("head", None, None, None),
            P("head", None),
            P("seq", "head"),
            P("seq", "head"),
            P("seq", "head"),
        ),
        out_specs=(P("seq", "head"), P("head", "seq", None, None)),
        check_vma=False,
    )
```

profile of v0, /device:TPU:0, one launch (start us, length us, event | category | flops | bytes accessed | tf_op | source)
XLA Modules:
  0.0 227.6 jit_solution(874992664136219652)
XLA Ops:
  7.2 0.0 copy-start
  7.2 0.0 copy-start.2
  7.2 0.0 all-reduce.2.cloned.1.call-start
  7.2 1.2 copy.24
  8.5 1.1 copy.25
  9.6 1.1 copy.26
  10.7 1.1 copy.27
  11.8 0.0 copy-start.6
  11.8 0.0 copy-start.7
  11.8 1.1 pad_maximum_fusion.2
  12.9 1.3 collective-permute-start.1
  14.2 6.6 %collective-permute-start = (bf16[4,512,256]{1,2,0:T(8,128)(2,1)}, bf16[4,512,256]{1,2,0:T(8,128)(2,1)}, u32[]{:S(2)}, u32[]{:S(2)}) collective-permute-start(bf16[4,512,256]{1,2,0:T(8,128)(2,1)} %pad_maximum_fusion.2), channel_id=1, source_target_pairs={{0,4},{4,8},{8,12},{12,16},{16,20},{20,24},{24,28},{1,5},{5,9},{9,... | collective-permute-start | bytes 3145736 | tf_op jit(solution)/shard_map/ppermute | solution.py:22
  20.8 0.0 copy-done
  20.8 0.5 convolution_multiply_fusion.2
  21.3 0.5 convolution_multiply_fusion.3
  21.7 0.0 copy-done.6
  21.8 0.0 copy-done.7
  21.8 0.5 convolution_multiply_fusion.4
  22.3 0.7 convolution_bitcast_fusion
  23.0 0.8 convolution_bitcast_fusion.2
  23.8 0.5 convolution_bitcast_fusion.1
  24.3 2.0 pad_maximum_fusion.1
  26.3 0.0 all-reduce.2.cloned.1.call-update
  26.3 0.2 reduce-scatter.2.cloned.1.call-start
  26.6 2.0 fusion.11
  28.6 19.9 %collective-permute-done.1 = bf16[4,512,256]{1,2,0:T(8,128)(2,1)} collective-permute-done((bf16[4,512,256]{1,2,0:T(8,128)(2,1)}, bf16[4,512,256]{1,2,0:T(8,128)(2,1)}, u32[]{:S(2)}, u32[]{:S(2)}) %collective-permute-start.1) | collective-permute-done | bytes 1048608 | tf_op jit(solution)/shard_map/ppermute | solution.py:23
  48.5 26.6 %collective-permute-done = bf16[4,512,256]{1,2,0:T(8,128)(2,1)} collective-permute-done((bf16[4,512,256]{1,2,0:T(8,128)(2,1)}, bf16[4,512,256]{1,2,0:T(8,128)(2,1)}, u32[]{:S(2)}, u32[]{:S(2)}) %collective-permute-start) | collective-permute-done | bytes 1048608 | tf_op jit(solution)/shard_map/ppermute | solution.py:22
  75.1 1.7 pad_maximum_fusion
  76.8 0.0 copy-start.8
  76.8 1.4 fusion.92
  78.2 3.8 %fusion.93 = f32[2,512]{1,0:T(2,128)S(1)} fusion(pred[512,1536]{0,1:T(8,128)(4,1)} %fusion.11, bf16[1536,2,128]{0,2,1:T(8,128)(2,1)} %bitcast.169, bf16[512,256]{1,0:T(8,128)(2,1)S(1)} %copy-done.8), kind=kOutput, calls=%fused_computation.118 | convolution fusion | flops 408946176 | bytes 1839104 | tf_op jit(solution)/shard_map/while/body/eval_jaxpr/sub | solution.py:61
  82.1 4.9 %multiply_reduce_fusion.3 = (f32[512]{0:T(512)S(1)}, f32[2,128,512]{2,1,0:T(8,128)S(1)}) fusion(bf16[1536,2,128]{0,2,1:T(8,128)(2,1)} %bitcast.171, f32[2,512]{1,0:T(2,128)S(1)} %fusion.93, pred[512,1536]{0,1:T(8,128)(4,1)} %fusion.11, bf16[1536,2,128]{0,2,1:T(8,128)(2,1)} %bitcast.170, bf16[512,256]{1,0:T(8,128)(2,1)} %param.12), kind=kOutput, calls=%fused_computation.80 | convolution fusion | flops 813434880 | bytes 3151872 | tf_op jit(solution)/shard_map/while/body/eval_jaxpr/hqk,khd->qhd/dot_general | solution.py:65
  87.0 1.3 convolution_convert_fusion.1
  88.3 83.6 %all-reduce.2.cloned.1.call-done = f32[512,3,512]{2,0,1:T(8,128)} async-done(((f32[512,3,512]{2,0,1:T(8,128)}), f32[512,3,512]{2,0,1:T(8,128)}) %all-reduce.2.cloned.1.call-update) | async-done | bytes 3145744 | tf_op jit(solution)/shard_map/psum | solution.py:168
  172.0 3.3 %multiply_reduce_fusion.1 = f32[]{:T(128)} fusion(f32[512,3,512]{2,0,1:T(8,128)} %all-reduce.2.cloned.1.call-done), kind=kLoop, calls=%fused_computation.18 | loop fusion | flops 1572863 | bytes 3145732 | tf_op jit(solution)/shard_map/reduce_sum | solution.py:169
  176.0 2.8 %fusion.4 = (f32[512,3]{0,1:T(4,128)S(1)}, f32[512,3]{0,1:T(4,128)S(1)}) fusion(bf16[1,512,3,512]{3,1,2,0:T(8,128)(2,1)S(1)} %copy-done.2, f32[512,3,512]{2,0,1:T(8,128)} %all-reduce.2.cloned.1.call-done, f32[]{:T(128)S(6)} %min.3), kind=kLoop, calls=%fused_computation.12 | loop fusion | flops 5501952 | bytes 4730884 | tf_op jit(solution)/shard_map/reduce_sum | solution.py:97
  178.9 1.0 multiply_convert_fusion
  179.8 1.1 copy-done.3
  181.0 0.5 convolution_multiply_fusion.1
  181.4 3.2 %multiply_reduce_fusion.2 = (f32[512]{0:T(512)S(1)}, f32[512,512]{0,1:T(8,128)}) fusion(bf16[512,3,512]{2,0,1:T(8,128)(2,1)} %copy-done.3, bf16[512,512]{1,0:T(8,128)(2,1)S(1)} %convolution_convert_fusion.1, f32[512,512]{1,0:T(8,128)S(1)} %convolution_multiply_fusion.1), kind=kOutput, calls=%fused_computation.49 | convolution fusion | flops 539229696 | bytes 3672064 | tf_op jit(solution)/shard_map/tu,ud->td/dot_general | solution.py:89
  184.6 3.3 %fusion.17 = bf16[4,512,256]{2,1,0:T(8,128)(2,1)} fusion(bf16[64,4,8,256]{3,2,1,0:T(8,128)(2,1)} %bitcast.175, f32[512,512]{0,1:T(8,128)} %get-tuple-element.41, f32[512]{0:T(512)S(1)} %add_rsqrt_fusion.2), kind=kOutput, calls=%fused_computation.41 | convolution fusion | flops 537919488 | bytes 3147776 | tf_op jit(solution)/shard_map/td,dgc->gtc/dot_general | solution.py:178
  188.0 0.0 reduce-scatter.2.cloned.1.call-update
  188.0 1.6 dynamic-slice_bitcast_fusion
  189.6 22.3 %reduce-scatter.2.cloned.1.call-done = bf16[1,512,256]{2,1,0:T(8,128)(2,1)} async-done(((bf16[4,512,256]{2,1,0:T(8,128)(2,1)}), bf16[1,512,256]{2,1,0:T(8,128)(2,1)}) %reduce-scatter.2.cloned.1.call-update) | async-done | bytes 262160 | tf_op jit(solution)/shard_map/reduce_scatter | solution.py:177
  212.0 3.6 %fusion.98 = f32[2,512]{1,0:T(2,128)S(1)} fusion(pred[512,1536]{0,1:T(8,128)(4,1)S(1)} %copy-done.5, bf16[1536,2,128]{0,2,1:T(8,128)(2,1)S(1)} %bitcast.166, bf16[512,256]{1,0:T(8,128)(2,1)S(1)} %copy-done.9, bf16[1,512,256]{2,1,0:T(8,128)(2,1)} %reduce-scatter.2.cloned.1.call-done), kind=kOutput, calls=%fused_computation.119 | convolution fusion | flops 409470464 | bytes 2101248 | tf_op jit(solution)/shard_map/while/body/eval_jaxpr/sub | solution.py:61
  215.5 4.2 %fusion.35 = (f32[512]{0:T(512)S(1)}, f32[2,128,512]{2,1,0:T(8,128)S(1)}) fusion(bf16[1536,2,128]{0,2,1:T(8,128)(2,1)S(1)} %bitcast.168, f32[2,512]{1,0:T(2,128)S(1)} %fusion.98, pred[512,1536]{0,1:T(8,128)(4,1)S(1)} %copy-done.5, bf16[1536,2,128]{0,2,1:T(8,128)(2,1)S(1)} %bitcast.167, bf16[512,256]{1,0:T(8,128)(2,1)} %param.21, ...), kind=kOutput, calls=%fused_computation.72 | convolution fusion | flops 813959168 | bytes 3414016 | tf_op jit(solution)/shard_map/while/body/eval_jaxpr/hqk,khd->qhd/dot_general | solution.py:65
  219.7 0.2 copy.37
  219.9 0.8 multiply_convert_fusion.7
  (19 shorter events, 0.1 us)
Async XLA Ops:
  7.2 13.6 %copy-start = (bf16[512,512]{1,0:T(8,128)(2,1)S(1)}, bf16[512,512]{1,0:T(8,128)(2,1)}, u32[]{:S(2)}) copy-start(bf16[512,512]{1,0:T(8,128)(2,1)} %param.16) | copy-start | bytes 1572868
  7.2 13.6 %copy-start.2 = (bf16[1,512,3,512]{3,1,2,0:T(8,128)(2,1)S(1)}, bf16[1,512,3,512]{3,1,2,0:T(8,128)(2,1)}, u32[]{:S(2)}) copy-start(bf16[1,512,3,512]{3,1,2,0:T(8,128)(2,1)} %param.19) | copy-start | bytes 4718596
  7.2 164.8 %all-reduce.2.cloned.1.call-start = ((), (), s32[]{:S(2)}) async-start(), calls=%async_computation.1 | async-start | bytes 6291456 | tf_op jit(solution)/shard_map/psum | solution.py:168
  11.8 10.0 %copy-start.6 = (bf16[512,512]{1,0:T(8,128)(2,1)S(1)}, bf16[512,512]{1,0:T(8,128)(2,1)}, u32[]{:S(2)}) copy-start(bf16[512,512]{1,0:T(8,128)(2,1)} %param.17) | copy-start | bytes 1572868
  11.8 10.0 %copy-start.7 = (f32[512,1]{0,1:T(1,128)S(1)}, f32[512,1]{0,1:T(1,128)}, u32[]{:S(2)}) copy-start(f32[512,1]{0,1:T(1,128)} %param.18) | copy-start | bytes 6148
  12.9 35.6 %collective-permute-start.1 = (bf16[4,512,256]{1,2,0:T(8,128)(2,1)}, bf16[4,512,256]{1,2,0:T(8,128)(2,1)}, u32[]{:S(2)}, u32[]{:S(2)}) collective-permute-start(bf16[4,512,256]{1,2,0:T(8,128)(2,1)} %pad_maximum_fusion.2), channel_id=1, source_target_pairs={{4,0},{8,4},{12,8},{16,12},{20,16},{24,20},{28,24},{5,1},{9,5},{13... | collective-permute-start | bytes 3145736 | tf_op jit(solution)/shard_map/ppermute | solution.py:23
  14.2 60.9 %collective-permute-start = (bf16[4,512,256]{1,2,0:T(8,128)(2,1)}, bf16[4,512,256]{1,2,0:T(8,128)(2,1)}, u32[]{:S(2)}, u32[]{:S(2)}) collective-permute-start(bf16[4,512,256]{1,2,0:T(8,128)(2,1)} %pad_maximum_fusion.2), channel_id=1, source_target_pairs={{0,4},{4,8},{8,12},{12,16},{16,20},{20,24},{24,28},{1,5},{5,9},{9,... | collective-permute-start | bytes 3145736 | tf_op jit(solution)/shard_map/ppermute | solution.py:22
  26.3 185.6 %reduce-scatter.2.cloned.1.call-start = ((), (), s32[]{:S(2)}) async-start(), calls=%async_computation.2 | async-start | bytes 1310720 | tf_op jit(solution)/shard_map/reduce_scatter | solution.py:177
  76.8 1.5 copy-start.8
  176.0 2.9 %copy-start.1 = (f32[512,3,512]{2,0,1:T(8,128)S(1)}, f32[512,3,512]{2,0,1:T(8,128)}, u32[]{:S(2)}) copy-start(f32[512,3,512]{2,0,1:T(8,128)} %all-reduce.2.cloned.1.call-done) | copy-start | bytes 9437188
  179.8 1.2 copy-start.3
  184.6 27.3 %copy-start.5 = (pred[512,1536]{0,1:T(8,128)(4,1)S(1)}, pred[512,1536]{0,1:T(8,128)(4,1)}, u32[]{:S(2)}) copy-start(pred[512,1536]{0,1:T(8,128)(4,1)} %fusion.11) | copy-start | bytes 2359300
  184.6 27.3 %copy-start.9 = (bf16[512,256]{1,0:T(8,128)(2,1)S(1)}, bf16[512,256]{1,0:T(8,128)(2,1)}, u32[]{:S(2)}) copy-start(bf16[512,256]{1,0:T(8,128)(2,1)} %param.21) | copy-start | bytes 786436
  212.0 3.6 %copy-start.4 = (bf16[1,1536,256]{1,2,0:T(8,128)(2,1)S(1)}, bf16[1,1536,256]{1,2,0:T(8,128)(2,1)}, u32[]{:S(2)}) copy-start(bf16[1,1536,256]{1,2,0:T(8,128)(2,1)} %get-tuple-element.37) | copy-start | bytes 2359300
Sparse Core Ops, SparseCore 0:
  26.5 145.4 all-reduce.1
  188.1 23.8 reduce-scatter.1
where the time goes:
time: 228 us
  waiting for transfers between devices  152 us (67%)
  matrix products  28.2 us (12%)
  between operations  15 us (7%)
  other arithmetic  14.9 us (7%)
  local copies, waits for them, and re-layouts  8.96 us (4%)
  starting transfers between devices  8.12 us (4%)
    psum x1, waiting for transfers between devices, local(): gradient = lax.psum(gradient_rows(0, hidden_size), 'seq')  83.6 us
    ppermute x1, waiting for transfers between devices, padded(): before = lax.ppermute(last, axis, up)  26.6 us
    reduce_scatter x1, waiting for transfers between devices, local(): lax.psum_scatter(jnp.einsum('td,dgc->gtc', fast_out, output_split, prefer...  22.3 us
    ppermute x1, waiting for transfers between devices, padded(): after = lax.ppermute(first, axis, down)  19.9 us
    dot_general x2, matrix products, attend_block(): jnp.einsum('hqk,khd->qhd', weights_bf, value_block, preferred_element_typ...  9.09 us
    sub x2, matrix products, attend_block(): weights_exp = jnp.exp(scores - highest)  7.38 us
    ppermute x1, starting transfers between devices, padded(): before = lax.ppermute(last, axis, up)  6.58 us
    unnamed x24, local copies, waits for them, and re-layouts  5.7 us
  transfers between devices with their start and end apart: 4, of which 4 were waited for; matrix products, arithmetic and copies ran while one was open for 10% of the time, Pallas kernels for 0%

commit v1 on v0

v1 whole, which is shorter than its diff:
```python
import functools
import math

import jax
import jax.numpy as jnp
from jax import lax
from jax.experimental import pallas as pl
from jax.experimental.pallas import tpu as pltpu
from jax.sharding import PartitionSpec as P

HALF_WIN = 512
HEAD_DIM = 128
HEADS_GRP = 2
FAST_DIM = 512
FAST_HIDDEN = 512
TILE = 128
VMEM_LIMIT = 48 * 1024 * 1024

BF16 = jnp.bfloat16
F32 = jnp.float32
INVERSE = 1.0 / math.sqrt(FAST_DIM)


def dot_nn(left, right):
    return lax.dot_general(left, right, (((1,), (0,)), ((), ())), preferred_element_type=F32)


def dot_nt(left, right):
    return lax.dot_general(left, right, (((1,), (1,)), ((), ())), preferred_element_type=F32)


def call(body, out_shapes, operands, flops, moved, scalars=0, scratch=()):
    in_specs = [pl.BlockSpec(memory_space=pltpu.SMEM)] * scalars + [
        pl.BlockSpec(memory_space=pltpu.VMEM)
    ] * (len(operands) - scalars)
    return pl.pallas_call(
        body,
        out_shape=out_shapes,
        in_specs=in_specs,
        out_specs=jax.tree.map(lambda _: pl.BlockSpec(memory_space=pltpu.VMEM), out_shapes),
        scratch_shapes=scratch,
        compiler_params=pltpu.CompilerParams(vmem_limit_bytes=VMEM_LIMIT),
        cost_estimate=pl.CostEstimate(flops=flops, bytes_accessed=moved, transcendentals=0),
    )(*operands)


def gradient_kernel(rates_ref, keys_ref, values_ref, weights_ref, out_ref):
    rates = rates_ref[...]
    keys = keys_ref[...]
    values = values_ref[...]
    step = 128
    for low in range(0, weights_ref.shape[1], step):
        rows = slice(low, low + step)
        gate = dot_nt(weights_ref[0, rows, :], keys) * INVERSE
        up = dot_nt(weights_ref[1, rows, :], keys) * INVERSE
        sigmoid = jax.nn.sigmoid(gate)
        silu = gate * sigmoid
        hidden = (rates * silu * up).astype(BF16)
        backward = rates * dot_nt(weights_ref[2, rows, :], values)
        d_gate = (
            backward * up * sigmoid * (1.0 + gate * (1.0 - sigmoid)) * INVERSE
        ).astype(BF16)
        d_up = (backward * silu * INVERSE).astype(BF16)
        out_ref[0, rows, :] = dot_nn(d_gate, keys).astype(BF16)
        out_ref[1, rows, :] = dot_nn(d_up, keys).astype(BF16)
        out_ref[2, rows, :] = dot_nn(hidden, values).astype(BF16)


def attend_rows(edge_ref, index, query_tile, keys_prev, keys_own, keys_next,
                values_prev, values_own, values_next):
    scale = 1.0 / math.sqrt(HEAD_DIM)
    row = lax.broadcasted_iota(jnp.int32, (TILE, TILE), 0)
    col = lax.broadcasted_iota(jnp.int32, (TILE, TILE), 1)
    minus = jnp.float32(-jnp.inf)
    edge_prev = edge_ref[0, 0]
    edge_next = edge_ref[0, 1]
    score_prev = dot_nt(query_tile, keys_prev)
    score_own = dot_nt(query_tile, keys_own)
    score_next = dot_nt(query_tile, keys_next)
    first = score_prev[:, :TILE] + jnp.where(col >= row, edge_prev, minus)
    parts = [first]
    if score_prev.shape[1] > TILE:
        parts.append(score_prev[:, TILE:] + edge_prev)
    parts.append(score_own)
    if score_next.shape[1] > TILE:
        parts.append(score_next[:, :-TILE] + edge_next)
    parts.append(score_next[:, -TILE:] + jnp.where(col <= row, edge_next, minus))
    scores = jnp.concatenate(parts, axis=1)
    highest = jnp.max(scores, axis=1, keepdims=True)
    weights = jnp.exp((scores - highest) * scale)
    total = jnp.sum(weights, axis=1, keepdims=True)
    weights = weights.astype(BF16)
    width_prev, width_own = score_prev.shape[1], score_own.shape[1]
    attended = (
        dot_nn(weights[:, :width_prev], values_prev)
        + dot_nn(weights[:, width_prev:width_prev + width_own], values_own)
        + dot_nn(weights[:, width_prev + width_own:], values_next)
    )
    return attended / total


def window_tile(edge_ref, index, query_tile, prev_ref, keys_ref, values_ref, next_ref):
    reach = keys_ref.shape[0]
    heads = []
    for head in range(HEADS_GRP):
        cols = slice(head * HEAD_DIM, (head + 1) * HEAD_DIM)
        low, high = index * TILE, (index + 1) * TILE
        heads.append(
            attend_rows(
                edge_ref, index, query_tile[:, cols],
                prev_ref[low:reach, cols], keys_ref[:, cols], next_ref[:high, cols],
                prev_ref[reach + low:, cols], values_ref[:, cols],
                next_ref[reach:reach + high, cols],
            )
        )
    both = jnp.concatenate(heads, axis=1)
    mean = jnp.mean(both * both, axis=1, keepdims=True)
    return (both * lax.rsqrt(mean + 1e-05)).astype(BF16)


def first_kernel(edge_ref, queries_ref, prev_ref, keys_ref, values_ref, next_ref, map_ref, out_ref):
    for index in range(queries_ref.shape[0] // TILE):
        rows = slice(index * TILE, (index + 1) * TILE)
        normed = window_tile(
            edge_ref, index, queries_ref[rows, :], prev_ref, keys_ref, values_ref, next_ref
        )
        out_ref[rows, :] = dot_nn(normed, map_ref[...]).astype(BF16)


def second_kernel(edge_ref, queries_ref, keep_ref, near_ref, far_ref,
                  prev_ref, keys_ref, values_ref, next_ref, out_ref):
    for index in range(queries_ref.shape[0] // TILE):
        rows = slice(index * TILE, (index + 1) * TILE)
        mixed = (
            keep_ref[1, rows, :].astype(F32)
            + near_ref[1, rows, :].astype(F32)
            + far_ref[rows, :].astype(F32)
        )
        query = (queries_ref[rows, :].astype(F32) + mixed).astype(BF16)
        out_ref[rows, :] = window_tile(
            edge_ref, index, query, prev_ref, keys_ref, values_ref, next_ref
        )


def renew_kernel(gradient_ref, weights_ref, query_ref, new_ref, fast_ref):
    limit_norm = math.sqrt(FAST_HIDDEN * FAST_DIM) / 2.0
    square = jnp.zeros((1, weights_ref.shape[2]), F32)
    step = 64
    for matrix in range(3):
        for low in range(0, weights_ref.shape[1], step):
            part = gradient_ref[matrix, low:low + step, :].astype(F32)
            square = square + jnp.sum(part * part, axis=0, keepdims=True)
    square = jnp.sum(square, axis=1, keepdims=True)
    factor = jnp.minimum(1.0, limit_norm * lax.rsqrt(square + 1e-06))
    for matrix in range(3):
        for low in range(0, weights_ref.shape[1], step):
            rows = slice(low, low + step)
            old = weights_ref[matrix, rows, :].astype(F32)
            stepped = old + factor * gradient_ref[matrix, rows, :].astype(F32)
            norm = jnp.sqrt(jnp.sum(old * old, axis=1, keepdims=True))
            size = jnp.sum(stepped * stepped, axis=1, keepdims=True)
            new_ref[matrix, rows, :] = (stepped * norm * lax.rsqrt(size + 1e-06)).astype(BF16)
    step = 128
    for low in range(0, query_ref.shape[0], step):
        rows = slice(low, low + step)
        query = query_ref[rows, :]
        gate = dot_nt(query, new_ref[0]) * INVERSE
        up = dot_nt(query, new_ref[1]) * INVERSE
        hidden = (jax.nn.silu(gate) * up).astype(BF16)
        raw = dot_nn(hidden, new_ref[2])
        mean = jnp.mean(raw * raw, axis=1, keepdims=True)
        fast_ref[rows, :] = (raw * lax.rsqrt(mean + 1e-05)).astype(BF16)


def mix_kernel(place_ref, fast_ref, map_ref, out_ref):
    width = out_ref.shape[2]
    for slot in range(2):
        start = pl.multiple_of(place_ref[0, slot] * width, width)
        columns = map_ref[:, pl.ds(start, width)]
        out_ref[slot] = dot_nn(fast_ref[...], columns).astype(BF16)


def seq_shift(value, up):
    peers = lax.axis_size("seq")
    pairs = [(i, i + 1) for i in range(peers - 1)]
    return lax.ppermute(value, "seq", pairs if up else [(j, i) for i, j in pairs])


def head_swap(value, bit):
    return lax.ppermute(value, "head", [(i, i ^ bit) for i in range(lax.axis_size("head"))])


def local(
    queries_first,
    keys_first,
    values_first,
    input_map,
    fast_keys,
    fast_values,
    step_rates,
    fast_weights,
    output_map,
    queries_second,
    keys_second,
    values_second,
):
    rows, width = queries_first.shape
    seq_count = lax.axis_size("seq")
    seq_place = lax.axis_index("seq")
    head_place = lax.axis_index("head")
    weights = jnp.transpose(fast_weights[0], (1, 0, 2))
    hidden_size, fast_width = weights.shape[1:]
    shape = jax.ShapeDtypeStruct
    minus = jnp.float32(-jnp.inf)
    edges = jnp.stack(
        [
            jnp.where(seq_place > 0, 0.0, minus),
            jnp.where(seq_place < seq_count - 1, 0.0, minus),
        ]
    ).reshape(1, 2)

    gradient = call(
        gradient_kernel,
        shape(weights.shape, BF16),
        (step_rates.reshape(1, rows), fast_keys, fast_values, weights),
        12 * rows * hidden_size * fast_width,
        8 * rows * fast_width,
    )
    share = lax.psum_scatter(gradient, "seq", scatter_dimension=1, tiled=True)
    gathered = lax.all_gather(share, "seq", axis=1, tiled=True)

    both_first = jnp.concatenate([keys_first, values_first])
    prev_first = seq_shift(both_first, True)
    next_first = seq_shift(both_first, False)
    attend_flops = 12 * rows * rows * width
    fast_query = call(
        first_kernel,
        shape((rows, fast_width), BF16),
        (edges, queries_first, prev_first, keys_first, values_first, next_first, input_map[0]),
        attend_flops,
        16 * rows * width,
        scalars=1,
    )
    both_second = jnp.concatenate([keys_second, values_second])
    prev_second = seq_shift(both_second, True)
    next_second = seq_shift(both_second, False)

    updated, fast_out = call(
        renew_kernel,
        (shape(weights.shape, BF16), shape((rows, fast_width), BF16)),
        (gathered, weights, fast_query),
        6 * rows * hidden_size * fast_width,
        12 * hidden_size * fast_width,
    )
    share_rows = hidden_size // seq_count
    own_new = lax.dynamic_slice_in_dim(updated, seq_place * share_rows, share_rows, 1)

    def mixed_for(low_bit):
        far = (head_place // 2) ^ 1
        near = head_place // 2
        places = jnp.stack([far * 2 + low_bit, near * 2 + low_bit]).reshape(1, 2)
        return call(
            mix_kernel,
            shape((2, rows, width), BF16),
            (places, fast_out, output_map),
            4 * rows * fast_width * width,
            8 * rows * width,
            scalars=1,
        )

    my_bit = head_place % 2
    near_part = head_swap(mixed_for(1 - my_bit), 1)
    keep_part = mixed_for(my_bit)
    to_send = (keep_part[0].astype(F32) + near_part[0].astype(F32)).astype(BF16)
    far_part = head_swap(to_send, 2)

    normed_second = call(
        second_kernel,
        shape((rows, width), BF16),
        (edges, queries_second, keep_part, near_part, far_part,
         prev_second, keys_second, values_second, next_second),
        attend_flops,
        16 * rows * width,
        scalars=1,
    )
    return (normed_second, jnp.transpose(own_new, (1, 0, 2))[None])


def solution(mesh):
    return jax.shard_map(
        local,
        mesh=mesh,
        in_specs=(
            P("seq", "head"),
            P("seq", "head"),
            P("seq", "head"),
            P("head", None, None),
            P("seq", "head"),
            P("seq", "head"),
            P("seq", "head"),
            P("head", None, None, None),
            P("head", None),
            P("seq", "head"),
            P("seq", "head"),
            P("seq", "head"),
        ),
        out_specs=(P("seq", "head"), P("head", "seq", None, None)),
        check_vma=False,
    )
```

time: 228 us -> 187 us (0.82)
  matrix products: 28.2 us -> 0 us
  waiting for transfers between devices: 152 us -> 128 us
  Pallas kernels: 0 us -> 21.3 us
  other arithmetic: 14.9 us -> 0.29 us
  starting transfers between devices: 8.12 us -> 10.5 us
    psum x1 -> x0, waiting for transfers between devices: 83.6 us -> none  [local(): gradient = lax.psum(gradient_rows(0, hidden_size), 'seq')]
    reduce_scatter x1, waiting for transfers between devices: 22.3 us -> 68.3 us  [local(): share = lax.psum_scatter(gradient, 'seq', scatter_dimension=1, tiled=True)]
    all_gather x0 -> x1, waiting for transfers between devices: none -> 21.9 us  [local(): gathered = lax.all_gather(share, 'seq', axis=1, tiled=True)]
    pallas_call x0 -> x6, Pallas kernels: none -> 21.3 us  [call(): pl.pallas_call(body, out_shape=out_shapes, in_specs=in_specs, out_specs=j...]
    dot_general x12 -> x0, matrix products: 20.8 us -> none  [the longest x2 9.09 us: attend_block(): jnp.einsum('hqk,khd->qhd', weights_bf, value_block, preferred_element_typ...]
    ppermute x2 -> x6, waiting for transfers between devices: 46.5 us -> 37.9 us  [the longest x4 37.9 us: seq_shift(): lax.ppermute(value, 'seq', pairs if up else [(j, i) for i, j in pairs])]
    sub x2 -> x0, matrix products: 7.38 us -> none  [attend_block(): weights_exp = jnp.exp(scores - highest)]
    reduce_sum x2 -> x0, other arithmetic: 6.15 us -> none  [the longest x1 3.3 us: local(): jnp.sum(gradient * gradient) + 1e-06]
  transfers between devices with their start and end apart: 4 -> 8, of which waited for: 4 -> 4; matrix products, arithmetic and copies ran while one was open for 10% -> 2% of each run, Pallas kernels for 0% -> 3%
where the time goes in v1:
time: 187 us; the launch traced here: 185 us
  waiting for transfers between devices  128 us (68%)
  Pallas kernels  21.3 us (11%)
  between operations  14.2 us (8%)
  starting transfers between devices  10.5 us (6%)
  local copies, waits for them, and re-layouts  10.1 us (5%)
    reduce_scatter x1, waiting for transfers between devices, local(): share = lax.psum_scatter(gradient, 'seq', scatter_dimension=1, tiled=True)  68.3 us
    ppermute x4, waiting for transfers between devices, seq_shift(): lax.ppermute(value, 'seq', pairs if up else [(j, i) for i, j in pairs])  37.9 us
    all_gather x1, waiting for transfers between devices, local(): gathered = lax.all_gather(share, 'seq', axis=1, tiled=True)  21.9 us
    pallas_call x6, Pallas kernels, call(): pl.pallas_call(body, out_shape=out_shapes, in_specs=in_specs, out_specs=j...  21.3 us
    ppermute x4, starting transfers between devices, seq_shift(): lax.ppermute(value, 'seq', pairs if up else [(j, i) for i, j in pairs])  8.92 us
    unnamed x32, local copies, waits for them, and re-layouts  7.75 us
  transfers between devices with their start and end apart: 8, of which 4 were waited for; matrix products, arithmetic and copies ran while one was open for 2% of the time, Pallas kernels for 3%

profile of v1, /device:TPU:0, one launch (start us, length us, event | category | flops | bytes accessed | tf_op | source)
XLA Modules:
  0.0 184.6 jit_solution(5876575216824499250)
XLA Ops:
  7.2 0.0 reduce-scatter.2.cloned.1.call-start
  7.2 0.0 copy-start.1
  7.2 1.4 copy-done.1
  8.6 1.0 copy-done.10
  9.7 1.0 copy-done.11
  10.7 0.7 copy-done.14
  11.4 4.8 %shard_map.131 = bf16[3,512,512]{2,1,0:T(8,128)(2,1)} custom-call(f32[1,512]{1,0:T(1,128)S(1)} %bitcast.26, bf16[512,512]{1,0:T(8,128)(2,1)S(1)} %copy-done.10, bf16[512,512]{1,0:T(8,128)(2,1)S(1)} %copy-done.11, bf16[3,512,512]{2,1,0:T(8,128)(2,1)S(1)} %bitcast.23), custom_call_target="tpu_custom_call" | custom-call | flops 1610612736 | bytes 2097152 | tf_op jit(solution)/shard_map/pallas_call | solution.py:36
  16.2 0.0 reduce-scatter.2.cloned.1.call-update
  16.2 0.0 all-gather.2.cloned.1.call-start
  16.2 68.3 %reduce-scatter.2.cloned.1.call-done = bf16[3,64,512]{2,1,0:T(8,128)(2,1)} async-done(((bf16[3,512,512]{2,1,0:T(8,128)(2,1)}), bf16[3,64,512]{2,1,0:T(8,128)(2,1)}) %reduce-scatter.2.cloned.1.call-update) | async-done | bytes 196624 | tf_op jit(solution)/shard_map/reduce_scatter | solution.py:229
  84.6 0.0 all-gather.2.cloned.1.call-update
  84.6 0.0 copy-done.7
  84.6 0.0 copy-done.8
  84.7 2.9 %collective-permute-start = (bf16[1024,256]{1,0:T(8,128)(2,1)S(1)}, bf16[1024,256]{1,0:T(8,128)(2,1)S(1)}, u32[]{:S(2)}, u32[]{:S(2)}) collective-permute-start(bf16[1024,256]{1,0:T(8,128)(2,1)S(1)} %constant_dynamic-update-slice_fusion), channel_id=1, source_target_pairs={{0,4},{4,8},{8,12},{12,16},{16,20},{20,24},{24,28},{1,5},{5,9},{9,... | collective-permute-start | bytes 1572872 | tf_op jit(solution)/shard_map/ppermute | solution.py:186
  87.6 1.3 collective-permute-start.1
  88.9 0.1 add_bitcast_fusion.1.place_ref
  89.0 0.1 maximum_bitcast_fusion.edge_ref
  89.1 21.1 %collective-permute-done.prev_ref = bf16[1024,256]{1,0:T(8,128)(2,1)S(1)} collective-permute-done((bf16[1024,256]{1,0:T(8,128)(2,1)S(1)}, bf16[1024,256]{1,0:T(8,128)(2,1)S(1)}, u32[]{:S(2)}, u32[]{:S(2)}) %collective-permute-start) | collective-permute-done | bytes 524320 | tf_op jit(solution)/shard_map/ppermute | solution.py:186
  110.2 0.0 collective-permute-done.1.next_ref
  110.2 0.0 copy-done.12
  110.2 0.0 copy-done.13
  110.2 4.9 %shard_map.132.query_ref = bf16[512,512]{1,0:T(8,128)(2,1)S(1)} custom-call(f32[1,2]{1,0:T(1,128)S(1)} %maximum_bitcast_fusion.edge_ref, bf16[512,256]{1,0:T(8,128)(2,1)S(1)} %copy-done.12, bf16[1024,256]{1,0:T(8,128)(2,1)S(1)} %collective-permute-done.prev_ref, bf16[512,256]{1,0:T(8,128)(2,1)S(1)} %copy-done.7, bf16[512,256]{1,0:T(8,128)(2,1)S(1)} %copy-done.8, ...), custom_call_target="tpu_custom_call" | custom-call | flops 805306368 | bytes 2097152 | tf_op jit(solution)/shard_map/pallas_call | solution.py:36
  115.1 0.0 copy-start
  115.1 21.9 %all-gather.2.cloned.1.call-done.gradient_ref = bf16[3,512,512]{2,1,0:T(8,128)(2,1)} async-done(((bf16[3,64,512]{2,1,0:T(8,128)(2,1)}), bf16[3,512,512]{2,1,0:T(8,128)(2,1)}) %all-gather.2.cloned.1.call-update) | async-done | bytes 1572880 | tf_op jit(solution)/shard_map/all_gather | solution.py:230
  137.0 1.4 copy-done.2
  138.4 1.4 copy-done.3
  139.8 3.4 %shard_map.133 = (bf16[3,512,512]{2,1,0:T(8,128)(2,1)S(1)}, bf16[512,512]{1,0:T(8,128)(2,1)S(1)}) custom-call(bf16[3,512,512]{2,1,0:T(8,128)(2,1)S(1)} %copy-done.3, bf16[3,512,512]{2,1,0:T(8,128)(2,1)S(1)} %bitcast.24, bf16[512,512]{1,0:T(8,128)(2,1)S(1)} %shard_map.132.query_ref), custom_call_target="tpu_custom_call" | custom-call | flops 805306368 | bytes 3145728 | tf_op jit(solution)/shard_map/pallas_call | solution.py:36
  143.2 0.0 copy-start.9
  143.2 0.0 copy-start.4
  143.2 0.0 copy-start.5
  143.2 0.0 copy-done
  143.2 1.8 shard_map.135
  145.0 0.0 collective-permute-start.2
  145.0 0.7 constant_dynamic-update-slice_fusion.3
  145.7 0.0 copy-done.5
  145.7 0.7 constant_dynamic-update-slice_fusion.2
  146.5 3.3 %collective-permute-start.4 = (bf16[1024,256]{1,0:T(8,128)(2,1)}, bf16[1024,256]{1,0:T(8,128)(2,1)}, u32[]{:S(2)}, u32[]{:S(2)}) collective-permute-start(bf16[1024,256]{1,0:T(8,128)(2,1)} %constant_dynamic-update-slice_fusion.2), channel_id=1, source_target_pairs={{0,4},{4,8},{8,12},{12,16},{16,20},{20,24},{24,28},{1,5},{5,9},{9,... | collective-permute-start | bytes 1572872 | tf_op jit(solution)/shard_map/ppermute | solution.py:186
  149.7 1.5 collective-permute-start.5
  151.2 0.1 add_bitcast_fusion.place_ref
  151.3 1.0 shard_map.134.keep_ref
  152.3 0.0 collective-permute-done.2.near_ref
  152.3 0.1 fusion
  152.4 1.5 collective-permute-start.3
  153.9 1.6 dynamic-slice_bitcast_fusion
  155.5 16.8 %collective-permute-done.4.prev_ref = bf16[1024,256]{1,0:T(8,128)(2,1)} collective-permute-done((bf16[1024,256]{1,0:T(8,128)(2,1)}, bf16[1024,256]{1,0:T(8,128)(2,1)}, u32[]{:S(2)}, u32[]{:S(2)}) %collective-permute-start.4) | collective-permute-done | bytes 524320 | tf_op jit(solution)/shard_map/ppermute | solution.py:186
  172.3 0.0 collective-permute-done.5.next_ref
  172.3 0.0 collective-permute-done.3.far_ref
  172.3 5.4 %shard_map.136 = bf16[512,256]{1,0:T(8,128)(2,1)} custom-call(f32[1,2]{1,0:T(1,128)S(1)} %maximum_bitcast_fusion.edge_ref, bf16[512,256]{1,0:T(8,128)(2,1)S(1)} %copy-done.6, bf16[2,512,256]{2,1,0:T(8,128)(2,1)S(1)} %shard_map.134.keep_ref, bf16[2,512,256]{2,1,0:T(8,128)(2,1)S(1)} %collective-permute-done.2.near_ref, ...), custom_call_target="tpu_custom_call" | custom-call | flops 805306368 | bytes 2097152 | tf_op jit(solution)/shard_map/pallas_call | solution.py:36
  (15 shorter events, 0.1 us)
Async XLA Ops:
  7.2 77.4 %reduce-scatter.2.cloned.1.call-start = ((), (), s32[]{:S(2)}) async-start(), calls=%async_computation.1 | async-start | bytes 1769472 | tf_op jit(solution)/shard_map/reduce_scatter | solution.py:229
  7.2 1.4 copy-start.1
  8.6 1.0 copy-start.10
  9.7 1.0 copy-start.11
  10.7 0.7 copy-start.14
  16.2 68.4 %copy-start.7 = (bf16[512,256]{1,0:T(8,128)(2,1)S(1)}, bf16[512,256]{1,0:T(8,128)(2,1)}, u32[]{:S(2)}) copy-start(bf16[512,256]{1,0:T(8,128)(2,1)} %keys_ref.4) | copy-start | bytes 786436
  16.2 68.5 %copy-start.8 = (bf16[512,256]{1,0:T(8,128)(2,1)S(1)}, bf16[512,256]{1,0:T(8,128)(2,1)}, u32[]{:S(2)}) copy-start(bf16[512,256]{1,0:T(8,128)(2,1)} %values_ref.4) | copy-start | bytes 786436
  16.2 94.0 %copy-start.12 = (bf16[512,256]{1,0:T(8,128)(2,1)S(1)}, bf16[512,256]{1,0:T(8,128)(2,1)}, u32[]{:S(2)}) copy-start(bf16[512,256]{1,0:T(8,128)(2,1)} %queries_ref.2) | copy-start | bytes 786436
  16.2 94.0 %copy-start.13 = (bf16[1,256,512]{2,1,0:T(8,128)(2,1)S(1)}, bf16[1,256,512]{2,1,0:T(8,128)(2,1)}, u32[]{:S(2)}) copy-start(bf16[1,256,512]{2,1,0:T(8,128)(2,1)} %param.15) | copy-start | bytes 786436
  16.2 120.8 %all-gather.2.cloned.1.call-start = ((), (), s32[]{:S(2)}) async-start(), calls=%async_computation.2 | async-start | bytes 1769472 | tf_op jit(solution)/shard_map/all_gather | solution.py:230
  84.7 25.5 %collective-permute-start = (bf16[1024,256]{1,0:T(8,128)(2,1)S(1)}, bf16[1024,256]{1,0:T(8,128)(2,1)S(1)}, u32[]{:S(2)}, u32[]{:S(2)}) collective-permute-start(bf16[1024,256]{1,0:T(8,128)(2,1)S(1)} %constant_dynamic-update-slice_fusion), channel_id=1, source_target_pairs={{0,4},{4,8},{8,12},{12,16},{16,20},{20,24},{24,28},{1,5},{5,9},{9,... | collective-permute-start | bytes 1572872 | tf_op jit(solution)/shard_map/ppermute | solution.py:186
  87.6 22.6 %collective-permute-start.1 = (bf16[1024,256]{1,0:T(8,128)(2,1)S(1)}, bf16[1024,256]{1,0:T(8,128)(2,1)S(1)}, u32[]{:S(2)}, u32[]{:S(2)}) collective-permute-start(bf16[1024,256]{1,0:T(8,128)(2,1)S(1)} %constant_dynamic-update-slice_fusion), channel_id=1, source_target_pairs={{4,0},{8,4},{12,8},{16,12},{20,16},{24,20},{28,24},{5,1},{9,5},{13... | collective-permute-start | bytes 1572872 | tf_op jit(solution)/shard_map/ppermute | solution.py:186
  115.1 28.1 %copy-start = (bf16[512,1024]{1,0:T(8,128)(2,1)S(1)}, bf16[512,1024]{1,0:T(8,128)(2,1)}, u32[]{:S(2)}) copy-start(bf16[512,1024]{1,0:T(8,128)(2,1)} %map_ref.3) | copy-start | bytes 3145732
  137.0 1.4 copy-start.2
  138.4 1.4 copy-start.3
  143.2 3.3 %copy-start.9 = (bf16[3,512,512]{2,1,0:T(8,128)(2,1)}, bf16[3,512,512]{2,1,0:T(8,128)(2,1)S(1)}, u32[]{:S(2)}) copy-start(bf16[3,512,512]{2,1,0:T(8,128)(2,1)S(1)} %get-tuple-element.5) | copy-start | bytes 4718596
  143.2 1.8 copy-start.4
  143.2 2.5 %copy-start.5 = (bf16[512,256]{1,0:T(8,128)(2,1)S(1)}, bf16[512,256]{1,0:T(8,128)(2,1)}, u32[]{:S(2)}) copy-start(bf16[512,256]{1,0:T(8,128)(2,1)} %values_ref.5) | copy-start | bytes 786436
  145.0 7.2 %collective-permute-start.2 = (bf16[2,512,256]{2,1,0:T(8,128)(2,1)}, bf16[2,512,256]{2,1,0:T(8,128)(2,1)S(1)}, u32[]{:S(2)}, u32[]{:S(2)}) collective-permute-start(bf16[2,512,256]{2,1,0:T(8,128)(2,1)} %shard_map.135), channel_id=1, source_target_pairs={{0,1},{1,0},{2,3},{3,2},{4,5},{5,4},{6,7},{7,6},{8,9},{9,8},{10,11... | collective-permute-start | bytes 1572872 | tf_op jit(solution)/shard_map/ppermute | solution.py:190
  146.5 25.8 %collective-permute-start.4 = (bf16[1024,256]{1,0:T(8,128)(2,1)}, bf16[1024,256]{1,0:T(8,128)(2,1)}, u32[]{:S(2)}, u32[]{:S(2)}) collective-permute-start(bf16[1024,256]{1,0:T(8,128)(2,1)} %constant_dynamic-update-slice_fusion.2), channel_id=1, source_target_pairs={{0,4},{4,8},{8,12},{12,16},{16,20},{20,24},{24,28},{1,5},{5,9},{9,... | collective-permute-start | bytes 1572872 | tf_op jit(solution)/shard_map/ppermute | solution.py:186
  149.7 22.6 %collective-permute-start.5 = (bf16[1024,256]{1,0:T(8,128)(2,1)}, bf16[1024,256]{1,0:T(8,128)(2,1)}, u32[]{:S(2)}, u32[]{:S(2)}) collective-permute-start(bf16[1024,256]{1,0:T(8,128)(2,1)} %constant_dynamic-update-slice_fusion.2), channel_id=1, source_target_pairs={{4,0},{8,4},{12,8},{16,12},{20,16},{24,20},{28,24},{5,1},{9,5},{13... | collective-permute-start | bytes 1572872 | tf_op jit(solution)/shard_map/ppermute | solution.py:186
  151.3 21.1 %copy-start.6 = (bf16[512,256]{1,0:T(8,128)(2,1)S(1)}, bf16[512,256]{1,0:T(8,128)(2,1)}, u32[]{:S(2)}) copy-start(bf16[512,256]{1,0:T(8,128)(2,1)} %queries_ref.3) | copy-start | bytes 786436
  152.4 20.0 %collective-permute-start.3 = (bf16[512,256]{1,0:T(8,128)(2,1)S(1)}, bf16[512,256]{1,0:T(8,128)(2,1)S(1)}, u32[]{:S(2)}, u32[]{:S(2)}) collective-permute-start(bf16[512,256]{1,0:T(8,128)(2,1)S(1)} %fusion), channel_id=1, source_target_pairs={{0,2},{1,3},{2,0},{3,1},{4,6},{5,7},{6,4},{7,5},{8,10},{9,11},{10,... | collective-permute-start | bytes 786440 | tf_op jit(solution)/shard_map/ppermute | solution.py:190
Sparse Core Ops, SparseCore 0:
  16.3 68.2 reduce-scatter.1
  87.0 49.9 all-gather.1

commit v2 on v1

--- a/solution.py
+++ b/solution.py
@@ -44,12 +44,40 @@
     )(*operands)
 
 
-def gradient_kernel(rates_ref, keys_ref, values_ref, weights_ref, out_ref):
+def slot_of(block, order):
+    slot = 0
+    for bit in order:
+        slot = slot * 2 + ((block >> bit) & 1)
+    return slot
+
+
+def block_at(slot, order):
+    block = 0
+    for place, bit in enumerate(reversed(order)):
+        block |= ((slot >> place) & 1) << bit
+    return block
+
+
+def gradient_kernel(orders, place_ref, rates_ref, keys_ref, values_ref, weights_ref, *out_refs):
+    place = place_ref[0, 0]
     rates = rates_ref[...]
     keys = keys_ref[...]
     values = values_ref[...]
+    hidden_size = weights_ref.shape[1]
     step = 128
-    for low in range(0, weights_ref.shape[1], step):
+
+    def put(matrix, low, product):
+        order = orders[matrix]
+        block_rows = hidden_size >> len(order)
+        for start in range(0, step, block_rows):
+            if not order:
+                out_refs[matrix][low:low + step, :] = product.astype(BF16)
+                break
+            slot = slot_of(((low + start) // block_rows) ^ place, order)
+            rows = pl.ds(pl.multiple_of(slot * block_rows, block_rows), block_rows)
+            out_refs[matrix][rows, :] = product[start:start + block_rows].astype(BF16)
+
+    for low in range(0, hidden_size, step):
         rows = slice(low, low + step)
         gate = dot_nt(weights_ref[0, rows, :], keys) * INVERSE
         up = dot_nt(weights_ref[1, rows, :], keys) * INVERSE
@@ -61,9 +89,9 @@
             backward * up * sigmoid * (1.0 + gate * (1.0 - sigmoid)) * INVERSE
         ).astype(BF16)
         d_up = (backward * silu * INVERSE).astype(BF16)
-        out_ref[0, rows, :] = dot_nn(d_gate, keys).astype(BF16)
-        out_ref[1, rows, :] = dot_nn(d_up, keys).astype(BF16)
-        out_ref[2, rows, :] = dot_nn(hidden, values).astype(BF16)
+        put(0, low, dot_nn(d_gate, keys))
+        put(1, low, dot_nn(d_up, keys))
+        put(2, low, dot_nn(hidden, values))
 
 
 def attend_rows(edge_ref, index, query_tile, keys_prev, keys_own, keys_next,
@@ -142,24 +170,38 @@
         )
 
 
-def renew_kernel(gradient_ref, weights_ref, query_ref, new_ref, fast_ref):
+def renew_kernel(orders, place_ref, weights_ref, query_ref, *refs):
+    pieces, (own_ref, fast_ref, new_ref) = refs[:-3], refs[-3:]
+    place = place_ref[0, 0]
     limit_norm = math.sqrt(FAST_HIDDEN * FAST_DIM) / 2.0
     square = jnp.zeros((1, weights_ref.shape[2]), F32)
     step = 64
-    for matrix in range(3):
-        for low in range(0, weights_ref.shape[1], step):
-            part = gradient_ref[matrix, low:low + step, :].astype(F32)
+    for piece in pieces:
+        for low in range(0, piece.shape[0], step):
+            part = piece[low:low + step, :].astype(F32)
             square = square + jnp.sum(part * part, axis=0, keepdims=True)
     square = jnp.sum(square, axis=1, keepdims=True)
     factor = jnp.minimum(1.0, limit_norm * lax.rsqrt(square + 1e-06))
-    for matrix in range(3):
-        for low in range(0, weights_ref.shape[1], step):
-            rows = slice(low, low + step)
-            old = weights_ref[matrix, rows, :].astype(F32)
-            stepped = old + factor * gradient_ref[matrix, rows, :].astype(F32)
-            norm = jnp.sqrt(jnp.sum(old * old, axis=1, keepdims=True))
-            size = jnp.sum(stepped * stepped, axis=1, keepdims=True)
-            new_ref[matrix, rows, :] = (stepped * norm * lax.rsqrt(size + 1e-06)).astype(BF16)
+    per_matrix = len(pieces) // 3
+    for matrix, order in enumerate(orders):
+        block_rows = weights_ref.shape[1] >> len(order)
+        slots = 1 << len(order)
+        for slot in range(slots):
+            piece = pieces[matrix * per_matrix + slot * per_matrix // slots]
+            inside = slot % (slots // per_matrix)
+            block = block_at(slot, order) ^ place if order else 0
+            for low in range(0, block_rows, step):
+                count = min(step, block_rows)
+                rows = pl.ds(pl.multiple_of(block * block_rows + low, count), count)
+                old = weights_ref[matrix, rows, :].astype(F32)
+                part = piece[inside * block_rows + low:inside * block_rows + low + count, :]
+                stepped = old + factor * part.astype(F32)
+                norm = jnp.sqrt(jnp.sum(old * old, axis=1, keepdims=True))
+                size = jnp.sum(stepped * stepped, axis=1, keepdims=True)
+                fresh = (stepped * norm * lax.rsqrt(size + 1e-06)).astype(BF16)
+                new_ref[matrix, rows, :] = fresh
+                if slot == 0:
+                    own_ref[matrix, low:low + count, :] = fresh
     step = 128
     for low in range(0, query_ref.shape[0], step):
         rows = slice(low, low + step)
@@ -188,6 +230,30 @@
 
 def head_swap(value, bit):
     return lax.ppermute(value, "head", [(i, i ^ bit) for i in range(lax.axis_size("head"))])
+
+
+def seq_swap(value, bit):
+    step = 1 << bit
+    return lax.ppermute(value, "seq", [(i, i ^ step) for i in range(lax.axis_size("seq"))])
+
+
+def sum_over_seq(chunks, orders):
+    keeps = [[chunk] for chunk in chunks]
+    for turn in range(len(orders[0])):
+        swapped = []
+        for keep, order in zip(keeps, orders):
+            half = keep[0].shape[0] // 2
+            total = sum(part[half:].astype(F32) for part in keep).astype(BF16)
+            swapped.append(seq_swap(total, order[turn]))
+        keeps = [
+            [part[:part.shape[0] // 2] for part in keep] + [new]
+            for keep, new in zip(keeps, swapped)
+        ]
+    held = [(sum(part.astype(F32) for part in keep).astype(BF16),) for keep in keeps]
+    for turn in reversed(range(len(orders[0]))):
+        whole = [jnp.concatenate(parts) if len(parts) > 1 else parts[0] for parts in held]
+        held = [(own, seq_swap(own, order[turn])) for own, order in zip(whole, orders)]
+    return [part for parts in held for part in parts]
 
 
 def local(
@@ -219,15 +285,25 @@
         ]
     ).reshape(1, 2)
 
-    gradient = call(
-        gradient_kernel,
-        shape(weights.shape, BF16),
-        (step_rates.reshape(1, rows), fast_keys, fast_values, weights),
+    bits = tuple(range(seq_count.bit_length() - 1))
+    halving = seq_count == 1 << len(bits) and len(bits) > 1 and hidden_size >> len(bits) >= 16
+    if halving:
+        orders = (bits, bits, bits[1:] + bits[:1])
+    else:
+        orders = ((), (), ())
+    place = seq_place.astype(jnp.int32).reshape(1, 1)
+    gradients = call(
+        functools.partial(gradient_kernel, orders),
+        [shape(weights.shape[1:], BF16)] * 3,
+        (place, step_rates.reshape(1, rows), fast_keys, fast_values, weights),
         12 * rows * hidden_size * fast_width,
         8 * rows * fast_width,
-    )
-    share = lax.psum_scatter(gradient, "seq", scatter_dimension=1, tiled=True)
-    gathered = lax.all_gather(share, "seq", axis=1, tiled=True)
+        scalars=1,
+    )
+    if halving:
+        gathered = sum_over_seq(gradients, orders)
+    else:
+        gathered = lax.psum(gradients, "seq")
 
     both_first = jnp.concatenate([keys_first, values_first])
     prev_first = seq_shift(both_first, True)
@@ -245,15 +321,19 @@
     prev_second = seq_shift(both_second, True)
     next_second = seq_shift(both_second, False)
 
-    updated, fast_out = call(
-        renew_kernel,
-        (shape(weights.shape, BF16), shape((rows, fast_width), BF16)),
-        (gathered, weights, fast_query),
+    own_rows = hidden_size >> len(orders[0])
+    own_new, fast_out = call(
+        functools.partial(renew_kernel, orders),
+        [shape((3, own_rows, fast_width), BF16), shape((rows, fast_width), BF16)],
+        (place, weights, fast_query, *gathered),
         6 * rows * hidden_size * fast_width,
         12 * hidden_size * fast_width,
-    )
-    share_rows = hidden_size // seq_count
-    own_new = lax.dynamic_slice_in_dim(updated, seq_place * share_rows, share_rows, 1)
+        scalars=1,
+        scratch=[pltpu.VMEM(weights.shape, BF16)],
+    )
+    if not halving:
+        share_rows = hidden_size // seq_count
+        own_new = lax.dynamic_slice_in_dim(own_new, seq_place * share_rows, share_rows, 1)
 
     def mixed_for(low_bit):
         far = (head_place // 2) ^ 1

time: 187 us -> 122 us (0.65)
  waiting for transfers between devices: 128 us -> 41.6 us
  starting transfers between devices: 10.5 us -> 42 us
  between operations: 14.2 us -> 0.94 us
  other arithmetic: 0.29 us -> 6.73 us
    reduce_scatter x1 -> x0, waiting for transfers between devices: 68.3 us -> none  [local(): share = lax.psum_scatter(gradient, 'seq', scatter_dimension=1, tiled=True)]
    ppermute x0 -> x18, starting transfers between devices: none -> 28.9 us  [seq_swap(): lax.ppermute(value, 'seq', [(i, i ^ step) for i in range(lax.axis_size('s...]
    ppermute x0 -> x18, waiting for transfers between devices: none -> 23.2 us  [seq_swap(): lax.ppermute(value, 'seq', [(i, i ^ step) for i in range(lax.axis_size('s...]
    all_gather x1 -> x0, waiting for transfers between devices: 21.9 us -> none  [local(): gathered = lax.all_gather(share, 'seq', axis=1, tiled=True)]
    ppermute x4, waiting for transfers between devices: 37.9 us -> 18.4 us  [seq_shift(): lax.ppermute(value, 'seq', pairs if up else [(j, i) for i, j in pairs])]
    convert_element_type x0 -> x9, other arithmetic: none -> 6.34 us  [the longest x6 3.67 us: sum_over_seq(): total = sum((part[half:].astype(F32) for part in keep)).astype(BF16)]
    ppermute x4, starting transfers between devices: 8.92 us -> 11.5 us  [seq_shift(): lax.ppermute(value, 'seq', pairs if up else [(j, i) for i, j in pairs])]
    slice x0 -> x3, local copies, waits for them, and re-layouts: none -> 2.15 us  [sum_over_seq(): total = sum((part[half:].astype(F32) for part in keep)).astype(BF16)]
  transfers between devices with their start and end apart: 8 -> 24, of which waited for: 4 -> 11; matrix products, arithmetic and copies ran while one was open for 2% -> 9% of each run, Pallas kernels for 3% -> 5%
where the time goes in v2:
time: 122 us; the launch traced here: 121 us
  starting transfers between devices  42 us (34%)
  waiting for transfers between devices  41.6 us (34%)
  Pallas kernels  20.4 us (17%)
  local copies, waits for them, and re-layouts  9.21 us (8%)
  other arithmetic  6.73 us (6%)
    ppermute x18, starting transfers between devices, seq_swap(): lax.ppermute(value, 'seq', [(i, i ^ step) for i in range(lax.axis_size('s...  28.9 us
    ppermute x18, waiting for transfers between devices, seq_swap(): lax.ppermute(value, 'seq', [(i, i ^ step) for i in range(lax.axis_size('s...  23.2 us
    pallas_call x6, Pallas kernels, call(): pl.pallas_call(body, out_shape=out_shapes, in_specs=in_specs, out_specs=j...  20.4 us
    ppermute x4, waiting for transfers between devices, seq_shift(): lax.ppermute(value, 'seq', pairs if up else [(j, i) for i, j in pairs])  18.4 us
    ppermute x4, starting transfers between devices, seq_shift(): lax.ppermute(value, 'seq', pairs if up else [(j, i) for i, j in pairs])  11.5 us
    unnamed x30, local copies, waits for them, and re-layouts  5.64 us
    convert_element_type x6, other arithmetic, sum_over_seq(): total = sum((part[half:].astype(F32) for part in keep)).astype(BF16)  3.67 us
    convert_element_type x3, other arithmetic, sum_over_seq(): sum((part.astype(F32) for part in keep)).astype(BF16)  2.67 us
  transfers between devices with their start and end apart: 24, of which 11 were waited for; matrix products, arithmetic and copies ran while one was open for 9% of the time, Pallas kernels for 5%

profile of v2, /device:TPU:0, one launch (start us, length us, event | category | flops | bytes accessed | tf_op | source)
XLA Modules:
  0.0 120.9 jit_solution(6910133153158542519)
XLA Ops:
  0.6 1.4 %copy-done.1 = bf16[1,512,3,512]{3,1,2,0:T(8,128)(2,1)S(1)} copy-done((bf16[1,512,3,512]{3,1,2,0:T(8,128)(2,1)S(1)}, bf16[1,512,3,512]{3,1,2,0:T(8,128)(2,1)}, u32[]{:S(2)}) %copy-start.1) | copy-done | bytes 1572888
  2.0 1.0 copy-done.8
  3.1 1.0 copy-done.9
  4.1 0.7 copy-done.12
  4.8 3.6 %shard_map.132 = (bf16[512,512]{1,0:T(8,128)(2,1)S(1)}, bf16[512,512]{1,0:T(8,128)(2,1)S(1)}, bf16[512,512]{1,0:T(8,128)(2,1)S(1)}) custom-call(s32[1,1]{1,0:T(1,128)} %bitcast.6.place_ref, f32[1,512]{1,0:T(1,128)S(1)} %bitcast.26, bf16[512,512]{1,0:T(8,128)(2,1)S(1)} %copy-done.8, bf16[512,512]{1,0:T(8,128)(2,1)S(1)} %copy-done.9, ...), custom_call_target="tpu_custom_call" | custom-call | flops 1610612736 | bytes 2097152 | tf_op jit(solution)/shard_map/pallas_call | solution.py:36
  8.4 0.7 slice.115
  9.2 3.0 %collective-permute-start.2 = (bf16[256,512]{1,0:T(8,128)(2,1)}, bf16[256,512]{1,0:T(8,128)(2,1)}, u32[]{:S(2)}, u32[]{:S(2)}) collective-permute-start(bf16[256,512]{1,0:T(8,128)(2,1)} %slice.115), channel_id=1, source_target_pairs={{0,4},{4,0},{8,12},{12,8},{16,20},{20,16},{24,28},{28,24},{1,5},{5... | collective-permute-start | bytes 786440 | tf_op jit(solution)/shard_map/ppermute | solution.py:237
  12.1 0.7 slice.124
  12.8 0.7 constant_dynamic-update-slice_fusion.1
  13.6 0.7 constant_dynamic-update-slice_fusion
  14.3 3.9 %collective-permute-start = (bf16[1024,256]{1,0:T(8,128)(2,1)}, bf16[1024,256]{1,0:T(8,128)(2,1)S(1)}, u32[]{:S(2)}, u32[]{:S(2)}) collective-permute-start(bf16[1024,256]{1,0:T(8,128)(2,1)} %constant_dynamic-update-slice_fusion), channel_id=1, source_target_pairs={{0,4},{4,8},{8,12},{12,16},{16,20},{20,24},{24,28},{1,5},{5,9},{9,... | collective-permute-start | bytes 1572872 | tf_op jit(solution)/shard_map/ppermute | solution.py:228
  18.2 1.3 %collective-permute-start.1 = (bf16[1024,256]{1,0:T(8,128)(2,1)}, bf16[1024,256]{1,0:T(8,128)(2,1)S(1)}, u32[]{:S(2)}, u32[]{:S(2)}) collective-permute-start(bf16[1024,256]{1,0:T(8,128)(2,1)} %constant_dynamic-update-slice_fusion), channel_id=1, source_target_pairs={{4,0},{8,4},{12,8},{16,12},{20,16},{24,20},{28,24},{5,1},{9,5},{13... | collective-permute-start | bytes 1572872 | tf_op jit(solution)/shard_map/ppermute | solution.py:228
  19.5 0.7 slice.133
  20.2 3.6 %collective-permute-start.14 = (bf16[256,512]{1,0:T(8,128)(2,1)}, bf16[256,512]{1,0:T(8,128)(2,1)}, u32[]{:S(2)}, u32[]{:S(2)}) collective-permute-start(bf16[256,512]{1,0:T(8,128)(2,1)} %slice.133), channel_id=1, source_target_pairs={{0,8},{4,12},{8,0},{12,4},{16,24},{20,28},{24,16},{28,20},{1,9},{5... | collective-permute-start | bytes 786440 | tf_op jit(solution)/shard_map/ppermute | solution.py:237
  23.8 0.9 add_convert_fusion.3
  24.8 7.8 %collective-permute-start.3 = (bf16[128,512]{1,0:T(8,128)(2,1)S(1)}, bf16[128,512]{1,0:T(8,128)(2,1)S(1)}, u32[]{:S(2)}, u32[]{:S(2)}) collective-permute-start(bf16[128,512]{1,0:T(8,128)(2,1)S(1)} %add_convert_fusion.3), channel_id=1, source_target_pairs={{0,8},{4,12},{8,0},{12,4},{16,24},{20,28},{24,16},{28,20},{1,9},{5... | collective-permute-start | bytes 393224 | tf_op jit(solution)/shard_map/ppermute | solution.py:237
  32.6 3.4 %collective-permute-done.8 = bf16[256,512]{1,0:T(8,128)(2,1)S(1)} collective-permute-done((bf16[256,512]{1,0:T(8,128)(2,1)}, bf16[256,512]{1,0:T(8,128)(2,1)S(1)}, u32[]{:S(2)}, u32[]{:S(2)}) %collective-permute-start.8) | collective-permute-done | bytes 262176 | tf_op jit(solution)/shard_map/ppermute | solution.py:237
  36.0 2.5 %collective-permute-start.9 = (bf16[128,512]{1,0:T(8,128)(2,1)S(1)}, bf16[128,512]{1,0:T(8,128)(2,1)S(1)}, u32[]{:S(2)}, u32[]{:S(2)}) collective-permute-start(bf16[128,512]{1,0:T(8,128)(2,1)S(1)} %add_convert_fusion.2), channel_id=1, source_target_pairs={{0,8},{4,12},{8,0},{12,4},{16,24},{20,28},{24,16},{28,20},{1,9},{5... | collective-permute-start | bytes 393224 | tf_op jit(solution)/shard_map/ppermute | solution.py:237
  38.6 3.3 %collective-permute-done.14 = bf16[256,512]{1,0:T(8,128)(2,1)} collective-permute-done((bf16[256,512]{1,0:T(8,128)(2,1)}, bf16[256,512]{1,0:T(8,128)(2,1)}, u32[]{:S(2)}, u32[]{:S(2)}) %collective-permute-start.14) | collective-permute-done | bytes 262176 | tf_op jit(solution)/shard_map/ppermute | solution.py:237
  41.9 0.9 add_convert_fusion.1
  42.8 2.6 %collective-permute-start.15 = (bf16[128,512]{1,0:T(8,128)(2,1)S(1)}, bf16[128,512]{1,0:T(8,128)(2,1)S(1)}, u32[]{:S(2)}, u32[]{:S(2)}) collective-permute-start(bf16[128,512]{1,0:T(8,128)(2,1)S(1)} %add_convert_fusion.1), channel_id=1, source_target_pairs={{0,16},{4,20},{8,24},{12,28},{16,0},{20,4},{24,8},{28,12},{1,17},{... | collective-permute-start | bytes 393224 | tf_op jit(solution)/shard_map/ppermute | solution.py:237
  45.4 0.9 add_convert_fusion.9
  46.3 1.8 %collective-permute-start.4 = (bf16[64,512]{1,0:T(8,128)(2,1)S(1)}, bf16[64,512]{1,0:T(8,128)(2,1)S(1)}, u32[]{:S(2)}, u32[]{:S(2)}) collective-permute-start(bf16[64,512]{1,0:T(8,128)(2,1)S(1)} %add_convert_fusion.9), channel_id=1, source_target_pairs={{0,16},{4,20},{8,24},{12,28},{16,0},{20,4},{24,8},{28,12},{1,17},{... | collective-permute-start | bytes 196616 | tf_op jit(solution)/shard_map/ppermute | solution.py:237
  48.1 1.9 %collective-permute-start.10 = (bf16[64,512]{1,0:T(8,128)(2,1)S(1)}, bf16[64,512]{1,0:T(8,128)(2,1)S(1)}, u32[]{:S(2)}, u32[]{:S(2)}) collective-permute-start(bf16[64,512]{1,0:T(8,128)(2,1)S(1)} %add_convert_fusion.7), channel_id=1, source_target_pairs={{0,16},{4,20},{8,24},{12,28},{16,0},{20,4},{24,8},{28,12},{1,17},{... | collective-permute-start | bytes 196616 | tf_op jit(solution)/shard_map/ppermute | solution.py:237
  50.0 4.1 %collective-permute-done.15 = bf16[128,512]{1,0:T(8,128)(2,1)S(1)} collective-permute-done((bf16[128,512]{1,0:T(8,128)(2,1)S(1)}, bf16[128,512]{1,0:T(8,128)(2,1)S(1)}, u32[]{:S(2)}, u32[]{:S(2)}) %collective-permute-start.15) | collective-permute-done | bytes 131104 | tf_op jit(solution)/shard_map/ppermute | solution.py:237
  54.2 0.9 add_convert_fusion.5
  55.1 1.8 %collective-permute-done.4 = bf16[64,512]{1,0:T(8,128)(2,1)S(1)} collective-permute-done((bf16[64,512]{1,0:T(8,128)(2,1)S(1)}, bf16[64,512]{1,0:T(8,128)(2,1)S(1)}, u32[]{:S(2)}, u32[]{:S(2)}) %collective-permute-start.4) | collective-permute-done | bytes 65568 | tf_op jit(solution)/shard_map/ppermute | solution.py:237
  56.9 0.9 add_convert_fusion.8
  57.9 0.9 add_convert_fusion.6
  58.8 2.9 %collective-permute-start.11 = (bf16[64,512]{1,0:T(8,128)(2,1)S(1)}, bf16[64,512]{1,0:T(8,128)(2,1)S(1)}, u32[]{:S(2)}, u32[]{:S(2)}) collective-permute-start(bf16[64,512]{1,0:T(8,128)(2,1)S(1)} %add_convert_fusion.6), channel_id=1, source_target_pairs={{0,16},{4,20},{8,24},{12,28},{16,0},{20,4},{24,8},{28,12},{1,17},{... | collective-permute-start | bytes 196616 | tf_op jit(solution)/shard_map/ppermute | solution.py:237
  61.7 0.9 add_convert_fusion.4
  63.2 3.4 %collective-permute-done.11 = bf16[64,512]{1,0:T(8,128)(2,1)S(1)} collective-permute-done((bf16[64,512]{1,0:T(8,128)(2,1)S(1)}, bf16[64,512]{1,0:T(8,128)(2,1)S(1)}, u32[]{:S(2)}, u32[]{:S(2)}) %collective-permute-start.11) | collective-permute-done | bytes 65568 | tf_op jit(solution)/shard_map/ppermute | solution.py:237
  66.7 1.0 collective-permute-done.17
  67.8 1.1 collective-permute-done.6
  69.0 0.9 collective-permute-start.7
  69.8 4.6 %collective-permute-done.12 = bf16[128,512]{1,0:T(8,128)(2,1)S(1)} collective-permute-done((bf16[128,512]{1,0:T(8,128)(2,1)S(1)}, bf16[128,512]{1,0:T(8,128)(2,1)S(1)}, u32[]{:S(2)}, u32[]{:S(2)}) %collective-permute-start.12) | collective-permute-done | bytes 131104 | tf_op jit(solution)/shard_map/ppermute | solution.py:237
  74.6 1.1 collective-permute-start.19
  76.0 4.9 %shard_map.131.query_ref = bf16[512,512]{1,0:T(8,128)(2,1)S(1)} custom-call(f32[1,2]{1,0:T(1,128)S(1)} %maximum_bitcast_fusion.edge_ref, bf16[512,256]{1,0:T(8,128)(2,1)S(1)} %copy-done.10, bf16[1024,256]{1,0:T(8,128)(2,1)S(1)} %collective-permute-done.prev_ref, bf16[512,256]{1,0:T(8,128)(2,1)S(1)} %copy-done.6, bf16[512,256]{1,0:T(8,128)(2,1)S(1)} %copy-done.7, ...), custom_call_target="tpu_custom_call" | custom-call | flops 805306368 | bytes 2097152 | tf_op jit(solution)/shard_map/pallas_call | solution.py:36
  81.1 4.4 %shard_map.133 = (bf16[3,64,512]{2,1,0:T(8,128)(2,1)}, bf16[512,512]{1,0:T(8,128)(2,1)S(1)}) custom-call(s32[1,1]{1,0:T(1,128)} %bitcast.6.place_ref, bf16[3,512,512]{2,1,0:T(8,128)(2,1)S(1)} %bitcast.24, bf16[512,512]{1,0:T(8,128)(2,1)S(1)} %shard_map.131.query_ref, bf16[256,512]{1,0:T(8,128)(2,1)S(1)} %pad_maximum_fusion.refs_0_, ...), custom_call_target="tpu_custom_call" | custom-call | flops 805306368 | bytes 3145728 | tf_op jit(solution)/shard_map/pallas_call | solution.py:36
  85.5 1.0 shard_map.135
  86.6 0.7 constant_dynamic-update-slice_fusion.3
  87.3 0.7 constant_dynamic-update-slice_fusion.2
  88.0 4.8 %collective-permute-start.22 = (bf16[1024,256]{1,0:T(8,128)(2,1)}, bf16[1024,256]{1,0:T(8,128)(2,1)}, u32[]{:S(2)}, u32[]{:S(2)}) collective-permute-start(bf16[1024,256]{1,0:T(8,128)(2,1)} %constant_dynamic-update-slice_fusion.2), channel_id=1, source_target_pairs={{0,4},{4,8},{8,12},{12,16},{16,20},{20,24},{24,28},{1,5},{5,9},{9,... | collective-permute-start | bytes 1572872 | tf_op jit(solution)/shard_map/ppermute | solution.py:228
  92.8 1.5 %collective-permute-start.23 = (bf16[1024,256]{1,0:T(8,128)(2,1)}, bf16[1024,256]{1,0:T(8,128)(2,1)}, u32[]{:S(2)}, u32[]{:S(2)}) collective-permute-start(bf16[1024,256]{1,0:T(8,128)(2,1)} %constant_dynamic-update-slice_fusion.2), channel_id=1, source_target_pairs={{4,0},{8,4},{12,8},{16,12},{20,16},{24,20},{28,24},{5,1},{9,5},{13... | collective-permute-start | bytes 1572872 | tf_op jit(solution)/shard_map/ppermute | solution.py:228
  94.4 1.0 shard_map.134.keep_ref
  95.5 1.5 %collective-permute-start.21 = (bf16[512,256]{1,0:T(8,128)(2,1)S(1)}, bf16[512,256]{1,0:T(8,128)(2,1)S(1)}, u32[]{:S(2)}, u32[]{:S(2)}) collective-permute-start(bf16[512,256]{1,0:T(8,128)(2,1)S(1)} %fusion), channel_id=1, source_target_pairs={{0,2},{1,3},{2,0},{3,1},{4,6},{5,7},{6,4},{7,5},{8,10},{9,11},{10,... | collective-permute-start | bytes 786440 | tf_op jit(solution)/shard_map/ppermute | solution.py:232
  97.0 18.4 %collective-permute-done.22.prev_ref = bf16[1024,256]{1,0:T(8,128)(2,1)} collective-permute-done((bf16[1024,256]{1,0:T(8,128)(2,1)}, bf16[1024,256]{1,0:T(8,128)(2,1)}, u32[]{:S(2)}, u32[]{:S(2)}) %collective-permute-start.22) | collective-permute-done | bytes 524320 | tf_op jit(solution)/shard_map/ppermute | solution.py:228
  115.4 5.5 %shard_map.136 = bf16[512,256]{1,0:T(8,128)(2,1)} custom-call(f32[1,2]{1,0:T(1,128)S(1)} %maximum_bitcast_fusion.edge_ref, bf16[512,256]{1,0:T(8,128)(2,1)S(1)} %copy-done.5, bf16[2,512,256]{2,1,0:T(8,128)(2,1)S(1)} %shard_map.134.keep_ref, bf16[2,512,256]{2,1,0:T(8,128)(2,1)S(1)} %collective-permute-done.20.near_ref, ...), custom_call_target="tpu_custom_call" | custom-call | flops 805306368 | bytes 2097152 | tf_op jit(solution)/shard_map/pallas_call | solution.py:36
  (60 shorter events, 1.7 us)
Async XLA Ops:
  0.6 1.4 %copy-start.1 = (bf16[1,512,3,512]{3,1,2,0:T(8,128)(2,1)S(1)}, bf16[1,512,3,512]{3,1,2,0:T(8,128)(2,1)}, u32[]{:S(2)}) copy-start(bf16[1,512,3,512]{3,1,2,0:T(8,128)(2,1)} %param.19) | copy-start | bytes 4718596
  2.0 1.0 copy-start.8
  3.1 1.0 copy-start.9
  4.1 0.7 copy-start.12
  4.8 8.0 %copy-start.6 = (bf16[512,256]{1,0:T(8,128)(2,1)S(1)}, bf16[512,256]{1,0:T(8,128)(2,1)}, u32[]{:S(2)}) copy-start(bf16[512,256]{1,0:T(8,128)(2,1)} %keys_ref.3) | copy-start | bytes 786436
  8.4 5.1 %copy-start.7 = (bf16[512,256]{1,0:T(8,128)(2,1)S(1)}, bf16[512,256]{1,0:T(8,128)(2,1)}, u32[]{:S(2)}) copy-start(bf16[512,256]{1,0:T(8,128)(2,1)} %values_ref.3) | copy-start | bytes 786436
  9.2 14.7 %collective-permute-start.2 = (bf16[256,512]{1,0:T(8,128)(2,1)}, bf16[256,512]{1,0:T(8,128)(2,1)}, u32[]{:S(2)}, u32[]{:S(2)}) collective-permute-start(bf16[256,512]{1,0:T(8,128)(2,1)} %slice.115), channel_id=1, source_target_pairs={{0,4},{4,0},{8,12},{12,8},{16,20},{20,16},{24,28},{28,24},{1,5},{5... | collective-permute-start | bytes 786440 | tf_op jit(solution)/shard_map/ppermute | solution.py:237
  12.8 23.2 %collective-permute-start.8 = (bf16[256,512]{1,0:T(8,128)(2,1)}, bf16[256,512]{1,0:T(8,128)(2,1)S(1)}, u32[]{:S(2)}, u32[]{:S(2)}) collective-permute-start(bf16[256,512]{1,0:T(8,128)(2,1)} %slice.124), channel_id=1, source_target_pairs={{0,4},{4,0},{8,12},{12,8},{16,20},{20,16},{24,28},{28,24},{1,5},{5... | collective-permute-start | bytes 786440 | tf_op jit(solution)/shard_map/ppermute | solution.py:237
  14.3 61.7 %collective-permute-start = (bf16[1024,256]{1,0:T(8,128)(2,1)}, bf16[1024,256]{1,0:T(8,128)(2,1)S(1)}, u32[]{:S(2)}, u32[]{:S(2)}) collective-permute-start(bf16[1024,256]{1,0:T(8,128)(2,1)} %constant_dynamic-update-slice_fusion), channel_id=1, source_target_pairs={{0,4},{4,8},{8,12},{12,16},{16,20},{20,24},{24,28},{1,5},{5,9},{9,... | collective-permute-start | bytes 1572872 | tf_op jit(solution)/shard_map/ppermute | solution.py:228
  18.2 57.7 %collective-permute-start.1 = (bf16[1024,256]{1,0:T(8,128)(2,1)}, bf16[1024,256]{1,0:T(8,128)(2,1)S(1)}, u32[]{:S(2)}, u32[]{:S(2)}) collective-permute-start(bf16[1024,256]{1,0:T(8,128)(2,1)} %constant_dynamic-update-slice_fusion), channel_id=1, source_target_pairs={{4,0},{8,4},{12,8},{16,12},{20,16},{24,20},{28,24},{5,1},{9,5},{13... | collective-permute-start | bytes 1572872 | tf_op jit(solution)/shard_map/ppermute | solution.py:228
  20.2 21.6 %collective-permute-start.14 = (bf16[256,512]{1,0:T(8,128)(2,1)}, bf16[256,512]{1,0:T(8,128)(2,1)}, u32[]{:S(2)}, u32[]{:S(2)}) collective-permute-start(bf16[256,512]{1,0:T(8,128)(2,1)} %slice.133), channel_id=1, source_target_pairs={{0,8},{4,12},{8,0},{12,4},{16,24},{20,28},{24,16},{28,20},{1,9},{5... | collective-permute-start | bytes 786440 | tf_op jit(solution)/shard_map/ppermute | solution.py:237
  24.8 20.7 %collective-permute-start.3 = (bf16[128,512]{1,0:T(8,128)(2,1)S(1)}, bf16[128,512]{1,0:T(8,128)(2,1)S(1)}, u32[]{:S(2)}, u32[]{:S(2)}) collective-permute-start(bf16[128,512]{1,0:T(8,128)(2,1)S(1)} %add_convert_fusion.3), channel_id=1, source_target_pairs={{0,8},{4,12},{8,0},{12,4},{16,24},{20,28},{24,16},{28,20},{1,9},{5... | collective-permute-start | bytes 393224 | tf_op jit(solution)/shard_map/ppermute | solution.py:237
  36.0 20.9 %copy-start.13 = (bf16[256,512]{1,0:T(8,128)(2,1)}, bf16[256,512]{1,0:T(8,128)(2,1)S(1)}, u32[]{:S(2)}) copy-start(bf16[256,512]{1,0:T(8,128)(2,1)S(1)} %collective-permute-done.8) | copy-start | bytes 786436
  36.0 12.0 %collective-permute-start.9 = (bf16[128,512]{1,0:T(8,128)(2,1)S(1)}, bf16[128,512]{1,0:T(8,128)(2,1)S(1)}, u32[]{:S(2)}, u32[]{:S(2)}) collective-permute-start(bf16[128,512]{1,0:T(8,128)(2,1)S(1)} %add_convert_fusion.2), channel_id=1, source_target_pairs={{0,8},{4,12},{8,0},{12,4},{16,24},{20,28},{24,16},{28,20},{1,9},{5... | collective-permute-start | bytes 393224 | tf_op jit(solution)/shard_map/ppermute | solution.py:237
  42.8 11.4 %collective-permute-start.15 = (bf16[128,512]{1,0:T(8,128)(2,1)S(1)}, bf16[128,512]{1,0:T(8,128)(2,1)S(1)}, u32[]{:S(2)}, u32[]{:S(2)}) collective-permute-start(bf16[128,512]{1,0:T(8,128)(2,1)S(1)} %add_convert_fusion.1), channel_id=1, source_target_pairs={{0,16},{4,20},{8,24},{12,28},{16,0},{20,4},{24,8},{28,12},{1,17},{... | collective-permute-start | bytes 393224 | tf_op jit(solution)/shard_map/ppermute | solution.py:237
  46.3 10.6 %collective-permute-start.4 = (bf16[64,512]{1,0:T(8,128)(2,1)S(1)}, bf16[64,512]{1,0:T(8,128)(2,1)S(1)}, u32[]{:S(2)}, u32[]{:S(2)}) collective-permute-start(bf16[64,512]{1,0:T(8,128)(2,1)S(1)} %add_convert_fusion.9), channel_id=1, source_target_pairs={{0,16},{4,20},{8,24},{12,28},{16,0},{20,4},{24,8},{28,12},{1,17},{... | collective-permute-start | bytes 196616 | tf_op jit(solution)/shard_map/ppermute | solution.py:237
  48.1 9.8 %collective-permute-start.10 = (bf16[64,512]{1,0:T(8,128)(2,1)S(1)}, bf16[64,512]{1,0:T(8,128)(2,1)S(1)}, u32[]{:S(2)}, u32[]{:S(2)}) collective-permute-start(bf16[64,512]{1,0:T(8,128)(2,1)S(1)} %add_convert_fusion.7), channel_id=1, source_target_pairs={{0,16},{4,20},{8,24},{12,28},{16,0},{20,4},{24,8},{28,12},{1,17},{... | collective-permute-start | bytes 196616 | tf_op jit(solution)/shard_map/ppermute | solution.py:237
  55.1 6.7 %collective-permute-start.16 = (bf16[64,512]{1,0:T(8,128)(2,1)S(1)}, bf16[64,512]{1,0:T(8,128)(2,1)S(1)}, u32[]{:S(2)}, u32[]{:S(2)}) collective-permute-start(bf16[64,512]{1,0:T(8,128)(2,1)S(1)} %add_convert_fusion.5), channel_id=1, source_target_pairs={{0,4},{4,0},{8,12},{12,8},{16,20},{20,16},{24,28},{28,24},{1,5},{5... | collective-permute-start | bytes 196616 | tf_op jit(solution)/shard_map/ppermute | solution.py:237
  57.8 18.2 %copy-start.10 = (bf16[512,256]{1,0:T(8,128)(2,1)S(1)}, bf16[512,256]{1,0:T(8,128)(2,1)}, u32[]{:S(2)}) copy-start(bf16[512,256]{1,0:T(8,128)(2,1)} %queries_ref.2) | copy-start | bytes 786436
  57.8 18.2 %copy-start.11 = (bf16[1,256,512]{2,1,0:T(8,128)(2,1)S(1)}, bf16[1,256,512]{2,1,0:T(8,128)(2,1)}, u32[]{:S(2)}) copy-start(bf16[1,256,512]{2,1,0:T(8,128)(2,1)} %param.15) | copy-start | bytes 786436
  57.8 5.3 %collective-permute-start.5 = (bf16[64,512]{1,0:T(8,128)(2,1)S(1)}, bf16[64,512]{1,0:T(8,128)(2,1)S(1)}, u32[]{:S(2)}, u32[]{:S(2)}) collective-permute-start(bf16[64,512]{1,0:T(8,128)(2,1)S(1)} %add_convert_fusion.8), channel_id=1, source_target_pairs={{0,16},{4,20},{8,24},{12,28},{16,0},{20,4},{24,8},{28,12},{1,17},{... | collective-permute-start | bytes 196616 | tf_op jit(solution)/shard_map/ppermute | solution.py:237
  58.8 7.8 %collective-permute-start.11 = (bf16[64,512]{1,0:T(8,128)(2,1)S(1)}, bf16[64,512]{1,0:T(8,128)(2,1)S(1)}, u32[]{:S(2)}, u32[]{:S(2)}) collective-permute-start(bf16[64,512]{1,0:T(8,128)(2,1)S(1)} %add_convert_fusion.6), channel_id=1, source_target_pairs={{0,16},{4,20},{8,24},{12,28},{16,0},{20,4},{24,8},{28,12},{1,17},{... | collective-permute-start | bytes 196616 | tf_op jit(solution)/shard_map/ppermute | solution.py:237
  62.6 5.1 %collective-permute-start.17 = (bf16[64,512]{1,0:T(8,128)(2,1)S(1)}, bf16[64,512]{1,0:T(8,128)(2,1)S(1)}, u32[]{:S(2)}, u32[]{:S(2)}) collective-permute-start(bf16[64,512]{1,0:T(8,128)(2,1)S(1)} %add_convert_fusion.4), channel_id=1, source_target_pairs={{0,4},{4,0},{8,12},{12,8},{16,20},{20,16},{24,28},{28,24},{1,5},{5... | collective-permute-start | bytes 196616 | tf_op jit(solution)/shard_map/ppermute | solution.py:237
  63.1 5.8 %collective-permute-start.6 = (bf16[128,512]{1,0:T(8,128)(2,1)S(1)}, bf16[128,512]{1,0:T(8,128)(2,1)S(1)}, u32[]{:S(2)}, u32[]{:S(2)}) collective-permute-start(bf16[128,512]{1,0:T(8,128)(2,1)S(1)} %pad_maximum_fusion.3), channel_id=1, source_target_pairs={{0,8},{4,12},{8,0},{12,4},{16,24},{20,28},{24,16},{28,20},{1,9},{5... | collective-permute-start | bytes 393224 | tf_op jit(solution)/shard_map/ppermute | solution.py:237
  66.7 7.8 %collective-permute-start.12 = (bf16[128,512]{1,0:T(8,128)(2,1)S(1)}, bf16[128,512]{1,0:T(8,128)(2,1)S(1)}, u32[]{:S(2)}, u32[]{:S(2)}) collective-permute-start(bf16[128,512]{1,0:T(8,128)(2,1)S(1)} %pad_maximum_fusion.4), channel_id=1, source_target_pairs={{0,8},{4,12},{8,0},{12,4},{16,24},{20,28},{24,16},{28,20},{1,9},{5... | collective-permute-start | bytes 393224 | tf_op jit(solution)/shard_map/ppermute | solution.py:237
  67.7 6.9 %collective-permute-start.18 = (bf16[128,512]{1,0:T(8,128)(2,1)S(1)}, bf16[128,512]{1,0:T(8,128)(2,1)S(1)}, u32[]{:S(2)}, u32[]{:S(2)}) collective-permute-start(bf16[128,512]{1,0:T(8,128)(2,1)S(1)} %pad_maximum_fusion.5), channel_id=1, source_target_pairs={{0,16},{4,20},{8,24},{12,28},{16,0},{20,4},{24,8},{28,12},{1,17},{... | collective-permute-start | bytes 393224 | tf_op jit(solution)/shard_map/ppermute | solution.py:237
  69.0 11.9 %collective-permute-start.7 = (bf16[256,512]{1,0:T(8,128)(2,1)S(1)}, bf16[256,512]{1,0:T(8,128)(2,1)S(1)}, u32[]{:S(2)}, u32[]{:S(2)}) collective-permute-start(bf16[256,512]{1,0:T(8,128)(2,1)S(1)} %pad_maximum_fusion.refs_0_), channel_id=1, source_target_pairs={{0,4},{4,0},{8,12},{12,8},{16,20},{20,16},{24,28},{28,24},{1,5},{5... | collective-permute-start | bytes 786440 | tf_op jit(solution)/shard_map/ppermute | solution.py:237
  74.5 6.4 %collective-permute-start.13 = (bf16[256,512]{1,0:T(8,128)(2,1)S(1)}, bf16[256,512]{1,0:T(8,128)(2,1)S(1)}, u32[]{:S(2)}, u32[]{:S(2)}) collective-permute-start(bf16[256,512]{1,0:T(8,128)(2,1)S(1)} %pad_maximum_fusion.1.refs_2_), channel_id=1, source_target_pairs={{0,4},{4,0},{8,12},{12,8},{16,20},{20,16},{24,28},{28,24},{1,5},{5... | collective-permute-start | bytes 786440 | tf_op jit(solution)/shard_map/ppermute | solution.py:237
  74.6 6.5 %copy-start.2 = (bf16[1,512,3,512]{3,1,2,0:T(8,128)(2,1)S(1)}, bf16[1,512,3,512]{3,1,2,0:T(8,128)(2,1)}, u32[]{:S(2)}) copy-start(bf16[1,512,3,512]{3,1,2,0:T(8,128)(2,1)} %param.19) | copy-start | bytes 4718596
  74.6 6.4 %collective-permute-start.19 = (bf16[256,512]{1,0:T(8,128)(2,1)S(1)}, bf16[256,512]{1,0:T(8,128)(2,1)S(1)}, u32[]{:S(2)}, u32[]{:S(2)}) collective-permute-start(bf16[256,512]{1,0:T(8,128)(2,1)S(1)} %pad_maximum_fusion.2.refs_4_), channel_id=1, source_target_pairs={{0,8},{4,12},{8,0},{12,4},{16,24},{20,28},{24,16},{28,20},{1,9},{5... | collective-permute-start | bytes 786440 | tf_op jit(solution)/shard_map/ppermute | solution.py:237
  80.9 4.6 %copy-start = (bf16[512,1024]{1,0:T(8,128)(2,1)S(1)}, bf16[512,1024]{1,0:T(8,128)(2,1)}, u32[]{:S(2)}) copy-start(bf16[512,1024]{1,0:T(8,128)(2,1)} %map_ref.3) | copy-start | bytes 3145732
  85.5 1.1 copy-start.3
  85.5 1.8 %copy-start.4 = (bf16[512,256]{1,0:T(8,128)(2,1)S(1)}, bf16[512,256]{1,0:T(8,128)(2,1)}, u32[]{:S(2)}) copy-start(bf16[512,256]{1,0:T(8,128)(2,1)} %values_ref.5) | copy-start | bytes 786436
  86.5 8.9 %collective-permute-start.20 = (bf16[2,512,256]{2,1,0:T(8,128)(2,1)S(1)}, bf16[2,512,256]{2,1,0:T(8,128)(2,1)S(1)}, u32[]{:S(2)}, u32[]{:S(2)}) collective-permute-start(bf16[2,512,256]{2,1,0:T(8,128)(2,1)S(1)} %shard_map.135), channel_id=1, source_target_pairs={{0,1},{1,0},{2,3},{3,2},{4,5},{5,4},{6,7},{7,6},{8,9},{9,8},{10,11... | collective-permute-start | bytes 1572872 | tf_op jit(solution)/shard_map/ppermute | solution.py:232
  88.0 27.4 %copy-start.5 = (bf16[512,256]{1,0:T(8,128)(2,1)S(1)}, bf16[512,256]{1,0:T(8,128)(2,1)}, u32[]{:S(2)}) copy-start(bf16[512,256]{1,0:T(8,128)(2,1)} %queries_ref.3) | copy-start | bytes 786436
  88.0 27.4 %collective-permute-start.22 = (bf16[1024,256]{1,0:T(8,128)(2,1)}, bf16[1024,256]{1,0:T(8,128)(2,1)}, u32[]{:S(2)}, u32[]{:S(2)}) collective-permute-start(bf16[1024,256]{1,0:T(8,128)(2,1)} %constant_dynamic-update-slice_fusion.2), channel_id=1, source_target_pairs={{0,4},{4,8},{8,12},{12,16},{16,20},{20,24},{24,28},{1,5},{5,9},{9,... | collective-permute-start | bytes 1572872 | tf_op jit(solution)/shard_map/ppermute | solution.py:228
  92.8 22.6 %collective-permute-start.23 = (bf16[1024,256]{1,0:T(8,128)(2,1)}, bf16[1024,256]{1,0:T(8,128)(2,1)}, u32[]{:S(2)}, u32[]{:S(2)}) collective-permute-start(bf16[1024,256]{1,0:T(8,128)(2,1)} %constant_dynamic-update-slice_fusion.2), channel_id=1, source_target_pairs={{4,0},{8,4},{12,8},{16,12},{20,16},{24,20},{28,24},{5,1},{9,5},{13... | collective-permute-start | bytes 1572872 | tf_op jit(solution)/shard_map/ppermute | solution.py:228
  95.5 19.9 %collective-permute-start.21 = (bf16[512,256]{1,0:T(8,128)(2,1)S(1)}, bf16[512,256]{1,0:T(8,128)(2,1)S(1)}, u32[]{:S(2)}, u32[]{:S(2)}) collective-permute-start(bf16[512,256]{1,0:T(8,128)(2,1)S(1)} %fusion), channel_id=1, source_target_pairs={{0,2},{1,3},{2,0},{3,1},{4,6},{5,7},{6,4},{7,5},{8,10},{9,11},{10,... | collective-permute-start | bytes 786440 | tf_op jit(solution)/shard_map/ppermute | solution.py:232

commit v3 on v2

--- a/solution.py
+++ b/solution.py
@@ -29,26 +29,23 @@
     return lax.dot_general(left, right, (((1,), (1,)), ((), ())), preferred_element_type=F32)
 
 
-def call(body, out_shapes, operands, flops, moved, scalars=0, scratch=()):
-    in_specs = [pl.BlockSpec(memory_space=pltpu.SMEM)] * scalars + [
-        pl.BlockSpec(memory_space=pltpu.VMEM)
-    ] * (len(operands) - scalars)
+def call(body, out_shapes, operands, scalars=0, anywhere=0, scratch=(), cost=None):
+    vmem = pl.BlockSpec(memory_space=pltpu.VMEM)
+    in_specs = (
+        [pl.BlockSpec(memory_space=pltpu.SMEM)] * scalars
+        + [vmem] * (len(operands) - scalars - anywhere)
+        + [pl.BlockSpec(memory_space=pl.ANY)] * anywhere
+    )
+    flops, moved = cost or (1000, 1000)
     return pl.pallas_call(
         body,
         out_shape=out_shapes,
         in_specs=in_specs,
-        out_specs=jax.tree.map(lambda _: pl.BlockSpec(memory_space=pltpu.VMEM), out_shapes),
+        out_specs=jax.tree.map(lambda _: vmem, out_shapes),
         scratch_shapes=scratch,
         compiler_params=pltpu.CompilerParams(vmem_limit_bytes=VMEM_LIMIT),
         cost_estimate=pl.CostEstimate(flops=flops, bytes_accessed=moved, transcendentals=0),
     )(*operands)
-
-
-def slot_of(block, order):
-    slot = 0
-    for bit in order:
-        slot = slot * 2 + ((block >> bit) & 1)
-    return slot
 
 
 def block_at(slot, order):
@@ -58,55 +55,78 @@
     return block
 
 
-def gradient_kernel(orders, place_ref, rates_ref, keys_ref, values_ref, weights_ref, *out_refs):
+def load_rows(order, place, source, target, sems, first):
+    block_rows = target.shape[0] >> len(order)
+    copies = []
+    for slot in range(1 << len(order)):
+        block = (block_at(slot, order) ^ place) if order else 0
+        start = pl.multiple_of(block * block_rows, block_rows)
+        copies.append(
+            pltpu.make_async_copy(
+                source.at[pl.ds(start, block_rows), :],
+                target.at[pl.ds(slot * block_rows, block_rows), :],
+                sems.at[first + slot],
+            )
+        )
+    for copy in copies:
+        copy.start()
+    return copies
+
+
+def gradient_kernel(order, down, place_ref, rates_ref, keys_hbm, values_hbm, weights_hbm, *refs):
+    out_refs, (keys_ref, values_ref, weights_ref, sems) = refs[:-4], refs[-4:]
     place = place_ref[0, 0]
+    slots = 1 << len(order)
+    matrices = weights_ref.shape[0]
+    hidden_size = weights_ref.shape[1]
+    keys_copy = pltpu.make_async_copy(keys_hbm, keys_ref, sems.at[matrices * slots])
+    keys_copy.start()
+    copies = [keys_copy]
+    for matrix in range(matrices):
+        copies += load_rows(
+            order, place, weights_hbm.at[matrix], weights_ref.at[matrix], sems, matrix * slots
+        )
+    values_copy = pltpu.make_async_copy(values_hbm, values_ref, sems.at[matrices * slots + 1])
+    values_copy.start()
+    for copy in copies + [values_copy]:
+        copy.wait()
     rates = rates_ref[...]
     keys = keys_ref[...]
     values = values_ref[...]
-    hidden_size = weights_ref.shape[1]
     step = 128
-
-    def put(matrix, low, product):
-        order = orders[matrix]
-        block_rows = hidden_size >> len(order)
-        for start in range(0, step, block_rows):
-            if not order:
-                out_refs[matrix][low:low + step, :] = product.astype(BF16)
-                break
-            slot = slot_of(((low + start) // block_rows) ^ place, order)
-            rows = pl.ds(pl.multiple_of(slot * block_rows, block_rows), block_rows)
-            out_refs[matrix][rows, :] = product[start:start + block_rows].astype(BF16)
-
+    halves = 2 if order else 1
+    half_rows = hidden_size // halves
     for low in range(0, hidden_size, step):
         rows = slice(low, low + step)
+        half, start = low // half_rows, low % half_rows
+        target = slice(start, start + step)
         gate = dot_nt(weights_ref[0, rows, :], keys) * INVERSE
         up = dot_nt(weights_ref[1, rows, :], keys) * INVERSE
         sigmoid = jax.nn.sigmoid(gate)
         silu = gate * sigmoid
-        hidden = (rates * silu * up).astype(BF16)
+        if down:
+            hidden = (rates * silu * up).astype(BF16)
+            out_refs[half][target, :] = dot_nn(hidden, values).astype(BF16)
+            continue
         backward = rates * dot_nt(weights_ref[2, rows, :], values)
         d_gate = (
             backward * up * sigmoid * (1.0 + gate * (1.0 - sigmoid)) * INVERSE
         ).astype(BF16)
         d_up = (backward * silu * INVERSE).astype(BF16)
-        put(0, low, dot_nn(d_gate, keys))
-        put(1, low, dot_nn(d_up, keys))
-        put(2, low, dot_nn(hidden, values))
-
-
-def attend_rows(edge_ref, index, query_tile, keys_prev, keys_own, keys_next,
+        out_refs[half][target, :] = dot_nn(d_gate, keys).astype(BF16)
+        out_refs[halves + half][target, :] = dot_nn(d_up, keys).astype(BF16)
+
+
+def attend_rows(edge_prev, edge_next, query_tile, keys_prev, keys_own, keys_next,
                 values_prev, values_own, values_next):
     scale = 1.0 / math.sqrt(HEAD_DIM)
     row = lax.broadcasted_iota(jnp.int32, (TILE, TILE), 0)
     col = lax.broadcasted_iota(jnp.int32, (TILE, TILE), 1)
     minus = jnp.float32(-jnp.inf)
-    edge_prev = edge_ref[0, 0]
-    edge_next = edge_ref[0, 1]
     score_prev = dot_nt(query_tile, keys_prev)
     score_own = dot_nt(query_tile, keys_own)
     score_next = dot_nt(query_tile, keys_next)
-    first = score_prev[:, :TILE] + jnp.where(col >= row, edge_prev, minus)
-    parts = [first]
+    parts = [score_prev[:, :TILE] + jnp.where(col >= row, edge_prev, minus)]
     if score_prev.shape[1] > TILE:
         parts.append(score_prev[:, TILE:] + edge_prev)
     parts.append(score_own)
@@ -127,47 +147,97 @@
     return attended / total
 
 
-def window_tile(edge_ref, index, query_tile, prev_ref, keys_ref, values_ref, next_ref):
-    reach = keys_ref.shape[0]
-    heads = []
-    for head in range(HEADS_GRP):
-        cols = slice(head * HEAD_DIM, (head + 1) * HEAD_DIM)
+def pack_kernel(side_ref, queries_ref, keys_ref, values_ref, out_ref):
+    count = queries_ref.shape[0]
+    start = pl.multiple_of((1 - side_ref[0, 0]) * HEAD_DIM, HEAD_DIM)
+    for index, ref in enumerate((queries_ref, keys_ref, values_ref)):
+        out_ref[index * count:(index + 1) * count, :] = ref[:, pl.ds(start, HEAD_DIM)]
+
+
+def border_kernel(side_ref, keys_ref, values_ref, other_ref, low_ref, high_ref):
+    count = keys_ref.shape[0]
+    side = side_ref[0, 0]
+    start = pl.multiple_of(side * HEAD_DIM, HEAD_DIM)
+
+    def fill(own_ref, other_out_ref):
+        own_ref[:count, :] = keys_ref[:, pl.ds(start, HEAD_DIM)]
+        own_ref[count:, :] = values_ref[:, pl.ds(start, HEAD_DIM)]
+        other_out_ref[...] = other_ref[count:, :]
+
+    @pl.when(side == 0)
+    def _():
+        fill(low_ref, high_ref)
+
+    @pl.when(side != 0)
+    def _():
+        fill(high_ref, low_ref)
+
+
+def first_kernel(edge_ref, side_ref, queries_ref, other_ref, prev_ref, low_ref, high_ref, next_ref,
+                 keep_ref, send_ref, keys_ref, values_ref):
+    count = queries_ref.shape[0]
+    side = side_ref[0, 0]
+    for index, ref in enumerate((prev_ref, low_ref, high_ref, next_ref)):
+        rows = slice(index * count, (index + 1) * count)
+        keys_ref[rows, :] = ref[:count, :]
+        values_ref[rows, :] = ref[count:, :]
+    start = pl.multiple_of(side * HEAD_DIM, HEAD_DIM)
+    for turn, out_ref in enumerate((keep_ref, send_ref)):
+        base = (side if turn == 0 else 1 - side) * count
+
+        def span(ref, low, length):
+            return ref[pl.ds(pl.multiple_of(base + low, TILE), length), :]
+
+        for index in range(count // TILE):
+            low, high = index * TILE, (index + 1) * TILE
+            query = queries_ref[low:high, pl.ds(start, HEAD_DIM)] if turn == 0 else other_ref[low:high, :]
+            out_ref[low:high, :] = attend_rows(
+                edge_ref[turn, 0], edge_ref[turn, 1], query,
+                span(keys_ref, low, count - low), span(keys_ref, count, count),
+                span(keys_ref, 2 * count, high),
+                span(values_ref, low, count - low), span(values_ref, count, count),
+                span(values_ref, 2 * count, high),
+            ).astype(BF16)
+
+
+def query_kernel(side_ref, keep_ref, other_ref, map_ref, out_ref):
+    side = side_ref[0, 0]
+    own = keep_ref[...].astype(F32)
+    other = other_ref[...].astype(F32)
+    square = jnp.sum(own * own + other * other, axis=1, keepdims=True)
+    norm = lax.rsqrt(square / (HEADS_GRP * HEAD_DIM) + 1e-05)
+    own_map = map_ref[pl.ds(pl.multiple_of(side * HEAD_DIM, HEAD_DIM), HEAD_DIM), :]
+    other_map = map_ref[pl.ds(pl.multiple_of((1 - side) * HEAD_DIM, HEAD_DIM), HEAD_DIM), :]
+    out_ref[...] = (
+        dot_nn((own * norm).astype(BF16), own_map) + dot_nn((other * norm).astype(BF16), other_map)
+    ).astype(BF16)
+
+
+def second_kernel(edge_ref, queries_ref, keep_ref, near_ref, far_ref, keys_prev_ref, keys_ref, keys_next_ref,
+                  values_prev_ref, values_ref, values_next_ref, out_ref):
+    count = keys_ref.shape[0]
+    for index in range(count // TILE):
         low, high = index * TILE, (index + 1) * TILE
-        heads.append(
-            attend_rows(
-                edge_ref, index, query_tile[:, cols],
-                prev_ref[low:reach, cols], keys_ref[:, cols], next_ref[:high, cols],
-                prev_ref[reach + low:, cols], values_ref[:, cols],
-                next_ref[reach:reach + high, cols],
-            )
-        )
-    both = jnp.concatenate(heads, axis=1)
-    mean = jnp.mean(both * both, axis=1, keepdims=True)
-    return (both * lax.rsqrt(mean + 1e-05)).astype(BF16)
-
-
-def first_kernel(edge_ref, queries_ref, prev_ref, keys_ref, values_ref, next_ref, map_ref, out_ref):
-    for index in range(queries_ref.shape[0] // TILE):
-        rows = slice(index * TILE, (index + 1) * TILE)
-        normed = window_tile(
-            edge_ref, index, queries_ref[rows, :], prev_ref, keys_ref, values_ref, next_ref
-        )
-        out_ref[rows, :] = dot_nn(normed, map_ref[...]).astype(BF16)
-
-
-def second_kernel(edge_ref, queries_ref, keep_ref, near_ref, far_ref,
-                  prev_ref, keys_ref, values_ref, next_ref, out_ref):
-    for index in range(queries_ref.shape[0] // TILE):
-        rows = slice(index * TILE, (index + 1) * TILE)
+        rows = slice(low, high)
         mixed = (
             keep_ref[1, rows, :].astype(F32)
             + near_ref[1, rows, :].astype(F32)
             + far_ref[rows, :].astype(F32)
         )
         query = (queries_ref[rows, :].astype(F32) + mixed).astype(BF16)
-        out_ref[rows, :] = window_tile(
-            edge_ref, index, query, prev_ref, keys_ref, values_ref, next_ref
-        )
+        heads = []
+        for head in range(HEADS_GRP):
+            cols = slice(head * HEAD_DIM, (head + 1) * HEAD_DIM)
+            heads.append(
+                attend_rows(
+                    edge_ref[0, 0], edge_ref[0, 1], query[:, cols],
+                    keys_prev_ref[low:, cols], keys_ref[:, cols], keys_next_ref[:high, cols],
+                    values_prev_ref[low:, cols], values_ref[:, cols], values_next_ref[:high, cols],
+                )
+            )
+        both = jnp.concatenate(heads, axis=1)
+        mean = jnp.mean(both * both, axis=1, keepdims=True)
+        out_ref[rows, :] = (both * lax.rsqrt(mean + 1e-05)).astype(BF16)
 
 
 def renew_kernel(orders, place_ref, weights_ref, query_ref, *refs):
@@ -222,10 +292,11 @@
         out_ref[slot] = dot_nn(fast_ref[...], columns).astype(BF16)
 
 
-def seq_shift(value, up):
+def seq_shift(value, step):
     peers = lax.axis_size("seq")
-    pairs = [(i, i + 1) for i in range(peers - 1)]
-    return lax.ppermute(value, "seq", pairs if up else [(j, i) for i, j in pairs])
+    return lax.ppermute(
+        value, "seq", [(i, i + step) for i in range(peers) if 0 <= i + step < peers]
+    )
 
 
 def head_swap(value, bit):
@@ -238,17 +309,18 @@
 
 
 def sum_over_seq(chunks, orders):
-    keeps = [[chunk] for chunk in chunks]
+    keeps = [[keep] for keep, _ in chunks]
     for turn in range(len(orders[0])):
         swapped = []
-        for keep, order in zip(keeps, orders):
-            half = keep[0].shape[0] // 2
-            total = sum(part[half:].astype(F32) for part in keep).astype(BF16)
+        for index, order in enumerate(orders):
+            if turn == 0:
+                total = chunks[index][1]
+            else:
+                half = keeps[index][0].shape[0] // 2
+                total = sum(part[half:].astype(F32) for part in keeps[index]).astype(BF16)
+                keeps[index] = [part[:half] for part in keeps[index]]
             swapped.append(seq_swap(total, order[turn]))
-        keeps = [
-            [part[:part.shape[0] // 2] for part in keep] + [new]
-            for keep, new in zip(keeps, swapped)
-        ]
+        keeps = [keep + [new] for keep, new in zip(keeps, swapped)]
     held = [(sum(part.astype(F32) for part in keep).astype(BF16),) for keep in keeps]
     for turn in reversed(range(len(orders[0]))):
         whole = [jnp.concatenate(parts) if len(parts) > 1 else parts[0] for parts in held]
@@ -278,56 +350,85 @@
     hidden_size, fast_width = weights.shape[1:]
     shape = jax.ShapeDtypeStruct
     minus = jnp.float32(-jnp.inf)
-    edges = jnp.stack(
-        [
-            jnp.where(seq_place > 0, 0.0, minus),
-            jnp.where(seq_place < seq_count - 1, 0.0, minus),
-        ]
-    ).reshape(1, 2)
+    side = seq_place % 2
+
+    def edges_of(block):
+        return [jnp.where(block > 0, 0.0, minus), jnp.where(block < seq_count - 1, 0.0, minus)]
+
+    edges = jnp.stack(edges_of(seq_place) + edges_of(seq_place ^ 1)).reshape(2, 2)
+    side_scalar = side.astype(jnp.int32).reshape(1, 1)
+    place = seq_place.astype(jnp.int32).reshape(1, 1)
+
+    packed = call(
+        pack_kernel,
+        shape((3 * rows, HEAD_DIM), BF16),
+        (side_scalar, queries_first, keys_first, values_first),
+        scalars=1,
+    )
+    other_first = seq_swap(packed, 0)
 
     bits = tuple(range(seq_count.bit_length() - 1))
     halving = seq_count == 1 << len(bits) and len(bits) > 1 and hidden_size >> len(bits) >= 16
+    order, down_order = (bits, bits[1:] + bits[:1]) if halving else ((), ())
+    orders = (order, order, down_order)
+    halves = 2 if halving else 1
+
+    def gradient_of(order, down):
+        matrices, chunks = (2, 1) if down else (3, 2)
+        return call(
+            functools.partial(gradient_kernel, order, down),
+            [shape((hidden_size // halves, fast_width), BF16)] * (halves * chunks),
+            (place, step_rates.reshape(1, rows), fast_keys, fast_values, weights),
+            scalars=1,
+            anywhere=3,
+            scratch=[
+                pltpu.VMEM(fast_keys.shape, BF16),
+                pltpu.VMEM(fast_values.shape, BF16),
+                pltpu.VMEM((matrices, hidden_size, fast_width), BF16),
+                pltpu.SemaphoreType.DMA((matrices * (1 << len(order)) + 2,)),
+            ],
+        )
+
+    down_halves = gradient_of(down_order, True)
+    gate_up_halves = gradient_of(order, False)
+    halves_of = [gate_up_halves[:halves], gate_up_halves[halves:], down_halves]
     if halving:
-        orders = (bits, bits, bits[1:] + bits[:1])
+        gathered = sum_over_seq(halves_of, orders)
     else:
-        orders = ((), (), ())
-    place = seq_place.astype(jnp.int32).reshape(1, 1)
-    gradients = call(
-        functools.partial(gradient_kernel, orders),
-        [shape(weights.shape[1:], BF16)] * 3,
-        (place, step_rates.reshape(1, rows), fast_keys, fast_values, weights),
-        12 * rows * hidden_size * fast_width,
-        8 * rows * fast_width,
+        gathered = lax.psum([part for (part,) in halves_of], "seq")
+
+    low_block, high_block = call(
+        border_kernel,
+        [shape((2 * rows, HEAD_DIM), BF16)] * 2,
+        (side_scalar, keys_first, values_first, other_first),
         scalars=1,
     )
-    if halving:
-        gathered = sum_over_seq(gradients, orders)
-    else:
-        gathered = lax.psum(gradients, "seq")
-
-    both_first = jnp.concatenate([keys_first, values_first])
-    prev_first = seq_shift(both_first, True)
-    next_first = seq_shift(both_first, False)
-    attend_flops = 12 * rows * rows * width
+    prev_first = seq_shift(high_block, 2)
+    next_first = seq_shift(low_block, -2)
+    keep_first, send_first = call(
+        first_kernel,
+        [shape((rows, HEAD_DIM), BF16)] * 2,
+        (edges, side_scalar, queries_first, other_first, prev_first, low_block, high_block, next_first),
+        scalars=2,
+        scratch=[pltpu.VMEM((4 * rows, HEAD_DIM), BF16)] * 2,
+        cost=(12 * rows * rows * width, 16 * rows * width),
+    )
     fast_query = call(
-        first_kernel,
+        query_kernel,
         shape((rows, fast_width), BF16),
-        (edges, queries_first, prev_first, keys_first, values_first, next_first, input_map[0]),
-        attend_flops,
-        16 * rows * width,
+        (side_scalar, keep_first, seq_swap(send_first, 0), input_map[0]),
         scalars=1,
     )
-    both_second = jnp.concatenate([keys_second, values_second])
-    prev_second = seq_shift(both_second, True)
-    next_second = seq_shift(both_second, False)
+
+    keys_prev, keys_next = seq_shift(keys_second, 1), seq_shift(keys_second, -1)
+    values_prev, values_next = seq_shift(values_second, 1), seq_shift(values_second, -1)
+    fast_query, keys_prev, keys_next = lax.optimization_barrier((fast_query, keys_prev, keys_next))
 
     own_rows = hidden_size >> len(orders[0])
     own_new, fast_out = call(
         functools.partial(renew_kernel, orders),
         [shape((3, own_rows, fast_width), BF16), shape((rows, fast_width), BF16)],
         (place, weights, fast_query, *gathered),
-        6 * rows * hidden_size * fast_width,
-        12 * hidden_size * fast_width,
         scalars=1,
         scratch=[pltpu.VMEM(weights.shape, BF16)],
     )
@@ -343,8 +444,6 @@
             mix_kernel,
             shape((2, rows, width), BF16),
             (places, fast_out, output_map),
-            4 * rows * fast_width * width,
-            8 * rows * width,
             scalars=1,
         )
 
@@ -358,10 +457,9 @@
         second_kernel,
         shape((rows, width), BF16),
         (edges, queries_second, keep_part, near_part, far_part,
-         prev_second, keys_second, values_second, next_second),
-        attend_flops,
-        16 * rows * width,
+         keys_prev, keys_second, keys_next, values_prev, values_second, values_next),
         scalars=1,
+        cost=(12 * rows * rows * width, 16 * rows * width),
     )
     return (normed_second, jnp.transpose(own_new, (1, 0, 2))[None])
 

time: 122 us -> 122 us (level)
  waiting for transfers between devices: 41.6 us -> 31.1 us
  starting transfers between devices: 42 us -> 49.8 us
  Pallas kernels: 20.4 us -> 27 us
  local copies, waits for them, and re-layouts: 9.21 us -> 6.21 us
    ppermute x4 -> x6, waiting for transfers between devices: 18.4 us -> 7.79 us  [seq_shift(): lax.ppermute(value, 'seq', [(i, i + step) for i in range(peers) if 0 <= i...]
    ppermute x18 -> x20, starting transfers between devices: 28.9 us -> 36 us  [seq_swap(): lax.ppermute(value, 'seq', [(i, i ^ step) for i in range(lax.axis_size('s...]
    pallas_call x6 -> x10, Pallas kernels: 20.4 us -> 27 us  [call(): pl.pallas_call(body, out_shape=out_shapes, in_specs=in_specs, out_specs=j...]
    slice x3 -> x0, local copies, waits for them, and re-layouts: 2.15 us -> none  [sum_over_seq(): total = sum((part[half:].astype(F32) for part in keep)).astype(BF16)]
    concatenate x2 -> x0, local copies, waits for them, and re-layouts: 1.43 us -> none  [the longest x1 0.72 us: local(): both_second = jnp.concatenate([keys_second, values_second])]
    ppermute x4 -> x6, starting transfers between devices: 11.5 us -> 12.1 us  [seq_shift(): lax.ppermute(value, 'seq', [(i, i + step) for i in range(peers) if 0 <= i...]
    unnamed x30 -> x32, local copies, waits for them, and re-layouts: 5.64 us -> 6.12 us
    ppermute x18 -> x20, waiting for transfers between devices: 23.2 us -> 23.3 us  [seq_swap(): lax.ppermute(value, 'seq', [(i, i ^ step) for i in range(lax.axis_size('s...]
  transfers between devices with their start and end apart: 24 -> 28, of which waited for: 11 -> 10; matrix products, arithmetic and copies ran while one was open for 9% -> 5% of each run, Pallas kernels for 5% -> 9%
where the time goes in v3:
time: 122 us; the launch traced here: 121 us
  starting transfers between devices  49.8 us (41%)
  waiting for transfers between devices  31.1 us (25%)
  Pallas kernels  27 us (22%)
  local copies, waits for them, and re-layouts  6.21 us (5%)
  other arithmetic  5.85 us (5%)
    ppermute x20, starting transfers between devices, seq_swap(): lax.ppermute(value, 'seq', [(i, i ^ step) for i in range(lax.axis_size('s...  36 us
    pallas_call x10, Pallas kernels, call(): pl.pallas_call(body, out_shape=out_shapes, in_specs=in_specs, out_specs=j...  27 us
    ppermute x20, waiting for transfers between devices, seq_swap(): lax.ppermute(value, 'seq', [(i, i ^ step) for i in range(lax.axis_size('s...  23.3 us
    ppermute x6, starting transfers between devices, seq_shift(): lax.ppermute(value, 'seq', [(i, i + step) for i in range(peers) if 0 <= i...  12.1 us
    ppermute x6, waiting for transfers between devices, seq_shift(): lax.ppermute(value, 'seq', [(i, i + step) for i in range(peers) if 0 <= i...  7.79 us
    unnamed x32, local copies, waits for them, and re-layouts  6.12 us
    convert_element_type x6, other arithmetic, sum_over_seq(): total = sum((part[half:].astype(F32) for part in keeps[index])).astype(BF16)  3.67 us
  transfers between devices with their start and end apart: 28, of which 10 were waited for; matrix products, arithmetic and copies ran while one was open for 5% of the time, Pallas kernels for 9%

profile of v3, /device:TPU:0, one launch (start us, length us, event | category | flops | bytes accessed | tf_op | source)
XLA Modules:
  0.0 120.9 jit_solution(15153216332799000158)
XLA Ops:
  0.6 1.4 %copy-done = bf16[1,512,3,512]{3,1,2,0:T(8,128)(2,1)S(1)} copy-done((bf16[1,512,3,512]{3,1,2,0:T(8,128)(2,1)S(1)}, bf16[1,512,3,512]{3,1,2,0:T(8,128)(2,1)}, u32[]{:S(2)}) %copy-start) | copy-done | bytes 1572888
  2.0 1.0 copy-done.3
  3.1 1.0 copy-done.4
  4.1 0.7 copy-done.15
  4.8 3.8 %shard_map.136 = (bf16[256,512]{1,0:T(8,128)(2,1)S(1)}, bf16[256,512]{1,0:T(8,128)(2,1)S(1)}) custom-call(s32[1,1]{1,0:T(1,128)} %bitcast.7.place_ref, f32[1,512]{1,0:T(1,128)S(1)} %bitcast.28, bf16[512,512]{1,0:T(8,128)(2,1)S(1)} %copy-done.3, bf16[512,512]{1,0:T(8,128)(2,1)S(1)} %copy-done.4, bf16[3,512,512]{2,1,0:T(8,128)(2,1)S(1)} %bitcast.24), custom_call_target="tpu_custom_call" | custom-call | flops 1000 | bytes 1000 | tf_op jit(solution)/shard_map/pallas_call | solution.py:40
  8.7 3.1 %collective-permute-start.18 = (bf16[256,512]{1,0:T(8,128)(2,1)S(1)}, bf16[256,512]{1,0:T(8,128)(2,1)}, u32[]{:S(2)}, u32[]{:S(2)}) collective-permute-start(bf16[256,512]{1,0:T(8,128)(2,1)S(1)} %get-tuple-element.27), channel_id=1, source_target_pairs={{0,8},{4,12},{8,0},{12,4},{16,24},{20,28},{24,16},{28,20},{1,9},{5... | collective-permute-start | bytes 786440 | tf_op jit(solution)/shard_map/ppermute | solution.py:308
  11.8 5.8 %shard_map.135 = (bf16[256,512]{1,0:T(8,128)(2,1)S(1)}, bf16[256,512]{1,0:T(8,128)(2,1)S(1)}, bf16[256,512]{1,0:T(8,128)(2,1)S(1)}, bf16[256,512]{1,0:T(8,128)(2,1)S(1)}) custom-call(s32[1,1]{1,0:T(1,128)} %bitcast.7.place_ref, f32[1,512]{1,0:T(1,128)S(1)} %bitcast.29, bf16[512,512]{1,0:T(8,128)(2,1)S(1)} %copy-done.3, bf16[512,512]{1,0:T(8,128)(2,1)S(1)} %copy-done.4, ...), custom_call_target="tpu_custom_call" | custom-call | flops 1000 | bytes 1000 | tf_op jit(solution)/shard_map/pallas_call | solution.py:40
  17.5 1.6 %collective-permute-start.12 = (bf16[256,512]{1,0:T(8,128)(2,1)S(1)}, bf16[256,512]{1,0:T(8,128)(2,1)}, u32[]{:S(2)}, u32[]{:S(2)}) collective-permute-start(bf16[256,512]{1,0:T(8,128)(2,1)S(1)} %get-tuple-element.25), channel_id=1, source_target_pairs={{0,4},{4,0},{8,12},{12,8},{16,20},{20,16},{24,28},{28,24},{1,5},{5... | collective-permute-start | bytes 786440 | tf_op jit(solution)/shard_map/ppermute | solution.py:308
  19.7 1.6 %collective-permute-start = (bf16[1536,128]{1,0:T(8,128)(2,1)S(1)}, bf16[1536,128]{1,0:T(8,128)(2,1)S(1)}, u32[]{:S(2)}, u32[]{:S(2)}) collective-permute-start(bf16[1536,128]{1,0:T(8,128)(2,1)S(1)} %shard_map.131), channel_id=1, source_target_pairs={{0,4},{4,0},{8,12},{12,8},{16,20},{20,16},{24,28},{28,24},{1,5},{5... | collective-permute-start | bytes 1179656 | tf_op jit(solution)/shard_map/ppermute | solution.py:308
  21.3 3.1 %collective-permute-start.4 = (bf16[512,256]{1,0:T(8,128)(2,1)}, bf16[512,256]{1,0:T(8,128)(2,1)}, u32[]{:S(2)}, u32[]{:S(2)}) collective-permute-start(bf16[512,256]{1,0:T(8,128)(2,1)} %keys_ref.5), channel_id=1, source_target_pairs={{0,4},{4,8},{8,12},{12,16},{16,20},{20,24},{24,28},{1,5},{5,9},{9,... | collective-permute-start | bytes 786440 | tf_op jit(solution)/shard_map/ppermute | solution.py:297
  24.6 0.9 add_convert_fusion.1
  25.5 2.0 %collective-permute-start.19 = (bf16[128,512]{1,0:T(8,128)(2,1)S(1)}, bf16[128,512]{1,0:T(8,128)(2,1)S(1)}, u32[]{:S(2)}, u32[]{:S(2)}) collective-permute-start(bf16[128,512]{1,0:T(8,128)(2,1)S(1)} %add_convert_fusion.1), channel_id=1, source_target_pairs={{0,16},{4,20},{8,24},{12,28},{16,0},{20,4},{24,8},{28,12},{1,17},{... | collective-permute-start | bytes 393224 | tf_op jit(solution)/shard_map/ppermute | solution.py:308
  27.5 0.9 add_convert_fusion.2
  28.4 3.5 %collective-permute-start.13 = (bf16[128,512]{1,0:T(8,128)(2,1)S(1)}, bf16[128,512]{1,0:T(8,128)(2,1)S(1)}, u32[]{:S(2)}, u32[]{:S(2)}) collective-permute-start(bf16[128,512]{1,0:T(8,128)(2,1)S(1)} %add_convert_fusion.2), channel_id=1, source_target_pairs={{0,8},{4,12},{8,0},{12,4},{16,24},{20,28},{24,16},{28,20},{1,9},{5... | collective-permute-start | bytes 393224 | tf_op jit(solution)/shard_map/ppermute | solution.py:308
  32.5 5.7 %collective-permute-start.7 = (bf16[128,512]{1,0:T(8,128)(2,1)S(1)}, bf16[128,512]{1,0:T(8,128)(2,1)S(1)}, u32[]{:S(2)}, u32[]{:S(2)}) collective-permute-start(bf16[128,512]{1,0:T(8,128)(2,1)S(1)} %add_convert_fusion.3), channel_id=1, source_target_pairs={{0,8},{4,12},{8,0},{12,4},{16,24},{20,28},{24,16},{28,20},{1,9},{5... | collective-permute-start | bytes 393224 | tf_op jit(solution)/shard_map/ppermute | solution.py:308
  38.1 0.9 add_convert_fusion.5
  39.1 0.9 add_convert_fusion.7
  40.0 3.1 %collective-permute-start.14 = (bf16[64,512]{1,0:T(8,128)(2,1)S(1)}, bf16[64,512]{1,0:T(8,128)(2,1)S(1)}, u32[]{:S(2)}, u32[]{:S(2)}) collective-permute-start(bf16[64,512]{1,0:T(8,128)(2,1)S(1)} %add_convert_fusion.7), channel_id=1, source_target_pairs={{0,16},{4,20},{8,24},{12,28},{16,0},{20,4},{24,8},{28,12},{1,17},{... | collective-permute-start | bytes 196616 | tf_op jit(solution)/shard_map/ppermute | solution.py:308
  43.1 3.1 %collective-permute-start.8 = (bf16[64,512]{1,0:T(8,128)(2,1)S(1)}, bf16[64,512]{1,0:T(8,128)(2,1)S(1)}, u32[]{:S(2)}, u32[]{:S(2)}) collective-permute-start(bf16[64,512]{1,0:T(8,128)(2,1)S(1)} %add_convert_fusion.9), channel_id=1, source_target_pairs={{0,16},{4,20},{8,24},{12,28},{16,0},{20,4},{24,8},{28,12},{1,17},{... | collective-permute-start | bytes 196616 | tf_op jit(solution)/shard_map/ppermute | solution.py:308
  46.3 2.1 %collective-permute-start.1 = (bf16[1024,128]{1,0:T(8,128)(2,1)S(1)}, bf16[1024,128]{1,0:T(8,128)(2,1)S(1)}, u32[]{:S(2)}, u32[]{:S(2)}) collective-permute-start(bf16[1024,128]{1,0:T(8,128)(2,1)S(1)} %get-tuple-element.17.high_ref), channel_id=1, source_target_pairs={{0,8},{4,12},{8,16},{12,20},{16,24},{20,28},{1,9},{5,13},{9,17},{1... | collective-permute-start | bytes 786440 | tf_op jit(solution)/shard_map/ppermute | solution.py:297
  48.4 1.3 %collective-permute-start.2 = (bf16[1024,128]{1,0:T(8,128)(2,1)S(1)}, bf16[1024,128]{1,0:T(8,128)(2,1)S(1)}, u32[]{:S(2)}, u32[]{:S(2)}) collective-permute-start(bf16[1024,128]{1,0:T(8,128)(2,1)S(1)} %get-tuple-element.18.low_ref), channel_id=1, source_target_pairs={{8,0},{12,4},{16,8},{20,12},{24,16},{28,20},{9,1},{13,5},{17,9},{2... | collective-permute-start | bytes 786440 | tf_op jit(solution)/shard_map/ppermute | solution.py:297
  49.7 0.9 add_convert_fusion.4
  51.1 0.9 add_convert_fusion.6
  52.0 4.2 %collective-permute-start.15 = (bf16[64,512]{1,0:T(8,128)(2,1)S(1)}, bf16[64,512]{1,0:T(8,128)(2,1)S(1)}, u32[]{:S(2)}, u32[]{:S(2)}) collective-permute-start(bf16[64,512]{1,0:T(8,128)(2,1)S(1)} %add_convert_fusion.6), channel_id=1, source_target_pairs={{0,16},{4,20},{8,24},{12,28},{16,0},{20,4},{24,8},{28,12},{1,17},{... | collective-permute-start | bytes 196616 | tf_op jit(solution)/shard_map/ppermute | solution.py:308
  56.2 3.2 %collective-permute-start.9 = (bf16[64,512]{1,0:T(8,128)(2,1)S(1)}, bf16[64,512]{1,0:T(8,128)(2,1)S(1)}, u32[]{:S(2)}, u32[]{:S(2)}) collective-permute-start(bf16[64,512]{1,0:T(8,128)(2,1)S(1)} %add_convert_fusion.8), channel_id=1, source_target_pairs={{0,16},{4,20},{8,24},{12,28},{16,0},{20,4},{24,8},{28,12},{1,17},{... | collective-permute-start | bytes 196616 | tf_op jit(solution)/shard_map/ppermute | solution.py:308
  59.5 6.8 %collective-permute-done.15 = bf16[64,512]{1,0:T(8,128)(2,1)S(1)} collective-permute-done((bf16[64,512]{1,0:T(8,128)(2,1)S(1)}, bf16[64,512]{1,0:T(8,128)(2,1)S(1)}, u32[]{:S(2)}, u32[]{:S(2)}) %collective-permute-start.15) | collective-permute-done | bytes 65568 | tf_op jit(solution)/shard_map/ppermute | solution.py:308
  66.3 2.8 %collective-permute-done.9 = bf16[64,512]{1,0:T(8,128)(2,1)S(1)} collective-permute-done((bf16[64,512]{1,0:T(8,128)(2,1)S(1)}, bf16[64,512]{1,0:T(8,128)(2,1)S(1)}, u32[]{:S(2)}, u32[]{:S(2)}) %collective-permute-start.9) | collective-permute-done | bytes 65568 | tf_op jit(solution)/shard_map/ppermute | solution.py:308
  69.1 1.5 %collective-permute-start.5 = (bf16[512,256]{1,0:T(8,128)(2,1)}, bf16[512,256]{1,0:T(8,128)(2,1)}, u32[]{:S(2)}, u32[]{:S(2)}) collective-permute-start(bf16[512,256]{1,0:T(8,128)(2,1)} %keys_ref.5), channel_id=1, source_target_pairs={{4,0},{8,4},{12,8},{16,12},{20,16},{24,20},{28,24},{5,1},{9,5},{13... | collective-permute-start | bytes 786440 | tf_op jit(solution)/shard_map/ppermute | solution.py:297
  70.6 1.7 %collective-permute-done.22 = bf16[128,512]{1,0:T(8,128)(2,1)S(1)} collective-permute-done((bf16[128,512]{1,0:T(8,128)(2,1)S(1)}, bf16[128,512]{1,0:T(8,128)(2,1)S(1)}, u32[]{:S(2)}, u32[]{:S(2)}) %collective-permute-start.22) | collective-permute-done | bytes 131104 | tf_op jit(solution)/shard_map/ppermute | solution.py:308
  72.3 2.1 %collective-permute-start.10 = (bf16[128,512]{1,0:T(8,128)(2,1)S(1)}, bf16[128,512]{1,0:T(8,128)(2,1)S(1)}, u32[]{:S(2)}, u32[]{:S(2)}) collective-permute-start(bf16[128,512]{1,0:T(8,128)(2,1)S(1)} %pad_maximum_fusion.3), channel_id=1, source_target_pairs={{0,8},{4,12},{8,0},{12,4},{16,24},{20,28},{24,16},{28,20},{1,9},{5... | collective-permute-start | bytes 393224 | tf_op jit(solution)/shard_map/ppermute | solution.py:308
  74.5 4.0 %shard_map.133 = (bf16[512,128]{1,0:T(8,128)(2,1)S(1)}, bf16[512,128]{1,0:T(8,128)(2,1)S(1)}) custom-call(f32[2,2]{1,0:T(2,128)S(1)} %reshape.27.edge_ref, s32[1,1]{1,0:T(1,128)} %bitcast.10.side_ref, bf16[512,256]{1,0:T(8,128)(2,1)S(1)} %copy-done.13, bf16[1536,128]{1,0:T(8,128)(2,1)S(1)} %collective-permute-done.other_ref, ...), custom_call_target="tpu_custom_call" | custom-call | flops 805306368 | bytes 2097152 | tf_op jit(solution)/shard_map/pallas_call | solution.py:40
  78.5 2.0 %collective-permute-done.16 = bf16[128,512]{1,0:T(8,128)(2,1)S(1)} collective-permute-done((bf16[128,512]{1,0:T(8,128)(2,1)S(1)}, bf16[128,512]{1,0:T(8,128)(2,1)S(1)}, u32[]{:S(2)}, u32[]{:S(2)}) %collective-permute-start.16) | collective-permute-done | bytes 131104 | tf_op jit(solution)/shard_map/ppermute | solution.py:308
  80.5 1.4 %collective-permute-done.10 = bf16[128,512]{1,0:T(8,128)(2,1)S(1)} collective-permute-done((bf16[128,512]{1,0:T(8,128)(2,1)S(1)}, bf16[128,512]{1,0:T(8,128)(2,1)S(1)}, u32[]{:S(2)}, u32[]{:S(2)}) %collective-permute-start.10) | collective-permute-done | bytes 131104 | tf_op jit(solution)/shard_map/ppermute | solution.py:308
  81.8 0.7 collective-permute-start.17
  82.6 3.3 %collective-permute-done.3.other_ref = bf16[512,128]{1,0:T(8,128)(2,1)S(1)} collective-permute-done((bf16[512,128]{1,0:T(8,128)(2,1)S(1)}, bf16[512,128]{1,0:T(8,128)(2,1)S(1)}, u32[]{:S(2)}, u32[]{:S(2)}) %collective-permute-start.3) | collective-permute-done | bytes 131104 | tf_op jit(solution)/shard_map/ppermute | solution.py:308
  85.9 1.0 collective-permute-start.11
  87.5 1.3 %collective-permute-done.17.refs_3_ = bf16[256,512]{1,0:T(8,128)(2,1)} collective-permute-done((bf16[256,512]{1,0:T(8,128)(2,1)S(1)}, bf16[256,512]{1,0:T(8,128)(2,1)}, u32[]{:S(2)}, u32[]{:S(2)}) %collective-permute-start.17) | collective-permute-done | bytes 262176 | tf_op jit(solution)/shard_map/ppermute | solution.py:308
  88.8 3.6 %collective-permute-done.11.refs_1_ = bf16[256,512]{1,0:T(8,128)(2,1)} collective-permute-done((bf16[256,512]{1,0:T(8,128)(2,1)S(1)}, bf16[256,512]{1,0:T(8,128)(2,1)}, u32[]{:S(2)}, u32[]{:S(2)}) %collective-permute-start.11) | collective-permute-done | bytes 262176 | tf_op jit(solution)/shard_map/ppermute | solution.py:308
  92.4 0.9 copy-done.8
  93.3 0.9 copy-done.10
  94.3 5.5 %shard_map.137 = (bf16[3,64,512]{2,1,0:T(8,128)(2,1)}, bf16[512,512]{1,0:T(8,128)(2,1)S(1)}) custom-call(s32[1,1]{1,0:T(1,128)} %bitcast.7.place_ref, bf16[3,512,512]{2,1,0:T(8,128)(2,1)S(1)} %bitcast.26, bf16[512,512]{1,0:T(8,128)(2,1)S(1)} %shard_map.134.query_ref, bf16[256,512]{1,0:T(8,128)(2,1)S(1)} %copy-done.10, ...), custom_call_target="tpu_custom_call" | custom-call | flops 1000 | bytes 1000 | tf_op jit(solution)/shard_map/pallas_call | solution.py:40
  99.8 1.0 shard_map.139
  100.9 2.9 %collective-permute-start.26 = (bf16[512,256]{1,0:T(8,128)(2,1)S(1)}, bf16[512,256]{1,0:T(8,128)(2,1)S(1)}, u32[]{:S(2)}, u32[]{:S(2)}) collective-permute-start(bf16[512,256]{1,0:T(8,128)(2,1)S(1)} %copy-done.12), channel_id=1, source_target_pairs={{0,4},{4,8},{8,12},{12,16},{16,20},{20,24},{24,28},{1,5},{5,9},{9,... | collective-permute-start | bytes 786440 | tf_op jit(solution)/shard_map/ppermute | solution.py:297
  103.8 1.3 %collective-permute-start.27 = (bf16[512,256]{1,0:T(8,128)(2,1)S(1)}, bf16[512,256]{1,0:T(8,128)(2,1)S(1)}, u32[]{:S(2)}, u32[]{:S(2)}) collective-permute-start(bf16[512,256]{1,0:T(8,128)(2,1)S(1)} %copy-done.12), channel_id=1, source_target_pairs={{4,0},{8,4},{12,8},{16,12},{20,16},{24,20},{28,24},{5,1},{9,5},{13... | collective-permute-start | bytes 786440 | tf_op jit(solution)/shard_map/ppermute | solution.py:297
  105.1 1.0 shard_map.138.keep_ref
  106.2 1.6 %collective-permute-start.25 = (bf16[512,256]{1,0:T(8,128)(2,1)S(1)}, bf16[512,256]{1,0:T(8,128)(2,1)S(1)}, u32[]{:S(2)}, u32[]{:S(2)}) collective-permute-start(bf16[512,256]{1,0:T(8,128)(2,1)S(1)} %fusion), channel_id=1, source_target_pairs={{0,2},{1,3},{2,0},{3,1},{4,6},{5,7},{6,4},{7,5},{8,10},{9,11},{10,... | collective-permute-start | bytes 786440 | tf_op jit(solution)/shard_map/ppermute | solution.py:303
  107.8 7.8 %collective-permute-done.26.values_prev_ref = bf16[512,256]{1,0:T(8,128)(2,1)S(1)} collective-permute-done((bf16[512,256]{1,0:T(8,128)(2,1)S(1)}, bf16[512,256]{1,0:T(8,128)(2,1)S(1)}, u32[]{:S(2)}, u32[]{:S(2)}) %collective-permute-start.26) | collective-permute-done | bytes 262176 | tf_op jit(solution)/shard_map/ppermute | solution.py:297
  115.5 5.4 %shard_map.140 = bf16[512,256]{1,0:T(8,128)(2,1)} custom-call(f32[2,2]{1,0:T(2,128)S(1)} %reshape.27.edge_ref, bf16[512,256]{1,0:T(8,128)(2,1)S(1)} %copy-done.11, bf16[2,512,256]{2,1,0:T(8,128)(2,1)S(1)} %shard_map.138.keep_ref, bf16[2,512,256]{2,1,0:T(8,128)(2,1)S(1)} %collective-permute-done.24.near_ref, ...), custom_call_target="tpu_custom_call" | custom-call | flops 805306368 | bytes 2097152 | tf_op jit(solution)/shard_map/pallas_call | solution.py:40
  (70 shorter events, 3.0 us)
Async XLA Ops:
  0.6 1.4 %copy-start = (bf16[1,512,3,512]{3,1,2,0:T(8,128)(2,1)S(1)}, bf16[1,512,3,512]{3,1,2,0:T(8,128)(2,1)}, u32[]{:S(2)}) copy-start(bf16[1,512,3,512]{3,1,2,0:T(8,128)(2,1)} %param.19) | copy-start | bytes 4718596
  2.0 1.0 copy-start.3
  3.1 1.0 copy-start.4
  4.1 0.7 copy-start.15
  8.6 11.0 %copy-start.5 = (bf16[512,256]{1,0:T(8,128)(2,1)S(1)}, bf16[512,256]{1,0:T(8,128)(2,1)}, u32[]{:S(2)}) copy-start(bf16[512,256]{1,0:T(8,128)(2,1)} %keys_ref.4) | copy-start | bytes 786436
  8.6 11.0 %copy-start.6 = (bf16[512,256]{1,0:T(8,128)(2,1)S(1)}, bf16[512,256]{1,0:T(8,128)(2,1)}, u32[]{:S(2)}) copy-start(bf16[512,256]{1,0:T(8,128)(2,1)} %values_ref.4) | copy-start | bytes 786436
  8.7 11.0 %copy-start.13 = (bf16[512,256]{1,0:T(8,128)(2,1)S(1)}, bf16[512,256]{1,0:T(8,128)(2,1)}, u32[]{:S(2)}) copy-start(bf16[512,256]{1,0:T(8,128)(2,1)} %queries_ref.4) | copy-start | bytes 786436
  8.7 15.9 %collective-permute-start.18 = (bf16[256,512]{1,0:T(8,128)(2,1)S(1)}, bf16[256,512]{1,0:T(8,128)(2,1)}, u32[]{:S(2)}, u32[]{:S(2)}) collective-permute-start(bf16[256,512]{1,0:T(8,128)(2,1)S(1)} %get-tuple-element.27), channel_id=1, source_target_pairs={{0,8},{4,12},{8,0},{12,4},{16,24},{20,28},{24,16},{28,20},{1,9},{5... | collective-permute-start | bytes 786440 | tf_op jit(solution)/shard_map/ppermute | solution.py:308
  17.5 10.0 %collective-permute-start.12 = (bf16[256,512]{1,0:T(8,128)(2,1)S(1)}, bf16[256,512]{1,0:T(8,128)(2,1)}, u32[]{:S(2)}, u32[]{:S(2)}) collective-permute-start(bf16[256,512]{1,0:T(8,128)(2,1)S(1)} %get-tuple-element.25), channel_id=1, source_target_pairs={{0,4},{4,0},{8,12},{12,8},{16,20},{20,16},{24,28},{28,24},{1,5},{5... | collective-permute-start | bytes 786440 | tf_op jit(solution)/shard_map/ppermute | solution.py:308
  19.1 13.3 %collective-permute-start.6 = (bf16[256,512]{1,0:T(8,128)(2,1)S(1)}, bf16[256,512]{1,0:T(8,128)(2,1)S(1)}, u32[]{:S(2)}, u32[]{:S(2)}) collective-permute-start(bf16[256,512]{1,0:T(8,128)(2,1)S(1)} %get-tuple-element.23), channel_id=1, source_target_pairs={{0,4},{4,0},{8,12},{12,8},{16,20},{20,16},{24,28},{28,24},{1,5},{5... | collective-permute-start | bytes 786440 | tf_op jit(solution)/shard_map/ppermute | solution.py:308
  19.7 26.5 %collective-permute-start = (bf16[1536,128]{1,0:T(8,128)(2,1)S(1)}, bf16[1536,128]{1,0:T(8,128)(2,1)S(1)}, u32[]{:S(2)}, u32[]{:S(2)}) collective-permute-start(bf16[1536,128]{1,0:T(8,128)(2,1)S(1)} %shard_map.131), channel_id=1, source_target_pairs={{0,4},{4,0},{8,12},{12,8},{16,20},{20,16},{24,28},{28,24},{1,5},{5... | collective-permute-start | bytes 1179656 | tf_op jit(solution)/shard_map/ppermute | solution.py:308
  21.3 66.2 %collective-permute-start.4 = (bf16[512,256]{1,0:T(8,128)(2,1)}, bf16[512,256]{1,0:T(8,128)(2,1)}, u32[]{:S(2)}, u32[]{:S(2)}) collective-permute-start(bf16[512,256]{1,0:T(8,128)(2,1)} %keys_ref.5), channel_id=1, source_target_pairs={{0,4},{4,8},{8,12},{12,16},{16,20},{20,24},{24,28},{1,5},{5,9},{9,... | collective-permute-start | bytes 786440 | tf_op jit(solution)/shard_map/ppermute | solution.py:297
  25.5 12.6 %collective-permute-start.19 = (bf16[128,512]{1,0:T(8,128)(2,1)S(1)}, bf16[128,512]{1,0:T(8,128)(2,1)S(1)}, u32[]{:S(2)}, u32[]{:S(2)}) collective-permute-start(bf16[128,512]{1,0:T(8,128)(2,1)S(1)} %add_convert_fusion.1), channel_id=1, source_target_pairs={{0,16},{4,20},{8,24},{12,28},{16,0},{20,4},{24,8},{28,12},{1,17},{... | collective-permute-start | bytes 393224 | tf_op jit(solution)/shard_map/ppermute | solution.py:308
  28.4 10.7 %collective-permute-start.13 = (bf16[128,512]{1,0:T(8,128)(2,1)S(1)}, bf16[128,512]{1,0:T(8,128)(2,1)S(1)}, u32[]{:S(2)}, u32[]{:S(2)}) collective-permute-start(bf16[128,512]{1,0:T(8,128)(2,1)S(1)} %add_convert_fusion.2), channel_id=1, source_target_pairs={{0,8},{4,12},{8,0},{12,4},{16,24},{20,28},{24,16},{28,20},{1,9},{5... | collective-permute-start | bytes 393224 | tf_op jit(solution)/shard_map/ppermute | solution.py:308
  32.5 10.6 %collective-permute-start.7 = (bf16[128,512]{1,0:T(8,128)(2,1)S(1)}, bf16[128,512]{1,0:T(8,128)(2,1)S(1)}, u32[]{:S(2)}, u32[]{:S(2)}) collective-permute-start(bf16[128,512]{1,0:T(8,128)(2,1)S(1)} %add_convert_fusion.3), channel_id=1, source_target_pairs={{0,8},{4,12},{8,0},{12,4},{16,24},{20,28},{24,16},{28,20},{1,9},{5... | collective-permute-start | bytes 393224 | tf_op jit(solution)/shard_map/ppermute | solution.py:308
  39.0 9.4 %collective-permute-start.20 = (bf16[64,512]{1,0:T(8,128)(2,1)S(1)}, bf16[64,512]{1,0:T(8,128)(2,1)S(1)}, u32[]{:S(2)}, u32[]{:S(2)}) collective-permute-start(bf16[64,512]{1,0:T(8,128)(2,1)S(1)} %add_convert_fusion.5), channel_id=1, source_target_pairs={{0,4},{4,0},{8,12},{12,8},{16,20},{20,16},{24,28},{28,24},{1,5},{5... | collective-permute-start | bytes 196616 | tf_op jit(solution)/shard_map/ppermute | solution.py:308
  40.0 10.6 %collective-permute-start.14 = (bf16[64,512]{1,0:T(8,128)(2,1)S(1)}, bf16[64,512]{1,0:T(8,128)(2,1)S(1)}, u32[]{:S(2)}, u32[]{:S(2)}) collective-permute-start(bf16[64,512]{1,0:T(8,128)(2,1)S(1)} %add_convert_fusion.7), channel_id=1, source_target_pairs={{0,16},{4,20},{8,24},{12,28},{16,0},{20,4},{24,8},{28,12},{1,17},{... | collective-permute-start | bytes 196616 | tf_op jit(solution)/shard_map/ppermute | solution.py:308
  43.1 8.8 %collective-permute-start.8 = (bf16[64,512]{1,0:T(8,128)(2,1)S(1)}, bf16[64,512]{1,0:T(8,128)(2,1)S(1)}, u32[]{:S(2)}, u32[]{:S(2)}) collective-permute-start(bf16[64,512]{1,0:T(8,128)(2,1)S(1)} %add_convert_fusion.9), channel_id=1, source_target_pairs={{0,16},{4,20},{8,24},{12,28},{16,0},{20,4},{24,8},{28,12},{1,17},{... | collective-permute-start | bytes 196616 | tf_op jit(solution)/shard_map/ppermute | solution.py:308
  46.3 26.0 %collective-permute-start.1 = (bf16[1024,128]{1,0:T(8,128)(2,1)S(1)}, bf16[1024,128]{1,0:T(8,128)(2,1)S(1)}, u32[]{:S(2)}, u32[]{:S(2)}) collective-permute-start(bf16[1024,128]{1,0:T(8,128)(2,1)S(1)} %get-tuple-element.17.high_ref), channel_id=1, source_target_pairs={{0,8},{4,12},{8,16},{12,20},{16,24},{20,28},{1,9},{5,13},{9,17},{1... | collective-permute-start | bytes 786440 | tf_op jit(solution)/shard_map/ppermute | solution.py:297
  48.4 26.0 %collective-permute-start.2 = (bf16[1024,128]{1,0:T(8,128)(2,1)S(1)}, bf16[1024,128]{1,0:T(8,128)(2,1)S(1)}, u32[]{:S(2)}, u32[]{:S(2)}) collective-permute-start(bf16[1024,128]{1,0:T(8,128)(2,1)S(1)} %get-tuple-element.18.low_ref), channel_id=1, source_target_pairs={{8,0},{12,4},{16,8},{20,12},{24,16},{28,20},{9,1},{13,5},{17,9},{2... | collective-permute-start | bytes 786440 | tf_op jit(solution)/shard_map/ppermute | solution.py:297
  50.6 5.6 %collective-permute-start.21 = (bf16[64,512]{1,0:T(8,128)(2,1)S(1)}, bf16[64,512]{1,0:T(8,128)(2,1)S(1)}, u32[]{:S(2)}, u32[]{:S(2)}) collective-permute-start(bf16[64,512]{1,0:T(8,128)(2,1)S(1)} %add_convert_fusion.4), channel_id=1, source_target_pairs={{0,4},{4,0},{8,12},{12,8},{16,20},{20,16},{24,28},{28,24},{1,5},{5... | collective-permute-start | bytes 196616 | tf_op jit(solution)/shard_map/ppermute | solution.py:308
  52.0 14.3 %collective-permute-start.15 = (bf16[64,512]{1,0:T(8,128)(2,1)S(1)}, bf16[64,512]{1,0:T(8,128)(2,1)S(1)}, u32[]{:S(2)}, u32[]{:S(2)}) collective-permute-start(bf16[64,512]{1,0:T(8,128)(2,1)S(1)} %add_convert_fusion.6), channel_id=1, source_target_pairs={{0,16},{4,20},{8,24},{12,28},{16,0},{20,4},{24,8},{28,12},{1,17},{... | collective-permute-start | bytes 196616 | tf_op jit(solution)/shard_map/ppermute | solution.py:308
  56.2 12.9 %collective-permute-start.9 = (bf16[64,512]{1,0:T(8,128)(2,1)S(1)}, bf16[64,512]{1,0:T(8,128)(2,1)S(1)}, u32[]{:S(2)}, u32[]{:S(2)}) collective-permute-start(bf16[64,512]{1,0:T(8,128)(2,1)S(1)} %add_convert_fusion.8), channel_id=1, source_target_pairs={{0,16},{4,20},{8,24},{12,28},{16,0},{20,4},{24,8},{28,12},{1,17},{... | collective-permute-start | bytes 196616 | tf_op jit(solution)/shard_map/ppermute | solution.py:308
  66.3 6.0 %collective-permute-start.22 = (bf16[128,512]{1,0:T(8,128)(2,1)S(1)}, bf16[128,512]{1,0:T(8,128)(2,1)S(1)}, u32[]{:S(2)}, u32[]{:S(2)}) collective-permute-start(bf16[128,512]{1,0:T(8,128)(2,1)S(1)} %pad_maximum_fusion.5), channel_id=1, source_target_pairs={{0,16},{4,20},{8,24},{12,28},{16,0},{20,4},{24,8},{28,12},{1,17},{... | collective-permute-start | bytes 393224 | tf_op jit(solution)/shard_map/ppermute | solution.py:308
  69.1 18.4 %collective-permute-start.5 = (bf16[512,256]{1,0:T(8,128)(2,1)}, bf16[512,256]{1,0:T(8,128)(2,1)}, u32[]{:S(2)}, u32[]{:S(2)}) collective-permute-start(bf16[512,256]{1,0:T(8,128)(2,1)} %keys_ref.5), channel_id=1, source_target_pairs={{4,0},{8,4},{12,8},{16,12},{20,16},{24,20},{28,24},{5,1},{9,5},{13... | collective-permute-start | bytes 786440 | tf_op jit(solution)/shard_map/ppermute | solution.py:297
  72.2 8.2 %collective-permute-start.16 = (bf16[128,512]{1,0:T(8,128)(2,1)S(1)}, bf16[128,512]{1,0:T(8,128)(2,1)S(1)}, u32[]{:S(2)}, u32[]{:S(2)}) collective-permute-start(bf16[128,512]{1,0:T(8,128)(2,1)S(1)} %pad_maximum_fusion.4), channel_id=1, source_target_pairs={{0,8},{4,12},{8,0},{12,4},{16,24},{20,28},{24,16},{28,20},{1,9},{5... | collective-permute-start | bytes 393224 | tf_op jit(solution)/shard_map/ppermute | solution.py:308
  72.3 14.7 %copy-start.14 = (bf16[1,256,512]{2,1,0:T(8,128)(2,1)S(1)}, bf16[1,256,512]{2,1,0:T(8,128)(2,1)}, u32[]{:S(2)}) copy-start(bf16[1,256,512]{2,1,0:T(8,128)(2,1)} %param.15) | copy-start | bytes 786436
  72.3 9.6 %collective-permute-start.10 = (bf16[128,512]{1,0:T(8,128)(2,1)S(1)}, bf16[128,512]{1,0:T(8,128)(2,1)S(1)}, u32[]{:S(2)}, u32[]{:S(2)}) collective-permute-start(bf16[128,512]{1,0:T(8,128)(2,1)S(1)} %pad_maximum_fusion.3), channel_id=1, source_target_pairs={{0,8},{4,12},{8,0},{12,4},{16,24},{20,28},{24,16},{28,20},{1,9},{5... | collective-permute-start | bytes 393224 | tf_op jit(solution)/shard_map/ppermute | solution.py:308
  74.4 13.1 %collective-permute-start.23 = (bf16[256,512]{1,0:T(8,128)(2,1)S(1)}, bf16[256,512]{1,0:T(8,128)(2,1)}, u32[]{:S(2)}, u32[]{:S(2)}) collective-permute-start(bf16[256,512]{1,0:T(8,128)(2,1)S(1)} %pad_maximum_fusion.2.refs_4_), channel_id=1, source_target_pairs={{0,8},{4,12},{8,0},{12,4},{16,24},{20,28},{24,16},{28,20},{1,9},{5... | collective-permute-start | bytes 786440 | tf_op jit(solution)/shard_map/ppermute | solution.py:308
  78.4 13.9 %copy-start.1 = (bf16[1,512,3,512]{3,1,2,0:T(8,128)(2,1)S(1)}, bf16[1,512,3,512]{3,1,2,0:T(8,128)(2,1)}, u32[]{:S(2)}) copy-start(bf16[1,512,3,512]{3,1,2,0:T(8,128)(2,1)} %param.19) | copy-start | bytes 4718596
  80.4 5.5 %collective-permute-start.3 = (bf16[512,128]{1,0:T(8,128)(2,1)S(1)}, bf16[512,128]{1,0:T(8,128)(2,1)S(1)}, u32[]{:S(2)}, u32[]{:S(2)}) collective-permute-start(bf16[512,128]{1,0:T(8,128)(2,1)S(1)} %get-tuple-element.20), channel_id=1, source_target_pairs={{0,4},{4,0},{8,12},{12,8},{16,20},{20,16},{24,28},{28,24},{1,5},{5... | collective-permute-start | bytes 393224 | tf_op jit(solution)/shard_map/ppermute | solution.py:308
  80.5 8.4 %copy-start.7 = (bf16[256,512]{1,0:T(8,128)(2,1)}, bf16[256,512]{1,0:T(8,128)(2,1)S(1)}, u32[]{:S(2)}) copy-start(bf16[256,512]{1,0:T(8,128)(2,1)S(1)} %pad_maximum_fusion.1.refs_2_) | copy-start | bytes 786436
  81.8 7.0 %collective-permute-start.17 = (bf16[256,512]{1,0:T(8,128)(2,1)S(1)}, bf16[256,512]{1,0:T(8,128)(2,1)}, u32[]{:S(2)}, u32[]{:S(2)}) collective-permute-start(bf16[256,512]{1,0:T(8,128)(2,1)S(1)} %pad_maximum_fusion.1.refs_2_), channel_id=1, source_target_pairs={{0,4},{4,0},{8,12},{12,8},{16,20},{20,16},{24,28},{28,24},{1,5},{5... | collective-permute-start | bytes 786440 | tf_op jit(solution)/shard_map/ppermute | solution.py:308
  82.6 6.2 %copy-start.9 = (bf16[256,512]{1,0:T(8,128)(2,1)}, bf16[256,512]{1,0:T(8,128)(2,1)S(1)}, u32[]{:S(2)}) copy-start(bf16[256,512]{1,0:T(8,128)(2,1)S(1)} %pad_maximum_fusion.refs_0_) | copy-start | bytes 786436
  85.9 6.5 %collective-permute-start.11 = (bf16[256,512]{1,0:T(8,128)(2,1)S(1)}, bf16[256,512]{1,0:T(8,128)(2,1)}, u32[]{:S(2)}, u32[]{:S(2)}) collective-permute-start(bf16[256,512]{1,0:T(8,128)(2,1)S(1)} %pad_maximum_fusion.refs_0_), channel_id=1, source_target_pairs={{0,4},{4,0},{8,12},{12,8},{16,20},{20,16},{24,28},{28,24},{1,5},{5... | collective-permute-start | bytes 786440 | tf_op jit(solution)/shard_map/ppermute | solution.py:308
  87.4 12.3 %copy-start.2 = (bf16[512,1024]{1,0:T(8,128)(2,1)S(1)}, bf16[512,1024]{1,0:T(8,128)(2,1)}, u32[]{:S(2)}) copy-start(bf16[512,1024]{1,0:T(8,128)(2,1)} %map_ref.3) | copy-start | bytes 3145732
  92.4 1.0 copy-start.8
  93.3 0.9 copy-start.10
  99.8 1.1 copy-start.12
  100.8 14.8 %copy-start.11 = (bf16[512,256]{1,0:T(8,128)(2,1)S(1)}, bf16[512,256]{1,0:T(8,128)(2,1)}, u32[]{:S(2)}) copy-start(bf16[512,256]{1,0:T(8,128)(2,1)} %queries_ref.5) | copy-start | bytes 786436
  100.8 5.3 %collective-permute-start.24 = (bf16[2,512,256]{2,1,0:T(8,128)(2,1)S(1)}, bf16[2,512,256]{2,1,0:T(8,128)(2,1)S(1)}, u32[]{:S(2)}, u32[]{:S(2)}) collective-permute-start(bf16[2,512,256]{2,1,0:T(8,128)(2,1)S(1)} %shard_map.139), channel_id=1, source_target_pairs={{0,1},{1,0},{2,3},{3,2},{4,5},{5,4},{6,7},{7,6},{8,9},{9,8},{10,11... | collective-permute-start | bytes 1572872 | tf_op jit(solution)/shard_map/ppermute | solution.py:303
  100.9 14.7 %collective-permute-start.26 = (bf16[512,256]{1,0:T(8,128)(2,1)S(1)}, bf16[512,256]{1,0:T(8,128)(2,1)S(1)}, u32[]{:S(2)}, u32[]{:S(2)}) collective-permute-start(bf16[512,256]{1,0:T(8,128)(2,1)S(1)} %copy-done.12), channel_id=1, source_target_pairs={{0,4},{4,8},{8,12},{12,16},{16,20},{20,24},{24,28},{1,5},{5,9},{9,... | collective-permute-start | bytes 786440 | tf_op jit(solution)/shard_map/ppermute | solution.py:297
  103.8 11.7 %collective-permute-start.27 = (bf16[512,256]{1,0:T(8,128)(2,1)S(1)}, bf16[512,256]{1,0:T(8,128)(2,1)S(1)}, u32[]{:S(2)}, u32[]{:S(2)}) collective-permute-start(bf16[512,256]{1,0:T(8,128)(2,1)S(1)} %copy-done.12), channel_id=1, source_target_pairs={{4,0},{8,4},{12,8},{16,12},{20,16},{24,20},{28,24},{5,1},{9,5},{13... | collective-permute-start | bytes 786440 | tf_op jit(solution)/shard_map/ppermute | solution.py:297
  106.2 9.3 %collective-permute-start.25 = (bf16[512,256]{1,0:T(8,128)(2,1)S(1)}, bf16[512,256]{1,0:T(8,128)(2,1)S(1)}, u32[]{:S(2)}, u32[]{:S(2)}) collective-permute-start(bf16[512,256]{1,0:T(8,128)(2,1)S(1)} %fusion), channel_id=1, source_target_pairs={{0,2},{1,3},{2,0},{3,1},{4,6},{5,7},{6,4},{7,5},{8,10},{9,11},{10,... | collective-permute-start | bytes 786440 | tf_op jit(solution)/shard_map/ppermute | solution.py:303

commit v4 on v3

--- a/solution.py
+++ b/solution.py
@@ -48,73 +48,54 @@
     )(*operands)
 
 
-def block_at(slot, order):
-    block = 0
-    for place, bit in enumerate(reversed(order)):
-        block |= ((slot >> place) & 1) << bit
-    return block
-
-
-def load_rows(order, place, source, target, sems, first):
-    block_rows = target.shape[0] >> len(order)
-    copies = []
-    for slot in range(1 << len(order)):
-        block = (block_at(slot, order) ^ place) if order else 0
-        start = pl.multiple_of(block * block_rows, block_rows)
-        copies.append(
-            pltpu.make_async_copy(
-                source.at[pl.ds(start, block_rows), :],
-                target.at[pl.ds(slot * block_rows, block_rows), :],
-                sems.at[first + slot],
-            )
-        )
-    for copy in copies:
-        copy.start()
-    return copies
-
-
-def gradient_kernel(order, down, place_ref, rates_ref, keys_hbm, values_hbm, weights_hbm, *refs):
-    out_refs, (keys_ref, values_ref, weights_ref, sems) = refs[:-4], refs[-4:]
+def slot_of(block, order):
+    slot = 0
+    for bit in order:
+        slot = slot * 2 + ((block >> bit) & 1)
+    return slot
+
+
+def gradient_kernel(orders, place_ref, rates_ref, keys_ref, values_ref, weights_ref, *refs):
+    out_refs, chunk_refs = refs[:-2], refs[-2:]
     place = place_ref[0, 0]
-    slots = 1 << len(order)
-    matrices = weights_ref.shape[0]
-    hidden_size = weights_ref.shape[1]
-    keys_copy = pltpu.make_async_copy(keys_hbm, keys_ref, sems.at[matrices * slots])
-    keys_copy.start()
-    copies = [keys_copy]
-    for matrix in range(matrices):
-        copies += load_rows(
-            order, place, weights_hbm.at[matrix], weights_ref.at[matrix], sems, matrix * slots
-        )
-    values_copy = pltpu.make_async_copy(values_hbm, values_ref, sems.at[matrices * slots + 1])
-    values_copy.start()
-    for copy in copies + [values_copy]:
-        copy.wait()
     rates = rates_ref[...]
     keys = keys_ref[...]
     values = values_ref[...]
+    hidden_size, width = weights_ref.shape[1:]
     step = 128
-    halves = 2 if order else 1
-    half_rows = hidden_size // halves
+
+    def put(chunk, low, columns, product):
+        order = orders[chunk]
+        block_rows = min(step, hidden_size >> len(order))
+        for start in range(0, step, block_rows):
+            row = low + start
+            if order:
+                slot = slot_of((row // block_rows) ^ place, order)
+                row = pl.multiple_of(slot * block_rows, block_rows)
+            chunk_refs[chunk][pl.ds(row, block_rows), columns] = product[start:start + block_rows]
+
     for low in range(0, hidden_size, step):
         rows = slice(low, low + step)
-        half, start = low // half_rows, low % half_rows
-        target = slice(start, start + step)
         gate = dot_nt(weights_ref[0, rows, :], keys) * INVERSE
         up = dot_nt(weights_ref[1, rows, :], keys) * INVERSE
         sigmoid = jax.nn.sigmoid(gate)
         silu = gate * sigmoid
-        if down:
-            hidden = (rates * silu * up).astype(BF16)
-            out_refs[half][target, :] = dot_nn(hidden, values).astype(BF16)
-            continue
+        hidden = (rates * silu * up).astype(BF16)
         backward = rates * dot_nt(weights_ref[2, rows, :], values)
         d_gate = (
             backward * up * sigmoid * (1.0 + gate * (1.0 - sigmoid)) * INVERSE
         ).astype(BF16)
         d_up = (backward * silu * INVERSE).astype(BF16)
-        out_refs[half][target, :] = dot_nn(d_gate, keys).astype(BF16)
-        out_refs[halves + half][target, :] = dot_nn(d_up, keys).astype(BF16)
+        up_part = dot_nn(d_up, keys).astype(BF16)
+        put(0, low, slice(0, width), dot_nn(d_gate, keys).astype(BF16))
+        put(0, low, slice(width, width + width // 2), up_part[:, :width // 2])
+        put(1, low, slice(0, width), dot_nn(hidden, values).astype(BF16))
+        put(1, low, slice(width, width + width // 2), up_part[:, width // 2:])
+    halves = len(out_refs) // 2
+    half_rows = hidden_size // halves
+    for index, out_ref in enumerate(out_refs):
+        half = index % halves
+        out_ref[...] = chunk_refs[index // halves][half * half_rows:(half + 1) * half_rows, :]
 
 
 def attend_rows(edge_prev, edge_next, query_tile, keys_prev, keys_own, keys_next,
@@ -243,34 +224,45 @@
 def renew_kernel(orders, place_ref, weights_ref, query_ref, *refs):
     pieces, (own_ref, fast_ref, new_ref) = refs[:-3], refs[-3:]
     place = place_ref[0, 0]
+    hidden_size, width = weights_ref.shape[1:]
     limit_norm = math.sqrt(FAST_HIDDEN * FAST_DIM) / 2.0
-    square = jnp.zeros((1, weights_ref.shape[2]), F32)
     step = 64
+    square = jnp.zeros((1, pieces[0].shape[1]), F32)
     for piece in pieces:
         for low in range(0, piece.shape[0], step):
             part = piece[low:low + step, :].astype(F32)
             square = square + jnp.sum(part * part, axis=0, keepdims=True)
     square = jnp.sum(square, axis=1, keepdims=True)
     factor = jnp.minimum(1.0, limit_norm * lax.rsqrt(square + 1e-06))
-    per_matrix = len(pieces) // 3
-    for matrix, order in enumerate(orders):
-        block_rows = weights_ref.shape[1] >> len(order)
-        slots = 1 << len(order)
-        for slot in range(slots):
-            piece = pieces[matrix * per_matrix + slot * per_matrix // slots]
-            inside = slot % (slots // per_matrix)
-            block = block_at(slot, order) ^ place if order else 0
-            for low in range(0, block_rows, step):
-                count = min(step, block_rows)
-                rows = pl.ds(pl.multiple_of(block * block_rows + low, count), count)
+    per_chunk = len(pieces) // 2
+    piece_rows = pieces[0].shape[0]
+    blocks = 1 << len(orders[0])
+    block_rows = hidden_size // blocks
+    count = min(step, block_rows)
+    for block in range(blocks):
+        starts = [slot_of(block, order) * block_rows for order in orders]
+        for low in range(0, block_rows, count):
+            found = []
+            for chunk, start in enumerate(starts):
+                piece = pieces[chunk * per_chunk + start // piece_rows]
+                inside = start % piece_rows + low
+                found.append(piece[inside:inside + count, :].astype(F32))
+            parts = [
+                found[0][:, :width],
+                jnp.concatenate([found[0][:, width:], found[1][:, width:]], axis=1),
+                found[1][:, :width],
+            ]
+            rows = slice(low, low + count)
+            if blocks > 1:
+                rows = pl.ds(pl.multiple_of((block ^ place) * block_rows + low, count), count)
+            for matrix, part in enumerate(parts):
                 old = weights_ref[matrix, rows, :].astype(F32)
-                part = piece[inside * block_rows + low:inside * block_rows + low + count, :]
-                stepped = old + factor * part.astype(F32)
+                stepped = old + factor * part
                 norm = jnp.sqrt(jnp.sum(old * old, axis=1, keepdims=True))
                 size = jnp.sum(stepped * stepped, axis=1, keepdims=True)
                 fresh = (stepped * norm * lax.rsqrt(size + 1e-06)).astype(BF16)
                 new_ref[matrix, rows, :] = fresh
-                if slot == 0:
+                if block == 0:
                     own_ref[matrix, low:low + count, :] = fresh
     step = 128
     for low in range(0, query_ref.shape[0], step):
@@ -369,33 +361,20 @@
 
     bits = tuple(range(seq_count.bit_length() - 1))
     halving = seq_count == 1 << len(bits) and len(bits) > 1 and hidden_size >> len(bits) >= 16
-    order, down_order = (bits, bits[1:] + bits[:1]) if halving else ((), ())
-    orders = (order, order, down_order)
+    orders = (bits, bits[1:] + bits[:1]) if halving else ((), ())
     halves = 2 if halving else 1
-
-    def gradient_of(order, down):
-        matrices, chunks = (2, 1) if down else (3, 2)
-        return call(
-            functools.partial(gradient_kernel, order, down),
-            [shape((hidden_size // halves, fast_width), BF16)] * (halves * chunks),
-            (place, step_rates.reshape(1, rows), fast_keys, fast_values, weights),
-            scalars=1,
-            anywhere=3,
-            scratch=[
-                pltpu.VMEM(fast_keys.shape, BF16),
-                pltpu.VMEM(fast_values.shape, BF16),
-                pltpu.VMEM((matrices, hidden_size, fast_width), BF16),
-                pltpu.SemaphoreType.DMA((matrices * (1 << len(order)) + 2,)),
-            ],
-        )
-
-    down_halves = gradient_of(down_order, True)
-    gate_up_halves = gradient_of(order, False)
-    halves_of = [gate_up_halves[:halves], gate_up_halves[halves:], down_halves]
+    chunk_width = fast_width + fast_width // 2
+    gradients = call(
+        functools.partial(gradient_kernel, orders),
+        [shape((hidden_size // halves, chunk_width), BF16)] * (2 * halves),
+        (place, step_rates.reshape(1, rows), fast_keys, fast_values, weights),
+        scalars=1,
+        scratch=[pltpu.VMEM((hidden_size, chunk_width), BF16)] * 2,
+    )
     if halving:
-        gathered = sum_over_seq(halves_of, orders)
+        gathered = sum_over_seq([gradients[:2], gradients[2:]], orders)
     else:
-        gathered = lax.psum([part for (part,) in halves_of], "seq")
+        gathered = lax.psum(gradients, "seq")
 
     low_block, high_block = call(
         border_kernel,

time: 122 us -> 114 us (0.934)
  the two profiles are of different devices: /device:TPU:0 before, /device:TPU:25 now
where the time goes in v4:
time: 114 us
  waiting for transfers between devices  41.4 us (36%)
  starting transfers between devices  34 us (30%)
  Pallas kernels  23 us (20%)
  local copies, waits for them, and re-layouts  8.1 us (7%)
  other arithmetic  6.09 us (5%)
    ppermute x14, waiting for transfers between devices, seq_swap(): lax.ppermute(value, 'seq', [(i, i ^ step) for i in range(lax.axis_size('s...  32.4 us
    pallas_call x9, Pallas kernels, call(): pl.pallas_call(body, out_shape=out_shapes, in_specs=in_specs, out_specs=j...  23 us
    ppermute x6, starting transfers between devices, seq_shift(): lax.ppermute(value, 'seq', [(i, i + step) for i in range(peers) if 0 <= i...  18.7 us
    ppermute x14, starting transfers between devices, seq_swap(): lax.ppermute(value, 'seq', [(i, i ^ step) for i in range(lax.axis_size('s...  13.5 us
    ppermute x6, waiting for transfers between devices, seq_shift(): lax.ppermute(value, 'seq', [(i, i + step) for i in range(peers) if 0 <= i...  9.04 us
    unnamed x36, local copies, waits for them, and re-layouts  8.02 us
    convert_element_type x4, other arithmetic, sum_over_seq(): total = sum((part[half:].astype(F32) for part in keeps[index])).astype(BF16)  3.81 us
  transfers between devices with their start and end apart: 22, of which 10 were waited for; matrix products, arithmetic and copies ran while one was open for 5% of the time, Pallas kernels for 7%

profile of v4, /device:TPU:25, one launch (start us, length us, event | category | flops | bytes accessed | tf_op | source)
XLA Modules:
  0.0 113.6 jit_solution(3297210232141571058)
XLA Ops:
  0.6 1.4 %copy-done = bf16[1,512,3,512]{3,1,2,0:T(8,128)(2,1)S(1)} copy-done((bf16[1,512,3,512]{3,1,2,0:T(8,128)(2,1)S(1)}, bf16[1,512,3,512]{3,1,2,0:T(8,128)(2,1)}, u32[]{:S(2)}) %copy-start) | copy-done | bytes 1572888
  2.1 1.0 copy-done.7
  3.1 1.0 copy-done.8
  4.1 0.7 copy-done.13
  4.8 3.7 %shard_map.135 = (bf16[256,768]{1,0:T(8,128)(2,1)S(1)}, bf16[256,768]{1,0:T(8,128)(2,1)S(1)}, bf16[256,768]{1,0:T(8,128)(2,1)S(1)}, bf16[256,768]{1,0:T(8,128)(2,1)S(1)}) custom-call(s32[1,1]{1,0:T(1,128)} %bitcast.7.place_ref, f32[1,512]{1,0:T(1,128)S(1)} %bitcast.27, bf16[512,512]{1,0:T(8,128)(2,1)S(1)} %copy-done.7, bf16[512,512]{1,0:T(8,128)(2,1)S(1)} %copy-done.8, ...), custom_call_target="tpu_custom_call" | custom-call | flops 1000 | bytes 1000 | tf_op jit(solution)/shard_map/pallas_call | solution.py:40
  8.8 1.2 %collective-permute-start.6 = (bf16[256,768]{1,0:T(8,128)(2,1)S(1)}, bf16[256,768]{1,0:T(8,128)(2,1)}, u32[]{:S(2)}, u32[]{:S(2)}) collective-permute-start(bf16[256,768]{1,0:T(8,128)(2,1)S(1)} %get-tuple-element.21), channel_id=1, source_target_pairs={{0,4},{4,0},{8,12},{12,8},{16,20},{20,16},{24,28},{28,24},{1,5},{5... | collective-permute-start | bytes 1179656 | tf_op jit(solution)/shard_map/ppermute | solution.py:300
  10.1 0.3 collective-permute-start
  10.4 8.3 %collective-permute-done.12 = bf16[256,768]{1,0:T(8,128)(2,1)} collective-permute-done((bf16[256,768]{1,0:T(8,128)(2,1)S(1)}, bf16[256,768]{1,0:T(8,128)(2,1)}, u32[]{:S(2)}, u32[]{:S(2)}) %collective-permute-start.12) | collective-permute-done | bytes 393248 | tf_op jit(solution)/shard_map/ppermute | solution.py:300
  18.7 1.0 add_convert_fusion.1
  19.8 1.0 add_convert_fusion.2
  20.8 0.4 collective-permute-start.7
  21.2 10.4 %collective-permute-done.13 = bf16[128,768]{1,0:T(8,128)(2,1)S(1)} collective-permute-done((bf16[128,768]{1,0:T(8,128)(2,1)S(1)}, bf16[128,768]{1,0:T(8,128)(2,1)S(1)}, u32[]{:S(2)}, u32[]{:S(2)}) %collective-permute-start.13) | collective-permute-done | bytes 196640 | tf_op jit(solution)/shard_map/ppermute | solution.py:300
  31.6 0.9 add_convert_fusion.4
  32.5 1.3 %collective-permute-start.14 = (bf16[64,768]{1,0:T(8,128)(2,1)S(1)}, bf16[64,768]{1,0:T(8,128)(2,1)S(1)}, u32[]{:S(2)}, u32[]{:S(2)}) collective-permute-start(bf16[64,768]{1,0:T(8,128)(2,1)S(1)} %add_convert_fusion.4), channel_id=1, source_target_pairs={{0,4},{4,0},{8,12},{12,8},{16,20},{20,16},{24,28},{28,24},{1,5},{5... | collective-permute-start | bytes 294920 | tf_op jit(solution)/shard_map/ppermute | solution.py:300
  33.9 0.9 add_convert_fusion.6
  34.9 1.5 %collective-permute-done.14 = bf16[64,768]{1,0:T(8,128)(2,1)S(1)} collective-permute-done((bf16[64,768]{1,0:T(8,128)(2,1)S(1)}, bf16[64,768]{1,0:T(8,128)(2,1)S(1)}, u32[]{:S(2)}, u32[]{:S(2)}) %collective-permute-start.14) | collective-permute-done | bytes 98336 | tf_op jit(solution)/shard_map/ppermute | solution.py:300
  36.4 0.9 add_convert_fusion.3
  37.4 1.3 %collective-permute-start.15 = (bf16[64,768]{1,0:T(8,128)(2,1)S(1)}, bf16[64,768]{1,0:T(8,128)(2,1)S(1)}, u32[]{:S(2)}, u32[]{:S(2)}) collective-permute-start(bf16[64,768]{1,0:T(8,128)(2,1)S(1)} %add_convert_fusion.3), channel_id=1, source_target_pairs={{0,4},{4,0},{8,12},{12,8},{16,20},{20,16},{24,28},{28,24},{1,5},{5... | collective-permute-start | bytes 294920 | tf_op jit(solution)/shard_map/ppermute | solution.py:300
  38.7 0.6 collective-permute-done.8
  39.2 0.9 add_convert_fusion.5
  40.2 0.4 collective-permute-start.9
  40.6 0.6 collective-permute-done.15
  41.2 1.5 %collective-permute-start.16 = (bf16[128,768]{1,0:T(8,128)(2,1)S(1)}, bf16[128,768]{1,0:T(8,128)(2,1)S(1)}, u32[]{:S(2)}, u32[]{:S(2)}) collective-permute-start(bf16[128,768]{1,0:T(8,128)(2,1)S(1)} %pad_maximum_fusion.3), channel_id=1, source_target_pairs={{0,16},{4,20},{8,24},{12,28},{16,0},{20,4},{24,8},{28,12},{1,17},{... | collective-permute-start | bytes 589832 | tf_op jit(solution)/shard_map/ppermute | solution.py:300
  42.7 4.0 %collective-permute-done.9 = bf16[64,768]{1,0:T(8,128)(2,1)S(1)} collective-permute-done((bf16[64,768]{1,0:T(8,128)(2,1)S(1)}, bf16[64,768]{1,0:T(8,128)(2,1)S(1)}, u32[]{:S(2)}, u32[]{:S(2)}) %collective-permute-start.9) | collective-permute-done | bytes 98336 | tf_op jit(solution)/shard_map/ppermute | solution.py:300
  46.8 0.8 shard_map.132
  47.6 1.3 %collective-permute-start.1 = (bf16[1024,128]{1,0:T(8,128)(2,1)S(1)}, bf16[1024,128]{1,0:T(8,128)(2,1)S(1)}, u32[]{:S(2)}, u32[]{:S(2)}) collective-permute-start(bf16[1024,128]{1,0:T(8,128)(2,1)S(1)} %get-tuple-element.15.high_ref), channel_id=1, source_target_pairs={{0,8},{4,12},{8,16},{12,20},{16,24},{20,28},{1,9},{5,13},{9,17},{1... | collective-permute-start | bytes 786440 | tf_op jit(solution)/shard_map/ppermute | solution.py:289
  48.9 4.7 %collective-permute-start.2 = (bf16[1024,128]{1,0:T(8,128)(2,1)}, bf16[1024,128]{1,0:T(8,128)(2,1)}, u32[]{:S(2)}, u32[]{:S(2)}) collective-permute-start(bf16[1024,128]{1,0:T(8,128)(2,1)} %get-tuple-element.16.low_ref), channel_id=1, source_target_pairs={{8,0},{12,4},{16,8},{20,12},{24,16},{28,20},{9,1},{13,5},{17,9},{2... | collective-permute-start | bytes 786440 | tf_op jit(solution)/shard_map/ppermute | solution.py:289
  53.6 0.8 collective-permute-start.17
  54.7 4.5 %collective-permute-start.11 = (bf16[256,768]{1,0:T(8,128)(2,1)S(1)}, bf16[256,768]{1,0:T(8,128)(2,1)}, u32[]{:S(2)}, u32[]{:S(2)}) collective-permute-start(bf16[256,768]{1,0:T(8,128)(2,1)S(1)} %pad_maximum_fusion.refs_0_), channel_id=1, source_target_pairs={{0,4},{4,0},{8,12},{12,8},{16,20},{20,16},{24,28},{28,24},{1,5},{5... | collective-permute-start | bytes 1179656 | tf_op jit(solution)/shard_map/ppermute | solution.py:300
  59.2 2.1 %collective-permute-start.4 = (bf16[512,256]{1,0:T(8,128)(2,1)}, bf16[512,256]{1,0:T(8,128)(2,1)}, u32[]{:S(2)}, u32[]{:S(2)}) collective-permute-start(bf16[512,256]{1,0:T(8,128)(2,1)} %keys_ref.7), channel_id=1, source_target_pairs={{0,4},{4,8},{8,12},{12,16},{16,20},{20,24},{24,28},{1,5},{5,9},{9,... | collective-permute-start | bytes 786440 | tf_op jit(solution)/shard_map/ppermute | solution.py:289
  61.3 0.7 copy-done.16
  62.0 4.3 %collective-permute-start.5 = (bf16[512,256]{1,0:T(8,128)(2,1)}, bf16[512,256]{1,0:T(8,128)(2,1)}, u32[]{:S(2)}, u32[]{:S(2)}) collective-permute-start(bf16[512,256]{1,0:T(8,128)(2,1)} %keys_ref.7), channel_id=1, source_target_pairs={{4,0},{8,4},{12,8},{16,12},{20,16},{24,20},{28,24},{5,1},{9,5},{13... | collective-permute-start | bytes 786440 | tf_op jit(solution)/shard_map/ppermute | solution.py:289
  66.5 1.1 copy-done.15
  67.6 0.9 copy-done.17
  68.5 5.1 %shard_map.133 = (bf16[512,128]{1,0:T(8,128)(2,1)S(1)}, bf16[512,128]{1,0:T(8,128)(2,1)}) custom-call(f32[2,2]{1,0:T(2,128)S(1)} %reshape.26.edge_ref, s32[1,1]{1,0:T(1,128)} %bitcast.10.side_ref, bf16[512,256]{1,0:T(8,128)(2,1)S(1)} %copy-done.11, bf16[1536,128]{1,0:T(8,128)(2,1)S(1)} %collective-permute-done.other_ref, bf16[1024,128]{1,0:T(8,128)(2,1)S(1)} %copy-done.17, ...), custom_call_target="tpu_custom_call" | custom-call | flops 805306368 | bytes 2097152 | tf_op jit(solution)/shard_map/pallas_call | solution.py:40
  73.6 1.2 %collective-permute-start.3 = (bf16[512,128]{1,0:T(8,128)(2,1)}, bf16[512,128]{1,0:T(8,128)(2,1)S(1)}, u32[]{:S(2)}, u32[]{:S(2)}) collective-permute-start(bf16[512,128]{1,0:T(8,128)(2,1)} %get-tuple-element.18), channel_id=1, source_target_pairs={{0,4},{4,0},{8,12},{12,8},{16,20},{20,16},{24,28},{28,24},{1,5},{5... | collective-permute-start | bytes 393224 | tf_op jit(solution)/shard_map/ppermute | solution.py:300
  74.9 6.7 %collective-permute-done.3.other_ref = bf16[512,128]{1,0:T(8,128)(2,1)S(1)} collective-permute-done((bf16[512,128]{1,0:T(8,128)(2,1)}, bf16[512,128]{1,0:T(8,128)(2,1)S(1)}, u32[]{:S(2)}, u32[]{:S(2)}) %collective-permute-start.3) | collective-permute-done | bytes 131104 | tf_op jit(solution)/shard_map/ppermute | solution.py:300
  81.6 0.5 shard_map.134.query_ref
  82.2 1.1 copy-done.4
  83.3 5.5 %shard_map.136 = (bf16[3,64,512]{2,1,0:T(8,128)(2,1)}, bf16[512,512]{1,0:T(8,128)(2,1)S(1)}) custom-call(s32[1,1]{1,0:T(1,128)} %bitcast.7.place_ref, bf16[3,512,512]{2,1,0:T(8,128)(2,1)S(1)} %bitcast.25, bf16[512,512]{1,0:T(8,128)(2,1)S(1)} %shard_map.134.query_ref, bf16[256,768]{1,0:T(8,128)(2,1)S(1)} %copy-done.4, ...), custom_call_target="tpu_custom_call" | custom-call | flops 1000 | bytes 1000 | tf_op jit(solution)/shard_map/pallas_call | solution.py:40
  88.8 1.0 shard_map.138
  89.8 1.8 %collective-permute-start.18 = (bf16[2,512,256]{2,1,0:T(8,128)(2,1)S(1)}, bf16[2,512,256]{2,1,0:T(8,128)(2,1)S(1)}, u32[]{:S(2)}, u32[]{:S(2)}) collective-permute-start(bf16[2,512,256]{2,1,0:T(8,128)(2,1)S(1)} %shard_map.138), channel_id=1, source_target_pairs={{0,1},{1,0},{2,3},{3,2},{4,5},{5,4},{6,7},{7,6},{8,9},{9,8},{10,11... | collective-permute-start | bytes 1572872 | tf_op jit(solution)/shard_map/ppermute | solution.py:295
  91.6 2.1 %collective-permute-start.20 = (bf16[512,256]{1,0:T(8,128)(2,1)S(1)}, bf16[512,256]{1,0:T(8,128)(2,1)S(1)}, u32[]{:S(2)}, u32[]{:S(2)}) collective-permute-start(bf16[512,256]{1,0:T(8,128)(2,1)S(1)} %copy-done.10), channel_id=1, source_target_pairs={{0,4},{4,8},{8,12},{12,16},{16,20},{20,24},{24,28},{1,5},{5,9},{9,... | collective-permute-start | bytes 786440 | tf_op jit(solution)/shard_map/ppermute | solution.py:289
  93.8 4.2 %collective-permute-start.21 = (bf16[512,256]{1,0:T(8,128)(2,1)S(1)}, bf16[512,256]{1,0:T(8,128)(2,1)S(1)}, u32[]{:S(2)}, u32[]{:S(2)}) collective-permute-start(bf16[512,256]{1,0:T(8,128)(2,1)S(1)} %copy-done.10), channel_id=1, source_target_pairs={{4,0},{8,4},{12,8},{16,12},{20,16},{24,20},{28,24},{5,1},{9,5},{13... | collective-permute-start | bytes 786440 | tf_op jit(solution)/shard_map/ppermute | solution.py:289
  98.0 1.0 shard_map.137.keep_ref
  99.2 3.1 %collective-permute-done.20.values_prev_ref = bf16[512,256]{1,0:T(8,128)(2,1)S(1)} collective-permute-done((bf16[512,256]{1,0:T(8,128)(2,1)S(1)}, bf16[512,256]{1,0:T(8,128)(2,1)S(1)}, u32[]{:S(2)}, u32[]{:S(2)}) %collective-permute-start.20) | collective-permute-done | bytes 262176 | tf_op jit(solution)/shard_map/ppermute | solution.py:289
  102.3 6.0 %collective-permute-done.21.values_next_ref = bf16[512,256]{1,0:T(8,128)(2,1)S(1)} collective-permute-done((bf16[512,256]{1,0:T(8,128)(2,1)S(1)}, bf16[512,256]{1,0:T(8,128)(2,1)S(1)}, u32[]{:S(2)}, u32[]{:S(2)}) %collective-permute-start.21) | collective-permute-done | bytes 262176 | tf_op jit(solution)/shard_map/ppermute | solution.py:289
  108.3 5.4 %shard_map.139 = bf16[512,256]{1,0:T(8,128)(2,1)} custom-call(f32[2,2]{1,0:T(2,128)S(1)} %reshape.26.edge_ref, bf16[512,256]{1,0:T(8,128)(2,1)S(1)} %copy-done.9, bf16[2,512,256]{2,1,0:T(8,128)(2,1)S(1)} %shard_map.137.keep_ref, bf16[2,512,256]{2,1,0:T(8,128)(2,1)S(1)} %collective-permute-done.18.near_ref, ...), custom_call_target="tpu_custom_call" | custom-call | flops 805306368 | bytes 2097152 | tf_op jit(solution)/shard_map/pallas_call | solution.py:40
  (56 shorter events, 1.5 us)
Async XLA Ops:
  0.6 1.4 %copy-start = (bf16[1,512,3,512]{3,1,2,0:T(8,128)(2,1)S(1)}, bf16[1,512,3,512]{3,1,2,0:T(8,128)(2,1)}, u32[]{:S(2)}) copy-start(bf16[1,512,3,512]{3,1,2,0:T(8,128)(2,1)} %param.19) | copy-start | bytes 4718596
  2.0 1.0 copy-start.7
  3.1 1.0 copy-start.8
  4.1 0.7 copy-start.13
  4.8 5.2 %copy-start.5 = (bf16[512,256]{1,0:T(8,128)(2,1)S(1)}, bf16[512,256]{1,0:T(8,128)(2,1)}, u32[]{:S(2)}) copy-start(bf16[512,256]{1,0:T(8,128)(2,1)} %keys_ref.5) | copy-start | bytes 786436
  4.8 5.2 %copy-start.6 = (bf16[512,256]{1,0:T(8,128)(2,1)S(1)}, bf16[512,256]{1,0:T(8,128)(2,1)}, u32[]{:S(2)}) copy-start(bf16[512,256]{1,0:T(8,128)(2,1)} %values_ref.5) | copy-start | bytes 786436
  4.8 5.2 %copy-start.11 = (bf16[512,256]{1,0:T(8,128)(2,1)S(1)}, bf16[512,256]{1,0:T(8,128)(2,1)}, u32[]{:S(2)}) copy-start(bf16[512,256]{1,0:T(8,128)(2,1)} %queries_ref.4) | copy-start | bytes 786436
  8.6 10.1 %collective-permute-start.12 = (bf16[256,768]{1,0:T(8,128)(2,1)S(1)}, bf16[256,768]{1,0:T(8,128)(2,1)}, u32[]{:S(2)}, u32[]{:S(2)}) collective-permute-start(bf16[256,768]{1,0:T(8,128)(2,1)S(1)} %get-tuple-element.23), channel_id=1, source_target_pairs={{0,8},{4,12},{8,0},{12,4},{16,24},{20,28},{24,16},{28,20},{1,9},{5... | collective-permute-start | bytes 1179656 | tf_op jit(solution)/shard_map/ppermute | solution.py:300
  8.8 11.0 %collective-permute-start.6 = (bf16[256,768]{1,0:T(8,128)(2,1)S(1)}, bf16[256,768]{1,0:T(8,128)(2,1)}, u32[]{:S(2)}, u32[]{:S(2)}) collective-permute-start(bf16[256,768]{1,0:T(8,128)(2,1)S(1)} %get-tuple-element.21), channel_id=1, source_target_pairs={{0,4},{4,0},{8,12},{12,8},{16,20},{20,16},{24,28},{28,24},{1,5},{5... | collective-permute-start | bytes 1179656 | tf_op jit(solution)/shard_map/ppermute | solution.py:300
  10.1 36.7 %collective-permute-start = (bf16[1536,128]{1,0:T(8,128)(2,1)S(1)}, bf16[1536,128]{1,0:T(8,128)(2,1)S(1)}, u32[]{:S(2)}, u32[]{:S(2)}) collective-permute-start(bf16[1536,128]{1,0:T(8,128)(2,1)S(1)} %shard_map.131), channel_id=1, source_target_pairs={{0,4},{4,0},{8,12},{12,8},{16,20},{20,16},{24,28},{28,24},{1,5},{5... | collective-permute-start | bytes 1179656 | tf_op jit(solution)/shard_map/ppermute | solution.py:300
  19.7 11.9 %collective-permute-start.13 = (bf16[128,768]{1,0:T(8,128)(2,1)S(1)}, bf16[128,768]{1,0:T(8,128)(2,1)S(1)}, u32[]{:S(2)}, u32[]{:S(2)}) collective-permute-start(bf16[128,768]{1,0:T(8,128)(2,1)S(1)} %add_convert_fusion.1), channel_id=1, source_target_pairs={{0,16},{4,20},{8,24},{12,28},{16,0},{20,4},{24,8},{28,12},{1,17},{... | collective-permute-start | bytes 589832 | tf_op jit(solution)/shard_map/ppermute | solution.py:300
  20.8 13.1 %collective-permute-start.7 = (bf16[128,768]{1,0:T(8,128)(2,1)S(1)}, bf16[128,768]{1,0:T(8,128)(2,1)S(1)}, u32[]{:S(2)}, u32[]{:S(2)}) collective-permute-start(bf16[128,768]{1,0:T(8,128)(2,1)S(1)} %add_convert_fusion.2), channel_id=1, source_target_pairs={{0,8},{4,12},{8,0},{12,4},{16,24},{20,28},{24,16},{28,20},{1,9},{5... | collective-permute-start | bytes 589832 | tf_op jit(solution)/shard_map/ppermute | solution.py:300
  32.5 3.9 %collective-permute-start.14 = (bf16[64,768]{1,0:T(8,128)(2,1)S(1)}, bf16[64,768]{1,0:T(8,128)(2,1)S(1)}, u32[]{:S(2)}, u32[]{:S(2)}) collective-permute-start(bf16[64,768]{1,0:T(8,128)(2,1)S(1)} %add_convert_fusion.4), channel_id=1, source_target_pairs={{0,4},{4,0},{8,12},{12,8},{16,20},{20,16},{24,28},{28,24},{1,5},{5... | collective-permute-start | bytes 294920 | tf_op jit(solution)/shard_map/ppermute | solution.py:300
  34.8 4.4 %collective-permute-start.8 = (bf16[64,768]{1,0:T(8,128)(2,1)S(1)}, bf16[64,768]{1,0:T(8,128)(2,1)S(1)}, u32[]{:S(2)}, u32[]{:S(2)}) collective-permute-start(bf16[64,768]{1,0:T(8,128)(2,1)S(1)} %add_convert_fusion.6), channel_id=1, source_target_pairs={{0,16},{4,20},{8,24},{12,28},{16,0},{20,4},{24,8},{28,12},{1,17},{... | collective-permute-start | bytes 294920 | tf_op jit(solution)/shard_map/ppermute | solution.py:300
  37.4 3.8 %collective-permute-start.15 = (bf16[64,768]{1,0:T(8,128)(2,1)S(1)}, bf16[64,768]{1,0:T(8,128)(2,1)S(1)}, u32[]{:S(2)}, u32[]{:S(2)}) collective-permute-start(bf16[64,768]{1,0:T(8,128)(2,1)S(1)} %add_convert_fusion.3), channel_id=1, source_target_pairs={{0,4},{4,0},{8,12},{12,8},{16,20},{20,16},{24,28},{28,24},{1,5},{5... | collective-permute-start | bytes 294920 | tf_op jit(solution)/shard_map/ppermute | solution.py:300
  40.2 6.5 %collective-permute-start.9 = (bf16[64,768]{1,0:T(8,128)(2,1)S(1)}, bf16[64,768]{1,0:T(8,128)(2,1)S(1)}, u32[]{:S(2)}, u32[]{:S(2)}) collective-permute-start(bf16[64,768]{1,0:T(8,128)(2,1)S(1)} %add_convert_fusion.5), channel_id=1, source_target_pairs={{0,16},{4,20},{8,24},{12,28},{16,0},{20,4},{24,8},{28,12},{1,17},{... | collective-permute-start | bytes 294920 | tf_op jit(solution)/shard_map/ppermute | solution.py:300
  41.2 12.4 %collective-permute-start.16 = (bf16[128,768]{1,0:T(8,128)(2,1)S(1)}, bf16[128,768]{1,0:T(8,128)(2,1)S(1)}, u32[]{:S(2)}, u32[]{:S(2)}) collective-permute-start(bf16[128,768]{1,0:T(8,128)(2,1)S(1)} %pad_maximum_fusion.3), channel_id=1, source_target_pairs={{0,16},{4,20},{8,24},{12,28},{16,0},{20,4},{24,8},{28,12},{1,17},{... | collective-permute-start | bytes 589832 | tf_op jit(solution)/shard_map/ppermute | solution.py:300
  46.7 8.0 %collective-permute-start.10 = (bf16[128,768]{1,0:T(8,128)(2,1)S(1)}, bf16[128,768]{1,0:T(8,128)(2,1)S(1)}, u32[]{:S(2)}, u32[]{:S(2)}) collective-permute-start(bf16[128,768]{1,0:T(8,128)(2,1)S(1)} %pad_maximum_fusion.2), channel_id=1, source_target_pairs={{0,8},{4,12},{8,0},{12,4},{16,24},{20,28},{24,16},{28,20},{1,9},{5... | collective-permute-start | bytes 589832 | tf_op jit(solution)/shard_map/ppermute | solution.py:300
  47.6 18.8 %copy-start.14 = (bf16[1024,128]{1,0:T(8,128)(2,1)}, bf16[1024,128]{1,0:T(8,128)(2,1)S(1)}, u32[]{:S(2)}) copy-start(bf16[1024,128]{1,0:T(8,128)(2,1)S(1)} %get-tuple-element.15.high_ref) | copy-start | bytes 786436
  47.6 13.7 %collective-permute-start.1 = (bf16[1024,128]{1,0:T(8,128)(2,1)S(1)}, bf16[1024,128]{1,0:T(8,128)(2,1)S(1)}, u32[]{:S(2)}, u32[]{:S(2)}) collective-permute-start(bf16[1024,128]{1,0:T(8,128)(2,1)S(1)} %get-tuple-element.15.high_ref), channel_id=1, source_target_pairs={{0,8},{4,12},{8,16},{12,20},{16,24},{20,28},{1,9},{5,13},{9,17},{1... | collective-permute-start | bytes 786440 | tf_op jit(solution)/shard_map/ppermute | solution.py:289
  48.9 17.6 %collective-permute-start.2 = (bf16[1024,128]{1,0:T(8,128)(2,1)}, bf16[1024,128]{1,0:T(8,128)(2,1)}, u32[]{:S(2)}, u32[]{:S(2)}) collective-permute-start(bf16[1024,128]{1,0:T(8,128)(2,1)} %get-tuple-element.16.low_ref), channel_id=1, source_target_pairs={{8,0},{12,4},{16,8},{20,12},{24,16},{28,20},{9,1},{13,5},{17,9},{2... | collective-permute-start | bytes 786440 | tf_op jit(solution)/shard_map/ppermute | solution.py:289
  53.6 28.6 %collective-permute-start.17 = (bf16[256,768]{1,0:T(8,128)(2,1)S(1)}, bf16[256,768]{1,0:T(8,128)(2,1)}, u32[]{:S(2)}, u32[]{:S(2)}) collective-permute-start(bf16[256,768]{1,0:T(8,128)(2,1)S(1)} %pad_maximum_fusion.1.refs_2_), channel_id=1, source_target_pairs={{0,8},{4,12},{8,0},{12,4},{16,24},{20,28},{24,16},{28,20},{1,9},{5... | collective-permute-start | bytes 1179656 | tf_op jit(solution)/shard_map/ppermute | solution.py:300
  54.7 27.4 %copy-start.3 = (bf16[256,768]{1,0:T(8,128)(2,1)}, bf16[256,768]{1,0:T(8,128)(2,1)S(1)}, u32[]{:S(2)}) copy-start(bf16[256,768]{1,0:T(8,128)(2,1)S(1)} %pad_maximum_fusion.refs_0_) | copy-start | bytes 1179652
  54.7 26.9 %copy-start.12 = (bf16[1,256,512]{2,1,0:T(8,128)(2,1)S(1)}, bf16[1,256,512]{2,1,0:T(8,128)(2,1)}, u32[]{:S(2)}) copy-start(bf16[1,256,512]{2,1,0:T(8,128)(2,1)} %param.15) | copy-start | bytes 786436
  54.7 27.5 %collective-permute-start.11 = (bf16[256,768]{1,0:T(8,128)(2,1)S(1)}, bf16[256,768]{1,0:T(8,128)(2,1)}, u32[]{:S(2)}, u32[]{:S(2)}) collective-permute-start(bf16[256,768]{1,0:T(8,128)(2,1)S(1)} %pad_maximum_fusion.refs_0_), channel_id=1, source_target_pairs={{0,4},{4,0},{8,12},{12,8},{16,20},{20,16},{24,28},{28,24},{1,5},{5... | collective-permute-start | bytes 1179656 | tf_op jit(solution)/shard_map/ppermute | solution.py:300
  59.2 22.9 %collective-permute-start.4 = (bf16[512,256]{1,0:T(8,128)(2,1)}, bf16[512,256]{1,0:T(8,128)(2,1)}, u32[]{:S(2)}, u32[]{:S(2)}) collective-permute-start(bf16[512,256]{1,0:T(8,128)(2,1)} %keys_ref.7), channel_id=1, source_target_pairs={{0,4},{4,8},{8,12},{12,16},{16,20},{20,24},{24,28},{1,5},{5,9},{9,... | collective-permute-start | bytes 786440 | tf_op jit(solution)/shard_map/ppermute | solution.py:289
  61.3 0.7 copy-start.16
  62.0 20.1 %collective-permute-start.5 = (bf16[512,256]{1,0:T(8,128)(2,1)}, bf16[512,256]{1,0:T(8,128)(2,1)}, u32[]{:S(2)}, u32[]{:S(2)}) collective-permute-start(bf16[512,256]{1,0:T(8,128)(2,1)} %keys_ref.7), channel_id=1, source_target_pairs={{4,0},{8,4},{12,8},{16,12},{20,16},{24,20},{28,24},{5,1},{9,5},{13... | collective-permute-start | bytes 786440 | tf_op jit(solution)/shard_map/ppermute | solution.py:289
  66.5 15.7 %copy-start.1 = (bf16[1,512,3,512]{3,1,2,0:T(8,128)(2,1)S(1)}, bf16[1,512,3,512]{3,1,2,0:T(8,128)(2,1)}, u32[]{:S(2)}) copy-start(bf16[1,512,3,512]{3,1,2,0:T(8,128)(2,1)} %param.19) | copy-start | bytes 4718596
  66.5 1.1 copy-start.15
  67.6 0.9 copy-start.17
  73.6 8.0 %collective-permute-start.3 = (bf16[512,128]{1,0:T(8,128)(2,1)}, bf16[512,128]{1,0:T(8,128)(2,1)S(1)}, u32[]{:S(2)}, u32[]{:S(2)}) collective-permute-start(bf16[512,128]{1,0:T(8,128)(2,1)} %get-tuple-element.18), channel_id=1, source_target_pairs={{0,4},{4,0},{8,12},{12,8},{16,20},{20,16},{24,28},{28,24},{1,5},{5... | collective-permute-start | bytes 393224 | tf_op jit(solution)/shard_map/ppermute | solution.py:300
  82.1 6.6 %copy-start.2 = (bf16[512,1024]{1,0:T(8,128)(2,1)S(1)}, bf16[512,1024]{1,0:T(8,128)(2,1)}, u32[]{:S(2)}) copy-start(bf16[512,1024]{1,0:T(8,128)(2,1)} %map_ref.3) | copy-start | bytes 3145732
  82.2 1.1 copy-start.4
  88.8 2.8 %copy-start.10 = (bf16[512,256]{1,0:T(8,128)(2,1)S(1)}, bf16[512,256]{1,0:T(8,128)(2,1)}, u32[]{:S(2)}) copy-start(bf16[512,256]{1,0:T(8,128)(2,1)} %values_ref.7) | copy-start | bytes 786436
  89.8 18.5 %copy-start.9 = (bf16[512,256]{1,0:T(8,128)(2,1)S(1)}, bf16[512,256]{1,0:T(8,128)(2,1)}, u32[]{:S(2)}) copy-start(bf16[512,256]{1,0:T(8,128)(2,1)} %queries_ref.5) | copy-start | bytes 786436
  89.8 9.2 %collective-permute-start.18 = (bf16[2,512,256]{2,1,0:T(8,128)(2,1)S(1)}, bf16[2,512,256]{2,1,0:T(8,128)(2,1)S(1)}, u32[]{:S(2)}, u32[]{:S(2)}) collective-permute-start(bf16[2,512,256]{2,1,0:T(8,128)(2,1)S(1)} %shard_map.138), channel_id=1, source_target_pairs={{0,1},{1,0},{2,3},{3,2},{4,5},{5,4},{6,7},{7,6},{8,9},{9,8},{10,11... | collective-permute-start | bytes 1572872 | tf_op jit(solution)/shard_map/ppermute | solution.py:295
  91.6 10.7 %collective-permute-start.20 = (bf16[512,256]{1,0:T(8,128)(2,1)S(1)}, bf16[512,256]{1,0:T(8,128)(2,1)S(1)}, u32[]{:S(2)}, u32[]{:S(2)}) collective-permute-start(bf16[512,256]{1,0:T(8,128)(2,1)S(1)} %copy-done.10), channel_id=1, source_target_pairs={{0,4},{4,8},{8,12},{12,16},{16,20},{20,24},{24,28},{1,5},{5,9},{9,... | collective-permute-start | bytes 786440 | tf_op jit(solution)/shard_map/ppermute | solution.py:289
  93.8 14.5 %collective-permute-start.21 = (bf16[512,256]{1,0:T(8,128)(2,1)S(1)}, bf16[512,256]{1,0:T(8,128)(2,1)S(1)}, u32[]{:S(2)}, u32[]{:S(2)}) collective-permute-start(bf16[512,256]{1,0:T(8,128)(2,1)S(1)} %copy-done.10), channel_id=1, source_target_pairs={{4,0},{8,4},{12,8},{16,12},{20,16},{24,20},{28,24},{5,1},{9,5},{13... | collective-permute-start | bytes 786440 | tf_op jit(solution)/shard_map/ppermute | solution.py:289
  99.1 9.2 %collective-permute-start.19 = (bf16[512,256]{1,0:T(8,128)(2,1)S(1)}, bf16[512,256]{1,0:T(8,128)(2,1)S(1)}, u32[]{:S(2)}, u32[]{:S(2)}) collective-permute-start(bf16[512,256]{1,0:T(8,128)(2,1)S(1)} %fusion), channel_id=1, source_target_pairs={{0,2},{1,3},{2,0},{3,1},{4,6},{5,7},{6,4},{7,5},{8,10},{9,11},{10,... | collective-permute-start | bytes 786440 | tf_op jit(solution)/shard_map/ppermute | solution.py:295

commit v5 on v4

--- a/solution.py
+++ b/solution.py
@@ -14,7 +14,8 @@
 FAST_DIM = 512
 FAST_HIDDEN = 512
 TILE = 128
-VMEM_LIMIT = 48 * 1024 * 1024
+VMEM_LIMIT = 24 * 1024 * 1024
+VMEM_MOST = 60 * 1024 * 1024
 
 BF16 = jnp.bfloat16
 F32 = jnp.float32
@@ -29,7 +30,7 @@
     return lax.dot_general(left, right, (((1,), (1,)), ((), ())), preferred_element_type=F32)
 
 
-def call(body, out_shapes, operands, scalars=0, anywhere=0, scratch=(), cost=None):
+def call(body, out_shapes, operands, scalars=0, anywhere=0, scratch=(), cost=None, limit=VMEM_LIMIT):
     vmem = pl.BlockSpec(memory_space=pltpu.VMEM)
     in_specs = (
         [pl.BlockSpec(memory_space=pltpu.SMEM)] * scalars
@@ -43,7 +44,7 @@
         in_specs=in_specs,
         out_specs=jax.tree.map(lambda _: vmem, out_shapes),
         scratch_shapes=scratch,
-        compiler_params=pltpu.CompilerParams(vmem_limit_bytes=VMEM_LIMIT),
+        compiler_params=pltpu.CompilerParams(vmem_limit_bytes=limit),
         cost_estimate=pl.CostEstimate(flops=flops, bytes_accessed=moved, transcendentals=0),
     )(*operands)
 
@@ -300,23 +301,37 @@
     return lax.ppermute(value, "seq", [(i, i ^ step) for i in range(lax.axis_size("seq"))])
 
 
-def sum_over_seq(chunks, orders):
-    keeps = [[keep] for keep, _ in chunks]
-    for turn in range(len(orders[0])):
-        swapped = []
-        for index, order in enumerate(orders):
-            if turn == 0:
-                total = chunks[index][1]
-            else:
-                half = keeps[index][0].shape[0] // 2
-                total = sum(part[half:].astype(F32) for part in keeps[index]).astype(BF16)
-                keeps[index] = [part[:half] for part in keeps[index]]
-            swapped.append(seq_swap(total, order[turn]))
-        keeps = [keep + [new] for keep, new in zip(keeps, swapped)]
-    held = [(sum(part.astype(F32) for part in keep).astype(BF16),) for keep in keeps]
-    for turn in reversed(range(len(orders[0]))):
+def after(value, others):
+    return lax.optimization_barrier((value, others))[0]
+
+
+def sum_over_seq(chunks, orders, waits):
+    turns = len(orders[0])
+
+    def swapped(values, stage, turn):
+        values = list(values)
+        if stage in waits:
+            values[0] = after(values[0], waits[stage])
+        return [seq_swap(value, order[turn]) for value, order in zip(values, orders)]
+
+    keeps = [keep for keep, _ in chunks]
+    sends = [send for _, send in chunks]
+    for turn in range(turns):
+        found = swapped(sends, turn, turn)
+        sends, rest = [], []
+        for keep, new in zip(keeps, found):
+            if turn == turns - 1:
+                rest.append((keep.astype(F32) + new.astype(F32)).astype(BF16))
+                continue
+            half = keep.shape[0] // 2
+            sends.append((keep[half:].astype(F32) + new[half:].astype(F32)).astype(BF16))
+            rest.append(lax.optimization_barrier(keep[:half].astype(F32) + new[:half].astype(F32)))
+        keeps = rest
+    held = [(keep,) for keep in keeps]
+    for turn in reversed(range(turns)):
         whole = [jnp.concatenate(parts) if len(parts) > 1 else parts[0] for parts in held]
-        held = [(own, seq_swap(own, order[turn])) for own, order in zip(whole, orders)]
+        found = swapped(whole, 2 * turns - 1 - turn, turn)
+        held = list(zip(whole, found))
     return [part for parts in held for part in parts]
 
 
@@ -370,12 +385,8 @@
         (place, step_rates.reshape(1, rows), fast_keys, fast_values, weights),
         scalars=1,
         scratch=[pltpu.VMEM((hidden_size, chunk_width), BF16)] * 2,
-    )
-    if halving:
-        gathered = sum_over_seq([gradients[:2], gradients[2:]], orders)
-    else:
-        gathered = lax.psum(gradients, "seq")
-
+        limit=VMEM_MOST,
+    )
     low_block, high_block = call(
         border_kernel,
         [shape((2 * rows, HEAD_DIM), BF16)] * 2,
@@ -401,7 +412,16 @@
 
     keys_prev, keys_next = seq_shift(keys_second, 1), seq_shift(keys_second, -1)
     values_prev, values_next = seq_shift(values_second, 1), seq_shift(values_second, -1)
-    fast_query, keys_prev, keys_next = lax.optimization_barrier((fast_query, keys_prev, keys_next))
+    if halving:
+        stages = 2 * len(bits)
+        waits = {
+            len(bits) - 1: (low_block, high_block),
+            stages - 2: (prev_first, next_first),
+            stages - 1: (keep_first, send_first, keys_prev, keys_next),
+        }
+        gathered = sum_over_seq([gradients[:2], gradients[2:]], orders, waits)
+    else:
+        gathered = lax.psum(gradients, "seq")
 
     own_rows = hidden_size >> len(orders[0])
     own_new, fast_out = call(
@@ -414,6 +434,8 @@
     if not halving:
         share_rows = hidden_size // seq_count
         own_new = lax.dynamic_slice_in_dim(own_new, seq_place * share_rows, share_rows, 1)
+
+    fast_out = after(fast_out, (values_prev, values_next))
 
     def mixed_for(low_bit):
         far = (head_place // 2) ^ 1

time: 114 us -> 122 us (1.070)
  the two profiles are of different devices: /device:TPU:25 before, /device:TPU:0 now
where the time goes in v5:
time: 122 us; the launch traced here: 121 us
  starting transfers between devices  44.9 us (37%)
  waiting for transfers between devices  43.1 us (35%)
  Pallas kernels  24.1 us (20%)
  other arithmetic  4.65 us (4%)
  local copies, waits for them, and re-layouts  2.67 us (2%)
    ppermute x14, waiting for transfers between devices, seq_swap(): lax.ppermute(value, 'seq', [(i, i ^ step) for i in range(lax.axis_size('s...  35.5 us
    ppermute x14, starting transfers between devices, seq_swap(): lax.ppermute(value, 'seq', [(i, i ^ step) for i in range(lax.axis_size('s...  29.3 us
    pallas_call x9, Pallas kernels, call(): pl.pallas_call(body, out_shape=out_shapes, in_specs=in_specs, out_specs=j...  24.1 us
    ppermute x6, starting transfers between devices, seq_shift(): lax.ppermute(value, 'seq', [(i, i + step) for i in range(peers) if 0 <= i...  13.9 us
    ppermute x2, waiting for transfers between devices, head_swap(): lax.ppermute(value, 'head', [(i, i ^ bit) for i in range(lax.axis_size('h...  7.58 us
    unnamed x34, local copies, waits for them, and re-layouts  2.58 us
  transfers between devices with their start and end apart: 22, of which 9 were waited for; matrix products, arithmetic and copies ran while one was open for 4% of the time, Pallas kernels for 9%

profile of v5, /device:TPU:0, one launch (start us, length us, event | category | flops | bytes accessed | tf_op | source)
XLA Modules:
  0.0 120.6 jit_solution(8734012593537964812)
XLA Ops:
  0.7 6.7 %shard_map.135 = (bf16[256,768]{1,0:T(8,128)(2,1)}, bf16[256,768]{1,0:T(8,128)(2,1)}, bf16[256,768]{1,0:T(8,128)(2,1)}, bf16[256,768]{1,0:T(8,128)(2,1)}) custom-call(s32[1,1]{1,0:T(1,128)} %bitcast.7.place_ref, f32[1,512]{1,0:T(1,128)} %bitcast.27, bf16[512,512]{1,0:T(8,128)(2,1)} %keys_ref.6, bf16[512,512]{1,0:T(8,128)(2,1)} %values_ref.6, ...), custom_call_target="tpu_custom_call" | custom-call | flops 1000 | bytes 1000 | tf_op jit(solution)/shard_map/pallas_call | solution.py:41
  7.3 3.0 %collective-permute-start.12 = (bf16[256,768]{1,0:T(8,128)(2,1)}, bf16[256,768]{1,0:T(8,128)(2,1)S(1)}, u32[]{:S(2)}, u32[]{:S(2)}) collective-permute-start(bf16[256,768]{1,0:T(8,128)(2,1)} %get-tuple-element.26), channel_id=1, source_target_pairs={{0,8},{4,12},{8,0},{12,4},{16,24},{20,28},{24,16},{28,20},{1,9},{5... | collective-permute-start | bytes 1179656 | tf_op jit(solution)/shard_map/ppermute | solution.py:301
  10.4 1.5 %collective-permute-start.4 = (bf16[256,768]{1,0:T(8,128)(2,1)}, bf16[256,768]{1,0:T(8,128)(2,1)}, u32[]{:S(2)}, u32[]{:S(2)}) collective-permute-start(bf16[256,768]{1,0:T(8,128)(2,1)} %get-tuple-element.21), channel_id=1, source_target_pairs={{0,4},{4,0},{8,12},{12,8},{16,20},{20,16},{24,28},{28,24},{1,5},{5... | collective-permute-start | bytes 1179656 | tf_op jit(solution)/shard_map/ppermute | solution.py:301
  12.0 0.6 collective-permute-start
  12.6 1.3 %collective-permute-start.10 = (bf16[512,256]{1,0:T(8,128)(2,1)S(1)}, bf16[512,256]{1,0:T(8,128)(2,1)S(1)}, u32[]{:S(2)}, u32[]{:S(2)}) collective-permute-start(bf16[512,256]{1,0:T(8,128)(2,1)S(1)} %copy-done.7), channel_id=1, source_target_pairs={{4,0},{8,4},{12,8},{16,12},{20,16},{24,20},{28,24},{5,1},{9,5},{13... | collective-permute-start | bytes 786440 | tf_op jit(solution)/shard_map/ppermute | solution.py:290
  13.9 6.7 %collective-permute-done.12 = bf16[256,768]{1,0:T(8,128)(2,1)S(1)} collective-permute-done((bf16[256,768]{1,0:T(8,128)(2,1)}, bf16[256,768]{1,0:T(8,128)(2,1)S(1)}, u32[]{:S(2)}, u32[]{:S(2)}) %collective-permute-start.12) | collective-permute-done | bytes 393248 | tf_op jit(solution)/shard_map/ppermute | solution.py:301
  20.5 1.1 add_convert_fusion.1
  21.6 3.1 %collective-permute-start.13 = (bf16[128,768]{1,0:T(8,128)(2,1)S(1)}, bf16[128,768]{1,0:T(8,128)(2,1)S(1)}, u32[]{:S(2)}, u32[]{:S(2)}) collective-permute-start(bf16[128,768]{1,0:T(8,128)(2,1)S(1)} %get-tuple-element.30), channel_id=1, source_target_pairs={{0,16},{4,20},{8,24},{12,28},{16,0},{20,4},{24,8},{28,12},{1,17},{... | collective-permute-start | bytes 589832 | tf_op jit(solution)/shard_map/ppermute | solution.py:301
  24.8 1.7 %collective-permute-done.4 = bf16[256,768]{1,0:T(8,128)(2,1)} collective-permute-done((bf16[256,768]{1,0:T(8,128)(2,1)}, bf16[256,768]{1,0:T(8,128)(2,1)}, u32[]{:S(2)}, u32[]{:S(2)}) %collective-permute-start.4) | collective-permute-done | bytes 393248 | tf_op jit(solution)/shard_map/ppermute | solution.py:301
  26.5 1.1 add_convert_fusion.2
  27.6 1.4 %collective-permute-start.5 = (bf16[128,768]{1,0:T(8,128)(2,1)S(1)}, bf16[128,768]{1,0:T(8,128)(2,1)S(1)}, u32[]{:S(2)}, u32[]{:S(2)}) collective-permute-start(bf16[128,768]{1,0:T(8,128)(2,1)S(1)} %get-tuple-element.32), channel_id=1, source_target_pairs={{0,8},{4,12},{8,0},{12,4},{16,24},{20,28},{24,16},{28,20},{1,9},{5... | collective-permute-start | bytes 589832 | tf_op jit(solution)/shard_map/ppermute | solution.py:301
  29.0 5.2 %collective-permute-done.other_ref = bf16[1536,128]{1,0:T(8,128)(2,1)S(1)} collective-permute-done((bf16[1536,128]{1,0:T(8,128)(2,1)S(1)}, bf16[1536,128]{1,0:T(8,128)(2,1)S(1)}, u32[]{:S(2)}, u32[]{:S(2)}) %collective-permute-start) | collective-permute-done | bytes 393248 | tf_op jit(solution)/shard_map/ppermute | solution.py:301
  34.3 2.4 %collective-permute-start.1 = (bf16[1024,128]{1,0:T(8,128)(2,1)S(1)}, bf16[1024,128]{1,0:T(8,128)(2,1)S(1)}, u32[]{:S(2)}, u32[]{:S(2)}) collective-permute-start(bf16[1024,128]{1,0:T(8,128)(2,1)S(1)} %get-tuple-element.16.high_ref), channel_id=1, source_target_pairs={{0,8},{4,12},{8,16},{12,20},{16,24},{20,28},{1,9},{5,13},{9,17},{1... | collective-permute-start | bytes 786440 | tf_op jit(solution)/shard_map/ppermute | solution.py:290
  36.7 1.3 %collective-permute-start.2 = (bf16[1024,128]{1,0:T(8,128)(2,1)S(1)}, bf16[1024,128]{1,0:T(8,128)(2,1)S(1)}, u32[]{:S(2)}, u32[]{:S(2)}) collective-permute-start(bf16[1024,128]{1,0:T(8,128)(2,1)S(1)} %get-tuple-element.17.low_ref), channel_id=1, source_target_pairs={{8,0},{12,4},{16,8},{20,12},{24,16},{28,20},{9,1},{13,5},{17,9},{2... | collective-permute-start | bytes 786440 | tf_op jit(solution)/shard_map/ppermute | solution.py:290
  38.0 2.5 %collective-permute-start.14 = (bf16[64,768]{1,0:T(8,128)(2,1)S(1)}, bf16[64,768]{1,0:T(8,128)(2,1)S(1)}, u32[]{:S(2)}, u32[]{:S(2)}) collective-permute-start(bf16[64,768]{1,0:T(8,128)(2,1)S(1)} %get-tuple-element.34), channel_id=1, source_target_pairs={{0,4},{4,0},{8,12},{12,8},{16,20},{20,16},{24,28},{28,24},{1,5},{5... | collective-permute-start | bytes 294920 | tf_op jit(solution)/shard_map/ppermute | solution.py:301
  40.6 4.8 %collective-permute-start.6 = (bf16[64,768]{1,0:T(8,128)(2,1)S(1)}, bf16[64,768]{1,0:T(8,128)(2,1)S(1)}, u32[]{:S(2)}, u32[]{:S(2)}) collective-permute-start(bf16[64,768]{1,0:T(8,128)(2,1)S(1)} %get-tuple-element.22), channel_id=1, source_target_pairs={{0,16},{4,20},{8,24},{12,28},{16,0},{20,4},{24,8},{28,12},{1,17},{... | collective-permute-start | bytes 294920 | tf_op jit(solution)/shard_map/ppermute | solution.py:301
  45.5 0.1 collective-permute-start.15
  45.6 13.0 %collective-permute-done.6 = bf16[64,768]{1,0:T(8,128)(2,1)S(1)} collective-permute-done((bf16[64,768]{1,0:T(8,128)(2,1)S(1)}, bf16[64,768]{1,0:T(8,128)(2,1)S(1)}, u32[]{:S(2)}, u32[]{:S(2)}) %collective-permute-start.6) | collective-permute-done | bytes 98336 | tf_op jit(solution)/shard_map/ppermute | solution.py:301
  58.6 0.1 collective-permute-start.7
  58.7 3.0 %collective-permute-start.16 = (bf16[128,768]{1,0:T(8,128)(2,1)S(1)}, bf16[128,768]{1,0:T(8,128)(2,1)}, u32[]{:S(2)}, u32[]{:S(2)}) collective-permute-start(bf16[128,768]{1,0:T(8,128)(2,1)S(1)} %pad_maximum_fusion.3), channel_id=1, source_target_pairs={{0,16},{4,20},{8,24},{12,28},{16,0},{20,4},{24,8},{28,12},{1,17},{... | collective-permute-start | bytes 589832 | tf_op jit(solution)/shard_map/ppermute | solution.py:301
  61.7 0.1 pad_maximum_fusion.4
  61.7 0.1 reshape.26.edge_ref
  61.8 2.3 %collective-permute-done.7 = bf16[64,768]{1,0:T(8,128)(2,1)S(1)} collective-permute-done((bf16[64,768]{1,0:T(8,128)(2,1)S(1)}, bf16[64,768]{1,0:T(8,128)(2,1)S(1)}, u32[]{:S(2)}, u32[]{:S(2)}) %collective-permute-start.7) | collective-permute-done | bytes 98336 | tf_op jit(solution)/shard_map/ppermute | solution.py:301
  64.2 4.9 %collective-permute-start.9 = (bf16[512,256]{1,0:T(8,128)(2,1)S(1)}, bf16[512,256]{1,0:T(8,128)(2,1)S(1)}, u32[]{:S(2)}, u32[]{:S(2)}) collective-permute-start(bf16[512,256]{1,0:T(8,128)(2,1)S(1)} %copy-done.7), channel_id=1, source_target_pairs={{0,4},{4,8},{8,12},{12,16},{16,20},{20,24},{24,28},{1,5},{5,9},{9,... | collective-permute-start | bytes 786440 | tf_op jit(solution)/shard_map/ppermute | solution.py:290
  69.3 4.0 %shard_map.133 = (bf16[512,128]{1,0:T(8,128)(2,1)S(1)}, bf16[512,128]{1,0:T(8,128)(2,1)S(1)}) custom-call(f32[2,2]{1,0:T(2,128)S(1)} %reshape.26.edge_ref, s32[1,1]{1,0:T(1,128)} %bitcast.10.side_ref, bf16[512,256]{1,0:T(8,128)(2,1)S(1)} %copy-done.13, bf16[1536,128]{1,0:T(8,128)(2,1)S(1)} %collective-permute-done.other_ref, ...), custom_call_target="tpu_custom_call" | custom-call | flops 805306368 | bytes 2097152 | tf_op jit(solution)/shard_map/pallas_call | solution.py:41
  73.3 1.1 pad_maximum_fusion.1.refs_2_
  74.3 2.1 %collective-permute-start.17 = (bf16[256,768]{1,0:T(8,128)(2,1)S(1)}, bf16[256,768]{1,0:T(8,128)(2,1)}, u32[]{:S(2)}, u32[]{:S(2)}) collective-permute-start(bf16[256,768]{1,0:T(8,128)(2,1)S(1)} %pad_maximum_fusion.1.refs_2_), channel_id=1, source_target_pairs={{0,8},{4,12},{8,0},{12,4},{16,24},{20,28},{24,16},{28,20},{1,9},{5... | collective-permute-start | bytes 1179656 | tf_op jit(solution)/shard_map/ppermute | solution.py:301
  76.4 0.7 collective-permute-done.8
  77.1 0.9 pad_maximum_fusion.refs_0_
  78.0 0.7 copy-done.9
  78.8 0.7 copy-done.11
  79.5 3.0 %collective-permute-start.11 = (bf16[256,768]{1,0:T(8,128)(2,1)S(1)}, bf16[256,768]{1,0:T(8,128)(2,1)}, u32[]{:S(2)}, u32[]{:S(2)}) collective-permute-start(bf16[256,768]{1,0:T(8,128)(2,1)S(1)} %pad_maximum_fusion.refs_0_), channel_id=1, source_target_pairs={{0,4},{4,0},{8,12},{12,8},{16,20},{20,16},{24,28},{28,24},{1,5},{5... | collective-permute-start | bytes 1179656 | tf_op jit(solution)/shard_map/ppermute | solution.py:301
  82.5 2.6 %collective-permute-start.18 = (bf16[512,256]{1,0:T(8,128)(2,1)}, bf16[512,256]{1,0:T(8,128)(2,1)}, u32[]{:S(2)}, u32[]{:S(2)}) collective-permute-start(bf16[512,256]{1,0:T(8,128)(2,1)} %values_ref.7), channel_id=1, source_target_pairs={{0,4},{4,8},{8,12},{12,16},{16,20},{20,24},{24,28},{1,5},{5,9},{9,... | collective-permute-start | bytes 786440 | tf_op jit(solution)/shard_map/ppermute | solution.py:290
  85.1 1.5 %collective-permute-start.19 = (bf16[512,256]{1,0:T(8,128)(2,1)}, bf16[512,256]{1,0:T(8,128)(2,1)}, u32[]{:S(2)}, u32[]{:S(2)}) collective-permute-start(bf16[512,256]{1,0:T(8,128)(2,1)} %values_ref.7), channel_id=1, source_target_pairs={{4,0},{8,4},{12,8},{16,12},{20,16},{24,20},{28,24},{5,1},{9,5},{13... | collective-permute-start | bytes 786440 | tf_op jit(solution)/shard_map/ppermute | solution.py:290
  86.5 4.0 %collective-permute-start.3 = (bf16[512,128]{1,0:T(8,128)(2,1)S(1)}, bf16[512,128]{1,0:T(8,128)(2,1)S(1)}, u32[]{:S(2)}, u32[]{:S(2)}) collective-permute-start(bf16[512,128]{1,0:T(8,128)(2,1)S(1)} %get-tuple-element.19), channel_id=1, source_target_pairs={{0,4},{4,0},{8,12},{12,8},{16,20},{20,16},{24,28},{28,24},{1,5},{5... | collective-permute-start | bytes 393224 | tf_op jit(solution)/shard_map/ppermute | solution.py:301
  90.5 0.1 add_bitcast_fusion.1.place_ref
  90.6 5.9 %collective-permute-done.3.other_ref = bf16[512,128]{1,0:T(8,128)(2,1)S(1)} collective-permute-done((bf16[512,128]{1,0:T(8,128)(2,1)S(1)}, bf16[512,128]{1,0:T(8,128)(2,1)S(1)}, u32[]{:S(2)}, u32[]{:S(2)}) %collective-permute-start.3) | collective-permute-done | bytes 131104 | tf_op jit(solution)/shard_map/ppermute | solution.py:301
  96.5 0.5 shard_map.134.query_ref
  97.1 1.1 copy-done.3
  98.1 5.5 %shard_map.136 = (bf16[3,64,512]{2,1,0:T(8,128)(2,1)}, bf16[512,512]{1,0:T(8,128)(2,1)S(1)}) custom-call(s32[1,1]{1,0:T(1,128)} %bitcast.7.place_ref, bf16[3,512,512]{2,1,0:T(8,128)(2,1)S(1)} %bitcast.25, bf16[512,512]{1,0:T(8,128)(2,1)S(1)} %shard_map.134.query_ref, bf16[256,768]{1,0:T(8,128)(2,1)S(1)} %copy-done.3, ...), custom_call_target="tpu_custom_call" | custom-call | flops 1000 | bytes 1000 | tf_op jit(solution)/shard_map/pallas_call | solution.py:41
  103.6 1.0 shard_map.138
  104.8 0.1 add_bitcast_fusion.place_ref
  104.8 1.0 shard_map.137.keep_ref
  105.8 0.8 collective-permute-done.20.near_ref
  106.7 0.1 fusion
  106.7 1.6 %collective-permute-start.21 = (bf16[512,256]{1,0:T(8,128)(2,1)S(1)}, bf16[512,256]{1,0:T(8,128)(2,1)S(1)}, u32[]{:S(2)}, u32[]{:S(2)}) collective-permute-start(bf16[512,256]{1,0:T(8,128)(2,1)S(1)} %fusion), channel_id=1, source_target_pairs={{0,2},{1,3},{2,0},{3,1},{4,6},{5,7},{6,4},{7,5},{8,10},{9,11},{10,... | collective-permute-start | bytes 786440 | tf_op jit(solution)/shard_map/ppermute | solution.py:296
  108.4 6.8 %collective-permute-done.21.far_ref = bf16[512,256]{1,0:T(8,128)(2,1)S(1)} collective-permute-done((bf16[512,256]{1,0:T(8,128)(2,1)S(1)}, bf16[512,256]{1,0:T(8,128)(2,1)S(1)}, u32[]{:S(2)}, u32[]{:S(2)}) %collective-permute-start.21) | collective-permute-done | bytes 262176 | tf_op jit(solution)/shard_map/ppermute | solution.py:296
  115.2 5.4 %shard_map.139 = bf16[512,256]{1,0:T(8,128)(2,1)} custom-call(f32[2,2]{1,0:T(2,128)S(1)} %reshape.26.edge_ref, bf16[512,256]{1,0:T(8,128)(2,1)S(1)} %copy-done.6, bf16[2,512,256]{2,1,0:T(8,128)(2,1)S(1)} %shard_map.137.keep_ref, bf16[2,512,256]{2,1,0:T(8,128)(2,1)S(1)} %collective-permute-done.20.near_ref, ...), custom_call_target="tpu_custom_call" | custom-call | flops 805306368 | bytes 2097152 | tf_op jit(solution)/shard_map/pallas_call | solution.py:41
  (54 shorter events, 0.5 us)
Async XLA Ops:
  0.6 11.2 %copy-start.13 = (bf16[512,256]{1,0:T(8,128)(2,1)S(1)}, bf16[512,256]{1,0:T(8,128)(2,1)}, u32[]{:S(2)}) copy-start(bf16[512,256]{1,0:T(8,128)(2,1)} %queries_ref.4) | copy-start | bytes 786436
  0.6 11.2 %copy-start.4 = (bf16[512,256]{1,0:T(8,128)(2,1)S(1)}, bf16[512,256]{1,0:T(8,128)(2,1)}, u32[]{:S(2)}) copy-start(bf16[512,256]{1,0:T(8,128)(2,1)} %keys_ref.5) | copy-start | bytes 786436
  0.7 11.2 %copy-start.5 = (bf16[512,256]{1,0:T(8,128)(2,1)S(1)}, bf16[512,256]{1,0:T(8,128)(2,1)}, u32[]{:S(2)}) copy-start(bf16[512,256]{1,0:T(8,128)(2,1)} %values_ref.5) | copy-start | bytes 786436
  0.7 11.9 %copy-start.7 = (bf16[512,256]{1,0:T(8,128)(2,1)S(1)}, bf16[512,256]{1,0:T(8,128)(2,1)}, u32[]{:S(2)}) copy-start(bf16[512,256]{1,0:T(8,128)(2,1)} %keys_ref.7) | copy-start | bytes 786436
  7.3 19.1 %copy-start.16 = (bf16[256,768]{1,0:T(8,128)(2,1)S(1)}, bf16[256,768]{1,0:T(8,128)(2,1)}, u32[]{:S(2)}) copy-start(bf16[256,768]{1,0:T(8,128)(2,1)} %get-tuple-element.20) | copy-start | bytes 1179652
  7.3 13.2 %collective-permute-start.12 = (bf16[256,768]{1,0:T(8,128)(2,1)}, bf16[256,768]{1,0:T(8,128)(2,1)S(1)}, u32[]{:S(2)}, u32[]{:S(2)}) collective-permute-start(bf16[256,768]{1,0:T(8,128)(2,1)} %get-tuple-element.26), channel_id=1, source_target_pairs={{0,8},{4,12},{8,0},{12,4},{16,24},{20,28},{24,16},{28,20},{1,9},{5... | collective-permute-start | bytes 1179656 | tf_op jit(solution)/shard_map/ppermute | solution.py:301
  10.4 16.1 %collective-permute-start.4 = (bf16[256,768]{1,0:T(8,128)(2,1)}, bf16[256,768]{1,0:T(8,128)(2,1)}, u32[]{:S(2)}, u32[]{:S(2)}) collective-permute-start(bf16[256,768]{1,0:T(8,128)(2,1)} %get-tuple-element.21), channel_id=1, source_target_pairs={{0,4},{4,0},{8,12},{12,8},{16,20},{20,16},{24,28},{28,24},{1,5},{5... | collective-permute-start | bytes 1179656 | tf_op jit(solution)/shard_map/ppermute | solution.py:301
  12.0 22.3 %collective-permute-start = (bf16[1536,128]{1,0:T(8,128)(2,1)S(1)}, bf16[1536,128]{1,0:T(8,128)(2,1)S(1)}, u32[]{:S(2)}, u32[]{:S(2)}) collective-permute-start(bf16[1536,128]{1,0:T(8,128)(2,1)S(1)} %shard_map.131), channel_id=1, source_target_pairs={{0,4},{4,0},{8,12},{12,8},{16,20},{20,16},{24,28},{28,24},{1,5},{5... | collective-permute-start | bytes 1179656 | tf_op jit(solution)/shard_map/ppermute | solution.py:301
  12.6 65.5 %collective-permute-start.10 = (bf16[512,256]{1,0:T(8,128)(2,1)S(1)}, bf16[512,256]{1,0:T(8,128)(2,1)S(1)}, u32[]{:S(2)}, u32[]{:S(2)}) collective-permute-start(bf16[512,256]{1,0:T(8,128)(2,1)S(1)} %copy-done.7), channel_id=1, source_target_pairs={{4,0},{8,4},{12,8},{16,12},{20,16},{24,20},{28,24},{5,1},{9,5},{13... | collective-permute-start | bytes 786440 | tf_op jit(solution)/shard_map/ppermute | solution.py:290
  21.6 16.4 %collective-permute-start.13 = (bf16[128,768]{1,0:T(8,128)(2,1)S(1)}, bf16[128,768]{1,0:T(8,128)(2,1)S(1)}, u32[]{:S(2)}, u32[]{:S(2)}) collective-permute-start(bf16[128,768]{1,0:T(8,128)(2,1)S(1)} %get-tuple-element.30), channel_id=1, source_target_pairs={{0,16},{4,20},{8,24},{12,28},{16,0},{20,4},{24,8},{28,12},{1,17},{... | collective-permute-start | bytes 589832 | tf_op jit(solution)/shard_map/ppermute | solution.py:301
  27.6 13.0 %collective-permute-start.5 = (bf16[128,768]{1,0:T(8,128)(2,1)S(1)}, bf16[128,768]{1,0:T(8,128)(2,1)S(1)}, u32[]{:S(2)}, u32[]{:S(2)}) collective-permute-start(bf16[128,768]{1,0:T(8,128)(2,1)S(1)} %get-tuple-element.32), channel_id=1, source_target_pairs={{0,8},{4,12},{8,0},{12,4},{16,24},{20,28},{24,16},{28,20},{1,9},{5... | collective-permute-start | bytes 589832 | tf_op jit(solution)/shard_map/ppermute | solution.py:301
  34.3 34.8 %collective-permute-start.1 = (bf16[1024,128]{1,0:T(8,128)(2,1)S(1)}, bf16[1024,128]{1,0:T(8,128)(2,1)S(1)}, u32[]{:S(2)}, u32[]{:S(2)}) collective-permute-start(bf16[1024,128]{1,0:T(8,128)(2,1)S(1)} %get-tuple-element.16.high_ref), channel_id=1, source_target_pairs={{0,8},{4,12},{8,16},{12,20},{16,24},{20,28},{1,9},{5,13},{9,17},{1... | collective-permute-start | bytes 786440 | tf_op jit(solution)/shard_map/ppermute | solution.py:290
  36.7 32.5 %collective-permute-start.2 = (bf16[1024,128]{1,0:T(8,128)(2,1)S(1)}, bf16[1024,128]{1,0:T(8,128)(2,1)S(1)}, u32[]{:S(2)}, u32[]{:S(2)}) collective-permute-start(bf16[1024,128]{1,0:T(8,128)(2,1)S(1)} %get-tuple-element.17.low_ref), channel_id=1, source_target_pairs={{8,0},{12,4},{16,8},{20,12},{24,16},{28,20},{9,1},{13,5},{17,9},{2... | collective-permute-start | bytes 786440 | tf_op jit(solution)/shard_map/ppermute | solution.py:290
  38.0 7.4 %collective-permute-start.14 = (bf16[64,768]{1,0:T(8,128)(2,1)S(1)}, bf16[64,768]{1,0:T(8,128)(2,1)S(1)}, u32[]{:S(2)}, u32[]{:S(2)}) collective-permute-start(bf16[64,768]{1,0:T(8,128)(2,1)S(1)} %get-tuple-element.34), channel_id=1, source_target_pairs={{0,4},{4,0},{8,12},{12,8},{16,20},{20,16},{24,28},{28,24},{1,5},{5... | collective-permute-start | bytes 294920 | tf_op jit(solution)/shard_map/ppermute | solution.py:301
  40.6 17.9 %collective-permute-start.6 = (bf16[64,768]{1,0:T(8,128)(2,1)S(1)}, bf16[64,768]{1,0:T(8,128)(2,1)S(1)}, u32[]{:S(2)}, u32[]{:S(2)}) collective-permute-start(bf16[64,768]{1,0:T(8,128)(2,1)S(1)} %get-tuple-element.22), channel_id=1, source_target_pairs={{0,16},{4,20},{8,24},{12,28},{16,0},{20,4},{24,8},{28,12},{1,17},{... | collective-permute-start | bytes 294920 | tf_op jit(solution)/shard_map/ppermute | solution.py:301
  45.5 13.2 %collective-permute-start.15 = (bf16[64,768]{1,0:T(8,128)(2,1)S(1)}, bf16[64,768]{1,0:T(8,128)(2,1)S(1)}, u32[]{:S(2)}, u32[]{:S(2)}) collective-permute-start(bf16[64,768]{1,0:T(8,128)(2,1)S(1)} %add_convert_fusion.3), channel_id=1, source_target_pairs={{0,4},{4,0},{8,12},{12,8},{16,20},{20,16},{24,28},{28,24},{1,5},{5... | collective-permute-start | bytes 294920 | tf_op jit(solution)/shard_map/ppermute | solution.py:301
  58.6 5.6 %collective-permute-start.7 = (bf16[64,768]{1,0:T(8,128)(2,1)S(1)}, bf16[64,768]{1,0:T(8,128)(2,1)S(1)}, u32[]{:S(2)}, u32[]{:S(2)}) collective-permute-start(bf16[64,768]{1,0:T(8,128)(2,1)S(1)} %add_convert_fusion.4), channel_id=1, source_target_pairs={{0,16},{4,20},{8,24},{12,28},{16,0},{20,4},{24,8},{28,12},{1,17},{... | collective-permute-start | bytes 294920 | tf_op jit(solution)/shard_map/ppermute | solution.py:301
  58.7 14.6 %collective-permute-start.16 = (bf16[128,768]{1,0:T(8,128)(2,1)S(1)}, bf16[128,768]{1,0:T(8,128)(2,1)}, u32[]{:S(2)}, u32[]{:S(2)}) collective-permute-start(bf16[128,768]{1,0:T(8,128)(2,1)S(1)} %pad_maximum_fusion.3), channel_id=1, source_target_pairs={{0,16},{4,20},{8,24},{12,28},{16,0},{20,4},{24,8},{28,12},{1,17},{... | collective-permute-start | bytes 589832 | tf_op jit(solution)/shard_map/ppermute | solution.py:301
  64.2 5.1 %copy-start.15 = (bf16[64,768]{1,0:T(8,128)(2,1)}, bf16[64,768]{1,0:T(8,128)(2,1)S(1)}, u32[]{:S(2)}) copy-start(bf16[64,768]{1,0:T(8,128)(2,1)S(1)} %collective-permute-done.7) | copy-start | bytes 294916
  64.2 14.6 %collective-permute-start.9 = (bf16[512,256]{1,0:T(8,128)(2,1)S(1)}, bf16[512,256]{1,0:T(8,128)(2,1)S(1)}, u32[]{:S(2)}, u32[]{:S(2)}) collective-permute-start(bf16[512,256]{1,0:T(8,128)(2,1)S(1)} %copy-done.7), channel_id=1, source_target_pairs={{0,4},{4,8},{8,12},{12,16},{16,20},{20,24},{24,28},{1,5},{5,9},{9,... | collective-permute-start | bytes 786440 | tf_op jit(solution)/shard_map/ppermute | solution.py:290
  69.1 27.4 %copy-start.14 = (bf16[1,256,512]{2,1,0:T(8,128)(2,1)S(1)}, bf16[1,256,512]{2,1,0:T(8,128)(2,1)}, u32[]{:S(2)}) copy-start(bf16[1,256,512]{2,1,0:T(8,128)(2,1)} %param.15) | copy-start | bytes 786436
  69.2 7.9 %collective-permute-start.8 = (bf16[128,768]{1,0:T(8,128)(2,1)S(1)}, bf16[128,768]{1,0:T(8,128)(2,1)S(1)}, u32[]{:S(2)}, u32[]{:S(2)}) collective-permute-start(bf16[128,768]{1,0:T(8,128)(2,1)S(1)} %pad_maximum_fusion.2), channel_id=1, source_target_pairs={{0,8},{4,12},{8,0},{12,4},{16,24},{20,28},{24,16},{28,20},{1,9},{5... | collective-permute-start | bytes 589832 | tf_op jit(solution)/shard_map/ppermute | solution.py:301
  73.2 23.8 %copy-start = (bf16[1,512,3,512]{3,1,2,0:T(8,128)(2,1)S(1)}, bf16[1,512,3,512]{3,1,2,0:T(8,128)(2,1)}, u32[]{:S(2)}) copy-start(bf16[1,512,3,512]{3,1,2,0:T(8,128)(2,1)} %param.19) | copy-start | bytes 4718596
  74.3 22.7 %collective-permute-start.17 = (bf16[256,768]{1,0:T(8,128)(2,1)S(1)}, bf16[256,768]{1,0:T(8,128)(2,1)}, u32[]{:S(2)}, u32[]{:S(2)}) collective-permute-start(bf16[256,768]{1,0:T(8,128)(2,1)S(1)} %pad_maximum_fusion.1.refs_2_), channel_id=1, source_target_pairs={{0,8},{4,12},{8,0},{12,4},{16,24},{20,28},{24,16},{28,20},{1,9},{5... | collective-permute-start | bytes 1179656 | tf_op jit(solution)/shard_map/ppermute | solution.py:301
  78.0 19.0 %copy-start.2 = (bf16[256,768]{1,0:T(8,128)(2,1)}, bf16[256,768]{1,0:T(8,128)(2,1)S(1)}, u32[]{:S(2)}) copy-start(bf16[256,768]{1,0:T(8,128)(2,1)S(1)} %pad_maximum_fusion.refs_0_) | copy-start | bytes 1179652
  78.0 0.7 copy-start.9
  78.8 0.7 copy-start.11
  79.5 17.6 %collective-permute-start.11 = (bf16[256,768]{1,0:T(8,128)(2,1)S(1)}, bf16[256,768]{1,0:T(8,128)(2,1)}, u32[]{:S(2)}, u32[]{:S(2)}) collective-permute-start(bf16[256,768]{1,0:T(8,128)(2,1)S(1)} %pad_maximum_fusion.refs_0_), channel_id=1, source_target_pairs={{0,4},{4,0},{8,12},{12,8},{16,20},{20,16},{24,28},{28,24},{1,5},{5... | collective-permute-start | bytes 1179656 | tf_op jit(solution)/shard_map/ppermute | solution.py:301
  82.5 21.2 %collective-permute-start.18 = (bf16[512,256]{1,0:T(8,128)(2,1)}, bf16[512,256]{1,0:T(8,128)(2,1)}, u32[]{:S(2)}, u32[]{:S(2)}) collective-permute-start(bf16[512,256]{1,0:T(8,128)(2,1)} %values_ref.7), channel_id=1, source_target_pairs={{0,4},{4,8},{8,12},{12,16},{16,20},{20,24},{24,28},{1,5},{5,9},{9,... | collective-permute-start | bytes 786440 | tf_op jit(solution)/shard_map/ppermute | solution.py:290
  85.1 18.6 %collective-permute-start.19 = (bf16[512,256]{1,0:T(8,128)(2,1)}, bf16[512,256]{1,0:T(8,128)(2,1)}, u32[]{:S(2)}, u32[]{:S(2)}) collective-permute-start(bf16[512,256]{1,0:T(8,128)(2,1)} %values_ref.7), channel_id=1, source_target_pairs={{4,0},{8,4},{12,8},{16,12},{20,16},{24,20},{28,24},{5,1},{9,5},{13... | collective-permute-start | bytes 786440 | tf_op jit(solution)/shard_map/ppermute | solution.py:290
  86.5 9.9 %collective-permute-start.3 = (bf16[512,128]{1,0:T(8,128)(2,1)S(1)}, bf16[512,128]{1,0:T(8,128)(2,1)S(1)}, u32[]{:S(2)}, u32[]{:S(2)}) collective-permute-start(bf16[512,128]{1,0:T(8,128)(2,1)S(1)} %get-tuple-element.19), channel_id=1, source_target_pairs={{0,4},{4,0},{8,12},{12,8},{16,20},{20,16},{24,28},{28,24},{1,5},{5... | collective-permute-start | bytes 393224 | tf_op jit(solution)/shard_map/ppermute | solution.py:301
  97.0 6.6 %copy-start.1 = (bf16[512,1024]{1,0:T(8,128)(2,1)S(1)}, bf16[512,1024]{1,0:T(8,128)(2,1)}, u32[]{:S(2)}) copy-start(bf16[512,1024]{1,0:T(8,128)(2,1)} %map_ref.3) | copy-start | bytes 3145732
  97.1 1.1 copy-start.3
  104.6 10.5 %copy-start.6 = (bf16[512,256]{1,0:T(8,128)(2,1)S(1)}, bf16[512,256]{1,0:T(8,128)(2,1)}, u32[]{:S(2)}) copy-start(bf16[512,256]{1,0:T(8,128)(2,1)} %queries_ref.5) | copy-start | bytes 786436
  104.7 10.5 %copy-start.8 = (bf16[512,256]{1,0:T(8,128)(2,1)S(1)}, bf16[512,256]{1,0:T(8,128)(2,1)}, u32[]{:S(2)}) copy-start(bf16[512,256]{1,0:T(8,128)(2,1)} %keys_ref.7) | copy-start | bytes 786436
  104.7 10.5 %copy-start.10 = (bf16[512,256]{1,0:T(8,128)(2,1)S(1)}, bf16[512,256]{1,0:T(8,128)(2,1)}, u32[]{:S(2)}) copy-start(bf16[512,256]{1,0:T(8,128)(2,1)} %copy-done.9) | copy-start | bytes 786436
  104.7 2.0 %collective-permute-start.20 = (bf16[2,512,256]{2,1,0:T(8,128)(2,1)S(1)}, bf16[2,512,256]{2,1,0:T(8,128)(2,1)S(1)}, u32[]{:S(2)}, u32[]{:S(2)}) collective-permute-start(bf16[2,512,256]{2,1,0:T(8,128)(2,1)S(1)} %shard_map.138), channel_id=1, source_target_pairs={{0,1},{1,0},{2,3},{3,2},{4,5},{5,4},{6,7},{7,6},{8,9},{9,8},{10,11... | collective-permute-start | bytes 1572872 | tf_op jit(solution)/shard_map/ppermute | solution.py:296
  104.8 10.4 %copy-start.12 = (bf16[512,256]{1,0:T(8,128)(2,1)S(1)}, bf16[512,256]{1,0:T(8,128)(2,1)}, u32[]{:S(2)}) copy-start(bf16[512,256]{1,0:T(8,128)(2,1)} %copy-done.11) | copy-start | bytes 786436
  106.7 8.4 %collective-permute-start.21 = (bf16[512,256]{1,0:T(8,128)(2,1)S(1)}, bf16[512,256]{1,0:T(8,128)(2,1)S(1)}, u32[]{:S(2)}, u32[]{:S(2)}) collective-permute-start(bf16[512,256]{1,0:T(8,128)(2,1)S(1)} %fusion), channel_id=1, source_target_pairs={{0,2},{1,3},{2,0},{3,1},{4,6},{5,7},{6,4},{7,5},{8,10},{9,11},{10,... | collective-permute-start | bytes 786440 | tf_op jit(solution)/shard_map/ppermute | solution.py:296

commit v6 on v5

--- a/solution.py
+++ b/solution.py
@@ -195,8 +195,8 @@
     ).astype(BF16)
 
 
-def second_kernel(edge_ref, queries_ref, keep_ref, near_ref, far_ref, keys_prev_ref, keys_ref, keys_next_ref,
-                  values_prev_ref, values_ref, values_next_ref, out_ref):
+def second_kernel(edge_ref, queries_ref, keep_ref, near_ref, far_ref, prev_ref, keys_ref, values_ref, next_ref,
+                  out_ref):
     count = keys_ref.shape[0]
     for index in range(count // TILE):
         low, high = index * TILE, (index + 1) * TILE
@@ -213,8 +213,8 @@
             heads.append(
                 attend_rows(
                     edge_ref[0, 0], edge_ref[0, 1], query[:, cols],
-                    keys_prev_ref[low:, cols], keys_ref[:, cols], keys_next_ref[:high, cols],
-                    values_prev_ref[low:, cols], values_ref[:, cols], values_next_ref[:high, cols],
+                    prev_ref[low:count, cols], keys_ref[:, cols], next_ref[:high, cols],
+                    prev_ref[count + low:, cols], values_ref[:, cols], next_ref[count:count + high, cols],
                 )
             )
         both = jnp.concatenate(heads, axis=1)
@@ -305,7 +305,13 @@
     return lax.optimization_barrier((value, others))[0]
 
 
-def sum_over_seq(chunks, orders, waits):
+def sum_started(chunks, orders):
+    return [keep for keep, _ in chunks], [
+        seq_swap(send, order[0]) for (_, send), order in zip(chunks, orders)
+    ]
+
+
+def sum_over_seq(keeps, found, orders, waits):
     turns = len(orders[0])
 
     def swapped(values, stage, turn):
@@ -314,20 +320,15 @@
             values[0] = after(values[0], waits[stage])
         return [seq_swap(value, order[turn]) for value, order in zip(values, orders)]
 
-    keeps = [keep for keep, _ in chunks]
-    sends = [send for _, send in chunks]
-    for turn in range(turns):
-        found = swapped(sends, turn, turn)
+    for turn in range(1, turns):
         sends, rest = [], []
         for keep, new in zip(keeps, found):
-            if turn == turns - 1:
-                rest.append((keep.astype(F32) + new.astype(F32)).astype(BF16))
-                continue
             half = keep.shape[0] // 2
             sends.append((keep[half:].astype(F32) + new[half:].astype(F32)).astype(BF16))
             rest.append(lax.optimization_barrier(keep[:half].astype(F32) + new[:half].astype(F32)))
         keeps = rest
-    held = [(keep,) for keep in keeps]
+        found = swapped(sends, turn, turn)
+    held = [((keep.astype(F32) + new.astype(F32)).astype(BF16),) for keep, new in zip(keeps, found)]
     for turn in reversed(range(turns)):
         whole = [jnp.concatenate(parts) if len(parts) > 1 else parts[0] for parts in held]
         found = swapped(whole, 2 * turns - 1 - turn, turn)
@@ -410,17 +411,19 @@
         scalars=1,
     )
 
-    keys_prev, keys_next = seq_shift(keys_second, 1), seq_shift(keys_second, -1)
-    values_prev, values_next = seq_shift(values_second, 1), seq_shift(values_second, -1)
+    both_second = jnp.concatenate([keys_second, values_second])
     if halving:
         stages = 2 * len(bits)
+        started = sum_started([gradients[:2], gradients[2:]], orders)
+        both_second = after(both_second, started[1])
+        prev_second, next_second = seq_shift(both_second, 1), seq_shift(both_second, -1)
         waits = {
-            len(bits) - 1: (low_block, high_block),
-            stages - 2: (prev_first, next_first),
-            stages - 1: (keep_first, send_first, keys_prev, keys_next),
+            stages - 2: (prev_first, next_first, prev_second),
+            stages - 1: (keep_first, send_first, next_second),
         }
-        gathered = sum_over_seq([gradients[:2], gradients[2:]], orders, waits)
+        gathered = sum_over_seq(*started, orders, waits)
     else:
+        prev_second, next_second = seq_shift(both_second, 1), seq_shift(both_second, -1)
         gathered = lax.psum(gradients, "seq")
 
     own_rows = hidden_size >> len(orders[0])
@@ -434,8 +437,6 @@
     if not halving:
         share_rows = hidden_size // seq_count
         own_new = lax.dynamic_slice_in_dim(own_new, seq_place * share_rows, share_rows, 1)
-
-    fast_out = after(fast_out, (values_prev, values_next))
 
     def mixed_for(low_bit):
         far = (head_place // 2) ^ 1
@@ -458,7 +459,7 @@
         second_kernel,
         shape((rows, width), BF16),
         (edges, queries_second, keep_part, near_part, far_part,
-         keys_prev, keys_second, keys_next, values_prev, values_second, values_next),
+         prev_second, keys_second, values_second, next_second),
         scalars=1,
         cost=(12 * rows * rows * width, 16 * rows * width),
     )

time: 122 us -> 135 us (1.11)
  waiting for transfers between devices: 43.1 us -> 76 us
  starting transfers between devices: 44.9 us -> 24.4 us
    ppermute x14, waiting for transfers between devices: 35.5 us -> 67.9 us  [seq_swap(): lax.ppermute(value, 'seq', [(i, i ^ step) for i in range(lax.axis_size('s...]
    ppermute x14, starting transfers between devices: 29.3 us -> 11.4 us  [seq_swap(): lax.ppermute(value, 'seq', [(i, i ^ step) for i in range(lax.axis_size('s...]
    ppermute x6 -> x4, starting transfers between devices: 13.9 us -> 11.5 us  [seq_shift(): lax.ppermute(value, 'seq', [(i, i + step) for i in range(peers) if 0 <= i...]
    unnamed x34 -> x52, local copies, waits for them, and re-layouts: 2.58 us -> 2.87 us
  transfers between devices with their start and end apart: 22 -> 20, of which waited for: 9 -> 14; matrix products, arithmetic and copies ran while one was open for 4% -> 4% of each run, Pallas kernels for 9% -> 5%
where the time goes in v6:
time: 135 us
  waiting for transfers between devices  76 us (56%)
  Pallas kernels  25 us (19%)
  starting transfers between devices  24.4 us (18%)
  other arithmetic  5.34 us (4%)
  local copies, waits for them, and re-layouts  2.96 us (2%)
    ppermute x14, waiting for transfers between devices, seq_swap(): lax.ppermute(value, 'seq', [(i, i ^ step) for i in range(lax.axis_size('s...  67.9 us
    pallas_call x9, Pallas kernels, call(): pl.pallas_call(body, out_shape=out_shapes, in_specs=in_specs, out_specs=j...  25 us
    ppermute x4, starting transfers between devices, seq_shift(): lax.ppermute(value, 'seq', [(i, i + step) for i in range(peers) if 0 <= i...  11.5 us
    ppermute x14, starting transfers between devices, seq_swap(): lax.ppermute(value, 'seq', [(i, i ^ step) for i in range(lax.axis_size('s...  11.4 us
    ppermute x2, waiting for transfers between devices, head_swap(): lax.ppermute(value, 'head', [(i, i ^ bit) for i in range(lax.axis_size('h...  8.05 us
    unnamed x52, local copies, waits for them, and re-layouts  2.87 us
    concatenate x4, other arithmetic, sum_over_seq(): jnp.concatenate(parts)  2.7 us
  transfers between devices with their start and end apart: 20, of which 14 were waited for; matrix products, arithmetic and copies ran while one was open for 4% of the time, Pallas kernels for 5%

profile of v6, /device:TPU:0, one launch (start us, length us, event | category | flops | bytes accessed | tf_op | source)
XLA Modules:
  0.0 134.7 jit_solution(17822110091226111584)
XLA Ops:
  0.7 6.6 %shard_map.135 = (bf16[256,768]{1,0:T(8,128)(2,1)}, bf16[256,768]{1,0:T(8,128)(2,1)}, bf16[256,768]{1,0:T(8,128)(2,1)}, bf16[256,768]{1,0:T(8,128)(2,1)}) custom-call(s32[1,1]{1,0:T(1,128)} %bitcast.7.place_ref, f32[1,512]{1,0:T(1,128)} %bitcast.27, bf16[512,512]{1,0:T(8,128)(2,1)} %keys_ref.6, bf16[512,512]{1,0:T(8,128)(2,1)} %values_ref.6, ...), custom_call_target="tpu_custom_call" | custom-call | flops 1000 | bytes 1000 | tf_op jit(solution)/shard_map/pallas_call | solution.py:41
  7.3 3.0 %collective-permute-start.4 = (bf16[256,768]{1,0:T(8,128)(2,1)}, bf16[256,768]{1,0:T(8,128)(2,1)S(1)}, u32[]{:S(2)}, u32[]{:S(2)}) collective-permute-start(bf16[256,768]{1,0:T(8,128)(2,1)} %get-tuple-element.20), channel_id=1, source_target_pairs={{0,4},{4,0},{8,12},{12,8},{16,20},{20,16},{24,28},{28,24},{1,5},{5... | collective-permute-start | bytes 1179656 | tf_op jit(solution)/shard_map/ppermute | solution.py:301
  10.3 1.6 %collective-permute-start.8 = (bf16[256,768]{1,0:T(8,128)(2,1)}, bf16[256,768]{1,0:T(8,128)(2,1)S(1)}, u32[]{:S(2)}, u32[]{:S(2)}) collective-permute-start(bf16[256,768]{1,0:T(8,128)(2,1)} %get-tuple-element.21), channel_id=1, source_target_pairs={{0,8},{4,12},{8,0},{12,4},{16,24},{20,28},{24,16},{28,20},{1,9},{5... | collective-permute-start | bytes 1179656 | tf_op jit(solution)/shard_map/ppermute | solution.py:301
  11.9 0.6 collective-permute-start
  12.5 0.8 pad_maximum_fusion
  13.3 7.1 %collective-permute-done.4 = bf16[256,768]{1,0:T(8,128)(2,1)S(1)} collective-permute-done((bf16[256,768]{1,0:T(8,128)(2,1)}, bf16[256,768]{1,0:T(8,128)(2,1)S(1)}, u32[]{:S(2)}, u32[]{:S(2)}) %collective-permute-start.4) | collective-permute-done | bytes 393248 | tf_op jit(solution)/shard_map/ppermute | solution.py:301
  20.4 0.6 collective-permute-done.8
  21.1 0.1 copy-done.23
  21.2 4.0 %collective-permute-start.9 = (bf16[1024,256]{1,0:T(8,128)(2,1)}, bf16[1024,256]{1,0:T(8,128)(2,1)S(1)}, u32[]{:S(2)}, u32[]{:S(2)}) collective-permute-start(bf16[1024,256]{1,0:T(8,128)(2,1)} %pad_maximum_fusion), channel_id=1, source_target_pairs={{0,4},{4,8},{8,12},{12,16},{16,20},{20,24},{24,28},{1,5},{5,9},{9,... | collective-permute-start | bytes 1572872 | tf_op jit(solution)/shard_map/ppermute | solution.py:290
  25.2 1.4 %collective-permute-start.11 = (bf16[1024,256]{1,0:T(8,128)(2,1)}, bf16[1024,256]{1,0:T(8,128)(2,1)S(1)}, u32[]{:S(2)}, u32[]{:S(2)}) collective-permute-start(bf16[1024,256]{1,0:T(8,128)(2,1)} %pad_maximum_fusion), channel_id=1, source_target_pairs={{4,0},{8,4},{12,8},{16,12},{20,16},{24,20},{28,24},{5,1},{9,5},{13... | collective-permute-start | bytes 1572872 | tf_op jit(solution)/shard_map/ppermute | solution.py:290
  26.6 12.9 %collective-permute-done.other_ref = bf16[1536,128]{1,0:T(8,128)(2,1)S(1)} collective-permute-done((bf16[1536,128]{1,0:T(8,128)(2,1)S(1)}, bf16[1536,128]{1,0:T(8,128)(2,1)S(1)}, u32[]{:S(2)}, u32[]{:S(2)}) %collective-permute-start) | collective-permute-done | bytes 393248 | tf_op jit(solution)/shard_map/ppermute | solution.py:301
  39.6 4.6 %collective-permute-start.1 = (bf16[1024,128]{1,0:T(8,128)(2,1)S(1)}, bf16[1024,128]{1,0:T(8,128)(2,1)S(1)}, u32[]{:S(2)}, u32[]{:S(2)}) collective-permute-start(bf16[1024,128]{1,0:T(8,128)(2,1)S(1)} %get-tuple-element.15.high_ref), channel_id=1, source_target_pairs={{0,8},{4,12},{8,16},{12,20},{16,24},{20,28},{1,9},{5,13},{9,17},{1... | collective-permute-start | bytes 786440 | tf_op jit(solution)/shard_map/ppermute | solution.py:290
  44.2 1.5 %collective-permute-start.2 = (bf16[1024,128]{1,0:T(8,128)(2,1)S(1)}, bf16[1024,128]{1,0:T(8,128)(2,1)S(1)}, u32[]{:S(2)}, u32[]{:S(2)}) collective-permute-start(bf16[1024,128]{1,0:T(8,128)(2,1)S(1)} %get-tuple-element.16.low_ref), channel_id=1, source_target_pairs={{8,0},{12,4},{16,8},{20,12},{24,16},{28,20},{9,1},{13,5},{17,9},{2... | collective-permute-start | bytes 786440 | tf_op jit(solution)/shard_map/ppermute | solution.py:290
  45.7 1.3 add_convert_fusion.1
  47.0 3.7 %collective-permute-start.13 = (bf16[128,768]{1,0:T(8,128)(2,1)S(1)}, bf16[128,768]{1,0:T(8,128)(2,1)S(1)}, u32[]{:S(2)}, u32[]{:S(2)}) collective-permute-start(bf16[128,768]{1,0:T(8,128)(2,1)S(1)} %get-tuple-element.28), channel_id=1, source_target_pairs={{0,16},{4,20},{8,24},{12,28},{16,0},{20,4},{24,8},{28,12},{1,17},{... | collective-permute-start | bytes 589832 | tf_op jit(solution)/shard_map/ppermute | solution.py:301
  50.7 0.1 add_convert_fusion.2
  50.8 10.6 %collective-permute-done.13 = bf16[128,768]{1,0:T(8,128)(2,1)S(1)} collective-permute-done((bf16[128,768]{1,0:T(8,128)(2,1)S(1)}, bf16[128,768]{1,0:T(8,128)(2,1)S(1)}, u32[]{:S(2)}, u32[]{:S(2)}) %collective-permute-start.13) | collective-permute-done | bytes 196640 | tf_op jit(solution)/shard_map/ppermute | solution.py:301
  61.4 5.6 %collective-permute-done.5 = bf16[128,768]{1,0:T(8,128)(2,1)S(1)} collective-permute-done((bf16[128,768]{1,0:T(8,128)(2,1)S(1)}, bf16[128,768]{1,0:T(8,128)(2,1)S(1)}, u32[]{:S(2)}, u32[]{:S(2)}) %collective-permute-start.5) | collective-permute-done | bytes 196640 | tf_op jit(solution)/shard_map/ppermute | solution.py:301
  67.1 4.6 %collective-permute-done.14 = bf16[64,768]{1,0:T(8,128)(2,1)S(1)} collective-permute-done((bf16[64,768]{1,0:T(8,128)(2,1)S(1)}, bf16[64,768]{1,0:T(8,128)(2,1)S(1)}, u32[]{:S(2)}, u32[]{:S(2)}) %collective-permute-start.14) | collective-permute-done | bytes 98336 | tf_op jit(solution)/shard_map/ppermute | solution.py:301
  71.7 7.2 %collective-permute-done.6 = bf16[64,768]{1,0:T(8,128)(2,1)S(1)} collective-permute-done((bf16[64,768]{1,0:T(8,128)(2,1)S(1)}, bf16[64,768]{1,0:T(8,128)(2,1)S(1)}, u32[]{:S(2)}, u32[]{:S(2)}) %collective-permute-start.6) | collective-permute-done | bytes 98336 | tf_op jit(solution)/shard_map/ppermute | solution.py:301
  78.9 4.6 %collective-permute-done.15 = bf16[64,768]{1,0:T(8,128)(2,1)S(1)} collective-permute-done((bf16[64,768]{1,0:T(8,128)(2,1)S(1)}, bf16[64,768]{1,0:T(8,128)(2,1)S(1)}, u32[]{:S(2)}, u32[]{:S(2)}) %collective-permute-start.15) | collective-permute-done | bytes 98336 | tf_op jit(solution)/shard_map/ppermute | solution.py:301
  83.5 0.7 pad_maximum_fusion.4
  84.2 4.8 %collective-permute-done.7 = bf16[64,768]{1,0:T(8,128)(2,1)S(1)} collective-permute-done((bf16[64,768]{1,0:T(8,128)(2,1)S(1)}, bf16[64,768]{1,0:T(8,128)(2,1)S(1)}, u32[]{:S(2)}, u32[]{:S(2)}) %collective-permute-start.7) | collective-permute-done | bytes 98336 | tf_op jit(solution)/shard_map/ppermute | solution.py:301
  89.0 0.1 collective-permute-start.16
  89.1 0.1 pad_maximum_fusion.5
  89.2 0.1 reshape.26.edge_ref
  89.4 0.8 copy-done.10
  90.1 0.4 collective-permute-start.10
  90.5 4.6 %shard_map.133 = (bf16[512,128]{1,0:T(8,128)(2,1)S(1)}, bf16[512,128]{1,0:T(8,128)(2,1)}) custom-call(f32[2,2]{1,0:T(2,128)S(1)} %reshape.26.edge_ref, s32[1,1]{1,0:T(1,128)} %bitcast.10.side_ref, bf16[512,256]{1,0:T(8,128)(2,1)S(1)} %copy-done.15, bf16[1536,128]{1,0:T(8,128)(2,1)S(1)} %collective-permute-done.other_ref, ...), custom_call_target="tpu_custom_call" | custom-call | flops 805306368 | bytes 2097152 | tf_op jit(solution)/shard_map/pallas_call | solution.py:41
  95.1 2.2 %collective-permute-done.16 = bf16[128,768]{1,0:T(8,128)(2,1)} collective-permute-done((bf16[128,768]{1,0:T(8,128)(2,1)}, bf16[128,768]{1,0:T(8,128)(2,1)}, u32[]{:S(2)}, u32[]{:S(2)}) %collective-permute-start.16) | collective-permute-done | bytes 196640 | tf_op jit(solution)/shard_map/ppermute | solution.py:301
  97.4 1.0 pad_maximum_fusion.2.refs_2_
  98.5 0.7 collective-permute-done.10
  99.2 1.0 pad_maximum_fusion.1.refs_0_
  100.2 0.8 copy-done.12
  101.0 1.5 %collective-permute-start.12 = (bf16[256,768]{1,0:T(8,128)(2,1)S(1)}, bf16[256,768]{1,0:T(8,128)(2,1)}, u32[]{:S(2)}, u32[]{:S(2)}) collective-permute-start(bf16[256,768]{1,0:T(8,128)(2,1)S(1)} %pad_maximum_fusion.1.refs_0_), channel_id=1, source_target_pairs={{0,4},{4,0},{8,12},{12,8},{16,20},{20,16},{24,28},{28,24},{1,5},{5... | collective-permute-start | bytes 1179656 | tf_op jit(solution)/shard_map/ppermute | solution.py:301
  102.4 0.6 collective-permute-start.3
  103.0 0.1 add_bitcast_fusion.1.place_ref
  103.1 7.1 %collective-permute-done.3.other_ref = bf16[512,128]{1,0:T(8,128)(2,1)S(1)} collective-permute-done((bf16[512,128]{1,0:T(8,128)(2,1)}, bf16[512,128]{1,0:T(8,128)(2,1)S(1)}, u32[]{:S(2)}, u32[]{:S(2)}) %collective-permute-start.3) | collective-permute-done | bytes 131104 | tf_op jit(solution)/shard_map/ppermute | solution.py:301
  110.2 0.5 shard_map.134.query_ref
  110.7 1.1 copy-done.3
  111.8 5.5 %shard_map.136 = (bf16[3,64,512]{2,1,0:T(8,128)(2,1)}, bf16[512,512]{1,0:T(8,128)(2,1)S(1)}) custom-call(s32[1,1]{1,0:T(1,128)} %bitcast.7.place_ref, bf16[3,512,512]{2,1,0:T(8,128)(2,1)S(1)} %bitcast.25, bf16[512,512]{1,0:T(8,128)(2,1)S(1)} %shard_map.134.query_ref, bf16[256,768]{1,0:T(8,128)(2,1)S(1)} %copy-done.3, ...), custom_call_target="tpu_custom_call" | custom-call | flops 1000 | bytes 1000 | tf_op jit(solution)/shard_map/pallas_call | solution.py:41
  117.3 1.8 %shard_map.138 = bf16[2,512,256]{2,1,0:T(8,128)(2,1)} custom-call(s32[1,2]{1,0:T(1,128)S(1)} %add_bitcast_fusion.1.place_ref, bf16[512,512]{1,0:T(8,128)(2,1)S(1)} %get-tuple-element.26.fast_ref, bf16[512,1024]{1,0:T(8,128)(2,1)S(1)} %copy-done.1), custom_call_target="tpu_custom_call" | custom-call | flops 1000 | bytes 1000 | tf_op jit(solution)/shard_map/pallas_call | solution.py:41
  119.2 0.1 add_bitcast_fusion.place_ref
  119.3 1.0 shard_map.137.keep_ref
  120.3 1.0 collective-permute-done.18.near_ref
  121.4 1.4 %collective-permute-start.19 = (bf16[512,256]{1,0:T(8,128)(2,1)S(1)}, bf16[512,256]{1,0:T(8,128)(2,1)S(1)}, u32[]{:S(2)}, u32[]{:S(2)}) collective-permute-start(bf16[512,256]{1,0:T(8,128)(2,1)S(1)} %fusion), channel_id=1, source_target_pairs={{0,2},{1,3},{2,0},{3,1},{4,6},{5,7},{6,4},{7,5},{8,10},{9,11},{10,... | collective-permute-start | bytes 786440 | tf_op jit(solution)/shard_map/ppermute | solution.py:296
  122.8 7.0 %collective-permute-done.19.far_ref = bf16[512,256]{1,0:T(8,128)(2,1)S(1)} collective-permute-done((bf16[512,256]{1,0:T(8,128)(2,1)S(1)}, bf16[512,256]{1,0:T(8,128)(2,1)S(1)}, u32[]{:S(2)}, u32[]{:S(2)}) %collective-permute-start.19) | collective-permute-done | bytes 262176 | tf_op jit(solution)/shard_map/ppermute | solution.py:296
  129.8 4.9 %shard_map.139 = bf16[512,256]{1,0:T(8,128)(2,1)} custom-call(f32[2,2]{1,0:T(2,128)S(1)} %reshape.26.edge_ref, bf16[512,256]{1,0:T(8,128)(2,1)S(1)} %copy-done.14, bf16[2,512,256]{2,1,0:T(8,128)(2,1)S(1)} %shard_map.137.keep_ref, bf16[2,512,256]{2,1,0:T(8,128)(2,1)S(1)} %collective-permute-done.18.near_ref, ...), custom_call_target="tpu_custom_call" | custom-call | flops 805306368 | bytes 2097152 | tf_op jit(solution)/shard_map/pallas_call | solution.py:41
  (69 shorter events, 0.6 us)
Async XLA Ops:
  0.6 11.2 %copy-start.15 = (bf16[512,256]{1,0:T(8,128)(2,1)S(1)}, bf16[512,256]{1,0:T(8,128)(2,1)}, u32[]{:S(2)}) copy-start(bf16[512,256]{1,0:T(8,128)(2,1)} %queries_ref.4) | copy-start | bytes 786436
  0.6 11.2 %copy-start.4 = (bf16[512,256]{1,0:T(8,128)(2,1)S(1)}, bf16[512,256]{1,0:T(8,128)(2,1)}, u32[]{:S(2)}) copy-start(bf16[512,256]{1,0:T(8,128)(2,1)} %keys_ref.5) | copy-start | bytes 786436
  0.7 11.2 %copy-start.5 = (bf16[512,256]{1,0:T(8,128)(2,1)S(1)}, bf16[512,256]{1,0:T(8,128)(2,1)}, u32[]{:S(2)}) copy-start(bf16[512,256]{1,0:T(8,128)(2,1)} %values_ref.5) | copy-start | bytes 786436
  0.7 11.9 %copy-start.6 = (bf16[512,256]{1,0:T(8,128)(2,1)S(1)}, bf16[512,256]{1,0:T(8,128)(2,1)}, u32[]{:S(2)}) copy-start(bf16[512,256]{1,0:T(8,128)(2,1)} %values_ref.7) | copy-start | bytes 786436
  0.7 11.8 %copy-start.8 = (bf16[512,256]{1,0:T(8,128)(2,1)S(1)}, bf16[512,256]{1,0:T(8,128)(2,1)}, u32[]{:S(2)}) copy-start(bf16[512,256]{1,0:T(8,128)(2,1)} %keys_ref.7) | copy-start | bytes 786436
  7.3 13.1 %collective-permute-start.4 = (bf16[256,768]{1,0:T(8,128)(2,1)}, bf16[256,768]{1,0:T(8,128)(2,1)S(1)}, u32[]{:S(2)}, u32[]{:S(2)}) collective-permute-start(bf16[256,768]{1,0:T(8,128)(2,1)} %get-tuple-element.20), channel_id=1, source_target_pairs={{0,4},{4,0},{8,12},{12,8},{16,20},{20,16},{24,28},{28,24},{1,5},{5... | collective-permute-start | bytes 1179656 | tf_op jit(solution)/shard_map/ppermute | solution.py:301
  10.3 10.8 %collective-permute-start.8 = (bf16[256,768]{1,0:T(8,128)(2,1)}, bf16[256,768]{1,0:T(8,128)(2,1)S(1)}, u32[]{:S(2)}, u32[]{:S(2)}) collective-permute-start(bf16[256,768]{1,0:T(8,128)(2,1)} %get-tuple-element.21), channel_id=1, source_target_pairs={{0,8},{4,12},{8,0},{12,4},{16,24},{20,28},{24,16},{28,20},{1,9},{5... | collective-permute-start | bytes 1179656 | tf_op jit(solution)/shard_map/ppermute | solution.py:301
  11.9 27.6 %collective-permute-start = (bf16[1536,128]{1,0:T(8,128)(2,1)S(1)}, bf16[1536,128]{1,0:T(8,128)(2,1)S(1)}, u32[]{:S(2)}, u32[]{:S(2)}) collective-permute-start(bf16[1536,128]{1,0:T(8,128)(2,1)S(1)} %shard_map.131), channel_id=1, source_target_pairs={{0,4},{4,0},{8,12},{12,8},{16,20},{20,16},{24,28},{28,24},{1,5},{5... | collective-permute-start | bytes 1179656 | tf_op jit(solution)/shard_map/ppermute | solution.py:301
  12.5 38.2 %copy-start.22 = (bf16[256,768]{1,0:T(8,128)(2,1)S(1)}, bf16[256,768]{1,0:T(8,128)(2,1)}, u32[]{:S(2)}) copy-start(bf16[256,768]{1,0:T(8,128)(2,1)} %get-tuple-element.19) | copy-start | bytes 1179652
  20.4 0.7 copy-start.23
  21.2 5.4 %copy-start.25 = (bf16[256,768]{1,0:T(8,128)(2,1)}, bf16[256,768]{1,0:T(8,128)(2,1)S(1)}, u32[]{:S(2)}) copy-start(bf16[256,768]{1,0:T(8,128)(2,1)S(1)} %collective-permute-done.8) | copy-start | bytes 1179652
  21.2 68.2 %collective-permute-start.9 = (bf16[1024,256]{1,0:T(8,128)(2,1)}, bf16[1024,256]{1,0:T(8,128)(2,1)S(1)}, u32[]{:S(2)}, u32[]{:S(2)}) collective-permute-start(bf16[1024,256]{1,0:T(8,128)(2,1)} %pad_maximum_fusion), channel_id=1, source_target_pairs={{0,4},{4,8},{8,12},{12,16},{16,20},{20,24},{24,28},{1,5},{5,9},{9,... | collective-permute-start | bytes 1572872 | tf_op jit(solution)/shard_map/ppermute | solution.py:290
  25.2 25.6 %copy-start.24 = (bf16[256,768]{1,0:T(8,128)(2,1)S(1)}, bf16[256,768]{1,0:T(8,128)(2,1)}, u32[]{:S(2)}) copy-start(bf16[256,768]{1,0:T(8,128)(2,1)} %copy-done.23) | copy-start | bytes 1179652
  25.2 75.0 %collective-permute-start.11 = (bf16[1024,256]{1,0:T(8,128)(2,1)}, bf16[1024,256]{1,0:T(8,128)(2,1)S(1)}, u32[]{:S(2)}, u32[]{:S(2)}) collective-permute-start(bf16[1024,256]{1,0:T(8,128)(2,1)} %pad_maximum_fusion), channel_id=1, source_target_pairs={{4,0},{8,4},{12,8},{16,12},{20,16},{24,20},{28,24},{5,1},{9,5},{13... | collective-permute-start | bytes 1572872 | tf_op jit(solution)/shard_map/ppermute | solution.py:290
  39.6 49.7 %collective-permute-start.1 = (bf16[1024,128]{1,0:T(8,128)(2,1)S(1)}, bf16[1024,128]{1,0:T(8,128)(2,1)S(1)}, u32[]{:S(2)}, u32[]{:S(2)}) collective-permute-start(bf16[1024,128]{1,0:T(8,128)(2,1)S(1)} %get-tuple-element.15.high_ref), channel_id=1, source_target_pairs={{0,8},{4,12},{8,16},{12,20},{16,24},{20,28},{1,9},{5,13},{9,17},{1... | collective-permute-start | bytes 786440 | tf_op jit(solution)/shard_map/ppermute | solution.py:290
  44.2 45.1 %collective-permute-start.2 = (bf16[1024,128]{1,0:T(8,128)(2,1)S(1)}, bf16[1024,128]{1,0:T(8,128)(2,1)S(1)}, u32[]{:S(2)}, u32[]{:S(2)}) collective-permute-start(bf16[1024,128]{1,0:T(8,128)(2,1)S(1)} %get-tuple-element.16.low_ref), channel_id=1, source_target_pairs={{8,0},{12,4},{16,8},{20,12},{24,16},{28,20},{9,1},{13,5},{17,9},{2... | collective-permute-start | bytes 786440 | tf_op jit(solution)/shard_map/ppermute | solution.py:290
  47.0 14.4 %collective-permute-start.13 = (bf16[128,768]{1,0:T(8,128)(2,1)S(1)}, bf16[128,768]{1,0:T(8,128)(2,1)S(1)}, u32[]{:S(2)}, u32[]{:S(2)}) collective-permute-start(bf16[128,768]{1,0:T(8,128)(2,1)S(1)} %get-tuple-element.28), channel_id=1, source_target_pairs={{0,16},{4,20},{8,24},{12,28},{16,0},{20,4},{24,8},{28,12},{1,17},{... | collective-permute-start | bytes 589832 | tf_op jit(solution)/shard_map/ppermute | solution.py:301
  61.4 5.7 %collective-permute-start.5 = (bf16[128,768]{1,0:T(8,128)(2,1)S(1)}, bf16[128,768]{1,0:T(8,128)(2,1)S(1)}, u32[]{:S(2)}, u32[]{:S(2)}) collective-permute-start(bf16[128,768]{1,0:T(8,128)(2,1)S(1)} %get-tuple-element.30), channel_id=1, source_target_pairs={{0,8},{4,12},{8,0},{12,4},{16,24},{20,28},{24,16},{28,20},{1,9},{5... | collective-permute-start | bytes 589832 | tf_op jit(solution)/shard_map/ppermute | solution.py:301
  67.1 4.6 %collective-permute-start.14 = (bf16[64,768]{1,0:T(8,128)(2,1)S(1)}, bf16[64,768]{1,0:T(8,128)(2,1)S(1)}, u32[]{:S(2)}, u32[]{:S(2)}) collective-permute-start(bf16[64,768]{1,0:T(8,128)(2,1)S(1)} %get-tuple-element.32), channel_id=1, source_target_pairs={{0,4},{4,0},{8,12},{12,8},{16,20},{20,16},{24,28},{28,24},{1,5},{5... | collective-permute-start | bytes 294920 | tf_op jit(solution)/shard_map/ppermute | solution.py:301
  71.7 7.2 %collective-permute-start.6 = (bf16[64,768]{1,0:T(8,128)(2,1)S(1)}, bf16[64,768]{1,0:T(8,128)(2,1)S(1)}, u32[]{:S(2)}, u32[]{:S(2)}) collective-permute-start(bf16[64,768]{1,0:T(8,128)(2,1)S(1)} %get-tuple-element.34), channel_id=1, source_target_pairs={{0,16},{4,20},{8,24},{12,28},{16,0},{20,4},{24,8},{28,12},{1,17},{... | collective-permute-start | bytes 294920 | tf_op jit(solution)/shard_map/ppermute | solution.py:301
  71.7 18.8 %copy-start.18 = (bf16[64,768]{1,0:T(8,128)(2,1)}, bf16[64,768]{1,0:T(8,128)(2,1)S(1)}, u32[]{:S(2)}) copy-start(bf16[64,768]{1,0:T(8,128)(2,1)S(1)} %add_convert_fusion.3) | copy-start | bytes 294916
  78.9 4.6 %collective-permute-start.15 = (bf16[64,768]{1,0:T(8,128)(2,1)S(1)}, bf16[64,768]{1,0:T(8,128)(2,1)S(1)}, u32[]{:S(2)}, u32[]{:S(2)}) collective-permute-start(bf16[64,768]{1,0:T(8,128)(2,1)S(1)} %add_convert_fusion.3), channel_id=1, source_target_pairs={{0,4},{4,0},{8,12},{12,8},{16,20},{20,16},{24,28},{28,24},{1,5},{5... | collective-permute-start | bytes 294920 | tf_op jit(solution)/shard_map/ppermute | solution.py:301
  78.9 11.6 %copy-start.17 = (bf16[64,768]{1,0:T(8,128)(2,1)}, bf16[64,768]{1,0:T(8,128)(2,1)S(1)}, u32[]{:S(2)}) copy-start(bf16[64,768]{1,0:T(8,128)(2,1)S(1)} %add_convert_fusion.4) | copy-start | bytes 294916
  83.5 5.8 %copy-start.20 = (bf16[64,768]{1,0:T(8,128)(2,1)}, bf16[64,768]{1,0:T(8,128)(2,1)S(1)}, u32[]{:S(2)}) copy-start(bf16[64,768]{1,0:T(8,128)(2,1)S(1)} %collective-permute-done.15) | copy-start | bytes 294916
  83.5 5.5 %collective-permute-start.7 = (bf16[64,768]{1,0:T(8,128)(2,1)S(1)}, bf16[64,768]{1,0:T(8,128)(2,1)S(1)}, u32[]{:S(2)}, u32[]{:S(2)}) collective-permute-start(bf16[64,768]{1,0:T(8,128)(2,1)S(1)} %add_convert_fusion.4), channel_id=1, source_target_pairs={{0,16},{4,20},{8,24},{12,28},{16,0},{20,4},{24,8},{28,12},{1,17},{... | collective-permute-start | bytes 294920 | tf_op jit(solution)/shard_map/ppermute | solution.py:301
  89.0 1.5 %copy-start.19 = (bf16[64,768]{1,0:T(8,128)(2,1)}, bf16[64,768]{1,0:T(8,128)(2,1)S(1)}, u32[]{:S(2)}) copy-start(bf16[64,768]{1,0:T(8,128)(2,1)S(1)} %collective-permute-done.7) | copy-start | bytes 294916
  89.0 8.4 %collective-permute-start.16 = (bf16[128,768]{1,0:T(8,128)(2,1)}, bf16[128,768]{1,0:T(8,128)(2,1)}, u32[]{:S(2)}, u32[]{:S(2)}) collective-permute-start(bf16[128,768]{1,0:T(8,128)(2,1)} %pad_maximum_fusion.4), channel_id=1, source_target_pairs={{0,16},{4,20},{8,24},{12,28},{16,0},{20,4},{24,8},{28,12},{1,17},{... | collective-permute-start | bytes 589832 | tf_op jit(solution)/shard_map/ppermute | solution.py:301
  89.3 8.1 %copy-start.21 = (bf16[64,768]{1,0:T(8,128)(2,1)S(1)}, bf16[64,768]{1,0:T(8,128)(2,1)}, u32[]{:S(2)}) copy-start(bf16[64,768]{1,0:T(8,128)(2,1)} %copy-done.20) | copy-start | bytes 294916
  89.3 20.9 %copy-start.16 = (bf16[1,256,512]{2,1,0:T(8,128)(2,1)S(1)}, bf16[1,256,512]{2,1,0:T(8,128)(2,1)}, u32[]{:S(2)}) copy-start(bf16[1,256,512]{2,1,0:T(8,128)(2,1)} %param.15) | copy-start | bytes 786436
  89.3 0.8 copy-start.10
  90.1 9.0 %collective-permute-start.10 = (bf16[128,768]{1,0:T(8,128)(2,1)S(1)}, bf16[128,768]{1,0:T(8,128)(2,1)S(1)}, u32[]{:S(2)}, u32[]{:S(2)}) collective-permute-start(bf16[128,768]{1,0:T(8,128)(2,1)S(1)} %pad_maximum_fusion.3), channel_id=1, source_target_pairs={{0,8},{4,12},{8,0},{12,4},{16,24},{20,28},{24,16},{28,20},{1,9},{5... | collective-permute-start | bytes 589832 | tf_op jit(solution)/shard_map/ppermute | solution.py:301
  95.1 15.6 %copy-start = (bf16[1,512,3,512]{3,1,2,0:T(8,128)(2,1)S(1)}, bf16[1,512,3,512]{3,1,2,0:T(8,128)(2,1)}, u32[]{:S(2)}) copy-start(bf16[1,512,3,512]{3,1,2,0:T(8,128)(2,1)} %param.19) | copy-start | bytes 4718596
  98.4 12.3 %collective-permute-start.17 = (bf16[256,768]{1,0:T(8,128)(2,1)S(1)}, bf16[256,768]{1,0:T(8,128)(2,1)}, u32[]{:S(2)}, u32[]{:S(2)}) collective-permute-start(bf16[256,768]{1,0:T(8,128)(2,1)S(1)} %pad_maximum_fusion.2.refs_2_), channel_id=1, source_target_pairs={{0,8},{4,12},{8,0},{12,4},{16,24},{20,28},{24,16},{28,20},{1,9},{5... | collective-permute-start | bytes 1179656 | tf_op jit(solution)/shard_map/ppermute | solution.py:301
  100.1 10.6 %copy-start.2 = (bf16[256,768]{1,0:T(8,128)(2,1)}, bf16[256,768]{1,0:T(8,128)(2,1)S(1)}, u32[]{:S(2)}) copy-start(bf16[256,768]{1,0:T(8,128)(2,1)S(1)} %pad_maximum_fusion.1.refs_0_) | copy-start | bytes 1179652
  100.2 0.8 copy-start.12
  101.0 9.7 %collective-permute-start.12 = (bf16[256,768]{1,0:T(8,128)(2,1)S(1)}, bf16[256,768]{1,0:T(8,128)(2,1)}, u32[]{:S(2)}, u32[]{:S(2)}) collective-permute-start(bf16[256,768]{1,0:T(8,128)(2,1)S(1)} %pad_maximum_fusion.1.refs_0_), channel_id=1, source_target_pairs={{0,4},{4,0},{8,12},{12,8},{16,20},{20,16},{24,28},{28,24},{1,5},{5... | collective-permute-start | bytes 1179656 | tf_op jit(solution)/shard_map/ppermute | solution.py:301
  102.4 7.7 %collective-permute-start.3 = (bf16[512,128]{1,0:T(8,128)(2,1)}, bf16[512,128]{1,0:T(8,128)(2,1)S(1)}, u32[]{:S(2)}, u32[]{:S(2)}) collective-permute-start(bf16[512,128]{1,0:T(8,128)(2,1)} %get-tuple-element.18), channel_id=1, source_target_pairs={{0,4},{4,0},{8,12},{12,8},{16,20},{20,16},{24,28},{28,24},{1,5},{5... | collective-permute-start | bytes 393224 | tf_op jit(solution)/shard_map/ppermute | solution.py:301
  110.7 6.6 %copy-start.1 = (bf16[512,1024]{1,0:T(8,128)(2,1)S(1)}, bf16[512,1024]{1,0:T(8,128)(2,1)}, u32[]{:S(2)}) copy-start(bf16[512,1024]{1,0:T(8,128)(2,1)} %map_ref.3) | copy-start | bytes 3145732
  110.7 1.1 copy-start.3
  119.1 10.7 %copy-start.7 = (bf16[512,256]{1,0:T(8,128)(2,1)S(1)}, bf16[512,256]{1,0:T(8,128)(2,1)}, u32[]{:S(2)}) copy-start(bf16[512,256]{1,0:T(8,128)(2,1)} %values_ref.7) | copy-start | bytes 786436
  119.1 10.7 %copy-start.9 = (bf16[512,256]{1,0:T(8,128)(2,1)S(1)}, bf16[512,256]{1,0:T(8,128)(2,1)}, u32[]{:S(2)}) copy-start(bf16[512,256]{1,0:T(8,128)(2,1)} %keys_ref.7) | copy-start | bytes 786436
  119.1 10.7 %copy-start.11 = (bf16[1024,256]{1,0:T(8,128)(2,1)S(1)}, bf16[1024,256]{1,0:T(8,128)(2,1)}, u32[]{:S(2)}) copy-start(bf16[1024,256]{1,0:T(8,128)(2,1)} %copy-done.10) | copy-start | bytes 1572868
  119.1 10.7 %copy-start.14 = (bf16[512,256]{1,0:T(8,128)(2,1)S(1)}, bf16[512,256]{1,0:T(8,128)(2,1)}, u32[]{:S(2)}) copy-start(bf16[512,256]{1,0:T(8,128)(2,1)} %queries_ref.5) | copy-start | bytes 786436
  119.1 2.2 %collective-permute-start.18 = (bf16[2,512,256]{2,1,0:T(8,128)(2,1)}, bf16[2,512,256]{2,1,0:T(8,128)(2,1)S(1)}, u32[]{:S(2)}, u32[]{:S(2)}) collective-permute-start(bf16[2,512,256]{2,1,0:T(8,128)(2,1)} %shard_map.138), channel_id=1, source_target_pairs={{0,1},{1,0},{2,3},{3,2},{4,5},{5,4},{6,7},{7,6},{8,9},{9,8},{10,11... | collective-permute-start | bytes 1572872 | tf_op jit(solution)/shard_map/ppermute | solution.py:296
  119.2 10.6 %copy-start.13 = (bf16[1024,256]{1,0:T(8,128)(2,1)S(1)}, bf16[1024,256]{1,0:T(8,128)(2,1)}, u32[]{:S(2)}) copy-start(bf16[1024,256]{1,0:T(8,128)(2,1)} %copy-done.12) | copy-start | bytes 1572868
  121.4 8.4 %collective-permute-start.19 = (bf16[512,256]{1,0:T(8,128)(2,1)S(1)}, bf16[512,256]{1,0:T(8,128)(2,1)S(1)}, u32[]{:S(2)}, u32[]{:S(2)}) collective-permute-start(bf16[512,256]{1,0:T(8,128)(2,1)S(1)} %fusion), channel_id=1, source_target_pairs={{0,2},{1,3},{2,0},{3,1},{4,6},{5,7},{6,4},{7,5},{8,10},{9,11},{10,... | collective-permute-start | bytes 786440 | tf_op jit(solution)/shard_map/ppermute | solution.py:296

commit v7 on v4

--- a/solution.py
+++ b/solution.py
@@ -14,7 +14,8 @@
 FAST_DIM = 512
 FAST_HIDDEN = 512
 TILE = 128
-VMEM_LIMIT = 48 * 1024 * 1024
+VMEM_LIMIT = 24 * 1024 * 1024
+VMEM_MOST = 60 * 1024 * 1024
 
 BF16 = jnp.bfloat16
 F32 = jnp.float32
@@ -29,7 +30,7 @@
     return lax.dot_general(left, right, (((1,), (1,)), ((), ())), preferred_element_type=F32)
 
 
-def call(body, out_shapes, operands, scalars=0, anywhere=0, scratch=(), cost=None):
+def call(body, out_shapes, operands, scalars=0, anywhere=0, scratch=(), cost=None, limit=VMEM_LIMIT):
     vmem = pl.BlockSpec(memory_space=pltpu.VMEM)
     in_specs = (
         [pl.BlockSpec(memory_space=pltpu.SMEM)] * scalars
@@ -43,7 +44,7 @@
         in_specs=in_specs,
         out_specs=jax.tree.map(lambda _: vmem, out_shapes),
         scratch_shapes=scratch,
-        compiler_params=pltpu.CompilerParams(vmem_limit_bytes=VMEM_LIMIT),
+        compiler_params=pltpu.CompilerParams(vmem_limit_bytes=limit),
         cost_estimate=pl.CostEstimate(flops=flops, bytes_accessed=moved, transcendentals=0),
     )(*operands)
 
@@ -300,24 +301,29 @@
     return lax.ppermute(value, "seq", [(i, i ^ step) for i in range(lax.axis_size("seq"))])
 
 
-def sum_over_seq(chunks, orders):
-    keeps = [[keep] for keep, _ in chunks]
-    for turn in range(len(orders[0])):
-        swapped = []
-        for index, order in enumerate(orders):
-            if turn == 0:
-                total = chunks[index][1]
-            else:
-                half = keeps[index][0].shape[0] // 2
-                total = sum(part[half:].astype(F32) for part in keeps[index]).astype(BF16)
-                keeps[index] = [part[:half] for part in keeps[index]]
-            swapped.append(seq_swap(total, order[turn]))
-        keeps = [keep + [new] for keep, new in zip(keeps, swapped)]
-    held = [(sum(part.astype(F32) for part in keep).astype(BF16),) for keep in keeps]
-    for turn in reversed(range(len(orders[0]))):
-        whole = [jnp.concatenate(parts) if len(parts) > 1 else parts[0] for parts in held]
-        held = [(own, seq_swap(own, order[turn])) for own, order in zip(whole, orders)]
-    return [part for parts in held for part in parts]
+def after(value, others):
+    return lax.optimization_barrier((value, others))[0]
+
+
+def halving_start(chunks, orders):
+    keeps = [keep for keep, _ in chunks]
+    return keeps, [seq_swap(send, order[0]) for (_, send), order in zip(chunks, orders)]
+
+
+def halving_step(keeps, found, orders, turn, wait=()):
+    sends, rest = [], []
+    for keep, new in zip(keeps, found):
+        half = keep.shape[0] // 2
+        sends.append((keep[half:].astype(F32) + new[half:].astype(F32)).astype(BF16))
+        rest.append(lax.optimization_barrier(keep[:half].astype(F32) + new[:half].astype(F32)))
+    sends = after(sends, wait) if wait else sends
+    return rest, [seq_swap(send, order[turn]) for send, order in zip(sends, orders)]
+
+
+def doubling_step(held, orders, turn, wait=()):
+    whole = [jnp.concatenate(parts) if len(parts) > 1 else parts[0] for parts in held]
+    whole = after(whole, wait) if wait else whole
+    return [(own, seq_swap(own, order[turn])) for own, order in zip(whole, orders)]
 
 
 def local(
@@ -370,38 +376,62 @@
         (place, step_rates.reshape(1, rows), fast_keys, fast_values, weights),
         scalars=1,
         scratch=[pltpu.VMEM((hidden_size, chunk_width), BF16)] * 2,
-    )
-    if halving:
-        gathered = sum_over_seq([gradients[:2], gradients[2:]], orders)
-    else:
-        gathered = lax.psum(gradients, "seq")
-
+        limit=VMEM_MOST,
+    )
     low_block, high_block = call(
         border_kernel,
         [shape((2 * rows, HEAD_DIM), BF16)] * 2,
         (side_scalar, keys_first, values_first, other_first),
         scalars=1,
     )
-    prev_first = seq_shift(high_block, 2)
-    next_first = seq_shift(low_block, -2)
-    keep_first, send_first = call(
-        first_kernel,
-        [shape((rows, HEAD_DIM), BF16)] * 2,
-        (edges, side_scalar, queries_first, other_first, prev_first, low_block, high_block, next_first),
-        scalars=2,
-        scratch=[pltpu.VMEM((4 * rows, HEAD_DIM), BF16)] * 2,
-        cost=(12 * rows * rows * width, 16 * rows * width),
-    )
+
+    def first_halos(low_block, high_block):
+        return seq_shift(high_block, 2), seq_shift(low_block, -2)
+
+    def first_attention(prev_first, next_first):
+        keep_first, send_first = call(
+            first_kernel,
+            [shape((rows, HEAD_DIM), BF16)] * 2,
+            (edges, side_scalar, queries_first, other_first, prev_first, low_block, high_block, next_first),
+            scalars=2,
+            scratch=[pltpu.VMEM((4 * rows, HEAD_DIM), BF16)] * 2,
+            cost=(12 * rows * rows * width, 16 * rows * width),
+        )
+        return keep_first, seq_swap(send_first, 0)
+
+    def second_halos(array):
+        return seq_shift(array, 1), seq_shift(array, -1)
+
+    if halving:
+        turns = len(bits)
+        keeps, found = halving_start([gradients[:2], gradients[2:]], orders)
+        for turn in range(1, turns):
+            if turn == turns - 1:
+                prev_first, next_first = first_halos(*after((low_block, high_block), found))
+            keeps, found = halving_step(keeps, found, orders, turn)
+        held = [((keep.astype(F32) + new.astype(F32)).astype(BF16),) for keep, new in zip(keeps, found)]
+        keys_prev, keys_next = second_halos(after(keys_second, found))
+        for turn in reversed(range(turns)):
+            wait = ()
+            if turn == 1:
+                wait = (prev_first, next_first)
+            if turn == 0:
+                keep_first, back_first = first_attention(prev_first, next_first)
+                wait = (keep_first, keys_prev, keys_next)
+            held = doubling_step(held, orders, turn, wait)
+        gathered = [part for parts in held for part in parts]
+        values_prev, values_next = second_halos(after(values_second, gathered))
+    else:
+        gathered = lax.psum(gradients, "seq")
+        keep_first, back_first = first_attention(*first_halos(low_block, high_block))
+        keys_prev, keys_next = second_halos(keys_second)
+        values_prev, values_next = second_halos(values_second)
     fast_query = call(
         query_kernel,
         shape((rows, fast_width), BF16),
-        (side_scalar, keep_first, seq_swap(send_first, 0), input_map[0]),
-        scalars=1,
-    )
-
-    keys_prev, keys_next = seq_shift(keys_second, 1), seq_shift(keys_second, -1)
-    values_prev, values_next = seq_shift(values_second, 1), seq_shift(values_second, -1)
-    fast_query, keys_prev, keys_next = lax.optimization_barrier((fast_query, keys_prev, keys_next))
+        (side_scalar, keep_first, back_first, input_map[0]),
+        scalars=1,
+    )
 
     own_rows = hidden_size >> len(orders[0])
     own_new, fast_out = call(
@@ -414,6 +444,8 @@
     if not halving:
         share_rows = hidden_size // seq_count
         own_new = lax.dynamic_slice_in_dim(own_new, seq_place * share_rows, share_rows, 1)
+
+    fast_out = after(fast_out, (values_prev, values_next))
 
     def mixed_for(low_bit):
         far = (head_place // 2) ^ 1

time: 114 us -> 124 us (1.088)
  the two profiles are of different devices: /device:TPU:25 before, /device:TPU:0 now
where the time goes in v7:
time: 124 us; the launch traced here: 123 us
  starting transfers between devices  45.1 us (36%)
  waiting for transfers between devices  44.1 us (36%)
  Pallas kernels  23.7 us (19%)
  local copies, waits for them, and re-layouts  5.35 us (4%)
  other arithmetic  3.66 us (3%)
    ppermute x14, waiting for transfers between devices, seq_swap(): lax.ppermute(value, 'seq', [(i, i ^ step) for i in range(lax.axis_size('s...  36.6 us
    ppermute x14, starting transfers between devices, seq_swap(): lax.ppermute(value, 'seq', [(i, i ^ step) for i in range(lax.axis_size('s...  26.4 us
    pallas_call x9, Pallas kernels, call(): pl.pallas_call(body, out_shape=out_shapes, in_specs=in_specs, out_specs=j...  23.7 us
    ppermute x6, starting transfers between devices, seq_shift(): lax.ppermute(value, 'seq', [(i, i + step) for i in range(peers) if 0 <= i...  17 us
    ppermute x2, waiting for transfers between devices, head_swap(): lax.ppermute(value, 'head', [(i, i ^ bit) for i in range(lax.axis_size('h...  7.55 us
    unnamed x42, local copies, waits for them, and re-layouts  5.26 us
  transfers between devices with their start and end apart: 22, of which 11 were waited for; matrix products, arithmetic and copies ran while one was open for 3% of the time, Pallas kernels for 9%

profile of v7, /device:TPU:0, one launch (start us, length us, event | category | flops | bytes accessed | tf_op | source)
XLA Modules:
  0.0 122.9 jit_solution(8096251588824347989)
XLA Ops:
  0.7 6.6 %shard_map.133 = (bf16[256,768]{1,0:T(8,128)(2,1)}, bf16[256,768]{1,0:T(8,128)(2,1)}, bf16[256,768]{1,0:T(8,128)(2,1)}, bf16[256,768]{1,0:T(8,128)(2,1)}) custom-call(s32[1,1]{1,0:T(1,128)} %bitcast.7.place_ref, f32[1,512]{1,0:T(1,128)} %bitcast.27, bf16[512,512]{1,0:T(8,128)(2,1)} %keys_ref.6, bf16[512,512]{1,0:T(8,128)(2,1)} %values_ref.6, ...), custom_call_target="tpu_custom_call" | custom-call | flops 1000 | bytes 1000 | tf_op jit(solution)/shard_map/pallas_call | solution.py:41
  7.3 3.0 %collective-permute-start.1 = (bf16[256,768]{1,0:T(8,128)(2,1)}, bf16[256,768]{1,0:T(8,128)(2,1)S(1)}, u32[]{:S(2)}, u32[]{:S(2)}) collective-permute-start(bf16[256,768]{1,0:T(8,128)(2,1)} %get-tuple-element.24), channel_id=1, source_target_pairs={{0,4},{4,0},{8,12},{12,8},{16,20},{20,16},{24,28},{28,24},{1,5},{5... | collective-permute-start | bytes 1179656 | tf_op jit(solution)/shard_map/ppermute | solution.py:301
  10.3 1.6 %collective-permute-start.3 = (bf16[256,768]{1,0:T(8,128)(2,1)}, bf16[256,768]{1,0:T(8,128)(2,1)S(1)}, u32[]{:S(2)}, u32[]{:S(2)}) collective-permute-start(bf16[256,768]{1,0:T(8,128)(2,1)} %get-tuple-element.26), channel_id=1, source_target_pairs={{0,8},{4,12},{8,0},{12,4},{16,24},{20,28},{24,16},{28,20},{1,9},{5... | collective-permute-start | bytes 1179656 | tf_op jit(solution)/shard_map/ppermute | solution.py:301
  11.9 0.6 collective-permute-start
  12.5 7.9 %collective-permute-done.1 = bf16[256,768]{1,0:T(8,128)(2,1)S(1)} collective-permute-done((bf16[256,768]{1,0:T(8,128)(2,1)}, bf16[256,768]{1,0:T(8,128)(2,1)S(1)}, u32[]{:S(2)}, u32[]{:S(2)}) %collective-permute-start.1) | collective-permute-done | bytes 393248 | tf_op jit(solution)/shard_map/ppermute | solution.py:301
  20.4 1.1 convert_add_fusion.1
  21.5 2.2 %collective-permute-start.2 = (bf16[128,768]{1,0:T(8,128)(2,1)S(1)}, bf16[128,768]{1,0:T(8,128)(2,1)S(1)}, u32[]{:S(2)}, u32[]{:S(2)}) collective-permute-start(bf16[128,768]{1,0:T(8,128)(2,1)S(1)} %get-tuple-element.43), channel_id=1, source_target_pairs={{0,8},{4,12},{8,0},{12,4},{16,24},{20,28},{24,16},{28,20},{1,9},{5... | collective-permute-start | bytes 589832 | tf_op jit(solution)/shard_map/ppermute | solution.py:301
  23.7 0.1 convert_add_fusion
  23.8 2.6 %collective-permute-start.4 = (bf16[128,768]{1,0:T(8,128)(2,1)S(1)}, bf16[128,768]{1,0:T(8,128)(2,1)S(1)}, u32[]{:S(2)}, u32[]{:S(2)}) collective-permute-start(bf16[128,768]{1,0:T(8,128)(2,1)S(1)} %get-tuple-element.41), channel_id=1, source_target_pairs={{0,16},{4,20},{8,24},{12,28},{16,0},{20,4},{24,8},{28,12},{1,17},{... | collective-permute-start | bytes 589832 | tf_op jit(solution)/shard_map/ppermute | solution.py:301
  26.5 1.6 %collective-permute-done.other_ref = bf16[1536,128]{1,0:T(8,128)(2,1)S(1)} collective-permute-done((bf16[1536,128]{1,0:T(8,128)(2,1)S(1)}, bf16[1536,128]{1,0:T(8,128)(2,1)S(1)}, u32[]{:S(2)}, u32[]{:S(2)}) %collective-permute-start) | collective-permute-done | bytes 393248 | tf_op jit(solution)/shard_map/ppermute | solution.py:301
  28.1 1.7 %collective-permute-done.2 = bf16[128,768]{1,0:T(8,128)(2,1)S(1)} collective-permute-done((bf16[128,768]{1,0:T(8,128)(2,1)S(1)}, bf16[128,768]{1,0:T(8,128)(2,1)S(1)}, u32[]{:S(2)}, u32[]{:S(2)}) %collective-permute-start.2) | collective-permute-done | bytes 196640 | tf_op jit(solution)/shard_map/ppermute | solution.py:301
  29.9 1.9 %collective-permute-start.8 = (bf16[64,768]{1,0:T(8,128)(2,1)S(1)}, bf16[64,768]{1,0:T(8,128)(2,1)S(1)}, u32[]{:S(2)}, u32[]{:S(2)}) collective-permute-start(bf16[64,768]{1,0:T(8,128)(2,1)S(1)} %get-tuple-element.46), channel_id=1, source_target_pairs={{0,16},{4,20},{8,24},{12,28},{16,0},{20,4},{24,8},{28,12},{1,17},{... | collective-permute-start | bytes 294920 | tf_op jit(solution)/shard_map/ppermute | solution.py:301
  31.8 2.8 %collective-permute-done.4 = bf16[128,768]{1,0:T(8,128)(2,1)S(1)} collective-permute-done((bf16[128,768]{1,0:T(8,128)(2,1)S(1)}, bf16[128,768]{1,0:T(8,128)(2,1)S(1)}, u32[]{:S(2)}, u32[]{:S(2)}) %collective-permute-start.4) | collective-permute-done | bytes 196640 | tf_op jit(solution)/shard_map/ppermute | solution.py:301
  34.6 1.7 %collective-permute-start.10 = (bf16[64,768]{1,0:T(8,128)(2,1)S(1)}, bf16[64,768]{1,0:T(8,128)(2,1)S(1)}, u32[]{:S(2)}, u32[]{:S(2)}) collective-permute-start(bf16[64,768]{1,0:T(8,128)(2,1)S(1)} %get-tuple-element.44), channel_id=1, source_target_pairs={{0,4},{4,0},{8,12},{12,8},{16,20},{20,16},{24,28},{28,24},{1,5},{5... | collective-permute-start | bytes 294920 | tf_op jit(solution)/shard_map/ppermute | solution.py:301
  36.4 3.1 %collective-permute-start.5 = (bf16[1024,128]{1,0:T(8,128)(2,1)S(1)}, bf16[1024,128]{1,0:T(8,128)(2,1)S(1)}, u32[]{:S(2)}, u32[]{:S(2)}) collective-permute-start(bf16[1024,128]{1,0:T(8,128)(2,1)S(1)} %get-tuple-element.27.high_ref), channel_id=1, source_target_pairs={{0,8},{4,12},{8,16},{12,20},{16,24},{20,28},{1,9},{5,13},{9,17},{1... | collective-permute-start | bytes 786440 | tf_op jit(solution)/shard_map/ppermute | solution.py:290
  39.5 1.3 %collective-permute-start.6 = (bf16[1024,128]{1,0:T(8,128)(2,1)S(1)}, bf16[1024,128]{1,0:T(8,128)(2,1)S(1)}, u32[]{:S(2)}, u32[]{:S(2)}) collective-permute-start(bf16[1024,128]{1,0:T(8,128)(2,1)S(1)} %get-tuple-element.28.low_ref), channel_id=1, source_target_pairs={{8,0},{12,4},{16,8},{20,12},{24,16},{28,20},{9,1},{13,5},{17,9},{2... | collective-permute-start | bytes 786440 | tf_op jit(solution)/shard_map/ppermute | solution.py:290
  40.8 4.3 %collective-permute-start.9 = (bf16[64,768]{1,0:T(8,128)(2,1)S(1)}, bf16[64,768]{1,0:T(8,128)(2,1)S(1)}, u32[]{:S(2)}, u32[]{:S(2)}) collective-permute-start(bf16[64,768]{1,0:T(8,128)(2,1)S(1)} %add_convert_fusion.4), channel_id=1, source_target_pairs={{0,16},{4,20},{8,24},{12,28},{16,0},{20,4},{24,8},{28,12},{1,17},{... | collective-permute-start | bytes 294920 | tf_op jit(solution)/shard_map/ppermute | solution.py:301
  45.2 0.5 collective-permute-start.11
  45.7 5.2 %collective-permute-done.9 = bf16[64,768]{1,0:T(8,128)(2,1)S(1)} collective-permute-done((bf16[64,768]{1,0:T(8,128)(2,1)S(1)}, bf16[64,768]{1,0:T(8,128)(2,1)S(1)}, u32[]{:S(2)}, u32[]{:S(2)}) %collective-permute-start.9) | collective-permute-done | bytes 98336 | tf_op jit(solution)/shard_map/ppermute | solution.py:301
  51.0 4.2 %collective-permute-start.12 = (bf16[128,768]{1,0:T(8,128)(2,1)S(1)}, bf16[128,768]{1,0:T(8,128)(2,1)}, u32[]{:S(2)}, u32[]{:S(2)}) collective-permute-start(bf16[128,768]{1,0:T(8,128)(2,1)S(1)} %pad_maximum_fusion.2), channel_id=1, source_target_pairs={{0,8},{4,12},{8,0},{12,4},{16,24},{20,28},{24,16},{28,20},{1,9},{5... | collective-permute-start | bytes 589832 | tf_op jit(solution)/shard_map/ppermute | solution.py:301
  55.3 0.1 reshape.26.edge_ref
  55.4 1.4 %collective-permute-start.15 = (bf16[512,256]{1,0:T(8,128)(2,1)S(1)}, bf16[512,256]{1,0:T(8,128)(2,1)S(1)}, u32[]{:S(2)}, u32[]{:S(2)}) collective-permute-start(bf16[512,256]{1,0:T(8,128)(2,1)S(1)} %copy-done.11), channel_id=1, source_target_pairs={{4,0},{8,4},{12,8},{16,12},{20,16},{24,20},{28,24},{5,1},{9,5},{13... | collective-permute-start | bytes 786440 | tf_op jit(solution)/shard_map/ppermute | solution.py:290
  56.8 4.6 %collective-permute-start.14 = (bf16[512,256]{1,0:T(8,128)(2,1)S(1)}, bf16[512,256]{1,0:T(8,128)(2,1)S(1)}, u32[]{:S(2)}, u32[]{:S(2)}) collective-permute-start(bf16[512,256]{1,0:T(8,128)(2,1)S(1)} %copy-done.11), channel_id=1, source_target_pairs={{0,4},{4,8},{8,12},{12,16},{16,20},{20,24},{24,28},{1,5},{5,9},{9,... | collective-permute-start | bytes 786440 | tf_op jit(solution)/shard_map/ppermute | solution.py:290
  61.5 4.6 %shard_map.134 = (bf16[512,128]{1,0:T(8,128)(2,1)S(1)}, bf16[512,128]{1,0:T(8,128)(2,1)}) custom-call(f32[2,2]{1,0:T(2,128)S(1)} %reshape.26.edge_ref, s32[1,1]{1,0:T(1,128)} %bitcast.10.side_ref, bf16[512,256]{1,0:T(8,128)(2,1)S(1)} %copy-done.17, bf16[1536,128]{1,0:T(8,128)(2,1)S(1)} %collective-permute-done.other_ref, ...), custom_call_target="tpu_custom_call" | custom-call | flops 805306368 | bytes 2097152 | tf_op jit(solution)/shard_map/pallas_call | solution.py:41
  66.1 1.1 pad_maximum_fusion.refs_0_
  67.2 2.6 %collective-permute-done.13 = bf16[128,768]{1,0:T(8,128)(2,1)S(1)} collective-permute-done((bf16[128,768]{1,0:T(8,128)(2,1)S(1)}, bf16[128,768]{1,0:T(8,128)(2,1)S(1)}, u32[]{:S(2)}, u32[]{:S(2)}) %collective-permute-start.13) | collective-permute-done | bytes 196640 | tf_op jit(solution)/shard_map/ppermute | solution.py:301
  69.8 1.0 pad_maximum_fusion.1.refs_2_
  70.8 0.7 copy-done.13
  71.5 0.7 copy-done.15
  72.2 1.4 %collective-permute-start.16 = (bf16[256,768]{1,0:T(8,128)(2,1)S(1)}, bf16[256,768]{1,0:T(8,128)(2,1)S(1)}, u32[]{:S(2)}, u32[]{:S(2)}) collective-permute-start(bf16[256,768]{1,0:T(8,128)(2,1)S(1)} %pad_maximum_fusion.refs_0_), channel_id=1, source_target_pairs={{0,4},{4,0},{8,12},{12,8},{16,20},{20,16},{24,28},{28,24},{1,5},{5... | collective-permute-start | bytes 1179656 | tf_op jit(solution)/shard_map/ppermute | solution.py:301
  73.6 9.8 %collective-permute-done.16.refs_1_ = bf16[256,768]{1,0:T(8,128)(2,1)S(1)} collective-permute-done((bf16[256,768]{1,0:T(8,128)(2,1)S(1)}, bf16[256,768]{1,0:T(8,128)(2,1)S(1)}, u32[]{:S(2)}, u32[]{:S(2)}) %collective-permute-start.16) | collective-permute-done | bytes 393248 | tf_op jit(solution)/shard_map/ppermute | solution.py:301
  83.5 0.7 collective-permute-done.17.refs_3_
  84.2 0.8 copy-done.8
  85.0 1.3 %collective-permute-start.19 = (bf16[512,256]{1,0:T(8,128)(2,1)}, bf16[512,256]{1,0:T(8,128)(2,1)}, u32[]{:S(2)}, u32[]{:S(2)}) collective-permute-start(bf16[512,256]{1,0:T(8,128)(2,1)} %values_ref.7), channel_id=1, source_target_pairs={{4,0},{8,4},{12,8},{16,12},{20,16},{24,20},{28,24},{5,1},{9,5},{13... | collective-permute-start | bytes 786440 | tf_op jit(solution)/shard_map/ppermute | solution.py:290
  86.3 5.3 %collective-permute-start.18 = (bf16[512,256]{1,0:T(8,128)(2,1)}, bf16[512,256]{1,0:T(8,128)(2,1)}, u32[]{:S(2)}, u32[]{:S(2)}) collective-permute-start(bf16[512,256]{1,0:T(8,128)(2,1)} %values_ref.7), channel_id=1, source_target_pairs={{0,4},{4,8},{8,12},{12,16},{16,20},{20,24},{24,28},{1,5},{5,9},{9,... | collective-permute-start | bytes 786440 | tf_op jit(solution)/shard_map/ppermute | solution.py:290
  91.5 2.2 %collective-permute-start.7 = (bf16[512,128]{1,0:T(8,128)(2,1)}, bf16[512,128]{1,0:T(8,128)(2,1)S(1)}, u32[]{:S(2)}, u32[]{:S(2)}) collective-permute-start(bf16[512,128]{1,0:T(8,128)(2,1)} %get-tuple-element.30), channel_id=1, source_target_pairs={{0,4},{4,0},{8,12},{12,8},{16,20},{20,16},{24,28},{28,24},{1,5},{5... | collective-permute-start | bytes 393224 | tf_op jit(solution)/shard_map/ppermute | solution.py:301
  93.8 4.2 %collective-permute-done.7.other_ref = bf16[512,128]{1,0:T(8,128)(2,1)S(1)} collective-permute-done((bf16[512,128]{1,0:T(8,128)(2,1)}, bf16[512,128]{1,0:T(8,128)(2,1)S(1)}, u32[]{:S(2)}, u32[]{:S(2)}) %collective-permute-start.7) | collective-permute-done | bytes 131104 | tf_op jit(solution)/shard_map/ppermute | solution.py:301
  98.0 0.5 shard_map.135.query_ref
  98.6 1.0 copy-done.3
  99.6 1.0 copy-done.7
  100.6 1.0 copy-done.9
  101.6 4.4 %shard_map.136 = (bf16[3,64,512]{2,1,0:T(8,128)(2,1)}, bf16[512,512]{1,0:T(8,128)(2,1)S(1)}) custom-call(s32[1,1]{1,0:T(1,128)} %bitcast.7.place_ref, bf16[3,512,512]{2,1,0:T(8,128)(2,1)S(1)} %bitcast.25, bf16[512,512]{1,0:T(8,128)(2,1)S(1)} %shard_map.135.query_ref, bf16[256,768]{1,0:T(8,128)(2,1)S(1)} %pad_maximum_fusion.refs_0_, ...), custom_call_target="tpu_custom_call" | custom-call | flops 1000 | bytes 1000 | tf_op jit(solution)/shard_map/pallas_call | solution.py:41
  106.0 1.0 shard_map.138
  107.2 1.0 shard_map.137.keep_ref
  108.2 0.8 collective-permute-done.20.near_ref
  109.1 1.7 %collective-permute-start.21 = (bf16[512,256]{1,0:T(8,128)(2,1)S(1)}, bf16[512,256]{1,0:T(8,128)(2,1)S(1)}, u32[]{:S(2)}, u32[]{:S(2)}) collective-permute-start(bf16[512,256]{1,0:T(8,128)(2,1)S(1)} %fusion), channel_id=1, source_target_pairs={{0,2},{1,3},{2,0},{3,1},{4,6},{5,7},{6,4},{7,5},{8,10},{9,11},{10,... | collective-permute-start | bytes 786440 | tf_op jit(solution)/shard_map/ppermute | solution.py:296
  110.8 6.7 %collective-permute-done.21.far_ref = bf16[512,256]{1,0:T(8,128)(2,1)S(1)} collective-permute-done((bf16[512,256]{1,0:T(8,128)(2,1)S(1)}, bf16[512,256]{1,0:T(8,128)(2,1)S(1)}, u32[]{:S(2)}, u32[]{:S(2)}) %collective-permute-start.21) | collective-permute-done | bytes 262176 | tf_op jit(solution)/shard_map/ppermute | solution.py:296
  117.5 5.4 %shard_map.139 = bf16[512,256]{1,0:T(8,128)(2,1)} custom-call(f32[2,2]{1,0:T(2,128)S(1)} %reshape.26.edge_ref, bf16[512,256]{1,0:T(8,128)(2,1)S(1)} %copy-done.10, bf16[2,512,256]{2,1,0:T(8,128)(2,1)S(1)} %shard_map.137.keep_ref, bf16[2,512,256]{2,1,0:T(8,128)(2,1)S(1)} %collective-permute-done.20.near_ref, ...), custom_call_target="tpu_custom_call" | custom-call | flops 805306368 | bytes 2097152 | tf_op jit(solution)/shard_map/pallas_call | solution.py:41
  (62 shorter events, 0.8 us)
Async XLA Ops:
  0.6 11.2 %copy-start.5 = (bf16[512,256]{1,0:T(8,128)(2,1)S(1)}, bf16[512,256]{1,0:T(8,128)(2,1)}, u32[]{:S(2)}) copy-start(bf16[512,256]{1,0:T(8,128)(2,1)} %values_ref.5) | copy-start | bytes 786436
  0.6 11.2 %copy-start.4 = (bf16[512,256]{1,0:T(8,128)(2,1)S(1)}, bf16[512,256]{1,0:T(8,128)(2,1)}, u32[]{:S(2)}) copy-start(bf16[512,256]{1,0:T(8,128)(2,1)} %keys_ref.5) | copy-start | bytes 786436
  0.7 11.2 %copy-start.17 = (bf16[512,256]{1,0:T(8,128)(2,1)S(1)}, bf16[512,256]{1,0:T(8,128)(2,1)}, u32[]{:S(2)}) copy-start(bf16[512,256]{1,0:T(8,128)(2,1)} %queries_ref.4) | copy-start | bytes 786436
  7.3 16.4 %copy-start.20 = (bf16[256,768]{1,0:T(8,128)(2,1)S(1)}, bf16[256,768]{1,0:T(8,128)(2,1)}, u32[]{:S(2)}) copy-start(bf16[256,768]{1,0:T(8,128)(2,1)} %get-tuple-element.25) | copy-start | bytes 1179652
  7.3 13.1 %collective-permute-start.1 = (bf16[256,768]{1,0:T(8,128)(2,1)}, bf16[256,768]{1,0:T(8,128)(2,1)S(1)}, u32[]{:S(2)}, u32[]{:S(2)}) collective-permute-start(bf16[256,768]{1,0:T(8,128)(2,1)} %get-tuple-element.24), channel_id=1, source_target_pairs={{0,4},{4,0},{8,12},{12,8},{16,20},{20,16},{24,28},{28,24},{1,5},{5... | collective-permute-start | bytes 1179656 | tf_op jit(solution)/shard_map/ppermute | solution.py:301
  10.3 13.5 %collective-permute-start.3 = (bf16[256,768]{1,0:T(8,128)(2,1)}, bf16[256,768]{1,0:T(8,128)(2,1)S(1)}, u32[]{:S(2)}, u32[]{:S(2)}) collective-permute-start(bf16[256,768]{1,0:T(8,128)(2,1)} %get-tuple-element.26), channel_id=1, source_target_pairs={{0,8},{4,12},{8,0},{12,4},{16,24},{20,28},{24,16},{28,20},{1,9},{5... | collective-permute-start | bytes 1179656 | tf_op jit(solution)/shard_map/ppermute | solution.py:301
  11.9 16.1 %collective-permute-start = (bf16[1536,128]{1,0:T(8,128)(2,1)S(1)}, bf16[1536,128]{1,0:T(8,128)(2,1)S(1)}, u32[]{:S(2)}, u32[]{:S(2)}) collective-permute-start(bf16[1536,128]{1,0:T(8,128)(2,1)S(1)} %shard_map.131), channel_id=1, source_target_pairs={{0,4},{4,0},{8,12},{12,8},{16,20},{20,16},{24,28},{28,24},{1,5},{5... | collective-permute-start | bytes 1179656 | tf_op jit(solution)/shard_map/ppermute | solution.py:301
  21.5 8.3 %collective-permute-start.2 = (bf16[128,768]{1,0:T(8,128)(2,1)S(1)}, bf16[128,768]{1,0:T(8,128)(2,1)S(1)}, u32[]{:S(2)}, u32[]{:S(2)}) collective-permute-start(bf16[128,768]{1,0:T(8,128)(2,1)S(1)} %get-tuple-element.43), channel_id=1, source_target_pairs={{0,8},{4,12},{8,0},{12,4},{16,24},{20,28},{24,16},{28,20},{1,9},{5... | collective-permute-start | bytes 589832 | tf_op jit(solution)/shard_map/ppermute | solution.py:301
  23.8 10.8 %collective-permute-start.4 = (bf16[128,768]{1,0:T(8,128)(2,1)S(1)}, bf16[128,768]{1,0:T(8,128)(2,1)S(1)}, u32[]{:S(2)}, u32[]{:S(2)}) collective-permute-start(bf16[128,768]{1,0:T(8,128)(2,1)S(1)} %get-tuple-element.41), channel_id=1, source_target_pairs={{0,16},{4,20},{8,24},{12,28},{16,0},{20,4},{24,8},{28,12},{1,17},{... | collective-permute-start | bytes 589832 | tf_op jit(solution)/shard_map/ppermute | solution.py:301
  28.1 27.3 %copy-start.11 = (bf16[512,256]{1,0:T(8,128)(2,1)S(1)}, bf16[512,256]{1,0:T(8,128)(2,1)}, u32[]{:S(2)}) copy-start(bf16[512,256]{1,0:T(8,128)(2,1)} %keys_ref.7) | copy-start | bytes 786436
  29.9 10.9 %collective-permute-start.8 = (bf16[64,768]{1,0:T(8,128)(2,1)S(1)}, bf16[64,768]{1,0:T(8,128)(2,1)S(1)}, u32[]{:S(2)}, u32[]{:S(2)}) collective-permute-start(bf16[64,768]{1,0:T(8,128)(2,1)S(1)} %get-tuple-element.46), channel_id=1, source_target_pairs={{0,16},{4,20},{8,24},{12,28},{16,0},{20,4},{24,8},{28,12},{1,17},{... | collective-permute-start | bytes 294920 | tf_op jit(solution)/shard_map/ppermute | solution.py:301
  34.6 10.5 %collective-permute-start.10 = (bf16[64,768]{1,0:T(8,128)(2,1)S(1)}, bf16[64,768]{1,0:T(8,128)(2,1)S(1)}, u32[]{:S(2)}, u32[]{:S(2)}) collective-permute-start(bf16[64,768]{1,0:T(8,128)(2,1)S(1)} %get-tuple-element.44), channel_id=1, source_target_pairs={{0,4},{4,0},{8,12},{12,8},{16,20},{20,16},{24,28},{28,24},{1,5},{5... | collective-permute-start | bytes 294920 | tf_op jit(solution)/shard_map/ppermute | solution.py:301
  36.4 14.6 %collective-permute-start.5 = (bf16[1024,128]{1,0:T(8,128)(2,1)S(1)}, bf16[1024,128]{1,0:T(8,128)(2,1)S(1)}, u32[]{:S(2)}, u32[]{:S(2)}) collective-permute-start(bf16[1024,128]{1,0:T(8,128)(2,1)S(1)} %get-tuple-element.27.high_ref), channel_id=1, source_target_pairs={{0,8},{4,12},{8,16},{12,20},{16,24},{20,28},{1,9},{5,13},{9,17},{1... | collective-permute-start | bytes 786440 | tf_op jit(solution)/shard_map/ppermute | solution.py:290
  39.5 11.5 %collective-permute-start.6 = (bf16[1024,128]{1,0:T(8,128)(2,1)S(1)}, bf16[1024,128]{1,0:T(8,128)(2,1)S(1)}, u32[]{:S(2)}, u32[]{:S(2)}) collective-permute-start(bf16[1024,128]{1,0:T(8,128)(2,1)S(1)} %get-tuple-element.28.low_ref), channel_id=1, source_target_pairs={{8,0},{12,4},{16,8},{20,12},{24,16},{28,20},{9,1},{13,5},{17,9},{2... | collective-permute-start | bytes 786440 | tf_op jit(solution)/shard_map/ppermute | solution.py:290
  40.8 10.1 %collective-permute-start.9 = (bf16[64,768]{1,0:T(8,128)(2,1)S(1)}, bf16[64,768]{1,0:T(8,128)(2,1)S(1)}, u32[]{:S(2)}, u32[]{:S(2)}) collective-permute-start(bf16[64,768]{1,0:T(8,128)(2,1)S(1)} %add_convert_fusion.4), channel_id=1, source_target_pairs={{0,16},{4,20},{8,24},{12,28},{16,0},{20,4},{24,8},{28,12},{1,17},{... | collective-permute-start | bytes 294920 | tf_op jit(solution)/shard_map/ppermute | solution.py:301
  45.2 5.8 %collective-permute-start.11 = (bf16[64,768]{1,0:T(8,128)(2,1)S(1)}, bf16[64,768]{1,0:T(8,128)(2,1)S(1)}, u32[]{:S(2)}, u32[]{:S(2)}) collective-permute-start(bf16[64,768]{1,0:T(8,128)(2,1)S(1)} %add_convert_fusion.3), channel_id=1, source_target_pairs={{0,4},{4,0},{8,12},{12,8},{16,20},{20,16},{24,28},{28,24},{1,5},{5... | collective-permute-start | bytes 294920 | tf_op jit(solution)/shard_map/ppermute | solution.py:301
  51.0 16.2 %copy-start.19 = (bf16[128,768]{1,0:T(8,128)(2,1)}, bf16[128,768]{1,0:T(8,128)(2,1)S(1)}, u32[]{:S(2)}) copy-start(bf16[128,768]{1,0:T(8,128)(2,1)S(1)} %pad_maximum_fusion.3) | copy-start | bytes 589828
  51.0 15.1 %collective-permute-start.12 = (bf16[128,768]{1,0:T(8,128)(2,1)S(1)}, bf16[128,768]{1,0:T(8,128)(2,1)}, u32[]{:S(2)}, u32[]{:S(2)}) collective-permute-start(bf16[128,768]{1,0:T(8,128)(2,1)S(1)} %pad_maximum_fusion.2), channel_id=1, source_target_pairs={{0,8},{4,12},{8,0},{12,4},{16,24},{20,28},{24,16},{28,20},{1,9},{5... | collective-permute-start | bytes 589832 | tf_op jit(solution)/shard_map/ppermute | solution.py:301
  55.4 42.6 %copy-start.18 = (bf16[1,256,512]{2,1,0:T(8,128)(2,1)S(1)}, bf16[1,256,512]{2,1,0:T(8,128)(2,1)}, u32[]{:S(2)}) copy-start(bf16[1,256,512]{2,1,0:T(8,128)(2,1)} %param.15) | copy-start | bytes 786436
  55.4 15.3 %collective-permute-start.15 = (bf16[512,256]{1,0:T(8,128)(2,1)S(1)}, bf16[512,256]{1,0:T(8,128)(2,1)S(1)}, u32[]{:S(2)}, u32[]{:S(2)}) collective-permute-start(bf16[512,256]{1,0:T(8,128)(2,1)S(1)} %copy-done.11), channel_id=1, source_target_pairs={{4,0},{8,4},{12,8},{16,12},{20,16},{24,20},{28,24},{5,1},{9,5},{13... | collective-permute-start | bytes 786440 | tf_op jit(solution)/shard_map/ppermute | solution.py:290
  56.8 14.7 %collective-permute-start.14 = (bf16[512,256]{1,0:T(8,128)(2,1)S(1)}, bf16[512,256]{1,0:T(8,128)(2,1)S(1)}, u32[]{:S(2)}, u32[]{:S(2)}) collective-permute-start(bf16[512,256]{1,0:T(8,128)(2,1)S(1)} %copy-done.11), channel_id=1, source_target_pairs={{0,4},{4,8},{8,12},{12,16},{16,20},{20,24},{24,28},{1,5},{5,9},{9,... | collective-permute-start | bytes 786440 | tf_op jit(solution)/shard_map/ppermute | solution.py:290
  61.4 8.4 %collective-permute-start.13 = (bf16[128,768]{1,0:T(8,128)(2,1)S(1)}, bf16[128,768]{1,0:T(8,128)(2,1)S(1)}, u32[]{:S(2)}, u32[]{:S(2)}) collective-permute-start(bf16[128,768]{1,0:T(8,128)(2,1)S(1)} %pad_maximum_fusion.3), channel_id=1, source_target_pairs={{0,16},{4,20},{8,24},{12,28},{16,0},{20,4},{24,8},{28,12},{1,17},{... | collective-permute-start | bytes 589832 | tf_op jit(solution)/shard_map/ppermute | solution.py:301
  66.1 32.5 %copy-start = (bf16[1,512,3,512]{3,1,2,0:T(8,128)(2,1)S(1)}, bf16[1,512,3,512]{3,1,2,0:T(8,128)(2,1)}, u32[]{:S(2)}) copy-start(bf16[1,512,3,512]{3,1,2,0:T(8,128)(2,1)} %param.19) | copy-start | bytes 4718596
  70.7 27.7 %copy-start.2 = (bf16[256,768]{1,0:T(8,128)(2,1)}, bf16[256,768]{1,0:T(8,128)(2,1)S(1)}, u32[]{:S(2)}) copy-start(bf16[256,768]{1,0:T(8,128)(2,1)S(1)} %pad_maximum_fusion.1.refs_2_) | copy-start | bytes 1179652
  70.8 0.8 copy-start.13
  71.5 0.7 copy-start.15
  72.2 11.3 %collective-permute-start.16 = (bf16[256,768]{1,0:T(8,128)(2,1)S(1)}, bf16[256,768]{1,0:T(8,128)(2,1)S(1)}, u32[]{:S(2)}, u32[]{:S(2)}) collective-permute-start(bf16[256,768]{1,0:T(8,128)(2,1)S(1)} %pad_maximum_fusion.refs_0_), channel_id=1, source_target_pairs={{0,4},{4,0},{8,12},{12,8},{16,20},{20,16},{24,28},{28,24},{1,5},{5... | collective-permute-start | bytes 1179656 | tf_op jit(solution)/shard_map/ppermute | solution.py:301
  73.6 10.6 %collective-permute-start.17 = (bf16[256,768]{1,0:T(8,128)(2,1)S(1)}, bf16[256,768]{1,0:T(8,128)(2,1)S(1)}, u32[]{:S(2)}, u32[]{:S(2)}) collective-permute-start(bf16[256,768]{1,0:T(8,128)(2,1)S(1)} %pad_maximum_fusion.1.refs_2_), channel_id=1, source_target_pairs={{0,8},{4,12},{8,0},{12,4},{16,24},{20,28},{24,16},{28,20},{1,9},{5... | collective-permute-start | bytes 1179656 | tf_op jit(solution)/shard_map/ppermute | solution.py:301
  83.5 15.0 %copy-start.6 = (bf16[256,768]{1,0:T(8,128)(2,1)}, bf16[256,768]{1,0:T(8,128)(2,1)S(1)}, u32[]{:S(2)}) copy-start(bf16[256,768]{1,0:T(8,128)(2,1)S(1)} %collective-permute-done.16.refs_1_) | copy-start | bytes 1179652
  84.2 0.8 copy-start.8
  85.0 21.0 %collective-permute-start.19 = (bf16[512,256]{1,0:T(8,128)(2,1)}, bf16[512,256]{1,0:T(8,128)(2,1)}, u32[]{:S(2)}, u32[]{:S(2)}) collective-permute-start(bf16[512,256]{1,0:T(8,128)(2,1)} %values_ref.7), channel_id=1, source_target_pairs={{4,0},{8,4},{12,8},{16,12},{20,16},{24,20},{28,24},{5,1},{9,5},{13... | collective-permute-start | bytes 786440 | tf_op jit(solution)/shard_map/ppermute | solution.py:290
  86.3 19.7 %collective-permute-start.18 = (bf16[512,256]{1,0:T(8,128)(2,1)}, bf16[512,256]{1,0:T(8,128)(2,1)}, u32[]{:S(2)}, u32[]{:S(2)}) collective-permute-start(bf16[512,256]{1,0:T(8,128)(2,1)} %values_ref.7), channel_id=1, source_target_pairs={{0,4},{4,8},{8,12},{12,16},{16,20},{20,24},{24,28},{1,5},{5,9},{9,... | collective-permute-start | bytes 786440 | tf_op jit(solution)/shard_map/ppermute | solution.py:290
  91.5 6.5 %collective-permute-start.7 = (bf16[512,128]{1,0:T(8,128)(2,1)}, bf16[512,128]{1,0:T(8,128)(2,1)S(1)}, u32[]{:S(2)}, u32[]{:S(2)}) collective-permute-start(bf16[512,128]{1,0:T(8,128)(2,1)} %get-tuple-element.30), channel_id=1, source_target_pairs={{0,4},{4,0},{8,12},{12,8},{16,20},{20,16},{24,28},{28,24},{1,5},{5... | collective-permute-start | bytes 393224 | tf_op jit(solution)/shard_map/ppermute | solution.py:301
  98.6 1.0 copy-start.3
  99.6 1.0 copy-start.7
  100.6 1.0 copy-start.9
  101.6 4.4 %copy-start.1 = (bf16[512,1024]{1,0:T(8,128)(2,1)S(1)}, bf16[512,1024]{1,0:T(8,128)(2,1)}, u32[]{:S(2)}) copy-start(bf16[512,1024]{1,0:T(8,128)(2,1)} %map_ref.3) | copy-start | bytes 3145732
  107.0 10.5 %copy-start.10 = (bf16[512,256]{1,0:T(8,128)(2,1)S(1)}, bf16[512,256]{1,0:T(8,128)(2,1)}, u32[]{:S(2)}) copy-start(bf16[512,256]{1,0:T(8,128)(2,1)} %queries_ref.5) | copy-start | bytes 786436
  107.0 10.5 %copy-start.12 = (bf16[512,256]{1,0:T(8,128)(2,1)S(1)}, bf16[512,256]{1,0:T(8,128)(2,1)}, u32[]{:S(2)}) copy-start(bf16[512,256]{1,0:T(8,128)(2,1)} %keys_ref.7) | copy-start | bytes 786436
  107.0 10.5 %copy-start.14 = (bf16[512,256]{1,0:T(8,128)(2,1)S(1)}, bf16[512,256]{1,0:T(8,128)(2,1)}, u32[]{:S(2)}) copy-start(bf16[512,256]{1,0:T(8,128)(2,1)} %copy-done.13) | copy-start | bytes 786436
  107.0 2.0 %collective-permute-start.20 = (bf16[2,512,256]{2,1,0:T(8,128)(2,1)S(1)}, bf16[2,512,256]{2,1,0:T(8,128)(2,1)S(1)}, u32[]{:S(2)}, u32[]{:S(2)}) collective-permute-start(bf16[2,512,256]{2,1,0:T(8,128)(2,1)S(1)} %shard_map.138), channel_id=1, source_target_pairs={{0,1},{1,0},{2,3},{3,2},{4,5},{5,4},{6,7},{7,6},{8,9},{9,8},{10,11... | collective-permute-start | bytes 1572872 | tf_op jit(solution)/shard_map/ppermute | solution.py:296
  107.1 10.4 %copy-start.16 = (bf16[512,256]{1,0:T(8,128)(2,1)S(1)}, bf16[512,256]{1,0:T(8,128)(2,1)}, u32[]{:S(2)}) copy-start(bf16[512,256]{1,0:T(8,128)(2,1)} %copy-done.15) | copy-start | bytes 786436
  109.1 8.4 %collective-permute-start.21 = (bf16[512,256]{1,0:T(8,128)(2,1)S(1)}, bf16[512,256]{1,0:T(8,128)(2,1)S(1)}, u32[]{:S(2)}, u32[]{:S(2)}) collective-permute-start(bf16[512,256]{1,0:T(8,128)(2,1)S(1)} %fusion), channel_id=1, source_target_pairs={{0,2},{1,3},{2,0},{3,1},{4,6},{5,7},{6,4},{7,5},{8,10},{9,11},{10,... | collective-permute-start | bytes 786440 | tf_op jit(solution)/shard_map/ppermute | solution.py:296

commit v8 on v7

--- a/solution.py
+++ b/solution.py
@@ -62,41 +62,43 @@
     rates = rates_ref[...]
     keys = keys_ref[...]
     values = values_ref[...]
-    hidden_size, width = weights_ref.shape[1:]
-    step = 128
-
-    def put(chunk, low, columns, product):
+    hidden_size = chunk_refs[0].shape[0]
+    width = weights_ref.shape[2]
+    turn = pl.program_id(0)
+    step = weights_ref.shape[1]
+
+    def put(chunk, columns, product):
         order = orders[chunk]
         block_rows = min(step, hidden_size >> len(order))
         for start in range(0, step, block_rows):
-            row = low + start
+            row = turn * step + start
             if order:
-                slot = slot_of((row // block_rows) ^ place, order)
-                row = pl.multiple_of(slot * block_rows, block_rows)
+                block = turn * (step // block_rows) + start // block_rows
+                row = slot_of(block ^ place, order) * block_rows
+            row = pl.multiple_of(row, block_rows)
             chunk_refs[chunk][pl.ds(row, block_rows), columns] = product[start:start + block_rows]
 
-    for low in range(0, hidden_size, step):
-        rows = slice(low, low + step)
-        gate = dot_nt(weights_ref[0, rows, :], keys) * INVERSE
-        up = dot_nt(weights_ref[1, rows, :], keys) * INVERSE
-        sigmoid = jax.nn.sigmoid(gate)
-        silu = gate * sigmoid
-        hidden = (rates * silu * up).astype(BF16)
-        backward = rates * dot_nt(weights_ref[2, rows, :], values)
-        d_gate = (
-            backward * up * sigmoid * (1.0 + gate * (1.0 - sigmoid)) * INVERSE
-        ).astype(BF16)
-        d_up = (backward * silu * INVERSE).astype(BF16)
-        up_part = dot_nn(d_up, keys).astype(BF16)
-        put(0, low, slice(0, width), dot_nn(d_gate, keys).astype(BF16))
-        put(0, low, slice(width, width + width // 2), up_part[:, :width // 2])
-        put(1, low, slice(0, width), dot_nn(hidden, values).astype(BF16))
-        put(1, low, slice(width, width + width // 2), up_part[:, width // 2:])
-    halves = len(out_refs) // 2
-    half_rows = hidden_size // halves
-    for index, out_ref in enumerate(out_refs):
-        half = index % halves
-        out_ref[...] = chunk_refs[index // halves][half * half_rows:(half + 1) * half_rows, :]
+    gate = dot_nt(weights_ref[0], keys) * INVERSE
+    up = dot_nt(weights_ref[1], keys) * INVERSE
+    sigmoid = jax.nn.sigmoid(gate)
+    silu = gate * sigmoid
+    hidden = (rates * silu * up).astype(BF16)
+    backward = rates * dot_nt(weights_ref[2], values)
+    d_gate = (backward * up * sigmoid * (1.0 + gate * (1.0 - sigmoid)) * INVERSE).astype(BF16)
+    d_up = (backward * silu * INVERSE).astype(BF16)
+    up_part = dot_nn(d_up, keys).astype(BF16)
+    put(0, slice(0, width), dot_nn(d_gate, keys).astype(BF16))
+    put(0, slice(width, width + width // 2), up_part[:, :width // 2])
+    put(1, slice(0, width), dot_nn(hidden, values).astype(BF16))
+    put(1, slice(width, width + width // 2), up_part[:, width // 2:])
+
+    @pl.when(turn == pl.num_programs(0) - 1)
+    def _():
+        halves = len(out_refs) // 2
+        half_rows = hidden_size // halves
+        for index, out_ref in enumerate(out_refs):
+            half = index % halves
+            out_ref[...] = chunk_refs[index // halves][half * half_rows:(half + 1) * half_rows, :]
 
 
 def attend_rows(edge_prev, edge_next, query_tile, keys_prev, keys_own, keys_next,
@@ -195,8 +197,8 @@
     ).astype(BF16)
 
 
-def second_kernel(edge_ref, queries_ref, keep_ref, near_ref, far_ref, keys_prev_ref, keys_ref, keys_next_ref,
-                  values_prev_ref, values_ref, values_next_ref, out_ref):
+def second_kernel(edge_ref, queries_ref, keep_ref, near_ref, far_ref, prev_ref, keys_ref, values_ref, next_ref,
+                  out_ref):
     count = keys_ref.shape[0]
     for index in range(count // TILE):
         low, high = index * TILE, (index + 1) * TILE
@@ -213,8 +215,8 @@
             heads.append(
                 attend_rows(
                     edge_ref[0, 0], edge_ref[0, 1], query[:, cols],
-                    keys_prev_ref[low:, cols], keys_ref[:, cols], keys_next_ref[:high, cols],
-                    values_prev_ref[low:, cols], values_ref[:, cols], values_next_ref[:high, cols],
+                    prev_ref[low:count, cols], keys_ref[:, cols], next_ref[:high, cols],
+                    prev_ref[count + low:, cols], values_ref[:, cols], next_ref[count:count + high, cols],
                 )
             )
         both = jnp.concatenate(heads, axis=1)
@@ -370,14 +372,25 @@
     orders = (bits, bits[1:] + bits[:1]) if halving else ((), ())
     halves = 2 if halving else 1
     chunk_width = fast_width + fast_width // 2
-    gradients = call(
+    out_shapes = [shape((hidden_size // halves, chunk_width), BF16)] * (2 * halves)
+    whole = pl.BlockSpec(memory_space=pltpu.VMEM)
+    gradients = pl.pallas_call(
         functools.partial(gradient_kernel, orders),
-        [shape((hidden_size // halves, chunk_width), BF16)] * (2 * halves),
-        (place, step_rates.reshape(1, rows), fast_keys, fast_values, weights),
-        scalars=1,
-        scratch=[pltpu.VMEM((hidden_size, chunk_width), BF16)] * 2,
-        limit=VMEM_MOST,
-    )
+        grid=(hidden_size // TILE,),
+        out_shape=out_shapes,
+        in_specs=[
+            pl.BlockSpec(memory_space=pltpu.SMEM),
+            whole,
+            whole,
+            whole,
+            pl.BlockSpec((3, TILE, fast_width), lambda turn: (0, turn, 0)),
+        ],
+        out_specs=[whole] * len(out_shapes),
+        scratch_shapes=[pltpu.VMEM((hidden_size, chunk_width), BF16)] * 2,
+        compiler_params=pltpu.CompilerParams(vmem_limit_bytes=VMEM_MOST),
+        cost_estimate=pl.CostEstimate(flops=1000, bytes_accessed=1000, transcendentals=0),
+    )(place, step_rates.reshape(1, rows), fast_keys, fast_values, weights)
+
     low_block, high_block = call(
         border_kernel,
         [shape((2 * rows, HEAD_DIM), BF16)] * 2,
@@ -399,6 +412,8 @@
         )
         return keep_first, seq_swap(send_first, 0)
 
+    both_second = jnp.concatenate([keys_second, values_second])
+
     def second_halos(array):
         return seq_shift(array, 1), seq_shift(array, -1)
 
@@ -410,22 +425,20 @@
                 prev_first, next_first = first_halos(*after((low_block, high_block), found))
             keeps, found = halving_step(keeps, found, orders, turn)
         held = [((keep.astype(F32) + new.astype(F32)).astype(BF16),) for keep, new in zip(keeps, found)]
-        keys_prev, keys_next = second_halos(after(keys_second, found))
         for turn in reversed(range(turns)):
             wait = ()
             if turn == 1:
                 wait = (prev_first, next_first)
             if turn == 0:
                 keep_first, back_first = first_attention(prev_first, next_first)
-                wait = (keep_first, keys_prev, keys_next)
+                wait = (keep_first,)
             held = doubling_step(held, orders, turn, wait)
         gathered = [part for parts in held for part in parts]
-        values_prev, values_next = second_halos(after(values_second, gathered))
+        prev_second, next_second = second_halos(after(both_second, (gathered, back_first)))
     else:
         gathered = lax.psum(gradients, "seq")
         keep_first, back_first = first_attention(*first_halos(low_block, high_block))
-        keys_prev, keys_next = second_halos(keys_second)
-        values_prev, values_next = second_halos(values_second)
+        prev_second, next_second = second_halos(both_second)
     fast_query = call(
         query_kernel,
         shape((rows, fast_width), BF16),
@@ -444,8 +457,6 @@
     if not halving:
         share_rows = hidden_size // seq_count
         own_new = lax.dynamic_slice_in_dim(own_new, seq_place * share_rows, share_rows, 1)
-
-    fast_out = after(fast_out, (values_prev, values_next))
 
     def mixed_for(low_bit):
         far = (head_place // 2) ^ 1
@@ -468,7 +479,7 @@
         second_kernel,
         shape((rows, width), BF16),
         (edges, queries_second, keep_part, near_part, far_part,
-         keys_prev, keys_second, keys_next, values_prev, values_second, values_next),
+         prev_second, keys_second, values_second, next_second),
         scalars=1,
         cost=(12 * rows * rows * width, 16 * rows * width),
     )

time: 124 us -> 116 us (0.935)
  starting transfers between devices: 45.1 us -> 34.2 us
  waiting for transfers between devices: 44.1 us -> 52.9 us
  local copies, waits for them, and re-layouts: 5.35 us -> 1.2 us
  other arithmetic: 3.66 us -> 1.73 us
    ppermute x6 -> x4, waiting for transfers between devices: 0.02 us -> 17.5 us  [seq_shift(): lax.ppermute(value, 'seq', [(i, i + step) for i in range(peers) if 0 <= i...]
    ppermute x2, waiting for transfers between devices: 7.55 us -> 0.01 us  [head_swap(): lax.ppermute(value, 'head', [(i, i ^ bit) for i in range(lax.axis_size('h...]
    pallas_call x0 -> x1, Pallas kernels: none -> 6.85 us  [local(): pl.pallas_call(functools.partial(gradient_kernel, orders), grid=(hidden_s...]
    ppermute x6 -> x4, starting transfers between devices: 17 us -> 10.7 us  [seq_shift(): lax.ppermute(value, 'seq', [(i, i + step) for i in range(peers) if 0 <= i...]
    pallas_call x9 -> x8, Pallas kernels: 23.7 us -> 17.7 us  [call(): pl.pallas_call(body, out_shape=out_shapes, in_specs=in_specs, out_specs=j...]
    ppermute x14, starting transfers between devices: 26.4 us -> 22 us  [seq_swap(): lax.ppermute(value, 'seq', [(i, i ^ step) for i in range(lax.axis_size('s...]
    unnamed x42 -> x24, local copies, waits for them, and re-layouts: 5.26 us -> 1.12 us
    concatenate x4, other arithmetic: 2.05 us -> 0.08 us  [doubling_step(): jnp.concatenate(parts)]
  transfers between devices with their start and end apart: 22 -> 20, of which waited for: 11 -> 9; matrix products, arithmetic and copies ran while one was open for 3% -> 2% of each run, Pallas kernels for 9% -> 5%
where the time goes in v8:
time: 116 us
  waiting for transfers between devices  52.9 us (46%)
  starting transfers between devices  34.2 us (29%)
  Pallas kernels  24.6 us (21%)
  other arithmetic  1.73 us (1%)
  local copies, waits for them, and re-layouts  1.2 us (1%)
    ppermute x14, waiting for transfers between devices, seq_swap(): lax.ppermute(value, 'seq', [(i, i ^ step) for i in range(lax.axis_size('s...  35.4 us
    ppermute x14, starting transfers between devices, seq_swap(): lax.ppermute(value, 'seq', [(i, i ^ step) for i in range(lax.axis_size('s...  22 us
    pallas_call x8, Pallas kernels, call(): pl.pallas_call(body, out_shape=out_shapes, in_specs=in_specs, out_specs=j...  17.7 us
    ppermute x4, waiting for transfers between devices, seq_shift(): lax.ppermute(value, 'seq', [(i, i + step) for i in range(peers) if 0 <= i...  17.5 us
    ppermute x4, starting transfers between devices, seq_shift(): lax.ppermute(value, 'seq', [(i, i + step) for i in range(peers) if 0 <= i...  10.7 us
    pallas_call x1, Pallas kernels, local(): pl.pallas_call(functools.partial(gradient_kernel, orders), grid=(hidden_s...  6.85 us
  transfers between devices with their start and end apart: 20, of which 9 were waited for; matrix products, arithmetic and copies ran while one was open for 2% of the time, Pallas kernels for 5%

profile of v8, /device:TPU:0, one launch (start us, length us, event | category | flops | bytes accessed | tf_op | source)
XLA Modules:
  0.0 115.5 jit_solution(15994179436324955120)
XLA Ops:
  0.7 6.8 %shard_map.133 = (bf16[256,768]{1,0:T(8,128)(2,1)}, bf16[256,768]{1,0:T(8,128)(2,1)}, bf16[256,768]{1,0:T(8,128)(2,1)}, bf16[256,768]{1,0:T(8,128)(2,1)}) custom-call(s32[1,1]{1,0:T(1,128)} %bitcast.7.place_ref, f32[1,512]{1,0:T(1,128)} %bitcast.27, bf16[512,512]{1,0:T(8,128)(2,1)} %keys_ref.6, bf16[512,512]{1,0:T(8,128)(2,1)} %values_ref.6, ...), custom_call_target="tpu_custom_call" | custom-call | flops 1000 | bytes 1000 | tf_op jit(solution)/shard_map/pallas_call | solution.py:377
  7.5 3.0 %collective-permute-start.1 = (bf16[256,768]{1,0:T(8,128)(2,1)}, bf16[256,768]{1,0:T(8,128)(2,1)S(1)}, u32[]{:S(2)}, u32[]{:S(2)}) collective-permute-start(bf16[256,768]{1,0:T(8,128)(2,1)} %get-tuple-element.22), channel_id=1, source_target_pairs={{0,4},{4,0},{8,12},{12,8},{16,20},{20,16},{24,28},{28,24},{1,5},{5... | collective-permute-start | bytes 1179656 | tf_op jit(solution)/shard_map/ppermute | solution.py:303
  10.5 1.6 %collective-permute-start.3 = (bf16[256,768]{1,0:T(8,128)(2,1)}, bf16[256,768]{1,0:T(8,128)(2,1)S(1)}, u32[]{:S(2)}, u32[]{:S(2)}) collective-permute-start(bf16[256,768]{1,0:T(8,128)(2,1)} %get-tuple-element.24), channel_id=1, source_target_pairs={{0,8},{4,12},{8,0},{12,4},{16,24},{20,28},{24,16},{28,20},{1,9},{5... | collective-permute-start | bytes 1179656 | tf_op jit(solution)/shard_map/ppermute | solution.py:303
  12.1 0.1 shard_map.131
  12.2 0.6 collective-permute-start
  12.7 7.9 %collective-permute-done.1 = bf16[256,768]{1,0:T(8,128)(2,1)S(1)} collective-permute-done((bf16[256,768]{1,0:T(8,128)(2,1)}, bf16[256,768]{1,0:T(8,128)(2,1)S(1)}, u32[]{:S(2)}, u32[]{:S(2)}) %collective-permute-start.1) | collective-permute-done | bytes 393248 | tf_op jit(solution)/shard_map/ppermute | solution.py:303
  20.6 1.1 convert_add_fusion.1
  21.7 2.2 %collective-permute-start.2 = (bf16[128,768]{1,0:T(8,128)(2,1)S(1)}, bf16[128,768]{1,0:T(8,128)(2,1)S(1)}, u32[]{:S(2)}, u32[]{:S(2)}) collective-permute-start(bf16[128,768]{1,0:T(8,128)(2,1)S(1)} %get-tuple-element.39), channel_id=1, source_target_pairs={{0,8},{4,12},{8,0},{12,4},{16,24},{20,28},{24,16},{28,20},{1,9},{5... | collective-permute-start | bytes 589832 | tf_op jit(solution)/shard_map/ppermute | solution.py:303
  23.9 0.1 convert_add_fusion
  24.0 2.6 %collective-permute-start.4 = (bf16[128,768]{1,0:T(8,128)(2,1)S(1)}, bf16[128,768]{1,0:T(8,128)(2,1)S(1)}, u32[]{:S(2)}, u32[]{:S(2)}) collective-permute-start(bf16[128,768]{1,0:T(8,128)(2,1)S(1)} %get-tuple-element.37), channel_id=1, source_target_pairs={{0,16},{4,20},{8,24},{12,28},{16,0},{20,4},{24,8},{28,12},{1,17},{... | collective-permute-start | bytes 589832 | tf_op jit(solution)/shard_map/ppermute | solution.py:303
  26.7 1.6 %collective-permute-done.other_ref = bf16[1536,128]{1,0:T(8,128)(2,1)S(1)} collective-permute-done((bf16[1536,128]{1,0:T(8,128)(2,1)S(1)}, bf16[1536,128]{1,0:T(8,128)(2,1)S(1)}, u32[]{:S(2)}, u32[]{:S(2)}) %collective-permute-start) | collective-permute-done | bytes 393248 | tf_op jit(solution)/shard_map/ppermute | solution.py:303
  28.2 0.1 shard_map.132
  28.3 1.8 %collective-permute-done.2 = bf16[128,768]{1,0:T(8,128)(2,1)S(1)} collective-permute-done((bf16[128,768]{1,0:T(8,128)(2,1)S(1)}, bf16[128,768]{1,0:T(8,128)(2,1)S(1)}, u32[]{:S(2)}, u32[]{:S(2)}) %collective-permute-start.2) | collective-permute-done | bytes 196640 | tf_op jit(solution)/shard_map/ppermute | solution.py:303
  30.1 1.8 %collective-permute-start.8 = (bf16[64,768]{1,0:T(8,128)(2,1)S(1)}, bf16[64,768]{1,0:T(8,128)(2,1)S(1)}, u32[]{:S(2)}, u32[]{:S(2)}) collective-permute-start(bf16[64,768]{1,0:T(8,128)(2,1)S(1)} %get-tuple-element.42), channel_id=1, source_target_pairs={{0,16},{4,20},{8,24},{12,28},{16,0},{20,4},{24,8},{28,12},{1,17},{... | collective-permute-start | bytes 294920 | tf_op jit(solution)/shard_map/ppermute | solution.py:303
  31.9 2.8 %collective-permute-done.4 = bf16[128,768]{1,0:T(8,128)(2,1)S(1)} collective-permute-done((bf16[128,768]{1,0:T(8,128)(2,1)S(1)}, bf16[128,768]{1,0:T(8,128)(2,1)S(1)}, u32[]{:S(2)}, u32[]{:S(2)}) %collective-permute-start.4) | collective-permute-done | bytes 196640 | tf_op jit(solution)/shard_map/ppermute | solution.py:303
  34.8 1.7 %collective-permute-start.10 = (bf16[64,768]{1,0:T(8,128)(2,1)S(1)}, bf16[64,768]{1,0:T(8,128)(2,1)S(1)}, u32[]{:S(2)}, u32[]{:S(2)}) collective-permute-start(bf16[64,768]{1,0:T(8,128)(2,1)S(1)} %get-tuple-element.40), channel_id=1, source_target_pairs={{0,4},{4,0},{8,12},{12,8},{16,20},{20,16},{24,28},{28,24},{1,5},{5... | collective-permute-start | bytes 294920 | tf_op jit(solution)/shard_map/ppermute | solution.py:303
  36.5 3.2 %collective-permute-start.5 = (bf16[1024,128]{1,0:T(8,128)(2,1)S(1)}, bf16[1024,128]{1,0:T(8,128)(2,1)S(1)}, u32[]{:S(2)}, u32[]{:S(2)}) collective-permute-start(bf16[1024,128]{1,0:T(8,128)(2,1)S(1)} %get-tuple-element.25.high_ref), channel_id=1, source_target_pairs={{0,8},{4,12},{8,16},{12,20},{16,24},{20,28},{1,9},{5,13},{9,17},{1... | collective-permute-start | bytes 786440 | tf_op jit(solution)/shard_map/ppermute | solution.py:292
  39.7 1.3 %collective-permute-start.6 = (bf16[1024,128]{1,0:T(8,128)(2,1)S(1)}, bf16[1024,128]{1,0:T(8,128)(2,1)S(1)}, u32[]{:S(2)}, u32[]{:S(2)}) collective-permute-start(bf16[1024,128]{1,0:T(8,128)(2,1)S(1)} %get-tuple-element.26.low_ref), channel_id=1, source_target_pairs={{8,0},{12,4},{16,8},{20,12},{24,16},{28,20},{9,1},{13,5},{17,9},{2... | collective-permute-start | bytes 786440 | tf_op jit(solution)/shard_map/ppermute | solution.py:292
  41.0 4.3 %collective-permute-start.9 = (bf16[64,768]{1,0:T(8,128)(2,1)S(1)}, bf16[64,768]{1,0:T(8,128)(2,1)S(1)}, u32[]{:S(2)}, u32[]{:S(2)}) collective-permute-start(bf16[64,768]{1,0:T(8,128)(2,1)S(1)} %add_convert_fusion.4), channel_id=1, source_target_pairs={{0,16},{4,20},{8,24},{12,28},{16,0},{20,4},{24,8},{28,12},{1,17},{... | collective-permute-start | bytes 294920 | tf_op jit(solution)/shard_map/ppermute | solution.py:303
  45.4 0.6 collective-permute-start.11
  46.0 9.9 %collective-permute-done.9 = bf16[64,768]{1,0:T(8,128)(2,1)S(1)} collective-permute-done((bf16[64,768]{1,0:T(8,128)(2,1)S(1)}, bf16[64,768]{1,0:T(8,128)(2,1)S(1)}, u32[]{:S(2)}, u32[]{:S(2)}) %collective-permute-start.9) | collective-permute-done | bytes 98336 | tf_op jit(solution)/shard_map/ppermute | solution.py:303
  56.0 0.5 collective-permute-start.12
  56.4 0.1 pad_maximum_fusion.5
  56.5 0.1 reshape.26.edge_ref
  56.6 0.3 collective-permute-start.13
  56.9 4.0 %shard_map.134 = (bf16[512,128]{1,0:T(8,128)(2,1)S(1)}, bf16[512,128]{1,0:T(8,128)(2,1)S(1)}) custom-call(f32[2,2]{1,0:T(2,128)S(1)} %reshape.26.edge_ref, s32[1,1]{1,0:T(1,128)} %bitcast.10.side_ref, bf16[512,256]{1,0:T(8,128)(2,1)S(1)} %copy-done.9, bf16[1536,128]{1,0:T(8,128)(2,1)S(1)} %collective-permute-done.other_ref, ...), custom_call_target="tpu_custom_call" | custom-call | flops 805306368 | bytes 2097152 | tf_op jit(solution)/shard_map/pallas_call | solution.py:41
  60.9 0.0 copy-start
  60.9 5.1 %collective-permute-done.12 = bf16[128,768]{1,0:T(8,128)(2,1)S(1)} collective-permute-done((bf16[128,768]{1,0:T(8,128)(2,1)S(1)}, bf16[128,768]{1,0:T(8,128)(2,1)S(1)}, u32[]{:S(2)}, u32[]{:S(2)}) %collective-permute-start.12) | collective-permute-done | bytes 196640 | tf_op jit(solution)/shard_map/ppermute | solution.py:303
  66.1 0.4 collective-permute-start.14
  66.5 0.4 collective-permute-start.15
  66.9 1.9 %collective-permute-start.7 = (bf16[512,128]{1,0:T(8,128)(2,1)S(1)}, bf16[512,128]{1,0:T(8,128)(2,1)S(1)}, u32[]{:S(2)}, u32[]{:S(2)}) collective-permute-start(bf16[512,128]{1,0:T(8,128)(2,1)S(1)} %get-tuple-element.28), channel_id=1, source_target_pairs={{0,4},{4,0},{8,12},{12,8},{16,20},{20,16},{24,28},{28,24},{1,5},{5... | collective-permute-start | bytes 393224 | tf_op jit(solution)/shard_map/ppermute | solution.py:303
  68.9 0.1 add_bitcast_fusion.1.place_ref
  68.9 6.4 %collective-permute-done.7.other_ref = bf16[512,128]{1,0:T(8,128)(2,1)S(1)} collective-permute-done((bf16[512,128]{1,0:T(8,128)(2,1)S(1)}, bf16[512,128]{1,0:T(8,128)(2,1)S(1)}, u32[]{:S(2)}, u32[]{:S(2)}) %collective-permute-start.7) | collective-permute-done | bytes 131104 | tf_op jit(solution)/shard_map/ppermute | solution.py:303
  75.3 0.5 shard_map.135.query_ref
  75.8 0.0 copy-start.1
  75.9 1.1 copy-done.3
  76.9 5.5 %shard_map.136 = (bf16[3,64,512]{2,1,0:T(8,128)(2,1)}, bf16[512,512]{1,0:T(8,128)(2,1)S(1)}) custom-call(s32[1,1]{1,0:T(1,128)} %bitcast.7.place_ref, bf16[3,512,512]{2,1,0:T(8,128)(2,1)S(1)} %bitcast.25, bf16[512,512]{1,0:T(8,128)(2,1)S(1)} %shard_map.135.query_ref, bf16[256,768]{1,0:T(8,128)(2,1)S(1)} %pad_maximum_fusion.1.refs_0_, ...), custom_call_target="tpu_custom_call" | custom-call | flops 1000 | bytes 1000 | tf_op jit(solution)/shard_map/pallas_call | solution.py:41
  82.4 1.8 %shard_map.138 = bf16[2,512,256]{2,1,0:T(8,128)(2,1)} custom-call(s32[1,2]{1,0:T(1,128)S(1)} %add_bitcast_fusion.1.place_ref, bf16[512,512]{1,0:T(8,128)(2,1)S(1)} %get-tuple-element.33.fast_ref, bf16[512,1024]{1,0:T(8,128)(2,1)S(1)} %copy-done.1), custom_call_target="tpu_custom_call" | custom-call | flops 1000 | bytes 1000 | tf_op jit(solution)/shard_map/pallas_call | solution.py:41
  84.3 0.0 copy-start.8
  84.3 1.4 %collective-permute-start.19 = (bf16[1024,256]{1,0:T(8,128)(2,1)S(1)}, bf16[1024,256]{1,0:T(8,128)(2,1)S(1)}, u32[]{:S(2)}, u32[]{:S(2)}) collective-permute-start(bf16[1024,256]{1,0:T(8,128)(2,1)S(1)} %pad_maximum_fusion), channel_id=1, source_target_pairs={{4,0},{8,4},{12,8},{16,12},{20,16},{24,20},{28,24},{5,1},{9,5},{13... | collective-permute-start | bytes 1572872 | tf_op jit(solution)/shard_map/ppermute | solution.py:292
  85.7 4.8 %collective-permute-start.18 = (bf16[1024,256]{1,0:T(8,128)(2,1)S(1)}, bf16[1024,256]{1,0:T(8,128)(2,1)S(1)}, u32[]{:S(2)}, u32[]{:S(2)}) collective-permute-start(bf16[1024,256]{1,0:T(8,128)(2,1)S(1)} %pad_maximum_fusion), channel_id=1, source_target_pairs={{0,4},{4,8},{8,12},{12,16},{16,20},{20,24},{24,28},{1,5},{5,9},{9,... | collective-permute-start | bytes 1572872 | tf_op jit(solution)/shard_map/ppermute | solution.py:292
  90.5 0.1 add_bitcast_fusion.place_ref
  90.6 1.0 shard_map.137.keep_ref
  91.6 0.1 fusion
  91.7 1.6 %collective-permute-start.17 = (bf16[512,256]{1,0:T(8,128)(2,1)S(1)}, bf16[512,256]{1,0:T(8,128)(2,1)S(1)}, u32[]{:S(2)}, u32[]{:S(2)}) collective-permute-start(bf16[512,256]{1,0:T(8,128)(2,1)S(1)} %fusion), channel_id=1, source_target_pairs={{0,2},{1,3},{2,0},{3,1},{4,6},{5,7},{6,4},{7,5},{8,10},{9,11},{10,... | collective-permute-start | bytes 786440 | tf_op jit(solution)/shard_map/ppermute | solution.py:298
  93.2 7.4 %collective-permute-done.19.next_ref = bf16[1024,256]{1,0:T(8,128)(2,1)S(1)} collective-permute-done((bf16[1024,256]{1,0:T(8,128)(2,1)S(1)}, bf16[1024,256]{1,0:T(8,128)(2,1)S(1)}, u32[]{:S(2)}, u32[]{:S(2)}) %collective-permute-start.19) | collective-permute-done | bytes 524320 | tf_op jit(solution)/shard_map/ppermute | solution.py:292
  100.6 10.0 %collective-permute-done.18.prev_ref = bf16[1024,256]{1,0:T(8,128)(2,1)S(1)} collective-permute-done((bf16[1024,256]{1,0:T(8,128)(2,1)S(1)}, bf16[1024,256]{1,0:T(8,128)(2,1)S(1)}, u32[]{:S(2)}, u32[]{:S(2)}) %collective-permute-start.18) | collective-permute-done | bytes 524320 | tf_op jit(solution)/shard_map/ppermute | solution.py:292
  110.7 4.9 %shard_map.139 = bf16[512,256]{1,0:T(8,128)(2,1)} custom-call(f32[2,2]{1,0:T(2,128)S(1)} %reshape.26.edge_ref, bf16[512,256]{1,0:T(8,128)(2,1)S(1)} %copy-done.8, bf16[2,512,256]{2,1,0:T(8,128)(2,1)S(1)} %shard_map.137.keep_ref, bf16[2,512,256]{2,1,0:T(8,128)(2,1)S(1)} %collective-permute-done.16.near_ref, ...), custom_call_target="tpu_custom_call" | custom-call | flops 805306368 | bytes 2097152 | tf_op jit(solution)/shard_map/pallas_call | solution.py:41
  (41 shorter events, 0.3 us)
Async XLA Ops:
  0.6 11.4 %copy-start.5 = (bf16[512,256]{1,0:T(8,128)(2,1)S(1)}, bf16[512,256]{1,0:T(8,128)(2,1)}, u32[]{:S(2)}) copy-start(bf16[512,256]{1,0:T(8,128)(2,1)} %values_ref.5) | copy-start | bytes 786436
  0.6 11.4 %copy-start.4 = (bf16[512,256]{1,0:T(8,128)(2,1)S(1)}, bf16[512,256]{1,0:T(8,128)(2,1)}, u32[]{:S(2)}) copy-start(bf16[512,256]{1,0:T(8,128)(2,1)} %keys_ref.5) | copy-start | bytes 786436
  0.7 11.4 %copy-start.9 = (bf16[512,256]{1,0:T(8,128)(2,1)S(1)}, bf16[512,256]{1,0:T(8,128)(2,1)}, u32[]{:S(2)}) copy-start(bf16[512,256]{1,0:T(8,128)(2,1)} %queries_ref.4) | copy-start | bytes 786436
  7.5 16.4 %copy-start.11 = (bf16[256,768]{1,0:T(8,128)(2,1)S(1)}, bf16[256,768]{1,0:T(8,128)(2,1)}, u32[]{:S(2)}) copy-start(bf16[256,768]{1,0:T(8,128)(2,1)} %get-tuple-element.23) | copy-start | bytes 1179652
  7.5 13.1 %collective-permute-start.1 = (bf16[256,768]{1,0:T(8,128)(2,1)}, bf16[256,768]{1,0:T(8,128)(2,1)S(1)}, u32[]{:S(2)}, u32[]{:S(2)}) collective-permute-start(bf16[256,768]{1,0:T(8,128)(2,1)} %get-tuple-element.22), channel_id=1, source_target_pairs={{0,4},{4,0},{8,12},{12,8},{16,20},{20,16},{24,28},{28,24},{1,5},{5... | collective-permute-start | bytes 1179656 | tf_op jit(solution)/shard_map/ppermute | solution.py:303
  10.5 13.5 %collective-permute-start.3 = (bf16[256,768]{1,0:T(8,128)(2,1)}, bf16[256,768]{1,0:T(8,128)(2,1)S(1)}, u32[]{:S(2)}, u32[]{:S(2)}) collective-permute-start(bf16[256,768]{1,0:T(8,128)(2,1)} %get-tuple-element.24), channel_id=1, source_target_pairs={{0,8},{4,12},{8,0},{12,4},{16,24},{20,28},{24,16},{28,20},{1,9},{5... | collective-permute-start | bytes 1179656 | tf_op jit(solution)/shard_map/ppermute | solution.py:303
  12.2 16.1 %collective-permute-start = (bf16[1536,128]{1,0:T(8,128)(2,1)S(1)}, bf16[1536,128]{1,0:T(8,128)(2,1)S(1)}, u32[]{:S(2)}, u32[]{:S(2)}) collective-permute-start(bf16[1536,128]{1,0:T(8,128)(2,1)S(1)} %shard_map.131), channel_id=1, source_target_pairs={{0,4},{4,0},{8,12},{12,8},{16,20},{20,16},{24,28},{28,24},{1,5},{5... | collective-permute-start | bytes 1179656 | tf_op jit(solution)/shard_map/ppermute | solution.py:303
  21.7 8.3 %collective-permute-start.2 = (bf16[128,768]{1,0:T(8,128)(2,1)S(1)}, bf16[128,768]{1,0:T(8,128)(2,1)S(1)}, u32[]{:S(2)}, u32[]{:S(2)}) collective-permute-start(bf16[128,768]{1,0:T(8,128)(2,1)S(1)} %get-tuple-element.39), channel_id=1, source_target_pairs={{0,8},{4,12},{8,0},{12,4},{16,24},{20,28},{24,16},{28,20},{1,9},{5... | collective-permute-start | bytes 589832 | tf_op jit(solution)/shard_map/ppermute | solution.py:303
  24.0 10.7 %collective-permute-start.4 = (bf16[128,768]{1,0:T(8,128)(2,1)S(1)}, bf16[128,768]{1,0:T(8,128)(2,1)S(1)}, u32[]{:S(2)}, u32[]{:S(2)}) collective-permute-start(bf16[128,768]{1,0:T(8,128)(2,1)S(1)} %get-tuple-element.37), channel_id=1, source_target_pairs={{0,16},{4,20},{8,24},{12,28},{16,0},{20,4},{24,8},{28,12},{1,17},{... | collective-permute-start | bytes 589832 | tf_op jit(solution)/shard_map/ppermute | solution.py:303
  30.1 10.9 %collective-permute-start.8 = (bf16[64,768]{1,0:T(8,128)(2,1)S(1)}, bf16[64,768]{1,0:T(8,128)(2,1)S(1)}, u32[]{:S(2)}, u32[]{:S(2)}) collective-permute-start(bf16[64,768]{1,0:T(8,128)(2,1)S(1)} %get-tuple-element.42), channel_id=1, source_target_pairs={{0,16},{4,20},{8,24},{12,28},{16,0},{20,4},{24,8},{28,12},{1,17},{... | collective-permute-start | bytes 294920 | tf_op jit(solution)/shard_map/ppermute | solution.py:303
  34.8 10.6 %collective-permute-start.10 = (bf16[64,768]{1,0:T(8,128)(2,1)S(1)}, bf16[64,768]{1,0:T(8,128)(2,1)S(1)}, u32[]{:S(2)}, u32[]{:S(2)}) collective-permute-start(bf16[64,768]{1,0:T(8,128)(2,1)S(1)} %get-tuple-element.40), channel_id=1, source_target_pairs={{0,4},{4,0},{8,12},{12,8},{16,20},{20,16},{24,28},{28,24},{1,5},{5... | collective-permute-start | bytes 294920 | tf_op jit(solution)/shard_map/ppermute | solution.py:303
  36.5 19.4 %collective-permute-start.5 = (bf16[1024,128]{1,0:T(8,128)(2,1)S(1)}, bf16[1024,128]{1,0:T(8,128)(2,1)S(1)}, u32[]{:S(2)}, u32[]{:S(2)}) collective-permute-start(bf16[1024,128]{1,0:T(8,128)(2,1)S(1)} %get-tuple-element.25.high_ref), channel_id=1, source_target_pairs={{0,8},{4,12},{8,16},{12,20},{16,24},{20,28},{1,9},{5,13},{9,17},{1... | collective-permute-start | bytes 786440 | tf_op jit(solution)/shard_map/ppermute | solution.py:292
  39.7 16.2 %collective-permute-start.6 = (bf16[1024,128]{1,0:T(8,128)(2,1)S(1)}, bf16[1024,128]{1,0:T(8,128)(2,1)S(1)}, u32[]{:S(2)}, u32[]{:S(2)}) collective-permute-start(bf16[1024,128]{1,0:T(8,128)(2,1)S(1)} %get-tuple-element.26.low_ref), channel_id=1, source_target_pairs={{8,0},{12,4},{16,8},{20,12},{24,16},{28,20},{9,1},{13,5},{17,9},{2... | collective-permute-start | bytes 786440 | tf_op jit(solution)/shard_map/ppermute | solution.py:292
  41.0 14.8 %collective-permute-start.9 = (bf16[64,768]{1,0:T(8,128)(2,1)S(1)}, bf16[64,768]{1,0:T(8,128)(2,1)S(1)}, u32[]{:S(2)}, u32[]{:S(2)}) collective-permute-start(bf16[64,768]{1,0:T(8,128)(2,1)S(1)} %add_convert_fusion.4), channel_id=1, source_target_pairs={{0,16},{4,20},{8,24},{12,28},{16,0},{20,4},{24,8},{28,12},{1,17},{... | collective-permute-start | bytes 294920 | tf_op jit(solution)/shard_map/ppermute | solution.py:303
  45.4 10.5 %collective-permute-start.11 = (bf16[64,768]{1,0:T(8,128)(2,1)S(1)}, bf16[64,768]{1,0:T(8,128)(2,1)S(1)}, u32[]{:S(2)}, u32[]{:S(2)}) collective-permute-start(bf16[64,768]{1,0:T(8,128)(2,1)S(1)} %add_convert_fusion.3), channel_id=1, source_target_pairs={{0,4},{4,0},{8,12},{12,8},{16,20},{20,16},{24,28},{28,24},{1,5},{5... | collective-permute-start | bytes 294920 | tf_op jit(solution)/shard_map/ppermute | solution.py:303
  56.0 10.0 %collective-permute-start.12 = (bf16[128,768]{1,0:T(8,128)(2,1)S(1)}, bf16[128,768]{1,0:T(8,128)(2,1)S(1)}, u32[]{:S(2)}, u32[]{:S(2)}) collective-permute-start(bf16[128,768]{1,0:T(8,128)(2,1)S(1)} %pad_maximum_fusion.3), channel_id=1, source_target_pairs={{0,8},{4,12},{8,0},{12,4},{16,24},{20,28},{24,16},{28,20},{1,9},{5... | collective-permute-start | bytes 589832 | tf_op jit(solution)/shard_map/ppermute | solution.py:303
  56.6 18.7 %copy-start.10 = (bf16[1,256,512]{2,1,0:T(8,128)(2,1)S(1)}, bf16[1,256,512]{2,1,0:T(8,128)(2,1)}, u32[]{:S(2)}) copy-start(bf16[1,256,512]{2,1,0:T(8,128)(2,1)} %param.15) | copy-start | bytes 786436
  56.6 9.4 %collective-permute-start.13 = (bf16[128,768]{1,0:T(8,128)(2,1)S(1)}, bf16[128,768]{1,0:T(8,128)(2,1)S(1)}, u32[]{:S(2)}, u32[]{:S(2)}) collective-permute-start(bf16[128,768]{1,0:T(8,128)(2,1)S(1)} %pad_maximum_fusion.4), channel_id=1, source_target_pairs={{0,16},{4,20},{8,24},{12,28},{16,0},{20,4},{24,8},{28,12},{1,17},{... | collective-permute-start | bytes 589832 | tf_op jit(solution)/shard_map/ppermute | solution.py:303
  60.9 15.0 %copy-start = (bf16[1,512,3,512]{3,1,2,0:T(8,128)(2,1)S(1)}, bf16[1,512,3,512]{3,1,2,0:T(8,128)(2,1)}, u32[]{:S(2)}) copy-start(bf16[1,512,3,512]{3,1,2,0:T(8,128)(2,1)} %param.19) | copy-start | bytes 4718596
  66.0 9.8 %copy-start.2 = (bf16[256,768]{1,0:T(8,128)(2,1)}, bf16[256,768]{1,0:T(8,128)(2,1)S(1)}, u32[]{:S(2)}) copy-start(bf16[256,768]{1,0:T(8,128)(2,1)S(1)} %pad_maximum_fusion.2.refs_2_) | copy-start | bytes 1179652
  66.1 9.8 %collective-permute-start.14 = (bf16[256,768]{1,0:T(8,128)(2,1)S(1)}, bf16[256,768]{1,0:T(8,128)(2,1)}, u32[]{:S(2)}, u32[]{:S(2)}) collective-permute-start(bf16[256,768]{1,0:T(8,128)(2,1)S(1)} %pad_maximum_fusion.1.refs_0_), channel_id=1, source_target_pairs={{0,4},{4,0},{8,12},{12,8},{16,20},{20,16},{24,28},{28,24},{1,5},{5... | collective-permute-start | bytes 1179656 | tf_op jit(solution)/shard_map/ppermute | solution.py:303
  66.5 9.4 %collective-permute-start.15 = (bf16[256,768]{1,0:T(8,128)(2,1)S(1)}, bf16[256,768]{1,0:T(8,128)(2,1)}, u32[]{:S(2)}, u32[]{:S(2)}) collective-permute-start(bf16[256,768]{1,0:T(8,128)(2,1)S(1)} %pad_maximum_fusion.2.refs_2_), channel_id=1, source_target_pairs={{0,8},{4,12},{8,0},{12,4},{16,24},{20,28},{24,16},{28,20},{1,9},{5... | collective-permute-start | bytes 1179656 | tf_op jit(solution)/shard_map/ppermute | solution.py:303
  66.9 8.4 %collective-permute-start.7 = (bf16[512,128]{1,0:T(8,128)(2,1)S(1)}, bf16[512,128]{1,0:T(8,128)(2,1)S(1)}, u32[]{:S(2)}, u32[]{:S(2)}) collective-permute-start(bf16[512,128]{1,0:T(8,128)(2,1)S(1)} %get-tuple-element.28), channel_id=1, source_target_pairs={{0,4},{4,0},{8,12},{12,8},{16,20},{20,16},{24,28},{28,24},{1,5},{5... | collective-permute-start | bytes 393224 | tf_op jit(solution)/shard_map/ppermute | solution.py:303
  75.8 6.6 %copy-start.1 = (bf16[512,1024]{1,0:T(8,128)(2,1)S(1)}, bf16[512,1024]{1,0:T(8,128)(2,1)}, u32[]{:S(2)}) copy-start(bf16[512,1024]{1,0:T(8,128)(2,1)} %map_ref.3) | copy-start | bytes 3145732
  75.9 1.1 copy-start.3
  82.4 1.8 %copy-start.6 = (bf16[512,256]{1,0:T(8,128)(2,1)S(1)}, bf16[512,256]{1,0:T(8,128)(2,1)}, u32[]{:S(2)}) copy-start(bf16[512,256]{1,0:T(8,128)(2,1)} %values_ref.7) | copy-start | bytes 786436
  82.4 1.8 %copy-start.7 = (bf16[512,256]{1,0:T(8,128)(2,1)S(1)}, bf16[512,256]{1,0:T(8,128)(2,1)}, u32[]{:S(2)}) copy-start(bf16[512,256]{1,0:T(8,128)(2,1)} %keys_ref.7) | copy-start | bytes 786436
  84.2 7.3 %collective-permute-start.16 = (bf16[2,512,256]{2,1,0:T(8,128)(2,1)}, bf16[2,512,256]{2,1,0:T(8,128)(2,1)S(1)}, u32[]{:S(2)}, u32[]{:S(2)}) collective-permute-start(bf16[2,512,256]{2,1,0:T(8,128)(2,1)} %shard_map.138), channel_id=1, source_target_pairs={{0,1},{1,0},{2,3},{3,2},{4,5},{5,4},{6,7},{7,6},{8,9},{9,8},{10,11... | collective-permute-start | bytes 1572872 | tf_op jit(solution)/shard_map/ppermute | solution.py:298
  84.3 26.4 %copy-start.8 = (bf16[512,256]{1,0:T(8,128)(2,1)S(1)}, bf16[512,256]{1,0:T(8,128)(2,1)}, u32[]{:S(2)}) copy-start(bf16[512,256]{1,0:T(8,128)(2,1)} %queries_ref.5) | copy-start | bytes 786436
  84.3 16.4 %collective-permute-start.19 = (bf16[1024,256]{1,0:T(8,128)(2,1)S(1)}, bf16[1024,256]{1,0:T(8,128)(2,1)S(1)}, u32[]{:S(2)}, u32[]{:S(2)}) collective-permute-start(bf16[1024,256]{1,0:T(8,128)(2,1)S(1)} %pad_maximum_fusion), channel_id=1, source_target_pairs={{4,0},{8,4},{12,8},{16,12},{20,16},{24,20},{28,24},{5,1},{9,5},{13... | collective-permute-start | bytes 1572872 | tf_op jit(solution)/shard_map/ppermute | solution.py:292
  85.7 24.9 %collective-permute-start.18 = (bf16[1024,256]{1,0:T(8,128)(2,1)S(1)}, bf16[1024,256]{1,0:T(8,128)(2,1)S(1)}, u32[]{:S(2)}, u32[]{:S(2)}) collective-permute-start(bf16[1024,256]{1,0:T(8,128)(2,1)S(1)} %pad_maximum_fusion), channel_id=1, source_target_pairs={{0,4},{4,8},{8,12},{12,16},{16,20},{20,24},{24,28},{1,5},{5,9},{9,... | collective-permute-start | bytes 1572872 | tf_op jit(solution)/shard_map/ppermute | solution.py:292
  91.7 19.0 %collective-permute-start.17 = (bf16[512,256]{1,0:T(8,128)(2,1)S(1)}, bf16[512,256]{1,0:T(8,128)(2,1)S(1)}, u32[]{:S(2)}, u32[]{:S(2)}) collective-permute-start(bf16[512,256]{1,0:T(8,128)(2,1)S(1)} %fusion), channel_id=1, source_target_pairs={{0,2},{1,3},{2,0},{3,1},{4,6},{5,7},{6,4},{7,5},{8,10},{9,11},{10,... | collective-permute-start | bytes 786440 | tf_op jit(solution)/shard_map/ppermute | solution.py:298

commit v9 on v8

--- a/solution.py
+++ b/solution.py
@@ -414,31 +414,29 @@
 
     both_second = jnp.concatenate([keys_second, values_second])
 
-    def second_halos(array):
-        return seq_shift(array, 1), seq_shift(array, -1)
-
     if halving:
         turns = len(bits)
         keeps, found = halving_start([gradients[:2], gradients[2:]], orders)
         for turn in range(1, turns):
             if turn == turns - 1:
                 prev_first, next_first = first_halos(*after((low_block, high_block), found))
+                prev_second = seq_shift(after(both_second, found), 1)
             keeps, found = halving_step(keeps, found, orders, turn)
         held = [((keep.astype(F32) + new.astype(F32)).astype(BF16),) for keep, new in zip(keeps, found)]
         for turn in reversed(range(turns)):
             wait = ()
             if turn == 1:
-                wait = (prev_first, next_first)
+                wait = (prev_first, next_first, prev_second)
             if turn == 0:
                 keep_first, back_first = first_attention(prev_first, next_first)
                 wait = (keep_first,)
             held = doubling_step(held, orders, turn, wait)
         gathered = [part for parts in held for part in parts]
-        prev_second, next_second = second_halos(after(both_second, (gathered, back_first)))
+        next_second = seq_shift(after(both_second, (gathered, back_first)), -1)
     else:
         gathered = lax.psum(gradients, "seq")
         keep_first, back_first = first_attention(*first_halos(low_block, high_block))
-        prev_second, next_second = second_halos(both_second)
+        prev_second, next_second = seq_shift(both_second, 1), seq_shift(both_second, -1)
     fast_query = call(
         query_kernel,
         shape((rows, fast_width), BF16),

time: 116 us -> 112 us (0.966)
  waiting for transfers between devices: 52.9 us -> 44.8 us
  starting transfers between devices: 34.2 us -> 38 us
    ppermute x4, waiting for transfers between devices: 17.5 us -> 12.1 us  [seq_shift(): lax.ppermute(value, 'seq', [(i, i + step) for i in range(peers) if 0 <= i...]
    ppermute x14, starting transfers between devices: 22 us -> 26.3 us  [seq_swap(): lax.ppermute(value, 'seq', [(i, i ^ step) for i in range(lax.axis_size('s...]
    ppermute x14, waiting for transfers between devices: 35.4 us -> 32.7 us  [seq_swap(): lax.ppermute(value, 'seq', [(i, i ^ step) for i in range(lax.axis_size('s...]
  transfers between devices with their start and end apart: 20 -> 20, of which waited for: 9 -> 8; matrix products, arithmetic and copies ran while one was open for 2% -> 1% of each run, Pallas kernels for 5% -> 5%
where the time goes in v9:
time: 112 us; the launch traced here: 111 us
  waiting for transfers between devices  44.8 us (40%)
  starting transfers between devices  38 us (34%)
  Pallas kernels  24.6 us (22%)
  local copies, waits for them, and re-layouts  2.08 us (2%)
    ppermute x14, waiting for transfers between devices, seq_swap(): lax.ppermute(value, 'seq', [(i, i ^ step) for i in range(lax.axis_size('s...  32.7 us
    ppermute x14, starting transfers between devices, seq_swap(): lax.ppermute(value, 'seq', [(i, i ^ step) for i in range(lax.axis_size('s...  26.3 us
    pallas_call x8, Pallas kernels, call(): pl.pallas_call(body, out_shape=out_shapes, in_specs=in_specs, out_specs=j...  17.7 us
    ppermute x4, waiting for transfers between devices, seq_shift(): lax.ppermute(value, 'seq', [(i, i + step) for i in range(peers) if 0 <= i...  12.1 us
    ppermute x4, starting transfers between devices, seq_shift(): lax.ppermute(value, 'seq', [(i, i + step) for i in range(peers) if 0 <= i...  10 us
    pallas_call x1, Pallas kernels, local(): pl.pallas_call(functools.partial(gradient_kernel, orders), grid=(hidden_s...  6.87 us
  transfers between devices with their start and end apart: 20, of which 8 were waited for; matrix products, arithmetic and copies ran while one was open for 1% of the time, Pallas kernels for 5%

profile of v9, /device:TPU:0, one launch (start us, length us, event | category | flops | bytes accessed | tf_op | source)
XLA Modules:
  0.0 111.2 jit_solution(15031263117861702241)
XLA Ops:
  0.7 0.0 copy-start.6
  0.7 6.9 %shard_map.133 = (bf16[256,768]{1,0:T(8,128)(2,1)}, bf16[256,768]{1,0:T(8,128)(2,1)}, bf16[256,768]{1,0:T(8,128)(2,1)}, bf16[256,768]{1,0:T(8,128)(2,1)}) custom-call(s32[1,1]{1,0:T(1,128)} %bitcast.7.place_ref, f32[1,512]{1,0:T(1,128)} %bitcast.27, bf16[512,512]{1,0:T(8,128)(2,1)} %keys_ref.6, bf16[512,512]{1,0:T(8,128)(2,1)} %values_ref.6, ...), custom_call_target="tpu_custom_call" | custom-call | flops 1000 | bytes 1000 | tf_op jit(solution)/shard_map/pallas_call | solution.py:377
  7.6 3.0 %collective-permute-start.3 = (bf16[256,768]{1,0:T(8,128)(2,1)}, bf16[256,768]{1,0:T(8,128)(2,1)S(1)}, u32[]{:S(2)}, u32[]{:S(2)}) collective-permute-start(bf16[256,768]{1,0:T(8,128)(2,1)} %get-tuple-element.25), channel_id=1, source_target_pairs={{0,8},{4,12},{8,0},{12,4},{16,24},{20,28},{24,16},{28,20},{1,9},{5... | collective-permute-start | bytes 1179656 | tf_op jit(solution)/shard_map/ppermute | solution.py:303
  10.6 1.5 %collective-permute-start.1 = (bf16[256,768]{1,0:T(8,128)(2,1)}, bf16[256,768]{1,0:T(8,128)(2,1)S(1)}, u32[]{:S(2)}, u32[]{:S(2)}) collective-permute-start(bf16[256,768]{1,0:T(8,128)(2,1)} %get-tuple-element.23), channel_id=1, source_target_pairs={{0,4},{4,0},{8,12},{12,8},{16,20},{20,16},{24,28},{28,24},{1,5},{5... | collective-permute-start | bytes 1179656 | tf_op jit(solution)/shard_map/ppermute | solution.py:303
  12.1 0.1 shard_map.131
  12.2 0.6 collective-permute-start
  12.9 7.1 %collective-permute-done.3 = bf16[256,768]{1,0:T(8,128)(2,1)S(1)} collective-permute-done((bf16[256,768]{1,0:T(8,128)(2,1)}, bf16[256,768]{1,0:T(8,128)(2,1)S(1)}, u32[]{:S(2)}, u32[]{:S(2)}) %collective-permute-start.3) | collective-permute-done | bytes 393248 | tf_op jit(solution)/shard_map/ppermute | solution.py:303
  19.9 0.1 convert_add_fusion
  20.0 2.8 %collective-permute-start.4 = (bf16[128,768]{1,0:T(8,128)(2,1)S(1)}, bf16[128,768]{1,0:T(8,128)(2,1)S(1)}, u32[]{:S(2)}, u32[]{:S(2)}) collective-permute-start(bf16[128,768]{1,0:T(8,128)(2,1)S(1)} %get-tuple-element.39), channel_id=1, source_target_pairs={{0,16},{4,20},{8,24},{12,28},{16,0},{20,4},{24,8},{28,12},{1,17},{... | collective-permute-start | bytes 589832 | tf_op jit(solution)/shard_map/ppermute | solution.py:303
  22.8 0.0 collective-permute-done.1
  22.8 0.1 convert_add_fusion.1
  22.9 1.6 %collective-permute-start.2 = (bf16[128,768]{1,0:T(8,128)(2,1)S(1)}, bf16[128,768]{1,0:T(8,128)(2,1)S(1)}, u32[]{:S(2)}, u32[]{:S(2)}) collective-permute-start(bf16[128,768]{1,0:T(8,128)(2,1)S(1)} %get-tuple-element.41), channel_id=1, source_target_pairs={{0,8},{4,12},{8,0},{12,4},{16,24},{20,28},{24,16},{28,20},{1,9},{5... | collective-permute-start | bytes 589832 | tf_op jit(solution)/shard_map/ppermute | solution.py:303
  24.6 5.2 %collective-permute-done.other_ref = bf16[1536,128]{1,0:T(8,128)(2,1)S(1)} collective-permute-done((bf16[1536,128]{1,0:T(8,128)(2,1)S(1)}, bf16[1536,128]{1,0:T(8,128)(2,1)S(1)}, u32[]{:S(2)}, u32[]{:S(2)}) %collective-permute-start) | collective-permute-done | bytes 393248 | tf_op jit(solution)/shard_map/ppermute | solution.py:303
  29.8 0.1 shard_map.132
  29.9 1.5 %collective-permute-done.4 = bf16[128,768]{1,0:T(8,128)(2,1)S(1)} collective-permute-done((bf16[128,768]{1,0:T(8,128)(2,1)S(1)}, bf16[128,768]{1,0:T(8,128)(2,1)S(1)}, u32[]{:S(2)}, u32[]{:S(2)}) %collective-permute-start.4) | collective-permute-done | bytes 196640 | tf_op jit(solution)/shard_map/ppermute | solution.py:303
  31.4 1.4 %collective-permute-start.10 = (bf16[64,768]{1,0:T(8,128)(2,1)S(1)}, bf16[64,768]{1,0:T(8,128)(2,1)S(1)}, u32[]{:S(2)}, u32[]{:S(2)}) collective-permute-start(bf16[64,768]{1,0:T(8,128)(2,1)S(1)} %get-tuple-element.42), channel_id=1, source_target_pairs={{0,4},{4,0},{8,12},{12,8},{16,20},{20,16},{24,28},{28,24},{1,5},{5... | collective-permute-start | bytes 294920 | tf_op jit(solution)/shard_map/ppermute | solution.py:303
  32.9 1.3 %collective-permute-start.8 = (bf16[64,768]{1,0:T(8,128)(2,1)S(1)}, bf16[64,768]{1,0:T(8,128)(2,1)S(1)}, u32[]{:S(2)}, u32[]{:S(2)}) collective-permute-start(bf16[64,768]{1,0:T(8,128)(2,1)S(1)} %get-tuple-element.44), channel_id=1, source_target_pairs={{0,16},{4,20},{8,24},{12,28},{16,0},{20,4},{24,8},{28,12},{1,17},{... | collective-permute-start | bytes 294920 | tf_op jit(solution)/shard_map/ppermute | solution.py:303
  34.2 4.7 %collective-permute-start.5 = (bf16[1024,128]{1,0:T(8,128)(2,1)S(1)}, bf16[1024,128]{1,0:T(8,128)(2,1)S(1)}, u32[]{:S(2)}, u32[]{:S(2)}) collective-permute-start(bf16[1024,128]{1,0:T(8,128)(2,1)S(1)} %get-tuple-element.26.high_ref), channel_id=1, source_target_pairs={{0,8},{4,12},{8,16},{12,20},{16,24},{20,28},{1,9},{5,13},{9,17},{1... | collective-permute-start | bytes 786440 | tf_op jit(solution)/shard_map/ppermute | solution.py:292
  38.9 1.3 %collective-permute-start.6 = (bf16[1024,128]{1,0:T(8,128)(2,1)S(1)}, bf16[1024,128]{1,0:T(8,128)(2,1)S(1)}, u32[]{:S(2)}, u32[]{:S(2)}) collective-permute-start(bf16[1024,128]{1,0:T(8,128)(2,1)S(1)} %get-tuple-element.27.low_ref), channel_id=1, source_target_pairs={{8,0},{12,4},{16,8},{20,12},{24,16},{28,20},{9,1},{13,5},{17,9},{2... | collective-permute-start | bytes 786440 | tf_op jit(solution)/shard_map/ppermute | solution.py:292
  40.2 2.4 %collective-permute-start.12 = (bf16[1024,256]{1,0:T(8,128)(2,1)S(1)}, bf16[1024,256]{1,0:T(8,128)(2,1)S(1)}, u32[]{:S(2)}, u32[]{:S(2)}) collective-permute-start(bf16[1024,256]{1,0:T(8,128)(2,1)S(1)} %constant_dynamic-update-slice_fusion), channel_id=1, source_target_pairs={{0,4},{4,8},{8,12},{12,16},{16,20},{20,24},{24,28},{1,5},{5,9},{9,... | collective-permute-start | bytes 1572872 | tf_op jit(solution)/shard_map/ppermute | solution.py:292
  42.7 3.7 %collective-permute-start.11 = (bf16[64,768]{1,0:T(8,128)(2,1)S(1)}, bf16[64,768]{1,0:T(8,128)(2,1)S(1)}, u32[]{:S(2)}, u32[]{:S(2)}) collective-permute-start(bf16[64,768]{1,0:T(8,128)(2,1)S(1)} %add_convert_fusion.3), channel_id=1, source_target_pairs={{0,4},{4,0},{8,12},{12,8},{16,20},{20,16},{24,28},{28,24},{1,5},{5... | collective-permute-start | bytes 294920 | tf_op jit(solution)/shard_map/ppermute | solution.py:303
  46.4 0.1 collective-permute-start.9
  46.5 8.7 %collective-permute-done.11 = bf16[64,768]{1,0:T(8,128)(2,1)S(1)} collective-permute-done((bf16[64,768]{1,0:T(8,128)(2,1)S(1)}, bf16[64,768]{1,0:T(8,128)(2,1)S(1)}, u32[]{:S(2)}, u32[]{:S(2)}) %collective-permute-start.11) | collective-permute-done | bytes 98336 | tf_op jit(solution)/shard_map/ppermute | solution.py:303
  55.3 0.8 copy-done.10
  56.1 6.6 %collective-permute-start.14 = (bf16[128,768]{1,0:T(8,128)(2,1)S(1)}, bf16[128,768]{1,0:T(8,128)(2,1)S(1)}, u32[]{:S(2)}, u32[]{:S(2)}) collective-permute-start(bf16[128,768]{1,0:T(8,128)(2,1)S(1)} %pad_maximum_fusion.3), channel_id=1, source_target_pairs={{0,16},{4,20},{8,24},{12,28},{16,0},{20,4},{24,8},{28,12},{1,17},{... | collective-permute-start | bytes 589832 | tf_op jit(solution)/shard_map/ppermute | solution.py:303
  62.7 0.1 pad_maximum_fusion.4
  62.8 0.1 reshape.26.edge_ref
  62.9 4.0 %shard_map.134 = (bf16[512,128]{1,0:T(8,128)(2,1)S(1)}, bf16[512,128]{1,0:T(8,128)(2,1)S(1)}) custom-call(f32[2,2]{1,0:T(2,128)S(1)} %reshape.26.edge_ref, s32[1,1]{1,0:T(1,128)} %bitcast.10.side_ref, bf16[512,256]{1,0:T(8,128)(2,1)S(1)} %copy-done.13, bf16[1536,128]{1,0:T(8,128)(2,1)S(1)} %collective-permute-done.other_ref, ...), custom_call_target="tpu_custom_call" | custom-call | flops 805306368 | bytes 2097152 | tf_op jit(solution)/shard_map/pallas_call | solution.py:41
  66.9 1.7 %collective-permute-done.14 = bf16[128,768]{1,0:T(8,128)(2,1)S(1)} collective-permute-done((bf16[128,768]{1,0:T(8,128)(2,1)S(1)}, bf16[128,768]{1,0:T(8,128)(2,1)S(1)}, u32[]{:S(2)}, u32[]{:S(2)}) %collective-permute-start.14) | collective-permute-done | bytes 196640 | tf_op jit(solution)/shard_map/ppermute | solution.py:303
  68.6 0.7 collective-permute-done.13
  69.4 1.9 %collective-permute-start.15 = (bf16[256,768]{1,0:T(8,128)(2,1)S(1)}, bf16[256,768]{1,0:T(8,128)(2,1)}, u32[]{:S(2)}, u32[]{:S(2)}) collective-permute-start(bf16[256,768]{1,0:T(8,128)(2,1)S(1)} %pad_maximum_fusion.refs_0_), channel_id=1, source_target_pairs={{0,4},{4,0},{8,12},{12,8},{16,20},{20,16},{24,28},{28,24},{1,5},{5... | collective-permute-start | bytes 1179656 | tf_op jit(solution)/shard_map/ppermute | solution.py:303
  71.3 1.7 %collective-permute-start.16 = (bf16[256,768]{1,0:T(8,128)(2,1)S(1)}, bf16[256,768]{1,0:T(8,128)(2,1)}, u32[]{:S(2)}, u32[]{:S(2)}) collective-permute-start(bf16[256,768]{1,0:T(8,128)(2,1)S(1)} %pad_maximum_fusion.1.refs_2_), channel_id=1, source_target_pairs={{0,8},{4,12},{8,0},{12,4},{16,24},{20,28},{24,16},{28,20},{1,9},{5... | collective-permute-start | bytes 1179656 | tf_op jit(solution)/shard_map/ppermute | solution.py:303
  72.9 0.1 collective-permute-start.7
  73.0 0.1 add_bitcast_fusion.1.place_ref
  73.1 7.8 %collective-permute-done.7.other_ref = bf16[512,128]{1,0:T(8,128)(2,1)S(1)} collective-permute-done((bf16[512,128]{1,0:T(8,128)(2,1)S(1)}, bf16[512,128]{1,0:T(8,128)(2,1)S(1)}, u32[]{:S(2)}, u32[]{:S(2)}) %collective-permute-start.7) | collective-permute-done | bytes 131104 | tf_op jit(solution)/shard_map/ppermute | solution.py:303
  80.9 0.5 shard_map.135.query_ref
  81.4 0.0 copy-start.1
  81.4 1.1 copy-done.3
  82.5 5.5 %shard_map.136 = (bf16[3,64,512]{2,1,0:T(8,128)(2,1)}, bf16[512,512]{1,0:T(8,128)(2,1)S(1)}) custom-call(s32[1,1]{1,0:T(1,128)} %bitcast.7.place_ref, bf16[3,512,512]{2,1,0:T(8,128)(2,1)S(1)} %bitcast.25, bf16[512,512]{1,0:T(8,128)(2,1)S(1)} %shard_map.135.query_ref, bf16[256,768]{1,0:T(8,128)(2,1)S(1)} %copy-done.3, ...), custom_call_target="tpu_custom_call" | custom-call | flops 1000 | bytes 1000 | tf_op jit(solution)/shard_map/pallas_call | solution.py:41
  88.0 1.8 %shard_map.138 = bf16[2,512,256]{2,1,0:T(8,128)(2,1)} custom-call(s32[1,2]{1,0:T(1,128)S(1)} %add_bitcast_fusion.1.place_ref, bf16[512,512]{1,0:T(8,128)(2,1)S(1)} %get-tuple-element.35.fast_ref, bf16[512,1024]{1,0:T(8,128)(2,1)S(1)} %copy-done.1), custom_call_target="tpu_custom_call" | custom-call | flops 1000 | bytes 1000 | tf_op jit(solution)/shard_map/pallas_call | solution.py:41
  89.8 0.1 collective-permute-start.17
  89.9 1.6 %collective-permute-start.19 = (bf16[1024,256]{1,0:T(8,128)(2,1)}, bf16[1024,256]{1,0:T(8,128)(2,1)S(1)}, u32[]{:S(2)}, u32[]{:S(2)}) collective-permute-start(bf16[1024,256]{1,0:T(8,128)(2,1)} %copy-done.17), channel_id=1, source_target_pairs={{4,0},{8,4},{12,8},{16,12},{20,16},{24,20},{28,24},{5,1},{9,5},{13... | collective-permute-start | bytes 1572872 | tf_op jit(solution)/shard_map/ppermute | solution.py:292
  91.5 0.1 add_bitcast_fusion.place_ref
  91.6 1.0 shard_map.137.keep_ref
  92.6 0.1 fusion
  92.7 1.5 %collective-permute-start.18 = (bf16[512,256]{1,0:T(8,128)(2,1)S(1)}, bf16[512,256]{1,0:T(8,128)(2,1)S(1)}, u32[]{:S(2)}, u32[]{:S(2)}) collective-permute-start(bf16[512,256]{1,0:T(8,128)(2,1)S(1)} %fusion), channel_id=1, source_target_pairs={{0,2},{1,3},{2,0},{3,1},{4,6},{5,7},{6,4},{7,5},{8,10},{9,11},{10,... | collective-permute-start | bytes 786440 | tf_op jit(solution)/shard_map/ppermute | solution.py:298
  94.2 12.1 %collective-permute-done.19.next_ref = bf16[1024,256]{1,0:T(8,128)(2,1)S(1)} collective-permute-done((bf16[1024,256]{1,0:T(8,128)(2,1)}, bf16[1024,256]{1,0:T(8,128)(2,1)S(1)}, u32[]{:S(2)}, u32[]{:S(2)}) %collective-permute-start.19) | collective-permute-done | bytes 524320 | tf_op jit(solution)/shard_map/ppermute | solution.py:292
  106.3 4.9 %shard_map.139 = bf16[512,256]{1,0:T(8,128)(2,1)} custom-call(f32[2,2]{1,0:T(2,128)S(1)} %reshape.26.edge_ref, bf16[512,256]{1,0:T(8,128)(2,1)S(1)} %copy-done.12, bf16[2,512,256]{2,1,0:T(8,128)(2,1)S(1)} %shard_map.137.keep_ref, bf16[2,512,256]{2,1,0:T(8,128)(2,1)S(1)} %collective-permute-done.17.near_ref, ...), custom_call_target="tpu_custom_call" | custom-call | flops 805306368 | bytes 2097152 | tf_op jit(solution)/shard_map/pallas_call | solution.py:41
  (54 shorter events, 0.3 us)
Async XLA Ops:
  0.6 11.5 %copy-start.13 = (bf16[512,256]{1,0:T(8,128)(2,1)S(1)}, bf16[512,256]{1,0:T(8,128)(2,1)}, u32[]{:S(2)}) copy-start(bf16[512,256]{1,0:T(8,128)(2,1)} %queries_ref.4) | copy-start | bytes 786436
  0.6 11.5 %copy-start.8 = (bf16[512,256]{1,0:T(8,128)(2,1)S(1)}, bf16[512,256]{1,0:T(8,128)(2,1)}, u32[]{:S(2)}) copy-start(bf16[512,256]{1,0:T(8,128)(2,1)} %keys_ref.5) | copy-start | bytes 786436
  0.7 11.5 %copy-start.9 = (bf16[512,256]{1,0:T(8,128)(2,1)S(1)}, bf16[512,256]{1,0:T(8,128)(2,1)}, u32[]{:S(2)}) copy-start(bf16[512,256]{1,0:T(8,128)(2,1)} %values_ref.5) | copy-start | bytes 786436
  0.7 12.1 %copy-start.4 = (bf16[512,256]{1,0:T(8,128)(2,1)S(1)}, bf16[512,256]{1,0:T(8,128)(2,1)}, u32[]{:S(2)}) copy-start(bf16[512,256]{1,0:T(8,128)(2,1)} %keys_ref.7) | copy-start | bytes 786436
  0.7 12.1 %copy-start.6 = (bf16[512,256]{1,0:T(8,128)(2,1)S(1)}, bf16[512,256]{1,0:T(8,128)(2,1)}, u32[]{:S(2)}) copy-start(bf16[512,256]{1,0:T(8,128)(2,1)} %values_ref.7) | copy-start | bytes 786436
  7.6 12.4 %copy-start.16 = (bf16[256,768]{1,0:T(8,128)(2,1)S(1)}, bf16[256,768]{1,0:T(8,128)(2,1)}, u32[]{:S(2)}) copy-start(bf16[256,768]{1,0:T(8,128)(2,1)} %get-tuple-element.24) | copy-start | bytes 1179652
  7.6 12.4 %collective-permute-start.3 = (bf16[256,768]{1,0:T(8,128)(2,1)}, bf16[256,768]{1,0:T(8,128)(2,1)S(1)}, u32[]{:S(2)}, u32[]{:S(2)}) collective-permute-start(bf16[256,768]{1,0:T(8,128)(2,1)} %get-tuple-element.25), channel_id=1, source_target_pairs={{0,8},{4,12},{8,0},{12,4},{16,24},{20,28},{24,16},{28,20},{1,9},{5... | collective-permute-start | bytes 1179656 | tf_op jit(solution)/shard_map/ppermute | solution.py:303
  10.6 12.3 %collective-permute-start.1 = (bf16[256,768]{1,0:T(8,128)(2,1)}, bf16[256,768]{1,0:T(8,128)(2,1)S(1)}, u32[]{:S(2)}, u32[]{:S(2)}) collective-permute-start(bf16[256,768]{1,0:T(8,128)(2,1)} %get-tuple-element.23), channel_id=1, source_target_pairs={{0,4},{4,0},{8,12},{12,8},{16,20},{20,16},{24,28},{28,24},{1,5},{5... | collective-permute-start | bytes 1179656 | tf_op jit(solution)/shard_map/ppermute | solution.py:303
  12.1 10.7 %copy-start.15 = (bf16[256,768]{1,0:T(8,128)(2,1)S(1)}, bf16[256,768]{1,0:T(8,128)(2,1)}, u32[]{:S(2)}) copy-start(bf16[256,768]{1,0:T(8,128)(2,1)} %get-tuple-element.22) | copy-start | bytes 1179652
  12.2 17.6 %collective-permute-start = (bf16[1536,128]{1,0:T(8,128)(2,1)S(1)}, bf16[1536,128]{1,0:T(8,128)(2,1)S(1)}, u32[]{:S(2)}, u32[]{:S(2)}) collective-permute-start(bf16[1536,128]{1,0:T(8,128)(2,1)S(1)} %shard_map.131), channel_id=1, source_target_pairs={{0,4},{4,0},{8,12},{12,8},{16,20},{20,16},{24,28},{28,24},{1,5},{5... | collective-permute-start | bytes 1179656 | tf_op jit(solution)/shard_map/ppermute | solution.py:303
  12.8 42.4 %copy-start.17 = (bf16[1024,256]{1,0:T(8,128)(2,1)}, bf16[1024,256]{1,0:T(8,128)(2,1)S(1)}, u32[]{:S(2)}) copy-start(bf16[1024,256]{1,0:T(8,128)(2,1)S(1)} %constant_dynamic-update-slice_fusion) | copy-start | bytes 1572868
  20.0 11.4 %collective-permute-start.4 = (bf16[128,768]{1,0:T(8,128)(2,1)S(1)}, bf16[128,768]{1,0:T(8,128)(2,1)S(1)}, u32[]{:S(2)}, u32[]{:S(2)}) collective-permute-start(bf16[128,768]{1,0:T(8,128)(2,1)S(1)} %get-tuple-element.39), channel_id=1, source_target_pairs={{0,16},{4,20},{8,24},{12,28},{16,0},{20,4},{24,8},{28,12},{1,17},{... | collective-permute-start | bytes 589832 | tf_op jit(solution)/shard_map/ppermute | solution.py:303
  22.9 9.9 %collective-permute-start.2 = (bf16[128,768]{1,0:T(8,128)(2,1)S(1)}, bf16[128,768]{1,0:T(8,128)(2,1)S(1)}, u32[]{:S(2)}, u32[]{:S(2)}) collective-permute-start(bf16[128,768]{1,0:T(8,128)(2,1)S(1)} %get-tuple-element.41), channel_id=1, source_target_pairs={{0,8},{4,12},{8,0},{12,4},{16,24},{20,28},{24,16},{28,20},{1,9},{5... | collective-permute-start | bytes 589832 | tf_op jit(solution)/shard_map/ppermute | solution.py:303
  31.4 11.2 %collective-permute-start.10 = (bf16[64,768]{1,0:T(8,128)(2,1)S(1)}, bf16[64,768]{1,0:T(8,128)(2,1)S(1)}, u32[]{:S(2)}, u32[]{:S(2)}) collective-permute-start(bf16[64,768]{1,0:T(8,128)(2,1)S(1)} %get-tuple-element.42), channel_id=1, source_target_pairs={{0,4},{4,0},{8,12},{12,8},{16,20},{20,16},{24,28},{28,24},{1,5},{5... | collective-permute-start | bytes 294920 | tf_op jit(solution)/shard_map/ppermute | solution.py:303
  32.9 13.5 %collective-permute-start.8 = (bf16[64,768]{1,0:T(8,128)(2,1)S(1)}, bf16[64,768]{1,0:T(8,128)(2,1)S(1)}, u32[]{:S(2)}, u32[]{:S(2)}) collective-permute-start(bf16[64,768]{1,0:T(8,128)(2,1)S(1)} %get-tuple-element.44), channel_id=1, source_target_pairs={{0,16},{4,20},{8,24},{12,28},{16,0},{20,4},{24,8},{28,12},{1,17},{... | collective-permute-start | bytes 294920 | tf_op jit(solution)/shard_map/ppermute | solution.py:303
  34.2 21.0 %collective-permute-start.5 = (bf16[1024,128]{1,0:T(8,128)(2,1)S(1)}, bf16[1024,128]{1,0:T(8,128)(2,1)S(1)}, u32[]{:S(2)}, u32[]{:S(2)}) collective-permute-start(bf16[1024,128]{1,0:T(8,128)(2,1)S(1)} %get-tuple-element.26.high_ref), channel_id=1, source_target_pairs={{0,8},{4,12},{8,16},{12,20},{16,24},{20,28},{1,9},{5,13},{9,17},{1... | collective-permute-start | bytes 786440 | tf_op jit(solution)/shard_map/ppermute | solution.py:292
  38.9 16.3 %collective-permute-start.6 = (bf16[1024,128]{1,0:T(8,128)(2,1)S(1)}, bf16[1024,128]{1,0:T(8,128)(2,1)S(1)}, u32[]{:S(2)}, u32[]{:S(2)}) collective-permute-start(bf16[1024,128]{1,0:T(8,128)(2,1)S(1)} %get-tuple-element.27.low_ref), channel_id=1, source_target_pairs={{8,0},{12,4},{16,8},{20,12},{24,16},{28,20},{9,1},{13,5},{17,9},{2... | collective-permute-start | bytes 786440 | tf_op jit(solution)/shard_map/ppermute | solution.py:292
  40.2 15.0 %collective-permute-start.12 = (bf16[1024,256]{1,0:T(8,128)(2,1)S(1)}, bf16[1024,256]{1,0:T(8,128)(2,1)S(1)}, u32[]{:S(2)}, u32[]{:S(2)}) collective-permute-start(bf16[1024,256]{1,0:T(8,128)(2,1)S(1)} %constant_dynamic-update-slice_fusion), channel_id=1, source_target_pairs={{0,4},{4,8},{8,12},{12,16},{16,20},{20,24},{24,28},{1,5},{5,9},{9,... | collective-permute-start | bytes 1572872 | tf_op jit(solution)/shard_map/ppermute | solution.py:292
  42.7 12.5 %collective-permute-start.11 = (bf16[64,768]{1,0:T(8,128)(2,1)S(1)}, bf16[64,768]{1,0:T(8,128)(2,1)S(1)}, u32[]{:S(2)}, u32[]{:S(2)}) collective-permute-start(bf16[64,768]{1,0:T(8,128)(2,1)S(1)} %add_convert_fusion.3), channel_id=1, source_target_pairs={{0,4},{4,0},{8,12},{12,8},{16,20},{20,16},{24,28},{28,24},{1,5},{5... | collective-permute-start | bytes 294920 | tf_op jit(solution)/shard_map/ppermute | solution.py:303
  46.4 8.8 %collective-permute-start.9 = (bf16[64,768]{1,0:T(8,128)(2,1)S(1)}, bf16[64,768]{1,0:T(8,128)(2,1)S(1)}, u32[]{:S(2)}, u32[]{:S(2)}) collective-permute-start(bf16[64,768]{1,0:T(8,128)(2,1)S(1)} %add_convert_fusion.4), channel_id=1, source_target_pairs={{0,16},{4,20},{8,24},{12,28},{16,0},{20,4},{24,8},{28,12},{1,17},{... | collective-permute-start | bytes 294920 | tf_op jit(solution)/shard_map/ppermute | solution.py:303
  55.3 0.8 copy-start.10
  56.1 12.5 %collective-permute-start.14 = (bf16[128,768]{1,0:T(8,128)(2,1)S(1)}, bf16[128,768]{1,0:T(8,128)(2,1)S(1)}, u32[]{:S(2)}, u32[]{:S(2)}) collective-permute-start(bf16[128,768]{1,0:T(8,128)(2,1)S(1)} %pad_maximum_fusion.3), channel_id=1, source_target_pairs={{0,16},{4,20},{8,24},{12,28},{16,0},{20,4},{24,8},{28,12},{1,17},{... | collective-permute-start | bytes 589832 | tf_op jit(solution)/shard_map/ppermute | solution.py:303
  62.9 18.0 %copy-start.14 = (bf16[1,256,512]{2,1,0:T(8,128)(2,1)S(1)}, bf16[1,256,512]{2,1,0:T(8,128)(2,1)}, u32[]{:S(2)}) copy-start(bf16[1,256,512]{2,1,0:T(8,128)(2,1)} %param.15) | copy-start | bytes 786436
  62.9 6.4 %collective-permute-start.13 = (bf16[128,768]{1,0:T(8,128)(2,1)S(1)}, bf16[128,768]{1,0:T(8,128)(2,1)S(1)}, u32[]{:S(2)}, u32[]{:S(2)}) collective-permute-start(bf16[128,768]{1,0:T(8,128)(2,1)S(1)} %pad_maximum_fusion.2), channel_id=1, source_target_pairs={{0,8},{4,12},{8,0},{12,4},{16,24},{20,28},{24,16},{28,20},{1,9},{5... | collective-permute-start | bytes 589832 | tf_op jit(solution)/shard_map/ppermute | solution.py:303
  66.9 14.5 %copy-start = (bf16[1,512,3,512]{3,1,2,0:T(8,128)(2,1)S(1)}, bf16[1,512,3,512]{3,1,2,0:T(8,128)(2,1)}, u32[]{:S(2)}) copy-start(bf16[1,512,3,512]{3,1,2,0:T(8,128)(2,1)} %param.19) | copy-start | bytes 4718596
  69.4 12.0 %copy-start.2 = (bf16[256,768]{1,0:T(8,128)(2,1)}, bf16[256,768]{1,0:T(8,128)(2,1)S(1)}, u32[]{:S(2)}) copy-start(bf16[256,768]{1,0:T(8,128)(2,1)S(1)} %pad_maximum_fusion.refs_0_) | copy-start | bytes 1179652
  69.4 12.0 %collective-permute-start.15 = (bf16[256,768]{1,0:T(8,128)(2,1)S(1)}, bf16[256,768]{1,0:T(8,128)(2,1)}, u32[]{:S(2)}, u32[]{:S(2)}) collective-permute-start(bf16[256,768]{1,0:T(8,128)(2,1)S(1)} %pad_maximum_fusion.refs_0_), channel_id=1, source_target_pairs={{0,4},{4,0},{8,12},{12,8},{16,20},{20,16},{24,28},{28,24},{1,5},{5... | collective-permute-start | bytes 1179656 | tf_op jit(solution)/shard_map/ppermute | solution.py:303
  71.3 10.2 %collective-permute-start.16 = (bf16[256,768]{1,0:T(8,128)(2,1)S(1)}, bf16[256,768]{1,0:T(8,128)(2,1)}, u32[]{:S(2)}, u32[]{:S(2)}) collective-permute-start(bf16[256,768]{1,0:T(8,128)(2,1)S(1)} %pad_maximum_fusion.1.refs_2_), channel_id=1, source_target_pairs={{0,8},{4,12},{8,0},{12,4},{16,24},{20,28},{24,16},{28,20},{1,9},{5... | collective-permute-start | bytes 1179656 | tf_op jit(solution)/shard_map/ppermute | solution.py:303
  72.9 7.9 %collective-permute-start.7 = (bf16[512,128]{1,0:T(8,128)(2,1)S(1)}, bf16[512,128]{1,0:T(8,128)(2,1)S(1)}, u32[]{:S(2)}, u32[]{:S(2)}) collective-permute-start(bf16[512,128]{1,0:T(8,128)(2,1)S(1)} %get-tuple-element.29), channel_id=1, source_target_pairs={{0,4},{4,0},{8,12},{12,8},{16,20},{20,16},{24,28},{28,24},{1,5},{5... | collective-permute-start | bytes 393224 | tf_op jit(solution)/shard_map/ppermute | solution.py:303
  81.4 6.6 %copy-start.1 = (bf16[512,1024]{1,0:T(8,128)(2,1)S(1)}, bf16[512,1024]{1,0:T(8,128)(2,1)}, u32[]{:S(2)}) copy-start(bf16[512,1024]{1,0:T(8,128)(2,1)} %map_ref.3) | copy-start | bytes 3145732
  81.4 1.1 copy-start.3
  89.8 16.5 %copy-start.5 = (bf16[512,256]{1,0:T(8,128)(2,1)S(1)}, bf16[512,256]{1,0:T(8,128)(2,1)}, u32[]{:S(2)}) copy-start(bf16[512,256]{1,0:T(8,128)(2,1)} %keys_ref.7) | copy-start | bytes 786436
  89.8 16.5 %copy-start.7 = (bf16[512,256]{1,0:T(8,128)(2,1)S(1)}, bf16[512,256]{1,0:T(8,128)(2,1)}, u32[]{:S(2)}) copy-start(bf16[512,256]{1,0:T(8,128)(2,1)} %values_ref.7) | copy-start | bytes 786436
  89.8 16.5 %copy-start.11 = (bf16[1024,256]{1,0:T(8,128)(2,1)S(1)}, bf16[1024,256]{1,0:T(8,128)(2,1)}, u32[]{:S(2)}) copy-start(bf16[1024,256]{1,0:T(8,128)(2,1)} %copy-done.10) | copy-start | bytes 1572868
  89.8 16.5 %copy-start.12 = (bf16[512,256]{1,0:T(8,128)(2,1)S(1)}, bf16[512,256]{1,0:T(8,128)(2,1)}, u32[]{:S(2)}) copy-start(bf16[512,256]{1,0:T(8,128)(2,1)} %queries_ref.5) | copy-start | bytes 786436
  89.8 2.8 %collective-permute-start.17 = (bf16[2,512,256]{2,1,0:T(8,128)(2,1)}, bf16[2,512,256]{2,1,0:T(8,128)(2,1)S(1)}, u32[]{:S(2)}, u32[]{:S(2)}) collective-permute-start(bf16[2,512,256]{2,1,0:T(8,128)(2,1)} %shard_map.138), channel_id=1, source_target_pairs={{0,1},{1,0},{2,3},{3,2},{4,5},{5,4},{6,7},{7,6},{8,9},{9,8},{10,11... | collective-permute-start | bytes 1572872 | tf_op jit(solution)/shard_map/ppermute | solution.py:298
  89.9 16.4 %collective-permute-start.19 = (bf16[1024,256]{1,0:T(8,128)(2,1)}, bf16[1024,256]{1,0:T(8,128)(2,1)S(1)}, u32[]{:S(2)}, u32[]{:S(2)}) collective-permute-start(bf16[1024,256]{1,0:T(8,128)(2,1)} %copy-done.17), channel_id=1, source_target_pairs={{4,0},{8,4},{12,8},{16,12},{20,16},{24,20},{28,24},{5,1},{9,5},{13... | collective-permute-start | bytes 1572872 | tf_op jit(solution)/shard_map/ppermute | solution.py:292
  92.7 13.6 %collective-permute-start.18 = (bf16[512,256]{1,0:T(8,128)(2,1)S(1)}, bf16[512,256]{1,0:T(8,128)(2,1)S(1)}, u32[]{:S(2)}, u32[]{:S(2)}) collective-permute-start(bf16[512,256]{1,0:T(8,128)(2,1)S(1)} %fusion), channel_id=1, source_target_pairs={{0,2},{1,3},{2,0},{3,1},{4,6},{5,7},{6,4},{7,5},{8,10},{9,11},{10,... | collective-permute-start | bytes 786440 | tf_op jit(solution)/shard_map/ppermute | solution.py:298

commit v10 on v9

--- a/solution.py
+++ b/solution.py
@@ -420,19 +420,19 @@
         for turn in range(1, turns):
             if turn == turns - 1:
                 prev_first, next_first = first_halos(*after((low_block, high_block), found))
-                prev_second = seq_shift(after(both_second, found), 1)
+                both_second = after(both_second, found)
+                prev_second, next_second = seq_shift(both_second, 1), seq_shift(both_second, -1)
             keeps, found = halving_step(keeps, found, orders, turn)
         held = [((keep.astype(F32) + new.astype(F32)).astype(BF16),) for keep, new in zip(keeps, found)]
         for turn in reversed(range(turns)):
             wait = ()
             if turn == 1:
-                wait = (prev_first, next_first, prev_second)
+                wait = (prev_first, next_first, prev_second, next_second)
             if turn == 0:
                 keep_first, back_first = first_attention(prev_first, next_first)
                 wait = (keep_first,)
             held = doubling_step(held, orders, turn, wait)
         gathered = [part for parts in held for part in parts]
-        next_second = seq_shift(after(both_second, (gathered, back_first)), -1)
     else:
         gathered = lax.psum(gradients, "seq")
         keep_first, back_first = first_attention(*first_halos(low_block, high_block))

time: 112 us -> 127 us (1.13)
  waiting for transfers between devices: 44.8 us -> 58.9 us
    ppermute x14, waiting for transfers between devices: 32.7 us -> 51 us  [seq_swap(): lax.ppermute(value, 'seq', [(i, i ^ step) for i in range(lax.axis_size('s...]
    ppermute x4, waiting for transfers between devices: 12.1 us -> 0.01 us  [seq_shift(): lax.ppermute(value, 'seq', [(i, i + step) for i in range(peers) if 0 <= i...]
    ppermute x2, waiting for transfers between devices: 0.01 us -> 7.87 us  [head_swap(): lax.ppermute(value, 'head', [(i, i ^ bit) for i in range(lax.axis_size('h...]
    unnamed x37 -> x36, local copies, waits for them, and re-layouts: 1.98 us -> 2.75 us
  transfers between devices with their start and end apart: 20 -> 20, of which waited for: 8 -> 11; matrix products, arithmetic and copies ran while one was open for 1% -> 1% of each run, Pallas kernels for 5% -> 4%
where the time goes in v10:
time: 127 us
  waiting for transfers between devices  58.9 us (46%)
  starting transfers between devices  38 us (30%)
  Pallas kernels  24.6 us (19%)
  local copies, waits for them, and re-layouts  2.83 us (2%)
  other arithmetic  1.74 us (1%)
    ppermute x14, waiting for transfers between devices, seq_swap(): lax.ppermute(value, 'seq', [(i, i ^ step) for i in range(lax.axis_size('s...  51 us
    ppermute x14, starting transfers between devices, seq_swap(): lax.ppermute(value, 'seq', [(i, i ^ step) for i in range(lax.axis_size('s...  26.4 us
    pallas_call x8, Pallas kernels, call(): pl.pallas_call(body, out_shape=out_shapes, in_specs=in_specs, out_specs=j...  17.7 us
    ppermute x4, starting transfers between devices, seq_shift(): lax.ppermute(value, 'seq', [(i, i + step) for i in range(peers) if 0 <= i...  10 us
    ppermute x2, waiting for transfers between devices, head_swap(): lax.ppermute(value, 'head', [(i, i ^ bit) for i in range(lax.axis_size('h...  7.87 us
    pallas_call x1, Pallas kernels, local(): pl.pallas_call(functools.partial(gradient_kernel, orders), grid=(hidden_s...  6.82 us
    unnamed x36, local copies, waits for them, and re-layouts  2.75 us
  transfers between devices with their start and end apart: 20, of which 11 were waited for; matrix products, arithmetic and copies ran while one was open for 1% of the time, Pallas kernels for 4%

profile of v10, /device:TPU:0, one launch (start us, length us, event | category | flops | bytes accessed | tf_op | source)
XLA Modules:
  0.0 127.0 jit_solution(14761326709433352796)
XLA Ops:
  0.7 6.8 %shard_map.133 = (bf16[256,768]{1,0:T(8,128)(2,1)}, bf16[256,768]{1,0:T(8,128)(2,1)}, bf16[256,768]{1,0:T(8,128)(2,1)}, bf16[256,768]{1,0:T(8,128)(2,1)}) custom-call(s32[1,1]{1,0:T(1,128)} %bitcast.7.place_ref, f32[1,512]{1,0:T(1,128)} %bitcast.27, bf16[512,512]{1,0:T(8,128)(2,1)} %keys_ref.6, bf16[512,512]{1,0:T(8,128)(2,1)} %values_ref.6, ...), custom_call_target="tpu_custom_call" | custom-call | flops 1000 | bytes 1000 | tf_op jit(solution)/shard_map/pallas_call | solution.py:377
  7.5 3.0 %collective-permute-start.3 = (bf16[256,768]{1,0:T(8,128)(2,1)}, bf16[256,768]{1,0:T(8,128)(2,1)S(1)}, u32[]{:S(2)}, u32[]{:S(2)}) collective-permute-start(bf16[256,768]{1,0:T(8,128)(2,1)} %get-tuple-element.24), channel_id=1, source_target_pairs={{0,8},{4,12},{8,0},{12,4},{16,24},{20,28},{24,16},{28,20},{1,9},{5... | collective-permute-start | bytes 1179656 | tf_op jit(solution)/shard_map/ppermute | solution.py:303
  10.5 1.5 %collective-permute-start.1 = (bf16[256,768]{1,0:T(8,128)(2,1)}, bf16[256,768]{1,0:T(8,128)(2,1)S(1)}, u32[]{:S(2)}, u32[]{:S(2)}) collective-permute-start(bf16[256,768]{1,0:T(8,128)(2,1)} %get-tuple-element.22), channel_id=1, source_target_pairs={{0,4},{4,0},{8,12},{12,8},{16,20},{20,16},{24,28},{28,24},{1,5},{5... | collective-permute-start | bytes 1179656 | tf_op jit(solution)/shard_map/ppermute | solution.py:303
  12.0 0.1 shard_map.131
  12.1 0.6 collective-permute-start
  12.7 7.1 %collective-permute-done.3 = bf16[256,768]{1,0:T(8,128)(2,1)S(1)} collective-permute-done((bf16[256,768]{1,0:T(8,128)(2,1)}, bf16[256,768]{1,0:T(8,128)(2,1)S(1)}, u32[]{:S(2)}, u32[]{:S(2)}) %collective-permute-start.3) | collective-permute-done | bytes 393248 | tf_op jit(solution)/shard_map/ppermute | solution.py:303
  19.8 1.1 convert_add_fusion
  20.9 2.8 %collective-permute-start.4 = (bf16[128,768]{1,0:T(8,128)(2,1)S(1)}, bf16[128,768]{1,0:T(8,128)(2,1)S(1)}, u32[]{:S(2)}, u32[]{:S(2)}) collective-permute-start(bf16[128,768]{1,0:T(8,128)(2,1)S(1)} %get-tuple-element.37), channel_id=1, source_target_pairs={{0,16},{4,20},{8,24},{12,28},{16,0},{20,4},{24,8},{28,12},{1,17},{... | collective-permute-start | bytes 589832 | tf_op jit(solution)/shard_map/ppermute | solution.py:303
  23.8 0.1 convert_add_fusion.1
  23.9 1.6 %collective-permute-start.2 = (bf16[128,768]{1,0:T(8,128)(2,1)S(1)}, bf16[128,768]{1,0:T(8,128)(2,1)S(1)}, u32[]{:S(2)}, u32[]{:S(2)}) collective-permute-start(bf16[128,768]{1,0:T(8,128)(2,1)S(1)} %get-tuple-element.39), channel_id=1, source_target_pairs={{0,8},{4,12},{8,0},{12,4},{16,24},{20,28},{24,16},{28,20},{1,9},{5... | collective-permute-start | bytes 589832 | tf_op jit(solution)/shard_map/ppermute | solution.py:303
  25.5 4.2 %collective-permute-done.other_ref = bf16[1536,128]{1,0:T(8,128)(2,1)S(1)} collective-permute-done((bf16[1536,128]{1,0:T(8,128)(2,1)S(1)}, bf16[1536,128]{1,0:T(8,128)(2,1)S(1)}, u32[]{:S(2)}, u32[]{:S(2)}) %collective-permute-start) | collective-permute-done | bytes 393248 | tf_op jit(solution)/shard_map/ppermute | solution.py:303
  29.8 2.5 %collective-permute-done.4 = bf16[128,768]{1,0:T(8,128)(2,1)S(1)} collective-permute-done((bf16[128,768]{1,0:T(8,128)(2,1)S(1)}, bf16[128,768]{1,0:T(8,128)(2,1)S(1)}, u32[]{:S(2)}, u32[]{:S(2)}) %collective-permute-start.4) | collective-permute-done | bytes 196640 | tf_op jit(solution)/shard_map/ppermute | solution.py:303
  32.3 0.4 collective-permute-done.2
  32.7 3.3 %collective-permute-start.12 = (bf16[1024,256]{1,0:T(8,128)(2,1)S(1)}, bf16[1024,256]{1,0:T(8,128)(2,1)S(1)}, u32[]{:S(2)}, u32[]{:S(2)}) collective-permute-start(bf16[1024,256]{1,0:T(8,128)(2,1)S(1)} %pad_maximum_fusion), channel_id=1, source_target_pairs={{0,4},{4,8},{8,12},{12,16},{16,20},{20,24},{24,28},{1,5},{5,9},{9,... | collective-permute-start | bytes 1572872 | tf_op jit(solution)/shard_map/ppermute | solution.py:292
  36.0 1.3 %collective-permute-start.13 = (bf16[1024,256]{1,0:T(8,128)(2,1)S(1)}, bf16[1024,256]{1,0:T(8,128)(2,1)S(1)}, u32[]{:S(2)}, u32[]{:S(2)}) collective-permute-start(bf16[1024,256]{1,0:T(8,128)(2,1)S(1)} %pad_maximum_fusion), channel_id=1, source_target_pairs={{4,0},{8,4},{12,8},{16,12},{20,16},{24,20},{28,24},{5,1},{9,5},{13... | collective-permute-start | bytes 1572872 | tf_op jit(solution)/shard_map/ppermute | solution.py:292
  37.3 2.7 %collective-permute-start.10 = (bf16[64,768]{1,0:T(8,128)(2,1)S(1)}, bf16[64,768]{1,0:T(8,128)(2,1)S(1)}, u32[]{:S(2)}, u32[]{:S(2)}) collective-permute-start(bf16[64,768]{1,0:T(8,128)(2,1)S(1)} %get-tuple-element.40), channel_id=1, source_target_pairs={{0,4},{4,0},{8,12},{12,8},{16,20},{20,16},{24,28},{28,24},{1,5},{5... | collective-permute-start | bytes 294920 | tf_op jit(solution)/shard_map/ppermute | solution.py:303
  40.1 1.6 %collective-permute-start.8 = (bf16[64,768]{1,0:T(8,128)(2,1)S(1)}, bf16[64,768]{1,0:T(8,128)(2,1)S(1)}, u32[]{:S(2)}, u32[]{:S(2)}) collective-permute-start(bf16[64,768]{1,0:T(8,128)(2,1)S(1)} %get-tuple-element.42), channel_id=1, source_target_pairs={{0,16},{4,20},{8,24},{12,28},{16,0},{20,4},{24,8},{28,12},{1,17},{... | collective-permute-start | bytes 294920 | tf_op jit(solution)/shard_map/ppermute | solution.py:303
  41.6 4.0 %collective-permute-start.5 = (bf16[1024,128]{1,0:T(8,128)(2,1)S(1)}, bf16[1024,128]{1,0:T(8,128)(2,1)S(1)}, u32[]{:S(2)}, u32[]{:S(2)}) collective-permute-start(bf16[1024,128]{1,0:T(8,128)(2,1)S(1)} %get-tuple-element.25.high_ref), channel_id=1, source_target_pairs={{0,8},{4,12},{8,16},{12,20},{16,24},{20,28},{1,9},{5,13},{9,17},{1... | collective-permute-start | bytes 786440 | tf_op jit(solution)/shard_map/ppermute | solution.py:292
  45.6 13.4 %collective-permute-done.10 = bf16[64,768]{1,0:T(8,128)(2,1)S(1)} collective-permute-done((bf16[64,768]{1,0:T(8,128)(2,1)S(1)}, bf16[64,768]{1,0:T(8,128)(2,1)S(1)}, u32[]{:S(2)}, u32[]{:S(2)}) %collective-permute-start.10) | collective-permute-done | bytes 98336 | tf_op jit(solution)/shard_map/ppermute | solution.py:303
  59.0 1.5 %collective-permute-start.6 = (bf16[1024,128]{1,0:T(8,128)(2,1)S(1)}, bf16[1024,128]{1,0:T(8,128)(2,1)S(1)}, u32[]{:S(2)}, u32[]{:S(2)}) collective-permute-start(bf16[1024,128]{1,0:T(8,128)(2,1)S(1)} %get-tuple-element.26.low_ref), channel_id=1, source_target_pairs={{8,0},{12,4},{16,8},{20,12},{24,16},{28,20},{9,1},{13,5},{17,9},{2... | collective-permute-start | bytes 786440 | tf_op jit(solution)/shard_map/ppermute | solution.py:292
  60.5 2.5 %collective-permute-start.11 = (bf16[64,768]{1,0:T(8,128)(2,1)S(1)}, bf16[64,768]{1,0:T(8,128)(2,1)S(1)}, u32[]{:S(2)}, u32[]{:S(2)}) collective-permute-start(bf16[64,768]{1,0:T(8,128)(2,1)S(1)} %add_convert_fusion.3), channel_id=1, source_target_pairs={{0,4},{4,0},{8,12},{12,8},{16,20},{20,16},{24,28},{28,24},{1,5},{5... | collective-permute-start | bytes 294920 | tf_op jit(solution)/shard_map/ppermute | solution.py:303
  63.1 2.6 %collective-permute-done.11 = bf16[64,768]{1,0:T(8,128)(2,1)S(1)} collective-permute-done((bf16[64,768]{1,0:T(8,128)(2,1)S(1)}, bf16[64,768]{1,0:T(8,128)(2,1)S(1)}, u32[]{:S(2)}, u32[]{:S(2)}) %collective-permute-start.11) | collective-permute-done | bytes 98336 | tf_op jit(solution)/shard_map/ppermute | solution.py:303
  65.7 5.3 %collective-permute-start.9 = (bf16[64,768]{1,0:T(8,128)(2,1)S(1)}, bf16[64,768]{1,0:T(8,128)(2,1)S(1)}, u32[]{:S(2)}, u32[]{:S(2)}) collective-permute-start(bf16[64,768]{1,0:T(8,128)(2,1)S(1)} %add_convert_fusion.4), channel_id=1, source_target_pairs={{0,16},{4,20},{8,24},{12,28},{16,0},{20,4},{24,8},{28,12},{1,17},{... | collective-permute-start | bytes 294920 | tf_op jit(solution)/shard_map/ppermute | solution.py:303
  71.0 5.5 %collective-permute-done.9 = bf16[64,768]{1,0:T(8,128)(2,1)S(1)} collective-permute-done((bf16[64,768]{1,0:T(8,128)(2,1)S(1)}, bf16[64,768]{1,0:T(8,128)(2,1)S(1)}, u32[]{:S(2)}, u32[]{:S(2)}) %collective-permute-start.9) | collective-permute-done | bytes 98336 | tf_op jit(solution)/shard_map/ppermute | solution.py:303
  76.5 0.8 copy-done.10
  77.3 0.8 copy-done.12
  78.1 0.1 collective-permute-start.15
  78.3 0.1 pad_maximum_fusion.5
  78.3 0.1 reshape.26.edge_ref
  78.4 2.4 %collective-permute-start.14 = (bf16[128,768]{1,0:T(8,128)(2,1)S(1)}, bf16[128,768]{1,0:T(8,128)(2,1)S(1)}, u32[]{:S(2)}, u32[]{:S(2)}) collective-permute-start(bf16[128,768]{1,0:T(8,128)(2,1)S(1)} %pad_maximum_fusion.3), channel_id=1, source_target_pairs={{0,8},{4,12},{8,0},{12,4},{16,24},{20,28},{24,16},{28,20},{1,9},{5... | collective-permute-start | bytes 589832 | tf_op jit(solution)/shard_map/ppermute | solution.py:303
  80.9 4.0 %shard_map.134 = (bf16[512,128]{1,0:T(8,128)(2,1)S(1)}, bf16[512,128]{1,0:T(8,128)(2,1)S(1)}) custom-call(f32[2,2]{1,0:T(2,128)S(1)} %reshape.26.edge_ref, s32[1,1]{1,0:T(1,128)} %bitcast.10.side_ref, bf16[512,256]{1,0:T(8,128)(2,1)S(1)} %copy-done.15, bf16[1536,128]{1,0:T(8,128)(2,1)S(1)} %collective-permute-done.other_ref, ...), custom_call_target="tpu_custom_call" | custom-call | flops 805306368 | bytes 2097152 | tf_op jit(solution)/shard_map/pallas_call | solution.py:41
  84.9 3.7 %collective-permute-done.15 = bf16[128,768]{1,0:T(8,128)(2,1)S(1)} collective-permute-done((bf16[128,768]{1,0:T(8,128)(2,1)S(1)}, bf16[128,768]{1,0:T(8,128)(2,1)S(1)}, u32[]{:S(2)}, u32[]{:S(2)}) %collective-permute-start.15) | collective-permute-done | bytes 196640 | tf_op jit(solution)/shard_map/ppermute | solution.py:303
  88.7 0.1 collective-permute-start.16
  88.7 0.1 collective-permute-start.17
  88.8 1.9 %collective-permute-start.7 = (bf16[512,128]{1,0:T(8,128)(2,1)S(1)}, bf16[512,128]{1,0:T(8,128)(2,1)S(1)}, u32[]{:S(2)}, u32[]{:S(2)}) collective-permute-start(bf16[512,128]{1,0:T(8,128)(2,1)S(1)} %get-tuple-element.28), channel_id=1, source_target_pairs={{0,4},{4,0},{8,12},{12,8},{16,20},{20,16},{24,28},{28,24},{1,5},{5... | collective-permute-start | bytes 393224 | tf_op jit(solution)/shard_map/ppermute | solution.py:303
  90.8 0.1 add_bitcast_fusion.1.place_ref
  90.9 11.6 %collective-permute-done.7.other_ref = bf16[512,128]{1,0:T(8,128)(2,1)S(1)} collective-permute-done((bf16[512,128]{1,0:T(8,128)(2,1)S(1)}, bf16[512,128]{1,0:T(8,128)(2,1)S(1)}, u32[]{:S(2)}, u32[]{:S(2)}) %collective-permute-start.7) | collective-permute-done | bytes 131104 | tf_op jit(solution)/shard_map/ppermute | solution.py:303
  102.5 0.5 shard_map.135.query_ref
  103.1 1.1 copy-done.3
  104.1 5.5 %shard_map.136 = (bf16[3,64,512]{2,1,0:T(8,128)(2,1)}, bf16[512,512]{1,0:T(8,128)(2,1)S(1)}) custom-call(s32[1,1]{1,0:T(1,128)} %bitcast.7.place_ref, bf16[3,512,512]{2,1,0:T(8,128)(2,1)S(1)} %bitcast.25, bf16[512,512]{1,0:T(8,128)(2,1)S(1)} %shard_map.135.query_ref, bf16[256,768]{1,0:T(8,128)(2,1)S(1)} %copy-done.3, ...), custom_call_target="tpu_custom_call" | custom-call | flops 1000 | bytes 1000 | tf_op jit(solution)/shard_map/pallas_call | solution.py:41
  109.6 1.8 %shard_map.138 = bf16[2,512,256]{2,1,0:T(8,128)(2,1)} custom-call(s32[1,2]{1,0:T(1,128)S(1)} %add_bitcast_fusion.1.place_ref, bf16[512,512]{1,0:T(8,128)(2,1)S(1)} %get-tuple-element.34.fast_ref, bf16[512,1024]{1,0:T(8,128)(2,1)S(1)} %copy-done.1), custom_call_target="tpu_custom_call" | custom-call | flops 1000 | bytes 1000 | tf_op jit(solution)/shard_map/pallas_call | solution.py:41
  111.5 0.1 add_bitcast_fusion.place_ref
  111.6 1.0 shard_map.137.keep_ref
  112.6 1.0 collective-permute-done.18.near_ref
  113.6 0.1 fusion
  113.7 1.6 %collective-permute-start.19 = (bf16[512,256]{1,0:T(8,128)(2,1)S(1)}, bf16[512,256]{1,0:T(8,128)(2,1)S(1)}, u32[]{:S(2)}, u32[]{:S(2)}) collective-permute-start(bf16[512,256]{1,0:T(8,128)(2,1)S(1)} %fusion), channel_id=1, source_target_pairs={{0,2},{1,3},{2,0},{3,1},{4,6},{5,7},{6,4},{7,5},{8,10},{9,11},{10,... | collective-permute-start | bytes 786440 | tf_op jit(solution)/shard_map/ppermute | solution.py:298
  115.3 6.8 %collective-permute-done.19.far_ref = bf16[512,256]{1,0:T(8,128)(2,1)S(1)} collective-permute-done((bf16[512,256]{1,0:T(8,128)(2,1)S(1)}, bf16[512,256]{1,0:T(8,128)(2,1)S(1)}, u32[]{:S(2)}, u32[]{:S(2)}) %collective-permute-start.19) | collective-permute-done | bytes 262176 | tf_op jit(solution)/shard_map/ppermute | solution.py:298
  122.2 4.9 %shard_map.139 = bf16[512,256]{1,0:T(8,128)(2,1)} custom-call(f32[2,2]{1,0:T(2,128)S(1)} %reshape.26.edge_ref, bf16[512,256]{1,0:T(8,128)(2,1)S(1)} %copy-done.14, bf16[2,512,256]{2,1,0:T(8,128)(2,1)S(1)} %shard_map.137.keep_ref, bf16[2,512,256]{2,1,0:T(8,128)(2,1)S(1)} %collective-permute-done.18.near_ref, ...), custom_call_target="tpu_custom_call" | custom-call | flops 805306368 | bytes 2097152 | tf_op jit(solution)/shard_map/pallas_call | solution.py:41
  (53 shorter events, 0.5 us)
Async XLA Ops:
  0.6 11.4 %copy-start.15 = (bf16[512,256]{1,0:T(8,128)(2,1)S(1)}, bf16[512,256]{1,0:T(8,128)(2,1)}, u32[]{:S(2)}) copy-start(bf16[512,256]{1,0:T(8,128)(2,1)} %queries_ref.4) | copy-start | bytes 786436
  0.6 11.4 %copy-start.4 = (bf16[512,256]{1,0:T(8,128)(2,1)S(1)}, bf16[512,256]{1,0:T(8,128)(2,1)}, u32[]{:S(2)}) copy-start(bf16[512,256]{1,0:T(8,128)(2,1)} %keys_ref.5) | copy-start | bytes 786436
  0.7 11.4 %copy-start.5 = (bf16[512,256]{1,0:T(8,128)(2,1)S(1)}, bf16[512,256]{1,0:T(8,128)(2,1)}, u32[]{:S(2)}) copy-start(bf16[512,256]{1,0:T(8,128)(2,1)} %values_ref.5) | copy-start | bytes 786436
  7.5 16.3 %copy-start.17 = (bf16[256,768]{1,0:T(8,128)(2,1)S(1)}, bf16[256,768]{1,0:T(8,128)(2,1)}, u32[]{:S(2)}) copy-start(bf16[256,768]{1,0:T(8,128)(2,1)} %get-tuple-element.21) | copy-start | bytes 1179652
  7.5 12.3 %collective-permute-start.3 = (bf16[256,768]{1,0:T(8,128)(2,1)}, bf16[256,768]{1,0:T(8,128)(2,1)S(1)}, u32[]{:S(2)}, u32[]{:S(2)}) collective-permute-start(bf16[256,768]{1,0:T(8,128)(2,1)} %get-tuple-element.24), channel_id=1, source_target_pairs={{0,8},{4,12},{8,0},{12,4},{16,24},{20,28},{24,16},{28,20},{1,9},{5... | collective-permute-start | bytes 1179656 | tf_op jit(solution)/shard_map/ppermute | solution.py:303
  10.5 13.3 %collective-permute-start.1 = (bf16[256,768]{1,0:T(8,128)(2,1)}, bf16[256,768]{1,0:T(8,128)(2,1)S(1)}, u32[]{:S(2)}, u32[]{:S(2)}) collective-permute-start(bf16[256,768]{1,0:T(8,128)(2,1)} %get-tuple-element.22), channel_id=1, source_target_pairs={{0,4},{4,0},{8,12},{12,8},{16,20},{20,16},{24,28},{28,24},{1,5},{5... | collective-permute-start | bytes 1179656 | tf_op jit(solution)/shard_map/ppermute | solution.py:303
  12.1 13.4 %copy-start.6 = (bf16[512,256]{1,0:T(8,128)(2,1)S(1)}, bf16[512,256]{1,0:T(8,128)(2,1)}, u32[]{:S(2)}) copy-start(bf16[512,256]{1,0:T(8,128)(2,1)} %values_ref.7) | copy-start | bytes 786436
  12.1 13.4 %copy-start.8 = (bf16[512,256]{1,0:T(8,128)(2,1)S(1)}, bf16[512,256]{1,0:T(8,128)(2,1)}, u32[]{:S(2)}) copy-start(bf16[512,256]{1,0:T(8,128)(2,1)} %keys_ref.7) | copy-start | bytes 786436
  12.1 17.6 %collective-permute-start = (bf16[1536,128]{1,0:T(8,128)(2,1)S(1)}, bf16[1536,128]{1,0:T(8,128)(2,1)S(1)}, u32[]{:S(2)}, u32[]{:S(2)}) collective-permute-start(bf16[1536,128]{1,0:T(8,128)(2,1)S(1)} %shard_map.131), channel_id=1, source_target_pairs={{0,4},{4,0},{8,12},{12,8},{16,20},{20,16},{24,28},{28,24},{1,5},{5... | collective-permute-start | bytes 1179656 | tf_op jit(solution)/shard_map/ppermute | solution.py:303
  20.9 11.4 %collective-permute-start.4 = (bf16[128,768]{1,0:T(8,128)(2,1)S(1)}, bf16[128,768]{1,0:T(8,128)(2,1)S(1)}, u32[]{:S(2)}, u32[]{:S(2)}) collective-permute-start(bf16[128,768]{1,0:T(8,128)(2,1)S(1)} %get-tuple-element.37), channel_id=1, source_target_pairs={{0,16},{4,20},{8,24},{12,28},{16,0},{20,4},{24,8},{28,12},{1,17},{... | collective-permute-start | bytes 589832 | tf_op jit(solution)/shard_map/ppermute | solution.py:303
  23.9 8.8 %collective-permute-start.2 = (bf16[128,768]{1,0:T(8,128)(2,1)S(1)}, bf16[128,768]{1,0:T(8,128)(2,1)S(1)}, u32[]{:S(2)}, u32[]{:S(2)}) collective-permute-start(bf16[128,768]{1,0:T(8,128)(2,1)S(1)} %get-tuple-element.39), channel_id=1, source_target_pairs={{0,8},{4,12},{8,0},{12,4},{16,24},{20,28},{24,16},{28,20},{1,9},{5... | collective-permute-start | bytes 589832 | tf_op jit(solution)/shard_map/ppermute | solution.py:303
  32.7 43.8 %collective-permute-start.12 = (bf16[1024,256]{1,0:T(8,128)(2,1)S(1)}, bf16[1024,256]{1,0:T(8,128)(2,1)S(1)}, u32[]{:S(2)}, u32[]{:S(2)}) collective-permute-start(bf16[1024,256]{1,0:T(8,128)(2,1)S(1)} %pad_maximum_fusion), channel_id=1, source_target_pairs={{0,4},{4,8},{8,12},{12,16},{16,20},{20,24},{24,28},{1,5},{5,9},{9,... | collective-permute-start | bytes 1572872 | tf_op jit(solution)/shard_map/ppermute | solution.py:292
  36.0 41.3 %collective-permute-start.13 = (bf16[1024,256]{1,0:T(8,128)(2,1)S(1)}, bf16[1024,256]{1,0:T(8,128)(2,1)S(1)}, u32[]{:S(2)}, u32[]{:S(2)}) collective-permute-start(bf16[1024,256]{1,0:T(8,128)(2,1)S(1)} %pad_maximum_fusion), channel_id=1, source_target_pairs={{4,0},{8,4},{12,8},{16,12},{20,16},{24,20},{28,24},{5,1},{9,5},{13... | collective-permute-start | bytes 1572872 | tf_op jit(solution)/shard_map/ppermute | solution.py:292
  37.3 21.7 %collective-permute-start.10 = (bf16[64,768]{1,0:T(8,128)(2,1)S(1)}, bf16[64,768]{1,0:T(8,128)(2,1)S(1)}, u32[]{:S(2)}, u32[]{:S(2)}) collective-permute-start(bf16[64,768]{1,0:T(8,128)(2,1)S(1)} %get-tuple-element.40), channel_id=1, source_target_pairs={{0,4},{4,0},{8,12},{12,8},{16,20},{20,16},{24,28},{28,24},{1,5},{5... | collective-permute-start | bytes 294920 | tf_op jit(solution)/shard_map/ppermute | solution.py:303
  40.1 20.5 %collective-permute-start.8 = (bf16[64,768]{1,0:T(8,128)(2,1)S(1)}, bf16[64,768]{1,0:T(8,128)(2,1)S(1)}, u32[]{:S(2)}, u32[]{:S(2)}) collective-permute-start(bf16[64,768]{1,0:T(8,128)(2,1)S(1)} %get-tuple-element.42), channel_id=1, source_target_pairs={{0,16},{4,20},{8,24},{12,28},{16,0},{20,4},{24,8},{28,12},{1,17},{... | collective-permute-start | bytes 294920 | tf_op jit(solution)/shard_map/ppermute | solution.py:303
  41.6 34.9 %collective-permute-start.5 = (bf16[1024,128]{1,0:T(8,128)(2,1)S(1)}, bf16[1024,128]{1,0:T(8,128)(2,1)S(1)}, u32[]{:S(2)}, u32[]{:S(2)}) collective-permute-start(bf16[1024,128]{1,0:T(8,128)(2,1)S(1)} %get-tuple-element.25.high_ref), channel_id=1, source_target_pairs={{0,8},{4,12},{8,16},{12,20},{16,24},{20,28},{1,9},{5,13},{9,17},{1... | collective-permute-start | bytes 786440 | tf_op jit(solution)/shard_map/ppermute | solution.py:292
  59.0 17.5 %collective-permute-start.6 = (bf16[1024,128]{1,0:T(8,128)(2,1)S(1)}, bf16[1024,128]{1,0:T(8,128)(2,1)S(1)}, u32[]{:S(2)}, u32[]{:S(2)}) collective-permute-start(bf16[1024,128]{1,0:T(8,128)(2,1)S(1)} %get-tuple-element.26.low_ref), channel_id=1, source_target_pairs={{8,0},{12,4},{16,8},{20,12},{24,16},{28,20},{9,1},{13,5},{17,9},{2... | collective-permute-start | bytes 786440 | tf_op jit(solution)/shard_map/ppermute | solution.py:292
  60.5 5.1 %collective-permute-start.11 = (bf16[64,768]{1,0:T(8,128)(2,1)S(1)}, bf16[64,768]{1,0:T(8,128)(2,1)S(1)}, u32[]{:S(2)}, u32[]{:S(2)}) collective-permute-start(bf16[64,768]{1,0:T(8,128)(2,1)S(1)} %add_convert_fusion.3), channel_id=1, source_target_pairs={{0,4},{4,0},{8,12},{12,8},{16,20},{20,16},{24,28},{28,24},{1,5},{5... | collective-permute-start | bytes 294920 | tf_op jit(solution)/shard_map/ppermute | solution.py:303
  65.7 10.8 %collective-permute-start.9 = (bf16[64,768]{1,0:T(8,128)(2,1)S(1)}, bf16[64,768]{1,0:T(8,128)(2,1)S(1)}, u32[]{:S(2)}, u32[]{:S(2)}) collective-permute-start(bf16[64,768]{1,0:T(8,128)(2,1)S(1)} %add_convert_fusion.4), channel_id=1, source_target_pairs={{0,16},{4,20},{8,24},{12,28},{16,0},{20,4},{24,8},{28,12},{1,17},{... | collective-permute-start | bytes 294920 | tf_op jit(solution)/shard_map/ppermute | solution.py:303
  76.5 0.8 copy-start.10
  77.3 0.8 copy-start.12
  78.1 10.4 %collective-permute-start.15 = (bf16[128,768]{1,0:T(8,128)(2,1)S(1)}, bf16[128,768]{1,0:T(8,128)(2,1)S(1)}, u32[]{:S(2)}, u32[]{:S(2)}) collective-permute-start(bf16[128,768]{1,0:T(8,128)(2,1)S(1)} %pad_maximum_fusion.4), channel_id=1, source_target_pairs={{0,16},{4,20},{8,24},{12,28},{16,0},{20,4},{24,8},{28,12},{1,17},{... | collective-permute-start | bytes 589832 | tf_op jit(solution)/shard_map/ppermute | solution.py:303
  78.4 24.1 %copy-start.16 = (bf16[1,256,512]{2,1,0:T(8,128)(2,1)S(1)}, bf16[1,256,512]{2,1,0:T(8,128)(2,1)}, u32[]{:S(2)}) copy-start(bf16[1,256,512]{2,1,0:T(8,128)(2,1)} %param.15) | copy-start | bytes 786436
  78.4 10.2 %collective-permute-start.14 = (bf16[128,768]{1,0:T(8,128)(2,1)S(1)}, bf16[128,768]{1,0:T(8,128)(2,1)S(1)}, u32[]{:S(2)}, u32[]{:S(2)}) collective-permute-start(bf16[128,768]{1,0:T(8,128)(2,1)S(1)} %pad_maximum_fusion.3), channel_id=1, source_target_pairs={{0,8},{4,12},{8,0},{12,4},{16,24},{20,28},{24,16},{28,20},{1,9},{5... | collective-permute-start | bytes 589832 | tf_op jit(solution)/shard_map/ppermute | solution.py:303
  84.8 18.2 %copy-start = (bf16[1,512,3,512]{3,1,2,0:T(8,128)(2,1)S(1)}, bf16[1,512,3,512]{3,1,2,0:T(8,128)(2,1)}, u32[]{:S(2)}) copy-start(bf16[1,512,3,512]{3,1,2,0:T(8,128)(2,1)} %param.19) | copy-start | bytes 4718596
  88.7 14.4 %copy-start.2 = (bf16[256,768]{1,0:T(8,128)(2,1)}, bf16[256,768]{1,0:T(8,128)(2,1)S(1)}, u32[]{:S(2)}) copy-start(bf16[256,768]{1,0:T(8,128)(2,1)S(1)} %pad_maximum_fusion.1.refs_0_) | copy-start | bytes 1179652
  88.7 14.4 %collective-permute-start.16 = (bf16[256,768]{1,0:T(8,128)(2,1)S(1)}, bf16[256,768]{1,0:T(8,128)(2,1)}, u32[]{:S(2)}, u32[]{:S(2)}) collective-permute-start(bf16[256,768]{1,0:T(8,128)(2,1)S(1)} %pad_maximum_fusion.1.refs_0_), channel_id=1, source_target_pairs={{0,4},{4,0},{8,12},{12,8},{16,20},{20,16},{24,28},{28,24},{1,5},{5... | collective-permute-start | bytes 1179656 | tf_op jit(solution)/shard_map/ppermute | solution.py:303
  88.7 14.3 %collective-permute-start.17 = (bf16[256,768]{1,0:T(8,128)(2,1)S(1)}, bf16[256,768]{1,0:T(8,128)(2,1)}, u32[]{:S(2)}, u32[]{:S(2)}) collective-permute-start(bf16[256,768]{1,0:T(8,128)(2,1)S(1)} %pad_maximum_fusion.2.refs_2_), channel_id=1, source_target_pairs={{0,8},{4,12},{8,0},{12,4},{16,24},{20,28},{24,16},{28,20},{1,9},{5... | collective-permute-start | bytes 1179656 | tf_op jit(solution)/shard_map/ppermute | solution.py:303
  88.8 13.7 %collective-permute-start.7 = (bf16[512,128]{1,0:T(8,128)(2,1)S(1)}, bf16[512,128]{1,0:T(8,128)(2,1)S(1)}, u32[]{:S(2)}, u32[]{:S(2)}) collective-permute-start(bf16[512,128]{1,0:T(8,128)(2,1)S(1)} %get-tuple-element.28), channel_id=1, source_target_pairs={{0,4},{4,0},{8,12},{12,8},{16,20},{20,16},{24,28},{28,24},{1,5},{5... | collective-permute-start | bytes 393224 | tf_op jit(solution)/shard_map/ppermute | solution.py:303
  103.0 6.6 %copy-start.1 = (bf16[512,1024]{1,0:T(8,128)(2,1)S(1)}, bf16[512,1024]{1,0:T(8,128)(2,1)}, u32[]{:S(2)}) copy-start(bf16[512,1024]{1,0:T(8,128)(2,1)} %map_ref.3) | copy-start | bytes 3145732
  103.1 1.1 copy-start.3
  111.4 10.7 %copy-start.7 = (bf16[512,256]{1,0:T(8,128)(2,1)S(1)}, bf16[512,256]{1,0:T(8,128)(2,1)}, u32[]{:S(2)}) copy-start(bf16[512,256]{1,0:T(8,128)(2,1)} %values_ref.7) | copy-start | bytes 786436
  111.4 10.7 %copy-start.9 = (bf16[512,256]{1,0:T(8,128)(2,1)S(1)}, bf16[512,256]{1,0:T(8,128)(2,1)}, u32[]{:S(2)}) copy-start(bf16[512,256]{1,0:T(8,128)(2,1)} %keys_ref.7) | copy-start | bytes 786436
  111.4 10.7 %copy-start.11 = (bf16[1024,256]{1,0:T(8,128)(2,1)S(1)}, bf16[1024,256]{1,0:T(8,128)(2,1)}, u32[]{:S(2)}) copy-start(bf16[1024,256]{1,0:T(8,128)(2,1)} %copy-done.10) | copy-start | bytes 1572868
  111.4 10.7 %copy-start.14 = (bf16[512,256]{1,0:T(8,128)(2,1)S(1)}, bf16[512,256]{1,0:T(8,128)(2,1)}, u32[]{:S(2)}) copy-start(bf16[512,256]{1,0:T(8,128)(2,1)} %queries_ref.5) | copy-start | bytes 786436
  111.4 2.2 %collective-permute-start.18 = (bf16[2,512,256]{2,1,0:T(8,128)(2,1)}, bf16[2,512,256]{2,1,0:T(8,128)(2,1)S(1)}, u32[]{:S(2)}, u32[]{:S(2)}) collective-permute-start(bf16[2,512,256]{2,1,0:T(8,128)(2,1)} %shard_map.138), channel_id=1, source_target_pairs={{0,1},{1,0},{2,3},{3,2},{4,5},{5,4},{6,7},{7,6},{8,9},{9,8},{10,11... | collective-permute-start | bytes 1572872 | tf_op jit(solution)/shard_map/ppermute | solution.py:298
  111.5 10.6 %copy-start.13 = (bf16[1024,256]{1,0:T(8,128)(2,1)S(1)}, bf16[1024,256]{1,0:T(8,128)(2,1)}, u32[]{:S(2)}) copy-start(bf16[1024,256]{1,0:T(8,128)(2,1)} %copy-done.12) | copy-start | bytes 1572868
  113.7 8.4 %collective-permute-start.19 = (bf16[512,256]{1,0:T(8,128)(2,1)S(1)}, bf16[512,256]{1,0:T(8,128)(2,1)S(1)}, u32[]{:S(2)}, u32[]{:S(2)}) collective-permute-start(bf16[512,256]{1,0:T(8,128)(2,1)S(1)} %fusion), channel_id=1, source_target_pairs={{0,2},{1,3},{2,0},{3,1},{4,6},{5,7},{6,4},{7,5},{8,10},{9,11},{10,... | collective-permute-start | bytes 786440 | tf_op jit(solution)/shard_map/ppermute | solution.py:298

commit v11 on v9

--- a/solution.py
+++ b/solution.py
@@ -198,15 +198,20 @@
 
 
 def second_kernel(edge_ref, queries_ref, keep_ref, near_ref, far_ref, prev_ref, keys_ref, values_ref, next_ref,
-                  out_ref):
+                  *refs):
+    done_refs, out_ref = refs[:-1], refs[-1]
     count = keys_ref.shape[0]
-    for index in range(count // TILE):
-        low, high = index * TILE, (index + 1) * TILE
+    half = far_ref.shape[0]
+    offset = half if done_refs else 0
+    if done_refs:
+        out_ref[:half, :] = done_refs[0][...]
+    for low in range(offset, offset + half, TILE):
+        high = low + TILE
         rows = slice(low, high)
         mixed = (
-            keep_ref[1, rows, :].astype(F32)
-            + near_ref[1, rows, :].astype(F32)
-            + far_ref[rows, :].astype(F32)
+            keep_ref[rows, :].astype(F32)
+            + near_ref[rows, :].astype(F32)
+            + far_ref[low - offset:high - offset, :].astype(F32)
         )
         query = (queries_ref[rows, :].astype(F32) + mixed).astype(BF16)
         heads = []
@@ -224,8 +229,8 @@
         out_ref[rows, :] = (both * lax.rsqrt(mean + 1e-05)).astype(BF16)
 
 
-def renew_kernel(orders, place_ref, weights_ref, query_ref, *refs):
-    pieces, (own_ref, fast_ref, new_ref) = refs[:-3], refs[-3:]
+def renew_kernel(orders, place_ref, places_ref, weights_ref, query_ref, map_ref, *refs):
+    pieces, (own_ref, fast_ref, send_ref, keep_ref, new_ref) = refs[:-5], refs[-5:]
     place = place_ref[0, 0]
     hidden_size, width = weights_ref.shape[1:]
     limit_norm = math.sqrt(FAST_HIDDEN * FAST_DIM) / 2.0
@@ -277,14 +282,18 @@
         raw = dot_nn(hidden, new_ref[2])
         mean = jnp.mean(raw * raw, axis=1, keepdims=True)
         fast_ref[rows, :] = (raw * lax.rsqrt(mean + 1e-05)).astype(BF16)
-
-
-def mix_kernel(place_ref, fast_ref, map_ref, out_ref):
-    width = out_ref.shape[2]
-    for slot in range(2):
-        start = pl.multiple_of(place_ref[0, slot] * width, width)
-        columns = map_ref[:, pl.ds(start, width)]
-        out_ref[slot] = dot_nn(fast_ref[...], columns).astype(BF16)
+    mix([places_ref[0, 0], places_ref[0, 1]], fast_ref[...], map_ref, [send_ref, keep_ref])
+
+
+def mix(places, fast, map_ref, out_refs):
+    for place, out_ref in zip(places, out_refs):
+        width = out_ref.shape[1]
+        columns = map_ref[:, pl.ds(pl.multiple_of(place * width, width), width)]
+        out_ref[...] = dot_nn(fast, columns).astype(BF16)
+
+
+def mix_kernel(places_ref, fast_ref, map_ref, *out_refs):
+    mix([places_ref[0, 2], places_ref[0, 3]], fast_ref[...], map_ref, out_refs)
 
 
 def seq_shift(value, step):
@@ -445,42 +454,43 @@
     )
 
     own_rows = hidden_size >> len(orders[0])
-    own_new, fast_out = call(
+    my_bit, near = head_place % 2, head_place // 2
+    places = jnp.stack(
+        [2 * pair + bit for pair in (near ^ 1, near) for bit in (1 - my_bit, my_bit)]
+    ).astype(jnp.int32).reshape(1, 4)
+    share = shape((rows, width), BF16)
+    own_new, fast_out, far_send, far_keep = call(
         functools.partial(renew_kernel, orders),
-        [shape((3, own_rows, fast_width), BF16), shape((rows, fast_width), BF16)],
-        (place, weights, fast_query, *gathered),
-        scalars=1,
+        [shape((3, own_rows, fast_width), BF16), shape((rows, fast_width), BF16), share, share],
+        (place, places, weights, fast_query, output_map, *gathered),
+        scalars=2,
         scratch=[pltpu.VMEM(weights.shape, BF16)],
     )
+    far_near = head_swap(far_send, 1)
+    near_send, near_keep = call(
+        mix_kernel, [share, share], (places, fast_out, output_map), scalars=1
+    )
+    near_near = head_swap(near_send, 1)
+    half = rows // 2
+    far_parts = []
+    for part in (slice(0, half), slice(half, rows)):
+        far_sum = far_keep[part].astype(F32) + far_near[part].astype(F32)
+        far_parts.append(head_swap(far_sum.astype(BF16), 2))
     if not halving:
         share_rows = hidden_size // seq_count
         own_new = lax.dynamic_slice_in_dim(own_new, seq_place * share_rows, share_rows, 1)
 
-    def mixed_for(low_bit):
-        far = (head_place // 2) ^ 1
-        near = head_place // 2
-        places = jnp.stack([far * 2 + low_bit, near * 2 + low_bit]).reshape(1, 2)
+    def second_attention(part, *done):
         return call(
-            mix_kernel,
-            shape((2, rows, width), BF16),
-            (places, fast_out, output_map),
+            second_kernel,
+            shape((half * (1 + len(done)), width), BF16),
+            (edges, queries_second, near_keep, near_near, far_parts[part],
+             prev_second, keys_second, values_second, next_second, *done),
             scalars=1,
+            cost=(6 * rows * rows * width, 16 * rows * width),
         )
 
-    my_bit = head_place % 2
-    near_part = head_swap(mixed_for(1 - my_bit), 1)
-    keep_part = mixed_for(my_bit)
-    to_send = (keep_part[0].astype(F32) + near_part[0].astype(F32)).astype(BF16)
-    far_part = head_swap(to_send, 2)
-
-    normed_second = call(
-        second_kernel,
-        shape((rows, width), BF16),
-        (edges, queries_second, keep_part, near_part, far_part,
-         prev_second, keys_second, values_second, next_second),
-        scalars=1,
-        cost=(12 * rows * rows * width, 16 * rows * width),
-    )
+    normed_second = second_attention(1, second_attention(0))
     return (normed_second, jnp.transpose(own_new, (1, 0, 2))[None])
 
 

time: 112 us -> 112 us (level)
  waiting for transfers between devices: 44.8 us -> 33.4 us
  starting transfers between devices: 38 us -> 44.8 us
  other arithmetic: 0.68 us -> 4.8 us
    ppermute x14, waiting for transfers between devices: 32.7 us -> 22.4 us  [seq_swap(): lax.ppermute(value, 'seq', [(i, i ^ step) for i in range(lax.axis_size('s...]
    ppermute x14, starting transfers between devices: 26.3 us -> 32.8 us  [seq_swap(): lax.ppermute(value, 'seq', [(i, i ^ step) for i in range(lax.axis_size('s...]
    ppermute x4, waiting for transfers between devices: 12.1 us -> 6.71 us  [seq_shift(): lax.ppermute(value, 'seq', [(i, i + step) for i in range(peers) if 0 <= i...]
    ppermute x2 -> x4, waiting for transfers between devices: 0.01 us -> 4.32 us  [head_swap(): lax.ppermute(value, 'head', [(i, i ^ bit) for i in range(lax.axis_size('h...]
    concatenate x4, other arithmetic: 0.08 us -> 4.29 us  [doubling_step(): jnp.concatenate(parts)]
    ppermute x2 -> x4, starting transfers between devices: 1.62 us -> 2.57 us  [head_swap(): lax.ppermute(value, 'head', [(i, i ^ bit) for i in range(lax.axis_size('h...]
    unnamed x37 -> x35, local copies, waits for them, and re-layouts: 1.98 us -> 2.75 us
  transfers between devices with their start and end apart: 20 -> 22, of which waited for: 8 -> 9; matrix products, arithmetic and copies ran while one was open for 1% -> 3% of each run, Pallas kernels for 5% -> 9%
where the time goes in v11:
time: 112 us
  starting transfers between devices  44.8 us (40%)
  waiting for transfers between devices  33.4 us (30%)
  Pallas kernels  25.2 us (22%)
  other arithmetic  4.8 us (4%)
  local copies, waits for them, and re-layouts  2.85 us (3%)
    ppermute x14, starting transfers between devices, seq_swap(): lax.ppermute(value, 'seq', [(i, i ^ step) for i in range(lax.axis_size('s...  32.8 us
    ppermute x14, waiting for transfers between devices, seq_swap(): lax.ppermute(value, 'seq', [(i, i ^ step) for i in range(lax.axis_size('s...  22.4 us
    pallas_call x8, Pallas kernels, call(): pl.pallas_call(body, out_shape=out_shapes, in_specs=in_specs, out_specs=j...  18.4 us
    ppermute x4, starting transfers between devices, seq_shift(): lax.ppermute(value, 'seq', [(i, i + step) for i in range(peers) if 0 <= i...  9.47 us
    pallas_call x1, Pallas kernels, local(): pl.pallas_call(functools.partial(gradient_kernel, orders), grid=(hidden_s...  6.88 us
    ppermute x4, waiting for transfers between devices, seq_shift(): lax.ppermute(value, 'seq', [(i, i + step) for i in range(peers) if 0 <= i...  6.71 us
    ppermute x4, waiting for transfers between devices, head_swap(): lax.ppermute(value, 'head', [(i, i ^ bit) for i in range(lax.axis_size('h...  4.32 us
    concatenate x4, other arithmetic, doubling_step(): jnp.concatenate(parts)  4.29 us
  transfers between devices with their start and end apart: 22, of which 9 were waited for; matrix products, arithmetic and copies ran while one was open for 3% of the time, Pallas kernels for 9%

profile of v11, /device:TPU:0, one launch (start us, length us, event | category | flops | bytes accessed | tf_op | source)
XLA Modules:
  0.0 112.1 jit_solution(4406461177825910416)
XLA Ops:
  0.7 6.9 %shard_map.133 = (bf16[256,768]{1,0:T(8,128)(2,1)}, bf16[256,768]{1,0:T(8,128)(2,1)}, bf16[256,768]{1,0:T(8,128)(2,1)}, bf16[256,768]{1,0:T(8,128)(2,1)}) custom-call(s32[1,1]{1,0:T(1,128)} %bitcast.9.place_ref, f32[1,512]{1,0:T(1,128)} %bitcast.23, bf16[512,512]{1,0:T(8,128)(2,1)} %keys_ref.7, bf16[512,512]{1,0:T(8,128)(2,1)} %values_ref.7, ...), custom_call_target="tpu_custom_call" | custom-call | flops 1000 | bytes 1000 | tf_op jit(solution)/shard_map/pallas_call | solution.py:386
  7.6 3.0 %collective-permute-start.1 = (bf16[256,768]{1,0:T(8,128)(2,1)}, bf16[256,768]{1,0:T(8,128)(2,1)S(1)}, u32[]{:S(2)}, u32[]{:S(2)}) collective-permute-start(bf16[256,768]{1,0:T(8,128)(2,1)} %get-tuple-element.27), channel_id=1, source_target_pairs={{0,4},{4,0},{8,12},{12,8},{16,20},{20,16},{24,28},{28,24},{1,5},{5... | collective-permute-start | bytes 1179656 | tf_op jit(solution)/shard_map/ppermute | solution.py:312
  10.6 0.1 collective-permute-start
  10.7 2.0 %collective-permute-start.3 = (bf16[256,768]{1,0:T(8,128)(2,1)}, bf16[256,768]{1,0:T(8,128)(2,1)S(1)}, u32[]{:S(2)}, u32[]{:S(2)}) collective-permute-start(bf16[256,768]{1,0:T(8,128)(2,1)} %get-tuple-element.29), channel_id=1, source_target_pairs={{0,8},{4,12},{8,0},{12,4},{16,24},{20,28},{24,16},{28,20},{1,9},{5... | collective-permute-start | bytes 1179656 | tf_op jit(solution)/shard_map/ppermute | solution.py:312
  12.9 7.8 %collective-permute-done.1 = bf16[256,768]{1,0:T(8,128)(2,1)S(1)} collective-permute-done((bf16[256,768]{1,0:T(8,128)(2,1)}, bf16[256,768]{1,0:T(8,128)(2,1)S(1)}, u32[]{:S(2)}, u32[]{:S(2)}) %collective-permute-start.1) | collective-permute-done | bytes 393248 | tf_op jit(solution)/shard_map/ppermute | solution.py:312
  20.7 0.1 convert_add_fusion.1
  20.8 2.2 %collective-permute-start.2 = (bf16[128,768]{1,0:T(8,128)(2,1)S(1)}, bf16[128,768]{1,0:T(8,128)(2,1)S(1)}, u32[]{:S(2)}, u32[]{:S(2)}) collective-permute-start(bf16[128,768]{1,0:T(8,128)(2,1)S(1)} %get-tuple-element.49), channel_id=1, source_target_pairs={{0,8},{4,12},{8,0},{12,4},{16,24},{20,28},{24,16},{28,20},{1,9},{5... | collective-permute-start | bytes 589832 | tf_op jit(solution)/shard_map/ppermute | solution.py:312
  23.0 0.1 convert_add_fusion
  23.1 2.6 %collective-permute-start.4 = (bf16[128,768]{1,0:T(8,128)(2,1)S(1)}, bf16[128,768]{1,0:T(8,128)(2,1)S(1)}, u32[]{:S(2)}, u32[]{:S(2)}) collective-permute-start(bf16[128,768]{1,0:T(8,128)(2,1)S(1)} %get-tuple-element.47), channel_id=1, source_target_pairs={{0,16},{4,20},{8,24},{12,28},{16,0},{20,4},{24,8},{28,12},{1,17},{... | collective-permute-start | bytes 589832 | tf_op jit(solution)/shard_map/ppermute | solution.py:312
  25.7 2.6 %collective-permute-done.other_ref = bf16[1536,128]{1,0:T(8,128)(2,1)S(1)} collective-permute-done((bf16[1536,128]{1,0:T(8,128)(2,1)S(1)}, bf16[1536,128]{1,0:T(8,128)(2,1)S(1)}, u32[]{:S(2)}, u32[]{:S(2)}) %collective-permute-start) | collective-permute-done | bytes 393248 | tf_op jit(solution)/shard_map/ppermute | solution.py:312
  28.4 0.8 collective-permute-done.2
  29.2 2.1 %collective-permute-start.8 = (bf16[64,768]{1,0:T(8,128)(2,1)S(1)}, bf16[64,768]{1,0:T(8,128)(2,1)S(1)}, u32[]{:S(2)}, u32[]{:S(2)}) collective-permute-start(bf16[64,768]{1,0:T(8,128)(2,1)S(1)} %get-tuple-element.52), channel_id=1, source_target_pairs={{0,16},{4,20},{8,24},{12,28},{16,0},{20,4},{24,8},{28,12},{1,17},{... | collective-permute-start | bytes 294920 | tf_op jit(solution)/shard_map/ppermute | solution.py:312
  31.3 2.4 %collective-permute-done.4 = bf16[128,768]{1,0:T(8,128)(2,1)S(1)} collective-permute-done((bf16[128,768]{1,0:T(8,128)(2,1)S(1)}, bf16[128,768]{1,0:T(8,128)(2,1)S(1)}, u32[]{:S(2)}, u32[]{:S(2)}) %collective-permute-start.4) | collective-permute-done | bytes 196640 | tf_op jit(solution)/shard_map/ppermute | solution.py:312
  33.8 1.6 %collective-permute-start.10 = (bf16[64,768]{1,0:T(8,128)(2,1)S(1)}, bf16[64,768]{1,0:T(8,128)(2,1)S(1)}, u32[]{:S(2)}, u32[]{:S(2)}) collective-permute-start(bf16[64,768]{1,0:T(8,128)(2,1)S(1)} %get-tuple-element.50), channel_id=1, source_target_pairs={{0,4},{4,0},{8,12},{12,8},{16,20},{20,16},{24,28},{28,24},{1,5},{5... | collective-permute-start | bytes 294920 | tf_op jit(solution)/shard_map/ppermute | solution.py:312
  35.4 4.1 %collective-permute-start.5 = (bf16[1024,128]{1,0:T(8,128)(2,1)S(1)}, bf16[1024,128]{1,0:T(8,128)(2,1)S(1)}, u32[]{:S(2)}, u32[]{:S(2)}) collective-permute-start(bf16[1024,128]{1,0:T(8,128)(2,1)S(1)} %get-tuple-element.30.high_ref), channel_id=1, source_target_pairs={{0,8},{4,12},{8,16},{12,20},{16,24},{20,28},{1,9},{5,13},{9,17},{1... | collective-permute-start | bytes 786440 | tf_op jit(solution)/shard_map/ppermute | solution.py:301
  39.5 1.3 %collective-permute-start.6 = (bf16[1024,128]{1,0:T(8,128)(2,1)S(1)}, bf16[1024,128]{1,0:T(8,128)(2,1)S(1)}, u32[]{:S(2)}, u32[]{:S(2)}) collective-permute-start(bf16[1024,128]{1,0:T(8,128)(2,1)S(1)} %get-tuple-element.31.low_ref), channel_id=1, source_target_pairs={{8,0},{12,4},{16,8},{20,12},{24,16},{28,20},{9,1},{13,5},{17,9},{2... | collective-permute-start | bytes 786440 | tf_op jit(solution)/shard_map/ppermute | solution.py:301
  40.8 2.4 %collective-permute-start.12 = (bf16[1024,256]{1,0:T(8,128)(2,1)S(1)}, bf16[1024,256]{1,0:T(8,128)(2,1)S(1)}, u32[]{:S(2)}, u32[]{:S(2)}) collective-permute-start(bf16[1024,256]{1,0:T(8,128)(2,1)S(1)} %constant_dynamic-update-slice_fusion), channel_id=1, source_target_pairs={{0,4},{4,8},{8,12},{12,16},{16,20},{20,24},{24,28},{1,5},{5,9},{9,... | collective-permute-start | bytes 1572872 | tf_op jit(solution)/shard_map/ppermute | solution.py:301
  43.3 4.0 %collective-permute-start.9 = (bf16[64,768]{1,0:T(8,128)(2,1)S(1)}, bf16[64,768]{1,0:T(8,128)(2,1)S(1)}, u32[]{:S(2)}, u32[]{:S(2)}) collective-permute-start(bf16[64,768]{1,0:T(8,128)(2,1)S(1)} %add_convert_fusion.5), channel_id=1, source_target_pairs={{0,16},{4,20},{8,24},{12,28},{16,0},{20,4},{24,8},{28,12},{1,17},{... | collective-permute-start | bytes 294920 | tf_op jit(solution)/shard_map/ppermute | solution.py:312
  47.4 3.1 %collective-permute-start.11 = (bf16[64,768]{1,0:T(8,128)(2,1)S(1)}, bf16[64,768]{1,0:T(8,128)(2,1)S(1)}, u32[]{:S(2)}, u32[]{:S(2)}) collective-permute-start(bf16[64,768]{1,0:T(8,128)(2,1)S(1)} %add_convert_fusion.4), channel_id=1, source_target_pairs={{0,4},{4,0},{8,12},{12,8},{16,20},{20,16},{24,28},{28,24},{1,5},{5... | collective-permute-start | bytes 294920 | tf_op jit(solution)/shard_map/ppermute | solution.py:312
  50.4 0.7 pad_maximum_fusion.2
  51.1 1.9 %collective-permute-done.11 = bf16[64,768]{1,0:T(8,128)(2,1)S(1)} collective-permute-done((bf16[64,768]{1,0:T(8,128)(2,1)S(1)}, bf16[64,768]{1,0:T(8,128)(2,1)S(1)}, u32[]{:S(2)}, u32[]{:S(2)}) %collective-permute-start.11) | collective-permute-done | bytes 98336 | tf_op jit(solution)/shard_map/ppermute | solution.py:312
  53.0 0.7 pad_maximum_fusion.3
  53.7 0.8 copy-done.4
  54.6 5.3 %collective-permute-start.13 = (bf16[128,768]{1,0:T(8,128)(2,1)}, bf16[128,768]{1,0:T(8,128)(2,1)}, u32[]{:S(2)}, u32[]{:S(2)}) collective-permute-start(bf16[128,768]{1,0:T(8,128)(2,1)} %pad_maximum_fusion.2), channel_id=1, source_target_pairs={{0,8},{4,12},{8,0},{12,4},{16,24},{20,28},{24,16},{28,20},{1,9},{5... | collective-permute-start | bytes 589832 | tf_op jit(solution)/shard_map/ppermute | solution.py:312
  59.9 0.1 pad_maximum_fusion.4
  60.0 0.1 reshape.19.edge_ref
  60.1 4.1 %collective-permute-start.14 = (bf16[128,768]{1,0:T(8,128)(2,1)}, bf16[128,768]{1,0:T(8,128)(2,1)S(1)}, u32[]{:S(2)}, u32[]{:S(2)}) collective-permute-start(bf16[128,768]{1,0:T(8,128)(2,1)} %pad_maximum_fusion.3), channel_id=1, source_target_pairs={{0,16},{4,20},{8,24},{12,28},{16,0},{20,4},{24,8},{28,12},{1,17},{... | collective-permute-start | bytes 589832 | tf_op jit(solution)/shard_map/ppermute | solution.py:312
  64.2 4.6 %shard_map.134 = (bf16[512,128]{1,0:T(8,128)(2,1)S(1)}, bf16[512,128]{1,0:T(8,128)(2,1)}) custom-call(f32[2,2]{1,0:T(2,128)S(1)} %reshape.19.edge_ref, s32[1,1]{1,0:T(1,128)} %bitcast.12.side_ref, bf16[512,256]{1,0:T(8,128)(2,1)S(1)} %copy-done.9, bf16[1536,128]{1,0:T(8,128)(2,1)S(1)} %collective-permute-done.other_ref, ...), custom_call_target="tpu_custom_call" | custom-call | flops 805306368 | bytes 2097152 | tf_op jit(solution)/shard_map/pallas_call | solution.py:41
  68.8 1.2 %pad_maximum_fusion.refs_0_ = bf16[256,768]{1,0:T(8,128)(2,1)S(1)} fusion(bf16[128,768]{1,0:T(8,128)(2,1)} %collective-permute-done.13, bf16[128,768]{1,0:T(8,128)(2,1)} %pad_maximum_fusion.2), kind=kLoop, calls=%fused_computation | loop fusion | flops 786432 | bytes 786432 | tf_op jit(solution)/shard_map/concatenate | solution.py:335
  70.0 0.2 collective-permute-done.14
  70.2 1.7 %pad_maximum_fusion.1.refs_2_ = bf16[256,768]{1,0:T(8,128)(2,1)} fusion(bf16[128,768]{1,0:T(8,128)(2,1)S(1)} %collective-permute-done.14, bf16[128,768]{1,0:T(8,128)(2,1)} %pad_maximum_fusion.3), kind=kLoop, calls=%fused_computation.1 | loop fusion | flops 786432 | bytes 786432 | tf_op jit(solution)/shard_map/concatenate | solution.py:335
  72.0 1.1 %collective-permute-start.15 = (bf16[256,768]{1,0:T(8,128)(2,1)S(1)}, bf16[256,768]{1,0:T(8,128)(2,1)}, u32[]{:S(2)}, u32[]{:S(2)}) collective-permute-start(bf16[256,768]{1,0:T(8,128)(2,1)S(1)} %pad_maximum_fusion.refs_0_), channel_id=1, source_target_pairs={{0,4},{4,0},{8,12},{12,8},{16,20},{20,16},{24,28},{28,24},{1,5},{5... | collective-permute-start | bytes 1179656 | tf_op jit(solution)/shard_map/ppermute | solution.py:312
  73.1 1.4 %collective-permute-start.16 = (bf16[256,768]{1,0:T(8,128)(2,1)}, bf16[256,768]{1,0:T(8,128)(2,1)}, u32[]{:S(2)}, u32[]{:S(2)}) collective-permute-start(bf16[256,768]{1,0:T(8,128)(2,1)} %pad_maximum_fusion.1.refs_2_), channel_id=1, source_target_pairs={{0,8},{4,12},{8,0},{12,4},{16,24},{20,28},{24,16},{28,20},{1,9},{5... | collective-permute-start | bytes 1179656 | tf_op jit(solution)/shard_map/ppermute | solution.py:312
  74.5 0.1 add_bitcast_fusion.places_ref
  74.6 6.6 %collective-permute-done.7.other_ref = bf16[512,128]{1,0:T(8,128)(2,1)} collective-permute-done((bf16[512,128]{1,0:T(8,128)(2,1)}, bf16[512,128]{1,0:T(8,128)(2,1)}, u32[]{:S(2)}, u32[]{:S(2)}) %collective-permute-start.7) | collective-permute-done | bytes 131104 | tf_op jit(solution)/shard_map/ppermute | solution.py:312
  81.2 0.9 copy-done.10
  82.2 0.9 copy-done.12
  83.1 1.4 %shard_map.135.query_ref = bf16[512,512]{1,0:T(8,128)(2,1)S(1)} custom-call(s32[1,1]{1,0:T(1,128)} %bitcast.12.side_ref, bf16[512,128]{1,0:T(8,128)(2,1)S(1)} %copy-done.12, bf16[512,128]{1,0:T(8,128)(2,1)} %collective-permute-done.7.other_ref, bf16[256,512]{1,0:T(8,128)(2,1)S(1)} %bitcast.22), custom_call_target="tpu_custom_call" | custom-call | flops 1000 | bytes 1000 | tf_op jit(solution)/shard_map/pallas_call | solution.py:41
  84.6 5.6 %shard_map.136 = (bf16[3,64,512]{2,1,0:T(8,128)(2,1)}, bf16[512,512]{1,0:T(8,128)(2,1)S(1)}, bf16[512,256]{1,0:T(8,128)(2,1)S(1)}, bf16[512,256]{1,0:T(8,128)(2,1)S(1)}) custom-call(s32[1,1]{1,0:T(1,128)} %bitcast.9.place_ref, s32[1,4]{1,0:T(1,128)S(1)} %add_bitcast_fusion.places_ref, bf16[3,512,512]{2,1,0:T(8,128)(2,1)S(1)} %bitcast.21, ...), custom_call_target="tpu_custom_call" | custom-call | flops 1000 | bytes 1000 | tf_op jit(solution)/shard_map/pallas_call | solution.py:41
  90.3 1.6 %collective-permute-start.20 = (bf16[1024,256]{1,0:T(8,128)(2,1)S(1)}, bf16[1024,256]{1,0:T(8,128)(2,1)S(1)}, u32[]{:S(2)}, u32[]{:S(2)}) collective-permute-start(bf16[1024,256]{1,0:T(8,128)(2,1)S(1)} %copy-done.16), channel_id=1, source_target_pairs={{4,0},{8,4},{12,8},{16,12},{20,16},{24,20},{28,24},{5,1},{9,5},{13... | collective-permute-start | bytes 1572872 | tf_op jit(solution)/shard_map/ppermute | solution.py:301
  91.9 1.0 shard_map.137
  92.9 0.4 collective-permute-start.17
  93.4 1.5 %collective-permute-start.21 = (bf16[256,256]{1,0:T(8,128)(2,1)S(1)}, bf16[256,256]{1,0:T(8,128)(2,1)S(1)}, u32[]{:S(2)}, u32[]{:S(2)}) collective-permute-start(bf16[256,256]{1,0:T(8,128)(2,1)S(1)} %get-tuple-element.54), channel_id=1, source_target_pairs={{0,2},{1,3},{2,0},{3,1},{4,6},{5,7},{6,4},{7,5},{8,10},{9,11},{10,... | collective-permute-start | bytes 393224 | tf_op jit(solution)/shard_map/ppermute | solution.py:307
  94.9 0.6 collective-permute-start.19
  95.5 4.3 %collective-permute-done.21.far_ref = bf16[256,256]{1,0:T(8,128)(2,1)S(1)} collective-permute-done((bf16[256,256]{1,0:T(8,128)(2,1)S(1)}, bf16[256,256]{1,0:T(8,128)(2,1)S(1)}, u32[]{:S(2)}, u32[]{:S(2)}) %collective-permute-start.21) | collective-permute-done | bytes 131104 | tf_op jit(solution)/shard_map/ppermute | solution.py:307
  99.8 6.7 %collective-permute-done.20.next_ref = bf16[1024,256]{1,0:T(8,128)(2,1)S(1)} collective-permute-done((bf16[1024,256]{1,0:T(8,128)(2,1)S(1)}, bf16[1024,256]{1,0:T(8,128)(2,1)S(1)}, u32[]{:S(2)}, u32[]{:S(2)}) %collective-permute-start.20) | collective-permute-done | bytes 524320 | tf_op jit(solution)/shard_map/ppermute | solution.py:301
  106.5 2.4 %shard_map.138.refs_0_ = bf16[256,256]{1,0:T(8,128)(2,1)S(1)} custom-call(f32[2,2]{1,0:T(2,128)S(1)} %reshape.19.edge_ref, bf16[512,256]{1,0:T(8,128)(2,1)S(1)} %copy-done.8, bf16[512,256]{1,0:T(8,128)(2,1)S(1)} %get-tuple-element.40.keep_ref, bf16[512,256]{1,0:T(8,128)(2,1)S(1)} %collective-permute-done.17.near_ref, ...), custom_call_target="tpu_custom_call" | custom-call | flops 402653184 | bytes 2097152 | tf_op jit(solution)/shard_map/pallas_call | solution.py:41
  108.9 3.2 %shard_map.139 = bf16[512,256]{1,0:T(8,128)(2,1)} custom-call(f32[2,2]{1,0:T(2,128)S(1)} %reshape.19.edge_ref, bf16[512,256]{1,0:T(8,128)(2,1)S(1)} %copy-done.8, bf16[512,256]{1,0:T(8,128)(2,1)S(1)} %get-tuple-element.40.keep_ref, bf16[512,256]{1,0:T(8,128)(2,1)S(1)} %collective-permute-done.17.near_ref, ...), custom_call_target="tpu_custom_call" | custom-call | flops 402653184 | bytes 2097152 | tf_op jit(solution)/shard_map/pallas_call | solution.py:41
  (55 shorter events, 0.5 us)
Async XLA Ops:
  0.6 9.9 %copy-start.7 = (bf16[512,256]{1,0:T(8,128)(2,1)S(1)}, bf16[512,256]{1,0:T(8,128)(2,1)}, u32[]{:S(2)}) copy-start(bf16[512,256]{1,0:T(8,128)(2,1)} %values_ref.6) | copy-start | bytes 786436
  0.6 9.9 %copy-start.6 = (bf16[512,256]{1,0:T(8,128)(2,1)S(1)}, bf16[512,256]{1,0:T(8,128)(2,1)}, u32[]{:S(2)}) copy-start(bf16[512,256]{1,0:T(8,128)(2,1)} %keys_ref.6) | copy-start | bytes 786436
  0.7 9.9 %copy-start.9 = (bf16[512,256]{1,0:T(8,128)(2,1)S(1)}, bf16[512,256]{1,0:T(8,128)(2,1)}, u32[]{:S(2)}) copy-start(bf16[512,256]{1,0:T(8,128)(2,1)} %queries_ref.5) | copy-start | bytes 786436
  0.7 12.1 %copy-start.2 = (bf16[512,256]{1,0:T(8,128)(2,1)S(1)}, bf16[512,256]{1,0:T(8,128)(2,1)}, u32[]{:S(2)}) copy-start(bf16[512,256]{1,0:T(8,128)(2,1)} %keys_ref.9) | copy-start | bytes 786436
  0.7 12.1 %copy-start.3 = (bf16[512,256]{1,0:T(8,128)(2,1)S(1)}, bf16[512,256]{1,0:T(8,128)(2,1)}, u32[]{:S(2)}) copy-start(bf16[512,256]{1,0:T(8,128)(2,1)} %values_ref.9) | copy-start | bytes 786436
  7.6 13.1 %copy-start.14 = (bf16[256,768]{1,0:T(8,128)(2,1)S(1)}, bf16[256,768]{1,0:T(8,128)(2,1)}, u32[]{:S(2)}) copy-start(bf16[256,768]{1,0:T(8,128)(2,1)} %get-tuple-element.26) | copy-start | bytes 1179652
  7.6 13.1 %collective-permute-start.1 = (bf16[256,768]{1,0:T(8,128)(2,1)}, bf16[256,768]{1,0:T(8,128)(2,1)S(1)}, u32[]{:S(2)}, u32[]{:S(2)}) collective-permute-start(bf16[256,768]{1,0:T(8,128)(2,1)} %get-tuple-element.27), channel_id=1, source_target_pairs={{0,4},{4,0},{8,12},{12,8},{16,20},{20,16},{24,28},{28,24},{1,5},{5... | collective-permute-start | bytes 1179656 | tf_op jit(solution)/shard_map/ppermute | solution.py:312
  10.5 12.4 %copy-start.13 = (bf16[256,768]{1,0:T(8,128)(2,1)S(1)}, bf16[256,768]{1,0:T(8,128)(2,1)}, u32[]{:S(2)}) copy-start(bf16[256,768]{1,0:T(8,128)(2,1)} %get-tuple-element.28) | copy-start | bytes 1179652
  10.6 17.7 %collective-permute-start = (bf16[1536,128]{1,0:T(8,128)(2,1)S(1)}, bf16[1536,128]{1,0:T(8,128)(2,1)S(1)}, u32[]{:S(2)}, u32[]{:S(2)}) collective-permute-start(bf16[1536,128]{1,0:T(8,128)(2,1)S(1)} %shard_map.131), channel_id=1, source_target_pairs={{0,4},{4,0},{8,12},{12,8},{16,20},{20,16},{24,28},{28,24},{1,5},{5... | collective-permute-start | bytes 1179656 | tf_op jit(solution)/shard_map/ppermute | solution.py:312
  10.7 12.2 %collective-permute-start.3 = (bf16[256,768]{1,0:T(8,128)(2,1)}, bf16[256,768]{1,0:T(8,128)(2,1)S(1)}, u32[]{:S(2)}, u32[]{:S(2)}) collective-permute-start(bf16[256,768]{1,0:T(8,128)(2,1)} %get-tuple-element.29), channel_id=1, source_target_pairs={{0,8},{4,12},{8,0},{12,4},{16,24},{20,28},{24,16},{28,20},{1,9},{5... | collective-permute-start | bytes 1179656 | tf_op jit(solution)/shard_map/ppermute | solution.py:312
  12.8 28.0 %copy-start.15 = (bf16[1024,256]{1,0:T(8,128)(2,1)}, bf16[1024,256]{1,0:T(8,128)(2,1)S(1)}, u32[]{:S(2)}) copy-start(bf16[1024,256]{1,0:T(8,128)(2,1)S(1)} %constant_dynamic-update-slice_fusion) | copy-start | bytes 1572868
  20.8 8.3 %collective-permute-start.2 = (bf16[128,768]{1,0:T(8,128)(2,1)S(1)}, bf16[128,768]{1,0:T(8,128)(2,1)S(1)}, u32[]{:S(2)}, u32[]{:S(2)}) collective-permute-start(bf16[128,768]{1,0:T(8,128)(2,1)S(1)} %get-tuple-element.49), channel_id=1, source_target_pairs={{0,8},{4,12},{8,0},{12,4},{16,24},{20,28},{24,16},{28,20},{1,9},{5... | collective-permute-start | bytes 589832 | tf_op jit(solution)/shard_map/ppermute | solution.py:312
  23.1 10.7 %collective-permute-start.4 = (bf16[128,768]{1,0:T(8,128)(2,1)S(1)}, bf16[128,768]{1,0:T(8,128)(2,1)S(1)}, u32[]{:S(2)}, u32[]{:S(2)}) collective-permute-start(bf16[128,768]{1,0:T(8,128)(2,1)S(1)} %get-tuple-element.47), channel_id=1, source_target_pairs={{0,16},{4,20},{8,24},{12,28},{16,0},{20,4},{24,8},{28,12},{1,17},{... | collective-permute-start | bytes 589832 | tf_op jit(solution)/shard_map/ppermute | solution.py:312
  29.2 14.1 %collective-permute-start.8 = (bf16[64,768]{1,0:T(8,128)(2,1)S(1)}, bf16[64,768]{1,0:T(8,128)(2,1)S(1)}, u32[]{:S(2)}, u32[]{:S(2)}) collective-permute-start(bf16[64,768]{1,0:T(8,128)(2,1)S(1)} %get-tuple-element.52), channel_id=1, source_target_pairs={{0,16},{4,20},{8,24},{12,28},{16,0},{20,4},{24,8},{28,12},{1,17},{... | collective-permute-start | bytes 294920 | tf_op jit(solution)/shard_map/ppermute | solution.py:312
  33.8 13.6 %collective-permute-start.10 = (bf16[64,768]{1,0:T(8,128)(2,1)S(1)}, bf16[64,768]{1,0:T(8,128)(2,1)S(1)}, u32[]{:S(2)}, u32[]{:S(2)}) collective-permute-start(bf16[64,768]{1,0:T(8,128)(2,1)S(1)} %get-tuple-element.50), channel_id=1, source_target_pairs={{0,4},{4,0},{8,12},{12,8},{16,20},{20,16},{24,28},{28,24},{1,5},{5... | collective-permute-start | bytes 294920 | tf_op jit(solution)/shard_map/ppermute | solution.py:312
  35.4 18.4 %collective-permute-start.5 = (bf16[1024,128]{1,0:T(8,128)(2,1)S(1)}, bf16[1024,128]{1,0:T(8,128)(2,1)S(1)}, u32[]{:S(2)}, u32[]{:S(2)}) collective-permute-start(bf16[1024,128]{1,0:T(8,128)(2,1)S(1)} %get-tuple-element.30.high_ref), channel_id=1, source_target_pairs={{0,8},{4,12},{8,16},{12,20},{16,24},{20,28},{1,9},{5,13},{9,17},{1... | collective-permute-start | bytes 786440 | tf_op jit(solution)/shard_map/ppermute | solution.py:301
  39.5 14.2 %collective-permute-start.6 = (bf16[1024,128]{1,0:T(8,128)(2,1)S(1)}, bf16[1024,128]{1,0:T(8,128)(2,1)S(1)}, u32[]{:S(2)}, u32[]{:S(2)}) collective-permute-start(bf16[1024,128]{1,0:T(8,128)(2,1)S(1)} %get-tuple-element.31.low_ref), channel_id=1, source_target_pairs={{8,0},{12,4},{16,8},{20,12},{24,16},{28,20},{9,1},{13,5},{17,9},{2... | collective-permute-start | bytes 786440 | tf_op jit(solution)/shard_map/ppermute | solution.py:301
  40.8 12.9 %collective-permute-start.12 = (bf16[1024,256]{1,0:T(8,128)(2,1)S(1)}, bf16[1024,256]{1,0:T(8,128)(2,1)S(1)}, u32[]{:S(2)}, u32[]{:S(2)}) collective-permute-start(bf16[1024,256]{1,0:T(8,128)(2,1)S(1)} %constant_dynamic-update-slice_fusion), channel_id=1, source_target_pairs={{0,4},{4,8},{8,12},{12,16},{16,20},{20,24},{24,28},{1,5},{5,9},{9,... | collective-permute-start | bytes 1572872 | tf_op jit(solution)/shard_map/ppermute | solution.py:301
  43.3 7.1 %collective-permute-start.9 = (bf16[64,768]{1,0:T(8,128)(2,1)S(1)}, bf16[64,768]{1,0:T(8,128)(2,1)S(1)}, u32[]{:S(2)}, u32[]{:S(2)}) collective-permute-start(bf16[64,768]{1,0:T(8,128)(2,1)S(1)} %add_convert_fusion.5), channel_id=1, source_target_pairs={{0,16},{4,20},{8,24},{12,28},{16,0},{20,4},{24,8},{28,12},{1,17},{... | collective-permute-start | bytes 294920 | tf_op jit(solution)/shard_map/ppermute | solution.py:312
  47.4 5.7 %collective-permute-start.11 = (bf16[64,768]{1,0:T(8,128)(2,1)S(1)}, bf16[64,768]{1,0:T(8,128)(2,1)S(1)}, u32[]{:S(2)}, u32[]{:S(2)}) collective-permute-start(bf16[64,768]{1,0:T(8,128)(2,1)S(1)} %add_convert_fusion.4), channel_id=1, source_target_pairs={{0,4},{4,0},{8,12},{12,8},{16,20},{20,16},{24,28},{28,24},{1,5},{5... | collective-permute-start | bytes 294920 | tf_op jit(solution)/shard_map/ppermute | solution.py:312
  53.7 0.8 copy-start.4
  54.6 14.3 %collective-permute-start.13 = (bf16[128,768]{1,0:T(8,128)(2,1)}, bf16[128,768]{1,0:T(8,128)(2,1)}, u32[]{:S(2)}, u32[]{:S(2)}) collective-permute-start(bf16[128,768]{1,0:T(8,128)(2,1)} %pad_maximum_fusion.2), channel_id=1, source_target_pairs={{0,8},{4,12},{8,0},{12,4},{16,24},{20,28},{24,16},{28,20},{1,9},{5... | collective-permute-start | bytes 589832 | tf_op jit(solution)/shard_map/ppermute | solution.py:312
  60.1 10.2 %collective-permute-start.14 = (bf16[128,768]{1,0:T(8,128)(2,1)}, bf16[128,768]{1,0:T(8,128)(2,1)S(1)}, u32[]{:S(2)}, u32[]{:S(2)}) collective-permute-start(bf16[128,768]{1,0:T(8,128)(2,1)} %pad_maximum_fusion.3), channel_id=1, source_target_pairs={{0,16},{4,20},{8,24},{12,28},{16,0},{20,4},{24,8},{28,12},{1,17},{... | collective-permute-start | bytes 589832 | tf_op jit(solution)/shard_map/ppermute | solution.py:312
  68.8 3.1 %copy-start.11 = (bf16[512,128]{1,0:T(8,128)(2,1)}, bf16[512,128]{1,0:T(8,128)(2,1)S(1)}, u32[]{:S(2)}) copy-start(bf16[512,128]{1,0:T(8,128)(2,1)S(1)} %get-tuple-element.32.keep_ref) | copy-start | bytes 393220
  68.8 15.7 %copy-start = (bf16[1,512,3,512]{3,1,2,0:T(8,128)(2,1)S(1)}, bf16[1,512,3,512]{3,1,2,0:T(8,128)(2,1)}, u32[]{:S(2)}) copy-start(bf16[1,512,3,512]{3,1,2,0:T(8,128)(2,1)} %param.19) | copy-start | bytes 4718596
  68.8 15.7 %copy-start.1 = (bf16[512,1024]{1,0:T(8,128)(2,1)S(1)}, bf16[512,1024]{1,0:T(8,128)(2,1)}, u32[]{:S(2)}) copy-start(bf16[512,1024]{1,0:T(8,128)(2,1)} %map_ref.3) | copy-start | bytes 3145732
  72.0 12.6 %collective-permute-start.15 = (bf16[256,768]{1,0:T(8,128)(2,1)S(1)}, bf16[256,768]{1,0:T(8,128)(2,1)}, u32[]{:S(2)}, u32[]{:S(2)}) collective-permute-start(bf16[256,768]{1,0:T(8,128)(2,1)S(1)} %pad_maximum_fusion.refs_0_), channel_id=1, source_target_pairs={{0,4},{4,0},{8,12},{12,8},{16,20},{20,16},{24,28},{28,24},{1,5},{5... | collective-permute-start | bytes 1179656 | tf_op jit(solution)/shard_map/ppermute | solution.py:312
  73.1 11.4 %collective-permute-start.16 = (bf16[256,768]{1,0:T(8,128)(2,1)}, bf16[256,768]{1,0:T(8,128)(2,1)}, u32[]{:S(2)}, u32[]{:S(2)}) collective-permute-start(bf16[256,768]{1,0:T(8,128)(2,1)} %pad_maximum_fusion.1.refs_2_), channel_id=1, source_target_pairs={{0,8},{4,12},{8,0},{12,4},{16,24},{20,28},{24,16},{28,20},{1,9},{5... | collective-permute-start | bytes 1179656 | tf_op jit(solution)/shard_map/ppermute | solution.py:312
  74.5 6.7 %collective-permute-start.7 = (bf16[512,128]{1,0:T(8,128)(2,1)}, bf16[512,128]{1,0:T(8,128)(2,1)}, u32[]{:S(2)}, u32[]{:S(2)}) collective-permute-start(bf16[512,128]{1,0:T(8,128)(2,1)} %get-tuple-element.33), channel_id=1, source_target_pairs={{0,4},{4,0},{8,12},{12,8},{16,20},{20,16},{24,28},{28,24},{1,5},{5... | collective-permute-start | bytes 393224 | tf_op jit(solution)/shard_map/ppermute | solution.py:312
  81.2 1.0 copy-start.10
  82.2 0.9 copy-start.12
  84.5 5.8 %copy-start.16 = (bf16[1024,256]{1,0:T(8,128)(2,1)S(1)}, bf16[1024,256]{1,0:T(8,128)(2,1)}, u32[]{:S(2)}) copy-start(bf16[1024,256]{1,0:T(8,128)(2,1)} %copy-done.15) | copy-start | bytes 1572868
  90.2 16.3 %copy-start.5 = (bf16[1024,256]{1,0:T(8,128)(2,1)S(1)}, bf16[1024,256]{1,0:T(8,128)(2,1)}, u32[]{:S(2)}) copy-start(bf16[1024,256]{1,0:T(8,128)(2,1)} %copy-done.4) | copy-start | bytes 1572868
  90.2 16.3 %copy-start.8 = (bf16[512,256]{1,0:T(8,128)(2,1)S(1)}, bf16[512,256]{1,0:T(8,128)(2,1)}, u32[]{:S(2)}) copy-start(bf16[512,256]{1,0:T(8,128)(2,1)} %queries_ref.7) | copy-start | bytes 786436
  90.2 3.1 %collective-permute-start.18 = (bf16[512,256]{1,0:T(8,128)(2,1)S(1)}, bf16[512,256]{1,0:T(8,128)(2,1)S(1)}, u32[]{:S(2)}, u32[]{:S(2)}) collective-permute-start(bf16[512,256]{1,0:T(8,128)(2,1)S(1)} %get-tuple-element.43), channel_id=1, source_target_pairs={{0,1},{1,0},{2,3},{3,2},{4,5},{5,4},{6,7},{7,6},{8,9},{9,8},{10,11... | collective-permute-start | bytes 786440 | tf_op jit(solution)/shard_map/ppermute | solution.py:307
  90.3 16.2 %collective-permute-start.20 = (bf16[1024,256]{1,0:T(8,128)(2,1)S(1)}, bf16[1024,256]{1,0:T(8,128)(2,1)S(1)}, u32[]{:S(2)}, u32[]{:S(2)}) collective-permute-start(bf16[1024,256]{1,0:T(8,128)(2,1)S(1)} %copy-done.16), channel_id=1, source_target_pairs={{4,0},{8,4},{12,8},{16,12},{20,16},{24,20},{28,24},{5,1},{9,5},{13... | collective-permute-start | bytes 1572872 | tf_op jit(solution)/shard_map/ppermute | solution.py:301
  92.9 2.6 %collective-permute-start.17 = (bf16[512,256]{1,0:T(8,128)(2,1)S(1)}, bf16[512,256]{1,0:T(8,128)(2,1)S(1)}, u32[]{:S(2)}, u32[]{:S(2)}) collective-permute-start(bf16[512,256]{1,0:T(8,128)(2,1)S(1)} %get-tuple-element.41), channel_id=1, source_target_pairs={{0,1},{1,0},{2,3},{3,2},{4,5},{5,4},{6,7},{7,6},{8,9},{9,8},{10,11... | collective-permute-start | bytes 786440 | tf_op jit(solution)/shard_map/ppermute | solution.py:307
  93.4 6.4 %collective-permute-start.21 = (bf16[256,256]{1,0:T(8,128)(2,1)S(1)}, bf16[256,256]{1,0:T(8,128)(2,1)S(1)}, u32[]{:S(2)}, u32[]{:S(2)}) collective-permute-start(bf16[256,256]{1,0:T(8,128)(2,1)S(1)} %get-tuple-element.54), channel_id=1, source_target_pairs={{0,2},{1,3},{2,0},{3,1},{4,6},{5,7},{6,4},{7,5},{8,10},{9,11},{10,... | collective-permute-start | bytes 393224 | tf_op jit(solution)/shard_map/ppermute | solution.py:307
  94.9 14.0 %collective-permute-start.19 = (bf16[256,256]{1,0:T(8,128)(2,1)S(1)}, bf16[256,256]{1,0:T(8,128)(2,1)S(1)}, u32[]{:S(2)}, u32[]{:S(2)}) collective-permute-start(bf16[256,256]{1,0:T(8,128)(2,1)S(1)} %get-tuple-element.55), channel_id=1, source_target_pairs={{0,2},{1,3},{2,0},{3,1},{4,6},{5,7},{6,4},{7,5},{8,10},{9,11},{10,... | collective-permute-start | bytes 393224 | tf_op jit(solution)/shard_map/ppermute | solution.py:307

commit v12 on v11

--- a/solution.py
+++ b/solution.py
@@ -14,7 +14,7 @@
 FAST_DIM = 512
 FAST_HIDDEN = 512
 TILE = 128
-VMEM_LIMIT = 24 * 1024 * 1024
+VMEM_LIMIT = 16 * 1024 * 1024
 VMEM_MOST = 60 * 1024 * 1024
 
 BF16 = jnp.bfloat16
@@ -468,7 +468,7 @@
     )
     far_near = head_swap(far_send, 1)
     near_send, near_keep = call(
-        mix_kernel, [share, share], (places, fast_out, output_map), scalars=1
+        mix_kernel, [share, share], (places, after(fast_out, next_second), output_map), scalars=1
     )
     near_near = head_swap(near_send, 1)
     half = rows // 2

time: 112 us -> 118 us (1.054)
  the two profiles are of different devices: /device:TPU:0 before, /device:TPU:16 now
where the time goes in v12:
time: 118 us; the launch traced here: 117 us
  starting transfers between devices  40.5 us (34%)
  waiting for transfers between devices  36.7 us (31%)
  Pallas kernels  23.9 us (20%)
  local copies, waits for them, and re-layouts  11 us (9%)
  other arithmetic  3.9 us (3%)
    ppermute x14, waiting for transfers between devices, seq_swap(): lax.ppermute(value, 'seq', [(i, i ^ step) for i in range(lax.axis_size('s...  30.1 us
    ppermute x4, starting transfers between devices, seq_shift(): lax.ppermute(value, 'seq', [(i, i + step) for i in range(peers) if 0 <= i...  19.1 us
    ppermute x14, starting transfers between devices, seq_swap(): lax.ppermute(value, 'seq', [(i, i ^ step) for i in range(lax.axis_size('s...  18.7 us
    pallas_call x8, Pallas kernels, call(): pl.pallas_call(body, out_shape=out_shapes, in_specs=in_specs, out_specs=j...  17 us
    unnamed x47, local copies, waits for them, and re-layouts  10.2 us
    pallas_call x1, Pallas kernels, local(): pl.pallas_call(functools.partial(gradient_kernel, orders), grid=(hidden_s...  6.88 us
    ppermute x4, waiting for transfers between devices, head_swap(): lax.ppermute(value, 'head', [(i, i ^ bit) for i in range(lax.axis_size('h...  4.33 us
    concatenate x4, other arithmetic, doubling_step(): jnp.concatenate(parts)  3.38 us
  transfers between devices with their start and end apart: 22, of which 10 were waited for; matrix products, arithmetic and copies ran while one was open for 4% of the time, Pallas kernels for 11%

profile of v12, /device:TPU:16, one launch (start us, length us, event | category | flops | bytes accessed | tf_op | source)
XLA Modules:
  0.0 117.0 jit_solution(2506107239880544750)
XLA Ops:
  0.7 6.9 %shard_map.133 = (bf16[256,768]{1,0:T(8,128)(2,1)}, bf16[256,768]{1,0:T(8,128)(2,1)}, bf16[256,768]{1,0:T(8,128)(2,1)}, bf16[256,768]{1,0:T(8,128)(2,1)}) custom-call(s32[1,1]{1,0:T(1,128)} %bitcast.9.place_ref, f32[1,512]{1,0:T(1,128)} %bitcast.23, bf16[512,512]{1,0:T(8,128)(2,1)} %keys_ref.7, bf16[512,512]{1,0:T(8,128)(2,1)} %values_ref.7, ...), custom_call_target="tpu_custom_call" | custom-call | flops 1000 | bytes 1000 | tf_op jit(solution)/shard_map/pallas_call | solution.py:386
  7.6 1.5 %collective-permute-start.1 = (bf16[256,768]{1,0:T(8,128)(2,1)}, bf16[256,768]{1,0:T(8,128)(2,1)S(1)}, u32[]{:S(2)}, u32[]{:S(2)}) collective-permute-start(bf16[256,768]{1,0:T(8,128)(2,1)} %get-tuple-element.28), channel_id=1, source_target_pairs={{0,4},{4,0},{8,12},{12,8},{16,20},{20,16},{24,28},{28,24},{1,5},{5... | collective-permute-start | bytes 1179656 | tf_op jit(solution)/shard_map/ppermute | solution.py:312
  9.8 1.6 %collective-permute-start.3 = (bf16[256,768]{1,0:T(8,128)(2,1)}, bf16[256,768]{1,0:T(8,128)(2,1)S(1)}, u32[]{:S(2)}, u32[]{:S(2)}) collective-permute-start(bf16[256,768]{1,0:T(8,128)(2,1)} %get-tuple-element.30), channel_id=1, source_target_pairs={{0,8},{4,12},{8,0},{12,4},{16,24},{20,28},{24,16},{28,20},{1,9},{5... | collective-permute-start | bytes 1179656 | tf_op jit(solution)/shard_map/ppermute | solution.py:312
  11.3 0.7 constant_dynamic-update-slice_fusion.1
  12.1 0.7 constant_dynamic-update-slice_fusion
  12.8 7.0 %collective-permute-done.1 = bf16[256,768]{1,0:T(8,128)(2,1)S(1)} collective-permute-done((bf16[256,768]{1,0:T(8,128)(2,1)}, bf16[256,768]{1,0:T(8,128)(2,1)S(1)}, u32[]{:S(2)}, u32[]{:S(2)}) %collective-permute-start.1) | collective-permute-done | bytes 393248 | tf_op jit(solution)/shard_map/ppermute | solution.py:312
  19.9 1.6 %collective-permute-start.2 = (bf16[128,768]{1,0:T(8,128)(2,1)S(1)}, bf16[128,768]{1,0:T(8,128)(2,1)S(1)}, u32[]{:S(2)}, u32[]{:S(2)}) collective-permute-start(bf16[128,768]{1,0:T(8,128)(2,1)S(1)} %get-tuple-element.51), channel_id=1, source_target_pairs={{0,8},{4,12},{8,0},{12,4},{16,24},{20,28},{24,16},{28,20},{1,9},{5... | collective-permute-start | bytes 589832 | tf_op jit(solution)/shard_map/ppermute | solution.py:312
  22.0 5.0 %collective-permute-done.other_ref = bf16[1536,128]{1,0:T(8,128)(2,1)S(1)} collective-permute-done((bf16[1536,128]{1,0:T(8,128)(2,1)S(1)}, bf16[1536,128]{1,0:T(8,128)(2,1)S(1)}, u32[]{:S(2)}, u32[]{:S(2)}) %collective-permute-start) | collective-permute-done | bytes 393248 | tf_op jit(solution)/shard_map/ppermute | solution.py:312
  27.2 0.9 collective-permute-start.8
  28.1 1.0 collective-permute-done.4
  29.2 1.6 %collective-permute-start.10 = (bf16[64,768]{1,0:T(8,128)(2,1)S(1)}, bf16[64,768]{1,0:T(8,128)(2,1)S(1)}, u32[]{:S(2)}, u32[]{:S(2)}) collective-permute-start(bf16[64,768]{1,0:T(8,128)(2,1)S(1)} %get-tuple-element.52), channel_id=1, source_target_pairs={{0,4},{4,0},{8,12},{12,8},{16,20},{20,16},{24,28},{28,24},{1,5},{5... | collective-permute-start | bytes 294920 | tf_op jit(solution)/shard_map/ppermute | solution.py:312
  30.8 8.1 %collective-permute-start.5 = (bf16[1024,128]{1,0:T(8,128)(2,1)S(1)}, bf16[1024,128]{1,0:T(8,128)(2,1)S(1)}, u32[]{:S(2)}, u32[]{:S(2)}) collective-permute-start(bf16[1024,128]{1,0:T(8,128)(2,1)S(1)} %get-tuple-element.31.high_ref), channel_id=1, source_target_pairs={{0,8},{4,12},{8,16},{12,20},{16,24},{20,28},{1,9},{5,13},{9,17},{1... | collective-permute-start | bytes 786440 | tf_op jit(solution)/shard_map/ppermute | solution.py:301
  38.9 1.9 %collective-permute-start.6 = (bf16[1024,128]{1,0:T(8,128)(2,1)S(1)}, bf16[1024,128]{1,0:T(8,128)(2,1)S(1)}, u32[]{:S(2)}, u32[]{:S(2)}) collective-permute-start(bf16[1024,128]{1,0:T(8,128)(2,1)S(1)} %get-tuple-element.32.low_ref), channel_id=1, source_target_pairs={{8,0},{12,4},{16,8},{20,12},{24,16},{28,20},{9,1},{13,5},{17,9},{2... | collective-permute-start | bytes 786440 | tf_op jit(solution)/shard_map/ppermute | solution.py:301
  40.8 2.4 %collective-permute-start.12 = (bf16[1024,256]{1,0:T(8,128)(2,1)}, bf16[1024,256]{1,0:T(8,128)(2,1)S(1)}, u32[]{:S(2)}, u32[]{:S(2)}) collective-permute-start(bf16[1024,256]{1,0:T(8,128)(2,1)} %constant_dynamic-update-slice_fusion), channel_id=1, source_target_pairs={{0,4},{4,8},{8,12},{12,16},{16,20},{20,24},{24,28},{1,5},{5,9},{9,... | collective-permute-start | bytes 1572872 | tf_op jit(solution)/shard_map/ppermute | solution.py:301
  43.3 3.1 %collective-permute-start.11 = (bf16[64,768]{1,0:T(8,128)(2,1)S(1)}, bf16[64,768]{1,0:T(8,128)(2,1)S(1)}, u32[]{:S(2)}, u32[]{:S(2)}) collective-permute-start(bf16[64,768]{1,0:T(8,128)(2,1)S(1)} %add_convert_fusion.4), channel_id=1, source_target_pairs={{0,4},{4,0},{8,12},{12,8},{16,20},{20,16},{24,28},{28,24},{1,5},{5... | collective-permute-start | bytes 294920 | tf_op jit(solution)/shard_map/ppermute | solution.py:312
  46.4 2.4 %collective-permute-done.9 = bf16[64,768]{1,0:T(8,128)(2,1)S(1)} collective-permute-done((bf16[64,768]{1,0:T(8,128)(2,1)S(1)}, bf16[64,768]{1,0:T(8,128)(2,1)S(1)}, u32[]{:S(2)}, u32[]{:S(2)}) %collective-permute-start.9) | collective-permute-done | bytes 98336 | tf_op jit(solution)/shard_map/ppermute | solution.py:312
  48.9 0.7 pad_maximum_fusion.2
  49.6 2.5 %collective-permute-done.11 = bf16[64,768]{1,0:T(8,128)(2,1)S(1)} collective-permute-done((bf16[64,768]{1,0:T(8,128)(2,1)S(1)}, bf16[64,768]{1,0:T(8,128)(2,1)S(1)}, u32[]{:S(2)}, u32[]{:S(2)}) %collective-permute-start.11) | collective-permute-done | bytes 98336 | tf_op jit(solution)/shard_map/ppermute | solution.py:312
  52.1 0.7 pad_maximum_fusion.3
  52.8 2.2 %collective-permute-done.12.prev_ref = bf16[1024,256]{1,0:T(8,128)(2,1)S(1)} collective-permute-done((bf16[1024,256]{1,0:T(8,128)(2,1)}, bf16[1024,256]{1,0:T(8,128)(2,1)S(1)}, u32[]{:S(2)}, u32[]{:S(2)}) %collective-permute-start.12) | collective-permute-done | bytes 524320 | tf_op jit(solution)/shard_map/ppermute | solution.py:301
  55.0 0.8 copy-done.4
  55.8 4.4 %collective-permute-start.13 = (bf16[128,768]{1,0:T(8,128)(2,1)}, bf16[128,768]{1,0:T(8,128)(2,1)}, u32[]{:S(2)}, u32[]{:S(2)}) collective-permute-start(bf16[128,768]{1,0:T(8,128)(2,1)} %pad_maximum_fusion.2), channel_id=1, source_target_pairs={{0,8},{4,12},{8,0},{12,4},{16,24},{20,28},{24,16},{28,20},{1,9},{5... | collective-permute-start | bytes 589832 | tf_op jit(solution)/shard_map/ppermute | solution.py:312
  60.3 4.0 %shard_map.134 = (bf16[512,128]{1,0:T(8,128)(2,1)S(1)}, bf16[512,128]{1,0:T(8,128)(2,1)S(1)}) custom-call(f32[2,2]{1,0:T(2,128)S(1)} %reshape.19.edge_ref, s32[1,1]{1,0:T(1,128)} %bitcast.12.side_ref, bf16[512,256]{1,0:T(8,128)(2,1)S(1)} %copy-done.15, bf16[1536,128]{1,0:T(8,128)(2,1)S(1)} %collective-permute-done.other_ref, ...), custom_call_target="tpu_custom_call" | custom-call | flops 805306368 | bytes 2097152 | tf_op jit(solution)/shard_map/pallas_call | solution.py:41
  64.4 1.5 %collective-permute-done.13 = bf16[128,768]{1,0:T(8,128)(2,1)} collective-permute-done((bf16[128,768]{1,0:T(8,128)(2,1)}, bf16[128,768]{1,0:T(8,128)(2,1)}, u32[]{:S(2)}, u32[]{:S(2)}) %collective-permute-start.13) | collective-permute-done | bytes 196640 | tf_op jit(solution)/shard_map/ppermute | solution.py:312
  65.9 1.0 pad_maximum_fusion.refs_0_
  66.9 1.9 %collective-permute-done.14 = bf16[128,768]{1,0:T(8,128)(2,1)S(1)} collective-permute-done((bf16[128,768]{1,0:T(8,128)(2,1)}, bf16[128,768]{1,0:T(8,128)(2,1)S(1)}, u32[]{:S(2)}, u32[]{:S(2)}) %collective-permute-start.14) | collective-permute-done | bytes 196640 | tf_op jit(solution)/shard_map/ppermute | solution.py:312
  68.9 1.0 pad_maximum_fusion.1.refs_2_
  69.8 1.1 collective-permute-start.15
  70.9 1.1 collective-permute-start.16
  72.0 0.8 copy-done.6
  72.8 0.7 collective-permute-start.7
  73.5 8.6 %collective-permute-done.7.other_ref = bf16[512,128]{1,0:T(8,128)(2,1)S(1)} collective-permute-done((bf16[512,128]{1,0:T(8,128)(2,1)S(1)}, bf16[512,128]{1,0:T(8,128)(2,1)S(1)}, u32[]{:S(2)}, u32[]{:S(2)}) %collective-permute-start.7) | collective-permute-done | bytes 131104 | tf_op jit(solution)/shard_map/ppermute | solution.py:312
  82.1 0.7 copy-done.19
  82.8 0.7 copy-done.11
  83.5 0.7 copy-done.13
  84.3 6.7 %collective-permute-start.17 = (bf16[1024,256]{1,0:T(8,128)(2,1)}, bf16[1024,256]{1,0:T(8,128)(2,1)}, u32[]{:S(2)}, u32[]{:S(2)}) collective-permute-start(bf16[1024,256]{1,0:T(8,128)(2,1)} %constant_dynamic-update-slice_fusion), channel_id=1, source_target_pairs={{4,0},{8,4},{12,8},{16,12},{20,16},{24,20},{28,24},{5,1},{9,5},{13... | collective-permute-start | bytes 1572872 | tf_op jit(solution)/shard_map/ppermute | solution.py:301
  91.1 0.9 copy-done.16
  92.0 0.9 copy-done.18
  92.9 0.9 copy-done.20
  94.4 1.0 copy-done.7
  95.4 1.0 copy-done.12
  96.4 1.0 copy-done.14
  97.3 4.9 %shard_map.136 = (bf16[3,64,512]{2,1,0:T(8,128)(2,1)}, bf16[512,512]{1,0:T(8,128)(2,1)S(1)}, bf16[512,256]{1,0:T(8,128)(2,1)S(1)}, bf16[512,256]{1,0:T(8,128)(2,1)S(1)}) custom-call(s32[1,1]{1,0:T(1,128)} %bitcast.9.place_ref, s32[1,4]{1,0:T(1,128)S(1)} %add_bitcast_fusion.places_ref, bf16[3,512,512]{2,1,0:T(8,128)(2,1)S(1)} %bitcast.21, ...), custom_call_target="tpu_custom_call" | custom-call | flops 1000 | bytes 1000 | tf_op jit(solution)/shard_map/pallas_call | solution.py:41
  102.3 1.0 shard_map.137
  104.0 1.5 %collective-permute-start.21 = (bf16[256,256]{1,0:T(8,128)(2,1)S(1)}, bf16[256,256]{1,0:T(8,128)(2,1)S(1)}, u32[]{:S(2)}, u32[]{:S(2)}) collective-permute-start(bf16[256,256]{1,0:T(8,128)(2,1)S(1)} %get-tuple-element.56), channel_id=1, source_target_pairs={{0,2},{1,3},{2,0},{3,1},{4,6},{5,7},{6,4},{7,5},{8,10},{9,11},{10,... | collective-permute-start | bytes 393224 | tf_op jit(solution)/shard_map/ppermute | solution.py:307
  106.1 4.3 %collective-permute-done.21.far_ref = bf16[256,256]{1,0:T(8,128)(2,1)S(1)} collective-permute-done((bf16[256,256]{1,0:T(8,128)(2,1)S(1)}, bf16[256,256]{1,0:T(8,128)(2,1)S(1)}, u32[]{:S(2)}, u32[]{:S(2)}) %collective-permute-start.21) | collective-permute-done | bytes 131104 | tf_op jit(solution)/shard_map/ppermute | solution.py:307
  110.4 2.9 %shard_map.138.refs_0_ = bf16[256,256]{1,0:T(8,128)(2,1)S(1)} custom-call(f32[2,2]{1,0:T(2,128)S(1)} %reshape.19.edge_ref, bf16[512,256]{1,0:T(8,128)(2,1)S(1)} %copy-done.10, bf16[512,256]{1,0:T(8,128)(2,1)S(1)} %get-tuple-element.43.keep_ref, bf16[512,256]{1,0:T(8,128)(2,1)S(1)} %collective-permute-done.18.near_ref, ...), custom_call_target="tpu_custom_call" | custom-call | flops 402653184 | bytes 2097152 | tf_op jit(solution)/shard_map/pallas_call | solution.py:41
  113.3 3.7 %shard_map.139 = bf16[512,256]{1,0:T(8,128)(2,1)} custom-call(f32[2,2]{1,0:T(2,128)S(1)} %reshape.19.edge_ref, bf16[512,256]{1,0:T(8,128)(2,1)S(1)} %copy-done.10, bf16[512,256]{1,0:T(8,128)(2,1)S(1)} %get-tuple-element.43.keep_ref, bf16[512,256]{1,0:T(8,128)(2,1)S(1)} %collective-permute-done.18.near_ref, ...), custom_call_target="tpu_custom_call" | custom-call | flops 402653184 | bytes 2097152 | tf_op jit(solution)/shard_map/pallas_call | solution.py:41
  (67 shorter events, 3.6 us)
Async XLA Ops:
  0.6 8.5 %copy-start.9 = (bf16[512,256]{1,0:T(8,128)(2,1)S(1)}, bf16[512,256]{1,0:T(8,128)(2,1)}, u32[]{:S(2)}) copy-start(bf16[512,256]{1,0:T(8,128)(2,1)} %values_ref.6) | copy-start | bytes 786436
  0.6 8.5 %copy-start.8 = (bf16[512,256]{1,0:T(8,128)(2,1)S(1)}, bf16[512,256]{1,0:T(8,128)(2,1)}, u32[]{:S(2)}) copy-start(bf16[512,256]{1,0:T(8,128)(2,1)} %keys_ref.6) | copy-start | bytes 786436
  0.7 8.4 %copy-start.15 = (bf16[512,256]{1,0:T(8,128)(2,1)S(1)}, bf16[512,256]{1,0:T(8,128)(2,1)}, u32[]{:S(2)}) copy-start(bf16[512,256]{1,0:T(8,128)(2,1)} %queries_ref.5) | copy-start | bytes 786436
  0.7 10.7 %copy-start.2 = (bf16[512,256]{1,0:T(8,128)(2,1)S(1)}, bf16[512,256]{1,0:T(8,128)(2,1)}, u32[]{:S(2)}) copy-start(bf16[512,256]{1,0:T(8,128)(2,1)} %keys_ref.9) | copy-start | bytes 786436
  0.7 11.4 %copy-start.3 = (bf16[512,256]{1,0:T(8,128)(2,1)S(1)}, bf16[512,256]{1,0:T(8,128)(2,1)}, u32[]{:S(2)}) copy-start(bf16[512,256]{1,0:T(8,128)(2,1)} %values_ref.9) | copy-start | bytes 786436
  7.6 12.2 %copy-start.22 = (bf16[256,768]{1,0:T(8,128)(2,1)S(1)}, bf16[256,768]{1,0:T(8,128)(2,1)}, u32[]{:S(2)}) copy-start(bf16[256,768]{1,0:T(8,128)(2,1)} %get-tuple-element.27) | copy-start | bytes 1179652
  7.6 12.2 %collective-permute-start.1 = (bf16[256,768]{1,0:T(8,128)(2,1)}, bf16[256,768]{1,0:T(8,128)(2,1)S(1)}, u32[]{:S(2)}, u32[]{:S(2)}) collective-permute-start(bf16[256,768]{1,0:T(8,128)(2,1)} %get-tuple-element.28), channel_id=1, source_target_pairs={{0,4},{4,0},{8,12},{12,8},{16,20},{20,16},{24,28},{28,24},{1,5},{5... | collective-permute-start | bytes 1179656 | tf_op jit(solution)/shard_map/ppermute | solution.py:312
  9.1 12.4 %copy-start.21 = (bf16[256,768]{1,0:T(8,128)(2,1)S(1)}, bf16[256,768]{1,0:T(8,128)(2,1)}, u32[]{:S(2)}) copy-start(bf16[256,768]{1,0:T(8,128)(2,1)} %get-tuple-element.29) | copy-start | bytes 1179652
  9.2 17.9 %collective-permute-start = (bf16[1536,128]{1,0:T(8,128)(2,1)S(1)}, bf16[1536,128]{1,0:T(8,128)(2,1)S(1)}, u32[]{:S(2)}, u32[]{:S(2)}) collective-permute-start(bf16[1536,128]{1,0:T(8,128)(2,1)S(1)} %shard_map.131), channel_id=1, source_target_pairs={{0,4},{4,0},{8,12},{12,8},{16,20},{20,16},{24,28},{28,24},{1,5},{5... | collective-permute-start | bytes 1179656 | tf_op jit(solution)/shard_map/ppermute | solution.py:312
  9.8 11.8 %collective-permute-start.3 = (bf16[256,768]{1,0:T(8,128)(2,1)}, bf16[256,768]{1,0:T(8,128)(2,1)S(1)}, u32[]{:S(2)}, u32[]{:S(2)}) collective-permute-start(bf16[256,768]{1,0:T(8,128)(2,1)} %get-tuple-element.30), channel_id=1, source_target_pairs={{0,8},{4,12},{8,0},{12,4},{16,24},{20,28},{24,16},{28,20},{1,9},{5... | collective-permute-start | bytes 1179656 | tf_op jit(solution)/shard_map/ppermute | solution.py:312
  19.9 7.3 %collective-permute-start.2 = (bf16[128,768]{1,0:T(8,128)(2,1)S(1)}, bf16[128,768]{1,0:T(8,128)(2,1)S(1)}, u32[]{:S(2)}, u32[]{:S(2)}) collective-permute-start(bf16[128,768]{1,0:T(8,128)(2,1)S(1)} %get-tuple-element.51), channel_id=1, source_target_pairs={{0,8},{4,12},{8,0},{12,4},{16,24},{20,28},{24,16},{28,20},{1,9},{5... | collective-permute-start | bytes 589832 | tf_op jit(solution)/shard_map/ppermute | solution.py:312
  21.6 7.5 %collective-permute-start.4 = (bf16[128,768]{1,0:T(8,128)(2,1)S(1)}, bf16[128,768]{1,0:T(8,128)(2,1)S(1)}, u32[]{:S(2)}, u32[]{:S(2)}) collective-permute-start(bf16[128,768]{1,0:T(8,128)(2,1)S(1)} %get-tuple-element.49), channel_id=1, source_target_pairs={{0,16},{4,20},{8,24},{12,28},{16,0},{20,4},{24,8},{28,12},{1,17},{... | collective-permute-start | bytes 589832 | tf_op jit(solution)/shard_map/ppermute | solution.py:312
  27.2 16.0 %collective-permute-start.8 = (bf16[64,768]{1,0:T(8,128)(2,1)S(1)}, bf16[64,768]{1,0:T(8,128)(2,1)S(1)}, u32[]{:S(2)}, u32[]{:S(2)}) collective-permute-start(bf16[64,768]{1,0:T(8,128)(2,1)S(1)} %get-tuple-element.54), channel_id=1, source_target_pairs={{0,16},{4,20},{8,24},{12,28},{16,0},{20,4},{24,8},{28,12},{1,17},{... | collective-permute-start | bytes 294920 | tf_op jit(solution)/shard_map/ppermute | solution.py:312
  29.2 14.1 %collective-permute-start.10 = (bf16[64,768]{1,0:T(8,128)(2,1)S(1)}, bf16[64,768]{1,0:T(8,128)(2,1)S(1)}, u32[]{:S(2)}, u32[]{:S(2)}) collective-permute-start(bf16[64,768]{1,0:T(8,128)(2,1)S(1)} %get-tuple-element.52), channel_id=1, source_target_pairs={{0,4},{4,0},{8,12},{12,8},{16,20},{20,16},{24,28},{28,24},{1,5},{5... | collective-permute-start | bytes 294920 | tf_op jit(solution)/shard_map/ppermute | solution.py:312
  30.8 22.0 %collective-permute-start.5 = (bf16[1024,128]{1,0:T(8,128)(2,1)S(1)}, bf16[1024,128]{1,0:T(8,128)(2,1)S(1)}, u32[]{:S(2)}, u32[]{:S(2)}) collective-permute-start(bf16[1024,128]{1,0:T(8,128)(2,1)S(1)} %get-tuple-element.31.high_ref), channel_id=1, source_target_pairs={{0,8},{4,12},{8,16},{12,20},{16,24},{20,28},{1,9},{5,13},{9,17},{1... | collective-permute-start | bytes 786440 | tf_op jit(solution)/shard_map/ppermute | solution.py:301
  38.9 13.9 %collective-permute-start.6 = (bf16[1024,128]{1,0:T(8,128)(2,1)S(1)}, bf16[1024,128]{1,0:T(8,128)(2,1)S(1)}, u32[]{:S(2)}, u32[]{:S(2)}) collective-permute-start(bf16[1024,128]{1,0:T(8,128)(2,1)S(1)} %get-tuple-element.32.low_ref), channel_id=1, source_target_pairs={{8,0},{12,4},{16,8},{20,12},{24,16},{28,20},{9,1},{13,5},{17,9},{2... | collective-permute-start | bytes 786440 | tf_op jit(solution)/shard_map/ppermute | solution.py:301
  40.8 14.2 %collective-permute-start.12 = (bf16[1024,256]{1,0:T(8,128)(2,1)}, bf16[1024,256]{1,0:T(8,128)(2,1)S(1)}, u32[]{:S(2)}, u32[]{:S(2)}) collective-permute-start(bf16[1024,256]{1,0:T(8,128)(2,1)} %constant_dynamic-update-slice_fusion), channel_id=1, source_target_pairs={{0,4},{4,8},{8,12},{12,16},{16,20},{20,24},{24,28},{1,5},{5,9},{9,... | collective-permute-start | bytes 1572872 | tf_op jit(solution)/shard_map/ppermute | solution.py:301
  43.2 5.6 %collective-permute-start.9 = (bf16[64,768]{1,0:T(8,128)(2,1)S(1)}, bf16[64,768]{1,0:T(8,128)(2,1)S(1)}, u32[]{:S(2)}, u32[]{:S(2)}) collective-permute-start(bf16[64,768]{1,0:T(8,128)(2,1)S(1)} %add_convert_fusion.5), channel_id=1, source_target_pairs={{0,16},{4,20},{8,24},{12,28},{16,0},{20,4},{24,8},{28,12},{1,17},{... | collective-permute-start | bytes 294920 | tf_op jit(solution)/shard_map/ppermute | solution.py:312
  43.3 8.7 %collective-permute-start.11 = (bf16[64,768]{1,0:T(8,128)(2,1)S(1)}, bf16[64,768]{1,0:T(8,128)(2,1)S(1)}, u32[]{:S(2)}, u32[]{:S(2)}) collective-permute-start(bf16[64,768]{1,0:T(8,128)(2,1)S(1)} %add_convert_fusion.4), channel_id=1, source_target_pairs={{0,4},{4,0},{8,12},{12,8},{16,20},{20,16},{24,28},{28,24},{1,5},{5... | collective-permute-start | bytes 294920 | tf_op jit(solution)/shard_map/ppermute | solution.py:312
  55.0 0.8 copy-start.4
  55.8 10.1 %collective-permute-start.13 = (bf16[128,768]{1,0:T(8,128)(2,1)}, bf16[128,768]{1,0:T(8,128)(2,1)}, u32[]{:S(2)}, u32[]{:S(2)}) collective-permute-start(bf16[128,768]{1,0:T(8,128)(2,1)} %pad_maximum_fusion.2), channel_id=1, source_target_pairs={{0,8},{4,12},{8,0},{12,4},{16,24},{20,28},{24,16},{28,20},{1,9},{5... | collective-permute-start | bytes 589832 | tf_op jit(solution)/shard_map/ppermute | solution.py:312
  60.3 8.5 %collective-permute-start.14 = (bf16[128,768]{1,0:T(8,128)(2,1)}, bf16[128,768]{1,0:T(8,128)(2,1)S(1)}, u32[]{:S(2)}, u32[]{:S(2)}) collective-permute-start(bf16[128,768]{1,0:T(8,128)(2,1)} %pad_maximum_fusion.3), channel_id=1, source_target_pairs={{0,16},{4,20},{8,24},{12,28},{16,0},{20,4},{24,8},{28,12},{1,17},{... | collective-permute-start | bytes 589832 | tf_op jit(solution)/shard_map/ppermute | solution.py:312
  64.3 19.2 %copy-start.17 = (bf16[512,128]{1,0:T(8,128)(2,1)}, bf16[512,128]{1,0:T(8,128)(2,1)S(1)}, u32[]{:S(2)}) copy-start(bf16[512,128]{1,0:T(8,128)(2,1)S(1)} %get-tuple-element.33.keep_ref) | copy-start | bytes 393220
  64.3 30.0 %copy-start = (bf16[1,512,3,512]{3,1,2,0:T(8,128)(2,1)S(1)}, bf16[1,512,3,512]{3,1,2,0:T(8,128)(2,1)}, u32[]{:S(2)}) copy-start(bf16[1,512,3,512]{3,1,2,0:T(8,128)(2,1)} %param.19) | copy-start | bytes 4718596
  64.3 30.0 %copy-start.1 = (bf16[512,1024]{1,0:T(8,128)(2,1)S(1)}, bf16[512,1024]{1,0:T(8,128)(2,1)}, u32[]{:S(2)}) copy-start(bf16[512,1024]{1,0:T(8,128)(2,1)} %map_ref.3) | copy-start | bytes 3145732
  69.8 12.9 %collective-permute-start.15 = (bf16[256,768]{1,0:T(8,128)(2,1)S(1)}, bf16[256,768]{1,0:T(8,128)(2,1)S(1)}, u32[]{:S(2)}, u32[]{:S(2)}) collective-permute-start(bf16[256,768]{1,0:T(8,128)(2,1)S(1)} %pad_maximum_fusion.refs_0_), channel_id=1, source_target_pairs={{0,4},{4,0},{8,12},{12,8},{16,20},{20,16},{24,28},{28,24},{1,5},{5... | collective-permute-start | bytes 1179656 | tf_op jit(solution)/shard_map/ppermute | solution.py:312
  70.9 12.6 %collective-permute-start.16 = (bf16[256,768]{1,0:T(8,128)(2,1)S(1)}, bf16[256,768]{1,0:T(8,128)(2,1)S(1)}, u32[]{:S(2)}, u32[]{:S(2)}) collective-permute-start(bf16[256,768]{1,0:T(8,128)(2,1)S(1)} %pad_maximum_fusion.1.refs_2_), channel_id=1, source_target_pairs={{0,8},{4,12},{8,0},{12,4},{16,24},{20,28},{24,16},{28,20},{1,9},{5... | collective-permute-start | bytes 1179656 | tf_op jit(solution)/shard_map/ppermute | solution.py:312
  72.0 0.8 copy-start.6
  72.8 9.4 %collective-permute-start.7 = (bf16[512,128]{1,0:T(8,128)(2,1)S(1)}, bf16[512,128]{1,0:T(8,128)(2,1)S(1)}, u32[]{:S(2)}, u32[]{:S(2)}) collective-permute-start(bf16[512,128]{1,0:T(8,128)(2,1)S(1)} %get-tuple-element.34), channel_id=1, source_target_pairs={{0,4},{4,0},{8,12},{12,8},{16,20},{20,16},{24,28},{28,24},{1,5},{5... | collective-permute-start | bytes 393224 | tf_op jit(solution)/shard_map/ppermute | solution.py:312
  82.1 0.7 copy-start.19
  82.8 0.7 copy-start.11
  83.5 0.7 copy-start.13
  84.3 18.1 %collective-permute-start.17 = (bf16[1024,256]{1,0:T(8,128)(2,1)}, bf16[1024,256]{1,0:T(8,128)(2,1)}, u32[]{:S(2)}, u32[]{:S(2)}) collective-permute-start(bf16[1024,256]{1,0:T(8,128)(2,1)} %constant_dynamic-update-slice_fusion), channel_id=1, source_target_pairs={{4,0},{8,4},{12,8},{16,12},{20,16},{24,20},{28,24},{5,1},{9,5},{13... | collective-permute-start | bytes 1572872 | tf_op jit(solution)/shard_map/ppermute | solution.py:301
  91.1 1.0 copy-start.16
  92.0 0.9 copy-start.18
  92.9 0.9 copy-start.20
  94.4 1.0 copy-start.7
  95.4 1.0 copy-start.12
  96.4 1.0 copy-start.14
  102.2 8.2 %copy-start.5 = (bf16[1024,256]{1,0:T(8,128)(2,1)S(1)}, bf16[1024,256]{1,0:T(8,128)(2,1)}, u32[]{:S(2)}) copy-start(bf16[1024,256]{1,0:T(8,128)(2,1)} %copy-done.4) | copy-start | bytes 1572868
  102.2 8.2 %copy-start.10 = (bf16[512,256]{1,0:T(8,128)(2,1)S(1)}, bf16[512,256]{1,0:T(8,128)(2,1)}, u32[]{:S(2)}) copy-start(bf16[512,256]{1,0:T(8,128)(2,1)} %queries_ref.7) | copy-start | bytes 786436
  102.2 1.6 %collective-permute-start.19 = (bf16[512,256]{1,0:T(8,128)(2,1)S(1)}, bf16[512,256]{1,0:T(8,128)(2,1)S(1)}, u32[]{:S(2)}, u32[]{:S(2)}) collective-permute-start(bf16[512,256]{1,0:T(8,128)(2,1)S(1)} %get-tuple-element.46), channel_id=1, source_target_pairs={{0,1},{1,0},{2,3},{3,2},{4,5},{5,4},{6,7},{7,6},{8,9},{9,8},{10,11... | collective-permute-start | bytes 786440 | tf_op jit(solution)/shard_map/ppermute | solution.py:307
  103.3 7.1 %collective-permute-start.18 = (bf16[512,256]{1,0:T(8,128)(2,1)S(1)}, bf16[512,256]{1,0:T(8,128)(2,1)S(1)}, u32[]{:S(2)}, u32[]{:S(2)}) collective-permute-start(bf16[512,256]{1,0:T(8,128)(2,1)S(1)} %get-tuple-element.44), channel_id=1, source_target_pairs={{0,1},{1,0},{2,3},{3,2},{4,5},{5,4},{6,7},{7,6},{8,9},{9,8},{10,11... | collective-permute-start | bytes 786440 | tf_op jit(solution)/shard_map/ppermute | solution.py:307
  104.0 6.4 %collective-permute-start.21 = (bf16[256,256]{1,0:T(8,128)(2,1)S(1)}, bf16[256,256]{1,0:T(8,128)(2,1)S(1)}, u32[]{:S(2)}, u32[]{:S(2)}) collective-permute-start(bf16[256,256]{1,0:T(8,128)(2,1)S(1)} %get-tuple-element.56), channel_id=1, source_target_pairs={{0,2},{1,3},{2,0},{3,1},{4,6},{5,7},{6,4},{7,5},{8,10},{9,11},{10,... | collective-permute-start | bytes 393224 | tf_op jit(solution)/shard_map/ppermute | solution.py:307
  105.5 7.8 %collective-permute-start.20 = (bf16[256,256]{1,0:T(8,128)(2,1)S(1)}, bf16[256,256]{1,0:T(8,128)(2,1)S(1)}, u32[]{:S(2)}, u32[]{:S(2)}) collective-permute-start(bf16[256,256]{1,0:T(8,128)(2,1)S(1)} %get-tuple-element.57), channel_id=1, source_target_pairs={{0,2},{1,3},{2,0},{3,1},{4,6},{5,7},{6,4},{7,5},{8,10},{9,11},{10,... | collective-permute-start | bytes 393224 | tf_op jit(solution)/shard_map/ppermute | solution.py:307

commit v13 on v11

--- a/solution.py
+++ b/solution.py
@@ -229,8 +229,8 @@
         out_ref[rows, :] = (both * lax.rsqrt(mean + 1e-05)).astype(BF16)
 
 
-def renew_kernel(orders, place_ref, places_ref, weights_ref, query_ref, map_ref, *refs):
-    pieces, (own_ref, fast_ref, send_ref, keep_ref, new_ref) = refs[:-5], refs[-5:]
+def renew_kernel(orders, place_ref, weights_ref, query_ref, *refs):
+    pieces, (own_ref, fast_ref, new_ref) = refs[:-3], refs[-3:]
     place = place_ref[0, 0]
     hidden_size, width = weights_ref.shape[1:]
     limit_norm = math.sqrt(FAST_HIDDEN * FAST_DIM) / 2.0
@@ -282,18 +282,13 @@
         raw = dot_nn(hidden, new_ref[2])
         mean = jnp.mean(raw * raw, axis=1, keepdims=True)
         fast_ref[rows, :] = (raw * lax.rsqrt(mean + 1e-05)).astype(BF16)
-    mix([places_ref[0, 0], places_ref[0, 1]], fast_ref[...], map_ref, [send_ref, keep_ref])
-
-
-def mix(places, fast, map_ref, out_refs):
-    for place, out_ref in zip(places, out_refs):
+
+
+def mix_kernel(pair, places_ref, fast_ref, map_ref, *out_refs):
+    for index, out_ref in enumerate(out_refs):
         width = out_ref.shape[1]
-        columns = map_ref[:, pl.ds(pl.multiple_of(place * width, width), width)]
-        out_ref[...] = dot_nn(fast, columns).astype(BF16)
-
-
-def mix_kernel(places_ref, fast_ref, map_ref, *out_refs):
-    mix([places_ref[0, 2], places_ref[0, 3]], fast_ref[...], map_ref, out_refs)
+        start = pl.multiple_of(places_ref[0, 2 * pair + index] * width, width)
+        out_ref[...] = dot_nn(fast_ref[...], map_ref[:, pl.ds(start, width)]).astype(BF16)
 
 
 def seq_shift(value, step):
@@ -459,17 +454,22 @@
         [2 * pair + bit for pair in (near ^ 1, near) for bit in (1 - my_bit, my_bit)]
     ).astype(jnp.int32).reshape(1, 4)
     share = shape((rows, width), BF16)
-    own_new, fast_out, far_send, far_keep = call(
+    own_new, fast_out = call(
         functools.partial(renew_kernel, orders),
-        [shape((3, own_rows, fast_width), BF16), shape((rows, fast_width), BF16), share, share],
-        (place, places, weights, fast_query, output_map, *gathered),
-        scalars=2,
+        [shape((3, own_rows, fast_width), BF16), shape((rows, fast_width), BF16)],
+        (place, weights, fast_query, *gathered),
+        scalars=1,
         scratch=[pltpu.VMEM(weights.shape, BF16)],
     )
+
+    def mixed_for(pair, fast):
+        return call(
+            functools.partial(mix_kernel, pair), [share, share], (places, fast, output_map), scalars=1
+        )
+
+    far_send, far_keep = mixed_for(0, fast_out)
     far_near = head_swap(far_send, 1)
-    near_send, near_keep = call(
-        mix_kernel, [share, share], (places, fast_out, output_map), scalars=1
-    )
+    near_send, near_keep = mixed_for(1, after(fast_out, next_second))
     near_near = head_swap(near_send, 1)
     half = rows // 2
     far_parts = []

time: 112 us -> 118 us (1.054)
  the two profiles are of different devices: /device:TPU:0 before, /device:TPU:16 now
where the time goes in v13:
time: 118 us; the launch traced here: 117 us
  starting transfers between devices  40.2 us (34%)
  waiting for transfers between devices  39.2 us (33%)
  Pallas kernels  23.4 us (20%)
  local copies, waits for them, and re-layouts  10.2 us (9%)
  other arithmetic  3.12 us (3%)
    ppermute x14, waiting for transfers between devices, seq_swap(): lax.ppermute(value, 'seq', [(i, i ^ step) for i in range(lax.axis_size('s...  32.6 us
    ppermute x14, starting transfers between devices, seq_swap(): lax.ppermute(value, 'seq', [(i, i ^ step) for i in range(lax.axis_size('s...  20.2 us
    ppermute x4, starting transfers between devices, seq_shift(): lax.ppermute(value, 'seq', [(i, i + step) for i in range(peers) if 0 <= i...  17.3 us
    pallas_call x9, Pallas kernels, call(): pl.pallas_call(body, out_shape=out_shapes, in_specs=in_specs, out_specs=j...  16.5 us
    unnamed x43, local copies, waits for them, and re-layouts  9.41 us
    pallas_call x1, Pallas kernels, local(): pl.pallas_call(functools.partial(gradient_kernel, orders), grid=(hidden_s...  6.86 us
    ppermute x4, waiting for transfers between devices, head_swap(): lax.ppermute(value, 'head', [(i, i ^ bit) for i in range(lax.axis_size('h...  4.33 us
    ppermute x4, starting transfers between devices, head_swap(): lax.ppermute(value, 'head', [(i, i ^ bit) for i in range(lax.axis_size('h...  2.72 us
  transfers between devices with their start and end apart: 22, of which 10 were waited for; matrix products, arithmetic and copies ran while one was open for 3% of the time, Pallas kernels for 11%

profile of v13, /device:TPU:16, one launch (start us, length us, event | category | flops | bytes accessed | tf_op | source)
XLA Modules:
  0.0 117.1 jit_solution(14730611365416539654)
XLA Ops:
  0.7 6.9 %shard_map.133 = (bf16[256,768]{1,0:T(8,128)(2,1)}, bf16[256,768]{1,0:T(8,128)(2,1)}, bf16[256,768]{1,0:T(8,128)(2,1)}, bf16[256,768]{1,0:T(8,128)(2,1)}) custom-call(s32[1,1]{1,0:T(1,128)} %bitcast.9.place_ref, f32[1,512]{1,0:T(1,128)} %bitcast.23, bf16[512,512]{1,0:T(8,128)(2,1)} %keys_ref.7, bf16[512,512]{1,0:T(8,128)(2,1)} %values_ref.7, ...), custom_call_target="tpu_custom_call" | custom-call | flops 1000 | bytes 1000 | tf_op jit(solution)/shard_map/pallas_call | solution.py:381
  7.5 1.5 %collective-permute-start.1 = (bf16[256,768]{1,0:T(8,128)(2,1)}, bf16[256,768]{1,0:T(8,128)(2,1)S(1)}, u32[]{:S(2)}, u32[]{:S(2)}) collective-permute-start(bf16[256,768]{1,0:T(8,128)(2,1)} %get-tuple-element.28), channel_id=1, source_target_pairs={{0,4},{4,0},{8,12},{12,8},{16,20},{20,16},{24,28},{28,24},{1,5},{5... | collective-permute-start | bytes 1179656 | tf_op jit(solution)/shard_map/ppermute | solution.py:307
  9.2 0.6 collective-permute-start
  9.7 1.6 %collective-permute-start.3 = (bf16[256,768]{1,0:T(8,128)(2,1)}, bf16[256,768]{1,0:T(8,128)(2,1)S(1)}, u32[]{:S(2)}, u32[]{:S(2)}) collective-permute-start(bf16[256,768]{1,0:T(8,128)(2,1)} %get-tuple-element.30), channel_id=1, source_target_pairs={{0,8},{4,12},{8,0},{12,4},{16,24},{20,28},{24,16},{28,20},{1,9},{5... | collective-permute-start | bytes 1179656 | tf_op jit(solution)/shard_map/ppermute | solution.py:307
  11.3 0.7 constant_dynamic-update-slice_fusion.1
  12.0 0.7 constant_dynamic-update-slice_fusion
  12.8 7.0 %collective-permute-done.1 = bf16[256,768]{1,0:T(8,128)(2,1)S(1)} collective-permute-done((bf16[256,768]{1,0:T(8,128)(2,1)}, bf16[256,768]{1,0:T(8,128)(2,1)S(1)}, u32[]{:S(2)}, u32[]{:S(2)}) %collective-permute-start.1) | collective-permute-done | bytes 393248 | tf_op jit(solution)/shard_map/ppermute | solution.py:307
  19.9 1.6 %collective-permute-start.2 = (bf16[128,768]{1,0:T(8,128)(2,1)S(1)}, bf16[128,768]{1,0:T(8,128)(2,1)S(1)}, u32[]{:S(2)}, u32[]{:S(2)}) collective-permute-start(bf16[128,768]{1,0:T(8,128)(2,1)S(1)} %get-tuple-element.51), channel_id=1, source_target_pairs={{0,8},{4,12},{8,0},{12,4},{16,24},{20,28},{24,16},{28,20},{1,9},{5... | collective-permute-start | bytes 589832 | tf_op jit(solution)/shard_map/ppermute | solution.py:307
  22.0 5.0 %collective-permute-done.other_ref = bf16[1536,128]{1,0:T(8,128)(2,1)S(1)} collective-permute-done((bf16[1536,128]{1,0:T(8,128)(2,1)S(1)}, bf16[1536,128]{1,0:T(8,128)(2,1)S(1)}, u32[]{:S(2)}, u32[]{:S(2)}) %collective-permute-start) | collective-permute-done | bytes 393248 | tf_op jit(solution)/shard_map/ppermute | solution.py:307
  27.2 0.9 collective-permute-start.8
  28.1 1.0 collective-permute-done.4
  29.1 1.6 %collective-permute-start.10 = (bf16[64,768]{1,0:T(8,128)(2,1)S(1)}, bf16[64,768]{1,0:T(8,128)(2,1)S(1)}, u32[]{:S(2)}, u32[]{:S(2)}) collective-permute-start(bf16[64,768]{1,0:T(8,128)(2,1)S(1)} %get-tuple-element.52), channel_id=1, source_target_pairs={{0,4},{4,0},{8,12},{12,8},{16,20},{20,16},{24,28},{28,24},{1,5},{5... | collective-permute-start | bytes 294920 | tf_op jit(solution)/shard_map/ppermute | solution.py:307
  30.8 8.1 %collective-permute-start.5 = (bf16[1024,128]{1,0:T(8,128)(2,1)S(1)}, bf16[1024,128]{1,0:T(8,128)(2,1)S(1)}, u32[]{:S(2)}, u32[]{:S(2)}) collective-permute-start(bf16[1024,128]{1,0:T(8,128)(2,1)S(1)} %get-tuple-element.31.high_ref), channel_id=1, source_target_pairs={{0,8},{4,12},{8,16},{12,20},{16,24},{20,28},{1,9},{5,13},{9,17},{1... | collective-permute-start | bytes 786440 | tf_op jit(solution)/shard_map/ppermute | solution.py:296
  38.8 1.9 %collective-permute-start.6 = (bf16[1024,128]{1,0:T(8,128)(2,1)S(1)}, bf16[1024,128]{1,0:T(8,128)(2,1)S(1)}, u32[]{:S(2)}, u32[]{:S(2)}) collective-permute-start(bf16[1024,128]{1,0:T(8,128)(2,1)S(1)} %get-tuple-element.32.low_ref), channel_id=1, source_target_pairs={{8,0},{12,4},{16,8},{20,12},{24,16},{28,20},{9,1},{13,5},{17,9},{2... | collective-permute-start | bytes 786440 | tf_op jit(solution)/shard_map/ppermute | solution.py:296
  40.8 2.4 %collective-permute-start.12 = (bf16[1024,256]{1,0:T(8,128)(2,1)}, bf16[1024,256]{1,0:T(8,128)(2,1)S(1)}, u32[]{:S(2)}, u32[]{:S(2)}) collective-permute-start(bf16[1024,256]{1,0:T(8,128)(2,1)} %constant_dynamic-update-slice_fusion), channel_id=1, source_target_pairs={{0,4},{4,8},{8,12},{12,16},{16,20},{20,24},{24,28},{1,5},{5,9},{9,... | collective-permute-start | bytes 1572872 | tf_op jit(solution)/shard_map/ppermute | solution.py:296
  43.3 3.1 %collective-permute-start.11 = (bf16[64,768]{1,0:T(8,128)(2,1)S(1)}, bf16[64,768]{1,0:T(8,128)(2,1)S(1)}, u32[]{:S(2)}, u32[]{:S(2)}) collective-permute-start(bf16[64,768]{1,0:T(8,128)(2,1)S(1)} %add_convert_fusion.4), channel_id=1, source_target_pairs={{0,4},{4,0},{8,12},{12,8},{16,20},{20,16},{24,28},{28,24},{1,5},{5... | collective-permute-start | bytes 294920 | tf_op jit(solution)/shard_map/ppermute | solution.py:307
  46.4 2.4 %collective-permute-done.9 = bf16[64,768]{1,0:T(8,128)(2,1)S(1)} collective-permute-done((bf16[64,768]{1,0:T(8,128)(2,1)S(1)}, bf16[64,768]{1,0:T(8,128)(2,1)S(1)}, u32[]{:S(2)}, u32[]{:S(2)}) %collective-permute-start.9) | collective-permute-done | bytes 98336 | tf_op jit(solution)/shard_map/ppermute | solution.py:307
  48.9 3.2 %collective-permute-done.11 = bf16[64,768]{1,0:T(8,128)(2,1)S(1)} collective-permute-done((bf16[64,768]{1,0:T(8,128)(2,1)S(1)}, bf16[64,768]{1,0:T(8,128)(2,1)S(1)}, u32[]{:S(2)}, u32[]{:S(2)}) %collective-permute-start.11) | collective-permute-done | bytes 98336 | tf_op jit(solution)/shard_map/ppermute | solution.py:307
  52.0 0.7 pad_maximum_fusion.3
  52.7 2.2 %collective-permute-done.12.prev_ref = bf16[1024,256]{1,0:T(8,128)(2,1)S(1)} collective-permute-done((bf16[1024,256]{1,0:T(8,128)(2,1)}, bf16[1024,256]{1,0:T(8,128)(2,1)S(1)}, u32[]{:S(2)}, u32[]{:S(2)}) %collective-permute-start.12) | collective-permute-done | bytes 524320 | tf_op jit(solution)/shard_map/ppermute | solution.py:296
  55.0 6.3 %collective-permute-start.13 = (bf16[128,768]{1,0:T(8,128)(2,1)S(1)}, bf16[128,768]{1,0:T(8,128)(2,1)}, u32[]{:S(2)}, u32[]{:S(2)}) collective-permute-start(bf16[128,768]{1,0:T(8,128)(2,1)S(1)} %pad_maximum_fusion.2), channel_id=1, source_target_pairs={{0,8},{4,12},{8,0},{12,4},{16,24},{20,28},{24,16},{28,20},{1,9},{5... | collective-permute-start | bytes 589832 | tf_op jit(solution)/shard_map/ppermute | solution.py:307
  61.4 4.0 %shard_map.134 = (bf16[512,128]{1,0:T(8,128)(2,1)S(1)}, bf16[512,128]{1,0:T(8,128)(2,1)S(1)}) custom-call(f32[2,2]{1,0:T(2,128)S(1)} %reshape.19.edge_ref, s32[1,1]{1,0:T(1,128)} %bitcast.12.side_ref, bf16[512,256]{1,0:T(8,128)(2,1)S(1)} %copy-done.13, bf16[1536,128]{1,0:T(8,128)(2,1)S(1)} %collective-permute-done.other_ref, ...), custom_call_target="tpu_custom_call" | custom-call | flops 805306368 | bytes 2097152 | tf_op jit(solution)/shard_map/pallas_call | solution.py:41
  65.4 1.7 %collective-permute-done.13 = bf16[128,768]{1,0:T(8,128)(2,1)} collective-permute-done((bf16[128,768]{1,0:T(8,128)(2,1)S(1)}, bf16[128,768]{1,0:T(8,128)(2,1)}, u32[]{:S(2)}, u32[]{:S(2)}) %collective-permute-start.13) | collective-permute-done | bytes 196640 | tf_op jit(solution)/shard_map/ppermute | solution.py:307
  67.1 1.0 pad_maximum_fusion.refs_0_
  68.0 2.3 %collective-permute-done.14 = bf16[128,768]{1,0:T(8,128)(2,1)S(1)} collective-permute-done((bf16[128,768]{1,0:T(8,128)(2,1)}, bf16[128,768]{1,0:T(8,128)(2,1)S(1)}, u32[]{:S(2)}, u32[]{:S(2)}) %collective-permute-start.14) | collective-permute-done | bytes 196640 | tf_op jit(solution)/shard_map/ppermute | solution.py:307
  70.3 1.0 pad_maximum_fusion.1.refs_2_
  71.4 0.9 collective-permute-start.16
  72.3 0.7 copy-done.4
  73.0 1.5 %collective-permute-start.7 = (bf16[512,128]{1,0:T(8,128)(2,1)S(1)}, bf16[512,128]{1,0:T(8,128)(2,1)S(1)}, u32[]{:S(2)}, u32[]{:S(2)}) collective-permute-start(bf16[512,128]{1,0:T(8,128)(2,1)S(1)} %get-tuple-element.34), channel_id=1, source_target_pairs={{0,4},{4,0},{8,12},{12,8},{16,20},{20,16},{24,28},{28,24},{1,5},{5... | collective-permute-start | bytes 393224 | tf_op jit(solution)/shard_map/ppermute | solution.py:307
  74.6 10.0 %collective-permute-done.7.other_ref = bf16[512,128]{1,0:T(8,128)(2,1)S(1)} collective-permute-done((bf16[512,128]{1,0:T(8,128)(2,1)S(1)}, bf16[512,128]{1,0:T(8,128)(2,1)S(1)}, u32[]{:S(2)}, u32[]{:S(2)}) %collective-permute-start.7) | collective-permute-done | bytes 131104 | tf_op jit(solution)/shard_map/ppermute | solution.py:307
  84.5 0.7 copy-done.17
  85.2 0.8 copy-done.9
  86.0 0.7 copy-done.11
  86.7 4.9 %collective-permute-start.17 = (bf16[1024,256]{1,0:T(8,128)(2,1)}, bf16[1024,256]{1,0:T(8,128)(2,1)S(1)}, u32[]{:S(2)}, u32[]{:S(2)}) collective-permute-start(bf16[1024,256]{1,0:T(8,128)(2,1)} %constant_dynamic-update-slice_fusion), channel_id=1, source_target_pairs={{4,0},{8,4},{12,8},{16,12},{20,16},{24,20},{28,24},{5,1},{9,5},{13... | collective-permute-start | bytes 1572872 | tf_op jit(solution)/shard_map/ppermute | solution.py:296
  91.6 0.9 copy-done.14
  92.6 0.9 copy-done.16
  93.5 0.9 copy-done.18
  95.0 1.0 copy-done.5
  96.0 1.0 copy-done.10
  97.0 1.0 copy-done.12
  98.0 4.4 %shard_map.136 = (bf16[3,64,512]{2,1,0:T(8,128)(2,1)}, bf16[512,512]{1,0:T(8,128)(2,1)S(1)}) custom-call(s32[1,1]{1,0:T(1,128)} %bitcast.9.place_ref, bf16[3,512,512]{2,1,0:T(8,128)(2,1)S(1)} %bitcast.21, bf16[512,512]{1,0:T(8,128)(2,1)S(1)} %shard_map.135.query_ref, bf16[256,768]{1,0:T(8,128)(2,1)S(1)} %pad_maximum_fusion.refs_0_, ...), custom_call_target="tpu_custom_call" | custom-call | flops 1000 | bytes 1000 | tf_op jit(solution)/shard_map/pallas_call | solution.py:41
  102.4 1.0 shard_map.138
  103.5 1.0 shard_map.137
  105.1 1.5 %collective-permute-start.21 = (bf16[256,256]{1,0:T(8,128)(2,1)S(1)}, bf16[256,256]{1,0:T(8,128)(2,1)S(1)}, u32[]{:S(2)}, u32[]{:S(2)}) collective-permute-start(bf16[256,256]{1,0:T(8,128)(2,1)S(1)} %get-tuple-element.56), channel_id=1, source_target_pairs={{0,2},{1,3},{2,0},{3,1},{4,6},{5,7},{6,4},{7,5},{8,10},{9,11},{10,... | collective-permute-start | bytes 393224 | tf_op jit(solution)/shard_map/ppermute | solution.py:302
  106.6 0.6 collective-permute-start.20
  107.2 4.3 %collective-permute-done.21.far_ref = bf16[256,256]{1,0:T(8,128)(2,1)S(1)} collective-permute-done((bf16[256,256]{1,0:T(8,128)(2,1)S(1)}, bf16[256,256]{1,0:T(8,128)(2,1)S(1)}, u32[]{:S(2)}, u32[]{:S(2)}) %collective-permute-start.21) | collective-permute-done | bytes 131104 | tf_op jit(solution)/shard_map/ppermute | solution.py:302
  111.5 2.4 %shard_map.139.refs_0_ = bf16[256,256]{1,0:T(8,128)(2,1)S(1)} custom-call(f32[2,2]{1,0:T(2,128)S(1)} %reshape.19.edge_ref, bf16[512,256]{1,0:T(8,128)(2,1)S(1)} %copy-done.8, bf16[512,256]{1,0:T(8,128)(2,1)S(1)} %get-tuple-element.43.keep_ref, bf16[512,256]{1,0:T(8,128)(2,1)S(1)} %collective-permute-done.18.near_ref, ...), custom_call_target="tpu_custom_call" | custom-call | flops 402653184 | bytes 2097152 | tf_op jit(solution)/shard_map/pallas_call | solution.py:41
  113.9 3.1 %shard_map.140 = bf16[512,256]{1,0:T(8,128)(2,1)} custom-call(f32[2,2]{1,0:T(2,128)S(1)} %reshape.19.edge_ref, bf16[512,256]{1,0:T(8,128)(2,1)S(1)} %copy-done.8, bf16[512,256]{1,0:T(8,128)(2,1)S(1)} %get-tuple-element.43.keep_ref, bf16[512,256]{1,0:T(8,128)(2,1)S(1)} %collective-permute-done.18.near_ref, ...), custom_call_target="tpu_custom_call" | custom-call | flops 402653184 | bytes 2097152 | tf_op jit(solution)/shard_map/pallas_call | solution.py:41
  (64 shorter events, 2.5 us)
Async XLA Ops:
  0.6 8.4 %copy-start.7 = (bf16[512,256]{1,0:T(8,128)(2,1)S(1)}, bf16[512,256]{1,0:T(8,128)(2,1)}, u32[]{:S(2)}) copy-start(bf16[512,256]{1,0:T(8,128)(2,1)} %values_ref.6) | copy-start | bytes 786436
  0.6 8.4 %copy-start.6 = (bf16[512,256]{1,0:T(8,128)(2,1)S(1)}, bf16[512,256]{1,0:T(8,128)(2,1)}, u32[]{:S(2)}) copy-start(bf16[512,256]{1,0:T(8,128)(2,1)} %keys_ref.6) | copy-start | bytes 786436
  0.7 8.4 %copy-start.13 = (bf16[512,256]{1,0:T(8,128)(2,1)S(1)}, bf16[512,256]{1,0:T(8,128)(2,1)}, u32[]{:S(2)}) copy-start(bf16[512,256]{1,0:T(8,128)(2,1)} %queries_ref.5) | copy-start | bytes 786436
  0.7 10.6 %copy-start.2 = (bf16[512,256]{1,0:T(8,128)(2,1)S(1)}, bf16[512,256]{1,0:T(8,128)(2,1)}, u32[]{:S(2)}) copy-start(bf16[512,256]{1,0:T(8,128)(2,1)} %keys_ref.9) | copy-start | bytes 786436
  0.7 11.4 %copy-start.3 = (bf16[512,256]{1,0:T(8,128)(2,1)S(1)}, bf16[512,256]{1,0:T(8,128)(2,1)}, u32[]{:S(2)}) copy-start(bf16[512,256]{1,0:T(8,128)(2,1)} %values_ref.9) | copy-start | bytes 786436
  7.5 12.2 %copy-start.20 = (bf16[256,768]{1,0:T(8,128)(2,1)S(1)}, bf16[256,768]{1,0:T(8,128)(2,1)}, u32[]{:S(2)}) copy-start(bf16[256,768]{1,0:T(8,128)(2,1)} %get-tuple-element.27) | copy-start | bytes 1179652
  7.5 12.2 %collective-permute-start.1 = (bf16[256,768]{1,0:T(8,128)(2,1)}, bf16[256,768]{1,0:T(8,128)(2,1)S(1)}, u32[]{:S(2)}, u32[]{:S(2)}) collective-permute-start(bf16[256,768]{1,0:T(8,128)(2,1)} %get-tuple-element.28), channel_id=1, source_target_pairs={{0,4},{4,0},{8,12},{12,8},{16,20},{20,16},{24,28},{28,24},{1,5},{5... | collective-permute-start | bytes 1179656 | tf_op jit(solution)/shard_map/ppermute | solution.py:307
  9.1 12.4 %copy-start.19 = (bf16[256,768]{1,0:T(8,128)(2,1)S(1)}, bf16[256,768]{1,0:T(8,128)(2,1)}, u32[]{:S(2)}) copy-start(bf16[256,768]{1,0:T(8,128)(2,1)} %get-tuple-element.29) | copy-start | bytes 1179652
  9.2 17.9 %collective-permute-start = (bf16[1536,128]{1,0:T(8,128)(2,1)S(1)}, bf16[1536,128]{1,0:T(8,128)(2,1)S(1)}, u32[]{:S(2)}, u32[]{:S(2)}) collective-permute-start(bf16[1536,128]{1,0:T(8,128)(2,1)S(1)} %shard_map.131), channel_id=1, source_target_pairs={{0,4},{4,0},{8,12},{12,8},{16,20},{20,16},{24,28},{28,24},{1,5},{5... | collective-permute-start | bytes 1179656 | tf_op jit(solution)/shard_map/ppermute | solution.py:307
  9.7 11.8 %collective-permute-start.3 = (bf16[256,768]{1,0:T(8,128)(2,1)}, bf16[256,768]{1,0:T(8,128)(2,1)S(1)}, u32[]{:S(2)}, u32[]{:S(2)}) collective-permute-start(bf16[256,768]{1,0:T(8,128)(2,1)} %get-tuple-element.30), channel_id=1, source_target_pairs={{0,8},{4,12},{8,0},{12,4},{16,24},{20,28},{24,16},{28,20},{1,9},{5... | collective-permute-start | bytes 1179656 | tf_op jit(solution)/shard_map/ppermute | solution.py:307
  19.9 7.3 %collective-permute-start.2 = (bf16[128,768]{1,0:T(8,128)(2,1)S(1)}, bf16[128,768]{1,0:T(8,128)(2,1)S(1)}, u32[]{:S(2)}, u32[]{:S(2)}) collective-permute-start(bf16[128,768]{1,0:T(8,128)(2,1)S(1)} %get-tuple-element.51), channel_id=1, source_target_pairs={{0,8},{4,12},{8,0},{12,4},{16,24},{20,28},{24,16},{28,20},{1,9},{5... | collective-permute-start | bytes 589832 | tf_op jit(solution)/shard_map/ppermute | solution.py:307
  21.6 7.5 %collective-permute-start.4 = (bf16[128,768]{1,0:T(8,128)(2,1)S(1)}, bf16[128,768]{1,0:T(8,128)(2,1)S(1)}, u32[]{:S(2)}, u32[]{:S(2)}) collective-permute-start(bf16[128,768]{1,0:T(8,128)(2,1)S(1)} %get-tuple-element.49), channel_id=1, source_target_pairs={{0,16},{4,20},{8,24},{12,28},{16,0},{20,4},{24,8},{28,12},{1,17},{... | collective-permute-start | bytes 589832 | tf_op jit(solution)/shard_map/ppermute | solution.py:307
  27.2 16.0 %collective-permute-start.8 = (bf16[64,768]{1,0:T(8,128)(2,1)S(1)}, bf16[64,768]{1,0:T(8,128)(2,1)S(1)}, u32[]{:S(2)}, u32[]{:S(2)}) collective-permute-start(bf16[64,768]{1,0:T(8,128)(2,1)S(1)} %get-tuple-element.54), channel_id=1, source_target_pairs={{0,16},{4,20},{8,24},{12,28},{16,0},{20,4},{24,8},{28,12},{1,17},{... | collective-permute-start | bytes 294920 | tf_op jit(solution)/shard_map/ppermute | solution.py:307
  29.1 14.1 %collective-permute-start.10 = (bf16[64,768]{1,0:T(8,128)(2,1)S(1)}, bf16[64,768]{1,0:T(8,128)(2,1)S(1)}, u32[]{:S(2)}, u32[]{:S(2)}) collective-permute-start(bf16[64,768]{1,0:T(8,128)(2,1)S(1)} %get-tuple-element.52), channel_id=1, source_target_pairs={{0,4},{4,0},{8,12},{12,8},{16,20},{20,16},{24,28},{28,24},{1,5},{5... | collective-permute-start | bytes 294920 | tf_op jit(solution)/shard_map/ppermute | solution.py:307
  30.8 22.0 %collective-permute-start.5 = (bf16[1024,128]{1,0:T(8,128)(2,1)S(1)}, bf16[1024,128]{1,0:T(8,128)(2,1)S(1)}, u32[]{:S(2)}, u32[]{:S(2)}) collective-permute-start(bf16[1024,128]{1,0:T(8,128)(2,1)S(1)} %get-tuple-element.31.high_ref), channel_id=1, source_target_pairs={{0,8},{4,12},{8,16},{12,20},{16,24},{20,28},{1,9},{5,13},{9,17},{1... | collective-permute-start | bytes 786440 | tf_op jit(solution)/shard_map/ppermute | solution.py:296
  38.8 13.9 %collective-permute-start.6 = (bf16[1024,128]{1,0:T(8,128)(2,1)S(1)}, bf16[1024,128]{1,0:T(8,128)(2,1)S(1)}, u32[]{:S(2)}, u32[]{:S(2)}) collective-permute-start(bf16[1024,128]{1,0:T(8,128)(2,1)S(1)} %get-tuple-element.32.low_ref), channel_id=1, source_target_pairs={{8,0},{12,4},{16,8},{20,12},{24,16},{28,20},{9,1},{13,5},{17,9},{2... | collective-permute-start | bytes 786440 | tf_op jit(solution)/shard_map/ppermute | solution.py:296
  40.8 14.2 %collective-permute-start.12 = (bf16[1024,256]{1,0:T(8,128)(2,1)}, bf16[1024,256]{1,0:T(8,128)(2,1)S(1)}, u32[]{:S(2)}, u32[]{:S(2)}) collective-permute-start(bf16[1024,256]{1,0:T(8,128)(2,1)} %constant_dynamic-update-slice_fusion), channel_id=1, source_target_pairs={{0,4},{4,8},{8,12},{12,16},{16,20},{20,24},{24,28},{1,5},{5,9},{9,... | collective-permute-start | bytes 1572872 | tf_op jit(solution)/shard_map/ppermute | solution.py:296
  43.2 5.6 %collective-permute-start.9 = (bf16[64,768]{1,0:T(8,128)(2,1)S(1)}, bf16[64,768]{1,0:T(8,128)(2,1)S(1)}, u32[]{:S(2)}, u32[]{:S(2)}) collective-permute-start(bf16[64,768]{1,0:T(8,128)(2,1)S(1)} %add_convert_fusion.5), channel_id=1, source_target_pairs={{0,16},{4,20},{8,24},{12,28},{16,0},{20,4},{24,8},{28,12},{1,17},{... | collective-permute-start | bytes 294920 | tf_op jit(solution)/shard_map/ppermute | solution.py:307
  43.3 8.7 %collective-permute-start.11 = (bf16[64,768]{1,0:T(8,128)(2,1)S(1)}, bf16[64,768]{1,0:T(8,128)(2,1)S(1)}, u32[]{:S(2)}, u32[]{:S(2)}) collective-permute-start(bf16[64,768]{1,0:T(8,128)(2,1)S(1)} %add_convert_fusion.4), channel_id=1, source_target_pairs={{0,4},{4,0},{8,12},{12,8},{16,20},{20,16},{24,28},{28,24},{1,5},{5... | collective-permute-start | bytes 294920 | tf_op jit(solution)/shard_map/ppermute | solution.py:307
  55.0 12.1 %collective-permute-start.13 = (bf16[128,768]{1,0:T(8,128)(2,1)S(1)}, bf16[128,768]{1,0:T(8,128)(2,1)}, u32[]{:S(2)}, u32[]{:S(2)}) collective-permute-start(bf16[128,768]{1,0:T(8,128)(2,1)S(1)} %pad_maximum_fusion.2), channel_id=1, source_target_pairs={{0,8},{4,12},{8,0},{12,4},{16,24},{20,28},{24,16},{28,20},{1,9},{5... | collective-permute-start | bytes 589832 | tf_op jit(solution)/shard_map/ppermute | solution.py:307
  61.4 8.9 %collective-permute-start.14 = (bf16[128,768]{1,0:T(8,128)(2,1)}, bf16[128,768]{1,0:T(8,128)(2,1)S(1)}, u32[]{:S(2)}, u32[]{:S(2)}) collective-permute-start(bf16[128,768]{1,0:T(8,128)(2,1)} %pad_maximum_fusion.3), channel_id=1, source_target_pairs={{0,16},{4,20},{8,24},{12,28},{16,0},{20,4},{24,8},{28,12},{1,17},{... | collective-permute-start | bytes 589832 | tf_op jit(solution)/shard_map/ppermute | solution.py:307
  65.4 20.6 %copy-start.15 = (bf16[512,128]{1,0:T(8,128)(2,1)}, bf16[512,128]{1,0:T(8,128)(2,1)S(1)}, u32[]{:S(2)}) copy-start(bf16[512,128]{1,0:T(8,128)(2,1)S(1)} %get-tuple-element.33.keep_ref) | copy-start | bytes 393220
  65.4 29.6 %copy-start = (bf16[1,512,3,512]{3,1,2,0:T(8,128)(2,1)S(1)}, bf16[1,512,3,512]{3,1,2,0:T(8,128)(2,1)}, u32[]{:S(2)}) copy-start(bf16[1,512,3,512]{3,1,2,0:T(8,128)(2,1)} %param.19) | copy-start | bytes 4718596
  71.3 13.9 %collective-permute-start.15 = (bf16[256,768]{1,0:T(8,128)(2,1)S(1)}, bf16[256,768]{1,0:T(8,128)(2,1)S(1)}, u32[]{:S(2)}, u32[]{:S(2)}) collective-permute-start(bf16[256,768]{1,0:T(8,128)(2,1)S(1)} %pad_maximum_fusion.refs_0_), channel_id=1, source_target_pairs={{0,4},{4,0},{8,12},{12,8},{16,20},{20,16},{24,28},{28,24},{1,5},{5... | collective-permute-start | bytes 1179656 | tf_op jit(solution)/shard_map/ppermute | solution.py:307
  71.4 14.6 %collective-permute-start.16 = (bf16[256,768]{1,0:T(8,128)(2,1)S(1)}, bf16[256,768]{1,0:T(8,128)(2,1)S(1)}, u32[]{:S(2)}, u32[]{:S(2)}) collective-permute-start(bf16[256,768]{1,0:T(8,128)(2,1)S(1)} %pad_maximum_fusion.1.refs_2_), channel_id=1, source_target_pairs={{0,8},{4,12},{8,0},{12,4},{16,24},{20,28},{24,16},{28,20},{1,9},{5... | collective-permute-start | bytes 1179656 | tf_op jit(solution)/shard_map/ppermute | solution.py:307
  72.3 0.7 copy-start.4
  73.0 11.5 %collective-permute-start.7 = (bf16[512,128]{1,0:T(8,128)(2,1)S(1)}, bf16[512,128]{1,0:T(8,128)(2,1)S(1)}, u32[]{:S(2)}, u32[]{:S(2)}) collective-permute-start(bf16[512,128]{1,0:T(8,128)(2,1)S(1)} %get-tuple-element.34), channel_id=1, source_target_pairs={{0,4},{4,0},{8,12},{12,8},{16,20},{20,16},{24,28},{28,24},{1,5},{5... | collective-permute-start | bytes 393224 | tf_op jit(solution)/shard_map/ppermute | solution.py:307
  84.5 0.7 copy-start.17
  85.2 0.8 copy-start.9
  86.0 0.7 copy-start.11
  86.7 16.8 %collective-permute-start.17 = (bf16[1024,256]{1,0:T(8,128)(2,1)}, bf16[1024,256]{1,0:T(8,128)(2,1)S(1)}, u32[]{:S(2)}, u32[]{:S(2)}) collective-permute-start(bf16[1024,256]{1,0:T(8,128)(2,1)} %constant_dynamic-update-slice_fusion), channel_id=1, source_target_pairs={{4,0},{8,4},{12,8},{16,12},{20,16},{24,20},{28,24},{5,1},{9,5},{13... | collective-permute-start | bytes 1572872 | tf_op jit(solution)/shard_map/ppermute | solution.py:296
  91.6 1.0 copy-start.14
  92.6 0.9 copy-start.16
  93.5 0.9 copy-start.18
  95.0 1.0 copy-start.5
  96.0 1.0 copy-start.10
  97.0 1.0 copy-start.12
  98.0 4.4 %copy-start.1 = (bf16[512,1024]{1,0:T(8,128)(2,1)S(1)}, bf16[512,1024]{1,0:T(8,128)(2,1)}, u32[]{:S(2)}) copy-start(bf16[512,1024]{1,0:T(8,128)(2,1)} %map_ref.3) | copy-start | bytes 3145732
  103.4 8.1 %copy-start.8 = (bf16[512,256]{1,0:T(8,128)(2,1)S(1)}, bf16[512,256]{1,0:T(8,128)(2,1)}, u32[]{:S(2)}) copy-start(bf16[512,256]{1,0:T(8,128)(2,1)} %queries_ref.7) | copy-start | bytes 786436
  103.4 1.6 %collective-permute-start.19 = (bf16[512,256]{1,0:T(8,128)(2,1)S(1)}, bf16[512,256]{1,0:T(8,128)(2,1)S(1)}, u32[]{:S(2)}, u32[]{:S(2)}) collective-permute-start(bf16[512,256]{1,0:T(8,128)(2,1)S(1)} %get-tuple-element.46), channel_id=1, source_target_pairs={{0,1},{1,0},{2,3},{3,2},{4,5},{5,4},{6,7},{7,6},{8,9},{9,8},{10,11... | collective-permute-start | bytes 786440 | tf_op jit(solution)/shard_map/ppermute | solution.py:302
  104.5 7.0 %collective-permute-start.18 = (bf16[512,256]{1,0:T(8,128)(2,1)S(1)}, bf16[512,256]{1,0:T(8,128)(2,1)S(1)}, u32[]{:S(2)}, u32[]{:S(2)}) collective-permute-start(bf16[512,256]{1,0:T(8,128)(2,1)S(1)} %get-tuple-element.44), channel_id=1, source_target_pairs={{0,1},{1,0},{2,3},{3,2},{4,5},{5,4},{6,7},{7,6},{8,9},{9,8},{10,11... | collective-permute-start | bytes 786440 | tf_op jit(solution)/shard_map/ppermute | solution.py:302
  105.1 6.4 %collective-permute-start.21 = (bf16[256,256]{1,0:T(8,128)(2,1)S(1)}, bf16[256,256]{1,0:T(8,128)(2,1)S(1)}, u32[]{:S(2)}, u32[]{:S(2)}) collective-permute-start(bf16[256,256]{1,0:T(8,128)(2,1)S(1)} %get-tuple-element.56), channel_id=1, source_target_pairs={{0,2},{1,3},{2,0},{3,1},{4,6},{5,7},{6,4},{7,5},{8,10},{9,11},{10,... | collective-permute-start | bytes 393224 | tf_op jit(solution)/shard_map/ppermute | solution.py:302
  106.6 7.4 %collective-permute-start.20 = (bf16[256,256]{1,0:T(8,128)(2,1)S(1)}, bf16[256,256]{1,0:T(8,128)(2,1)S(1)}, u32[]{:S(2)}, u32[]{:S(2)}) collective-permute-start(bf16[256,256]{1,0:T(8,128)(2,1)S(1)} %get-tuple-element.57), channel_id=1, source_target_pairs={{0,2},{1,3},{2,0},{3,1},{4,6},{5,7},{6,4},{7,5},{8,10},{9,11},{10,... | collective-permute-start | bytes 393224 | tf_op jit(solution)/shard_map/ppermute | solution.py:302

commit v14 on v13

--- a/solution.py
+++ b/solution.py
@@ -182,19 +182,6 @@
                 span(values_ref, low, count - low), span(values_ref, count, count),
                 span(values_ref, 2 * count, high),
             ).astype(BF16)
-
-
-def query_kernel(side_ref, keep_ref, other_ref, map_ref, out_ref):
-    side = side_ref[0, 0]
-    own = keep_ref[...].astype(F32)
-    other = other_ref[...].astype(F32)
-    square = jnp.sum(own * own + other * other, axis=1, keepdims=True)
-    norm = lax.rsqrt(square / (HEADS_GRP * HEAD_DIM) + 1e-05)
-    own_map = map_ref[pl.ds(pl.multiple_of(side * HEAD_DIM, HEAD_DIM), HEAD_DIM), :]
-    other_map = map_ref[pl.ds(pl.multiple_of((1 - side) * HEAD_DIM, HEAD_DIM), HEAD_DIM), :]
-    out_ref[...] = (
-        dot_nn((own * norm).astype(BF16), own_map) + dot_nn((other * norm).astype(BF16), other_map)
-    ).astype(BF16)
 
 
 def second_kernel(edge_ref, queries_ref, keep_ref, near_ref, far_ref, prev_ref, keys_ref, values_ref, next_ref,
@@ -229,10 +216,22 @@
         out_ref[rows, :] = (both * lax.rsqrt(mean + 1e-05)).astype(BF16)
 
 
-def renew_kernel(orders, place_ref, weights_ref, query_ref, *refs):
-    pieces, (own_ref, fast_ref, new_ref) = refs[:-3], refs[-3:]
+def renew_kernel(orders, place_ref, side_ref, *refs):
+    count = (len(refs) - 4) // 2
+    sources, (own_ref, fast_ref), loaded = refs[:count], refs[count:count + 2], refs[count + 2:-2]
+    new_ref, sems = refs[-2:]
+    copies = [
+        pltpu.make_async_copy(source, target, sems.at[index])
+        for index, (source, target) in enumerate(zip(sources, loaded))
+    ]
+    for copy in copies:
+        copy.start()
+    pieces, (weights_ref, keep_ref, other_ref, map_ref) = loaded[:-4], loaded[-4:]
     place = place_ref[0, 0]
+    side = side_ref[0, 0]
     hidden_size, width = weights_ref.shape[1:]
+    for copy in copies[:-4]:
+        copy.wait()
     limit_norm = math.sqrt(FAST_HIDDEN * FAST_DIM) / 2.0
     step = 64
     square = jnp.zeros((1, pieces[0].shape[1]), F32)
@@ -242,6 +241,7 @@
             square = square + jnp.sum(part * part, axis=0, keepdims=True)
     square = jnp.sum(square, axis=1, keepdims=True)
     factor = jnp.minimum(1.0, limit_norm * lax.rsqrt(square + 1e-06))
+    copies[-4].wait()
     per_chunk = len(pieces) // 2
     piece_rows = pieces[0].shape[0]
     blocks = 1 << len(orders[0])
@@ -272,10 +272,19 @@
                 new_ref[matrix, rows, :] = fresh
                 if block == 0:
                     own_ref[matrix, low:low + count, :] = fresh
-    step = 128
-    for low in range(0, query_ref.shape[0], step):
-        rows = slice(low, low + step)
-        query = query_ref[rows, :]
+    for copy in copies[-3:]:
+        copy.wait()
+    own_map = map_ref[pl.ds(pl.multiple_of(side * HEAD_DIM, HEAD_DIM), HEAD_DIM), :]
+    other_map = map_ref[pl.ds(pl.multiple_of((1 - side) * HEAD_DIM, HEAD_DIM), HEAD_DIM), :]
+    for low in range(0, keep_ref.shape[0], TILE):
+        rows = slice(low, low + TILE)
+        own = keep_ref[rows, :].astype(F32)
+        other = other_ref[rows, :].astype(F32)
+        total = jnp.sum(own * own + other * other, axis=1, keepdims=True)
+        norm = lax.rsqrt(total / (HEADS_GRP * HEAD_DIM) + 1e-05)
+        query = (
+            dot_nn((own * norm).astype(BF16), own_map) + dot_nn((other * norm).astype(BF16), other_map)
+        ).astype(BF16)
         gate = dot_nt(query, new_ref[0]) * INVERSE
         up = dot_nt(query, new_ref[1]) * INVERSE
         hidden = (jax.nn.silu(gate) * up).astype(BF16)
@@ -436,30 +445,27 @@
                 wait = (keep_first,)
             held = doubling_step(held, orders, turn, wait)
         gathered = [part for parts in held for part in parts]
-        next_second = seq_shift(after(both_second, (gathered, back_first)), -1)
+        next_second = seq_shift(after(both_second, back_first), -1)
     else:
         gathered = lax.psum(gradients, "seq")
         keep_first, back_first = first_attention(*first_halos(low_block, high_block))
         prev_second, next_second = seq_shift(both_second, 1), seq_shift(both_second, -1)
-    fast_query = call(
-        query_kernel,
-        shape((rows, fast_width), BF16),
-        (side_scalar, keep_first, back_first, input_map[0]),
-        scalars=1,
-    )
-
     own_rows = hidden_size >> len(orders[0])
     my_bit, near = head_place % 2, head_place // 2
     places = jnp.stack(
         [2 * pair + bit for pair in (near ^ 1, near) for bit in (1 - my_bit, my_bit)]
     ).astype(jnp.int32).reshape(1, 4)
     share = shape((rows, width), BF16)
+    operands = (*gathered, weights, keep_first, back_first, input_map[0])
     own_new, fast_out = call(
         functools.partial(renew_kernel, orders),
         [shape((3, own_rows, fast_width), BF16), shape((rows, fast_width), BF16)],
-        (place, weights, fast_query, *gathered),
-        scalars=1,
-        scratch=[pltpu.VMEM(weights.shape, BF16)],
+        (place, side_scalar, *operands),
+        scalars=2,
+        anywhere=len(operands),
+        scratch=[pltpu.VMEM(operand.shape, BF16) for operand in operands]
+        + [pltpu.VMEM(weights.shape, BF16), pltpu.SemaphoreType.DMA((len(operands),))],
+        limit=VMEM_MOST,
     )
 
     def mixed_for(pair, fast):

time: 118 us -> 106 us (0.90)
  the two profiles are of different devices: /device:TPU:16 before, /device:TPU:0 now
where the time goes in v14:
time: 106 us
  starting transfers between devices  50.7 us (48%)
  Pallas kernels  25.4 us (24%)
  waiting for transfers between devices  24.3 us (23%)
  local copies, waits for them, and re-layouts  2.99 us (3%)
  other arithmetic  1.52 us (1%)
    ppermute x14, starting transfers between devices, seq_swap(): lax.ppermute(value, 'seq', [(i, i ^ step) for i in range(lax.axis_size('s...  38.6 us
    ppermute x14, waiting for transfers between devices, seq_swap(): lax.ppermute(value, 'seq', [(i, i ^ step) for i in range(lax.axis_size('s...  19.9 us
    pallas_call x8, Pallas kernels, call(): pl.pallas_call(body, out_shape=out_shapes, in_specs=in_specs, out_specs=j...  18.6 us
    ppermute x4, starting transfers between devices, seq_shift(): lax.ppermute(value, 'seq', [(i, i + step) for i in range(peers) if 0 <= i...  9.33 us
    pallas_call x1, Pallas kernels, local(): pl.pallas_call(functools.partial(gradient_kernel, orders), grid=(hidden_s...  6.84 us
    ppermute x4, waiting for transfers between devices, head_swap(): lax.ppermute(value, 'head', [(i, i ^ bit) for i in range(lax.axis_size('h...  4.32 us
    ppermute x4, starting transfers between devices, head_swap(): lax.ppermute(value, 'head', [(i, i ^ bit) for i in range(lax.axis_size('h...  2.71 us
    unnamed x31, local copies, waits for them, and re-layouts  2.19 us
  transfers between devices with their start and end apart: 22, of which 9 were waited for; matrix products, arithmetic and copies ran while one was open for 3% of the time, Pallas kernels for 15%

profile of v14, /device:TPU:0, one launch (start us, length us, event | category | flops | bytes accessed | tf_op | source)
XLA Modules:
  0.0 105.8 jit_solution(6919929662674967845)
XLA Ops:
  0.7 6.8 %shard_map.131 = (bf16[256,768]{1,0:T(8,128)(2,1)}, bf16[256,768]{1,0:T(8,128)(2,1)}, bf16[256,768]{1,0:T(8,128)(2,1)}, bf16[256,768]{1,0:T(8,128)(2,1)}) custom-call(s32[1,1]{1,0:T(1,128)} %bitcast.9.place_ref, f32[1,512]{1,0:T(1,128)} %bitcast.23, bf16[512,512]{1,0:T(8,128)(2,1)} %keys_ref.5, bf16[512,512]{1,0:T(8,128)(2,1)} %values_ref.5, ...), custom_call_target="tpu_custom_call" | custom-call | flops 1000 | bytes 1000 | tf_op jit(solution)/shard_map/pallas_call | solution.py:390
  7.5 3.0 %collective-permute-start = (bf16[256,768]{1,0:T(8,128)(2,1)}, bf16[256,768]{1,0:T(8,128)(2,1)S(1)}, u32[]{:S(2)}, u32[]{:S(2)}) collective-permute-start(bf16[256,768]{1,0:T(8,128)(2,1)} %get-tuple-element.26), channel_id=1, source_target_pairs={{0,4},{4,0},{8,12},{12,8},{16,20},{20,16},{24,28},{28,24},{1,5},{5... | collective-permute-start | bytes 1179656 | tf_op jit(solution)/shard_map/ppermute | solution.py:316
  10.5 0.1 shard_map.132
  10.6 0.1 collective-permute-start.8
  10.7 2.0 %collective-permute-start.4 = (bf16[256,768]{1,0:T(8,128)(2,1)}, bf16[256,768]{1,0:T(8,128)(2,1)S(1)}, u32[]{:S(2)}, u32[]{:S(2)}) collective-permute-start(bf16[256,768]{1,0:T(8,128)(2,1)} %get-tuple-element.28), channel_id=1, source_target_pairs={{0,8},{4,12},{8,0},{12,4},{16,24},{20,28},{24,16},{28,20},{1,9},{5... | collective-permute-start | bytes 1179656 | tf_op jit(solution)/shard_map/ppermute | solution.py:316
  12.7 0.7 constant_dynamic-update-slice_fusion.1
  13.5 0.7 constant_dynamic-update-slice_fusion
  14.2 6.4 %collective-permute-done = bf16[256,768]{1,0:T(8,128)(2,1)S(1)} collective-permute-done((bf16[256,768]{1,0:T(8,128)(2,1)}, bf16[256,768]{1,0:T(8,128)(2,1)S(1)}, u32[]{:S(2)}, u32[]{:S(2)}) %collective-permute-start) | collective-permute-done | bytes 393248 | tf_op jit(solution)/shard_map/ppermute | solution.py:316
  20.6 0.1 add_convert_fusion.1
  20.7 2.2 %collective-permute-start.1 = (bf16[128,768]{1,0:T(8,128)(2,1)S(1)}, bf16[128,768]{1,0:T(8,128)(2,1)S(1)}, u32[]{:S(2)}, u32[]{:S(2)}) collective-permute-start(bf16[128,768]{1,0:T(8,128)(2,1)S(1)} %get-tuple-element.50), channel_id=1, source_target_pairs={{0,8},{4,12},{8,0},{12,4},{16,24},{20,28},{24,16},{28,20},{1,9},{5... | collective-permute-start | bytes 589832 | tf_op jit(solution)/shard_map/ppermute | solution.py:316
  22.9 0.1 add_convert_fusion
  23.0 2.6 %collective-permute-start.5 = (bf16[128,768]{1,0:T(8,128)(2,1)S(1)}, bf16[128,768]{1,0:T(8,128)(2,1)S(1)}, u32[]{:S(2)}, u32[]{:S(2)}) collective-permute-start(bf16[128,768]{1,0:T(8,128)(2,1)S(1)} %get-tuple-element.48), channel_id=1, source_target_pairs={{0,16},{4,20},{8,24},{12,28},{16,0},{20,4},{24,8},{28,12},{1,17},{... | collective-permute-start | bytes 589832 | tf_op jit(solution)/shard_map/ppermute | solution.py:316
  25.7 2.6 %collective-permute-done.8.other_ref = bf16[1536,128]{1,0:T(8,128)(2,1)S(1)} collective-permute-done((bf16[1536,128]{1,0:T(8,128)(2,1)S(1)}, bf16[1536,128]{1,0:T(8,128)(2,1)S(1)}, u32[]{:S(2)}, u32[]{:S(2)}) %collective-permute-start.8) | collective-permute-done | bytes 393248 | tf_op jit(solution)/shard_map/ppermute | solution.py:316
  28.3 0.8 collective-permute-done.1
  29.1 2.1 %collective-permute-start.2 = (bf16[64,768]{1,0:T(8,128)(2,1)S(1)}, bf16[64,768]{1,0:T(8,128)(2,1)S(1)}, u32[]{:S(2)}, u32[]{:S(2)}) collective-permute-start(bf16[64,768]{1,0:T(8,128)(2,1)S(1)} %get-tuple-element.54), channel_id=1, source_target_pairs={{0,16},{4,20},{8,24},{12,28},{16,0},{20,4},{24,8},{28,12},{1,17},{... | collective-permute-start | bytes 294920 | tf_op jit(solution)/shard_map/ppermute | solution.py:316
  31.2 2.4 %collective-permute-done.5 = bf16[128,768]{1,0:T(8,128)(2,1)S(1)} collective-permute-done((bf16[128,768]{1,0:T(8,128)(2,1)S(1)}, bf16[128,768]{1,0:T(8,128)(2,1)S(1)}, u32[]{:S(2)}, u32[]{:S(2)}) %collective-permute-start.5) | collective-permute-done | bytes 196640 | tf_op jit(solution)/shard_map/ppermute | solution.py:316
  33.7 1.6 %collective-permute-start.6 = (bf16[64,768]{1,0:T(8,128)(2,1)S(1)}, bf16[64,768]{1,0:T(8,128)(2,1)S(1)}, u32[]{:S(2)}, u32[]{:S(2)}) collective-permute-start(bf16[64,768]{1,0:T(8,128)(2,1)S(1)} %get-tuple-element.52), channel_id=1, source_target_pairs={{0,4},{4,0},{8,12},{12,8},{16,20},{20,16},{24,28},{28,24},{1,5},{5... | collective-permute-start | bytes 294920 | tf_op jit(solution)/shard_map/ppermute | solution.py:316
  35.3 4.1 %collective-permute-start.9 = (bf16[1024,128]{1,0:T(8,128)(2,1)S(1)}, bf16[1024,128]{1,0:T(8,128)(2,1)S(1)}, u32[]{:S(2)}, u32[]{:S(2)}) collective-permute-start(bf16[1024,128]{1,0:T(8,128)(2,1)S(1)} %get-tuple-element.31.high_ref), channel_id=1, source_target_pairs={{0,8},{4,12},{8,16},{12,20},{16,24},{20,28},{1,9},{5,13},{9,17},{1... | collective-permute-start | bytes 786440 | tf_op jit(solution)/shard_map/ppermute | solution.py:305
  39.5 1.3 %collective-permute-start.10 = (bf16[1024,128]{1,0:T(8,128)(2,1)S(1)}, bf16[1024,128]{1,0:T(8,128)(2,1)S(1)}, u32[]{:S(2)}, u32[]{:S(2)}) collective-permute-start(bf16[1024,128]{1,0:T(8,128)(2,1)S(1)} %get-tuple-element.32.low_ref), channel_id=1, source_target_pairs={{8,0},{12,4},{16,8},{20,12},{24,16},{28,20},{9,1},{13,5},{17,9},{2... | collective-permute-start | bytes 786440 | tf_op jit(solution)/shard_map/ppermute | solution.py:305
  40.8 2.4 %collective-permute-start.11 = (bf16[1024,256]{1,0:T(8,128)(2,1)}, bf16[1024,256]{1,0:T(8,128)(2,1)S(1)}, u32[]{:S(2)}, u32[]{:S(2)}) collective-permute-start(bf16[1024,256]{1,0:T(8,128)(2,1)} %constant_dynamic-update-slice_fusion), channel_id=1, source_target_pairs={{0,4},{4,8},{8,12},{12,16},{16,20},{20,24},{24,28},{1,5},{5,9},{9,... | collective-permute-start | bytes 1572872 | tf_op jit(solution)/shard_map/ppermute | solution.py:305
  43.3 4.0 %collective-permute-start.3 = (bf16[64,768]{1,0:T(8,128)(2,1)S(1)}, bf16[64,768]{1,0:T(8,128)(2,1)S(1)}, u32[]{:S(2)}, u32[]{:S(2)}) collective-permute-start(bf16[64,768]{1,0:T(8,128)(2,1)S(1)} %add_convert_fusion.5), channel_id=1, source_target_pairs={{0,16},{4,20},{8,24},{12,28},{16,0},{20,4},{24,8},{28,12},{1,17},{... | collective-permute-start | bytes 294920 | tf_op jit(solution)/shard_map/ppermute | solution.py:316
  47.3 3.1 %collective-permute-start.7 = (bf16[64,768]{1,0:T(8,128)(2,1)S(1)}, bf16[64,768]{1,0:T(8,128)(2,1)S(1)}, u32[]{:S(2)}, u32[]{:S(2)}) collective-permute-start(bf16[64,768]{1,0:T(8,128)(2,1)S(1)} %add_convert_fusion.4), channel_id=1, source_target_pairs={{0,4},{4,0},{8,12},{12,8},{16,20},{20,16},{24,28},{28,24},{1,5},{5... | collective-permute-start | bytes 294920 | tf_op jit(solution)/shard_map/ppermute | solution.py:316
  50.4 2.6 %collective-permute-done.7 = bf16[64,768]{1,0:T(8,128)(2,1)S(1)} collective-permute-done((bf16[64,768]{1,0:T(8,128)(2,1)S(1)}, bf16[64,768]{1,0:T(8,128)(2,1)S(1)}, u32[]{:S(2)}, u32[]{:S(2)}) %collective-permute-start.7) | collective-permute-done | bytes 98336 | tf_op jit(solution)/shard_map/ppermute | solution.py:316
  53.0 7.5 %collective-permute-start.12 = (bf16[128,768]{1,0:T(8,128)(2,1)S(1)}, bf16[128,768]{1,0:T(8,128)(2,1)}, u32[]{:S(2)}, u32[]{:S(2)}) collective-permute-start(bf16[128,768]{1,0:T(8,128)(2,1)S(1)} %pad_maximum_fusion.2), channel_id=1, source_target_pairs={{0,8},{4,12},{8,0},{12,4},{16,24},{20,28},{24,16},{28,20},{1,9},{5... | collective-permute-start | bytes 589832 | tf_op jit(solution)/shard_map/ppermute | solution.py:316
  60.6 0.1 pad_maximum_fusion.4
  60.6 0.1 reshape.19.edge_ref
  60.7 5.3 %collective-permute-start.13 = (bf16[128,768]{1,0:T(8,128)(2,1)S(1)}, bf16[128,768]{1,0:T(8,128)(2,1)S(1)}, u32[]{:S(2)}, u32[]{:S(2)}) collective-permute-start(bf16[128,768]{1,0:T(8,128)(2,1)S(1)} %pad_maximum_fusion.3), channel_id=1, source_target_pairs={{0,16},{4,20},{8,24},{12,28},{16,0},{20,4},{24,8},{28,12},{1,17},{... | collective-permute-start | bytes 589832 | tf_op jit(solution)/shard_map/ppermute | solution.py:316
  66.0 4.0 %shard_map.134 = (bf16[512,128]{1,0:T(8,128)(2,1)S(1)}, bf16[512,128]{1,0:T(8,128)(2,1)S(1)}) custom-call(f32[2,2]{1,0:T(2,128)S(1)} %reshape.19.edge_ref, s32[1,1]{1,0:T(1,128)} %bitcast.10.side_ref, bf16[512,256]{1,0:T(8,128)(2,1)S(1)} %copy-done.7, bf16[1536,128]{1,0:T(8,128)(2,1)S(1)} %collective-permute-done.8.other_ref, ...), custom_call_target="tpu_custom_call" | custom-call | flops 805306368 | bytes 2097152 | tf_op jit(solution)/shard_map/pallas_call | solution.py:41
  70.0 0.1 collective-permute-start.16
  70.1 1.0 pad_maximum_fusion.refs_0_
  71.1 2.1 %collective-permute-start.14 = (bf16[256,768]{1,0:T(8,128)(2,1)S(1)}, bf16[256,768]{1,0:T(8,128)(2,1)S(1)}, u32[]{:S(2)}, u32[]{:S(2)}) collective-permute-start(bf16[256,768]{1,0:T(8,128)(2,1)S(1)} %pad_maximum_fusion.refs_0_), channel_id=1, source_target_pairs={{0,4},{4,0},{8,12},{12,8},{16,20},{20,16},{24,28},{28,24},{1,5},{5... | collective-permute-start | bytes 1179656 | tf_op jit(solution)/shard_map/ppermute | solution.py:316
  73.2 2.9 %collective-permute-start.15 = (bf16[256,768]{1,0:T(8,128)(2,1)S(1)}, bf16[256,768]{1,0:T(8,128)(2,1)}, u32[]{:S(2)}, u32[]{:S(2)}) collective-permute-start(bf16[256,768]{1,0:T(8,128)(2,1)S(1)} %pad_maximum_fusion.1.refs_2_), channel_id=1, source_target_pairs={{0,8},{4,12},{8,0},{12,4},{16,24},{20,28},{24,16},{28,20},{1,9},{5... | collective-permute-start | bytes 1179656 | tf_op jit(solution)/shard_map/ppermute | solution.py:316
  76.1 1.9 %collective-permute-done.16.refs_6_ = bf16[512,128]{1,0:T(8,128)(2,1)S(1)} collective-permute-done((bf16[512,128]{1,0:T(8,128)(2,1)S(1)}, bf16[512,128]{1,0:T(8,128)(2,1)S(1)}, u32[]{:S(2)}, u32[]{:S(2)}) %collective-permute-start.16) | collective-permute-done | bytes 131104 | tf_op jit(solution)/shard_map/ppermute | solution.py:316
  78.0 1.5 %collective-permute-start.17 = (bf16[1024,256]{1,0:T(8,128)(2,1)}, bf16[1024,256]{1,0:T(8,128)(2,1)S(1)}, u32[]{:S(2)}, u32[]{:S(2)}) collective-permute-start(bf16[1024,256]{1,0:T(8,128)(2,1)} %constant_dynamic-update-slice_fusion), channel_id=1, source_target_pairs={{4,0},{8,4},{12,8},{16,12},{20,16},{24,20},{28,24},{5,1},{9,5},{13... | collective-permute-start | bytes 1572872 | tf_op jit(solution)/shard_map/ppermute | solution.py:305
  79.5 0.1 add_bitcast_fusion.places_ref
  79.5 2.9 %collective-permute-done.14.refs_1_ = bf16[256,768]{1,0:T(8,128)(2,1)S(1)} collective-permute-done((bf16[256,768]{1,0:T(8,128)(2,1)S(1)}, bf16[256,768]{1,0:T(8,128)(2,1)S(1)}, u32[]{:S(2)}, u32[]{:S(2)}) %collective-permute-start.14) | collective-permute-done | bytes 393248 | tf_op jit(solution)/shard_map/ppermute | solution.py:316
  82.4 0.4 collective-permute-done.15.refs_3_
  82.8 0.4 copy-done.13
  83.2 6.9 %shard_map.135 = (bf16[3,64,512]{2,1,0:T(8,128)(2,1)}, bf16[512,512]{1,0:T(8,128)(2,1)}) custom-call(s32[1,1]{1,0:T(1,128)} %bitcast.9.place_ref, s32[1,1]{1,0:T(1,128)} %bitcast.10.side_ref, bf16[256,768]{1,0:T(8,128)(2,1)} %copy-done.9, bf16[256,768]{1,0:T(8,128)(2,1)} %copy-done.13, bf16[256,768]{1,0:T(8,128)(2,1)} %copy-done.10, ...), custom_call_target="tpu_custom_call" | custom-call | flops 1000 | bytes 1000 | tf_op jit(solution)/shard_map/pallas_call | solution.py:41
  90.1 1.0 copy-done.3
  91.1 1.0 shard_map.137
  92.2 1.0 shard_map.136
  93.2 0.6 collective-permute-start.18
  93.9 1.5 %collective-permute-start.21 = (bf16[256,256]{1,0:T(8,128)(2,1)S(1)}, bf16[256,256]{1,0:T(8,128)(2,1)S(1)}, u32[]{:S(2)}, u32[]{:S(2)}) collective-permute-start(bf16[256,256]{1,0:T(8,128)(2,1)S(1)} %get-tuple-element.56), channel_id=1, source_target_pairs={{0,2},{1,3},{2,0},{3,1},{4,6},{5,7},{6,4},{7,5},{8,10},{9,11},{10,... | collective-permute-start | bytes 393224 | tf_op jit(solution)/shard_map/ppermute | solution.py:311
  95.4 0.5 collective-permute-start.20
  96.0 4.3 %collective-permute-done.21.far_ref = bf16[256,256]{1,0:T(8,128)(2,1)S(1)} collective-permute-done((bf16[256,256]{1,0:T(8,128)(2,1)S(1)}, bf16[256,256]{1,0:T(8,128)(2,1)S(1)}, u32[]{:S(2)}, u32[]{:S(2)}) %collective-permute-start.21) | collective-permute-done | bytes 131104 | tf_op jit(solution)/shard_map/ppermute | solution.py:311
  100.3 2.4 %shard_map.138.refs_0_ = bf16[256,256]{1,0:T(8,128)(2,1)S(1)} custom-call(f32[2,2]{1,0:T(2,128)S(1)} %reshape.19.edge_ref, bf16[512,256]{1,0:T(8,128)(2,1)S(1)} %copy-done.6, bf16[512,256]{1,0:T(8,128)(2,1)S(1)} %get-tuple-element.43.keep_ref, bf16[512,256]{1,0:T(8,128)(2,1)S(1)} %collective-permute-done.18.near_ref, ...), custom_call_target="tpu_custom_call" | custom-call | flops 402653184 | bytes 2097152 | tf_op jit(solution)/shard_map/pallas_call | solution.py:41
  102.7 3.1 %shard_map.139 = bf16[512,256]{1,0:T(8,128)(2,1)} custom-call(f32[2,2]{1,0:T(2,128)S(1)} %reshape.19.edge_ref, bf16[512,256]{1,0:T(8,128)(2,1)S(1)} %copy-done.6, bf16[512,256]{1,0:T(8,128)(2,1)S(1)} %get-tuple-element.43.keep_ref, bf16[512,256]{1,0:T(8,128)(2,1)S(1)} %collective-permute-done.18.near_ref, ...), custom_call_target="tpu_custom_call" | custom-call | flops 402653184 | bytes 2097152 | tf_op jit(solution)/shard_map/pallas_call | solution.py:41
  (51 shorter events, 0.5 us)
Async XLA Ops:
  0.6 9.9 %copy-start.5 = (bf16[512,256]{1,0:T(8,128)(2,1)S(1)}, bf16[512,256]{1,0:T(8,128)(2,1)}, u32[]{:S(2)}) copy-start(bf16[512,256]{1,0:T(8,128)(2,1)} %values_ref.7) | copy-start | bytes 786436
  0.6 9.9 %copy-start.4 = (bf16[512,256]{1,0:T(8,128)(2,1)S(1)}, bf16[512,256]{1,0:T(8,128)(2,1)}, u32[]{:S(2)}) copy-start(bf16[512,256]{1,0:T(8,128)(2,1)} %keys_ref.7) | copy-start | bytes 786436
  0.7 9.8 %copy-start.7 = (bf16[512,256]{1,0:T(8,128)(2,1)S(1)}, bf16[512,256]{1,0:T(8,128)(2,1)}, u32[]{:S(2)}) copy-start(bf16[512,256]{1,0:T(8,128)(2,1)} %queries_ref.5) | copy-start | bytes 786436
  0.7 12.1 %copy-start.1 = (bf16[512,256]{1,0:T(8,128)(2,1)S(1)}, bf16[512,256]{1,0:T(8,128)(2,1)}, u32[]{:S(2)}) copy-start(bf16[512,256]{1,0:T(8,128)(2,1)} %keys_ref.9) | copy-start | bytes 786436
  0.7 12.8 %copy-start.2 = (bf16[512,256]{1,0:T(8,128)(2,1)S(1)}, bf16[512,256]{1,0:T(8,128)(2,1)}, u32[]{:S(2)}) copy-start(bf16[512,256]{1,0:T(8,128)(2,1)} %values_ref.9) | copy-start | bytes 786436
  7.5 13.1 %copy-start.12 = (bf16[256,768]{1,0:T(8,128)(2,1)S(1)}, bf16[256,768]{1,0:T(8,128)(2,1)}, u32[]{:S(2)}) copy-start(bf16[256,768]{1,0:T(8,128)(2,1)} %get-tuple-element.25) | copy-start | bytes 1179652
  7.5 13.1 %collective-permute-start = (bf16[256,768]{1,0:T(8,128)(2,1)}, bf16[256,768]{1,0:T(8,128)(2,1)S(1)}, u32[]{:S(2)}, u32[]{:S(2)}) collective-permute-start(bf16[256,768]{1,0:T(8,128)(2,1)} %get-tuple-element.26), channel_id=1, source_target_pairs={{0,4},{4,0},{8,12},{12,8},{16,20},{20,16},{24,28},{28,24},{1,5},{5... | collective-permute-start | bytes 1179656 | tf_op jit(solution)/shard_map/ppermute | solution.py:316
  10.5 12.4 %copy-start.11 = (bf16[256,768]{1,0:T(8,128)(2,1)S(1)}, bf16[256,768]{1,0:T(8,128)(2,1)}, u32[]{:S(2)}) copy-start(bf16[256,768]{1,0:T(8,128)(2,1)} %get-tuple-element.27) | copy-start | bytes 1179652
  10.6 17.7 %collective-permute-start.8 = (bf16[1536,128]{1,0:T(8,128)(2,1)S(1)}, bf16[1536,128]{1,0:T(8,128)(2,1)S(1)}, u32[]{:S(2)}, u32[]{:S(2)}) collective-permute-start(bf16[1536,128]{1,0:T(8,128)(2,1)S(1)} %shard_map.132), channel_id=1, source_target_pairs={{0,4},{4,0},{8,12},{12,8},{16,20},{20,16},{24,28},{28,24},{1,5},{5... | collective-permute-start | bytes 1179656 | tf_op jit(solution)/shard_map/ppermute | solution.py:316
  10.7 12.2 %collective-permute-start.4 = (bf16[256,768]{1,0:T(8,128)(2,1)}, bf16[256,768]{1,0:T(8,128)(2,1)S(1)}, u32[]{:S(2)}, u32[]{:S(2)}) collective-permute-start(bf16[256,768]{1,0:T(8,128)(2,1)} %get-tuple-element.28), channel_id=1, source_target_pairs={{0,8},{4,12},{8,0},{12,4},{16,24},{20,28},{24,16},{28,20},{1,9},{5... | collective-permute-start | bytes 1179656 | tf_op jit(solution)/shard_map/ppermute | solution.py:316
  20.7 8.3 %collective-permute-start.1 = (bf16[128,768]{1,0:T(8,128)(2,1)S(1)}, bf16[128,768]{1,0:T(8,128)(2,1)S(1)}, u32[]{:S(2)}, u32[]{:S(2)}) collective-permute-start(bf16[128,768]{1,0:T(8,128)(2,1)S(1)} %get-tuple-element.50), channel_id=1, source_target_pairs={{0,8},{4,12},{8,0},{12,4},{16,24},{20,28},{24,16},{28,20},{1,9},{5... | collective-permute-start | bytes 589832 | tf_op jit(solution)/shard_map/ppermute | solution.py:316
  23.0 10.7 %collective-permute-start.5 = (bf16[128,768]{1,0:T(8,128)(2,1)S(1)}, bf16[128,768]{1,0:T(8,128)(2,1)S(1)}, u32[]{:S(2)}, u32[]{:S(2)}) collective-permute-start(bf16[128,768]{1,0:T(8,128)(2,1)S(1)} %get-tuple-element.48), channel_id=1, source_target_pairs={{0,16},{4,20},{8,24},{12,28},{16,0},{20,4},{24,8},{28,12},{1,17},{... | collective-permute-start | bytes 589832 | tf_op jit(solution)/shard_map/ppermute | solution.py:316
  29.1 14.1 %collective-permute-start.2 = (bf16[64,768]{1,0:T(8,128)(2,1)S(1)}, bf16[64,768]{1,0:T(8,128)(2,1)S(1)}, u32[]{:S(2)}, u32[]{:S(2)}) collective-permute-start(bf16[64,768]{1,0:T(8,128)(2,1)S(1)} %get-tuple-element.54), channel_id=1, source_target_pairs={{0,16},{4,20},{8,24},{12,28},{16,0},{20,4},{24,8},{28,12},{1,17},{... | collective-permute-start | bytes 294920 | tf_op jit(solution)/shard_map/ppermute | solution.py:316
  33.7 13.6 %collective-permute-start.6 = (bf16[64,768]{1,0:T(8,128)(2,1)S(1)}, bf16[64,768]{1,0:T(8,128)(2,1)S(1)}, u32[]{:S(2)}, u32[]{:S(2)}) collective-permute-start(bf16[64,768]{1,0:T(8,128)(2,1)S(1)} %get-tuple-element.52), channel_id=1, source_target_pairs={{0,4},{4,0},{8,12},{12,8},{16,20},{20,16},{24,28},{28,24},{1,5},{5... | collective-permute-start | bytes 294920 | tf_op jit(solution)/shard_map/ppermute | solution.py:316
  35.3 17.7 %collective-permute-start.9 = (bf16[1024,128]{1,0:T(8,128)(2,1)S(1)}, bf16[1024,128]{1,0:T(8,128)(2,1)S(1)}, u32[]{:S(2)}, u32[]{:S(2)}) collective-permute-start(bf16[1024,128]{1,0:T(8,128)(2,1)S(1)} %get-tuple-element.31.high_ref), channel_id=1, source_target_pairs={{0,8},{4,12},{8,16},{12,20},{16,24},{20,28},{1,9},{5,13},{9,17},{1... | collective-permute-start | bytes 786440 | tf_op jit(solution)/shard_map/ppermute | solution.py:305
  39.5 13.5 %collective-permute-start.10 = (bf16[1024,128]{1,0:T(8,128)(2,1)S(1)}, bf16[1024,128]{1,0:T(8,128)(2,1)S(1)}, u32[]{:S(2)}, u32[]{:S(2)}) collective-permute-start(bf16[1024,128]{1,0:T(8,128)(2,1)S(1)} %get-tuple-element.32.low_ref), channel_id=1, source_target_pairs={{8,0},{12,4},{16,8},{20,12},{24,16},{28,20},{9,1},{13,5},{17,9},{2... | collective-permute-start | bytes 786440 | tf_op jit(solution)/shard_map/ppermute | solution.py:305
  40.8 12.2 %collective-permute-start.11 = (bf16[1024,256]{1,0:T(8,128)(2,1)}, bf16[1024,256]{1,0:T(8,128)(2,1)S(1)}, u32[]{:S(2)}, u32[]{:S(2)}) collective-permute-start(bf16[1024,256]{1,0:T(8,128)(2,1)} %constant_dynamic-update-slice_fusion), channel_id=1, source_target_pairs={{0,4},{4,8},{8,12},{12,16},{16,20},{20,24},{24,28},{1,5},{5,9},{9,... | collective-permute-start | bytes 1572872 | tf_op jit(solution)/shard_map/ppermute | solution.py:305
  43.3 7.1 %collective-permute-start.3 = (bf16[64,768]{1,0:T(8,128)(2,1)S(1)}, bf16[64,768]{1,0:T(8,128)(2,1)S(1)}, u32[]{:S(2)}, u32[]{:S(2)}) collective-permute-start(bf16[64,768]{1,0:T(8,128)(2,1)S(1)} %add_convert_fusion.5), channel_id=1, source_target_pairs={{0,16},{4,20},{8,24},{12,28},{16,0},{20,4},{24,8},{28,12},{1,17},{... | collective-permute-start | bytes 294920 | tf_op jit(solution)/shard_map/ppermute | solution.py:316
  47.3 5.7 %collective-permute-start.7 = (bf16[64,768]{1,0:T(8,128)(2,1)S(1)}, bf16[64,768]{1,0:T(8,128)(2,1)S(1)}, u32[]{:S(2)}, u32[]{:S(2)}) collective-permute-start(bf16[64,768]{1,0:T(8,128)(2,1)S(1)} %add_convert_fusion.4), channel_id=1, source_target_pairs={{0,4},{4,0},{8,12},{12,8},{16,20},{20,16},{24,28},{28,24},{1,5},{5... | collective-permute-start | bytes 294920 | tf_op jit(solution)/shard_map/ppermute | solution.py:316
  53.0 17.1 %collective-permute-start.12 = (bf16[128,768]{1,0:T(8,128)(2,1)S(1)}, bf16[128,768]{1,0:T(8,128)(2,1)}, u32[]{:S(2)}, u32[]{:S(2)}) collective-permute-start(bf16[128,768]{1,0:T(8,128)(2,1)S(1)} %pad_maximum_fusion.2), channel_id=1, source_target_pairs={{0,8},{4,12},{8,0},{12,4},{16,24},{20,28},{24,16},{28,20},{1,9},{5... | collective-permute-start | bytes 589832 | tf_op jit(solution)/shard_map/ppermute | solution.py:316
  60.7 10.3 %collective-permute-start.13 = (bf16[128,768]{1,0:T(8,128)(2,1)S(1)}, bf16[128,768]{1,0:T(8,128)(2,1)S(1)}, u32[]{:S(2)}, u32[]{:S(2)}) collective-permute-start(bf16[128,768]{1,0:T(8,128)(2,1)S(1)} %pad_maximum_fusion.3), channel_id=1, source_target_pairs={{0,16},{4,20},{8,24},{12,28},{16,0},{20,4},{24,8},{28,12},{1,17},{... | collective-permute-start | bytes 589832 | tf_op jit(solution)/shard_map/ppermute | solution.py:316
  70.0 6.1 %copy-start.8 = (bf16[512,128]{1,0:T(8,128)(2,1)}, bf16[512,128]{1,0:T(8,128)(2,1)S(1)}, u32[]{:S(2)}) copy-start(bf16[512,128]{1,0:T(8,128)(2,1)S(1)} %get-tuple-element.36.refs_5_) | copy-start | bytes 393220
  70.0 8.0 %collective-permute-start.16 = (bf16[512,128]{1,0:T(8,128)(2,1)S(1)}, bf16[512,128]{1,0:T(8,128)(2,1)S(1)}, u32[]{:S(2)}, u32[]{:S(2)}) collective-permute-start(bf16[512,128]{1,0:T(8,128)(2,1)S(1)} %get-tuple-element.39), channel_id=1, source_target_pairs={{0,4},{4,0},{8,12},{12,8},{16,20},{20,16},{24,28},{28,24},{1,5},{5... | collective-permute-start | bytes 393224 | tf_op jit(solution)/shard_map/ppermute | solution.py:316
  71.0 11.7 %copy-start.9 = (bf16[256,768]{1,0:T(8,128)(2,1)}, bf16[256,768]{1,0:T(8,128)(2,1)S(1)}, u32[]{:S(2)}) copy-start(bf16[256,768]{1,0:T(8,128)(2,1)S(1)} %pad_maximum_fusion.refs_0_) | copy-start | bytes 1179652
  71.1 11.7 %copy-start.10 = (bf16[256,768]{1,0:T(8,128)(2,1)}, bf16[256,768]{1,0:T(8,128)(2,1)S(1)}, u32[]{:S(2)}) copy-start(bf16[256,768]{1,0:T(8,128)(2,1)S(1)} %pad_maximum_fusion.1.refs_2_) | copy-start | bytes 1179652
  71.1 11.3 %collective-permute-start.14 = (bf16[256,768]{1,0:T(8,128)(2,1)S(1)}, bf16[256,768]{1,0:T(8,128)(2,1)S(1)}, u32[]{:S(2)}, u32[]{:S(2)}) collective-permute-start(bf16[256,768]{1,0:T(8,128)(2,1)S(1)} %pad_maximum_fusion.refs_0_), channel_id=1, source_target_pairs={{0,4},{4,0},{8,12},{12,8},{16,20},{20,16},{24,28},{28,24},{1,5},{5... | collective-permute-start | bytes 1179656 | tf_op jit(solution)/shard_map/ppermute | solution.py:316
  73.2 9.6 %collective-permute-start.15 = (bf16[256,768]{1,0:T(8,128)(2,1)S(1)}, bf16[256,768]{1,0:T(8,128)(2,1)}, u32[]{:S(2)}, u32[]{:S(2)}) collective-permute-start(bf16[256,768]{1,0:T(8,128)(2,1)S(1)} %pad_maximum_fusion.1.refs_2_), channel_id=1, source_target_pairs={{0,8},{4,12},{8,0},{12,4},{16,24},{20,28},{24,16},{28,20},{1,9},{5... | collective-permute-start | bytes 1179656 | tf_op jit(solution)/shard_map/ppermute | solution.py:316
  78.0 4.8 %copy-start.14 = (bf16[512,128]{1,0:T(8,128)(2,1)}, bf16[512,128]{1,0:T(8,128)(2,1)S(1)}, u32[]{:S(2)}) copy-start(bf16[512,128]{1,0:T(8,128)(2,1)S(1)} %collective-permute-done.16.refs_6_) | copy-start | bytes 393220
  78.0 14.3 %collective-permute-start.17 = (bf16[1024,256]{1,0:T(8,128)(2,1)}, bf16[1024,256]{1,0:T(8,128)(2,1)S(1)}, u32[]{:S(2)}, u32[]{:S(2)}) collective-permute-start(bf16[1024,256]{1,0:T(8,128)(2,1)} %constant_dynamic-update-slice_fusion), channel_id=1, source_target_pairs={{4,0},{8,4},{12,8},{16,12},{20,16},{24,20},{28,24},{5,1},{9,5},{13... | collective-permute-start | bytes 1572872 | tf_op jit(solution)/shard_map/ppermute | solution.py:305
  82.4 0.8 copy-start.13
  83.2 6.9 %copy-start = (bf16[512,1024]{1,0:T(8,128)(2,1)S(1)}, bf16[512,1024]{1,0:T(8,128)(2,1)}, u32[]{:S(2)}) copy-start(bf16[512,1024]{1,0:T(8,128)(2,1)} %map_ref.3) | copy-start | bytes 3145732
  90.1 1.0 copy-start.3
  92.1 8.1 %copy-start.6 = (bf16[512,256]{1,0:T(8,128)(2,1)S(1)}, bf16[512,256]{1,0:T(8,128)(2,1)}, u32[]{:S(2)}) copy-start(bf16[512,256]{1,0:T(8,128)(2,1)} %queries_ref.7) | copy-start | bytes 786436
  92.2 1.6 %collective-permute-start.19 = (bf16[512,256]{1,0:T(8,128)(2,1)S(1)}, bf16[512,256]{1,0:T(8,128)(2,1)S(1)}, u32[]{:S(2)}, u32[]{:S(2)}) collective-permute-start(bf16[512,256]{1,0:T(8,128)(2,1)S(1)} %get-tuple-element.46), channel_id=1, source_target_pairs={{0,1},{1,0},{2,3},{3,2},{4,5},{5,4},{6,7},{7,6},{8,9},{9,8},{10,11... | collective-permute-start | bytes 786440 | tf_op jit(solution)/shard_map/ppermute | solution.py:311
  93.2 2.7 %collective-permute-start.18 = (bf16[512,256]{1,0:T(8,128)(2,1)S(1)}, bf16[512,256]{1,0:T(8,128)(2,1)S(1)}, u32[]{:S(2)}, u32[]{:S(2)}) collective-permute-start(bf16[512,256]{1,0:T(8,128)(2,1)S(1)} %get-tuple-element.44), channel_id=1, source_target_pairs={{0,1},{1,0},{2,3},{3,2},{4,5},{5,4},{6,7},{7,6},{8,9},{9,8},{10,11... | collective-permute-start | bytes 786440 | tf_op jit(solution)/shard_map/ppermute | solution.py:311
  93.9 6.4 %collective-permute-start.21 = (bf16[256,256]{1,0:T(8,128)(2,1)S(1)}, bf16[256,256]{1,0:T(8,128)(2,1)S(1)}, u32[]{:S(2)}, u32[]{:S(2)}) collective-permute-start(bf16[256,256]{1,0:T(8,128)(2,1)S(1)} %get-tuple-element.56), channel_id=1, source_target_pairs={{0,2},{1,3},{2,0},{3,1},{4,6},{5,7},{6,4},{7,5},{8,10},{9,11},{10,... | collective-permute-start | bytes 393224 | tf_op jit(solution)/shard_map/ppermute | solution.py:311
  95.4 7.3 %collective-permute-start.20 = (bf16[256,256]{1,0:T(8,128)(2,1)S(1)}, bf16[256,256]{1,0:T(8,128)(2,1)S(1)}, u32[]{:S(2)}, u32[]{:S(2)}) collective-permute-start(bf16[256,256]{1,0:T(8,128)(2,1)S(1)} %get-tuple-element.57), channel_id=1, source_target_pairs={{0,2},{1,3},{2,0},{3,1},{4,6},{5,7},{6,4},{7,5},{8,10},{9,11},{10,... | collective-permute-start | bytes 393224 | tf_op jit(solution)/shard_map/ppermute | solution.py:311

commit v15 on v14

--- a/solution.py
+++ b/solution.py
@@ -14,6 +14,7 @@
 FAST_DIM = 512
 FAST_HIDDEN = 512
 TILE = 128
+QUERY_TILE = 256
 VMEM_LIMIT = 24 * 1024 * 1024
 VMEM_MOST = 60 * 1024 * 1024
 
@@ -103,23 +104,23 @@
 
 def attend_rows(edge_prev, edge_next, query_tile, keys_prev, keys_own, keys_next,
                 values_prev, values_own, values_next):
-    scale = 1.0 / math.sqrt(HEAD_DIM)
-    row = lax.broadcasted_iota(jnp.int32, (TILE, TILE), 0)
-    col = lax.broadcasted_iota(jnp.int32, (TILE, TILE), 1)
+    scale = math.log2(math.e) / math.sqrt(HEAD_DIM)
+    row = lax.broadcasted_iota(jnp.int32, (QUERY_TILE, QUERY_TILE), 0)
+    col = lax.broadcasted_iota(jnp.int32, (QUERY_TILE, QUERY_TILE), 1)
     minus = jnp.float32(-jnp.inf)
     score_prev = dot_nt(query_tile, keys_prev)
     score_own = dot_nt(query_tile, keys_own)
     score_next = dot_nt(query_tile, keys_next)
-    parts = [score_prev[:, :TILE] + jnp.where(col >= row, edge_prev, minus)]
-    if score_prev.shape[1] > TILE:
-        parts.append(score_prev[:, TILE:] + edge_prev)
+    parts = [score_prev[:, :QUERY_TILE] + jnp.where(col >= row, edge_prev, minus)]
+    if score_prev.shape[1] > QUERY_TILE:
+        parts.append(score_prev[:, QUERY_TILE:] + edge_prev)
     parts.append(score_own)
-    if score_next.shape[1] > TILE:
-        parts.append(score_next[:, :-TILE] + edge_next)
-    parts.append(score_next[:, -TILE:] + jnp.where(col <= row, edge_next, minus))
+    if score_next.shape[1] > QUERY_TILE:
+        parts.append(score_next[:, :-QUERY_TILE] + edge_next)
+    parts.append(score_next[:, -QUERY_TILE:] + jnp.where(col <= row, edge_next, minus))
     scores = jnp.concatenate(parts, axis=1)
     highest = jnp.max(scores, axis=1, keepdims=True)
-    weights = jnp.exp((scores - highest) * scale)
+    weights = jnp.exp2((scores - highest) * scale)
     total = jnp.sum(weights, axis=1, keepdims=True)
     weights = weights.astype(BF16)
     width_prev, width_own = score_prev.shape[1], score_own.shape[1]
@@ -170,10 +171,10 @@
         base = (side if turn == 0 else 1 - side) * count
 
         def span(ref, low, length):
-            return ref[pl.ds(pl.multiple_of(base + low, TILE), length), :]
-
-        for index in range(count // TILE):
-            low, high = index * TILE, (index + 1) * TILE
+            return ref[pl.ds(pl.multiple_of(base + low, QUERY_TILE), length), :]
+
+        for index in range(count // QUERY_TILE):
+            low, high = index * QUERY_TILE, (index + 1) * QUERY_TILE
             query = queries_ref[low:high, pl.ds(start, HEAD_DIM)] if turn == 0 else other_ref[low:high, :]
             out_ref[low:high, :] = attend_rows(
                 edge_ref[turn, 0], edge_ref[turn, 1], query,
@@ -192,8 +193,8 @@
     offset = half if done_refs else 0
     if done_refs:
         out_ref[:half, :] = done_refs[0][...]
-    for low in range(offset, offset + half, TILE):
-        high = low + TILE
+    for low in range(offset, offset + half, QUERY_TILE):
+        high = low + QUERY_TILE
         rows = slice(low, high)
         mixed = (
             keep_ref[rows, :].astype(F32)
@@ -216,21 +217,21 @@
         out_ref[rows, :] = (both * lax.rsqrt(mean + 1e-05)).astype(BF16)
 
 
-def renew_kernel(orders, place_ref, side_ref, *refs):
-    count = (len(refs) - 4) // 2
-    sources, (own_ref, fast_ref), loaded = refs[:count], refs[count:count + 2], refs[count + 2:-2]
-    new_ref, sems = refs[-2:]
+def renew_kernel(orders, place_ref, side_ref, places_ref, *refs):
+    count = (len(refs) - 8) // 2
+    sources, own_ref, share_refs = refs[:count], refs[count], refs[count + 1:count + 5]
+    loaded, (fast_ref, new_ref, sems) = refs[count + 5:-3], refs[-3:]
     copies = [
         pltpu.make_async_copy(source, target, sems.at[index])
         for index, (source, target) in enumerate(zip(sources, loaded))
     ]
     for copy in copies:
         copy.start()
-    pieces, (weights_ref, keep_ref, other_ref, map_ref) = loaded[:-4], loaded[-4:]
+    pieces, (weights_ref, keep_ref, other_ref, map_ref, output_ref) = loaded[:-5], loaded[-5:]
     place = place_ref[0, 0]
     side = side_ref[0, 0]
     hidden_size, width = weights_ref.shape[1:]
-    for copy in copies[:-4]:
+    for copy in copies[:-5]:
         copy.wait()
     limit_norm = math.sqrt(FAST_HIDDEN * FAST_DIM) / 2.0
     step = 64
@@ -241,7 +242,7 @@
             square = square + jnp.sum(part * part, axis=0, keepdims=True)
     square = jnp.sum(square, axis=1, keepdims=True)
     factor = jnp.minimum(1.0, limit_norm * lax.rsqrt(square + 1e-06))
-    copies[-4].wait()
+    copies[-5].wait()
     per_chunk = len(pieces) // 2
     piece_rows = pieces[0].shape[0]
     blocks = 1 << len(orders[0])
@@ -272,7 +273,7 @@
                 new_ref[matrix, rows, :] = fresh
                 if block == 0:
                     own_ref[matrix, low:low + count, :] = fresh
-    for copy in copies[-3:]:
+    for copy in copies[-4:-1]:
         copy.wait()
     own_map = map_ref[pl.ds(pl.multiple_of(side * HEAD_DIM, HEAD_DIM), HEAD_DIM), :]
     other_map = map_ref[pl.ds(pl.multiple_of((1 - side) * HEAD_DIM, HEAD_DIM), HEAD_DIM), :]
@@ -291,13 +292,11 @@
         raw = dot_nn(hidden, new_ref[2])
         mean = jnp.mean(raw * raw, axis=1, keepdims=True)
         fast_ref[rows, :] = (raw * lax.rsqrt(mean + 1e-05)).astype(BF16)
-
-
-def mix_kernel(pair, places_ref, fast_ref, map_ref, *out_refs):
-    for index, out_ref in enumerate(out_refs):
-        width = out_ref.shape[1]
-        start = pl.multiple_of(places_ref[0, 2 * pair + index] * width, width)
-        out_ref[...] = dot_nn(fast_ref[...], map_ref[:, pl.ds(start, width)]).astype(BF16)
+    copies[-1].wait()
+    for index, share_ref in enumerate(share_refs):
+        width = share_ref.shape[1]
+        start = pl.multiple_of(places_ref[0, index] * width, width)
+        share_ref[...] = dot_nn(fast_ref[...], output_ref[:, pl.ds(start, width)]).astype(BF16)
 
 
 def seq_shift(value, step):
@@ -456,27 +455,23 @@
         [2 * pair + bit for pair in (near ^ 1, near) for bit in (1 - my_bit, my_bit)]
     ).astype(jnp.int32).reshape(1, 4)
     share = shape((rows, width), BF16)
-    operands = (*gathered, weights, keep_first, back_first, input_map[0])
-    own_new, fast_out = call(
+    operands = (*gathered, weights, keep_first, back_first, input_map[0], output_map)
+    own_new, far_send, far_keep, near_send, near_keep = call(
         functools.partial(renew_kernel, orders),
-        [shape((3, own_rows, fast_width), BF16), shape((rows, fast_width), BF16)],
-        (place, side_scalar, *operands),
-        scalars=2,
+        [shape((3, own_rows, fast_width), BF16)] + [share] * 4,
+        (place, side_scalar, places, *operands),
+        scalars=3,
         anywhere=len(operands),
         scratch=[pltpu.VMEM(operand.shape, BF16) for operand in operands]
-        + [pltpu.VMEM(weights.shape, BF16), pltpu.SemaphoreType.DMA((len(operands),))],
+        + [
+            pltpu.VMEM((rows, fast_width), BF16),
+            pltpu.VMEM(weights.shape, BF16),
+            pltpu.SemaphoreType.DMA((len(operands),)),
+        ],
         limit=VMEM_MOST,
     )
-
-    def mixed_for(pair, fast):
-        return call(
-            functools.partial(mix_kernel, pair), [share, share], (places, fast, output_map), scalars=1
-        )
-
-    far_send, far_keep = mixed_for(0, fast_out)
     far_near = head_swap(far_send, 1)
-    near_send, near_keep = mixed_for(1, after(fast_out, next_second))
-    near_near = head_swap(near_send, 1)
+    near_near = head_swap(after(near_send, next_second), 1)
     half = rows // 2
     far_parts = []
     for part in (slice(0, half), slice(half, rows)):

time: 106 us -> 106 us (level)
  Pallas kernels: 25.4 us -> 23.2 us
    pallas_call x8 -> x6, Pallas kernels: 18.6 us -> 16.3 us  [call(): pl.pallas_call(body, out_shape=out_shapes, in_specs=in_specs, out_specs=j...]
    ppermute x4, waiting for transfers between devices: 4.32 us -> 5.55 us  [head_swap(): lax.ppermute(value, 'head', [(i, i ^ bit) for i in range(lax.axis_size('h...]
  transfers between devices with their start and end apart: 22 -> 22, of which waited for: 9 -> 11; matrix products, arithmetic and copies ran while one was open for 3% -> 3% of each run, Pallas kernels for 15% -> 13%
where the time goes in v15:
time: 106 us
  starting transfers between devices  51.3 us (48%)
  waiting for transfers between devices  25.2 us (24%)
  Pallas kernels  23.2 us (22%)
  local copies, waits for them, and re-layouts  3.27 us (3%)
  other arithmetic  2.08 us (2%)
    ppermute x14, starting transfers between devices, seq_swap(): lax.ppermute(value, 'seq', [(i, i ^ step) for i in range(lax.axis_size('s...  39.3 us
    ppermute x14, waiting for transfers between devices, seq_swap(): lax.ppermute(value, 'seq', [(i, i ^ step) for i in range(lax.axis_size('s...  19.6 us
    pallas_call x6, Pallas kernels, call(): pl.pallas_call(body, out_shape=out_shapes, in_specs=in_specs, out_specs=j...  16.3 us
    ppermute x4, starting transfers between devices, seq_shift(): lax.ppermute(value, 'seq', [(i, i + step) for i in range(peers) if 0 <= i...  9.33 us
    pallas_call x1, Pallas kernels, local(): pl.pallas_call(functools.partial(gradient_kernel, orders), grid=(hidden_s...  6.88 us
    ppermute x4, waiting for transfers between devices, head_swap(): lax.ppermute(value, 'head', [(i, i ^ bit) for i in range(lax.axis_size('h...  5.55 us
    ppermute x4, starting transfers between devices, head_swap(): lax.ppermute(value, 'head', [(i, i ^ bit) for i in range(lax.axis_size('h...  2.65 us
    unnamed x31, local copies, waits for them, and re-layouts  2.46 us
  transfers between devices with their start and end apart: 22, of which 11 were waited for; matrix products, arithmetic and copies ran while one was open for 3% of the time, Pallas kernels for 13%

profile of v15, /device:TPU:0, one launch (start us, length us, event | category | flops | bytes accessed | tf_op | source)
XLA Modules:
  0.0 106.0 jit_solution(14301801313269335016)
XLA Ops:
  0.7 6.9 %shard_map.131 = (bf16[256,768]{1,0:T(8,128)(2,1)}, bf16[256,768]{1,0:T(8,128)(2,1)}, bf16[256,768]{1,0:T(8,128)(2,1)}, bf16[256,768]{1,0:T(8,128)(2,1)}) custom-call(s32[1,1]{1,0:T(1,128)} %bitcast.4.place_ref, f32[1,512]{1,0:T(1,128)} %bitcast.23, bf16[512,512]{1,0:T(8,128)(2,1)} %keys_ref.5, bf16[512,512]{1,0:T(8,128)(2,1)} %values_ref.5, ...), custom_call_target="tpu_custom_call" | custom-call | flops 1000 | bytes 1000 | tf_op jit(solution)/shard_map/pallas_call | solution.py:389
  7.6 3.0 %collective-permute-start = (bf16[256,768]{1,0:T(8,128)(2,1)}, bf16[256,768]{1,0:T(8,128)(2,1)S(1)}, u32[]{:S(2)}, u32[]{:S(2)}) collective-permute-start(bf16[256,768]{1,0:T(8,128)(2,1)} %get-tuple-element.25), channel_id=1, source_target_pairs={{0,4},{4,0},{8,12},{12,8},{16,20},{20,16},{24,28},{28,24},{1,5},{5... | collective-permute-start | bytes 1179656 | tf_op jit(solution)/shard_map/ppermute | solution.py:315
  10.5 0.1 shard_map.132
  10.6 0.1 collective-permute-start.8
  10.7 2.0 %collective-permute-start.4 = (bf16[256,768]{1,0:T(8,128)(2,1)}, bf16[256,768]{1,0:T(8,128)(2,1)S(1)}, u32[]{:S(2)}, u32[]{:S(2)}) collective-permute-start(bf16[256,768]{1,0:T(8,128)(2,1)} %get-tuple-element.27), channel_id=1, source_target_pairs={{0,8},{4,12},{8,0},{12,4},{16,24},{20,28},{24,16},{28,20},{1,9},{5... | collective-permute-start | bytes 1179656 | tf_op jit(solution)/shard_map/ppermute | solution.py:315
  12.8 0.7 constant_dynamic-update-slice_fusion.1
  13.5 0.7 constant_dynamic-update-slice_fusion
  14.2 6.5 %collective-permute-done = bf16[256,768]{1,0:T(8,128)(2,1)S(1)} collective-permute-done((bf16[256,768]{1,0:T(8,128)(2,1)}, bf16[256,768]{1,0:T(8,128)(2,1)S(1)}, u32[]{:S(2)}, u32[]{:S(2)}) %collective-permute-start) | collective-permute-done | bytes 393248 | tf_op jit(solution)/shard_map/ppermute | solution.py:315
  20.7 0.1 add_convert_fusion.1
  20.8 2.2 %collective-permute-start.1 = (bf16[128,768]{1,0:T(8,128)(2,1)S(1)}, bf16[128,768]{1,0:T(8,128)(2,1)S(1)}, u32[]{:S(2)}, u32[]{:S(2)}) collective-permute-start(bf16[128,768]{1,0:T(8,128)(2,1)S(1)} %get-tuple-element.48), channel_id=1, source_target_pairs={{0,8},{4,12},{8,0},{12,4},{16,24},{20,28},{24,16},{28,20},{1,9},{5... | collective-permute-start | bytes 589832 | tf_op jit(solution)/shard_map/ppermute | solution.py:315
  23.0 0.1 add_convert_fusion
  23.1 2.6 %collective-permute-start.5 = (bf16[128,768]{1,0:T(8,128)(2,1)S(1)}, bf16[128,768]{1,0:T(8,128)(2,1)S(1)}, u32[]{:S(2)}, u32[]{:S(2)}) collective-permute-start(bf16[128,768]{1,0:T(8,128)(2,1)S(1)} %get-tuple-element.46), channel_id=1, source_target_pairs={{0,16},{4,20},{8,24},{12,28},{16,0},{20,4},{24,8},{28,12},{1,17},{... | collective-permute-start | bytes 589832 | tf_op jit(solution)/shard_map/ppermute | solution.py:315
  25.7 2.6 %collective-permute-done.8.other_ref = bf16[1536,128]{1,0:T(8,128)(2,1)S(1)} collective-permute-done((bf16[1536,128]{1,0:T(8,128)(2,1)S(1)}, bf16[1536,128]{1,0:T(8,128)(2,1)S(1)}, u32[]{:S(2)}, u32[]{:S(2)}) %collective-permute-start.8) | collective-permute-done | bytes 393248 | tf_op jit(solution)/shard_map/ppermute | solution.py:315
  28.4 0.8 collective-permute-done.1
  29.1 2.1 %collective-permute-start.2 = (bf16[64,768]{1,0:T(8,128)(2,1)S(1)}, bf16[64,768]{1,0:T(8,128)(2,1)S(1)}, u32[]{:S(2)}, u32[]{:S(2)}) collective-permute-start(bf16[64,768]{1,0:T(8,128)(2,1)S(1)} %get-tuple-element.52), channel_id=1, source_target_pairs={{0,16},{4,20},{8,24},{12,28},{16,0},{20,4},{24,8},{28,12},{1,17},{... | collective-permute-start | bytes 294920 | tf_op jit(solution)/shard_map/ppermute | solution.py:315
  31.3 2.4 %collective-permute-done.5 = bf16[128,768]{1,0:T(8,128)(2,1)S(1)} collective-permute-done((bf16[128,768]{1,0:T(8,128)(2,1)S(1)}, bf16[128,768]{1,0:T(8,128)(2,1)S(1)}, u32[]{:S(2)}, u32[]{:S(2)}) %collective-permute-start.5) | collective-permute-done | bytes 196640 | tf_op jit(solution)/shard_map/ppermute | solution.py:315
  33.8 1.6 %collective-permute-start.6 = (bf16[64,768]{1,0:T(8,128)(2,1)S(1)}, bf16[64,768]{1,0:T(8,128)(2,1)S(1)}, u32[]{:S(2)}, u32[]{:S(2)}) collective-permute-start(bf16[64,768]{1,0:T(8,128)(2,1)S(1)} %get-tuple-element.50), channel_id=1, source_target_pairs={{0,4},{4,0},{8,12},{12,8},{16,20},{20,16},{24,28},{28,24},{1,5},{5... | collective-permute-start | bytes 294920 | tf_op jit(solution)/shard_map/ppermute | solution.py:315
  35.4 4.1 %collective-permute-start.9 = (bf16[1024,128]{1,0:T(8,128)(2,1)S(1)}, bf16[1024,128]{1,0:T(8,128)(2,1)S(1)}, u32[]{:S(2)}, u32[]{:S(2)}) collective-permute-start(bf16[1024,128]{1,0:T(8,128)(2,1)S(1)} %get-tuple-element.30.high_ref), channel_id=1, source_target_pairs={{0,8},{4,12},{8,16},{12,20},{16,24},{20,28},{1,9},{5,13},{9,17},{1... | collective-permute-start | bytes 786440 | tf_op jit(solution)/shard_map/ppermute | solution.py:304
  39.5 1.3 %collective-permute-start.10 = (bf16[1024,128]{1,0:T(8,128)(2,1)S(1)}, bf16[1024,128]{1,0:T(8,128)(2,1)S(1)}, u32[]{:S(2)}, u32[]{:S(2)}) collective-permute-start(bf16[1024,128]{1,0:T(8,128)(2,1)S(1)} %get-tuple-element.31.low_ref), channel_id=1, source_target_pairs={{8,0},{12,4},{16,8},{20,12},{24,16},{28,20},{9,1},{13,5},{17,9},{2... | collective-permute-start | bytes 786440 | tf_op jit(solution)/shard_map/ppermute | solution.py:304
  40.8 2.4 %collective-permute-start.11 = (bf16[1024,256]{1,0:T(8,128)(2,1)}, bf16[1024,256]{1,0:T(8,128)(2,1)S(1)}, u32[]{:S(2)}, u32[]{:S(2)}) collective-permute-start(bf16[1024,256]{1,0:T(8,128)(2,1)} %constant_dynamic-update-slice_fusion), channel_id=1, source_target_pairs={{0,4},{4,8},{8,12},{12,16},{16,20},{20,24},{24,28},{1,5},{5,9},{9,... | collective-permute-start | bytes 1572872 | tf_op jit(solution)/shard_map/ppermute | solution.py:304
  43.3 4.0 %collective-permute-start.3 = (bf16[64,768]{1,0:T(8,128)(2,1)S(1)}, bf16[64,768]{1,0:T(8,128)(2,1)S(1)}, u32[]{:S(2)}, u32[]{:S(2)}) collective-permute-start(bf16[64,768]{1,0:T(8,128)(2,1)S(1)} %add_convert_fusion.5), channel_id=1, source_target_pairs={{0,16},{4,20},{8,24},{12,28},{16,0},{20,4},{24,8},{28,12},{1,17},{... | collective-permute-start | bytes 294920 | tf_op jit(solution)/shard_map/ppermute | solution.py:315
  47.3 3.1 %collective-permute-start.7 = (bf16[64,768]{1,0:T(8,128)(2,1)S(1)}, bf16[64,768]{1,0:T(8,128)(2,1)S(1)}, u32[]{:S(2)}, u32[]{:S(2)}) collective-permute-start(bf16[64,768]{1,0:T(8,128)(2,1)S(1)} %add_convert_fusion.4), channel_id=1, source_target_pairs={{0,4},{4,0},{8,12},{12,8},{16,20},{20,16},{24,28},{28,24},{1,5},{5... | collective-permute-start | bytes 294920 | tf_op jit(solution)/shard_map/ppermute | solution.py:315
  50.4 2.6 %collective-permute-done.7 = bf16[64,768]{1,0:T(8,128)(2,1)S(1)} collective-permute-done((bf16[64,768]{1,0:T(8,128)(2,1)S(1)}, bf16[64,768]{1,0:T(8,128)(2,1)S(1)}, u32[]{:S(2)}, u32[]{:S(2)}) %collective-permute-start.7) | collective-permute-done | bytes 98336 | tf_op jit(solution)/shard_map/ppermute | solution.py:315
  53.1 7.5 %collective-permute-start.12 = (bf16[128,768]{1,0:T(8,128)(2,1)S(1)}, bf16[128,768]{1,0:T(8,128)(2,1)S(1)}, u32[]{:S(2)}, u32[]{:S(2)}) collective-permute-start(bf16[128,768]{1,0:T(8,128)(2,1)S(1)} %pad_maximum_fusion.2), channel_id=1, source_target_pairs={{0,8},{4,12},{8,0},{12,4},{16,24},{20,28},{24,16},{28,20},{1,9},{5... | collective-permute-start | bytes 589832 | tf_op jit(solution)/shard_map/ppermute | solution.py:315
  60.6 0.1 pad_maximum_fusion.4
  60.7 0.1 reshape.19.edge_ref
  60.8 5.3 %collective-permute-start.13 = (bf16[128,768]{1,0:T(8,128)(2,1)S(1)}, bf16[128,768]{1,0:T(8,128)(2,1)S(1)}, u32[]{:S(2)}, u32[]{:S(2)}) collective-permute-start(bf16[128,768]{1,0:T(8,128)(2,1)S(1)} %pad_maximum_fusion.3), channel_id=1, source_target_pairs={{0,16},{4,20},{8,24},{12,28},{16,0},{20,4},{24,8},{28,12},{1,17},{... | collective-permute-start | bytes 589832 | tf_op jit(solution)/shard_map/ppermute | solution.py:315
  66.0 3.0 %shard_map.134 = (bf16[512,128]{1,0:T(8,128)(2,1)S(1)}, bf16[512,128]{1,0:T(8,128)(2,1)S(1)}) custom-call(f32[2,2]{1,0:T(2,128)S(1)} %reshape.19.edge_ref, s32[1,1]{1,0:T(1,128)} %bitcast.5.side_ref, bf16[512,256]{1,0:T(8,128)(2,1)S(1)} %copy-done.6, bf16[1536,128]{1,0:T(8,128)(2,1)S(1)} %collective-permute-done.8.other_ref, ...), custom_call_target="tpu_custom_call" | custom-call | flops 805306368 | bytes 2097152 | tf_op jit(solution)/shard_map/pallas_call | solution.py:42
  69.2 1.2 %collective-permute-done.13 = bf16[128,768]{1,0:T(8,128)(2,1)S(1)} collective-permute-done((bf16[128,768]{1,0:T(8,128)(2,1)S(1)}, bf16[128,768]{1,0:T(8,128)(2,1)S(1)}, u32[]{:S(2)}, u32[]{:S(2)}) %collective-permute-start.13) | collective-permute-done | bytes 196640 | tf_op jit(solution)/shard_map/ppermute | solution.py:315
  70.4 0.9 collective-permute-start.14
  71.3 4.8 %collective-permute-start.15 = (bf16[256,768]{1,0:T(8,128)(2,1)S(1)}, bf16[256,768]{1,0:T(8,128)(2,1)S(1)}, u32[]{:S(2)}, u32[]{:S(2)}) collective-permute-start(bf16[256,768]{1,0:T(8,128)(2,1)S(1)} %pad_maximum_fusion.1.refs_2_), channel_id=1, source_target_pairs={{0,8},{4,12},{8,0},{12,4},{16,24},{20,28},{24,16},{28,20},{1,9},{5... | collective-permute-start | bytes 1179656 | tf_op jit(solution)/shard_map/ppermute | solution.py:315
  76.1 1.1 %collective-permute-done.16.refs_6_ = bf16[512,128]{1,0:T(8,128)(2,1)S(1)} collective-permute-done((bf16[512,128]{1,0:T(8,128)(2,1)S(1)}, bf16[512,128]{1,0:T(8,128)(2,1)S(1)}, u32[]{:S(2)}, u32[]{:S(2)}) %collective-permute-start.16) | collective-permute-done | bytes 131104 | tf_op jit(solution)/shard_map/ppermute | solution.py:315
  77.3 1.5 %collective-permute-start.17 = (bf16[1024,256]{1,0:T(8,128)(2,1)}, bf16[1024,256]{1,0:T(8,128)(2,1)S(1)}, u32[]{:S(2)}, u32[]{:S(2)}) collective-permute-start(bf16[1024,256]{1,0:T(8,128)(2,1)} %constant_dynamic-update-slice_fusion), channel_id=1, source_target_pairs={{4,0},{8,4},{12,8},{16,12},{20,16},{24,20},{28,24},{5,1},{9,5},{13... | collective-permute-start | bytes 1572872 | tf_op jit(solution)/shard_map/ppermute | solution.py:304
  78.8 0.6 add_bitcast_fusion.places_ref
  79.4 2.1 %collective-permute-done.14.refs_1_ = bf16[256,768]{1,0:T(8,128)(2,1)S(1)} collective-permute-done((bf16[256,768]{1,0:T(8,128)(2,1)S(1)}, bf16[256,768]{1,0:T(8,128)(2,1)S(1)}, u32[]{:S(2)}, u32[]{:S(2)}) %collective-permute-start.14) | collective-permute-done | bytes 393248 | tf_op jit(solution)/shard_map/ppermute | solution.py:315
  81.5 0.4 collective-permute-done.15.refs_3_
  81.9 0.4 copy-done.12
  82.3 0.4 copy-done.13
  82.6 8.4 %shard_map.135 = (bf16[3,64,512]{2,1,0:T(8,128)(2,1)}, bf16[512,256]{1,0:T(8,128)(2,1)}, bf16[512,256]{1,0:T(8,128)(2,1)}, bf16[512,256]{1,0:T(8,128)(2,1)}, bf16[512,256]{1,0:T(8,128)(2,1)}) custom-call(s32[1,1]{1,0:T(1,128)} %bitcast.4.place_ref, s32[1,1]{1,0:T(1,128)} %bitcast.5.side_ref, s32[1,4]{1,0:T(1,128)} %add_bitcast_fusion.places_ref, ...), custom_call_target="tpu_custom_call" | custom-call | flops 1000 | bytes 1000 | tf_op jit(solution)/shard_map/pallas_call | solution.py:42
  91.1 0.5 collective-permute-start.18
  91.6 1.2 %collective-permute-done.19 = bf16[512,256]{1,0:T(8,128)(2,1)S(1)} collective-permute-done((bf16[512,256]{1,0:T(8,128)(2,1)}, bf16[512,256]{1,0:T(8,128)(2,1)S(1)}, u32[]{:S(2)}, u32[]{:S(2)}) %collective-permute-start.19) | collective-permute-done | bytes 262176 | tf_op jit(solution)/shard_map/ppermute | solution.py:310
  92.8 1.0 add_convert_fusion.2
  93.9 1.5 %collective-permute-start.21 = (bf16[256,256]{1,0:T(8,128)(2,1)S(1)}, bf16[256,256]{1,0:T(8,128)(2,1)S(1)}, u32[]{:S(2)}, u32[]{:S(2)}) collective-permute-start(bf16[256,256]{1,0:T(8,128)(2,1)S(1)} %get-tuple-element.54), channel_id=1, source_target_pairs={{0,2},{1,3},{2,0},{3,1},{4,6},{5,7},{6,4},{7,5},{8,10},{9,11},{10,... | collective-permute-start | bytes 393224 | tf_op jit(solution)/shard_map/ppermute | solution.py:310
  95.4 0.6 collective-permute-start.20
  96.0 4.3 %collective-permute-done.21.far_ref = bf16[256,256]{1,0:T(8,128)(2,1)S(1)} collective-permute-done((bf16[256,256]{1,0:T(8,128)(2,1)S(1)}, bf16[256,256]{1,0:T(8,128)(2,1)S(1)}, u32[]{:S(2)}, u32[]{:S(2)}) %collective-permute-start.21) | collective-permute-done | bytes 131104 | tf_op jit(solution)/shard_map/ppermute | solution.py:310
  100.3 0.9 copy-done.5
  101.2 2.0 %shard_map.136.refs_0_ = bf16[256,256]{1,0:T(8,128)(2,1)S(1)} custom-call(f32[2,2]{1,0:T(2,128)S(1)} %reshape.19.edge_ref, bf16[512,256]{1,0:T(8,128)(2,1)S(1)} %copy-done.4, bf16[512,256]{1,0:T(8,128)(2,1)S(1)} %copy-done.5, bf16[512,256]{1,0:T(8,128)(2,1)S(1)} %collective-permute-done.18.near_ref, bf16[256,256]{1,0:T(8,128)(2,1)S(1)} %collective-permute-done.21.far_ref, ...), custom_call_target="tpu_custom_call" | custom-call | flops 402653184 | bytes 2097152 | tf_op jit(solution)/shard_map/pallas_call | solution.py:42
  103.3 2.7 %shard_map.137 = bf16[512,256]{1,0:T(8,128)(2,1)} custom-call(f32[2,2]{1,0:T(2,128)S(1)} %reshape.19.edge_ref, bf16[512,256]{1,0:T(8,128)(2,1)S(1)} %copy-done.4, bf16[512,256]{1,0:T(8,128)(2,1)S(1)} %copy-done.5, bf16[512,256]{1,0:T(8,128)(2,1)S(1)} %collective-permute-done.18.near_ref, bf16[256,256]{1,0:T(8,128)(2,1)S(1)} %collective-permute-done.20.far_ref, ...), custom_call_target="tpu_custom_call" | custom-call | flops 402653184 | bytes 2097152 | tf_op jit(solution)/shard_map/pallas_call | solution.py:42
  (49 shorter events, 0.5 us)
Async XLA Ops:
  0.6 9.9 %copy-start.3 = (bf16[512,256]{1,0:T(8,128)(2,1)S(1)}, bf16[512,256]{1,0:T(8,128)(2,1)}, u32[]{:S(2)}) copy-start(bf16[512,256]{1,0:T(8,128)(2,1)} %values_ref.7) | copy-start | bytes 786436
  0.6 9.9 %copy-start.2 = (bf16[512,256]{1,0:T(8,128)(2,1)S(1)}, bf16[512,256]{1,0:T(8,128)(2,1)}, u32[]{:S(2)}) copy-start(bf16[512,256]{1,0:T(8,128)(2,1)} %keys_ref.7) | copy-start | bytes 786436
  0.7 9.9 %copy-start.6 = (bf16[512,256]{1,0:T(8,128)(2,1)S(1)}, bf16[512,256]{1,0:T(8,128)(2,1)}, u32[]{:S(2)}) copy-start(bf16[512,256]{1,0:T(8,128)(2,1)} %queries_ref.5) | copy-start | bytes 786436
  0.7 12.1 %copy-start = (bf16[512,256]{1,0:T(8,128)(2,1)S(1)}, bf16[512,256]{1,0:T(8,128)(2,1)}, u32[]{:S(2)}) copy-start(bf16[512,256]{1,0:T(8,128)(2,1)} %keys_ref.9) | copy-start | bytes 786436
  0.7 12.8 %copy-start.1 = (bf16[512,256]{1,0:T(8,128)(2,1)S(1)}, bf16[512,256]{1,0:T(8,128)(2,1)}, u32[]{:S(2)}) copy-start(bf16[512,256]{1,0:T(8,128)(2,1)} %values_ref.9) | copy-start | bytes 786436
  7.6 13.1 %copy-start.11 = (bf16[256,768]{1,0:T(8,128)(2,1)S(1)}, bf16[256,768]{1,0:T(8,128)(2,1)}, u32[]{:S(2)}) copy-start(bf16[256,768]{1,0:T(8,128)(2,1)} %get-tuple-element.24) | copy-start | bytes 1179652
  7.6 13.1 %collective-permute-start = (bf16[256,768]{1,0:T(8,128)(2,1)}, bf16[256,768]{1,0:T(8,128)(2,1)S(1)}, u32[]{:S(2)}, u32[]{:S(2)}) collective-permute-start(bf16[256,768]{1,0:T(8,128)(2,1)} %get-tuple-element.25), channel_id=1, source_target_pairs={{0,4},{4,0},{8,12},{12,8},{16,20},{20,16},{24,28},{28,24},{1,5},{5... | collective-permute-start | bytes 1179656 | tf_op jit(solution)/shard_map/ppermute | solution.py:315
  10.5 12.4 %copy-start.10 = (bf16[256,768]{1,0:T(8,128)(2,1)S(1)}, bf16[256,768]{1,0:T(8,128)(2,1)}, u32[]{:S(2)}) copy-start(bf16[256,768]{1,0:T(8,128)(2,1)} %get-tuple-element.26) | copy-start | bytes 1179652
  10.6 17.7 %collective-permute-start.8 = (bf16[1536,128]{1,0:T(8,128)(2,1)S(1)}, bf16[1536,128]{1,0:T(8,128)(2,1)S(1)}, u32[]{:S(2)}, u32[]{:S(2)}) collective-permute-start(bf16[1536,128]{1,0:T(8,128)(2,1)S(1)} %shard_map.132), channel_id=1, source_target_pairs={{0,4},{4,0},{8,12},{12,8},{16,20},{20,16},{24,28},{28,24},{1,5},{5... | collective-permute-start | bytes 1179656 | tf_op jit(solution)/shard_map/ppermute | solution.py:315
  10.7 12.2 %collective-permute-start.4 = (bf16[256,768]{1,0:T(8,128)(2,1)}, bf16[256,768]{1,0:T(8,128)(2,1)S(1)}, u32[]{:S(2)}, u32[]{:S(2)}) collective-permute-start(bf16[256,768]{1,0:T(8,128)(2,1)} %get-tuple-element.27), channel_id=1, source_target_pairs={{0,8},{4,12},{8,0},{12,4},{16,24},{20,28},{24,16},{28,20},{1,9},{5... | collective-permute-start | bytes 1179656 | tf_op jit(solution)/shard_map/ppermute | solution.py:315
  20.8 8.3 %collective-permute-start.1 = (bf16[128,768]{1,0:T(8,128)(2,1)S(1)}, bf16[128,768]{1,0:T(8,128)(2,1)S(1)}, u32[]{:S(2)}, u32[]{:S(2)}) collective-permute-start(bf16[128,768]{1,0:T(8,128)(2,1)S(1)} %get-tuple-element.48), channel_id=1, source_target_pairs={{0,8},{4,12},{8,0},{12,4},{16,24},{20,28},{24,16},{28,20},{1,9},{5... | collective-permute-start | bytes 589832 | tf_op jit(solution)/shard_map/ppermute | solution.py:315
  23.1 10.7 %collective-permute-start.5 = (bf16[128,768]{1,0:T(8,128)(2,1)S(1)}, bf16[128,768]{1,0:T(8,128)(2,1)S(1)}, u32[]{:S(2)}, u32[]{:S(2)}) collective-permute-start(bf16[128,768]{1,0:T(8,128)(2,1)S(1)} %get-tuple-element.46), channel_id=1, source_target_pairs={{0,16},{4,20},{8,24},{12,28},{16,0},{20,4},{24,8},{28,12},{1,17},{... | collective-permute-start | bytes 589832 | tf_op jit(solution)/shard_map/ppermute | solution.py:315
  29.1 14.1 %collective-permute-start.2 = (bf16[64,768]{1,0:T(8,128)(2,1)S(1)}, bf16[64,768]{1,0:T(8,128)(2,1)S(1)}, u32[]{:S(2)}, u32[]{:S(2)}) collective-permute-start(bf16[64,768]{1,0:T(8,128)(2,1)S(1)} %get-tuple-element.52), channel_id=1, source_target_pairs={{0,16},{4,20},{8,24},{12,28},{16,0},{20,4},{24,8},{28,12},{1,17},{... | collective-permute-start | bytes 294920 | tf_op jit(solution)/shard_map/ppermute | solution.py:315
  33.8 13.6 %collective-permute-start.6 = (bf16[64,768]{1,0:T(8,128)(2,1)S(1)}, bf16[64,768]{1,0:T(8,128)(2,1)S(1)}, u32[]{:S(2)}, u32[]{:S(2)}) collective-permute-start(bf16[64,768]{1,0:T(8,128)(2,1)S(1)} %get-tuple-element.50), channel_id=1, source_target_pairs={{0,4},{4,0},{8,12},{12,8},{16,20},{20,16},{24,28},{28,24},{1,5},{5... | collective-permute-start | bytes 294920 | tf_op jit(solution)/shard_map/ppermute | solution.py:315
  35.4 17.7 %collective-permute-start.9 = (bf16[1024,128]{1,0:T(8,128)(2,1)S(1)}, bf16[1024,128]{1,0:T(8,128)(2,1)S(1)}, u32[]{:S(2)}, u32[]{:S(2)}) collective-permute-start(bf16[1024,128]{1,0:T(8,128)(2,1)S(1)} %get-tuple-element.30.high_ref), channel_id=1, source_target_pairs={{0,8},{4,12},{8,16},{12,20},{16,24},{20,28},{1,9},{5,13},{9,17},{1... | collective-permute-start | bytes 786440 | tf_op jit(solution)/shard_map/ppermute | solution.py:304
  39.5 13.5 %collective-permute-start.10 = (bf16[1024,128]{1,0:T(8,128)(2,1)S(1)}, bf16[1024,128]{1,0:T(8,128)(2,1)S(1)}, u32[]{:S(2)}, u32[]{:S(2)}) collective-permute-start(bf16[1024,128]{1,0:T(8,128)(2,1)S(1)} %get-tuple-element.31.low_ref), channel_id=1, source_target_pairs={{8,0},{12,4},{16,8},{20,12},{24,16},{28,20},{9,1},{13,5},{17,9},{2... | collective-permute-start | bytes 786440 | tf_op jit(solution)/shard_map/ppermute | solution.py:304
  40.8 12.2 %collective-permute-start.11 = (bf16[1024,256]{1,0:T(8,128)(2,1)}, bf16[1024,256]{1,0:T(8,128)(2,1)S(1)}, u32[]{:S(2)}, u32[]{:S(2)}) collective-permute-start(bf16[1024,256]{1,0:T(8,128)(2,1)} %constant_dynamic-update-slice_fusion), channel_id=1, source_target_pairs={{0,4},{4,8},{8,12},{12,16},{16,20},{20,24},{24,28},{1,5},{5,9},{9,... | collective-permute-start | bytes 1572872 | tf_op jit(solution)/shard_map/ppermute | solution.py:304
  43.3 7.1 %collective-permute-start.3 = (bf16[64,768]{1,0:T(8,128)(2,1)S(1)}, bf16[64,768]{1,0:T(8,128)(2,1)S(1)}, u32[]{:S(2)}, u32[]{:S(2)}) collective-permute-start(bf16[64,768]{1,0:T(8,128)(2,1)S(1)} %add_convert_fusion.5), channel_id=1, source_target_pairs={{0,16},{4,20},{8,24},{12,28},{16,0},{20,4},{24,8},{28,12},{1,17},{... | collective-permute-start | bytes 294920 | tf_op jit(solution)/shard_map/ppermute | solution.py:315
  47.3 5.7 %collective-permute-start.7 = (bf16[64,768]{1,0:T(8,128)(2,1)S(1)}, bf16[64,768]{1,0:T(8,128)(2,1)S(1)}, u32[]{:S(2)}, u32[]{:S(2)}) collective-permute-start(bf16[64,768]{1,0:T(8,128)(2,1)S(1)} %add_convert_fusion.4), channel_id=1, source_target_pairs={{0,4},{4,0},{8,12},{12,8},{16,20},{20,16},{24,28},{28,24},{1,5},{5... | collective-permute-start | bytes 294920 | tf_op jit(solution)/shard_map/ppermute | solution.py:315
  53.1 16.1 %collective-permute-start.12 = (bf16[128,768]{1,0:T(8,128)(2,1)S(1)}, bf16[128,768]{1,0:T(8,128)(2,1)S(1)}, u32[]{:S(2)}, u32[]{:S(2)}) collective-permute-start(bf16[128,768]{1,0:T(8,128)(2,1)S(1)} %pad_maximum_fusion.2), channel_id=1, source_target_pairs={{0,8},{4,12},{8,0},{12,4},{16,24},{20,28},{24,16},{28,20},{1,9},{5... | collective-permute-start | bytes 589832 | tf_op jit(solution)/shard_map/ppermute | solution.py:315
  60.8 9.6 %collective-permute-start.13 = (bf16[128,768]{1,0:T(8,128)(2,1)S(1)}, bf16[128,768]{1,0:T(8,128)(2,1)S(1)}, u32[]{:S(2)}, u32[]{:S(2)}) collective-permute-start(bf16[128,768]{1,0:T(8,128)(2,1)S(1)} %pad_maximum_fusion.3), channel_id=1, source_target_pairs={{0,16},{4,20},{8,24},{12,28},{16,0},{20,4},{24,8},{28,12},{1,17},{... | collective-permute-start | bytes 589832 | tf_op jit(solution)/shard_map/ppermute | solution.py:315
  69.1 7.0 %copy-start.7 = (bf16[512,128]{1,0:T(8,128)(2,1)}, bf16[512,128]{1,0:T(8,128)(2,1)S(1)}, u32[]{:S(2)}) copy-start(bf16[512,128]{1,0:T(8,128)(2,1)S(1)} %get-tuple-element.35.refs_5_) | copy-start | bytes 393220
  69.1 8.2 %collective-permute-start.16 = (bf16[512,128]{1,0:T(8,128)(2,1)S(1)}, bf16[512,128]{1,0:T(8,128)(2,1)S(1)}, u32[]{:S(2)}, u32[]{:S(2)}) collective-permute-start(bf16[512,128]{1,0:T(8,128)(2,1)S(1)} %get-tuple-element.38), channel_id=1, source_target_pairs={{0,4},{4,0},{8,12},{12,8},{16,20},{20,16},{24,28},{28,24},{1,5},{5... | collective-permute-start | bytes 393224 | tf_op jit(solution)/shard_map/ppermute | solution.py:315
  69.2 12.7 %copy-start.8 = (bf16[256,768]{1,0:T(8,128)(2,1)}, bf16[256,768]{1,0:T(8,128)(2,1)S(1)}, u32[]{:S(2)}) copy-start(bf16[256,768]{1,0:T(8,128)(2,1)S(1)} %pad_maximum_fusion.refs_0_) | copy-start | bytes 1179652
  70.4 11.5 %copy-start.9 = (bf16[256,768]{1,0:T(8,128)(2,1)}, bf16[256,768]{1,0:T(8,128)(2,1)S(1)}, u32[]{:S(2)}) copy-start(bf16[256,768]{1,0:T(8,128)(2,1)S(1)} %pad_maximum_fusion.1.refs_2_) | copy-start | bytes 1179652
  70.4 11.0 %collective-permute-start.14 = (bf16[256,768]{1,0:T(8,128)(2,1)S(1)}, bf16[256,768]{1,0:T(8,128)(2,1)S(1)}, u32[]{:S(2)}, u32[]{:S(2)}) collective-permute-start(bf16[256,768]{1,0:T(8,128)(2,1)S(1)} %pad_maximum_fusion.refs_0_), channel_id=1, source_target_pairs={{0,4},{4,0},{8,12},{12,8},{16,20},{20,16},{24,28},{28,24},{1,5},{5... | collective-permute-start | bytes 1179656 | tf_op jit(solution)/shard_map/ppermute | solution.py:315
  71.3 10.5 %collective-permute-start.15 = (bf16[256,768]{1,0:T(8,128)(2,1)S(1)}, bf16[256,768]{1,0:T(8,128)(2,1)S(1)}, u32[]{:S(2)}, u32[]{:S(2)}) collective-permute-start(bf16[256,768]{1,0:T(8,128)(2,1)S(1)} %pad_maximum_fusion.1.refs_2_), channel_id=1, source_target_pairs={{0,8},{4,12},{8,0},{12,4},{16,24},{20,28},{24,16},{28,20},{1,9},{5... | collective-permute-start | bytes 1179656 | tf_op jit(solution)/shard_map/ppermute | solution.py:315
  77.3 4.6 %copy-start.14 = (bf16[512,128]{1,0:T(8,128)(2,1)}, bf16[512,128]{1,0:T(8,128)(2,1)S(1)}, u32[]{:S(2)}) copy-start(bf16[512,128]{1,0:T(8,128)(2,1)S(1)} %collective-permute-done.16.refs_6_) | copy-start | bytes 393220
  77.3 13.8 %collective-permute-start.17 = (bf16[1024,256]{1,0:T(8,128)(2,1)}, bf16[1024,256]{1,0:T(8,128)(2,1)S(1)}, u32[]{:S(2)}, u32[]{:S(2)}) collective-permute-start(bf16[1024,256]{1,0:T(8,128)(2,1)} %constant_dynamic-update-slice_fusion), channel_id=1, source_target_pairs={{4,0},{8,4},{12,8},{16,12},{20,16},{24,20},{28,24},{5,1},{9,5},{13... | collective-permute-start | bytes 1572872 | tf_op jit(solution)/shard_map/ppermute | solution.py:304
  81.5 0.8 copy-start.12
  81.9 0.7 copy-start.13
  82.6 17.7 %copy-start.4 = (bf16[512,256]{1,0:T(8,128)(2,1)S(1)}, bf16[512,256]{1,0:T(8,128)(2,1)}, u32[]{:S(2)}) copy-start(bf16[512,256]{1,0:T(8,128)(2,1)} %queries_ref.7) | copy-start | bytes 786436
  91.0 1.8 %collective-permute-start.19 = (bf16[512,256]{1,0:T(8,128)(2,1)}, bf16[512,256]{1,0:T(8,128)(2,1)S(1)}, u32[]{:S(2)}, u32[]{:S(2)}) collective-permute-start(bf16[512,256]{1,0:T(8,128)(2,1)} %get-tuple-element.44), channel_id=1, source_target_pairs={{0,1},{1,0},{2,3},{3,2},{4,5},{5,4},{6,7},{7,6},{8,9},{9,8},{10,11... | collective-permute-start | bytes 786440 | tf_op jit(solution)/shard_map/ppermute | solution.py:310
  91.1 4.9 %collective-permute-start.18 = (bf16[512,256]{1,0:T(8,128)(2,1)}, bf16[512,256]{1,0:T(8,128)(2,1)S(1)}, u32[]{:S(2)}, u32[]{:S(2)}) collective-permute-start(bf16[512,256]{1,0:T(8,128)(2,1)} %get-tuple-element.42), channel_id=1, source_target_pairs={{0,1},{1,0},{2,3},{3,2},{4,5},{5,4},{6,7},{7,6},{8,9},{9,8},{10,11... | collective-permute-start | bytes 786440 | tf_op jit(solution)/shard_map/ppermute | solution.py:310
  93.9 6.4 %collective-permute-start.21 = (bf16[256,256]{1,0:T(8,128)(2,1)S(1)}, bf16[256,256]{1,0:T(8,128)(2,1)S(1)}, u32[]{:S(2)}, u32[]{:S(2)}) collective-permute-start(bf16[256,256]{1,0:T(8,128)(2,1)S(1)} %get-tuple-element.54), channel_id=1, source_target_pairs={{0,2},{1,3},{2,0},{3,1},{4,6},{5,7},{6,4},{7,5},{8,10},{9,11},{10,... | collective-permute-start | bytes 393224 | tf_op jit(solution)/shard_map/ppermute | solution.py:310
  95.4 7.9 %collective-permute-start.20 = (bf16[256,256]{1,0:T(8,128)(2,1)S(1)}, bf16[256,256]{1,0:T(8,128)(2,1)S(1)}, u32[]{:S(2)}, u32[]{:S(2)}) collective-permute-start(bf16[256,256]{1,0:T(8,128)(2,1)S(1)} %get-tuple-element.55), channel_id=1, source_target_pairs={{0,2},{1,3},{2,0},{3,1},{4,6},{5,7},{6,4},{7,5},{8,10},{9,11},{10,... | collective-permute-start | bytes 393224 | tf_op jit(solution)/shard_map/ppermute | solution.py:310
  100.3 1.0 copy-start.5

commit v16 on v14

--- a/solution.py
+++ b/solution.py
@@ -14,6 +14,7 @@
 FAST_DIM = 512
 FAST_HIDDEN = 512
 TILE = 128
+QUERY_TILE = 256
 VMEM_LIMIT = 24 * 1024 * 1024
 VMEM_MOST = 60 * 1024 * 1024
 
@@ -103,23 +104,23 @@
 
 def attend_rows(edge_prev, edge_next, query_tile, keys_prev, keys_own, keys_next,
                 values_prev, values_own, values_next):
-    scale = 1.0 / math.sqrt(HEAD_DIM)
-    row = lax.broadcasted_iota(jnp.int32, (TILE, TILE), 0)
-    col = lax.broadcasted_iota(jnp.int32, (TILE, TILE), 1)
+    scale = math.log2(math.e) / math.sqrt(HEAD_DIM)
+    row = lax.broadcasted_iota(jnp.int32, (QUERY_TILE, QUERY_TILE), 0)
+    col = lax.broadcasted_iota(jnp.int32, (QUERY_TILE, QUERY_TILE), 1)
     minus = jnp.float32(-jnp.inf)
     score_prev = dot_nt(query_tile, keys_prev)
     score_own = dot_nt(query_tile, keys_own)
     score_next = dot_nt(query_tile, keys_next)
-    parts = [score_prev[:, :TILE] + jnp.where(col >= row, edge_prev, minus)]
-    if score_prev.shape[1] > TILE:
-        parts.append(score_prev[:, TILE:] + edge_prev)
+    parts = [score_prev[:, :QUERY_TILE] + jnp.where(col >= row, edge_prev, minus)]
+    if score_prev.shape[1] > QUERY_TILE:
+        parts.append(score_prev[:, QUERY_TILE:] + edge_prev)
     parts.append(score_own)
-    if score_next.shape[1] > TILE:
-        parts.append(score_next[:, :-TILE] + edge_next)
-    parts.append(score_next[:, -TILE:] + jnp.where(col <= row, edge_next, minus))
+    if score_next.shape[1] > QUERY_TILE:
+        parts.append(score_next[:, :-QUERY_TILE] + edge_next)
+    parts.append(score_next[:, -QUERY_TILE:] + jnp.where(col <= row, edge_next, minus))
     scores = jnp.concatenate(parts, axis=1)
     highest = jnp.max(scores, axis=1, keepdims=True)
-    weights = jnp.exp((scores - highest) * scale)
+    weights = jnp.exp2((scores - highest) * scale)
     total = jnp.sum(weights, axis=1, keepdims=True)
     weights = weights.astype(BF16)
     width_prev, width_own = score_prev.shape[1], score_own.shape[1]
@@ -170,10 +171,10 @@
         base = (side if turn == 0 else 1 - side) * count
 
         def span(ref, low, length):
-            return ref[pl.ds(pl.multiple_of(base + low, TILE), length), :]
-
-        for index in range(count // TILE):
-            low, high = index * TILE, (index + 1) * TILE
+            return ref[pl.ds(pl.multiple_of(base + low, QUERY_TILE), length), :]
+
+        for index in range(count // QUERY_TILE):
+            low, high = index * QUERY_TILE, (index + 1) * QUERY_TILE
             query = queries_ref[low:high, pl.ds(start, HEAD_DIM)] if turn == 0 else other_ref[low:high, :]
             out_ref[low:high, :] = attend_rows(
                 edge_ref[turn, 0], edge_ref[turn, 1], query,
@@ -192,8 +193,8 @@
     offset = half if done_refs else 0
     if done_refs:
         out_ref[:half, :] = done_refs[0][...]
-    for low in range(offset, offset + half, TILE):
-        high = low + TILE
+    for low in range(offset, offset + half, QUERY_TILE):
+        high = low + QUERY_TILE
         rows = slice(low, high)
         mixed = (
             keep_ref[rows, :].astype(F32)
@@ -430,10 +431,10 @@
     if halving:
         turns = len(bits)
         keeps, found = halving_start([gradients[:2], gradients[2:]], orders)
+        prev_second = seq_shift(both_second, 1)
         for turn in range(1, turns):
             if turn == turns - 1:
                 prev_first, next_first = first_halos(*after((low_block, high_block), found))
-                prev_second = seq_shift(after(both_second, found), 1)
             keeps, found = halving_step(keeps, found, orders, turn)
         held = [((keep.astype(F32) + new.astype(F32)).astype(BF16),) for keep, new in zip(keeps, found)]
         for turn in reversed(range(turns)):

time: 106 us -> 114 us (1.075)
  the two profiles are of different devices: /device:TPU:0 before, /device:TPU:6 now
where the time goes in v16:
time: 114 us
  waiting for transfers between devices  46.7 us (41%)
  starting transfers between devices  37.5 us (33%)
  Pallas kernels  23.6 us (21%)
  local copies, waits for them, and re-layouts  2.63 us (2%)
  other arithmetic  2.58 us (2%)
    ppermute x14, waiting for transfers between devices, seq_swap(): lax.ppermute(value, 'seq', [(i, i ^ step) for i in range(lax.axis_size('s...  42.4 us
    ppermute x14, starting transfers between devices, seq_swap(): lax.ppermute(value, 'seq', [(i, i ^ step) for i in range(lax.axis_size('s...  24.1 us
    pallas_call x8, Pallas kernels, call(): pl.pallas_call(body, out_shape=out_shapes, in_specs=in_specs, out_specs=j...  16.8 us
    ppermute x4, starting transfers between devices, seq_shift(): lax.ppermute(value, 'seq', [(i, i + step) for i in range(peers) if 0 <= i...  10.7 us
    pallas_call x1, Pallas kernels, local(): pl.pallas_call(functools.partial(gradient_kernel, orders), grid=(hidden_s...  6.82 us
    ppermute x4, waiting for transfers between devices, head_swap(): lax.ppermute(value, 'head', [(i, i ^ bit) for i in range(lax.axis_size('h...  4.32 us
    ppermute x4, starting transfers between devices, head_swap(): lax.ppermute(value, 'head', [(i, i ^ bit) for i in range(lax.axis_size('h...  2.71 us
  transfers between devices with their start and end apart: 22, of which 11 were waited for; matrix products, arithmetic and copies ran while one was open for 4% of the time, Pallas kernels for 12%

profile of v16, /device:TPU:6, one launch (start us, length us, event | category | flops | bytes accessed | tf_op | source)
XLA Modules:
  0.0 114.0 jit_solution(14459649481598617908)
XLA Ops:
  0.7 6.8 %shard_map.131 = (bf16[256,768]{1,0:T(8,128)(2,1)}, bf16[256,768]{1,0:T(8,128)(2,1)}, bf16[256,768]{1,0:T(8,128)(2,1)}, bf16[256,768]{1,0:T(8,128)(2,1)}) custom-call(s32[1,1]{1,0:T(1,128)} %bitcast.9.place_ref, f32[1,512]{1,0:T(1,128)} %bitcast.23, bf16[512,512]{1,0:T(8,128)(2,1)} %keys_ref.5, bf16[512,512]{1,0:T(8,128)(2,1)} %values_ref.5, ...), custom_call_target="tpu_custom_call" | custom-call | flops 1000 | bytes 1000 | tf_op jit(solution)/shard_map/pallas_call | solution.py:391
  7.5 1.6 %collective-permute-start.4 = (bf16[256,768]{1,0:T(8,128)(2,1)}, bf16[256,768]{1,0:T(8,128)(2,1)S(1)}, u32[]{:S(2)}, u32[]{:S(2)}) collective-permute-start(bf16[256,768]{1,0:T(8,128)(2,1)} %get-tuple-element.27), channel_id=1, source_target_pairs={{0,8},{4,12},{8,0},{12,4},{16,24},{20,28},{24,16},{28,20},{1,9},{5... | collective-permute-start | bytes 1179656 | tf_op jit(solution)/shard_map/ppermute | solution.py:317
  9.1 0.5 collective-permute-start
  9.7 1.6 %collective-permute-start.8 = (bf16[1536,128]{1,0:T(8,128)(2,1)S(1)}, bf16[1536,128]{1,0:T(8,128)(2,1)S(1)}, u32[]{:S(2)}, u32[]{:S(2)}) collective-permute-start(bf16[1536,128]{1,0:T(8,128)(2,1)S(1)} %shard_map.132), channel_id=1, source_target_pairs={{0,4},{4,0},{8,12},{12,8},{16,20},{20,16},{24,28},{28,24},{1,5},{5... | collective-permute-start | bytes 1179656 | tf_op jit(solution)/shard_map/ppermute | solution.py:317
  11.2 7.3 %collective-permute-done.4 = bf16[256,768]{1,0:T(8,128)(2,1)S(1)} collective-permute-done((bf16[256,768]{1,0:T(8,128)(2,1)}, bf16[256,768]{1,0:T(8,128)(2,1)S(1)}, u32[]{:S(2)}, u32[]{:S(2)}) %collective-permute-start.4) | collective-permute-done | bytes 393248 | tf_op jit(solution)/shard_map/ppermute | solution.py:317
  18.6 1.1 %add_convert_fusion = (bf16[128,768]{1,0:T(8,128)(2,1)S(1)}, f32[128,768]{1,0:T(8,128)S(1)}) fusion(bf16[256,768]{1,0:T(8,128)(2,1)S(1)} %collective-permute-done.4, bf16[256,768]{1,0:T(8,128)(2,1)} %get-tuple-element.26), kind=kLoop, calls=%fused_computation.2 | loop fusion | flops 688128 | bytes 1376256 | tf_op jit(solution)/shard_map/convert_element_type | solution.py:333
  19.7 2.6 %collective-permute-start.5 = (bf16[128,768]{1,0:T(8,128)(2,1)S(1)}, bf16[128,768]{1,0:T(8,128)(2,1)S(1)}, u32[]{:S(2)}, u32[]{:S(2)}) collective-permute-start(bf16[128,768]{1,0:T(8,128)(2,1)S(1)} %get-tuple-element.46), channel_id=1, source_target_pairs={{0,16},{4,20},{8,24},{12,28},{16,0},{20,4},{24,8},{28,12},{1,17},{... | collective-permute-start | bytes 589832 | tf_op jit(solution)/shard_map/ppermute | solution.py:317
  22.4 0.1 add_convert_fusion.1
  22.5 1.6 %collective-permute-start.1 = (bf16[128,768]{1,0:T(8,128)(2,1)S(1)}, bf16[128,768]{1,0:T(8,128)(2,1)S(1)}, u32[]{:S(2)}, u32[]{:S(2)}) collective-permute-start(bf16[128,768]{1,0:T(8,128)(2,1)S(1)} %get-tuple-element.48), channel_id=1, source_target_pairs={{0,8},{4,12},{8,0},{12,4},{16,24},{20,28},{24,16},{28,20},{1,9},{5... | collective-permute-start | bytes 589832 | tf_op jit(solution)/shard_map/ppermute | solution.py:317
  24.1 0.7 constant_dynamic-update-slice_fusion.1
  24.8 0.7 constant_dynamic-update-slice_fusion
  25.6 2.3 %collective-permute-start.11 = (bf16[1024,256]{1,0:T(8,128)(2,1)}, bf16[1024,256]{1,0:T(8,128)(2,1)S(1)}, u32[]{:S(2)}, u32[]{:S(2)}) collective-permute-start(bf16[1024,256]{1,0:T(8,128)(2,1)} %constant_dynamic-update-slice_fusion), channel_id=1, source_target_pairs={{0,4},{4,8},{8,12},{12,16},{16,20},{20,24},{24,28},{1,5},{5,9},{9,... | collective-permute-start | bytes 1572872 | tf_op jit(solution)/shard_map/ppermute | solution.py:306
  27.9 0.4 collective-permute-done.8.other_ref
  28.3 2.4 %collective-permute-done.5 = bf16[128,768]{1,0:T(8,128)(2,1)S(1)} collective-permute-done((bf16[128,768]{1,0:T(8,128)(2,1)S(1)}, bf16[128,768]{1,0:T(8,128)(2,1)S(1)}, u32[]{:S(2)}, u32[]{:S(2)}) %collective-permute-start.5) | collective-permute-done | bytes 196640 | tf_op jit(solution)/shard_map/ppermute | solution.py:317
  30.8 1.2 %collective-permute-done.1 = bf16[128,768]{1,0:T(8,128)(2,1)S(1)} collective-permute-done((bf16[128,768]{1,0:T(8,128)(2,1)S(1)}, bf16[128,768]{1,0:T(8,128)(2,1)S(1)}, u32[]{:S(2)}, u32[]{:S(2)}) %collective-permute-start.1) | collective-permute-done | bytes 196640 | tf_op jit(solution)/shard_map/ppermute | solution.py:317
  31.9 1.3 %collective-permute-start.10 = (bf16[1024,128]{1,0:T(8,128)(2,1)S(1)}, bf16[1024,128]{1,0:T(8,128)(2,1)S(1)}, u32[]{:S(2)}, u32[]{:S(2)}) collective-permute-start(bf16[1024,128]{1,0:T(8,128)(2,1)S(1)} %get-tuple-element.31.low_ref), channel_id=1, source_target_pairs={{8,0},{12,4},{16,8},{20,12},{24,16},{28,20},{9,1},{13,5},{17,9},{2... | collective-permute-start | bytes 786440 | tf_op jit(solution)/shard_map/ppermute | solution.py:306
  33.2 5.0 %collective-permute-start.9 = (bf16[1024,128]{1,0:T(8,128)(2,1)S(1)}, bf16[1024,128]{1,0:T(8,128)(2,1)S(1)}, u32[]{:S(2)}, u32[]{:S(2)}) collective-permute-start(bf16[1024,128]{1,0:T(8,128)(2,1)S(1)} %get-tuple-element.30.high_ref), channel_id=1, source_target_pairs={{0,8},{4,12},{8,16},{12,20},{16,24},{20,28},{1,9},{5,13},{9,17},{1... | collective-permute-start | bytes 786440 | tf_op jit(solution)/shard_map/ppermute | solution.py:306
  38.3 0.1 collective-permute-start.6
  38.4 1.5 %collective-permute-start.2 = (bf16[64,768]{1,0:T(8,128)(2,1)S(1)}, bf16[64,768]{1,0:T(8,128)(2,1)S(1)}, u32[]{:S(2)}, u32[]{:S(2)}) collective-permute-start(bf16[64,768]{1,0:T(8,128)(2,1)S(1)} %get-tuple-element.52), channel_id=1, source_target_pairs={{0,16},{4,20},{8,24},{12,28},{16,0},{20,4},{24,8},{28,12},{1,17},{... | collective-permute-start | bytes 294920 | tf_op jit(solution)/shard_map/ppermute | solution.py:317
  39.9 3.4 %collective-permute-done.6 = bf16[64,768]{1,0:T(8,128)(2,1)S(1)} collective-permute-done((bf16[64,768]{1,0:T(8,128)(2,1)S(1)}, bf16[64,768]{1,0:T(8,128)(2,1)S(1)}, u32[]{:S(2)}, u32[]{:S(2)}) %collective-permute-start.6) | collective-permute-done | bytes 98336 | tf_op jit(solution)/shard_map/ppermute | solution.py:317
  43.5 5.5 %collective-permute-done.2 = bf16[64,768]{1,0:T(8,128)(2,1)S(1)} collective-permute-done((bf16[64,768]{1,0:T(8,128)(2,1)S(1)}, bf16[64,768]{1,0:T(8,128)(2,1)S(1)}, u32[]{:S(2)}, u32[]{:S(2)}) %collective-permute-start.2) | collective-permute-done | bytes 98336 | tf_op jit(solution)/shard_map/ppermute | solution.py:317
  49.0 3.5 %collective-permute-start.3 = (bf16[64,768]{1,0:T(8,128)(2,1)S(1)}, bf16[64,768]{1,0:T(8,128)(2,1)S(1)}, u32[]{:S(2)}, u32[]{:S(2)}) collective-permute-start(bf16[64,768]{1,0:T(8,128)(2,1)S(1)} %add_convert_fusion.5), channel_id=1, source_target_pairs={{0,16},{4,20},{8,24},{12,28},{16,0},{20,4},{24,8},{28,12},{1,17},{... | collective-permute-start | bytes 294920 | tf_op jit(solution)/shard_map/ppermute | solution.py:317
  52.5 2.6 %collective-permute-done.3 = bf16[64,768]{1,0:T(8,128)(2,1)S(1)} collective-permute-done((bf16[64,768]{1,0:T(8,128)(2,1)S(1)}, bf16[64,768]{1,0:T(8,128)(2,1)S(1)}, u32[]{:S(2)}, u32[]{:S(2)}) %collective-permute-start.3) | collective-permute-done | bytes 98336 | tf_op jit(solution)/shard_map/ppermute | solution.py:317
  55.1 3.0 %collective-permute-start.13 = (bf16[128,768]{1,0:T(8,128)(2,1)S(1)}, bf16[128,768]{1,0:T(8,128)(2,1)}, u32[]{:S(2)}, u32[]{:S(2)}) collective-permute-start(bf16[128,768]{1,0:T(8,128)(2,1)S(1)} %pad_maximum_fusion.3), channel_id=1, source_target_pairs={{0,16},{4,20},{8,24},{12,28},{16,0},{20,4},{24,8},{28,12},{1,17},{... | collective-permute-start | bytes 589832 | tf_op jit(solution)/shard_map/ppermute | solution.py:317
  58.1 0.1 pad_maximum_fusion.4
  58.2 0.1 reshape.19.edge_ref
  58.3 5.9 %collective-permute-start.12 = (bf16[128,768]{1,0:T(8,128)(2,1)S(1)}, bf16[128,768]{1,0:T(8,128)(2,1)S(1)}, u32[]{:S(2)}, u32[]{:S(2)}) collective-permute-start(bf16[128,768]{1,0:T(8,128)(2,1)S(1)} %pad_maximum_fusion.2), channel_id=1, source_target_pairs={{0,8},{4,12},{8,0},{12,4},{16,24},{20,28},{24,16},{28,20},{1,9},{5... | collective-permute-start | bytes 589832 | tf_op jit(solution)/shard_map/ppermute | solution.py:317
  64.2 3.0 %shard_map.134 = (bf16[512,128]{1,0:T(8,128)(2,1)S(1)}, bf16[512,128]{1,0:T(8,128)(2,1)S(1)}) custom-call(f32[2,2]{1,0:T(2,128)S(1)} %reshape.19.edge_ref, s32[1,1]{1,0:T(1,128)} %bitcast.10.side_ref, bf16[512,256]{1,0:T(8,128)(2,1)S(1)} %copy-done.7, bf16[1536,128]{1,0:T(8,128)(2,1)S(1)} %collective-permute-done.8.other_ref, ...), custom_call_target="tpu_custom_call" | custom-call | flops 805306368 | bytes 2097152 | tf_op jit(solution)/shard_map/pallas_call | solution.py:42
  67.3 0.1 collective-permute-start.16
  67.4 1.0 pad_maximum_fusion.1.refs_2_
  68.3 0.7 collective-permute-done.12
  69.1 1.4 %collective-permute-start.14 = (bf16[256,768]{1,0:T(8,128)(2,1)S(1)}, bf16[256,768]{1,0:T(8,128)(2,1)}, u32[]{:S(2)}, u32[]{:S(2)}) collective-permute-start(bf16[256,768]{1,0:T(8,128)(2,1)S(1)} %pad_maximum_fusion.refs_0_), channel_id=1, source_target_pairs={{0,4},{4,0},{8,12},{12,8},{16,20},{20,16},{24,28},{28,24},{1,5},{5... | collective-permute-start | bytes 1179656 | tf_op jit(solution)/shard_map/ppermute | solution.py:317
  70.5 0.6 collective-permute-start.15
  71.0 2.7 %collective-permute-done.16.refs_6_ = bf16[512,128]{1,0:T(8,128)(2,1)S(1)} collective-permute-done((bf16[512,128]{1,0:T(8,128)(2,1)S(1)}, bf16[512,128]{1,0:T(8,128)(2,1)S(1)}, u32[]{:S(2)}, u32[]{:S(2)}) %collective-permute-start.16) | collective-permute-done | bytes 131104 | tf_op jit(solution)/shard_map/ppermute | solution.py:317
  73.7 2.1 %collective-permute-start.17 = (bf16[1024,256]{1,0:T(8,128)(2,1)}, bf16[1024,256]{1,0:T(8,128)(2,1)S(1)}, u32[]{:S(2)}, u32[]{:S(2)}) collective-permute-start(bf16[1024,256]{1,0:T(8,128)(2,1)} %constant_dynamic-update-slice_fusion), channel_id=1, source_target_pairs={{4,0},{8,4},{12,8},{16,12},{20,16},{24,20},{28,24},{5,1},{9,5},{13... | collective-permute-start | bytes 1572872 | tf_op jit(solution)/shard_map/ppermute | solution.py:306
  75.8 0.1 add_bitcast_fusion.places_ref
  75.9 16.2 %collective-permute-done.14.refs_1_ = bf16[256,768]{1,0:T(8,128)(2,1)} collective-permute-done((bf16[256,768]{1,0:T(8,128)(2,1)S(1)}, bf16[256,768]{1,0:T(8,128)(2,1)}, u32[]{:S(2)}, u32[]{:S(2)}) %collective-permute-start.14) | collective-permute-done | bytes 393248 | tf_op jit(solution)/shard_map/ppermute | solution.py:317
  92.1 6.9 %shard_map.135 = (bf16[3,64,512]{2,1,0:T(8,128)(2,1)}, bf16[512,512]{1,0:T(8,128)(2,1)}) custom-call(s32[1,1]{1,0:T(1,128)} %bitcast.9.place_ref, s32[1,1]{1,0:T(1,128)} %bitcast.10.side_ref, bf16[256,768]{1,0:T(8,128)(2,1)} %copy-done.10, bf16[256,768]{1,0:T(8,128)(2,1)} %collective-permute-done.14.refs_1_, bf16[256,768]{1,0:T(8,128)(2,1)} %copy-done.9, ...), custom_call_target="tpu_custom_call" | custom-call | flops 1000 | bytes 1000 | tf_op jit(solution)/shard_map/pallas_call | solution.py:42
  99.0 1.0 copy-done.3
  100.1 1.0 shard_map.137
  101.1 0.1 collective-permute-start.19
  101.2 1.0 shard_map.136
  102.2 0.6 collective-permute-start.18
  102.8 0.6 collective-permute-start.21
  103.4 1.5 %collective-permute-start.20 = (bf16[256,256]{1,0:T(8,128)(2,1)S(1)}, bf16[256,256]{1,0:T(8,128)(2,1)S(1)}, u32[]{:S(2)}, u32[]{:S(2)}) collective-permute-start(bf16[256,256]{1,0:T(8,128)(2,1)S(1)} %get-tuple-element.55), channel_id=1, source_target_pairs={{0,2},{1,3},{2,0},{3,1},{4,6},{5,7},{6,4},{7,5},{8,10},{9,11},{10,... | collective-permute-start | bytes 393224 | tf_op jit(solution)/shard_map/ppermute | solution.py:312
  104.9 4.3 %collective-permute-done.21.far_ref = bf16[256,256]{1,0:T(8,128)(2,1)S(1)} collective-permute-done((bf16[256,256]{1,0:T(8,128)(2,1)S(1)}, bf16[256,256]{1,0:T(8,128)(2,1)S(1)}, u32[]{:S(2)}, u32[]{:S(2)}) %collective-permute-start.21) | collective-permute-done | bytes 131104 | tf_op jit(solution)/shard_map/ppermute | solution.py:312
  109.2 2.0 %shard_map.138.refs_0_ = bf16[256,256]{1,0:T(8,128)(2,1)S(1)} custom-call(f32[2,2]{1,0:T(2,128)S(1)} %reshape.19.edge_ref, bf16[512,256]{1,0:T(8,128)(2,1)S(1)} %copy-done.6, bf16[512,256]{1,0:T(8,128)(2,1)S(1)} %get-tuple-element.41.keep_ref, bf16[512,256]{1,0:T(8,128)(2,1)S(1)} %collective-permute-done.18.near_ref, ...), custom_call_target="tpu_custom_call" | custom-call | flops 402653184 | bytes 2097152 | tf_op jit(solution)/shard_map/pallas_call | solution.py:42
  111.2 2.7 %shard_map.139 = bf16[512,256]{1,0:T(8,128)(2,1)} custom-call(f32[2,2]{1,0:T(2,128)S(1)} %reshape.19.edge_ref, bf16[512,256]{1,0:T(8,128)(2,1)S(1)} %copy-done.6, bf16[512,256]{1,0:T(8,128)(2,1)S(1)} %get-tuple-element.41.keep_ref, bf16[512,256]{1,0:T(8,128)(2,1)S(1)} %collective-permute-done.18.near_ref, ...), custom_call_target="tpu_custom_call" | custom-call | flops 402653184 | bytes 2097152 | tf_op jit(solution)/shard_map/pallas_call | solution.py:42
  (47 shorter events, 0.5 us)
Async XLA Ops:
  0.6 8.9 %copy-start.7 = (bf16[512,256]{1,0:T(8,128)(2,1)S(1)}, bf16[512,256]{1,0:T(8,128)(2,1)}, u32[]{:S(2)}) copy-start(bf16[512,256]{1,0:T(8,128)(2,1)} %queries_ref.5) | copy-start | bytes 786436
  0.6 8.9 %copy-start.4 = (bf16[512,256]{1,0:T(8,128)(2,1)S(1)}, bf16[512,256]{1,0:T(8,128)(2,1)}, u32[]{:S(2)}) copy-start(bf16[512,256]{1,0:T(8,128)(2,1)} %keys_ref.7) | copy-start | bytes 786436
  0.7 8.9 %copy-start.5 = (bf16[512,256]{1,0:T(8,128)(2,1)S(1)}, bf16[512,256]{1,0:T(8,128)(2,1)}, u32[]{:S(2)}) copy-start(bf16[512,256]{1,0:T(8,128)(2,1)} %values_ref.7) | copy-start | bytes 786436
  7.5 14.9 %copy-start.11 = (bf16[256,768]{1,0:T(8,128)(2,1)S(1)}, bf16[256,768]{1,0:T(8,128)(2,1)}, u32[]{:S(2)}) copy-start(bf16[256,768]{1,0:T(8,128)(2,1)} %get-tuple-element.24) | copy-start | bytes 1179652
  7.5 11.1 %collective-permute-start.4 = (bf16[256,768]{1,0:T(8,128)(2,1)}, bf16[256,768]{1,0:T(8,128)(2,1)S(1)}, u32[]{:S(2)}, u32[]{:S(2)}) collective-permute-start(bf16[256,768]{1,0:T(8,128)(2,1)} %get-tuple-element.27), channel_id=1, source_target_pairs={{0,8},{4,12},{8,0},{12,4},{16,24},{20,28},{24,16},{28,20},{1,9},{5... | collective-permute-start | bytes 1179656 | tf_op jit(solution)/shard_map/ppermute | solution.py:317
  9.1 13.3 %collective-permute-start = (bf16[256,768]{1,0:T(8,128)(2,1)}, bf16[256,768]{1,0:T(8,128)(2,1)S(1)}, u32[]{:S(2)}, u32[]{:S(2)}) collective-permute-start(bf16[256,768]{1,0:T(8,128)(2,1)} %get-tuple-element.25), channel_id=1, source_target_pairs={{0,4},{4,0},{8,12},{12,8},{16,20},{20,16},{24,28},{28,24},{1,5},{5... | collective-permute-start | bytes 1179656 | tf_op jit(solution)/shard_map/ppermute | solution.py:317
  9.7 14.4 %copy-start.1 = (bf16[512,256]{1,0:T(8,128)(2,1)S(1)}, bf16[512,256]{1,0:T(8,128)(2,1)}, u32[]{:S(2)}) copy-start(bf16[512,256]{1,0:T(8,128)(2,1)} %keys_ref.9) | copy-start | bytes 786436
  9.7 18.6 %collective-permute-start.8 = (bf16[1536,128]{1,0:T(8,128)(2,1)S(1)}, bf16[1536,128]{1,0:T(8,128)(2,1)S(1)}, u32[]{:S(2)}, u32[]{:S(2)}) collective-permute-start(bf16[1536,128]{1,0:T(8,128)(2,1)S(1)} %shard_map.132), channel_id=1, source_target_pairs={{0,4},{4,0},{8,12},{12,8},{16,20},{20,16},{24,28},{28,24},{1,5},{5... | collective-permute-start | bytes 1179656 | tf_op jit(solution)/shard_map/ppermute | solution.py:317
  18.6 6.3 %copy-start.2 = (bf16[512,256]{1,0:T(8,128)(2,1)S(1)}, bf16[512,256]{1,0:T(8,128)(2,1)}, u32[]{:S(2)}) copy-start(bf16[512,256]{1,0:T(8,128)(2,1)} %values_ref.9) | copy-start | bytes 786436
  19.7 11.1 %collective-permute-start.5 = (bf16[128,768]{1,0:T(8,128)(2,1)S(1)}, bf16[128,768]{1,0:T(8,128)(2,1)S(1)}, u32[]{:S(2)}, u32[]{:S(2)}) collective-permute-start(bf16[128,768]{1,0:T(8,128)(2,1)S(1)} %get-tuple-element.46), channel_id=1, source_target_pairs={{0,16},{4,20},{8,24},{12,28},{16,0},{20,4},{24,8},{28,12},{1,17},{... | collective-permute-start | bytes 589832 | tf_op jit(solution)/shard_map/ppermute | solution.py:317
  22.5 9.5 %collective-permute-start.1 = (bf16[128,768]{1,0:T(8,128)(2,1)S(1)}, bf16[128,768]{1,0:T(8,128)(2,1)S(1)}, u32[]{:S(2)}, u32[]{:S(2)}) collective-permute-start(bf16[128,768]{1,0:T(8,128)(2,1)S(1)} %get-tuple-element.48), channel_id=1, source_target_pairs={{0,8},{4,12},{8,0},{12,4},{16,24},{20,28},{24,16},{28,20},{1,9},{5... | collective-permute-start | bytes 589832 | tf_op jit(solution)/shard_map/ppermute | solution.py:317
  25.6 29.5 %collective-permute-start.11 = (bf16[1024,256]{1,0:T(8,128)(2,1)}, bf16[1024,256]{1,0:T(8,128)(2,1)S(1)}, u32[]{:S(2)}, u32[]{:S(2)}) collective-permute-start(bf16[1024,256]{1,0:T(8,128)(2,1)} %constant_dynamic-update-slice_fusion), channel_id=1, source_target_pairs={{0,4},{4,8},{8,12},{12,16},{16,20},{20,24},{24,28},{1,5},{5,9},{9,... | collective-permute-start | bytes 1572872 | tf_op jit(solution)/shard_map/ppermute | solution.py:306
  31.9 23.2 %collective-permute-start.10 = (bf16[1024,128]{1,0:T(8,128)(2,1)S(1)}, bf16[1024,128]{1,0:T(8,128)(2,1)S(1)}, u32[]{:S(2)}, u32[]{:S(2)}) collective-permute-start(bf16[1024,128]{1,0:T(8,128)(2,1)S(1)} %get-tuple-element.31.low_ref), channel_id=1, source_target_pairs={{8,0},{12,4},{16,8},{20,12},{24,16},{28,20},{9,1},{13,5},{17,9},{2... | collective-permute-start | bytes 786440 | tf_op jit(solution)/shard_map/ppermute | solution.py:306
  33.2 21.9 %collective-permute-start.9 = (bf16[1024,128]{1,0:T(8,128)(2,1)S(1)}, bf16[1024,128]{1,0:T(8,128)(2,1)S(1)}, u32[]{:S(2)}, u32[]{:S(2)}) collective-permute-start(bf16[1024,128]{1,0:T(8,128)(2,1)S(1)} %get-tuple-element.30.high_ref), channel_id=1, source_target_pairs={{0,8},{4,12},{8,16},{12,20},{16,24},{20,28},{1,9},{5,13},{9,17},{1... | collective-permute-start | bytes 786440 | tf_op jit(solution)/shard_map/ppermute | solution.py:306
  38.3 5.1 %collective-permute-start.6 = (bf16[64,768]{1,0:T(8,128)(2,1)S(1)}, bf16[64,768]{1,0:T(8,128)(2,1)S(1)}, u32[]{:S(2)}, u32[]{:S(2)}) collective-permute-start(bf16[64,768]{1,0:T(8,128)(2,1)S(1)} %get-tuple-element.50), channel_id=1, source_target_pairs={{0,4},{4,0},{8,12},{12,8},{16,20},{20,16},{24,28},{28,24},{1,5},{5... | collective-permute-start | bytes 294920 | tf_op jit(solution)/shard_map/ppermute | solution.py:317
  38.4 10.5 %collective-permute-start.2 = (bf16[64,768]{1,0:T(8,128)(2,1)S(1)}, bf16[64,768]{1,0:T(8,128)(2,1)S(1)}, u32[]{:S(2)}, u32[]{:S(2)}) collective-permute-start(bf16[64,768]{1,0:T(8,128)(2,1)S(1)} %get-tuple-element.52), channel_id=1, source_target_pairs={{0,16},{4,20},{8,24},{12,28},{16,0},{20,4},{24,8},{28,12},{1,17},{... | collective-permute-start | bytes 294920 | tf_op jit(solution)/shard_map/ppermute | solution.py:317
  43.4 9.1 %collective-permute-start.7 = (bf16[64,768]{1,0:T(8,128)(2,1)S(1)}, bf16[64,768]{1,0:T(8,128)(2,1)S(1)}, u32[]{:S(2)}, u32[]{:S(2)}) collective-permute-start(bf16[64,768]{1,0:T(8,128)(2,1)S(1)} %add_convert_fusion.4), channel_id=1, source_target_pairs={{0,4},{4,0},{8,12},{12,8},{16,20},{20,16},{24,28},{28,24},{1,5},{5... | collective-permute-start | bytes 294920 | tf_op jit(solution)/shard_map/ppermute | solution.py:317
  49.0 6.1 %collective-permute-start.3 = (bf16[64,768]{1,0:T(8,128)(2,1)S(1)}, bf16[64,768]{1,0:T(8,128)(2,1)S(1)}, u32[]{:S(2)}, u32[]{:S(2)}) collective-permute-start(bf16[64,768]{1,0:T(8,128)(2,1)S(1)} %add_convert_fusion.5), channel_id=1, source_target_pairs={{0,16},{4,20},{8,24},{12,28},{16,0},{20,4},{24,8},{28,12},{1,17},{... | collective-permute-start | bytes 294920 | tf_op jit(solution)/shard_map/ppermute | solution.py:317
  55.1 12.2 %collective-permute-start.13 = (bf16[128,768]{1,0:T(8,128)(2,1)S(1)}, bf16[128,768]{1,0:T(8,128)(2,1)}, u32[]{:S(2)}, u32[]{:S(2)}) collective-permute-start(bf16[128,768]{1,0:T(8,128)(2,1)S(1)} %pad_maximum_fusion.3), channel_id=1, source_target_pairs={{0,16},{4,20},{8,24},{12,28},{16,0},{20,4},{24,8},{28,12},{1,17},{... | collective-permute-start | bytes 589832 | tf_op jit(solution)/shard_map/ppermute | solution.py:317
  58.3 10.7 %collective-permute-start.12 = (bf16[128,768]{1,0:T(8,128)(2,1)S(1)}, bf16[128,768]{1,0:T(8,128)(2,1)S(1)}, u32[]{:S(2)}, u32[]{:S(2)}) collective-permute-start(bf16[128,768]{1,0:T(8,128)(2,1)S(1)} %pad_maximum_fusion.2), channel_id=1, source_target_pairs={{0,8},{4,12},{8,0},{12,4},{16,24},{20,28},{24,16},{28,20},{1,9},{5... | collective-permute-start | bytes 589832 | tf_op jit(solution)/shard_map/ppermute | solution.py:317
  67.3 3.8 %copy-start.8 = (bf16[512,128]{1,0:T(8,128)(2,1)}, bf16[512,128]{1,0:T(8,128)(2,1)S(1)}, u32[]{:S(2)}) copy-start(bf16[512,128]{1,0:T(8,128)(2,1)S(1)} %get-tuple-element.34.refs_5_) | copy-start | bytes 393220
  67.3 6.4 %collective-permute-start.16 = (bf16[512,128]{1,0:T(8,128)(2,1)S(1)}, bf16[512,128]{1,0:T(8,128)(2,1)S(1)}, u32[]{:S(2)}, u32[]{:S(2)}) collective-permute-start(bf16[512,128]{1,0:T(8,128)(2,1)S(1)} %get-tuple-element.37), channel_id=1, source_target_pairs={{0,4},{4,0},{8,12},{12,8},{16,20},{20,16},{24,28},{28,24},{1,5},{5... | collective-permute-start | bytes 393224 | tf_op jit(solution)/shard_map/ppermute | solution.py:317
  68.3 23.8 %copy-start.9 = (bf16[256,768]{1,0:T(8,128)(2,1)}, bf16[256,768]{1,0:T(8,128)(2,1)S(1)}, u32[]{:S(2)}) copy-start(bf16[256,768]{1,0:T(8,128)(2,1)S(1)} %pad_maximum_fusion.1.refs_2_) | copy-start | bytes 1179652
  69.0 23.0 %copy-start.10 = (bf16[256,768]{1,0:T(8,128)(2,1)}, bf16[256,768]{1,0:T(8,128)(2,1)S(1)}, u32[]{:S(2)}) copy-start(bf16[256,768]{1,0:T(8,128)(2,1)S(1)} %pad_maximum_fusion.refs_0_) | copy-start | bytes 1179652
  69.1 23.0 %collective-permute-start.14 = (bf16[256,768]{1,0:T(8,128)(2,1)S(1)}, bf16[256,768]{1,0:T(8,128)(2,1)}, u32[]{:S(2)}, u32[]{:S(2)}) collective-permute-start(bf16[256,768]{1,0:T(8,128)(2,1)S(1)} %pad_maximum_fusion.refs_0_), channel_id=1, source_target_pairs={{0,4},{4,0},{8,12},{12,8},{16,20},{20,16},{24,28},{28,24},{1,5},{5... | collective-permute-start | bytes 1179656 | tf_op jit(solution)/shard_map/ppermute | solution.py:317
  70.5 21.6 %collective-permute-start.15 = (bf16[256,768]{1,0:T(8,128)(2,1)S(1)}, bf16[256,768]{1,0:T(8,128)(2,1)}, u32[]{:S(2)}, u32[]{:S(2)}) collective-permute-start(bf16[256,768]{1,0:T(8,128)(2,1)S(1)} %pad_maximum_fusion.1.refs_2_), channel_id=1, source_target_pairs={{0,8},{4,12},{8,0},{12,4},{16,24},{20,28},{24,16},{28,20},{1,9},{5... | collective-permute-start | bytes 1179656 | tf_op jit(solution)/shard_map/ppermute | solution.py:317
  73.7 18.4 %copy-start.12 = (bf16[512,128]{1,0:T(8,128)(2,1)}, bf16[512,128]{1,0:T(8,128)(2,1)S(1)}, u32[]{:S(2)}) copy-start(bf16[512,128]{1,0:T(8,128)(2,1)S(1)} %collective-permute-done.16.refs_6_) | copy-start | bytes 393220
  73.7 27.5 %collective-permute-start.17 = (bf16[1024,256]{1,0:T(8,128)(2,1)}, bf16[1024,256]{1,0:T(8,128)(2,1)S(1)}, u32[]{:S(2)}, u32[]{:S(2)}) collective-permute-start(bf16[1024,256]{1,0:T(8,128)(2,1)} %constant_dynamic-update-slice_fusion), channel_id=1, source_target_pairs={{4,0},{8,4},{12,8},{16,12},{20,16},{24,20},{28,24},{5,1},{9,5},{13... | collective-permute-start | bytes 1572872 | tf_op jit(solution)/shard_map/ppermute | solution.py:306
  92.1 6.9 %copy-start = (bf16[512,1024]{1,0:T(8,128)(2,1)S(1)}, bf16[512,1024]{1,0:T(8,128)(2,1)}, u32[]{:S(2)}) copy-start(bf16[512,1024]{1,0:T(8,128)(2,1)} %map_ref.3) | copy-start | bytes 3145732
  99.0 1.0 copy-start.3
  101.1 8.1 %copy-start.6 = (bf16[512,256]{1,0:T(8,128)(2,1)S(1)}, bf16[512,256]{1,0:T(8,128)(2,1)}, u32[]{:S(2)}) copy-start(bf16[512,256]{1,0:T(8,128)(2,1)} %queries_ref.7) | copy-start | bytes 786436
  101.1 1.6 %collective-permute-start.19 = (bf16[512,256]{1,0:T(8,128)(2,1)S(1)}, bf16[512,256]{1,0:T(8,128)(2,1)S(1)}, u32[]{:S(2)}, u32[]{:S(2)}) collective-permute-start(bf16[512,256]{1,0:T(8,128)(2,1)S(1)} %get-tuple-element.44), channel_id=1, source_target_pairs={{0,1},{1,0},{2,3},{3,2},{4,5},{5,4},{6,7},{7,6},{8,9},{9,8},{10,11... | collective-permute-start | bytes 786440 | tf_op jit(solution)/shard_map/ppermute | solution.py:312
  102.2 2.7 %collective-permute-start.18 = (bf16[512,256]{1,0:T(8,128)(2,1)S(1)}, bf16[512,256]{1,0:T(8,128)(2,1)S(1)}, u32[]{:S(2)}, u32[]{:S(2)}) collective-permute-start(bf16[512,256]{1,0:T(8,128)(2,1)S(1)} %get-tuple-element.42), channel_id=1, source_target_pairs={{0,1},{1,0},{2,3},{3,2},{4,5},{5,4},{6,7},{7,6},{8,9},{9,8},{10,11... | collective-permute-start | bytes 786440 | tf_op jit(solution)/shard_map/ppermute | solution.py:312
  102.8 6.4 %collective-permute-start.21 = (bf16[256,256]{1,0:T(8,128)(2,1)S(1)}, bf16[256,256]{1,0:T(8,128)(2,1)S(1)}, u32[]{:S(2)}, u32[]{:S(2)}) collective-permute-start(bf16[256,256]{1,0:T(8,128)(2,1)S(1)} %get-tuple-element.54), channel_id=1, source_target_pairs={{0,2},{1,3},{2,0},{3,1},{4,6},{5,7},{6,4},{7,5},{8,10},{9,11},{10,... | collective-permute-start | bytes 393224 | tf_op jit(solution)/shard_map/ppermute | solution.py:312
  103.4 7.9 %collective-permute-start.20 = (bf16[256,256]{1,0:T(8,128)(2,1)S(1)}, bf16[256,256]{1,0:T(8,128)(2,1)S(1)}, u32[]{:S(2)}, u32[]{:S(2)}) collective-permute-start(bf16[256,256]{1,0:T(8,128)(2,1)S(1)} %get-tuple-element.55), channel_id=1, source_target_pairs={{0,2},{1,3},{2,0},{3,1},{4,6},{5,7},{6,4},{7,5},{8,10},{9,11},{10,... | collective-permute-start | bytes 393224 | tf_op jit(solution)/shard_map/ppermute | solution.py:312

commit v17 on v16

--- a/solution.py
+++ b/solution.py
@@ -431,10 +431,10 @@
     if halving:
         turns = len(bits)
         keeps, found = halving_start([gradients[:2], gradients[2:]], orders)
-        prev_second = seq_shift(both_second, 1)
         for turn in range(1, turns):
             if turn == turns - 1:
                 prev_first, next_first = first_halos(*after((low_block, high_block), found))
+                prev_second = seq_shift(after(both_second, found), 1)
             keeps, found = halving_step(keeps, found, orders, turn)
         held = [((keep.astype(F32) + new.astype(F32)).astype(BF16),) for keep, new in zip(keeps, found)]
         for turn in reversed(range(turns)):
@@ -466,7 +466,7 @@
         anywhere=len(operands),
         scratch=[pltpu.VMEM(operand.shape, BF16) for operand in operands]
         + [pltpu.VMEM(weights.shape, BF16), pltpu.SemaphoreType.DMA((len(operands),))],
-        limit=VMEM_MOST,
+        limit=VMEM_MOST - 3 * 1024 * 1024,
     )
 
     def mixed_for(pair, fast):

time: 114 us -> 105 us (0.921)
  the two profiles are of different devices: /device:TPU:6 before, /device:TPU:0 now
where the time goes in v17:
time: 105 us
  starting transfers between devices  51.4 us (49%)
  waiting for transfers between devices  24.5 us (23%)
  Pallas kernels  23.7 us (23%)
  local copies, waits for them, and re-layouts  3.4 us (3%)
    ppermute x14, starting transfers between devices, seq_swap(): lax.ppermute(value, 'seq', [(i, i ^ step) for i in range(lax.axis_size('s...  39.3 us
    ppermute x14, waiting for transfers between devices, seq_swap(): lax.ppermute(value, 'seq', [(i, i ^ step) for i in range(lax.axis_size('s...  20.1 us
    pallas_call x8, Pallas kernels, call(): pl.pallas_call(body, out_shape=out_shapes, in_specs=in_specs, out_specs=j...  16.8 us
    ppermute x4, starting transfers between devices, seq_shift(): lax.ppermute(value, 'seq', [(i, i + step) for i in range(peers) if 0 <= i...  9.33 us
    pallas_call x1, Pallas kernels, local(): pl.pallas_call(functools.partial(gradient_kernel, orders), grid=(hidden_s...  6.86 us
    ppermute x4, waiting for transfers between devices, head_swap(): lax.ppermute(value, 'head', [(i, i ^ bit) for i in range(lax.axis_size('h...  4.33 us
    ppermute x4, starting transfers between devices, head_swap(): lax.ppermute(value, 'head', [(i, i ^ bit) for i in range(lax.axis_size('h...  2.72 us
    unnamed x33, local copies, waits for them, and re-layouts  2.59 us
  transfers between devices with their start and end apart: 22, of which 10 were waited for; matrix products, arithmetic and copies ran while one was open for 2% of the time, Pallas kernels for 13%

profile of v17, /device:TPU:0, one launch (start us, length us, event | category | flops | bytes accessed | tf_op | source)
XLA Modules:
  0.0 104.5 jit_solution(11506428870654776358)
XLA Ops:
  0.7 6.9 %shard_map.131 = (bf16[256,768]{1,0:T(8,128)(2,1)}, bf16[256,768]{1,0:T(8,128)(2,1)}, bf16[256,768]{1,0:T(8,128)(2,1)}, bf16[256,768]{1,0:T(8,128)(2,1)}) custom-call(s32[1,1]{1,0:T(1,128)} %bitcast.9.place_ref, f32[1,512]{1,0:T(1,128)} %bitcast.23, bf16[512,512]{1,0:T(8,128)(2,1)} %keys_ref.5, bf16[512,512]{1,0:T(8,128)(2,1)} %values_ref.5, ...), custom_call_target="tpu_custom_call" | custom-call | flops 1000 | bytes 1000 | tf_op jit(solution)/shard_map/pallas_call | solution.py:391
  7.5 3.0 %collective-permute-start = (bf16[256,768]{1,0:T(8,128)(2,1)}, bf16[256,768]{1,0:T(8,128)(2,1)S(1)}, u32[]{:S(2)}, u32[]{:S(2)}) collective-permute-start(bf16[256,768]{1,0:T(8,128)(2,1)} %get-tuple-element.26), channel_id=1, source_target_pairs={{0,4},{4,0},{8,12},{12,8},{16,20},{20,16},{24,28},{28,24},{1,5},{5... | collective-permute-start | bytes 1179656 | tf_op jit(solution)/shard_map/ppermute | solution.py:317
  10.5 0.1 shard_map.132
  10.6 0.1 collective-permute-start.8
  10.7 2.0 %collective-permute-start.4 = (bf16[256,768]{1,0:T(8,128)(2,1)}, bf16[256,768]{1,0:T(8,128)(2,1)S(1)}, u32[]{:S(2)}, u32[]{:S(2)}) collective-permute-start(bf16[256,768]{1,0:T(8,128)(2,1)} %get-tuple-element.28), channel_id=1, source_target_pairs={{0,8},{4,12},{8,0},{12,4},{16,24},{20,28},{24,16},{28,20},{1,9},{5... | collective-permute-start | bytes 1179656 | tf_op jit(solution)/shard_map/ppermute | solution.py:317
  12.8 0.7 constant_dynamic-update-slice_fusion.1
  13.5 0.7 constant_dynamic-update-slice_fusion
  14.2 6.4 %collective-permute-done = bf16[256,768]{1,0:T(8,128)(2,1)S(1)} collective-permute-done((bf16[256,768]{1,0:T(8,128)(2,1)}, bf16[256,768]{1,0:T(8,128)(2,1)S(1)}, u32[]{:S(2)}, u32[]{:S(2)}) %collective-permute-start) | collective-permute-done | bytes 393248 | tf_op jit(solution)/shard_map/ppermute | solution.py:317
  20.7 0.1 add_convert_fusion.1
  20.8 2.2 %collective-permute-start.1 = (bf16[128,768]{1,0:T(8,128)(2,1)S(1)}, bf16[128,768]{1,0:T(8,128)(2,1)S(1)}, u32[]{:S(2)}, u32[]{:S(2)}) collective-permute-start(bf16[128,768]{1,0:T(8,128)(2,1)S(1)} %get-tuple-element.50), channel_id=1, source_target_pairs={{0,8},{4,12},{8,0},{12,4},{16,24},{20,28},{24,16},{28,20},{1,9},{5... | collective-permute-start | bytes 589832 | tf_op jit(solution)/shard_map/ppermute | solution.py:317
  23.0 0.1 add_convert_fusion
  23.0 2.6 %collective-permute-start.5 = (bf16[128,768]{1,0:T(8,128)(2,1)S(1)}, bf16[128,768]{1,0:T(8,128)(2,1)S(1)}, u32[]{:S(2)}, u32[]{:S(2)}) collective-permute-start(bf16[128,768]{1,0:T(8,128)(2,1)S(1)} %get-tuple-element.48), channel_id=1, source_target_pairs={{0,16},{4,20},{8,24},{12,28},{16,0},{20,4},{24,8},{28,12},{1,17},{... | collective-permute-start | bytes 589832 | tf_op jit(solution)/shard_map/ppermute | solution.py:317
  25.7 2.6 %collective-permute-done.8.other_ref = bf16[1536,128]{1,0:T(8,128)(2,1)S(1)} collective-permute-done((bf16[1536,128]{1,0:T(8,128)(2,1)S(1)}, bf16[1536,128]{1,0:T(8,128)(2,1)S(1)}, u32[]{:S(2)}, u32[]{:S(2)}) %collective-permute-start.8) | collective-permute-done | bytes 393248 | tf_op jit(solution)/shard_map/ppermute | solution.py:317
  28.3 0.8 collective-permute-done.1
  29.1 2.1 %collective-permute-start.2 = (bf16[64,768]{1,0:T(8,128)(2,1)S(1)}, bf16[64,768]{1,0:T(8,128)(2,1)S(1)}, u32[]{:S(2)}, u32[]{:S(2)}) collective-permute-start(bf16[64,768]{1,0:T(8,128)(2,1)S(1)} %get-tuple-element.54), channel_id=1, source_target_pairs={{0,16},{4,20},{8,24},{12,28},{16,0},{20,4},{24,8},{28,12},{1,17},{... | collective-permute-start | bytes 294920 | tf_op jit(solution)/shard_map/ppermute | solution.py:317
  31.3 2.4 %collective-permute-done.5 = bf16[128,768]{1,0:T(8,128)(2,1)S(1)} collective-permute-done((bf16[128,768]{1,0:T(8,128)(2,1)S(1)}, bf16[128,768]{1,0:T(8,128)(2,1)S(1)}, u32[]{:S(2)}, u32[]{:S(2)}) %collective-permute-start.5) | collective-permute-done | bytes 196640 | tf_op jit(solution)/shard_map/ppermute | solution.py:317
  33.7 1.6 %collective-permute-start.6 = (bf16[64,768]{1,0:T(8,128)(2,1)S(1)}, bf16[64,768]{1,0:T(8,128)(2,1)S(1)}, u32[]{:S(2)}, u32[]{:S(2)}) collective-permute-start(bf16[64,768]{1,0:T(8,128)(2,1)S(1)} %get-tuple-element.52), channel_id=1, source_target_pairs={{0,4},{4,0},{8,12},{12,8},{16,20},{20,16},{24,28},{28,24},{1,5},{5... | collective-permute-start | bytes 294920 | tf_op jit(solution)/shard_map/ppermute | solution.py:317
  35.3 4.1 %collective-permute-start.9 = (bf16[1024,128]{1,0:T(8,128)(2,1)S(1)}, bf16[1024,128]{1,0:T(8,128)(2,1)S(1)}, u32[]{:S(2)}, u32[]{:S(2)}) collective-permute-start(bf16[1024,128]{1,0:T(8,128)(2,1)S(1)} %get-tuple-element.31.high_ref), channel_id=1, source_target_pairs={{0,8},{4,12},{8,16},{12,20},{16,24},{20,28},{1,9},{5,13},{9,17},{1... | collective-permute-start | bytes 786440 | tf_op jit(solution)/shard_map/ppermute | solution.py:306
  39.5 1.3 %collective-permute-start.10 = (bf16[1024,128]{1,0:T(8,128)(2,1)S(1)}, bf16[1024,128]{1,0:T(8,128)(2,1)S(1)}, u32[]{:S(2)}, u32[]{:S(2)}) collective-permute-start(bf16[1024,128]{1,0:T(8,128)(2,1)S(1)} %get-tuple-element.32.low_ref), channel_id=1, source_target_pairs={{8,0},{12,4},{16,8},{20,12},{24,16},{28,20},{9,1},{13,5},{17,9},{2... | collective-permute-start | bytes 786440 | tf_op jit(solution)/shard_map/ppermute | solution.py:306
  40.8 2.4 %collective-permute-start.11 = (bf16[1024,256]{1,0:T(8,128)(2,1)}, bf16[1024,256]{1,0:T(8,128)(2,1)S(1)}, u32[]{:S(2)}, u32[]{:S(2)}) collective-permute-start(bf16[1024,256]{1,0:T(8,128)(2,1)} %constant_dynamic-update-slice_fusion), channel_id=1, source_target_pairs={{0,4},{4,8},{8,12},{12,16},{16,20},{20,24},{24,28},{1,5},{5,9},{9,... | collective-permute-start | bytes 1572872 | tf_op jit(solution)/shard_map/ppermute | solution.py:306
  43.3 4.0 %collective-permute-start.3 = (bf16[64,768]{1,0:T(8,128)(2,1)S(1)}, bf16[64,768]{1,0:T(8,128)(2,1)S(1)}, u32[]{:S(2)}, u32[]{:S(2)}) collective-permute-start(bf16[64,768]{1,0:T(8,128)(2,1)S(1)} %add_convert_fusion.5), channel_id=1, source_target_pairs={{0,16},{4,20},{8,24},{12,28},{16,0},{20,4},{24,8},{28,12},{1,17},{... | collective-permute-start | bytes 294920 | tf_op jit(solution)/shard_map/ppermute | solution.py:317
  47.3 3.1 %collective-permute-start.7 = (bf16[64,768]{1,0:T(8,128)(2,1)S(1)}, bf16[64,768]{1,0:T(8,128)(2,1)S(1)}, u32[]{:S(2)}, u32[]{:S(2)}) collective-permute-start(bf16[64,768]{1,0:T(8,128)(2,1)S(1)} %add_convert_fusion.4), channel_id=1, source_target_pairs={{0,4},{4,0},{8,12},{12,8},{16,20},{20,16},{24,28},{28,24},{1,5},{5... | collective-permute-start | bytes 294920 | tf_op jit(solution)/shard_map/ppermute | solution.py:317
  50.4 2.6 %collective-permute-done.7 = bf16[64,768]{1,0:T(8,128)(2,1)S(1)} collective-permute-done((bf16[64,768]{1,0:T(8,128)(2,1)S(1)}, bf16[64,768]{1,0:T(8,128)(2,1)S(1)}, u32[]{:S(2)}, u32[]{:S(2)}) %collective-permute-start.7) | collective-permute-done | bytes 98336 | tf_op jit(solution)/shard_map/ppermute | solution.py:317
  53.0 7.5 %collective-permute-start.12 = (bf16[128,768]{1,0:T(8,128)(2,1)S(1)}, bf16[128,768]{1,0:T(8,128)(2,1)S(1)}, u32[]{:S(2)}, u32[]{:S(2)}) collective-permute-start(bf16[128,768]{1,0:T(8,128)(2,1)S(1)} %pad_maximum_fusion.2), channel_id=1, source_target_pairs={{0,8},{4,12},{8,0},{12,4},{16,24},{20,28},{24,16},{28,20},{1,9},{5... | collective-permute-start | bytes 589832 | tf_op jit(solution)/shard_map/ppermute | solution.py:317
  60.6 0.1 pad_maximum_fusion.4
  60.7 0.1 reshape.19.edge_ref
  60.7 5.3 %collective-permute-start.13 = (bf16[128,768]{1,0:T(8,128)(2,1)S(1)}, bf16[128,768]{1,0:T(8,128)(2,1)S(1)}, u32[]{:S(2)}, u32[]{:S(2)}) collective-permute-start(bf16[128,768]{1,0:T(8,128)(2,1)S(1)} %pad_maximum_fusion.3), channel_id=1, source_target_pairs={{0,16},{4,20},{8,24},{12,28},{16,0},{20,4},{24,8},{28,12},{1,17},{... | collective-permute-start | bytes 589832 | tf_op jit(solution)/shard_map/ppermute | solution.py:317
  66.0 3.0 %shard_map.134 = (bf16[512,128]{1,0:T(8,128)(2,1)S(1)}, bf16[512,128]{1,0:T(8,128)(2,1)S(1)}) custom-call(f32[2,2]{1,0:T(2,128)S(1)} %reshape.19.edge_ref, s32[1,1]{1,0:T(1,128)} %bitcast.10.side_ref, bf16[512,256]{1,0:T(8,128)(2,1)S(1)} %copy-done.7, bf16[1536,128]{1,0:T(8,128)(2,1)S(1)} %collective-permute-done.8.other_ref, ...), custom_call_target="tpu_custom_call" | custom-call | flops 805306368 | bytes 2097152 | tf_op jit(solution)/shard_map/pallas_call | solution.py:42
  69.2 1.2 %collective-permute-done.13 = bf16[128,768]{1,0:T(8,128)(2,1)S(1)} collective-permute-done((bf16[128,768]{1,0:T(8,128)(2,1)S(1)}, bf16[128,768]{1,0:T(8,128)(2,1)S(1)}, u32[]{:S(2)}, u32[]{:S(2)}) %collective-permute-start.13) | collective-permute-done | bytes 196640 | tf_op jit(solution)/shard_map/ppermute | solution.py:317
  70.4 0.9 collective-permute-start.14
  71.3 4.8 %collective-permute-start.15 = (bf16[256,768]{1,0:T(8,128)(2,1)S(1)}, bf16[256,768]{1,0:T(8,128)(2,1)S(1)}, u32[]{:S(2)}, u32[]{:S(2)}) collective-permute-start(bf16[256,768]{1,0:T(8,128)(2,1)S(1)} %pad_maximum_fusion.1.refs_2_), channel_id=1, source_target_pairs={{0,8},{4,12},{8,0},{12,4},{16,24},{20,28},{24,16},{28,20},{1,9},{5... | collective-permute-start | bytes 1179656 | tf_op jit(solution)/shard_map/ppermute | solution.py:317
  76.1 1.1 %collective-permute-done.16.refs_6_ = bf16[512,128]{1,0:T(8,128)(2,1)S(1)} collective-permute-done((bf16[512,128]{1,0:T(8,128)(2,1)S(1)}, bf16[512,128]{1,0:T(8,128)(2,1)S(1)}, u32[]{:S(2)}, u32[]{:S(2)}) %collective-permute-start.16) | collective-permute-done | bytes 131104 | tf_op jit(solution)/shard_map/ppermute | solution.py:317
  77.3 1.5 %collective-permute-start.17 = (bf16[1024,256]{1,0:T(8,128)(2,1)}, bf16[1024,256]{1,0:T(8,128)(2,1)S(1)}, u32[]{:S(2)}, u32[]{:S(2)}) collective-permute-start(bf16[1024,256]{1,0:T(8,128)(2,1)} %constant_dynamic-update-slice_fusion), channel_id=1, source_target_pairs={{4,0},{8,4},{12,8},{16,12},{20,16},{24,20},{28,24},{5,1},{9,5},{13... | collective-permute-start | bytes 1572872 | tf_op jit(solution)/shard_map/ppermute | solution.py:306
  78.7 0.1 add_bitcast_fusion.places_ref
  78.8 2.6 %collective-permute-done.14.refs_1_ = bf16[256,768]{1,0:T(8,128)(2,1)S(1)} collective-permute-done((bf16[256,768]{1,0:T(8,128)(2,1)S(1)}, bf16[256,768]{1,0:T(8,128)(2,1)S(1)}, u32[]{:S(2)}, u32[]{:S(2)}) %collective-permute-start.14) | collective-permute-done | bytes 393248 | tf_op jit(solution)/shard_map/ppermute | solution.py:317
  81.5 0.4 collective-permute-done.15.refs_3_
  81.9 0.3 copy-done.13
  82.2 0.4 copy-done.14
  82.6 6.9 %shard_map.135 = (bf16[3,64,512]{2,1,0:T(8,128)(2,1)}, bf16[512,512]{1,0:T(8,128)(2,1)}) custom-call(s32[1,1]{1,0:T(1,128)} %bitcast.9.place_ref, s32[1,1]{1,0:T(1,128)} %bitcast.10.side_ref, bf16[256,768]{1,0:T(8,128)(2,1)} %copy-done.9, bf16[256,768]{1,0:T(8,128)(2,1)} %copy-done.13, bf16[256,768]{1,0:T(8,128)(2,1)} %copy-done.10, ...), custom_call_target="tpu_custom_call" | custom-call | flops 1000 | bytes 1000 | tf_op jit(solution)/shard_map/pallas_call | solution.py:42
  89.6 1.0 copy-done.3
  90.6 1.0 shard_map.137
  91.7 1.0 shard_map.136
  92.7 0.6 collective-permute-start.18
  93.3 1.5 %collective-permute-start.21 = (bf16[256,256]{1,0:T(8,128)(2,1)S(1)}, bf16[256,256]{1,0:T(8,128)(2,1)S(1)}, u32[]{:S(2)}, u32[]{:S(2)}) collective-permute-start(bf16[256,256]{1,0:T(8,128)(2,1)S(1)} %get-tuple-element.56), channel_id=1, source_target_pairs={{0,2},{1,3},{2,0},{3,1},{4,6},{5,7},{6,4},{7,5},{8,10},{9,11},{10,... | collective-permute-start | bytes 393224 | tf_op jit(solution)/shard_map/ppermute | solution.py:312
  94.9 0.5 collective-permute-start.20
  95.4 4.3 %collective-permute-done.21.far_ref = bf16[256,256]{1,0:T(8,128)(2,1)S(1)} collective-permute-done((bf16[256,256]{1,0:T(8,128)(2,1)S(1)}, bf16[256,256]{1,0:T(8,128)(2,1)S(1)}, u32[]{:S(2)}, u32[]{:S(2)}) %collective-permute-start.21) | collective-permute-done | bytes 131104 | tf_op jit(solution)/shard_map/ppermute | solution.py:312
  99.8 2.0 %shard_map.138.refs_0_ = bf16[256,256]{1,0:T(8,128)(2,1)S(1)} custom-call(f32[2,2]{1,0:T(2,128)S(1)} %reshape.19.edge_ref, bf16[512,256]{1,0:T(8,128)(2,1)S(1)} %copy-done.6, bf16[512,256]{1,0:T(8,128)(2,1)S(1)} %get-tuple-element.43.keep_ref, bf16[512,256]{1,0:T(8,128)(2,1)S(1)} %collective-permute-done.18.near_ref, ...), custom_call_target="tpu_custom_call" | custom-call | flops 402653184 | bytes 2097152 | tf_op jit(solution)/shard_map/pallas_call | solution.py:42
  101.8 2.7 %shard_map.139 = bf16[512,256]{1,0:T(8,128)(2,1)} custom-call(f32[2,2]{1,0:T(2,128)S(1)} %reshape.19.edge_ref, bf16[512,256]{1,0:T(8,128)(2,1)S(1)} %copy-done.6, bf16[512,256]{1,0:T(8,128)(2,1)S(1)} %get-tuple-element.43.keep_ref, bf16[512,256]{1,0:T(8,128)(2,1)S(1)} %collective-permute-done.18.near_ref, ...), custom_call_target="tpu_custom_call" | custom-call | flops 402653184 | bytes 2097152 | tf_op jit(solution)/shard_map/pallas_call | solution.py:42
  (53 shorter events, 0.6 us)
Async XLA Ops:
  0.6 9.9 %copy-start.5 = (bf16[512,256]{1,0:T(8,128)(2,1)S(1)}, bf16[512,256]{1,0:T(8,128)(2,1)}, u32[]{:S(2)}) copy-start(bf16[512,256]{1,0:T(8,128)(2,1)} %values_ref.7) | copy-start | bytes 786436
  0.6 9.9 %copy-start.4 = (bf16[512,256]{1,0:T(8,128)(2,1)S(1)}, bf16[512,256]{1,0:T(8,128)(2,1)}, u32[]{:S(2)}) copy-start(bf16[512,256]{1,0:T(8,128)(2,1)} %keys_ref.7) | copy-start | bytes 786436
  0.7 9.9 %copy-start.7 = (bf16[512,256]{1,0:T(8,128)(2,1)S(1)}, bf16[512,256]{1,0:T(8,128)(2,1)}, u32[]{:S(2)}) copy-start(bf16[512,256]{1,0:T(8,128)(2,1)} %queries_ref.5) | copy-start | bytes 786436
  0.7 12.1 %copy-start.1 = (bf16[512,256]{1,0:T(8,128)(2,1)S(1)}, bf16[512,256]{1,0:T(8,128)(2,1)}, u32[]{:S(2)}) copy-start(bf16[512,256]{1,0:T(8,128)(2,1)} %keys_ref.9) | copy-start | bytes 786436
  0.7 12.8 %copy-start.2 = (bf16[512,256]{1,0:T(8,128)(2,1)S(1)}, bf16[512,256]{1,0:T(8,128)(2,1)}, u32[]{:S(2)}) copy-start(bf16[512,256]{1,0:T(8,128)(2,1)} %values_ref.9) | copy-start | bytes 786436
  7.5 13.1 %copy-start.12 = (bf16[256,768]{1,0:T(8,128)(2,1)S(1)}, bf16[256,768]{1,0:T(8,128)(2,1)}, u32[]{:S(2)}) copy-start(bf16[256,768]{1,0:T(8,128)(2,1)} %get-tuple-element.25) | copy-start | bytes 1179652
  7.5 13.1 %collective-permute-start = (bf16[256,768]{1,0:T(8,128)(2,1)}, bf16[256,768]{1,0:T(8,128)(2,1)S(1)}, u32[]{:S(2)}, u32[]{:S(2)}) collective-permute-start(bf16[256,768]{1,0:T(8,128)(2,1)} %get-tuple-element.26), channel_id=1, source_target_pairs={{0,4},{4,0},{8,12},{12,8},{16,20},{20,16},{24,28},{28,24},{1,5},{5... | collective-permute-start | bytes 1179656 | tf_op jit(solution)/shard_map/ppermute | solution.py:317
  10.5 12.4 %copy-start.11 = (bf16[256,768]{1,0:T(8,128)(2,1)S(1)}, bf16[256,768]{1,0:T(8,128)(2,1)}, u32[]{:S(2)}) copy-start(bf16[256,768]{1,0:T(8,128)(2,1)} %get-tuple-element.27) | copy-start | bytes 1179652
  10.6 17.7 %collective-permute-start.8 = (bf16[1536,128]{1,0:T(8,128)(2,1)S(1)}, bf16[1536,128]{1,0:T(8,128)(2,1)S(1)}, u32[]{:S(2)}, u32[]{:S(2)}) collective-permute-start(bf16[1536,128]{1,0:T(8,128)(2,1)S(1)} %shard_map.132), channel_id=1, source_target_pairs={{0,4},{4,0},{8,12},{12,8},{16,20},{20,16},{24,28},{28,24},{1,5},{5... | collective-permute-start | bytes 1179656 | tf_op jit(solution)/shard_map/ppermute | solution.py:317
  10.7 12.2 %collective-permute-start.4 = (bf16[256,768]{1,0:T(8,128)(2,1)}, bf16[256,768]{1,0:T(8,128)(2,1)S(1)}, u32[]{:S(2)}, u32[]{:S(2)}) collective-permute-start(bf16[256,768]{1,0:T(8,128)(2,1)} %get-tuple-element.28), channel_id=1, source_target_pairs={{0,8},{4,12},{8,0},{12,4},{16,24},{20,28},{24,16},{28,20},{1,9},{5... | collective-permute-start | bytes 1179656 | tf_op jit(solution)/shard_map/ppermute | solution.py:317
  20.8 8.3 %collective-permute-start.1 = (bf16[128,768]{1,0:T(8,128)(2,1)S(1)}, bf16[128,768]{1,0:T(8,128)(2,1)S(1)}, u32[]{:S(2)}, u32[]{:S(2)}) collective-permute-start(bf16[128,768]{1,0:T(8,128)(2,1)S(1)} %get-tuple-element.50), channel_id=1, source_target_pairs={{0,8},{4,12},{8,0},{12,4},{16,24},{20,28},{24,16},{28,20},{1,9},{5... | collective-permute-start | bytes 589832 | tf_op jit(solution)/shard_map/ppermute | solution.py:317
  23.0 10.7 %collective-permute-start.5 = (bf16[128,768]{1,0:T(8,128)(2,1)S(1)}, bf16[128,768]{1,0:T(8,128)(2,1)S(1)}, u32[]{:S(2)}, u32[]{:S(2)}) collective-permute-start(bf16[128,768]{1,0:T(8,128)(2,1)S(1)} %get-tuple-element.48), channel_id=1, source_target_pairs={{0,16},{4,20},{8,24},{12,28},{16,0},{20,4},{24,8},{28,12},{1,17},{... | collective-permute-start | bytes 589832 | tf_op jit(solution)/shard_map/ppermute | solution.py:317
  29.1 14.1 %collective-permute-start.2 = (bf16[64,768]{1,0:T(8,128)(2,1)S(1)}, bf16[64,768]{1,0:T(8,128)(2,1)S(1)}, u32[]{:S(2)}, u32[]{:S(2)}) collective-permute-start(bf16[64,768]{1,0:T(8,128)(2,1)S(1)} %get-tuple-element.54), channel_id=1, source_target_pairs={{0,16},{4,20},{8,24},{12,28},{16,0},{20,4},{24,8},{28,12},{1,17},{... | collective-permute-start | bytes 294920 | tf_op jit(solution)/shard_map/ppermute | solution.py:317
  33.7 13.6 %collective-permute-start.6 = (bf16[64,768]{1,0:T(8,128)(2,1)S(1)}, bf16[64,768]{1,0:T(8,128)(2,1)S(1)}, u32[]{:S(2)}, u32[]{:S(2)}) collective-permute-start(bf16[64,768]{1,0:T(8,128)(2,1)S(1)} %get-tuple-element.52), channel_id=1, source_target_pairs={{0,4},{4,0},{8,12},{12,8},{16,20},{20,16},{24,28},{28,24},{1,5},{5... | collective-permute-start | bytes 294920 | tf_op jit(solution)/shard_map/ppermute | solution.py:317
  35.3 17.7 %collective-permute-start.9 = (bf16[1024,128]{1,0:T(8,128)(2,1)S(1)}, bf16[1024,128]{1,0:T(8,128)(2,1)S(1)}, u32[]{:S(2)}, u32[]{:S(2)}) collective-permute-start(bf16[1024,128]{1,0:T(8,128)(2,1)S(1)} %get-tuple-element.31.high_ref), channel_id=1, source_target_pairs={{0,8},{4,12},{8,16},{12,20},{16,24},{20,28},{1,9},{5,13},{9,17},{1... | collective-permute-start | bytes 786440 | tf_op jit(solution)/shard_map/ppermute | solution.py:306
  39.5 13.5 %collective-permute-start.10 = (bf16[1024,128]{1,0:T(8,128)(2,1)S(1)}, bf16[1024,128]{1,0:T(8,128)(2,1)S(1)}, u32[]{:S(2)}, u32[]{:S(2)}) collective-permute-start(bf16[1024,128]{1,0:T(8,128)(2,1)S(1)} %get-tuple-element.32.low_ref), channel_id=1, source_target_pairs={{8,0},{12,4},{16,8},{20,12},{24,16},{28,20},{9,1},{13,5},{17,9},{2... | collective-permute-start | bytes 786440 | tf_op jit(solution)/shard_map/ppermute | solution.py:306
  40.8 12.2 %collective-permute-start.11 = (bf16[1024,256]{1,0:T(8,128)(2,1)}, bf16[1024,256]{1,0:T(8,128)(2,1)S(1)}, u32[]{:S(2)}, u32[]{:S(2)}) collective-permute-start(bf16[1024,256]{1,0:T(8,128)(2,1)} %constant_dynamic-update-slice_fusion), channel_id=1, source_target_pairs={{0,4},{4,8},{8,12},{12,16},{16,20},{20,24},{24,28},{1,5},{5,9},{9,... | collective-permute-start | bytes 1572872 | tf_op jit(solution)/shard_map/ppermute | solution.py:306
  43.3 7.1 %collective-permute-start.3 = (bf16[64,768]{1,0:T(8,128)(2,1)S(1)}, bf16[64,768]{1,0:T(8,128)(2,1)S(1)}, u32[]{:S(2)}, u32[]{:S(2)}) collective-permute-start(bf16[64,768]{1,0:T(8,128)(2,1)S(1)} %add_convert_fusion.5), channel_id=1, source_target_pairs={{0,16},{4,20},{8,24},{12,28},{16,0},{20,4},{24,8},{28,12},{1,17},{... | collective-permute-start | bytes 294920 | tf_op jit(solution)/shard_map/ppermute | solution.py:317
  47.3 5.7 %collective-permute-start.7 = (bf16[64,768]{1,0:T(8,128)(2,1)S(1)}, bf16[64,768]{1,0:T(8,128)(2,1)S(1)}, u32[]{:S(2)}, u32[]{:S(2)}) collective-permute-start(bf16[64,768]{1,0:T(8,128)(2,1)S(1)} %add_convert_fusion.4), channel_id=1, source_target_pairs={{0,4},{4,0},{8,12},{12,8},{16,20},{20,16},{24,28},{28,24},{1,5},{5... | collective-permute-start | bytes 294920 | tf_op jit(solution)/shard_map/ppermute | solution.py:317
  53.0 16.1 %collective-permute-start.12 = (bf16[128,768]{1,0:T(8,128)(2,1)S(1)}, bf16[128,768]{1,0:T(8,128)(2,1)S(1)}, u32[]{:S(2)}, u32[]{:S(2)}) collective-permute-start(bf16[128,768]{1,0:T(8,128)(2,1)S(1)} %pad_maximum_fusion.2), channel_id=1, source_target_pairs={{0,8},{4,12},{8,0},{12,4},{16,24},{20,28},{24,16},{28,20},{1,9},{5... | collective-permute-start | bytes 589832 | tf_op jit(solution)/shard_map/ppermute | solution.py:317
  60.7 9.6 %collective-permute-start.13 = (bf16[128,768]{1,0:T(8,128)(2,1)S(1)}, bf16[128,768]{1,0:T(8,128)(2,1)S(1)}, u32[]{:S(2)}, u32[]{:S(2)}) collective-permute-start(bf16[128,768]{1,0:T(8,128)(2,1)S(1)} %pad_maximum_fusion.3), channel_id=1, source_target_pairs={{0,16},{4,20},{8,24},{12,28},{16,0},{20,4},{24,8},{28,12},{1,17},{... | collective-permute-start | bytes 589832 | tf_op jit(solution)/shard_map/ppermute | solution.py:317
  69.1 7.0 %copy-start.8 = (bf16[512,128]{1,0:T(8,128)(2,1)}, bf16[512,128]{1,0:T(8,128)(2,1)S(1)}, u32[]{:S(2)}) copy-start(bf16[512,128]{1,0:T(8,128)(2,1)S(1)} %get-tuple-element.36.refs_5_) | copy-start | bytes 393220
  69.1 8.2 %collective-permute-start.16 = (bf16[512,128]{1,0:T(8,128)(2,1)S(1)}, bf16[512,128]{1,0:T(8,128)(2,1)S(1)}, u32[]{:S(2)}, u32[]{:S(2)}) collective-permute-start(bf16[512,128]{1,0:T(8,128)(2,1)S(1)} %get-tuple-element.39), channel_id=1, source_target_pairs={{0,4},{4,0},{8,12},{12,8},{16,20},{20,16},{24,28},{28,24},{1,5},{5... | collective-permute-start | bytes 393224 | tf_op jit(solution)/shard_map/ppermute | solution.py:317
  69.2 12.7 %copy-start.9 = (bf16[256,768]{1,0:T(8,128)(2,1)}, bf16[256,768]{1,0:T(8,128)(2,1)S(1)}, u32[]{:S(2)}) copy-start(bf16[256,768]{1,0:T(8,128)(2,1)S(1)} %pad_maximum_fusion.refs_0_) | copy-start | bytes 1179652
  70.4 11.5 %copy-start.10 = (bf16[256,768]{1,0:T(8,128)(2,1)}, bf16[256,768]{1,0:T(8,128)(2,1)S(1)}, u32[]{:S(2)}) copy-start(bf16[256,768]{1,0:T(8,128)(2,1)S(1)} %pad_maximum_fusion.1.refs_2_) | copy-start | bytes 1179652
  70.4 11.0 %collective-permute-start.14 = (bf16[256,768]{1,0:T(8,128)(2,1)S(1)}, bf16[256,768]{1,0:T(8,128)(2,1)S(1)}, u32[]{:S(2)}, u32[]{:S(2)}) collective-permute-start(bf16[256,768]{1,0:T(8,128)(2,1)S(1)} %pad_maximum_fusion.refs_0_), channel_id=1, source_target_pairs={{0,4},{4,0},{8,12},{12,8},{16,20},{20,16},{24,28},{28,24},{1,5},{5... | collective-permute-start | bytes 1179656 | tf_op jit(solution)/shard_map/ppermute | solution.py:317
  71.3 10.5 %collective-permute-start.15 = (bf16[256,768]{1,0:T(8,128)(2,1)S(1)}, bf16[256,768]{1,0:T(8,128)(2,1)S(1)}, u32[]{:S(2)}, u32[]{:S(2)}) collective-permute-start(bf16[256,768]{1,0:T(8,128)(2,1)S(1)} %pad_maximum_fusion.1.refs_2_), channel_id=1, source_target_pairs={{0,8},{4,12},{8,0},{12,4},{16,24},{20,28},{24,16},{28,20},{1,9},{5... | collective-permute-start | bytes 1179656 | tf_op jit(solution)/shard_map/ppermute | solution.py:317
  77.3 4.6 %copy-start.15 = (bf16[512,128]{1,0:T(8,128)(2,1)}, bf16[512,128]{1,0:T(8,128)(2,1)S(1)}, u32[]{:S(2)}) copy-start(bf16[512,128]{1,0:T(8,128)(2,1)S(1)} %collective-permute-done.16.refs_6_) | copy-start | bytes 393220
  77.3 14.5 %collective-permute-start.17 = (bf16[1024,256]{1,0:T(8,128)(2,1)}, bf16[1024,256]{1,0:T(8,128)(2,1)S(1)}, u32[]{:S(2)}, u32[]{:S(2)}) collective-permute-start(bf16[1024,256]{1,0:T(8,128)(2,1)} %constant_dynamic-update-slice_fusion), channel_id=1, source_target_pairs={{4,0},{8,4},{12,8},{16,12},{20,16},{24,20},{28,24},{5,1},{9,5},{13... | collective-permute-start | bytes 1572872 | tf_op jit(solution)/shard_map/ppermute | solution.py:306
  81.5 0.7 copy-start.13
  81.9 0.8 copy-start.14
  82.6 6.9 %copy-start = (bf16[512,1024]{1,0:T(8,128)(2,1)S(1)}, bf16[512,1024]{1,0:T(8,128)(2,1)}, u32[]{:S(2)}) copy-start(bf16[512,1024]{1,0:T(8,128)(2,1)} %map_ref.3) | copy-start | bytes 3145732
  89.6 1.0 copy-start.3
  91.6 8.1 %copy-start.6 = (bf16[512,256]{1,0:T(8,128)(2,1)S(1)}, bf16[512,256]{1,0:T(8,128)(2,1)}, u32[]{:S(2)}) copy-start(bf16[512,256]{1,0:T(8,128)(2,1)} %queries_ref.7) | copy-start | bytes 786436
  91.6 1.6 %collective-permute-start.19 = (bf16[512,256]{1,0:T(8,128)(2,1)S(1)}, bf16[512,256]{1,0:T(8,128)(2,1)S(1)}, u32[]{:S(2)}, u32[]{:S(2)}) collective-permute-start(bf16[512,256]{1,0:T(8,128)(2,1)S(1)} %get-tuple-element.46), channel_id=1, source_target_pairs={{0,1},{1,0},{2,3},{3,2},{4,5},{5,4},{6,7},{7,6},{8,9},{9,8},{10,11... | collective-permute-start | bytes 786440 | tf_op jit(solution)/shard_map/ppermute | solution.py:312
  92.7 2.7 %collective-permute-start.18 = (bf16[512,256]{1,0:T(8,128)(2,1)S(1)}, bf16[512,256]{1,0:T(8,128)(2,1)S(1)}, u32[]{:S(2)}, u32[]{:S(2)}) collective-permute-start(bf16[512,256]{1,0:T(8,128)(2,1)S(1)} %get-tuple-element.44), channel_id=1, source_target_pairs={{0,1},{1,0},{2,3},{3,2},{4,5},{5,4},{6,7},{7,6},{8,9},{9,8},{10,11... | collective-permute-start | bytes 786440 | tf_op jit(solution)/shard_map/ppermute | solution.py:312
  93.3 6.4 %collective-permute-start.21 = (bf16[256,256]{1,0:T(8,128)(2,1)S(1)}, bf16[256,256]{1,0:T(8,128)(2,1)S(1)}, u32[]{:S(2)}, u32[]{:S(2)}) collective-permute-start(bf16[256,256]{1,0:T(8,128)(2,1)S(1)} %get-tuple-element.56), channel_id=1, source_target_pairs={{0,2},{1,3},{2,0},{3,1},{4,6},{5,7},{6,4},{7,5},{8,10},{9,11},{10,... | collective-permute-start | bytes 393224 | tf_op jit(solution)/shard_map/ppermute | solution.py:312
  94.9 6.9 %collective-permute-start.20 = (bf16[256,256]{1,0:T(8,128)(2,1)S(1)}, bf16[256,256]{1,0:T(8,128)(2,1)S(1)}, u32[]{:S(2)}, u32[]{:S(2)}) collective-permute-start(bf16[256,256]{1,0:T(8,128)(2,1)S(1)} %get-tuple-element.57), channel_id=1, source_target_pairs={{0,2},{1,3},{2,0},{3,1},{4,6},{5,7},{6,4},{7,5},{8,10},{9,11},{10,... | collective-permute-start | bytes 393224 | tf_op jit(solution)/shard_map/ppermute | solution.py:312

commit v18 on v17

--- a/solution.py
+++ b/solution.py
@@ -14,7 +14,7 @@
 FAST_DIM = 512
 FAST_HIDDEN = 512
 TILE = 128
-QUERY_TILE = 256
+ROW_TILE = 256
 VMEM_LIMIT = 24 * 1024 * 1024
 VMEM_MOST = 60 * 1024 * 1024
 
@@ -105,19 +105,19 @@
 def attend_rows(edge_prev, edge_next, query_tile, keys_prev, keys_own, keys_next,
                 values_prev, values_own, values_next):
     scale = math.log2(math.e) / math.sqrt(HEAD_DIM)
-    row = lax.broadcasted_iota(jnp.int32, (QUERY_TILE, QUERY_TILE), 0)
-    col = lax.broadcasted_iota(jnp.int32, (QUERY_TILE, QUERY_TILE), 1)
+    row = lax.broadcasted_iota(jnp.int32, (ROW_TILE, ROW_TILE), 0)
+    col = lax.broadcasted_iota(jnp.int32, (ROW_TILE, ROW_TILE), 1)
     minus = jnp.float32(-jnp.inf)
     score_prev = dot_nt(query_tile, keys_prev)
     score_own = dot_nt(query_tile, keys_own)
     score_next = dot_nt(query_tile, keys_next)
-    parts = [score_prev[:, :QUERY_TILE] + jnp.where(col >= row, edge_prev, minus)]
-    if score_prev.shape[1] > QUERY_TILE:
-        parts.append(score_prev[:, QUERY_TILE:] + edge_prev)
+    parts = [score_prev[:, :ROW_TILE] + jnp.where(col >= row, edge_prev, minus)]
+    if score_prev.shape[1] > ROW_TILE:
+        parts.append(score_prev[:, ROW_TILE:] + edge_prev)
     parts.append(score_own)
-    if score_next.shape[1] > QUERY_TILE:
-        parts.append(score_next[:, :-QUERY_TILE] + edge_next)
-    parts.append(score_next[:, -QUERY_TILE:] + jnp.where(col <= row, edge_next, minus))
+    if score_next.shape[1] > ROW_TILE:
+        parts.append(score_next[:, :-ROW_TILE] + edge_next)
+    parts.append(score_next[:, -ROW_TILE:] + jnp.where(col <= row, edge_next, minus))
     scores = jnp.concatenate(parts, axis=1)
     highest = jnp.max(scores, axis=1, keepdims=True)
     weights = jnp.exp2((scores - highest) * scale)
@@ -171,10 +171,10 @@
         base = (side if turn == 0 else 1 - side) * count
 
         def span(ref, low, length):
-            return ref[pl.ds(pl.multiple_of(base + low, QUERY_TILE), length), :]
-
-        for index in range(count // QUERY_TILE):
-            low, high = index * QUERY_TILE, (index + 1) * QUERY_TILE
+            return ref[pl.ds(pl.multiple_of(base + low, ROW_TILE), length), :]
+
+        for index in range(count // ROW_TILE):
+            low, high = index * ROW_TILE, (index + 1) * ROW_TILE
             query = queries_ref[low:high, pl.ds(start, HEAD_DIM)] if turn == 0 else other_ref[low:high, :]
             out_ref[low:high, :] = attend_rows(
                 edge_ref[turn, 0], edge_ref[turn, 1], query,
@@ -193,8 +193,8 @@
     offset = half if done_refs else 0
     if done_refs:
         out_ref[:half, :] = done_refs[0][...]
-    for low in range(offset, offset + half, QUERY_TILE):
-        high = low + QUERY_TILE
+    for low in range(offset, offset + half, ROW_TILE):
+        high = low + ROW_TILE
         rows = slice(low, high)
         mixed = (
             keep_ref[rows, :].astype(F32)
@@ -277,8 +277,8 @@
         copy.wait()
     own_map = map_ref[pl.ds(pl.multiple_of(side * HEAD_DIM, HEAD_DIM), HEAD_DIM), :]
     other_map = map_ref[pl.ds(pl.multiple_of((1 - side) * HEAD_DIM, HEAD_DIM), HEAD_DIM), :]
-    for low in range(0, keep_ref.shape[0], TILE):
-        rows = slice(low, low + TILE)
+    for low in range(0, keep_ref.shape[0], ROW_TILE):
+        rows = slice(low, low + ROW_TILE)
         own = keep_ref[rows, :].astype(F32)
         other = other_ref[rows, :].astype(F32)
         total = jnp.sum(own * own + other * other, axis=1, keepdims=True)
@@ -390,14 +390,14 @@
     whole = pl.BlockSpec(memory_space=pltpu.VMEM)
     gradients = pl.pallas_call(
         functools.partial(gradient_kernel, orders),
-        grid=(hidden_size // TILE,),
+        grid=(hidden_size // ROW_TILE,),
         out_shape=out_shapes,
         in_specs=[
             pl.BlockSpec(memory_space=pltpu.SMEM),
             whole,
             whole,
             whole,
-            pl.BlockSpec((3, TILE, fast_width), lambda turn: (0, turn, 0)),
+            pl.BlockSpec((3, ROW_TILE, fast_width), lambda turn: (0, turn, 0)),
         ],
         out_specs=[whole] * len(out_shapes),
         scratch_shapes=[pltpu.VMEM((hidden_size, chunk_width), BF16)] * 2,

time: 105 us -> 102 us (0.971)
  Pallas kernels: 23.7 us -> 21.2 us
    pallas_call x1, Pallas kernels: 6.86 us -> 5.47 us  [local(): pl.pallas_call(functools.partial(gradient_kernel, orders), grid=(hidden_s...]
    pallas_call x8, Pallas kernels: 16.8 us -> 15.7 us  [call(): pl.pallas_call(body, out_shape=out_shapes, in_specs=in_specs, out_specs=j...]
where the time goes in v18:
time: 102 us
  starting transfers between devices  51.4 us (50%)
  waiting for transfers between devices  24.5 us (24%)
  Pallas kernels  21.2 us (21%)
  local copies, waits for them, and re-layouts  3.4 us (3%)
    ppermute x14, starting transfers between devices, seq_swap(): lax.ppermute(value, 'seq', [(i, i ^ step) for i in range(lax.axis_size('s...  39.3 us
    ppermute x14, waiting for transfers between devices, seq_swap(): lax.ppermute(value, 'seq', [(i, i ^ step) for i in range(lax.axis_size('s...  20.1 us
    pallas_call x8, Pallas kernels, call(): pl.pallas_call(body, out_shape=out_shapes, in_specs=in_specs, out_specs=j...  15.7 us
    ppermute x4, starting transfers between devices, seq_shift(): lax.ppermute(value, 'seq', [(i, i + step) for i in range(peers) if 0 <= i...  9.33 us
    pallas_call x1, Pallas kernels, local(): pl.pallas_call(functools.partial(gradient_kernel, orders), grid=(hidden_s...  5.47 us
    ppermute x4, waiting for transfers between devices, head_swap(): lax.ppermute(value, 'head', [(i, i ^ bit) for i in range(lax.axis_size('h...  4.32 us
    ppermute x4, starting transfers between devices, head_swap(): lax.ppermute(value, 'head', [(i, i ^ bit) for i in range(lax.axis_size('h...  2.71 us
    unnamed x33, local copies, waits for them, and re-layouts  2.59 us
  transfers between devices with their start and end apart: 22, of which 10 were waited for; matrix products, arithmetic and copies ran while one was open for 2% of the time, Pallas kernels for 13%

profile of v18, /device:TPU:0, one launch (start us, length us, event | category | flops | bytes accessed | tf_op | source)
XLA Modules:
  0.0 102.0 jit_solution(13949304373016479131)
XLA Ops:
  0.7 5.5 %shard_map.131 = (bf16[256,768]{1,0:T(8,128)(2,1)}, bf16[256,768]{1,0:T(8,128)(2,1)}, bf16[256,768]{1,0:T(8,128)(2,1)}, bf16[256,768]{1,0:T(8,128)(2,1)}) custom-call(s32[1,1]{1,0:T(1,128)} %bitcast.9.place_ref, f32[1,512]{1,0:T(1,128)} %bitcast.23, bf16[512,512]{1,0:T(8,128)(2,1)} %keys_ref.5, bf16[512,512]{1,0:T(8,128)(2,1)} %values_ref.5, ...), custom_call_target="tpu_custom_call" | custom-call | flops 1000 | bytes 1000 | tf_op jit(solution)/shard_map/pallas_call | solution.py:391
  6.2 3.0 %collective-permute-start = (bf16[256,768]{1,0:T(8,128)(2,1)}, bf16[256,768]{1,0:T(8,128)(2,1)S(1)}, u32[]{:S(2)}, u32[]{:S(2)}) collective-permute-start(bf16[256,768]{1,0:T(8,128)(2,1)} %get-tuple-element.26), channel_id=1, source_target_pairs={{0,4},{4,0},{8,12},{12,8},{16,20},{20,16},{24,28},{28,24},{1,5},{5... | collective-permute-start | bytes 1179656 | tf_op jit(solution)/shard_map/ppermute | solution.py:317
  9.1 0.1 shard_map.132
  9.2 0.1 collective-permute-start.8
  9.3 2.0 %collective-permute-start.4 = (bf16[256,768]{1,0:T(8,128)(2,1)}, bf16[256,768]{1,0:T(8,128)(2,1)S(1)}, u32[]{:S(2)}, u32[]{:S(2)}) collective-permute-start(bf16[256,768]{1,0:T(8,128)(2,1)} %get-tuple-element.28), channel_id=1, source_target_pairs={{0,8},{4,12},{8,0},{12,4},{16,24},{20,28},{24,16},{28,20},{1,9},{5... | collective-permute-start | bytes 1179656 | tf_op jit(solution)/shard_map/ppermute | solution.py:317
  11.4 0.7 constant_dynamic-update-slice_fusion.1
  12.1 0.7 constant_dynamic-update-slice_fusion
  12.8 6.4 %collective-permute-done = bf16[256,768]{1,0:T(8,128)(2,1)S(1)} collective-permute-done((bf16[256,768]{1,0:T(8,128)(2,1)}, bf16[256,768]{1,0:T(8,128)(2,1)S(1)}, u32[]{:S(2)}, u32[]{:S(2)}) %collective-permute-start) | collective-permute-done | bytes 393248 | tf_op jit(solution)/shard_map/ppermute | solution.py:317
  19.3 0.1 add_convert_fusion.1
  19.4 2.2 %collective-permute-start.1 = (bf16[128,768]{1,0:T(8,128)(2,1)S(1)}, bf16[128,768]{1,0:T(8,128)(2,1)S(1)}, u32[]{:S(2)}, u32[]{:S(2)}) collective-permute-start(bf16[128,768]{1,0:T(8,128)(2,1)S(1)} %get-tuple-element.50), channel_id=1, source_target_pairs={{0,8},{4,12},{8,0},{12,4},{16,24},{20,28},{24,16},{28,20},{1,9},{5... | collective-permute-start | bytes 589832 | tf_op jit(solution)/shard_map/ppermute | solution.py:317
  21.6 0.1 add_convert_fusion
  21.7 2.6 %collective-permute-start.5 = (bf16[128,768]{1,0:T(8,128)(2,1)S(1)}, bf16[128,768]{1,0:T(8,128)(2,1)S(1)}, u32[]{:S(2)}, u32[]{:S(2)}) collective-permute-start(bf16[128,768]{1,0:T(8,128)(2,1)S(1)} %get-tuple-element.48), channel_id=1, source_target_pairs={{0,16},{4,20},{8,24},{12,28},{16,0},{20,4},{24,8},{28,12},{1,17},{... | collective-permute-start | bytes 589832 | tf_op jit(solution)/shard_map/ppermute | solution.py:317
  24.3 2.6 %collective-permute-done.8.other_ref = bf16[1536,128]{1,0:T(8,128)(2,1)S(1)} collective-permute-done((bf16[1536,128]{1,0:T(8,128)(2,1)S(1)}, bf16[1536,128]{1,0:T(8,128)(2,1)S(1)}, u32[]{:S(2)}, u32[]{:S(2)}) %collective-permute-start.8) | collective-permute-done | bytes 393248 | tf_op jit(solution)/shard_map/ppermute | solution.py:317
  26.9 0.8 collective-permute-done.1
  27.7 2.1 %collective-permute-start.2 = (bf16[64,768]{1,0:T(8,128)(2,1)S(1)}, bf16[64,768]{1,0:T(8,128)(2,1)S(1)}, u32[]{:S(2)}, u32[]{:S(2)}) collective-permute-start(bf16[64,768]{1,0:T(8,128)(2,1)S(1)} %get-tuple-element.54), channel_id=1, source_target_pairs={{0,16},{4,20},{8,24},{12,28},{16,0},{20,4},{24,8},{28,12},{1,17},{... | collective-permute-start | bytes 294920 | tf_op jit(solution)/shard_map/ppermute | solution.py:317
  29.9 2.4 %collective-permute-done.5 = bf16[128,768]{1,0:T(8,128)(2,1)S(1)} collective-permute-done((bf16[128,768]{1,0:T(8,128)(2,1)S(1)}, bf16[128,768]{1,0:T(8,128)(2,1)S(1)}, u32[]{:S(2)}, u32[]{:S(2)}) %collective-permute-start.5) | collective-permute-done | bytes 196640 | tf_op jit(solution)/shard_map/ppermute | solution.py:317
  32.4 1.6 %collective-permute-start.6 = (bf16[64,768]{1,0:T(8,128)(2,1)S(1)}, bf16[64,768]{1,0:T(8,128)(2,1)S(1)}, u32[]{:S(2)}, u32[]{:S(2)}) collective-permute-start(bf16[64,768]{1,0:T(8,128)(2,1)S(1)} %get-tuple-element.52), channel_id=1, source_target_pairs={{0,4},{4,0},{8,12},{12,8},{16,20},{20,16},{24,28},{28,24},{1,5},{5... | collective-permute-start | bytes 294920 | tf_op jit(solution)/shard_map/ppermute | solution.py:317
  34.0 4.1 %collective-permute-start.9 = (bf16[1024,128]{1,0:T(8,128)(2,1)S(1)}, bf16[1024,128]{1,0:T(8,128)(2,1)S(1)}, u32[]{:S(2)}, u32[]{:S(2)}) collective-permute-start(bf16[1024,128]{1,0:T(8,128)(2,1)S(1)} %get-tuple-element.31.high_ref), channel_id=1, source_target_pairs={{0,8},{4,12},{8,16},{12,20},{16,24},{20,28},{1,9},{5,13},{9,17},{1... | collective-permute-start | bytes 786440 | tf_op jit(solution)/shard_map/ppermute | solution.py:306
  38.1 1.3 %collective-permute-start.10 = (bf16[1024,128]{1,0:T(8,128)(2,1)S(1)}, bf16[1024,128]{1,0:T(8,128)(2,1)S(1)}, u32[]{:S(2)}, u32[]{:S(2)}) collective-permute-start(bf16[1024,128]{1,0:T(8,128)(2,1)S(1)} %get-tuple-element.32.low_ref), channel_id=1, source_target_pairs={{8,0},{12,4},{16,8},{20,12},{24,16},{28,20},{9,1},{13,5},{17,9},{2... | collective-permute-start | bytes 786440 | tf_op jit(solution)/shard_map/ppermute | solution.py:306
  39.4 2.4 %collective-permute-start.11 = (bf16[1024,256]{1,0:T(8,128)(2,1)}, bf16[1024,256]{1,0:T(8,128)(2,1)S(1)}, u32[]{:S(2)}, u32[]{:S(2)}) collective-permute-start(bf16[1024,256]{1,0:T(8,128)(2,1)} %constant_dynamic-update-slice_fusion), channel_id=1, source_target_pairs={{0,4},{4,8},{8,12},{12,16},{16,20},{20,24},{24,28},{1,5},{5,9},{9,... | collective-permute-start | bytes 1572872 | tf_op jit(solution)/shard_map/ppermute | solution.py:306
  41.9 4.0 %collective-permute-start.3 = (bf16[64,768]{1,0:T(8,128)(2,1)S(1)}, bf16[64,768]{1,0:T(8,128)(2,1)S(1)}, u32[]{:S(2)}, u32[]{:S(2)}) collective-permute-start(bf16[64,768]{1,0:T(8,128)(2,1)S(1)} %add_convert_fusion.5), channel_id=1, source_target_pairs={{0,16},{4,20},{8,24},{12,28},{16,0},{20,4},{24,8},{28,12},{1,17},{... | collective-permute-start | bytes 294920 | tf_op jit(solution)/shard_map/ppermute | solution.py:317
  45.9 3.1 %collective-permute-start.7 = (bf16[64,768]{1,0:T(8,128)(2,1)S(1)}, bf16[64,768]{1,0:T(8,128)(2,1)S(1)}, u32[]{:S(2)}, u32[]{:S(2)}) collective-permute-start(bf16[64,768]{1,0:T(8,128)(2,1)S(1)} %add_convert_fusion.4), channel_id=1, source_target_pairs={{0,4},{4,0},{8,12},{12,8},{16,20},{20,16},{24,28},{28,24},{1,5},{5... | collective-permute-start | bytes 294920 | tf_op jit(solution)/shard_map/ppermute | solution.py:317
  49.0 2.6 %collective-permute-done.7 = bf16[64,768]{1,0:T(8,128)(2,1)S(1)} collective-permute-done((bf16[64,768]{1,0:T(8,128)(2,1)S(1)}, bf16[64,768]{1,0:T(8,128)(2,1)S(1)}, u32[]{:S(2)}, u32[]{:S(2)}) %collective-permute-start.7) | collective-permute-done | bytes 98336 | tf_op jit(solution)/shard_map/ppermute | solution.py:317
  51.7 7.5 %collective-permute-start.12 = (bf16[128,768]{1,0:T(8,128)(2,1)S(1)}, bf16[128,768]{1,0:T(8,128)(2,1)S(1)}, u32[]{:S(2)}, u32[]{:S(2)}) collective-permute-start(bf16[128,768]{1,0:T(8,128)(2,1)S(1)} %pad_maximum_fusion.2), channel_id=1, source_target_pairs={{0,8},{4,12},{8,0},{12,4},{16,24},{20,28},{24,16},{28,20},{1,9},{5... | collective-permute-start | bytes 589832 | tf_op jit(solution)/shard_map/ppermute | solution.py:317
  59.2 0.1 pad_maximum_fusion.4
  59.3 0.1 reshape.19.edge_ref
  59.4 5.3 %collective-permute-start.13 = (bf16[128,768]{1,0:T(8,128)(2,1)S(1)}, bf16[128,768]{1,0:T(8,128)(2,1)S(1)}, u32[]{:S(2)}, u32[]{:S(2)}) collective-permute-start(bf16[128,768]{1,0:T(8,128)(2,1)S(1)} %pad_maximum_fusion.3), channel_id=1, source_target_pairs={{0,16},{4,20},{8,24},{12,28},{16,0},{20,4},{24,8},{28,12},{1,17},{... | collective-permute-start | bytes 589832 | tf_op jit(solution)/shard_map/ppermute | solution.py:317
  64.6 3.0 %shard_map.134 = (bf16[512,128]{1,0:T(8,128)(2,1)S(1)}, bf16[512,128]{1,0:T(8,128)(2,1)S(1)}) custom-call(f32[2,2]{1,0:T(2,128)S(1)} %reshape.19.edge_ref, s32[1,1]{1,0:T(1,128)} %bitcast.10.side_ref, bf16[512,256]{1,0:T(8,128)(2,1)S(1)} %copy-done.7, bf16[1536,128]{1,0:T(8,128)(2,1)S(1)} %collective-permute-done.8.other_ref, ...), custom_call_target="tpu_custom_call" | custom-call | flops 805306368 | bytes 2097152 | tf_op jit(solution)/shard_map/pallas_call | solution.py:42
  67.8 1.2 %collective-permute-done.13 = bf16[128,768]{1,0:T(8,128)(2,1)S(1)} collective-permute-done((bf16[128,768]{1,0:T(8,128)(2,1)S(1)}, bf16[128,768]{1,0:T(8,128)(2,1)S(1)}, u32[]{:S(2)}, u32[]{:S(2)}) %collective-permute-start.13) | collective-permute-done | bytes 196640 | tf_op jit(solution)/shard_map/ppermute | solution.py:317
  69.0 0.9 collective-permute-start.14
  70.0 4.8 %collective-permute-start.15 = (bf16[256,768]{1,0:T(8,128)(2,1)S(1)}, bf16[256,768]{1,0:T(8,128)(2,1)S(1)}, u32[]{:S(2)}, u32[]{:S(2)}) collective-permute-start(bf16[256,768]{1,0:T(8,128)(2,1)S(1)} %pad_maximum_fusion.1.refs_2_), channel_id=1, source_target_pairs={{0,8},{4,12},{8,0},{12,4},{16,24},{20,28},{24,16},{28,20},{1,9},{5... | collective-permute-start | bytes 1179656 | tf_op jit(solution)/shard_map/ppermute | solution.py:317
  74.7 1.1 %collective-permute-done.16.refs_6_ = bf16[512,128]{1,0:T(8,128)(2,1)S(1)} collective-permute-done((bf16[512,128]{1,0:T(8,128)(2,1)S(1)}, bf16[512,128]{1,0:T(8,128)(2,1)S(1)}, u32[]{:S(2)}, u32[]{:S(2)}) %collective-permute-start.16) | collective-permute-done | bytes 131104 | tf_op jit(solution)/shard_map/ppermute | solution.py:317
  75.9 1.5 %collective-permute-start.17 = (bf16[1024,256]{1,0:T(8,128)(2,1)}, bf16[1024,256]{1,0:T(8,128)(2,1)S(1)}, u32[]{:S(2)}, u32[]{:S(2)}) collective-permute-start(bf16[1024,256]{1,0:T(8,128)(2,1)} %constant_dynamic-update-slice_fusion), channel_id=1, source_target_pairs={{4,0},{8,4},{12,8},{16,12},{20,16},{24,20},{28,24},{5,1},{9,5},{13... | collective-permute-start | bytes 1572872 | tf_op jit(solution)/shard_map/ppermute | solution.py:306
  77.4 0.1 add_bitcast_fusion.places_ref
  77.4 2.6 %collective-permute-done.14.refs_1_ = bf16[256,768]{1,0:T(8,128)(2,1)S(1)} collective-permute-done((bf16[256,768]{1,0:T(8,128)(2,1)S(1)}, bf16[256,768]{1,0:T(8,128)(2,1)S(1)}, u32[]{:S(2)}, u32[]{:S(2)}) %collective-permute-start.14) | collective-permute-done | bytes 393248 | tf_op jit(solution)/shard_map/ppermute | solution.py:317
  80.1 0.4 collective-permute-done.15.refs_3_
  80.5 0.3 copy-done.13
  80.8 0.4 copy-done.14
  81.2 5.8 %shard_map.135 = (bf16[3,64,512]{2,1,0:T(8,128)(2,1)}, bf16[512,512]{1,0:T(8,128)(2,1)}) custom-call(s32[1,1]{1,0:T(1,128)} %bitcast.9.place_ref, s32[1,1]{1,0:T(1,128)} %bitcast.10.side_ref, bf16[256,768]{1,0:T(8,128)(2,1)} %copy-done.9, bf16[256,768]{1,0:T(8,128)(2,1)} %copy-done.13, bf16[256,768]{1,0:T(8,128)(2,1)} %copy-done.10, ...), custom_call_target="tpu_custom_call" | custom-call | flops 1000 | bytes 1000 | tf_op jit(solution)/shard_map/pallas_call | solution.py:42
  87.1 1.0 %copy-done.3 = bf16[512,512]{1,0:T(8,128)(2,1)S(1)} copy-done((bf16[512,512]{1,0:T(8,128)(2,1)S(1)}, bf16[512,512]{1,0:T(8,128)(2,1)}, u32[]{:S(2)}) %copy-start.3) | copy-done | bytes 524312
  88.1 1.0 shard_map.137
  89.2 1.0 shard_map.136
  90.2 0.6 collective-permute-start.18
  90.9 1.5 %collective-permute-start.21 = (bf16[256,256]{1,0:T(8,128)(2,1)S(1)}, bf16[256,256]{1,0:T(8,128)(2,1)S(1)}, u32[]{:S(2)}, u32[]{:S(2)}) collective-permute-start(bf16[256,256]{1,0:T(8,128)(2,1)S(1)} %get-tuple-element.56), channel_id=1, source_target_pairs={{0,2},{1,3},{2,0},{3,1},{4,6},{5,7},{6,4},{7,5},{8,10},{9,11},{10,... | collective-permute-start | bytes 393224 | tf_op jit(solution)/shard_map/ppermute | solution.py:312
  92.4 0.5 collective-permute-start.20
  93.0 4.3 %collective-permute-done.21.far_ref = bf16[256,256]{1,0:T(8,128)(2,1)S(1)} collective-permute-done((bf16[256,256]{1,0:T(8,128)(2,1)S(1)}, bf16[256,256]{1,0:T(8,128)(2,1)S(1)}, u32[]{:S(2)}, u32[]{:S(2)}) %collective-permute-start.21) | collective-permute-done | bytes 131104 | tf_op jit(solution)/shard_map/ppermute | solution.py:312
  97.3 2.0 %shard_map.138.refs_0_ = bf16[256,256]{1,0:T(8,128)(2,1)S(1)} custom-call(f32[2,2]{1,0:T(2,128)S(1)} %reshape.19.edge_ref, bf16[512,256]{1,0:T(8,128)(2,1)S(1)} %copy-done.6, bf16[512,256]{1,0:T(8,128)(2,1)S(1)} %get-tuple-element.43.keep_ref, bf16[512,256]{1,0:T(8,128)(2,1)S(1)} %collective-permute-done.18.near_ref, ...), custom_call_target="tpu_custom_call" | custom-call | flops 402653184 | bytes 2097152 | tf_op jit(solution)/shard_map/pallas_call | solution.py:42
  99.3 2.7 %shard_map.139 = bf16[512,256]{1,0:T(8,128)(2,1)} custom-call(f32[2,2]{1,0:T(2,128)S(1)} %reshape.19.edge_ref, bf16[512,256]{1,0:T(8,128)(2,1)S(1)} %copy-done.6, bf16[512,256]{1,0:T(8,128)(2,1)S(1)} %get-tuple-element.43.keep_ref, bf16[512,256]{1,0:T(8,128)(2,1)S(1)} %collective-permute-done.18.near_ref, ...), custom_call_target="tpu_custom_call" | custom-call | flops 402653184 | bytes 2097152 | tf_op jit(solution)/shard_map/pallas_call | solution.py:42
  (53 shorter events, 0.6 us)
Async XLA Ops:
  0.6 8.5 %copy-start.5 = (bf16[512,256]{1,0:T(8,128)(2,1)S(1)}, bf16[512,256]{1,0:T(8,128)(2,1)}, u32[]{:S(2)}) copy-start(bf16[512,256]{1,0:T(8,128)(2,1)} %values_ref.7) | copy-start | bytes 786436
  0.6 8.5 %copy-start.4 = (bf16[512,256]{1,0:T(8,128)(2,1)S(1)}, bf16[512,256]{1,0:T(8,128)(2,1)}, u32[]{:S(2)}) copy-start(bf16[512,256]{1,0:T(8,128)(2,1)} %keys_ref.7) | copy-start | bytes 786436
  0.7 8.5 %copy-start.7 = (bf16[512,256]{1,0:T(8,128)(2,1)S(1)}, bf16[512,256]{1,0:T(8,128)(2,1)}, u32[]{:S(2)}) copy-start(bf16[512,256]{1,0:T(8,128)(2,1)} %queries_ref.5) | copy-start | bytes 786436
  0.7 10.7 %copy-start.1 = (bf16[512,256]{1,0:T(8,128)(2,1)S(1)}, bf16[512,256]{1,0:T(8,128)(2,1)}, u32[]{:S(2)}) copy-start(bf16[512,256]{1,0:T(8,128)(2,1)} %keys_ref.9) | copy-start | bytes 786436
  0.7 11.4 %copy-start.2 = (bf16[512,256]{1,0:T(8,128)(2,1)S(1)}, bf16[512,256]{1,0:T(8,128)(2,1)}, u32[]{:S(2)}) copy-start(bf16[512,256]{1,0:T(8,128)(2,1)} %values_ref.9) | copy-start | bytes 786436
  6.2 13.1 %copy-start.12 = (bf16[256,768]{1,0:T(8,128)(2,1)S(1)}, bf16[256,768]{1,0:T(8,128)(2,1)}, u32[]{:S(2)}) copy-start(bf16[256,768]{1,0:T(8,128)(2,1)} %get-tuple-element.25) | copy-start | bytes 1179652
  6.2 13.1 %collective-permute-start = (bf16[256,768]{1,0:T(8,128)(2,1)}, bf16[256,768]{1,0:T(8,128)(2,1)S(1)}, u32[]{:S(2)}, u32[]{:S(2)}) collective-permute-start(bf16[256,768]{1,0:T(8,128)(2,1)} %get-tuple-element.26), channel_id=1, source_target_pairs={{0,4},{4,0},{8,12},{12,8},{16,20},{20,16},{24,28},{28,24},{1,5},{5... | collective-permute-start | bytes 1179656 | tf_op jit(solution)/shard_map/ppermute | solution.py:317
  9.1 12.4 %copy-start.11 = (bf16[256,768]{1,0:T(8,128)(2,1)S(1)}, bf16[256,768]{1,0:T(8,128)(2,1)}, u32[]{:S(2)}) copy-start(bf16[256,768]{1,0:T(8,128)(2,1)} %get-tuple-element.27) | copy-start | bytes 1179652
  9.2 17.6 %collective-permute-start.8 = (bf16[1536,128]{1,0:T(8,128)(2,1)S(1)}, bf16[1536,128]{1,0:T(8,128)(2,1)S(1)}, u32[]{:S(2)}, u32[]{:S(2)}) collective-permute-start(bf16[1536,128]{1,0:T(8,128)(2,1)S(1)} %shard_map.132), channel_id=1, source_target_pairs={{0,4},{4,0},{8,12},{12,8},{16,20},{20,16},{24,28},{28,24},{1,5},{5... | collective-permute-start | bytes 1179656 | tf_op jit(solution)/shard_map/ppermute | solution.py:317
  9.3 12.2 %collective-permute-start.4 = (bf16[256,768]{1,0:T(8,128)(2,1)}, bf16[256,768]{1,0:T(8,128)(2,1)S(1)}, u32[]{:S(2)}, u32[]{:S(2)}) collective-permute-start(bf16[256,768]{1,0:T(8,128)(2,1)} %get-tuple-element.28), channel_id=1, source_target_pairs={{0,8},{4,12},{8,0},{12,4},{16,24},{20,28},{24,16},{28,20},{1,9},{5... | collective-permute-start | bytes 1179656 | tf_op jit(solution)/shard_map/ppermute | solution.py:317
  19.4 8.3 %collective-permute-start.1 = (bf16[128,768]{1,0:T(8,128)(2,1)S(1)}, bf16[128,768]{1,0:T(8,128)(2,1)S(1)}, u32[]{:S(2)}, u32[]{:S(2)}) collective-permute-start(bf16[128,768]{1,0:T(8,128)(2,1)S(1)} %get-tuple-element.50), channel_id=1, source_target_pairs={{0,8},{4,12},{8,0},{12,4},{16,24},{20,28},{24,16},{28,20},{1,9},{5... | collective-permute-start | bytes 589832 | tf_op jit(solution)/shard_map/ppermute | solution.py:317
  21.7 10.7 %collective-permute-start.5 = (bf16[128,768]{1,0:T(8,128)(2,1)S(1)}, bf16[128,768]{1,0:T(8,128)(2,1)S(1)}, u32[]{:S(2)}, u32[]{:S(2)}) collective-permute-start(bf16[128,768]{1,0:T(8,128)(2,1)S(1)} %get-tuple-element.48), channel_id=1, source_target_pairs={{0,16},{4,20},{8,24},{12,28},{16,0},{20,4},{24,8},{28,12},{1,17},{... | collective-permute-start | bytes 589832 | tf_op jit(solution)/shard_map/ppermute | solution.py:317
  27.7 14.1 %collective-permute-start.2 = (bf16[64,768]{1,0:T(8,128)(2,1)S(1)}, bf16[64,768]{1,0:T(8,128)(2,1)S(1)}, u32[]{:S(2)}, u32[]{:S(2)}) collective-permute-start(bf16[64,768]{1,0:T(8,128)(2,1)S(1)} %get-tuple-element.54), channel_id=1, source_target_pairs={{0,16},{4,20},{8,24},{12,28},{16,0},{20,4},{24,8},{28,12},{1,17},{... | collective-permute-start | bytes 294920 | tf_op jit(solution)/shard_map/ppermute | solution.py:317
  32.4 13.6 %collective-permute-start.6 = (bf16[64,768]{1,0:T(8,128)(2,1)S(1)}, bf16[64,768]{1,0:T(8,128)(2,1)S(1)}, u32[]{:S(2)}, u32[]{:S(2)}) collective-permute-start(bf16[64,768]{1,0:T(8,128)(2,1)S(1)} %get-tuple-element.52), channel_id=1, source_target_pairs={{0,4},{4,0},{8,12},{12,8},{16,20},{20,16},{24,28},{28,24},{1,5},{5... | collective-permute-start | bytes 294920 | tf_op jit(solution)/shard_map/ppermute | solution.py:317
  34.0 17.7 %collective-permute-start.9 = (bf16[1024,128]{1,0:T(8,128)(2,1)S(1)}, bf16[1024,128]{1,0:T(8,128)(2,1)S(1)}, u32[]{:S(2)}, u32[]{:S(2)}) collective-permute-start(bf16[1024,128]{1,0:T(8,128)(2,1)S(1)} %get-tuple-element.31.high_ref), channel_id=1, source_target_pairs={{0,8},{4,12},{8,16},{12,20},{16,24},{20,28},{1,9},{5,13},{9,17},{1... | collective-permute-start | bytes 786440 | tf_op jit(solution)/shard_map/ppermute | solution.py:306
  38.1 13.5 %collective-permute-start.10 = (bf16[1024,128]{1,0:T(8,128)(2,1)S(1)}, bf16[1024,128]{1,0:T(8,128)(2,1)S(1)}, u32[]{:S(2)}, u32[]{:S(2)}) collective-permute-start(bf16[1024,128]{1,0:T(8,128)(2,1)S(1)} %get-tuple-element.32.low_ref), channel_id=1, source_target_pairs={{8,0},{12,4},{16,8},{20,12},{24,16},{28,20},{9,1},{13,5},{17,9},{2... | collective-permute-start | bytes 786440 | tf_op jit(solution)/shard_map/ppermute | solution.py:306
  39.4 12.2 %collective-permute-start.11 = (bf16[1024,256]{1,0:T(8,128)(2,1)}, bf16[1024,256]{1,0:T(8,128)(2,1)S(1)}, u32[]{:S(2)}, u32[]{:S(2)}) collective-permute-start(bf16[1024,256]{1,0:T(8,128)(2,1)} %constant_dynamic-update-slice_fusion), channel_id=1, source_target_pairs={{0,4},{4,8},{8,12},{12,16},{16,20},{20,24},{24,28},{1,5},{5,9},{9,... | collective-permute-start | bytes 1572872 | tf_op jit(solution)/shard_map/ppermute | solution.py:306
  41.9 7.1 %collective-permute-start.3 = (bf16[64,768]{1,0:T(8,128)(2,1)S(1)}, bf16[64,768]{1,0:T(8,128)(2,1)S(1)}, u32[]{:S(2)}, u32[]{:S(2)}) collective-permute-start(bf16[64,768]{1,0:T(8,128)(2,1)S(1)} %add_convert_fusion.5), channel_id=1, source_target_pairs={{0,16},{4,20},{8,24},{12,28},{16,0},{20,4},{24,8},{28,12},{1,17},{... | collective-permute-start | bytes 294920 | tf_op jit(solution)/shard_map/ppermute | solution.py:317
  45.9 5.7 %collective-permute-start.7 = (bf16[64,768]{1,0:T(8,128)(2,1)S(1)}, bf16[64,768]{1,0:T(8,128)(2,1)S(1)}, u32[]{:S(2)}, u32[]{:S(2)}) collective-permute-start(bf16[64,768]{1,0:T(8,128)(2,1)S(1)} %add_convert_fusion.4), channel_id=1, source_target_pairs={{0,4},{4,0},{8,12},{12,8},{16,20},{20,16},{24,28},{28,24},{1,5},{5... | collective-permute-start | bytes 294920 | tf_op jit(solution)/shard_map/ppermute | solution.py:317
  51.7 16.1 %collective-permute-start.12 = (bf16[128,768]{1,0:T(8,128)(2,1)S(1)}, bf16[128,768]{1,0:T(8,128)(2,1)S(1)}, u32[]{:S(2)}, u32[]{:S(2)}) collective-permute-start(bf16[128,768]{1,0:T(8,128)(2,1)S(1)} %pad_maximum_fusion.2), channel_id=1, source_target_pairs={{0,8},{4,12},{8,0},{12,4},{16,24},{20,28},{24,16},{28,20},{1,9},{5... | collective-permute-start | bytes 589832 | tf_op jit(solution)/shard_map/ppermute | solution.py:317
  59.4 9.6 %collective-permute-start.13 = (bf16[128,768]{1,0:T(8,128)(2,1)S(1)}, bf16[128,768]{1,0:T(8,128)(2,1)S(1)}, u32[]{:S(2)}, u32[]{:S(2)}) collective-permute-start(bf16[128,768]{1,0:T(8,128)(2,1)S(1)} %pad_maximum_fusion.3), channel_id=1, source_target_pairs={{0,16},{4,20},{8,24},{12,28},{16,0},{20,4},{24,8},{28,12},{1,17},{... | collective-permute-start | bytes 589832 | tf_op jit(solution)/shard_map/ppermute | solution.py:317
  67.7 7.0 %copy-start.8 = (bf16[512,128]{1,0:T(8,128)(2,1)}, bf16[512,128]{1,0:T(8,128)(2,1)S(1)}, u32[]{:S(2)}) copy-start(bf16[512,128]{1,0:T(8,128)(2,1)S(1)} %get-tuple-element.36.refs_5_) | copy-start | bytes 393220
  67.7 8.2 %collective-permute-start.16 = (bf16[512,128]{1,0:T(8,128)(2,1)S(1)}, bf16[512,128]{1,0:T(8,128)(2,1)S(1)}, u32[]{:S(2)}, u32[]{:S(2)}) collective-permute-start(bf16[512,128]{1,0:T(8,128)(2,1)S(1)} %get-tuple-element.39), channel_id=1, source_target_pairs={{0,4},{4,0},{8,12},{12,8},{16,20},{20,16},{24,28},{28,24},{1,5},{5... | collective-permute-start | bytes 393224 | tf_op jit(solution)/shard_map/ppermute | solution.py:317
  67.8 12.7 %copy-start.9 = (bf16[256,768]{1,0:T(8,128)(2,1)}, bf16[256,768]{1,0:T(8,128)(2,1)S(1)}, u32[]{:S(2)}) copy-start(bf16[256,768]{1,0:T(8,128)(2,1)S(1)} %pad_maximum_fusion.refs_0_) | copy-start | bytes 1179652
  69.0 11.5 %copy-start.10 = (bf16[256,768]{1,0:T(8,128)(2,1)}, bf16[256,768]{1,0:T(8,128)(2,1)S(1)}, u32[]{:S(2)}) copy-start(bf16[256,768]{1,0:T(8,128)(2,1)S(1)} %pad_maximum_fusion.1.refs_2_) | copy-start | bytes 1179652
  69.0 11.1 %collective-permute-start.14 = (bf16[256,768]{1,0:T(8,128)(2,1)S(1)}, bf16[256,768]{1,0:T(8,128)(2,1)S(1)}, u32[]{:S(2)}, u32[]{:S(2)}) collective-permute-start(bf16[256,768]{1,0:T(8,128)(2,1)S(1)} %pad_maximum_fusion.refs_0_), channel_id=1, source_target_pairs={{0,4},{4,0},{8,12},{12,8},{16,20},{20,16},{24,28},{28,24},{1,5},{5... | collective-permute-start | bytes 1179656 | tf_op jit(solution)/shard_map/ppermute | solution.py:317
  70.0 10.5 %collective-permute-start.15 = (bf16[256,768]{1,0:T(8,128)(2,1)S(1)}, bf16[256,768]{1,0:T(8,128)(2,1)S(1)}, u32[]{:S(2)}, u32[]{:S(2)}) collective-permute-start(bf16[256,768]{1,0:T(8,128)(2,1)S(1)} %pad_maximum_fusion.1.refs_2_), channel_id=1, source_target_pairs={{0,8},{4,12},{8,0},{12,4},{16,24},{20,28},{24,16},{28,20},{1,9},{5... | collective-permute-start | bytes 1179656 | tf_op jit(solution)/shard_map/ppermute | solution.py:317
  75.9 4.6 %copy-start.15 = (bf16[512,128]{1,0:T(8,128)(2,1)}, bf16[512,128]{1,0:T(8,128)(2,1)S(1)}, u32[]{:S(2)}) copy-start(bf16[512,128]{1,0:T(8,128)(2,1)S(1)} %collective-permute-done.16.refs_6_) | copy-start | bytes 393220
  75.9 13.4 %collective-permute-start.17 = (bf16[1024,256]{1,0:T(8,128)(2,1)}, bf16[1024,256]{1,0:T(8,128)(2,1)S(1)}, u32[]{:S(2)}, u32[]{:S(2)}) collective-permute-start(bf16[1024,256]{1,0:T(8,128)(2,1)} %constant_dynamic-update-slice_fusion), channel_id=1, source_target_pairs={{4,0},{8,4},{12,8},{16,12},{20,16},{24,20},{28,24},{5,1},{9,5},{13... | collective-permute-start | bytes 1572872 | tf_op jit(solution)/shard_map/ppermute | solution.py:306
  80.1 0.7 copy-start.13
  80.5 0.8 copy-start.14
  81.2 5.8 %copy-start = (bf16[512,1024]{1,0:T(8,128)(2,1)S(1)}, bf16[512,1024]{1,0:T(8,128)(2,1)}, u32[]{:S(2)}) copy-start(bf16[512,1024]{1,0:T(8,128)(2,1)} %map_ref.3) | copy-start | bytes 3145732
  87.1 1.0 %copy-start.3 = (bf16[512,512]{1,0:T(8,128)(2,1)S(1)}, bf16[512,512]{1,0:T(8,128)(2,1)}, u32[]{:S(2)}) copy-start(bf16[512,512]{1,0:T(8,128)(2,1)} %get-tuple-element.42.fast_ref) | copy-start | bytes 1572868
  89.1 8.1 %copy-start.6 = (bf16[512,256]{1,0:T(8,128)(2,1)S(1)}, bf16[512,256]{1,0:T(8,128)(2,1)}, u32[]{:S(2)}) copy-start(bf16[512,256]{1,0:T(8,128)(2,1)} %queries_ref.7) | copy-start | bytes 786436
  89.1 1.6 %collective-permute-start.19 = (bf16[512,256]{1,0:T(8,128)(2,1)S(1)}, bf16[512,256]{1,0:T(8,128)(2,1)S(1)}, u32[]{:S(2)}, u32[]{:S(2)}) collective-permute-start(bf16[512,256]{1,0:T(8,128)(2,1)S(1)} %get-tuple-element.46), channel_id=1, source_target_pairs={{0,1},{1,0},{2,3},{3,2},{4,5},{5,4},{6,7},{7,6},{8,9},{9,8},{10,11... | collective-permute-start | bytes 786440 | tf_op jit(solution)/shard_map/ppermute | solution.py:312
  90.2 2.7 %collective-permute-start.18 = (bf16[512,256]{1,0:T(8,128)(2,1)S(1)}, bf16[512,256]{1,0:T(8,128)(2,1)S(1)}, u32[]{:S(2)}, u32[]{:S(2)}) collective-permute-start(bf16[512,256]{1,0:T(8,128)(2,1)S(1)} %get-tuple-element.44), channel_id=1, source_target_pairs={{0,1},{1,0},{2,3},{3,2},{4,5},{5,4},{6,7},{7,6},{8,9},{9,8},{10,11... | collective-permute-start | bytes 786440 | tf_op jit(solution)/shard_map/ppermute | solution.py:312
  90.9 6.4 %collective-permute-start.21 = (bf16[256,256]{1,0:T(8,128)(2,1)S(1)}, bf16[256,256]{1,0:T(8,128)(2,1)S(1)}, u32[]{:S(2)}, u32[]{:S(2)}) collective-permute-start(bf16[256,256]{1,0:T(8,128)(2,1)S(1)} %get-tuple-element.56), channel_id=1, source_target_pairs={{0,2},{1,3},{2,0},{3,1},{4,6},{5,7},{6,4},{7,5},{8,10},{9,11},{10,... | collective-permute-start | bytes 393224 | tf_op jit(solution)/shard_map/ppermute | solution.py:312
  92.4 6.9 %collective-permute-start.20 = (bf16[256,256]{1,0:T(8,128)(2,1)S(1)}, bf16[256,256]{1,0:T(8,128)(2,1)S(1)}, u32[]{:S(2)}, u32[]{:S(2)}) collective-permute-start(bf16[256,256]{1,0:T(8,128)(2,1)S(1)} %get-tuple-element.57), channel_id=1, source_target_pairs={{0,2},{1,3},{2,0},{3,1},{4,6},{5,7},{6,4},{7,5},{8,10},{9,11},{10,... | collective-permute-start | bytes 393224 | tf_op jit(solution)/shard_map/ppermute | solution.py:312

commit v19 on v15

--- a/solution.py
+++ b/solution.py
@@ -14,7 +14,7 @@
 FAST_DIM = 512
 FAST_HIDDEN = 512
 TILE = 128
-QUERY_TILE = 256
+ROW_TILE = 256
 VMEM_LIMIT = 24 * 1024 * 1024
 VMEM_MOST = 60 * 1024 * 1024
 
@@ -105,19 +105,19 @@
 def attend_rows(edge_prev, edge_next, query_tile, keys_prev, keys_own, keys_next,
                 values_prev, values_own, values_next):
     scale = math.log2(math.e) / math.sqrt(HEAD_DIM)
-    row = lax.broadcasted_iota(jnp.int32, (QUERY_TILE, QUERY_TILE), 0)
-    col = lax.broadcasted_iota(jnp.int32, (QUERY_TILE, QUERY_TILE), 1)
+    row = lax.broadcasted_iota(jnp.int32, (ROW_TILE, ROW_TILE), 0)
+    col = lax.broadcasted_iota(jnp.int32, (ROW_TILE, ROW_TILE), 1)
     minus = jnp.float32(-jnp.inf)
     score_prev = dot_nt(query_tile, keys_prev)
     score_own = dot_nt(query_tile, keys_own)
     score_next = dot_nt(query_tile, keys_next)
-    parts = [score_prev[:, :QUERY_TILE] + jnp.where(col >= row, edge_prev, minus)]
-    if score_prev.shape[1] > QUERY_TILE:
-        parts.append(score_prev[:, QUERY_TILE:] + edge_prev)
+    parts = [score_prev[:, :ROW_TILE] + jnp.where(col >= row, edge_prev, minus)]
+    if score_prev.shape[1] > ROW_TILE:
+        parts.append(score_prev[:, ROW_TILE:] + edge_prev)
     parts.append(score_own)
-    if score_next.shape[1] > QUERY_TILE:
-        parts.append(score_next[:, :-QUERY_TILE] + edge_next)
-    parts.append(score_next[:, -QUERY_TILE:] + jnp.where(col <= row, edge_next, minus))
+    if score_next.shape[1] > ROW_TILE:
+        parts.append(score_next[:, :-ROW_TILE] + edge_next)
+    parts.append(score_next[:, -ROW_TILE:] + jnp.where(col <= row, edge_next, minus))
     scores = jnp.concatenate(parts, axis=1)
     highest = jnp.max(scores, axis=1, keepdims=True)
     weights = jnp.exp2((scores - highest) * scale)
@@ -171,10 +171,10 @@
         base = (side if turn == 0 else 1 - side) * count
 
         def span(ref, low, length):
-            return ref[pl.ds(pl.multiple_of(base + low, QUERY_TILE), length), :]
-
-        for index in range(count // QUERY_TILE):
-            low, high = index * QUERY_TILE, (index + 1) * QUERY_TILE
+            return ref[pl.ds(pl.multiple_of(base + low, ROW_TILE), length), :]
+
+        for index in range(count // ROW_TILE):
+            low, high = index * ROW_TILE, (index + 1) * ROW_TILE
             query = queries_ref[low:high, pl.ds(start, HEAD_DIM)] if turn == 0 else other_ref[low:high, :]
             out_ref[low:high, :] = attend_rows(
                 edge_ref[turn, 0], edge_ref[turn, 1], query,
@@ -193,8 +193,8 @@
     offset = half if done_refs else 0
     if done_refs:
         out_ref[:half, :] = done_refs[0][...]
-    for low in range(offset, offset + half, QUERY_TILE):
-        high = low + QUERY_TILE
+    for low in range(offset, offset + half, ROW_TILE):
+        high = low + ROW_TILE
         rows = slice(low, high)
         mixed = (
             keep_ref[rows, :].astype(F32)
@@ -277,8 +277,9 @@
         copy.wait()
     own_map = map_ref[pl.ds(pl.multiple_of(side * HEAD_DIM, HEAD_DIM), HEAD_DIM), :]
     other_map = map_ref[pl.ds(pl.multiple_of((1 - side) * HEAD_DIM, HEAD_DIM), HEAD_DIM), :]
-    for low in range(0, keep_ref.shape[0], TILE):
-        rows = slice(low, low + TILE)
+    step = keep_ref.shape[0]
+    for low in range(0, keep_ref.shape[0], step):
+        rows = slice(low, low + step)
         own = keep_ref[rows, :].astype(F32)
         other = other_ref[rows, :].astype(F32)
         total = jnp.sum(own * own + other * other, axis=1, keepdims=True)
@@ -388,14 +389,14 @@
     whole = pl.BlockSpec(memory_space=pltpu.VMEM)
     gradients = pl.pallas_call(
         functools.partial(gradient_kernel, orders),
-        grid=(hidden_size // TILE,),
+        grid=(hidden_size // ROW_TILE,),
         out_shape=out_shapes,
         in_specs=[
             pl.BlockSpec(memory_space=pltpu.SMEM),
             whole,
             whole,
             whole,
-            pl.BlockSpec((3, TILE, fast_width), lambda turn: (0, turn, 0)),
+            pl.BlockSpec((3, ROW_TILE, fast_width), lambda turn: (0, turn, 0)),
         ],
         out_specs=[whole] * len(out_shapes),
         scratch_shapes=[pltpu.VMEM((hidden_size, chunk_width), BF16)] * 2,
@@ -468,14 +469,15 @@
             pltpu.VMEM(weights.shape, BF16),
             pltpu.SemaphoreType.DMA((len(operands),)),
         ],
-        limit=VMEM_MOST,
+        limit=VMEM_MOST - 3 * 1024 * 1024,
     )
     far_near = head_swap(far_send, 1)
+    far_keep = lax.optimization_barrier(far_keep.astype(F32))
     near_near = head_swap(after(near_send, next_second), 1)
     half = rows // 2
     far_parts = []
     for part in (slice(0, half), slice(half, rows)):
-        far_sum = far_keep[part].astype(F32) + far_near[part].astype(F32)
+        far_sum = far_keep[part] + far_near[part].astype(F32)
         far_parts.append(head_swap(far_sum.astype(BF16), 2))
     if not halving:
         share_rows = hidden_size // seq_count

time: 106 us -> 101 us (0.953)
  Pallas kernels: 23.2 us -> 20.3 us
    pallas_call x6, Pallas kernels: 16.3 us -> 14.8 us  [call(): pl.pallas_call(body, out_shape=out_shapes, in_specs=in_specs, out_specs=j...]
    pallas_call x1, Pallas kernels: 6.88 us -> 5.49 us  [local(): pl.pallas_call(functools.partial(gradient_kernel, orders), grid=(hidden_s...]
  transfers between devices with their start and end apart: 22 -> 22, of which waited for: 11 -> 11; matrix products, arithmetic and copies ran while one was open for 3% -> 4% of each run, Pallas kernels for 13% -> 12%
where the time goes in v19:
time: 101 us
  starting transfers between devices  51.3 us (51%)
  waiting for transfers between devices  24.2 us (24%)
  Pallas kernels  20.3 us (20%)
  local copies, waits for them, and re-layouts  2.33 us (2%)
  other arithmetic  2.09 us (2%)
    ppermute x14, starting transfers between devices, seq_swap(): lax.ppermute(value, 'seq', [(i, i ^ step) for i in range(lax.axis_size('s...  39.3 us
    ppermute x14, waiting for transfers between devices, seq_swap(): lax.ppermute(value, 'seq', [(i, i ^ step) for i in range(lax.axis_size('s...  19.6 us
    pallas_call x6, Pallas kernels, call(): pl.pallas_call(body, out_shape=out_shapes, in_specs=in_specs, out_specs=j...  14.8 us
    ppermute x4, starting transfers between devices, seq_shift(): lax.ppermute(value, 'seq', [(i, i + step) for i in range(peers) if 0 <= i...  9.33 us
    pallas_call x1, Pallas kernels, local(): pl.pallas_call(functools.partial(gradient_kernel, orders), grid=(hidden_s...  5.49 us
    ppermute x4, waiting for transfers between devices, head_swap(): lax.ppermute(value, 'head', [(i, i ^ bit) for i in range(lax.axis_size('h...  4.56 us
    ppermute x4, starting transfers between devices, head_swap(): lax.ppermute(value, 'head', [(i, i ^ bit) for i in range(lax.axis_size('h...  2.65 us
  transfers between devices with their start and end apart: 22, of which 11 were waited for; matrix products, arithmetic and copies ran while one was open for 4% of the time, Pallas kernels for 12%

profile of v19, /device:TPU:0, one launch (start us, length us, event | category | flops | bytes accessed | tf_op | source)
XLA Modules:
  0.0 101.2 jit_solution(12386177619070947247)
XLA Ops:
  0.7 5.5 %shard_map.131 = (bf16[256,768]{1,0:T(8,128)(2,1)}, bf16[256,768]{1,0:T(8,128)(2,1)}, bf16[256,768]{1,0:T(8,128)(2,1)}, bf16[256,768]{1,0:T(8,128)(2,1)}) custom-call(s32[1,1]{1,0:T(1,128)} %bitcast.4.place_ref, f32[1,512]{1,0:T(1,128)} %bitcast.23, bf16[512,512]{1,0:T(8,128)(2,1)} %keys_ref.5, bf16[512,512]{1,0:T(8,128)(2,1)} %values_ref.5, ...), custom_call_target="tpu_custom_call" | custom-call | flops 1000 | bytes 1000 | tf_op jit(solution)/shard_map/pallas_call | solution.py:390
  6.2 3.0 %collective-permute-start = (bf16[256,768]{1,0:T(8,128)(2,1)}, bf16[256,768]{1,0:T(8,128)(2,1)S(1)}, u32[]{:S(2)}, u32[]{:S(2)}) collective-permute-start(bf16[256,768]{1,0:T(8,128)(2,1)} %get-tuple-element.25), channel_id=1, source_target_pairs={{0,4},{4,0},{8,12},{12,8},{16,20},{20,16},{24,28},{28,24},{1,5},{5... | collective-permute-start | bytes 1179656 | tf_op jit(solution)/shard_map/ppermute | solution.py:316
  9.2 0.1 shard_map.132
  9.2 0.1 collective-permute-start.8
  9.4 2.0 %collective-permute-start.4 = (bf16[256,768]{1,0:T(8,128)(2,1)}, bf16[256,768]{1,0:T(8,128)(2,1)S(1)}, u32[]{:S(2)}, u32[]{:S(2)}) collective-permute-start(bf16[256,768]{1,0:T(8,128)(2,1)} %get-tuple-element.27), channel_id=1, source_target_pairs={{0,8},{4,12},{8,0},{12,4},{16,24},{20,28},{24,16},{28,20},{1,9},{5... | collective-permute-start | bytes 1179656 | tf_op jit(solution)/shard_map/ppermute | solution.py:316
  11.4 0.7 constant_dynamic-update-slice_fusion.1
  12.1 0.7 constant_dynamic-update-slice_fusion
  12.9 6.5 %collective-permute-done = bf16[256,768]{1,0:T(8,128)(2,1)S(1)} collective-permute-done((bf16[256,768]{1,0:T(8,128)(2,1)}, bf16[256,768]{1,0:T(8,128)(2,1)S(1)}, u32[]{:S(2)}, u32[]{:S(2)}) %collective-permute-start) | collective-permute-done | bytes 393248 | tf_op jit(solution)/shard_map/ppermute | solution.py:316
  19.3 0.1 add_convert_fusion.1
  19.4 2.2 %collective-permute-start.1 = (bf16[128,768]{1,0:T(8,128)(2,1)S(1)}, bf16[128,768]{1,0:T(8,128)(2,1)S(1)}, u32[]{:S(2)}, u32[]{:S(2)}) collective-permute-start(bf16[128,768]{1,0:T(8,128)(2,1)S(1)} %get-tuple-element.50), channel_id=1, source_target_pairs={{0,8},{4,12},{8,0},{12,4},{16,24},{20,28},{24,16},{28,20},{1,9},{5... | collective-permute-start | bytes 589832 | tf_op jit(solution)/shard_map/ppermute | solution.py:316
  21.6 0.1 add_convert_fusion
  21.7 2.6 %collective-permute-start.5 = (bf16[128,768]{1,0:T(8,128)(2,1)S(1)}, bf16[128,768]{1,0:T(8,128)(2,1)S(1)}, u32[]{:S(2)}, u32[]{:S(2)}) collective-permute-start(bf16[128,768]{1,0:T(8,128)(2,1)S(1)} %get-tuple-element.48), channel_id=1, source_target_pairs={{0,16},{4,20},{8,24},{12,28},{16,0},{20,4},{24,8},{28,12},{1,17},{... | collective-permute-start | bytes 589832 | tf_op jit(solution)/shard_map/ppermute | solution.py:316
  24.3 2.6 %collective-permute-done.8.other_ref = bf16[1536,128]{1,0:T(8,128)(2,1)S(1)} collective-permute-done((bf16[1536,128]{1,0:T(8,128)(2,1)S(1)}, bf16[1536,128]{1,0:T(8,128)(2,1)S(1)}, u32[]{:S(2)}, u32[]{:S(2)}) %collective-permute-start.8) | collective-permute-done | bytes 393248 | tf_op jit(solution)/shard_map/ppermute | solution.py:316
  27.0 0.8 collective-permute-done.1
  27.8 2.1 %collective-permute-start.2 = (bf16[64,768]{1,0:T(8,128)(2,1)S(1)}, bf16[64,768]{1,0:T(8,128)(2,1)S(1)}, u32[]{:S(2)}, u32[]{:S(2)}) collective-permute-start(bf16[64,768]{1,0:T(8,128)(2,1)S(1)} %get-tuple-element.54), channel_id=1, source_target_pairs={{0,16},{4,20},{8,24},{12,28},{16,0},{20,4},{24,8},{28,12},{1,17},{... | collective-permute-start | bytes 294920 | tf_op jit(solution)/shard_map/ppermute | solution.py:316
  29.9 2.4 %collective-permute-done.5 = bf16[128,768]{1,0:T(8,128)(2,1)S(1)} collective-permute-done((bf16[128,768]{1,0:T(8,128)(2,1)S(1)}, bf16[128,768]{1,0:T(8,128)(2,1)S(1)}, u32[]{:S(2)}, u32[]{:S(2)}) %collective-permute-start.5) | collective-permute-done | bytes 196640 | tf_op jit(solution)/shard_map/ppermute | solution.py:316
  32.4 1.6 %collective-permute-start.6 = (bf16[64,768]{1,0:T(8,128)(2,1)S(1)}, bf16[64,768]{1,0:T(8,128)(2,1)S(1)}, u32[]{:S(2)}, u32[]{:S(2)}) collective-permute-start(bf16[64,768]{1,0:T(8,128)(2,1)S(1)} %get-tuple-element.52), channel_id=1, source_target_pairs={{0,4},{4,0},{8,12},{12,8},{16,20},{20,16},{24,28},{28,24},{1,5},{5... | collective-permute-start | bytes 294920 | tf_op jit(solution)/shard_map/ppermute | solution.py:316
  34.0 4.1 %collective-permute-start.9 = (bf16[1024,128]{1,0:T(8,128)(2,1)S(1)}, bf16[1024,128]{1,0:T(8,128)(2,1)S(1)}, u32[]{:S(2)}, u32[]{:S(2)}) collective-permute-start(bf16[1024,128]{1,0:T(8,128)(2,1)S(1)} %get-tuple-element.30.high_ref), channel_id=1, source_target_pairs={{0,8},{4,12},{8,16},{12,20},{16,24},{20,28},{1,9},{5,13},{9,17},{1... | collective-permute-start | bytes 786440 | tf_op jit(solution)/shard_map/ppermute | solution.py:305
  38.1 1.3 %collective-permute-start.10 = (bf16[1024,128]{1,0:T(8,128)(2,1)S(1)}, bf16[1024,128]{1,0:T(8,128)(2,1)S(1)}, u32[]{:S(2)}, u32[]{:S(2)}) collective-permute-start(bf16[1024,128]{1,0:T(8,128)(2,1)S(1)} %get-tuple-element.31.low_ref), channel_id=1, source_target_pairs={{8,0},{12,4},{16,8},{20,12},{24,16},{28,20},{9,1},{13,5},{17,9},{2... | collective-permute-start | bytes 786440 | tf_op jit(solution)/shard_map/ppermute | solution.py:305
  39.4 2.4 %collective-permute-start.11 = (bf16[1024,256]{1,0:T(8,128)(2,1)}, bf16[1024,256]{1,0:T(8,128)(2,1)S(1)}, u32[]{:S(2)}, u32[]{:S(2)}) collective-permute-start(bf16[1024,256]{1,0:T(8,128)(2,1)} %constant_dynamic-update-slice_fusion), channel_id=1, source_target_pairs={{0,4},{4,8},{8,12},{12,16},{16,20},{20,24},{24,28},{1,5},{5,9},{9,... | collective-permute-start | bytes 1572872 | tf_op jit(solution)/shard_map/ppermute | solution.py:305
  41.9 4.0 %collective-permute-start.3 = (bf16[64,768]{1,0:T(8,128)(2,1)S(1)}, bf16[64,768]{1,0:T(8,128)(2,1)S(1)}, u32[]{:S(2)}, u32[]{:S(2)}) collective-permute-start(bf16[64,768]{1,0:T(8,128)(2,1)S(1)} %add_convert_fusion.3), channel_id=1, source_target_pairs={{0,16},{4,20},{8,24},{12,28},{16,0},{20,4},{24,8},{28,12},{1,17},{... | collective-permute-start | bytes 294920 | tf_op jit(solution)/shard_map/ppermute | solution.py:316
  46.0 3.1 %collective-permute-start.7 = (bf16[64,768]{1,0:T(8,128)(2,1)S(1)}, bf16[64,768]{1,0:T(8,128)(2,1)S(1)}, u32[]{:S(2)}, u32[]{:S(2)}) collective-permute-start(bf16[64,768]{1,0:T(8,128)(2,1)S(1)} %add_convert_fusion.2), channel_id=1, source_target_pairs={{0,4},{4,0},{8,12},{12,8},{16,20},{20,16},{24,28},{28,24},{1,5},{5... | collective-permute-start | bytes 294920 | tf_op jit(solution)/shard_map/ppermute | solution.py:316
  49.0 2.6 %collective-permute-done.7 = bf16[64,768]{1,0:T(8,128)(2,1)S(1)} collective-permute-done((bf16[64,768]{1,0:T(8,128)(2,1)S(1)}, bf16[64,768]{1,0:T(8,128)(2,1)S(1)}, u32[]{:S(2)}, u32[]{:S(2)}) %collective-permute-start.7) | collective-permute-done | bytes 98336 | tf_op jit(solution)/shard_map/ppermute | solution.py:316
  51.7 7.5 %collective-permute-start.12 = (bf16[128,768]{1,0:T(8,128)(2,1)S(1)}, bf16[128,768]{1,0:T(8,128)(2,1)S(1)}, u32[]{:S(2)}, u32[]{:S(2)}) collective-permute-start(bf16[128,768]{1,0:T(8,128)(2,1)S(1)} %pad_maximum_fusion.2), channel_id=1, source_target_pairs={{0,8},{4,12},{8,0},{12,4},{16,24},{20,28},{24,16},{28,20},{1,9},{5... | collective-permute-start | bytes 589832 | tf_op jit(solution)/shard_map/ppermute | solution.py:316
  59.2 0.1 pad_maximum_fusion.4
  59.3 0.1 reshape.19.edge_ref
  59.4 5.3 %collective-permute-start.13 = (bf16[128,768]{1,0:T(8,128)(2,1)S(1)}, bf16[128,768]{1,0:T(8,128)(2,1)S(1)}, u32[]{:S(2)}, u32[]{:S(2)}) collective-permute-start(bf16[128,768]{1,0:T(8,128)(2,1)S(1)} %pad_maximum_fusion.3), channel_id=1, source_target_pairs={{0,16},{4,20},{8,24},{12,28},{16,0},{20,4},{24,8},{28,12},{1,17},{... | collective-permute-start | bytes 589832 | tf_op jit(solution)/shard_map/ppermute | solution.py:316
  64.6 3.0 %shard_map.134 = (bf16[512,128]{1,0:T(8,128)(2,1)S(1)}, bf16[512,128]{1,0:T(8,128)(2,1)S(1)}) custom-call(f32[2,2]{1,0:T(2,128)S(1)} %reshape.19.edge_ref, s32[1,1]{1,0:T(1,128)} %bitcast.5.side_ref, bf16[512,256]{1,0:T(8,128)(2,1)S(1)} %copy-done.6, bf16[1536,128]{1,0:T(8,128)(2,1)S(1)} %collective-permute-done.8.other_ref, ...), custom_call_target="tpu_custom_call" | custom-call | flops 805306368 | bytes 2097152 | tf_op jit(solution)/shard_map/pallas_call | solution.py:42
  67.7 0.1 collective-permute-start.16
  67.8 1.2 %collective-permute-done.13 = bf16[128,768]{1,0:T(8,128)(2,1)S(1)} collective-permute-done((bf16[128,768]{1,0:T(8,128)(2,1)S(1)}, bf16[128,768]{1,0:T(8,128)(2,1)S(1)}, u32[]{:S(2)}, u32[]{:S(2)}) %collective-permute-start.13) | collective-permute-done | bytes 196640 | tf_op jit(solution)/shard_map/ppermute | solution.py:316
  69.1 0.9 collective-permute-start.14
  70.0 4.8 %collective-permute-start.15 = (bf16[256,768]{1,0:T(8,128)(2,1)S(1)}, bf16[256,768]{1,0:T(8,128)(2,1)S(1)}, u32[]{:S(2)}, u32[]{:S(2)}) collective-permute-start(bf16[256,768]{1,0:T(8,128)(2,1)S(1)} %pad_maximum_fusion.1.refs_2_), channel_id=1, source_target_pairs={{0,8},{4,12},{8,0},{12,4},{16,24},{20,28},{24,16},{28,20},{1,9},{5... | collective-permute-start | bytes 1179656 | tf_op jit(solution)/shard_map/ppermute | solution.py:316
  74.7 1.1 %collective-permute-done.16.refs_6_ = bf16[512,128]{1,0:T(8,128)(2,1)S(1)} collective-permute-done((bf16[512,128]{1,0:T(8,128)(2,1)S(1)}, bf16[512,128]{1,0:T(8,128)(2,1)S(1)}, u32[]{:S(2)}, u32[]{:S(2)}) %collective-permute-start.16) | collective-permute-done | bytes 131104 | tf_op jit(solution)/shard_map/ppermute | solution.py:316
  75.9 1.5 %collective-permute-start.17 = (bf16[1024,256]{1,0:T(8,128)(2,1)}, bf16[1024,256]{1,0:T(8,128)(2,1)S(1)}, u32[]{:S(2)}, u32[]{:S(2)}) collective-permute-start(bf16[1024,256]{1,0:T(8,128)(2,1)} %constant_dynamic-update-slice_fusion), channel_id=1, source_target_pairs={{4,0},{8,4},{12,8},{16,12},{20,16},{24,20},{28,24},{5,1},{9,5},{13... | collective-permute-start | bytes 1572872 | tf_op jit(solution)/shard_map/ppermute | solution.py:305
  77.4 0.6 add_bitcast_fusion.places_ref
  78.0 2.1 %collective-permute-done.14.refs_1_ = bf16[256,768]{1,0:T(8,128)(2,1)S(1)} collective-permute-done((bf16[256,768]{1,0:T(8,128)(2,1)S(1)}, bf16[256,768]{1,0:T(8,128)(2,1)S(1)}, u32[]{:S(2)}, u32[]{:S(2)}) %collective-permute-start.14) | collective-permute-done | bytes 393248 | tf_op jit(solution)/shard_map/ppermute | solution.py:316
  80.1 0.4 collective-permute-done.15.refs_3_
  80.5 0.4 copy-done.12
  80.9 0.4 copy-done.13
  81.2 6.9 %shard_map.135 = (bf16[3,64,512]{2,1,0:T(8,128)(2,1)}, bf16[512,256]{1,0:T(8,128)(2,1)}, bf16[512,256]{1,0:T(8,128)(2,1)}, bf16[512,256]{1,0:T(8,128)(2,1)}, bf16[512,256]{1,0:T(8,128)(2,1)}) custom-call(s32[1,1]{1,0:T(1,128)} %bitcast.4.place_ref, s32[1,1]{1,0:T(1,128)} %bitcast.5.side_ref, s32[1,4]{1,0:T(1,128)} %add_bitcast_fusion.places_ref, ...), custom_call_target="tpu_custom_call" | custom-call | flops 1000 | bytes 1000 | tf_op jit(solution)/shard_map/pallas_call | solution.py:42
  88.3 0.5 collective-permute-start.18
  88.8 1.0 convert_element_type.95
  89.7 0.2 collective-permute-done.19
  90.0 1.5 %collective-permute-start.21 = (bf16[256,256]{1,0:T(8,128)(2,1)S(1)}, bf16[256,256]{1,0:T(8,128)(2,1)S(1)}, u32[]{:S(2)}, u32[]{:S(2)}) collective-permute-start(bf16[256,256]{1,0:T(8,128)(2,1)S(1)} %get-tuple-element.46), channel_id=1, source_target_pairs={{0,2},{1,3},{2,0},{3,1},{4,6},{5,7},{6,4},{7,5},{8,10},{9,11},{10,... | collective-permute-start | bytes 393224 | tf_op jit(solution)/shard_map/ppermute | solution.py:311
  91.6 0.6 collective-permute-start.20
  92.1 4.3 %collective-permute-done.21.far_ref = bf16[256,256]{1,0:T(8,128)(2,1)S(1)} collective-permute-done((bf16[256,256]{1,0:T(8,128)(2,1)S(1)}, bf16[256,256]{1,0:T(8,128)(2,1)S(1)}, u32[]{:S(2)}, u32[]{:S(2)}) %collective-permute-start.21) | collective-permute-done | bytes 131104 | tf_op jit(solution)/shard_map/ppermute | solution.py:311
  96.5 2.0 %shard_map.136.refs_0_ = bf16[256,256]{1,0:T(8,128)(2,1)S(1)} custom-call(f32[2,2]{1,0:T(2,128)S(1)} %reshape.19.edge_ref, bf16[512,256]{1,0:T(8,128)(2,1)S(1)} %copy-done.4, bf16[512,256]{1,0:T(8,128)(2,1)S(1)} %copy-done.5, bf16[512,256]{1,0:T(8,128)(2,1)S(1)} %collective-permute-done.18.near_ref, bf16[256,256]{1,0:T(8,128)(2,1)S(1)} %collective-permute-done.21.far_ref, ...), custom_call_target="tpu_custom_call" | custom-call | flops 402653184 | bytes 2097152 | tf_op jit(solution)/shard_map/pallas_call | solution.py:42
  98.5 2.7 %shard_map.137 = bf16[512,256]{1,0:T(8,128)(2,1)} custom-call(f32[2,2]{1,0:T(2,128)S(1)} %reshape.19.edge_ref, bf16[512,256]{1,0:T(8,128)(2,1)S(1)} %copy-done.4, bf16[512,256]{1,0:T(8,128)(2,1)S(1)} %copy-done.5, bf16[512,256]{1,0:T(8,128)(2,1)S(1)} %collective-permute-done.18.near_ref, bf16[256,256]{1,0:T(8,128)(2,1)S(1)} %collective-permute-done.20.far_ref, ...), custom_call_target="tpu_custom_call" | custom-call | flops 402653184 | bytes 2097152 | tf_op jit(solution)/shard_map/pallas_call | solution.py:42
  (50 shorter events, 0.5 us)
Async XLA Ops:
  0.6 8.5 %copy-start.3 = (bf16[512,256]{1,0:T(8,128)(2,1)S(1)}, bf16[512,256]{1,0:T(8,128)(2,1)}, u32[]{:S(2)}) copy-start(bf16[512,256]{1,0:T(8,128)(2,1)} %values_ref.7) | copy-start | bytes 786436
  0.6 8.5 %copy-start.2 = (bf16[512,256]{1,0:T(8,128)(2,1)S(1)}, bf16[512,256]{1,0:T(8,128)(2,1)}, u32[]{:S(2)}) copy-start(bf16[512,256]{1,0:T(8,128)(2,1)} %keys_ref.7) | copy-start | bytes 786436
  0.7 8.5 %copy-start.6 = (bf16[512,256]{1,0:T(8,128)(2,1)S(1)}, bf16[512,256]{1,0:T(8,128)(2,1)}, u32[]{:S(2)}) copy-start(bf16[512,256]{1,0:T(8,128)(2,1)} %queries_ref.5) | copy-start | bytes 786436
  0.7 10.7 %copy-start = (bf16[512,256]{1,0:T(8,128)(2,1)S(1)}, bf16[512,256]{1,0:T(8,128)(2,1)}, u32[]{:S(2)}) copy-start(bf16[512,256]{1,0:T(8,128)(2,1)} %keys_ref.9) | copy-start | bytes 786436
  0.7 11.4 %copy-start.1 = (bf16[512,256]{1,0:T(8,128)(2,1)S(1)}, bf16[512,256]{1,0:T(8,128)(2,1)}, u32[]{:S(2)}) copy-start(bf16[512,256]{1,0:T(8,128)(2,1)} %values_ref.9) | copy-start | bytes 786436
  6.2 13.1 %copy-start.11 = (bf16[256,768]{1,0:T(8,128)(2,1)S(1)}, bf16[256,768]{1,0:T(8,128)(2,1)}, u32[]{:S(2)}) copy-start(bf16[256,768]{1,0:T(8,128)(2,1)} %get-tuple-element.24) | copy-start | bytes 1179652
  6.2 13.1 %collective-permute-start = (bf16[256,768]{1,0:T(8,128)(2,1)}, bf16[256,768]{1,0:T(8,128)(2,1)S(1)}, u32[]{:S(2)}, u32[]{:S(2)}) collective-permute-start(bf16[256,768]{1,0:T(8,128)(2,1)} %get-tuple-element.25), channel_id=1, source_target_pairs={{0,4},{4,0},{8,12},{12,8},{16,20},{20,16},{24,28},{28,24},{1,5},{5... | collective-permute-start | bytes 1179656 | tf_op jit(solution)/shard_map/ppermute | solution.py:316
  9.2 12.4 %copy-start.10 = (bf16[256,768]{1,0:T(8,128)(2,1)S(1)}, bf16[256,768]{1,0:T(8,128)(2,1)}, u32[]{:S(2)}) copy-start(bf16[256,768]{1,0:T(8,128)(2,1)} %get-tuple-element.26) | copy-start | bytes 1179652
  9.2 17.6 %collective-permute-start.8 = (bf16[1536,128]{1,0:T(8,128)(2,1)S(1)}, bf16[1536,128]{1,0:T(8,128)(2,1)S(1)}, u32[]{:S(2)}, u32[]{:S(2)}) collective-permute-start(bf16[1536,128]{1,0:T(8,128)(2,1)S(1)} %shard_map.132), channel_id=1, source_target_pairs={{0,4},{4,0},{8,12},{12,8},{16,20},{20,16},{24,28},{28,24},{1,5},{5... | collective-permute-start | bytes 1179656 | tf_op jit(solution)/shard_map/ppermute | solution.py:316
  9.4 12.2 %collective-permute-start.4 = (bf16[256,768]{1,0:T(8,128)(2,1)}, bf16[256,768]{1,0:T(8,128)(2,1)S(1)}, u32[]{:S(2)}, u32[]{:S(2)}) collective-permute-start(bf16[256,768]{1,0:T(8,128)(2,1)} %get-tuple-element.27), channel_id=1, source_target_pairs={{0,8},{4,12},{8,0},{12,4},{16,24},{20,28},{24,16},{28,20},{1,9},{5... | collective-permute-start | bytes 1179656 | tf_op jit(solution)/shard_map/ppermute | solution.py:316
  19.4 8.3 %collective-permute-start.1 = (bf16[128,768]{1,0:T(8,128)(2,1)S(1)}, bf16[128,768]{1,0:T(8,128)(2,1)S(1)}, u32[]{:S(2)}, u32[]{:S(2)}) collective-permute-start(bf16[128,768]{1,0:T(8,128)(2,1)S(1)} %get-tuple-element.50), channel_id=1, source_target_pairs={{0,8},{4,12},{8,0},{12,4},{16,24},{20,28},{24,16},{28,20},{1,9},{5... | collective-permute-start | bytes 589832 | tf_op jit(solution)/shard_map/ppermute | solution.py:316
  21.7 10.7 %collective-permute-start.5 = (bf16[128,768]{1,0:T(8,128)(2,1)S(1)}, bf16[128,768]{1,0:T(8,128)(2,1)S(1)}, u32[]{:S(2)}, u32[]{:S(2)}) collective-permute-start(bf16[128,768]{1,0:T(8,128)(2,1)S(1)} %get-tuple-element.48), channel_id=1, source_target_pairs={{0,16},{4,20},{8,24},{12,28},{16,0},{20,4},{24,8},{28,12},{1,17},{... | collective-permute-start | bytes 589832 | tf_op jit(solution)/shard_map/ppermute | solution.py:316
  27.8 14.1 %collective-permute-start.2 = (bf16[64,768]{1,0:T(8,128)(2,1)S(1)}, bf16[64,768]{1,0:T(8,128)(2,1)S(1)}, u32[]{:S(2)}, u32[]{:S(2)}) collective-permute-start(bf16[64,768]{1,0:T(8,128)(2,1)S(1)} %get-tuple-element.54), channel_id=1, source_target_pairs={{0,16},{4,20},{8,24},{12,28},{16,0},{20,4},{24,8},{28,12},{1,17},{... | collective-permute-start | bytes 294920 | tf_op jit(solution)/shard_map/ppermute | solution.py:316
  32.4 13.6 %collective-permute-start.6 = (bf16[64,768]{1,0:T(8,128)(2,1)S(1)}, bf16[64,768]{1,0:T(8,128)(2,1)S(1)}, u32[]{:S(2)}, u32[]{:S(2)}) collective-permute-start(bf16[64,768]{1,0:T(8,128)(2,1)S(1)} %get-tuple-element.52), channel_id=1, source_target_pairs={{0,4},{4,0},{8,12},{12,8},{16,20},{20,16},{24,28},{28,24},{1,5},{5... | collective-permute-start | bytes 294920 | tf_op jit(solution)/shard_map/ppermute | solution.py:316
  34.0 17.7 %collective-permute-start.9 = (bf16[1024,128]{1,0:T(8,128)(2,1)S(1)}, bf16[1024,128]{1,0:T(8,128)(2,1)S(1)}, u32[]{:S(2)}, u32[]{:S(2)}) collective-permute-start(bf16[1024,128]{1,0:T(8,128)(2,1)S(1)} %get-tuple-element.30.high_ref), channel_id=1, source_target_pairs={{0,8},{4,12},{8,16},{12,20},{16,24},{20,28},{1,9},{5,13},{9,17},{1... | collective-permute-start | bytes 786440 | tf_op jit(solution)/shard_map/ppermute | solution.py:305
  38.1 13.5 %collective-permute-start.10 = (bf16[1024,128]{1,0:T(8,128)(2,1)S(1)}, bf16[1024,128]{1,0:T(8,128)(2,1)S(1)}, u32[]{:S(2)}, u32[]{:S(2)}) collective-permute-start(bf16[1024,128]{1,0:T(8,128)(2,1)S(1)} %get-tuple-element.31.low_ref), channel_id=1, source_target_pairs={{8,0},{12,4},{16,8},{20,12},{24,16},{28,20},{9,1},{13,5},{17,9},{2... | collective-permute-start | bytes 786440 | tf_op jit(solution)/shard_map/ppermute | solution.py:305
  39.4 12.2 %collective-permute-start.11 = (bf16[1024,256]{1,0:T(8,128)(2,1)}, bf16[1024,256]{1,0:T(8,128)(2,1)S(1)}, u32[]{:S(2)}, u32[]{:S(2)}) collective-permute-start(bf16[1024,256]{1,0:T(8,128)(2,1)} %constant_dynamic-update-slice_fusion), channel_id=1, source_target_pairs={{0,4},{4,8},{8,12},{12,16},{16,20},{20,24},{24,28},{1,5},{5,9},{9,... | collective-permute-start | bytes 1572872 | tf_op jit(solution)/shard_map/ppermute | solution.py:305
  41.9 7.1 %collective-permute-start.3 = (bf16[64,768]{1,0:T(8,128)(2,1)S(1)}, bf16[64,768]{1,0:T(8,128)(2,1)S(1)}, u32[]{:S(2)}, u32[]{:S(2)}) collective-permute-start(bf16[64,768]{1,0:T(8,128)(2,1)S(1)} %add_convert_fusion.3), channel_id=1, source_target_pairs={{0,16},{4,20},{8,24},{12,28},{16,0},{20,4},{24,8},{28,12},{1,17},{... | collective-permute-start | bytes 294920 | tf_op jit(solution)/shard_map/ppermute | solution.py:316
  46.0 5.7 %collective-permute-start.7 = (bf16[64,768]{1,0:T(8,128)(2,1)S(1)}, bf16[64,768]{1,0:T(8,128)(2,1)S(1)}, u32[]{:S(2)}, u32[]{:S(2)}) collective-permute-start(bf16[64,768]{1,0:T(8,128)(2,1)S(1)} %add_convert_fusion.2), channel_id=1, source_target_pairs={{0,4},{4,0},{8,12},{12,8},{16,20},{20,16},{24,28},{28,24},{1,5},{5... | collective-permute-start | bytes 294920 | tf_op jit(solution)/shard_map/ppermute | solution.py:316
  51.7 16.1 %collective-permute-start.12 = (bf16[128,768]{1,0:T(8,128)(2,1)S(1)}, bf16[128,768]{1,0:T(8,128)(2,1)S(1)}, u32[]{:S(2)}, u32[]{:S(2)}) collective-permute-start(bf16[128,768]{1,0:T(8,128)(2,1)S(1)} %pad_maximum_fusion.2), channel_id=1, source_target_pairs={{0,8},{4,12},{8,0},{12,4},{16,24},{20,28},{24,16},{28,20},{1,9},{5... | collective-permute-start | bytes 589832 | tf_op jit(solution)/shard_map/ppermute | solution.py:316
  59.4 9.6 %collective-permute-start.13 = (bf16[128,768]{1,0:T(8,128)(2,1)S(1)}, bf16[128,768]{1,0:T(8,128)(2,1)S(1)}, u32[]{:S(2)}, u32[]{:S(2)}) collective-permute-start(bf16[128,768]{1,0:T(8,128)(2,1)S(1)} %pad_maximum_fusion.3), channel_id=1, source_target_pairs={{0,16},{4,20},{8,24},{12,28},{16,0},{20,4},{24,8},{28,12},{1,17},{... | collective-permute-start | bytes 589832 | tf_op jit(solution)/shard_map/ppermute | solution.py:316
  67.7 7.0 %copy-start.7 = (bf16[512,128]{1,0:T(8,128)(2,1)}, bf16[512,128]{1,0:T(8,128)(2,1)S(1)}, u32[]{:S(2)}) copy-start(bf16[512,128]{1,0:T(8,128)(2,1)S(1)} %get-tuple-element.35.refs_5_) | copy-start | bytes 393220
  67.7 8.2 %collective-permute-start.16 = (bf16[512,128]{1,0:T(8,128)(2,1)S(1)}, bf16[512,128]{1,0:T(8,128)(2,1)S(1)}, u32[]{:S(2)}, u32[]{:S(2)}) collective-permute-start(bf16[512,128]{1,0:T(8,128)(2,1)S(1)} %get-tuple-element.38), channel_id=1, source_target_pairs={{0,4},{4,0},{8,12},{12,8},{16,20},{20,16},{24,28},{28,24},{1,5},{5... | collective-permute-start | bytes 393224 | tf_op jit(solution)/shard_map/ppermute | solution.py:316
  67.8 12.7 %copy-start.8 = (bf16[256,768]{1,0:T(8,128)(2,1)}, bf16[256,768]{1,0:T(8,128)(2,1)S(1)}, u32[]{:S(2)}) copy-start(bf16[256,768]{1,0:T(8,128)(2,1)S(1)} %pad_maximum_fusion.refs_0_) | copy-start | bytes 1179652
  69.0 11.5 %copy-start.9 = (bf16[256,768]{1,0:T(8,128)(2,1)}, bf16[256,768]{1,0:T(8,128)(2,1)S(1)}, u32[]{:S(2)}) copy-start(bf16[256,768]{1,0:T(8,128)(2,1)S(1)} %pad_maximum_fusion.1.refs_2_) | copy-start | bytes 1179652
  69.1 11.0 %collective-permute-start.14 = (bf16[256,768]{1,0:T(8,128)(2,1)S(1)}, bf16[256,768]{1,0:T(8,128)(2,1)S(1)}, u32[]{:S(2)}, u32[]{:S(2)}) collective-permute-start(bf16[256,768]{1,0:T(8,128)(2,1)S(1)} %pad_maximum_fusion.refs_0_), channel_id=1, source_target_pairs={{0,4},{4,0},{8,12},{12,8},{16,20},{20,16},{24,28},{28,24},{1,5},{5... | collective-permute-start | bytes 1179656 | tf_op jit(solution)/shard_map/ppermute | solution.py:316
  70.0 10.5 %collective-permute-start.15 = (bf16[256,768]{1,0:T(8,128)(2,1)S(1)}, bf16[256,768]{1,0:T(8,128)(2,1)S(1)}, u32[]{:S(2)}, u32[]{:S(2)}) collective-permute-start(bf16[256,768]{1,0:T(8,128)(2,1)S(1)} %pad_maximum_fusion.1.refs_2_), channel_id=1, source_target_pairs={{0,8},{4,12},{8,0},{12,4},{16,24},{20,28},{24,16},{28,20},{1,9},{5... | collective-permute-start | bytes 1179656 | tf_op jit(solution)/shard_map/ppermute | solution.py:316
  75.9 4.6 %copy-start.14 = (bf16[512,128]{1,0:T(8,128)(2,1)}, bf16[512,128]{1,0:T(8,128)(2,1)S(1)}, u32[]{:S(2)}) copy-start(bf16[512,128]{1,0:T(8,128)(2,1)S(1)} %collective-permute-done.16.refs_6_) | copy-start | bytes 393220
  75.9 12.4 %collective-permute-start.17 = (bf16[1024,256]{1,0:T(8,128)(2,1)}, bf16[1024,256]{1,0:T(8,128)(2,1)S(1)}, u32[]{:S(2)}, u32[]{:S(2)}) collective-permute-start(bf16[1024,256]{1,0:T(8,128)(2,1)} %constant_dynamic-update-slice_fusion), channel_id=1, source_target_pairs={{4,0},{8,4},{12,8},{16,12},{20,16},{24,20},{28,24},{5,1},{9,5},{13... | collective-permute-start | bytes 1572872 | tf_op jit(solution)/shard_map/ppermute | solution.py:305
  80.1 0.8 copy-start.12
  80.5 0.7 copy-start.13
  88.2 8.3 %copy-start.4 = (bf16[512,256]{1,0:T(8,128)(2,1)S(1)}, bf16[512,256]{1,0:T(8,128)(2,1)}, u32[]{:S(2)}) copy-start(bf16[512,256]{1,0:T(8,128)(2,1)} %queries_ref.7) | copy-start | bytes 786436
  88.2 8.3 %copy-start.5 = (bf16[512,256]{1,0:T(8,128)(2,1)S(1)}, bf16[512,256]{1,0:T(8,128)(2,1)}, u32[]{:S(2)}) copy-start(bf16[512,256]{1,0:T(8,128)(2,1)} %get-tuple-element.39.keep_ref) | copy-start | bytes 786436
  88.2 1.8 %collective-permute-start.19 = (bf16[512,256]{1,0:T(8,128)(2,1)}, bf16[512,256]{1,0:T(8,128)(2,1)S(1)}, u32[]{:S(2)}, u32[]{:S(2)}) collective-permute-start(bf16[512,256]{1,0:T(8,128)(2,1)} %get-tuple-element.44), channel_id=1, source_target_pairs={{0,1},{1,0},{2,3},{3,2},{4,5},{5,4},{6,7},{7,6},{8,9},{9,8},{10,11... | collective-permute-start | bytes 786440 | tf_op jit(solution)/shard_map/ppermute | solution.py:311
  88.3 3.9 %collective-permute-start.18 = (bf16[512,256]{1,0:T(8,128)(2,1)}, bf16[512,256]{1,0:T(8,128)(2,1)S(1)}, u32[]{:S(2)}, u32[]{:S(2)}) collective-permute-start(bf16[512,256]{1,0:T(8,128)(2,1)} %get-tuple-element.42), channel_id=1, source_target_pairs={{0,1},{1,0},{2,3},{3,2},{4,5},{5,4},{6,7},{7,6},{8,9},{9,8},{10,11... | collective-permute-start | bytes 786440 | tf_op jit(solution)/shard_map/ppermute | solution.py:311
  90.0 6.4 %collective-permute-start.21 = (bf16[256,256]{1,0:T(8,128)(2,1)S(1)}, bf16[256,256]{1,0:T(8,128)(2,1)S(1)}, u32[]{:S(2)}, u32[]{:S(2)}) collective-permute-start(bf16[256,256]{1,0:T(8,128)(2,1)S(1)} %get-tuple-element.46), channel_id=1, source_target_pairs={{0,2},{1,3},{2,0},{3,1},{4,6},{5,7},{6,4},{7,5},{8,10},{9,11},{10,... | collective-permute-start | bytes 393224 | tf_op jit(solution)/shard_map/ppermute | solution.py:311
  91.6 6.9 %collective-permute-start.20 = (bf16[256,256]{1,0:T(8,128)(2,1)S(1)}, bf16[256,256]{1,0:T(8,128)(2,1)S(1)}, u32[]{:S(2)}, u32[]{:S(2)}) collective-permute-start(bf16[256,256]{1,0:T(8,128)(2,1)S(1)} %get-tuple-element.47), channel_id=1, source_target_pairs={{0,2},{1,3},{2,0},{3,1},{4,6},{5,7},{6,4},{7,5},{8,10},{9,11},{10,... | collective-permute-start | bytes 393224 | tf_op jit(solution)/shard_map/ppermute | solution.py:311

commit v20 on v19

--- a/solution.py
+++ b/solution.py
@@ -186,20 +186,15 @@
 
 
 def second_kernel(edge_ref, queries_ref, keep_ref, near_ref, far_ref, prev_ref, keys_ref, values_ref, next_ref,
-                  *refs):
-    done_refs, out_ref = refs[:-1], refs[-1]
+                  out_ref):
     count = keys_ref.shape[0]
-    half = far_ref.shape[0]
-    offset = half if done_refs else 0
-    if done_refs:
-        out_ref[:half, :] = done_refs[0][...]
-    for low in range(offset, offset + half, ROW_TILE):
+    for low in range(0, count, ROW_TILE):
         high = low + ROW_TILE
         rows = slice(low, high)
         mixed = (
             keep_ref[rows, :].astype(F32)
             + near_ref[rows, :].astype(F32)
-            + far_ref[low - offset:high - offset, :].astype(F32)
+            + far_ref[rows, :].astype(F32)
         )
         query = (queries_ref[rows, :].astype(F32) + mixed).astype(BF16)
         heads = []
@@ -474,26 +469,19 @@
     far_near = head_swap(far_send, 1)
     far_keep = lax.optimization_barrier(far_keep.astype(F32))
     near_near = head_swap(after(near_send, next_second), 1)
-    half = rows // 2
-    far_parts = []
-    for part in (slice(0, half), slice(half, rows)):
-        far_sum = far_keep[part] + far_near[part].astype(F32)
-        far_parts.append(head_swap(far_sum.astype(BF16), 2))
+    far_far = head_swap((far_keep + far_near.astype(F32)).astype(BF16), 2)
     if not halving:
         share_rows = hidden_size // seq_count
         own_new = lax.dynamic_slice_in_dim(own_new, seq_place * share_rows, share_rows, 1)
 
-    def second_attention(part, *done):
-        return call(
-            second_kernel,
-            shape((half * (1 + len(done)), width), BF16),
-            (edges, queries_second, near_keep, near_near, far_parts[part],
-             prev_second, keys_second, values_second, next_second, *done),
-            scalars=1,
-            cost=(6 * rows * rows * width, 16 * rows * width),
-        )
-
-    normed_second = second_attention(1, second_attention(0))
+    normed_second = call(
+        second_kernel,
+        share,
+        (edges, queries_second, near_keep, near_near, far_far,
+         prev_second, keys_second, values_second, next_second),
+        scalars=1,
+        cost=(12 * rows * rows * width, 16 * rows * width),
+    )
     return (normed_second, jnp.transpose(own_new, (1, 0, 2))[None])
 
 

time: 101 us -> 103 us (1.020)
  waiting for transfers between devices: 24.2 us -> 26.2 us
    ppermute x4 -> x3, waiting for transfers between devices: 4.56 us -> 7.1 us  [head_swap(): lax.ppermute(value, 'head', [(i, i ^ bit) for i in range(lax.axis_size('h...]
    pallas_call x6 -> x5, Pallas kernels: 14.8 us -> 13.9 us  [call(): pl.pallas_call(body, out_shape=out_shapes, in_specs=in_specs, out_specs=j...]
    ppermute x4 -> x3, starting transfers between devices: 2.65 us -> 2.12 us  [head_swap(): lax.ppermute(value, 'head', [(i, i ^ bit) for i in range(lax.axis_size('h...]
  transfers between devices with their start and end apart: 22 -> 21, of which waited for: 11 -> 10; matrix products, arithmetic and copies ran while one was open for 4% -> 4% of each run, Pallas kernels for 12% -> 10%
where the time goes in v20:
time: 103 us; the launch traced here: 102 us
  starting transfers between devices  50.7 us (49%)
  waiting for transfers between devices  26.2 us (25%)
  Pallas kernels  19.4 us (19%)
  local copies, waits for them, and re-layouts  3.08 us (3%)
  other arithmetic  2.12 us (2%)
    ppermute x14, starting transfers between devices, seq_swap(): lax.ppermute(value, 'seq', [(i, i ^ step) for i in range(lax.axis_size('s...  39.3 us
    ppermute x14, waiting for transfers between devices, seq_swap(): lax.ppermute(value, 'seq', [(i, i ^ step) for i in range(lax.axis_size('s...  19.1 us
    pallas_call x5, Pallas kernels, call(): pl.pallas_call(body, out_shape=out_shapes, in_specs=in_specs, out_specs=j...  13.9 us
    ppermute x4, starting transfers between devices, seq_shift(): lax.ppermute(value, 'seq', [(i, i + step) for i in range(peers) if 0 <= i...  9.33 us
    ppermute x3, waiting for transfers between devices, head_swap(): lax.ppermute(value, 'head', [(i, i ^ bit) for i in range(lax.axis_size('h...  7.1 us
    pallas_call x1, Pallas kernels, local(): pl.pallas_call(functools.partial(gradient_kernel, orders), grid=(hidden_s...  5.49 us
    unnamed x31, local copies, waits for them, and re-layouts  2.28 us
    ppermute x3, starting transfers between devices, head_swap(): lax.ppermute(value, 'head', [(i, i ^ bit) for i in range(lax.axis_size('h...  2.12 us
  transfers between devices with their start and end apart: 21, of which 10 were waited for; matrix products, arithmetic and copies ran while one was open for 4% of the time, Pallas kernels for 10%

profile of v20, /device:TPU:0, one launch (start us, length us, event | category | flops | bytes accessed | tf_op | source)
XLA Modules:
  0.0 102.5 jit_solution(11836384418161541352)
XLA Ops:
  0.7 5.5 %shard_map.131 = (bf16[256,768]{1,0:T(8,128)(2,1)}, bf16[256,768]{1,0:T(8,128)(2,1)}, bf16[256,768]{1,0:T(8,128)(2,1)}, bf16[256,768]{1,0:T(8,128)(2,1)}) custom-call(s32[1,1]{1,0:T(1,128)} %bitcast.4.place_ref, f32[1,512]{1,0:T(1,128)} %bitcast.23, bf16[512,512]{1,0:T(8,128)(2,1)} %keys_ref.4, bf16[512,512]{1,0:T(8,128)(2,1)} %values_ref.4, ...), custom_call_target="tpu_custom_call" | custom-call | flops 1000 | bytes 1000 | tf_op jit(solution)/shard_map/pallas_call | solution.py:385
  6.2 3.0 %collective-permute-start = (bf16[256,768]{1,0:T(8,128)(2,1)}, bf16[256,768]{1,0:T(8,128)(2,1)S(1)}, u32[]{:S(2)}, u32[]{:S(2)}) collective-permute-start(bf16[256,768]{1,0:T(8,128)(2,1)} %get-tuple-element.25), channel_id=1, source_target_pairs={{0,4},{4,0},{8,12},{12,8},{16,20},{20,16},{24,28},{28,24},{1,5},{5... | collective-permute-start | bytes 1179656 | tf_op jit(solution)/shard_map/ppermute | solution.py:311
  9.2 0.1 shard_map.132
  9.2 0.1 collective-permute-start.8
  9.3 2.0 %collective-permute-start.4 = (bf16[256,768]{1,0:T(8,128)(2,1)}, bf16[256,768]{1,0:T(8,128)(2,1)S(1)}, u32[]{:S(2)}, u32[]{:S(2)}) collective-permute-start(bf16[256,768]{1,0:T(8,128)(2,1)} %get-tuple-element.27), channel_id=1, source_target_pairs={{0,8},{4,12},{8,0},{12,4},{16,24},{20,28},{24,16},{28,20},{1,9},{5... | collective-permute-start | bytes 1179656 | tf_op jit(solution)/shard_map/ppermute | solution.py:311
  11.4 0.7 constant_dynamic-update-slice_fusion.1
  12.1 0.7 constant_dynamic-update-slice_fusion
  12.8 6.5 %collective-permute-done = bf16[256,768]{1,0:T(8,128)(2,1)S(1)} collective-permute-done((bf16[256,768]{1,0:T(8,128)(2,1)}, bf16[256,768]{1,0:T(8,128)(2,1)S(1)}, u32[]{:S(2)}, u32[]{:S(2)}) %collective-permute-start) | collective-permute-done | bytes 393248 | tf_op jit(solution)/shard_map/ppermute | solution.py:311
  19.3 0.1 add_convert_fusion.2
  19.4 2.2 %collective-permute-start.1 = (bf16[128,768]{1,0:T(8,128)(2,1)S(1)}, bf16[128,768]{1,0:T(8,128)(2,1)S(1)}, u32[]{:S(2)}, u32[]{:S(2)}) collective-permute-start(bf16[128,768]{1,0:T(8,128)(2,1)S(1)} %get-tuple-element.48), channel_id=1, source_target_pairs={{0,8},{4,12},{8,0},{12,4},{16,24},{20,28},{24,16},{28,20},{1,9},{5... | collective-permute-start | bytes 589832 | tf_op jit(solution)/shard_map/ppermute | solution.py:311
  21.6 0.1 add_convert_fusion.1
  21.7 2.6 %collective-permute-start.5 = (bf16[128,768]{1,0:T(8,128)(2,1)S(1)}, bf16[128,768]{1,0:T(8,128)(2,1)S(1)}, u32[]{:S(2)}, u32[]{:S(2)}) collective-permute-start(bf16[128,768]{1,0:T(8,128)(2,1)S(1)} %get-tuple-element.46), channel_id=1, source_target_pairs={{0,16},{4,20},{8,24},{12,28},{16,0},{20,4},{24,8},{28,12},{1,17},{... | collective-permute-start | bytes 589832 | tf_op jit(solution)/shard_map/ppermute | solution.py:311
  24.3 2.6 %collective-permute-done.8.other_ref = bf16[1536,128]{1,0:T(8,128)(2,1)S(1)} collective-permute-done((bf16[1536,128]{1,0:T(8,128)(2,1)S(1)}, bf16[1536,128]{1,0:T(8,128)(2,1)S(1)}, u32[]{:S(2)}, u32[]{:S(2)}) %collective-permute-start.8) | collective-permute-done | bytes 393248 | tf_op jit(solution)/shard_map/ppermute | solution.py:311
  26.9 0.1 shard_map.133
  27.0 0.8 collective-permute-done.1
  27.8 2.1 %collective-permute-start.2 = (bf16[64,768]{1,0:T(8,128)(2,1)S(1)}, bf16[64,768]{1,0:T(8,128)(2,1)S(1)}, u32[]{:S(2)}, u32[]{:S(2)}) collective-permute-start(bf16[64,768]{1,0:T(8,128)(2,1)S(1)} %get-tuple-element.52), channel_id=1, source_target_pairs={{0,16},{4,20},{8,24},{12,28},{16,0},{20,4},{24,8},{28,12},{1,17},{... | collective-permute-start | bytes 294920 | tf_op jit(solution)/shard_map/ppermute | solution.py:311
  29.9 2.4 %collective-permute-done.5 = bf16[128,768]{1,0:T(8,128)(2,1)S(1)} collective-permute-done((bf16[128,768]{1,0:T(8,128)(2,1)S(1)}, bf16[128,768]{1,0:T(8,128)(2,1)S(1)}, u32[]{:S(2)}, u32[]{:S(2)}) %collective-permute-start.5) | collective-permute-done | bytes 196640 | tf_op jit(solution)/shard_map/ppermute | solution.py:311
  32.4 1.6 %collective-permute-start.6 = (bf16[64,768]{1,0:T(8,128)(2,1)S(1)}, bf16[64,768]{1,0:T(8,128)(2,1)S(1)}, u32[]{:S(2)}, u32[]{:S(2)}) collective-permute-start(bf16[64,768]{1,0:T(8,128)(2,1)S(1)} %get-tuple-element.50), channel_id=1, source_target_pairs={{0,4},{4,0},{8,12},{12,8},{16,20},{20,16},{24,28},{28,24},{1,5},{5... | collective-permute-start | bytes 294920 | tf_op jit(solution)/shard_map/ppermute | solution.py:311
  34.0 4.1 %collective-permute-start.9 = (bf16[1024,128]{1,0:T(8,128)(2,1)S(1)}, bf16[1024,128]{1,0:T(8,128)(2,1)S(1)}, u32[]{:S(2)}, u32[]{:S(2)}) collective-permute-start(bf16[1024,128]{1,0:T(8,128)(2,1)S(1)} %get-tuple-element.30.high_ref), channel_id=1, source_target_pairs={{0,8},{4,12},{8,16},{12,20},{16,24},{20,28},{1,9},{5,13},{9,17},{1... | collective-permute-start | bytes 786440 | tf_op jit(solution)/shard_map/ppermute | solution.py:300
  38.1 1.3 %collective-permute-start.10 = (bf16[1024,128]{1,0:T(8,128)(2,1)S(1)}, bf16[1024,128]{1,0:T(8,128)(2,1)S(1)}, u32[]{:S(2)}, u32[]{:S(2)}) collective-permute-start(bf16[1024,128]{1,0:T(8,128)(2,1)S(1)} %get-tuple-element.31.low_ref), channel_id=1, source_target_pairs={{8,0},{12,4},{16,8},{20,12},{24,16},{28,20},{9,1},{13,5},{17,9},{2... | collective-permute-start | bytes 786440 | tf_op jit(solution)/shard_map/ppermute | solution.py:300
  39.4 2.4 %collective-permute-start.11 = (bf16[1024,256]{1,0:T(8,128)(2,1)}, bf16[1024,256]{1,0:T(8,128)(2,1)S(1)}, u32[]{:S(2)}, u32[]{:S(2)}) collective-permute-start(bf16[1024,256]{1,0:T(8,128)(2,1)} %constant_dynamic-update-slice_fusion), channel_id=1, source_target_pairs={{0,4},{4,8},{8,12},{12,16},{16,20},{20,24},{24,28},{1,5},{5,9},{9,... | collective-permute-start | bytes 1572872 | tf_op jit(solution)/shard_map/ppermute | solution.py:300
  41.9 4.0 %collective-permute-start.3 = (bf16[64,768]{1,0:T(8,128)(2,1)S(1)}, bf16[64,768]{1,0:T(8,128)(2,1)S(1)}, u32[]{:S(2)}, u32[]{:S(2)}) collective-permute-start(bf16[64,768]{1,0:T(8,128)(2,1)S(1)} %add_convert_fusion.4), channel_id=1, source_target_pairs={{0,16},{4,20},{8,24},{12,28},{16,0},{20,4},{24,8},{28,12},{1,17},{... | collective-permute-start | bytes 294920 | tf_op jit(solution)/shard_map/ppermute | solution.py:311
  46.0 3.1 %collective-permute-start.7 = (bf16[64,768]{1,0:T(8,128)(2,1)S(1)}, bf16[64,768]{1,0:T(8,128)(2,1)S(1)}, u32[]{:S(2)}, u32[]{:S(2)}) collective-permute-start(bf16[64,768]{1,0:T(8,128)(2,1)S(1)} %add_convert_fusion.3), channel_id=1, source_target_pairs={{0,4},{4,0},{8,12},{12,8},{16,20},{20,16},{24,28},{28,24},{1,5},{5... | collective-permute-start | bytes 294920 | tf_op jit(solution)/shard_map/ppermute | solution.py:311
  49.0 2.6 %collective-permute-done.7 = bf16[64,768]{1,0:T(8,128)(2,1)S(1)} collective-permute-done((bf16[64,768]{1,0:T(8,128)(2,1)S(1)}, bf16[64,768]{1,0:T(8,128)(2,1)S(1)}, u32[]{:S(2)}, u32[]{:S(2)}) %collective-permute-start.7) | collective-permute-done | bytes 98336 | tf_op jit(solution)/shard_map/ppermute | solution.py:311
  51.7 7.5 %collective-permute-start.12 = (bf16[128,768]{1,0:T(8,128)(2,1)S(1)}, bf16[128,768]{1,0:T(8,128)(2,1)S(1)}, u32[]{:S(2)}, u32[]{:S(2)}) collective-permute-start(bf16[128,768]{1,0:T(8,128)(2,1)S(1)} %pad_maximum_fusion.2), channel_id=1, source_target_pairs={{0,8},{4,12},{8,0},{12,4},{16,24},{20,28},{24,16},{28,20},{1,9},{5... | collective-permute-start | bytes 589832 | tf_op jit(solution)/shard_map/ppermute | solution.py:311
  59.2 0.1 pad_maximum_fusion.4
  59.3 0.1 reshape.19.edge_ref
  59.4 5.3 %collective-permute-start.13 = (bf16[128,768]{1,0:T(8,128)(2,1)S(1)}, bf16[128,768]{1,0:T(8,128)(2,1)S(1)}, u32[]{:S(2)}, u32[]{:S(2)}) collective-permute-start(bf16[128,768]{1,0:T(8,128)(2,1)S(1)} %pad_maximum_fusion.3), channel_id=1, source_target_pairs={{0,16},{4,20},{8,24},{12,28},{16,0},{20,4},{24,8},{28,12},{1,17},{... | collective-permute-start | bytes 589832 | tf_op jit(solution)/shard_map/ppermute | solution.py:311
  64.6 3.1 %shard_map.134 = (bf16[512,128]{1,0:T(8,128)(2,1)S(1)}, bf16[512,128]{1,0:T(8,128)(2,1)S(1)}) custom-call(f32[2,2]{1,0:T(2,128)S(1)} %reshape.19.edge_ref, s32[1,1]{1,0:T(1,128)} %bitcast.5.side_ref, bf16[512,256]{1,0:T(8,128)(2,1)S(1)} %copy-done.4, bf16[1536,128]{1,0:T(8,128)(2,1)S(1)} %collective-permute-done.8.other_ref, ...), custom_call_target="tpu_custom_call" | custom-call | flops 805306368 | bytes 2097152 | tf_op jit(solution)/shard_map/pallas_call | solution.py:42
  67.7 0.6 copy-done.5
  68.4 0.6 collective-permute-done.13
  69.1 1.5 %collective-permute-start.14 = (bf16[256,768]{1,0:T(8,128)(2,1)S(1)}, bf16[256,768]{1,0:T(8,128)(2,1)S(1)}, u32[]{:S(2)}, u32[]{:S(2)}) collective-permute-start(bf16[256,768]{1,0:T(8,128)(2,1)S(1)} %pad_maximum_fusion.refs_0_), channel_id=1, source_target_pairs={{0,4},{4,0},{8,12},{12,8},{16,20},{20,16},{24,28},{28,24},{1,5},{5... | collective-permute-start | bytes 1179656 | tf_op jit(solution)/shard_map/ppermute | solution.py:311
  70.5 4.2 %collective-permute-start.15 = (bf16[256,768]{1,0:T(8,128)(2,1)S(1)}, bf16[256,768]{1,0:T(8,128)(2,1)S(1)}, u32[]{:S(2)}, u32[]{:S(2)}) collective-permute-start(bf16[256,768]{1,0:T(8,128)(2,1)S(1)} %pad_maximum_fusion.1.refs_2_), channel_id=1, source_target_pairs={{0,8},{4,12},{8,0},{12,4},{16,24},{20,28},{24,16},{28,20},{1,9},{5... | collective-permute-start | bytes 1179656 | tf_op jit(solution)/shard_map/ppermute | solution.py:311
  74.7 1.6 %collective-permute-done.16.refs_6_ = bf16[512,128]{1,0:T(8,128)(2,1)S(1)} collective-permute-done((bf16[512,128]{1,0:T(8,128)(2,1)S(1)}, bf16[512,128]{1,0:T(8,128)(2,1)S(1)}, u32[]{:S(2)}, u32[]{:S(2)}) %collective-permute-start.16) | collective-permute-done | bytes 131104 | tf_op jit(solution)/shard_map/ppermute | solution.py:311
  76.3 1.5 %collective-permute-start.17 = (bf16[1024,256]{1,0:T(8,128)(2,1)}, bf16[1024,256]{1,0:T(8,128)(2,1)S(1)}, u32[]{:S(2)}, u32[]{:S(2)}) collective-permute-start(bf16[1024,256]{1,0:T(8,128)(2,1)} %constant_dynamic-update-slice_fusion), channel_id=1, source_target_pairs={{4,0},{8,4},{12,8},{16,12},{20,16},{24,20},{28,24},{5,1},{9,5},{13... | collective-permute-start | bytes 1572872 | tf_op jit(solution)/shard_map/ppermute | solution.py:300
  77.8 0.7 add_bitcast_fusion.places_ref
  78.4 2.1 %collective-permute-done.14.refs_1_ = bf16[256,768]{1,0:T(8,128)(2,1)S(1)} collective-permute-done((bf16[256,768]{1,0:T(8,128)(2,1)S(1)}, bf16[256,768]{1,0:T(8,128)(2,1)S(1)}, u32[]{:S(2)}, u32[]{:S(2)}) %collective-permute-start.14) | collective-permute-done | bytes 393248 | tf_op jit(solution)/shard_map/ppermute | solution.py:311
  80.5 0.8 copy-done.12
  81.3 0.1 copy-done.13
  81.4 6.9 %shard_map.135 = (bf16[3,64,512]{2,1,0:T(8,128)(2,1)}, bf16[512,256]{1,0:T(8,128)(2,1)}, bf16[512,256]{1,0:T(8,128)(2,1)}, bf16[512,256]{1,0:T(8,128)(2,1)}, bf16[512,256]{1,0:T(8,128)(2,1)}) custom-call(s32[1,1]{1,0:T(1,128)} %bitcast.4.place_ref, s32[1,1]{1,0:T(1,128)} %bitcast.5.side_ref, s32[1,4]{1,0:T(1,128)} %add_bitcast_fusion.places_ref, ...), custom_call_target="tpu_custom_call" | custom-call | flops 1000 | bytes 1000 | tf_op jit(solution)/shard_map/pallas_call | solution.py:42
  88.3 0.1 collective-permute-start.19
  88.4 0.5 collective-permute-start.18
  88.9 1.0 convert_element_type.89
  89.9 0.2 collective-permute-done.19
  90.2 0.1 add_convert_fusion
  90.2 1.6 %collective-permute-start.20 = (bf16[512,256]{1,0:T(8,128)(2,1)S(1)}, bf16[512,256]{1,0:T(8,128)(2,1)S(1)}, u32[]{:S(2)}, u32[]{:S(2)}) collective-permute-start(bf16[512,256]{1,0:T(8,128)(2,1)S(1)} %add_convert_fusion), channel_id=1, source_target_pairs={{0,2},{1,3},{2,0},{3,1},{4,6},{5,7},{6,4},{7,5},{8,10},{9,11},{10,... | collective-permute-start | bytes 786440 | tf_op jit(solution)/shard_map/ppermute | solution.py:306
  91.8 6.9 %collective-permute-done.20.far_ref = bf16[512,256]{1,0:T(8,128)(2,1)S(1)} collective-permute-done((bf16[512,256]{1,0:T(8,128)(2,1)S(1)}, bf16[512,256]{1,0:T(8,128)(2,1)S(1)}, u32[]{:S(2)}, u32[]{:S(2)}) %collective-permute-start.20) | collective-permute-done | bytes 262176 | tf_op jit(solution)/shard_map/ppermute | solution.py:306
  98.6 3.8 %shard_map.136 = bf16[512,256]{1,0:T(8,128)(2,1)} custom-call(f32[2,2]{1,0:T(2,128)S(1)} %reshape.19.edge_ref, bf16[512,256]{1,0:T(8,128)(2,1)S(1)} %copy-done.6, bf16[512,256]{1,0:T(8,128)(2,1)S(1)} %copy-done.7, bf16[512,256]{1,0:T(8,128)(2,1)S(1)} %collective-permute-done.18.near_ref, bf16[512,256]{1,0:T(8,128)(2,1)S(1)} %collective-permute-done.20.far_ref, ...), custom_call_target="tpu_custom_call" | custom-call | flops 805306368 | bytes 2097152 | tf_op jit(solution)/shard_map/pallas_call | solution.py:42
  (47 shorter events, 0.3 us)
Async XLA Ops:
  0.6 8.5 %copy-start.1 = (bf16[512,256]{1,0:T(8,128)(2,1)S(1)}, bf16[512,256]{1,0:T(8,128)(2,1)}, u32[]{:S(2)}) copy-start(bf16[512,256]{1,0:T(8,128)(2,1)} %values_ref.6) | copy-start | bytes 786436
  0.6 8.5 %copy-start = (bf16[512,256]{1,0:T(8,128)(2,1)S(1)}, bf16[512,256]{1,0:T(8,128)(2,1)}, u32[]{:S(2)}) copy-start(bf16[512,256]{1,0:T(8,128)(2,1)} %keys_ref.6) | copy-start | bytes 786436
  0.7 8.5 %copy-start.4 = (bf16[512,256]{1,0:T(8,128)(2,1)S(1)}, bf16[512,256]{1,0:T(8,128)(2,1)}, u32[]{:S(2)}) copy-start(bf16[512,256]{1,0:T(8,128)(2,1)} %queries_ref.4) | copy-start | bytes 786436
  0.7 10.7 %copy-start.2 = (bf16[512,256]{1,0:T(8,128)(2,1)S(1)}, bf16[512,256]{1,0:T(8,128)(2,1)}, u32[]{:S(2)}) copy-start(bf16[512,256]{1,0:T(8,128)(2,1)} %keys_ref.7) | copy-start | bytes 786436
  0.7 11.4 %copy-start.3 = (bf16[512,256]{1,0:T(8,128)(2,1)S(1)}, bf16[512,256]{1,0:T(8,128)(2,1)}, u32[]{:S(2)}) copy-start(bf16[512,256]{1,0:T(8,128)(2,1)} %values_ref.7) | copy-start | bytes 786436
  6.2 13.1 %copy-start.11 = (bf16[256,768]{1,0:T(8,128)(2,1)S(1)}, bf16[256,768]{1,0:T(8,128)(2,1)}, u32[]{:S(2)}) copy-start(bf16[256,768]{1,0:T(8,128)(2,1)} %get-tuple-element.24) | copy-start | bytes 1179652
  6.2 13.1 %collective-permute-start = (bf16[256,768]{1,0:T(8,128)(2,1)}, bf16[256,768]{1,0:T(8,128)(2,1)S(1)}, u32[]{:S(2)}, u32[]{:S(2)}) collective-permute-start(bf16[256,768]{1,0:T(8,128)(2,1)} %get-tuple-element.25), channel_id=1, source_target_pairs={{0,4},{4,0},{8,12},{12,8},{16,20},{20,16},{24,28},{28,24},{1,5},{5... | collective-permute-start | bytes 1179656 | tf_op jit(solution)/shard_map/ppermute | solution.py:311
  9.2 12.4 %copy-start.10 = (bf16[256,768]{1,0:T(8,128)(2,1)S(1)}, bf16[256,768]{1,0:T(8,128)(2,1)}, u32[]{:S(2)}) copy-start(bf16[256,768]{1,0:T(8,128)(2,1)} %get-tuple-element.26) | copy-start | bytes 1179652
  9.2 17.6 %collective-permute-start.8 = (bf16[1536,128]{1,0:T(8,128)(2,1)S(1)}, bf16[1536,128]{1,0:T(8,128)(2,1)S(1)}, u32[]{:S(2)}, u32[]{:S(2)}) collective-permute-start(bf16[1536,128]{1,0:T(8,128)(2,1)S(1)} %shard_map.132), channel_id=1, source_target_pairs={{0,4},{4,0},{8,12},{12,8},{16,20},{20,16},{24,28},{28,24},{1,5},{5... | collective-permute-start | bytes 1179656 | tf_op jit(solution)/shard_map/ppermute | solution.py:311
  9.3 12.2 %collective-permute-start.4 = (bf16[256,768]{1,0:T(8,128)(2,1)}, bf16[256,768]{1,0:T(8,128)(2,1)S(1)}, u32[]{:S(2)}, u32[]{:S(2)}) collective-permute-start(bf16[256,768]{1,0:T(8,128)(2,1)} %get-tuple-element.27), channel_id=1, source_target_pairs={{0,8},{4,12},{8,0},{12,4},{16,24},{20,28},{24,16},{28,20},{1,9},{5... | collective-permute-start | bytes 1179656 | tf_op jit(solution)/shard_map/ppermute | solution.py:311
  19.4 8.3 %collective-permute-start.1 = (bf16[128,768]{1,0:T(8,128)(2,1)S(1)}, bf16[128,768]{1,0:T(8,128)(2,1)S(1)}, u32[]{:S(2)}, u32[]{:S(2)}) collective-permute-start(bf16[128,768]{1,0:T(8,128)(2,1)S(1)} %get-tuple-element.48), channel_id=1, source_target_pairs={{0,8},{4,12},{8,0},{12,4},{16,24},{20,28},{24,16},{28,20},{1,9},{5... | collective-permute-start | bytes 589832 | tf_op jit(solution)/shard_map/ppermute | solution.py:311
  21.7 10.7 %collective-permute-start.5 = (bf16[128,768]{1,0:T(8,128)(2,1)S(1)}, bf16[128,768]{1,0:T(8,128)(2,1)S(1)}, u32[]{:S(2)}, u32[]{:S(2)}) collective-permute-start(bf16[128,768]{1,0:T(8,128)(2,1)S(1)} %get-tuple-element.46), channel_id=1, source_target_pairs={{0,16},{4,20},{8,24},{12,28},{16,0},{20,4},{24,8},{28,12},{1,17},{... | collective-permute-start | bytes 589832 | tf_op jit(solution)/shard_map/ppermute | solution.py:311
  27.8 14.1 %collective-permute-start.2 = (bf16[64,768]{1,0:T(8,128)(2,1)S(1)}, bf16[64,768]{1,0:T(8,128)(2,1)S(1)}, u32[]{:S(2)}, u32[]{:S(2)}) collective-permute-start(bf16[64,768]{1,0:T(8,128)(2,1)S(1)} %get-tuple-element.52), channel_id=1, source_target_pairs={{0,16},{4,20},{8,24},{12,28},{16,0},{20,4},{24,8},{28,12},{1,17},{... | collective-permute-start | bytes 294920 | tf_op jit(solution)/shard_map/ppermute | solution.py:311
  32.4 13.6 %collective-permute-start.6 = (bf16[64,768]{1,0:T(8,128)(2,1)S(1)}, bf16[64,768]{1,0:T(8,128)(2,1)S(1)}, u32[]{:S(2)}, u32[]{:S(2)}) collective-permute-start(bf16[64,768]{1,0:T(8,128)(2,1)S(1)} %get-tuple-element.50), channel_id=1, source_target_pairs={{0,4},{4,0},{8,12},{12,8},{16,20},{20,16},{24,28},{28,24},{1,5},{5... | collective-permute-start | bytes 294920 | tf_op jit(solution)/shard_map/ppermute | solution.py:311
  34.0 17.7 %collective-permute-start.9 = (bf16[1024,128]{1,0:T(8,128)(2,1)S(1)}, bf16[1024,128]{1,0:T(8,128)(2,1)S(1)}, u32[]{:S(2)}, u32[]{:S(2)}) collective-permute-start(bf16[1024,128]{1,0:T(8,128)(2,1)S(1)} %get-tuple-element.30.high_ref), channel_id=1, source_target_pairs={{0,8},{4,12},{8,16},{12,20},{16,24},{20,28},{1,9},{5,13},{9,17},{1... | collective-permute-start | bytes 786440 | tf_op jit(solution)/shard_map/ppermute | solution.py:300
  38.1 13.5 %collective-permute-start.10 = (bf16[1024,128]{1,0:T(8,128)(2,1)S(1)}, bf16[1024,128]{1,0:T(8,128)(2,1)S(1)}, u32[]{:S(2)}, u32[]{:S(2)}) collective-permute-start(bf16[1024,128]{1,0:T(8,128)(2,1)S(1)} %get-tuple-element.31.low_ref), channel_id=1, source_target_pairs={{8,0},{12,4},{16,8},{20,12},{24,16},{28,20},{9,1},{13,5},{17,9},{2... | collective-permute-start | bytes 786440 | tf_op jit(solution)/shard_map/ppermute | solution.py:300
  39.4 12.2 %collective-permute-start.11 = (bf16[1024,256]{1,0:T(8,128)(2,1)}, bf16[1024,256]{1,0:T(8,128)(2,1)S(1)}, u32[]{:S(2)}, u32[]{:S(2)}) collective-permute-start(bf16[1024,256]{1,0:T(8,128)(2,1)} %constant_dynamic-update-slice_fusion), channel_id=1, source_target_pairs={{0,4},{4,8},{8,12},{12,16},{16,20},{20,24},{24,28},{1,5},{5,9},{9,... | collective-permute-start | bytes 1572872 | tf_op jit(solution)/shard_map/ppermute | solution.py:300
  41.9 7.1 %collective-permute-start.3 = (bf16[64,768]{1,0:T(8,128)(2,1)S(1)}, bf16[64,768]{1,0:T(8,128)(2,1)S(1)}, u32[]{:S(2)}, u32[]{:S(2)}) collective-permute-start(bf16[64,768]{1,0:T(8,128)(2,1)S(1)} %add_convert_fusion.4), channel_id=1, source_target_pairs={{0,16},{4,20},{8,24},{12,28},{16,0},{20,4},{24,8},{28,12},{1,17},{... | collective-permute-start | bytes 294920 | tf_op jit(solution)/shard_map/ppermute | solution.py:311
  46.0 5.7 %collective-permute-start.7 = (bf16[64,768]{1,0:T(8,128)(2,1)S(1)}, bf16[64,768]{1,0:T(8,128)(2,1)S(1)}, u32[]{:S(2)}, u32[]{:S(2)}) collective-permute-start(bf16[64,768]{1,0:T(8,128)(2,1)S(1)} %add_convert_fusion.3), channel_id=1, source_target_pairs={{0,4},{4,0},{8,12},{12,8},{16,20},{20,16},{24,28},{28,24},{1,5},{5... | collective-permute-start | bytes 294920 | tf_op jit(solution)/shard_map/ppermute | solution.py:311
  51.7 16.7 %collective-permute-start.12 = (bf16[128,768]{1,0:T(8,128)(2,1)S(1)}, bf16[128,768]{1,0:T(8,128)(2,1)S(1)}, u32[]{:S(2)}, u32[]{:S(2)}) collective-permute-start(bf16[128,768]{1,0:T(8,128)(2,1)S(1)} %pad_maximum_fusion.2), channel_id=1, source_target_pairs={{0,8},{4,12},{8,0},{12,4},{16,24},{20,28},{24,16},{28,20},{1,9},{5... | collective-permute-start | bytes 589832 | tf_op jit(solution)/shard_map/ppermute | solution.py:311
  59.4 9.6 %collective-permute-start.13 = (bf16[128,768]{1,0:T(8,128)(2,1)S(1)}, bf16[128,768]{1,0:T(8,128)(2,1)S(1)}, u32[]{:S(2)}, u32[]{:S(2)}) collective-permute-start(bf16[128,768]{1,0:T(8,128)(2,1)S(1)} %pad_maximum_fusion.3), channel_id=1, source_target_pairs={{0,16},{4,20},{8,24},{12,28},{16,0},{20,4},{24,8},{28,12},{1,17},{... | collective-permute-start | bytes 589832 | tf_op jit(solution)/shard_map/ppermute | solution.py:311
  67.7 0.7 copy-start.5
  68.4 7.9 %collective-permute-start.16 = (bf16[512,128]{1,0:T(8,128)(2,1)S(1)}, bf16[512,128]{1,0:T(8,128)(2,1)S(1)}, u32[]{:S(2)}, u32[]{:S(2)}) collective-permute-start(bf16[512,128]{1,0:T(8,128)(2,1)S(1)} %get-tuple-element.38), channel_id=1, source_target_pairs={{0,4},{4,0},{8,12},{12,8},{16,20},{20,16},{24,28},{28,24},{1,5},{5... | collective-permute-start | bytes 393224 | tf_op jit(solution)/shard_map/ppermute | solution.py:311
  68.4 12.1 %copy-start.8 = (bf16[256,768]{1,0:T(8,128)(2,1)}, bf16[256,768]{1,0:T(8,128)(2,1)S(1)}, u32[]{:S(2)}) copy-start(bf16[256,768]{1,0:T(8,128)(2,1)S(1)} %pad_maximum_fusion.refs_0_) | copy-start | bytes 1179652
  69.0 11.5 %copy-start.9 = (bf16[256,768]{1,0:T(8,128)(2,1)}, bf16[256,768]{1,0:T(8,128)(2,1)S(1)}, u32[]{:S(2)}) copy-start(bf16[256,768]{1,0:T(8,128)(2,1)S(1)} %pad_maximum_fusion.1.refs_2_) | copy-start | bytes 1179652
  69.1 11.5 %collective-permute-start.14 = (bf16[256,768]{1,0:T(8,128)(2,1)S(1)}, bf16[256,768]{1,0:T(8,128)(2,1)S(1)}, u32[]{:S(2)}, u32[]{:S(2)}) collective-permute-start(bf16[256,768]{1,0:T(8,128)(2,1)S(1)} %pad_maximum_fusion.refs_0_), channel_id=1, source_target_pairs={{0,4},{4,0},{8,12},{12,8},{16,20},{20,16},{24,28},{28,24},{1,5},{5... | collective-permute-start | bytes 1179656 | tf_op jit(solution)/shard_map/ppermute | solution.py:311
  70.5 10.0 %collective-permute-start.15 = (bf16[256,768]{1,0:T(8,128)(2,1)S(1)}, bf16[256,768]{1,0:T(8,128)(2,1)S(1)}, u32[]{:S(2)}, u32[]{:S(2)}) collective-permute-start(bf16[256,768]{1,0:T(8,128)(2,1)S(1)} %pad_maximum_fusion.1.refs_2_), channel_id=1, source_target_pairs={{0,8},{4,12},{8,0},{12,4},{16,24},{20,28},{24,16},{28,20},{1,9},{5... | collective-permute-start | bytes 1179656 | tf_op jit(solution)/shard_map/ppermute | solution.py:311
  76.3 4.2 %copy-start.14 = (bf16[512,128]{1,0:T(8,128)(2,1)}, bf16[512,128]{1,0:T(8,128)(2,1)S(1)}, u32[]{:S(2)}) copy-start(bf16[512,128]{1,0:T(8,128)(2,1)S(1)} %collective-permute-done.16.refs_6_) | copy-start | bytes 393220
  76.3 12.1 %collective-permute-start.17 = (bf16[1024,256]{1,0:T(8,128)(2,1)}, bf16[1024,256]{1,0:T(8,128)(2,1)S(1)}, u32[]{:S(2)}, u32[]{:S(2)}) collective-permute-start(bf16[1024,256]{1,0:T(8,128)(2,1)} %constant_dynamic-update-slice_fusion), channel_id=1, source_target_pairs={{4,0},{8,4},{12,8},{16,12},{20,16},{24,20},{28,24},{5,1},{9,5},{13... | collective-permute-start | bytes 1572872 | tf_op jit(solution)/shard_map/ppermute | solution.py:300
  80.5 0.8 copy-start.12
  80.5 0.9 copy-start.13
  88.3 10.3 %copy-start.6 = (bf16[512,256]{1,0:T(8,128)(2,1)S(1)}, bf16[512,256]{1,0:T(8,128)(2,1)}, u32[]{:S(2)}) copy-start(bf16[512,256]{1,0:T(8,128)(2,1)} %queries_ref.5) | copy-start | bytes 786436
  88.3 10.3 %copy-start.7 = (bf16[512,256]{1,0:T(8,128)(2,1)S(1)}, bf16[512,256]{1,0:T(8,128)(2,1)}, u32[]{:S(2)}) copy-start(bf16[512,256]{1,0:T(8,128)(2,1)} %get-tuple-element.39.keep_ref) | copy-start | bytes 786436
  88.3 1.8 %collective-permute-start.19 = (bf16[512,256]{1,0:T(8,128)(2,1)}, bf16[512,256]{1,0:T(8,128)(2,1)S(1)}, u32[]{:S(2)}, u32[]{:S(2)}) collective-permute-start(bf16[512,256]{1,0:T(8,128)(2,1)} %get-tuple-element.44), channel_id=1, source_target_pairs={{0,1},{1,0},{2,3},{3,2},{4,5},{5,4},{6,7},{7,6},{8,9},{9,8},{10,11... | collective-permute-start | bytes 786440 | tf_op jit(solution)/shard_map/ppermute | solution.py:306
  88.4 3.3 %collective-permute-start.18 = (bf16[512,256]{1,0:T(8,128)(2,1)}, bf16[512,256]{1,0:T(8,128)(2,1)S(1)}, u32[]{:S(2)}, u32[]{:S(2)}) collective-permute-start(bf16[512,256]{1,0:T(8,128)(2,1)} %get-tuple-element.42), channel_id=1, source_target_pairs={{0,1},{1,0},{2,3},{3,2},{4,5},{5,4},{6,7},{7,6},{8,9},{9,8},{10,11... | collective-permute-start | bytes 786440 | tf_op jit(solution)/shard_map/ppermute | solution.py:306
  90.2 8.4 %collective-permute-start.20 = (bf16[512,256]{1,0:T(8,128)(2,1)S(1)}, bf16[512,256]{1,0:T(8,128)(2,1)S(1)}, u32[]{:S(2)}, u32[]{:S(2)}) collective-permute-start(bf16[512,256]{1,0:T(8,128)(2,1)S(1)} %add_convert_fusion), channel_id=1, source_target_pairs={{0,2},{1,3},{2,0},{3,1},{4,6},{5,7},{6,4},{7,5},{8,10},{9,11},{10,... | collective-permute-start | bytes 786440 | tf_op jit(solution)/shard_map/ppermute | solution.py:306

commit v21 on v19

--- a/solution.py
+++ b/solution.py
@@ -389,14 +389,14 @@
     whole = pl.BlockSpec(memory_space=pltpu.VMEM)
     gradients = pl.pallas_call(
         functools.partial(gradient_kernel, orders),
-        grid=(hidden_size // ROW_TILE,),
+        grid=(1,),
         out_shape=out_shapes,
         in_specs=[
             pl.BlockSpec(memory_space=pltpu.SMEM),
             whole,
             whole,
             whole,
-            pl.BlockSpec((3, ROW_TILE, fast_width), lambda turn: (0, turn, 0)),
+            pl.BlockSpec((3, hidden_size, fast_width), lambda turn: (0, turn, 0)),
         ],
         out_specs=[whole] * len(out_shapes),
         scratch_shapes=[pltpu.VMEM((hidden_size, chunk_width), BF16)] * 2,

time: 101 us -> 101 us (level)
  no operation moved by 1% of the time
where the time goes in v21:
time: 101 us
  starting transfers between devices  51.2 us (51%)
  waiting for transfers between devices  24.3 us (24%)
  Pallas kernels  20 us (20%)
  local copies, waits for them, and re-layouts  2.33 us (2%)
  other arithmetic  2.09 us (2%)
    ppermute x14, starting transfers between devices, seq_swap(): lax.ppermute(value, 'seq', [(i, i ^ step) for i in range(lax.axis_size('s...  39.3 us
    ppermute x14, waiting for transfers between devices, seq_swap(): lax.ppermute(value, 'seq', [(i, i ^ step) for i in range(lax.axis_size('s...  19.8 us
    pallas_call x6, Pallas kernels, call(): pl.pallas_call(body, out_shape=out_shapes, in_specs=in_specs, out_specs=j...  14.8 us
    ppermute x4, starting transfers between devices, seq_shift(): lax.ppermute(value, 'seq', [(i, i + step) for i in range(peers) if 0 <= i...  9.26 us
    pallas_call x1, Pallas kernels, local(): pl.pallas_call(functools.partial(gradient_kernel, orders), grid=(1,), out...  5.16 us
    ppermute x4, waiting for transfers between devices, head_swap(): lax.ppermute(value, 'head', [(i, i ^ bit) for i in range(lax.axis_size('h...  4.56 us
    ppermute x4, starting transfers between devices, head_swap(): lax.ppermute(value, 'head', [(i, i ^ bit) for i in range(lax.axis_size('h...  2.65 us
  transfers between devices with their start and end apart: 22, of which 11 were waited for; matrix products, arithmetic and copies ran while one was open for 4% of the time, Pallas kernels for 12%

profile of v21, /device:TPU:0, one launch (start us, length us, event | category | flops | bytes accessed | tf_op | source)
XLA Modules:
  0.0 100.9 jit_solution(10645016839763129913)
XLA Ops:
  0.7 5.2 %shard_map.131 = (bf16[256,768]{1,0:T(8,128)(2,1)}, bf16[256,768]{1,0:T(8,128)(2,1)}, bf16[256,768]{1,0:T(8,128)(2,1)}, bf16[256,768]{1,0:T(8,128)(2,1)}) custom-call(s32[1,1]{1,0:T(1,128)} %bitcast.4.place_ref, f32[1,512]{1,0:T(1,128)} %bitcast.23, bf16[512,512]{1,0:T(8,128)(2,1)} %keys_ref.5, bf16[512,512]{1,0:T(8,128)(2,1)} %values_ref.5, ...), custom_call_target="tpu_custom_call" | custom-call | flops 1000 | bytes 1000 | tf_op jit(solution)/shard_map/pallas_call | solution.py:390
  5.8 3.0 %collective-permute-start = (bf16[256,768]{1,0:T(8,128)(2,1)}, bf16[256,768]{1,0:T(8,128)(2,1)S(1)}, u32[]{:S(2)}, u32[]{:S(2)}) collective-permute-start(bf16[256,768]{1,0:T(8,128)(2,1)} %get-tuple-element.25), channel_id=1, source_target_pairs={{0,4},{4,0},{8,12},{12,8},{16,20},{20,16},{24,28},{28,24},{1,5},{5... | collective-permute-start | bytes 1179656 | tf_op jit(solution)/shard_map/ppermute | solution.py:316
  8.8 0.1 shard_map.132
  8.9 0.1 collective-permute-start.8
  9.0 2.1 %collective-permute-start.4 = (bf16[256,768]{1,0:T(8,128)(2,1)}, bf16[256,768]{1,0:T(8,128)(2,1)S(1)}, u32[]{:S(2)}, u32[]{:S(2)}) collective-permute-start(bf16[256,768]{1,0:T(8,128)(2,1)} %get-tuple-element.27), channel_id=1, source_target_pairs={{0,8},{4,12},{8,0},{12,4},{16,24},{20,28},{24,16},{28,20},{1,9},{5... | collective-permute-start | bytes 1179656 | tf_op jit(solution)/shard_map/ppermute | solution.py:316
  11.1 0.7 constant_dynamic-update-slice_fusion.1
  11.8 0.7 constant_dynamic-update-slice_fusion
  12.5 6.5 %collective-permute-done = bf16[256,768]{1,0:T(8,128)(2,1)S(1)} collective-permute-done((bf16[256,768]{1,0:T(8,128)(2,1)}, bf16[256,768]{1,0:T(8,128)(2,1)S(1)}, u32[]{:S(2)}, u32[]{:S(2)}) %collective-permute-start) | collective-permute-done | bytes 393248 | tf_op jit(solution)/shard_map/ppermute | solution.py:316
  19.0 0.1 add_convert_fusion.1
  19.1 2.2 %collective-permute-start.1 = (bf16[128,768]{1,0:T(8,128)(2,1)S(1)}, bf16[128,768]{1,0:T(8,128)(2,1)S(1)}, u32[]{:S(2)}, u32[]{:S(2)}) collective-permute-start(bf16[128,768]{1,0:T(8,128)(2,1)S(1)} %get-tuple-element.50), channel_id=1, source_target_pairs={{0,8},{4,12},{8,0},{12,4},{16,24},{20,28},{24,16},{28,20},{1,9},{5... | collective-permute-start | bytes 589832 | tf_op jit(solution)/shard_map/ppermute | solution.py:316
  21.2 0.1 add_convert_fusion
  21.3 2.7 %collective-permute-start.5 = (bf16[128,768]{1,0:T(8,128)(2,1)S(1)}, bf16[128,768]{1,0:T(8,128)(2,1)S(1)}, u32[]{:S(2)}, u32[]{:S(2)}) collective-permute-start(bf16[128,768]{1,0:T(8,128)(2,1)S(1)} %get-tuple-element.48), channel_id=1, source_target_pairs={{0,16},{4,20},{8,24},{12,28},{16,0},{20,4},{24,8},{28,12},{1,17},{... | collective-permute-start | bytes 589832 | tf_op jit(solution)/shard_map/ppermute | solution.py:316
  24.0 2.6 %collective-permute-done.8.other_ref = bf16[1536,128]{1,0:T(8,128)(2,1)S(1)} collective-permute-done((bf16[1536,128]{1,0:T(8,128)(2,1)S(1)}, bf16[1536,128]{1,0:T(8,128)(2,1)S(1)}, u32[]{:S(2)}, u32[]{:S(2)}) %collective-permute-start.8) | collective-permute-done | bytes 393248 | tf_op jit(solution)/shard_map/ppermute | solution.py:316
  26.7 0.7 collective-permute-done.1
  27.4 2.1 %collective-permute-start.2 = (bf16[64,768]{1,0:T(8,128)(2,1)S(1)}, bf16[64,768]{1,0:T(8,128)(2,1)S(1)}, u32[]{:S(2)}, u32[]{:S(2)}) collective-permute-start(bf16[64,768]{1,0:T(8,128)(2,1)S(1)} %get-tuple-element.54), channel_id=1, source_target_pairs={{0,16},{4,20},{8,24},{12,28},{16,0},{20,4},{24,8},{28,12},{1,17},{... | collective-permute-start | bytes 294920 | tf_op jit(solution)/shard_map/ppermute | solution.py:316
  29.6 2.5 %collective-permute-done.5 = bf16[128,768]{1,0:T(8,128)(2,1)S(1)} collective-permute-done((bf16[128,768]{1,0:T(8,128)(2,1)S(1)}, bf16[128,768]{1,0:T(8,128)(2,1)S(1)}, u32[]{:S(2)}, u32[]{:S(2)}) %collective-permute-start.5) | collective-permute-done | bytes 196640 | tf_op jit(solution)/shard_map/ppermute | solution.py:316
  32.1 1.6 %collective-permute-start.6 = (bf16[64,768]{1,0:T(8,128)(2,1)S(1)}, bf16[64,768]{1,0:T(8,128)(2,1)S(1)}, u32[]{:S(2)}, u32[]{:S(2)}) collective-permute-start(bf16[64,768]{1,0:T(8,128)(2,1)S(1)} %get-tuple-element.52), channel_id=1, source_target_pairs={{0,4},{4,0},{8,12},{12,8},{16,20},{20,16},{24,28},{28,24},{1,5},{5... | collective-permute-start | bytes 294920 | tf_op jit(solution)/shard_map/ppermute | solution.py:316
  33.7 4.1 %collective-permute-start.9 = (bf16[1024,128]{1,0:T(8,128)(2,1)S(1)}, bf16[1024,128]{1,0:T(8,128)(2,1)S(1)}, u32[]{:S(2)}, u32[]{:S(2)}) collective-permute-start(bf16[1024,128]{1,0:T(8,128)(2,1)S(1)} %get-tuple-element.30.high_ref), channel_id=1, source_target_pairs={{0,8},{4,12},{8,16},{12,20},{16,24},{20,28},{1,9},{5,13},{9,17},{1... | collective-permute-start | bytes 786440 | tf_op jit(solution)/shard_map/ppermute | solution.py:305
  37.8 1.3 %collective-permute-start.10 = (bf16[1024,128]{1,0:T(8,128)(2,1)S(1)}, bf16[1024,128]{1,0:T(8,128)(2,1)S(1)}, u32[]{:S(2)}, u32[]{:S(2)}) collective-permute-start(bf16[1024,128]{1,0:T(8,128)(2,1)S(1)} %get-tuple-element.31.low_ref), channel_id=1, source_target_pairs={{8,0},{12,4},{16,8},{20,12},{24,16},{28,20},{9,1},{13,5},{17,9},{2... | collective-permute-start | bytes 786440 | tf_op jit(solution)/shard_map/ppermute | solution.py:305
  39.1 2.4 %collective-permute-start.11 = (bf16[1024,256]{1,0:T(8,128)(2,1)}, bf16[1024,256]{1,0:T(8,128)(2,1)S(1)}, u32[]{:S(2)}, u32[]{:S(2)}) collective-permute-start(bf16[1024,256]{1,0:T(8,128)(2,1)} %constant_dynamic-update-slice_fusion), channel_id=1, source_target_pairs={{0,4},{4,8},{8,12},{12,16},{16,20},{20,24},{24,28},{1,5},{5,9},{9,... | collective-permute-start | bytes 1572872 | tf_op jit(solution)/shard_map/ppermute | solution.py:305
  41.5 4.0 %collective-permute-start.3 = (bf16[64,768]{1,0:T(8,128)(2,1)S(1)}, bf16[64,768]{1,0:T(8,128)(2,1)S(1)}, u32[]{:S(2)}, u32[]{:S(2)}) collective-permute-start(bf16[64,768]{1,0:T(8,128)(2,1)S(1)} %add_convert_fusion.3), channel_id=1, source_target_pairs={{0,16},{4,20},{8,24},{12,28},{16,0},{20,4},{24,8},{28,12},{1,17},{... | collective-permute-start | bytes 294920 | tf_op jit(solution)/shard_map/ppermute | solution.py:316
  45.6 3.1 %collective-permute-start.7 = (bf16[64,768]{1,0:T(8,128)(2,1)S(1)}, bf16[64,768]{1,0:T(8,128)(2,1)S(1)}, u32[]{:S(2)}, u32[]{:S(2)}) collective-permute-start(bf16[64,768]{1,0:T(8,128)(2,1)S(1)} %add_convert_fusion.2), channel_id=1, source_target_pairs={{0,4},{4,0},{8,12},{12,8},{16,20},{20,16},{24,28},{28,24},{1,5},{5... | collective-permute-start | bytes 294920 | tf_op jit(solution)/shard_map/ppermute | solution.py:316
  48.7 2.6 %collective-permute-done.7 = bf16[64,768]{1,0:T(8,128)(2,1)S(1)} collective-permute-done((bf16[64,768]{1,0:T(8,128)(2,1)S(1)}, bf16[64,768]{1,0:T(8,128)(2,1)S(1)}, u32[]{:S(2)}, u32[]{:S(2)}) %collective-permute-start.7) | collective-permute-done | bytes 98336 | tf_op jit(solution)/shard_map/ppermute | solution.py:316
  51.3 7.5 %collective-permute-start.12 = (bf16[128,768]{1,0:T(8,128)(2,1)S(1)}, bf16[128,768]{1,0:T(8,128)(2,1)S(1)}, u32[]{:S(2)}, u32[]{:S(2)}) collective-permute-start(bf16[128,768]{1,0:T(8,128)(2,1)S(1)} %pad_maximum_fusion.2), channel_id=1, source_target_pairs={{0,8},{4,12},{8,0},{12,4},{16,24},{20,28},{24,16},{28,20},{1,9},{5... | collective-permute-start | bytes 589832 | tf_op jit(solution)/shard_map/ppermute | solution.py:316
  58.9 0.1 pad_maximum_fusion.4
  58.9 0.1 reshape.19.edge_ref
  59.0 5.2 %collective-permute-start.13 = (bf16[128,768]{1,0:T(8,128)(2,1)S(1)}, bf16[128,768]{1,0:T(8,128)(2,1)S(1)}, u32[]{:S(2)}, u32[]{:S(2)}) collective-permute-start(bf16[128,768]{1,0:T(8,128)(2,1)S(1)} %pad_maximum_fusion.3), channel_id=1, source_target_pairs={{0,16},{4,20},{8,24},{12,28},{16,0},{20,4},{24,8},{28,12},{1,17},{... | collective-permute-start | bytes 589832 | tf_op jit(solution)/shard_map/ppermute | solution.py:316
  64.2 3.1 %shard_map.134 = (bf16[512,128]{1,0:T(8,128)(2,1)S(1)}, bf16[512,128]{1,0:T(8,128)(2,1)S(1)}) custom-call(f32[2,2]{1,0:T(2,128)S(1)} %reshape.19.edge_ref, s32[1,1]{1,0:T(1,128)} %bitcast.5.side_ref, bf16[512,256]{1,0:T(8,128)(2,1)S(1)} %copy-done.6, bf16[1536,128]{1,0:T(8,128)(2,1)S(1)} %collective-permute-done.8.other_ref, ...), custom_call_target="tpu_custom_call" | custom-call | flops 805306368 | bytes 2097152 | tf_op jit(solution)/shard_map/pallas_call | solution.py:42
  67.3 0.1 collective-permute-start.16
  67.4 1.3 %collective-permute-done.13 = bf16[128,768]{1,0:T(8,128)(2,1)S(1)} collective-permute-done((bf16[128,768]{1,0:T(8,128)(2,1)S(1)}, bf16[128,768]{1,0:T(8,128)(2,1)S(1)}, u32[]{:S(2)}, u32[]{:S(2)}) %collective-permute-start.13) | collective-permute-done | bytes 196640 | tf_op jit(solution)/shard_map/ppermute | solution.py:316
  68.7 0.8 collective-permute-start.14
  69.6 4.9 %collective-permute-start.15 = (bf16[256,768]{1,0:T(8,128)(2,1)S(1)}, bf16[256,768]{1,0:T(8,128)(2,1)S(1)}, u32[]{:S(2)}, u32[]{:S(2)}) collective-permute-start(bf16[256,768]{1,0:T(8,128)(2,1)S(1)} %pad_maximum_fusion.1.refs_2_), channel_id=1, source_target_pairs={{0,8},{4,12},{8,0},{12,4},{16,24},{20,28},{24,16},{28,20},{1,9},{5... | collective-permute-start | bytes 1179656 | tf_op jit(solution)/shard_map/ppermute | solution.py:316
  74.5 1.0 %collective-permute-done.16.refs_6_ = bf16[512,128]{1,0:T(8,128)(2,1)S(1)} collective-permute-done((bf16[512,128]{1,0:T(8,128)(2,1)S(1)}, bf16[512,128]{1,0:T(8,128)(2,1)S(1)}, u32[]{:S(2)}, u32[]{:S(2)}) %collective-permute-start.16) | collective-permute-done | bytes 131104 | tf_op jit(solution)/shard_map/ppermute | solution.py:316
  75.5 1.5 %collective-permute-start.17 = (bf16[1024,256]{1,0:T(8,128)(2,1)}, bf16[1024,256]{1,0:T(8,128)(2,1)S(1)}, u32[]{:S(2)}, u32[]{:S(2)}) collective-permute-start(bf16[1024,256]{1,0:T(8,128)(2,1)} %constant_dynamic-update-slice_fusion), channel_id=1, source_target_pairs={{4,0},{8,4},{12,8},{16,12},{20,16},{24,20},{28,24},{5,1},{9,5},{13... | collective-permute-start | bytes 1572872 | tf_op jit(solution)/shard_map/ppermute | solution.py:305
  77.0 0.6 add_bitcast_fusion.places_ref
  77.6 2.1 %collective-permute-done.14.refs_1_ = bf16[256,768]{1,0:T(8,128)(2,1)S(1)} collective-permute-done((bf16[256,768]{1,0:T(8,128)(2,1)S(1)}, bf16[256,768]{1,0:T(8,128)(2,1)S(1)}, u32[]{:S(2)}, u32[]{:S(2)}) %collective-permute-start.14) | collective-permute-done | bytes 393248 | tf_op jit(solution)/shard_map/ppermute | solution.py:316
  79.7 0.5 collective-permute-done.15.refs_3_
  80.2 0.2 copy-done.12
  80.5 0.5 copy-done.13
  81.0 6.9 %shard_map.135 = (bf16[3,64,512]{2,1,0:T(8,128)(2,1)}, bf16[512,256]{1,0:T(8,128)(2,1)}, bf16[512,256]{1,0:T(8,128)(2,1)}, bf16[512,256]{1,0:T(8,128)(2,1)}, bf16[512,256]{1,0:T(8,128)(2,1)}) custom-call(s32[1,1]{1,0:T(1,128)} %bitcast.4.place_ref, s32[1,1]{1,0:T(1,128)} %bitcast.5.side_ref, s32[1,4]{1,0:T(1,128)} %add_bitcast_fusion.places_ref, ...), custom_call_target="tpu_custom_call" | custom-call | flops 1000 | bytes 1000 | tf_op jit(solution)/shard_map/pallas_call | solution.py:42
  88.0 0.5 collective-permute-start.18
  88.5 1.0 convert_element_type.95
  89.5 0.2 collective-permute-done.19
  89.8 1.5 %collective-permute-start.21 = (bf16[256,256]{1,0:T(8,128)(2,1)S(1)}, bf16[256,256]{1,0:T(8,128)(2,1)S(1)}, u32[]{:S(2)}, u32[]{:S(2)}) collective-permute-start(bf16[256,256]{1,0:T(8,128)(2,1)S(1)} %get-tuple-element.46), channel_id=1, source_target_pairs={{0,2},{1,3},{2,0},{3,1},{4,6},{5,7},{6,4},{7,5},{8,10},{9,11},{10,... | collective-permute-start | bytes 393224 | tf_op jit(solution)/shard_map/ppermute | solution.py:311
  91.2 0.6 collective-permute-start.20
  91.9 4.3 %collective-permute-done.21.far_ref = bf16[256,256]{1,0:T(8,128)(2,1)S(1)} collective-permute-done((bf16[256,256]{1,0:T(8,128)(2,1)S(1)}, bf16[256,256]{1,0:T(8,128)(2,1)S(1)}, u32[]{:S(2)}, u32[]{:S(2)}) %collective-permute-start.21) | collective-permute-done | bytes 131104 | tf_op jit(solution)/shard_map/ppermute | solution.py:311
  96.2 2.0 %shard_map.136.refs_0_ = bf16[256,256]{1,0:T(8,128)(2,1)S(1)} custom-call(f32[2,2]{1,0:T(2,128)S(1)} %reshape.19.edge_ref, bf16[512,256]{1,0:T(8,128)(2,1)S(1)} %copy-done.4, bf16[512,256]{1,0:T(8,128)(2,1)S(1)} %copy-done.5, bf16[512,256]{1,0:T(8,128)(2,1)S(1)} %collective-permute-done.18.near_ref, bf16[256,256]{1,0:T(8,128)(2,1)S(1)} %collective-permute-done.21.far_ref, ...), custom_call_target="tpu_custom_call" | custom-call | flops 402653184 | bytes 2097152 | tf_op jit(solution)/shard_map/pallas_call | solution.py:42
  98.2 2.7 %shard_map.137 = bf16[512,256]{1,0:T(8,128)(2,1)} custom-call(f32[2,2]{1,0:T(2,128)S(1)} %reshape.19.edge_ref, bf16[512,256]{1,0:T(8,128)(2,1)S(1)} %copy-done.4, bf16[512,256]{1,0:T(8,128)(2,1)S(1)} %copy-done.5, bf16[512,256]{1,0:T(8,128)(2,1)S(1)} %collective-permute-done.18.near_ref, bf16[256,256]{1,0:T(8,128)(2,1)S(1)} %collective-permute-done.20.far_ref, ...), custom_call_target="tpu_custom_call" | custom-call | flops 402653184 | bytes 2097152 | tf_op jit(solution)/shard_map/pallas_call | solution.py:42
  (50 shorter events, 0.5 us)
Async XLA Ops:
  0.6 8.2 %copy-start.3 = (bf16[512,256]{1,0:T(8,128)(2,1)S(1)}, bf16[512,256]{1,0:T(8,128)(2,1)}, u32[]{:S(2)}) copy-start(bf16[512,256]{1,0:T(8,128)(2,1)} %values_ref.7) | copy-start | bytes 786436
  0.6 8.2 %copy-start.2 = (bf16[512,256]{1,0:T(8,128)(2,1)S(1)}, bf16[512,256]{1,0:T(8,128)(2,1)}, u32[]{:S(2)}) copy-start(bf16[512,256]{1,0:T(8,128)(2,1)} %keys_ref.7) | copy-start | bytes 786436
  0.7 8.2 %copy-start.6 = (bf16[512,256]{1,0:T(8,128)(2,1)S(1)}, bf16[512,256]{1,0:T(8,128)(2,1)}, u32[]{:S(2)}) copy-start(bf16[512,256]{1,0:T(8,128)(2,1)} %queries_ref.5) | copy-start | bytes 786436
  0.7 10.4 %copy-start = (bf16[512,256]{1,0:T(8,128)(2,1)S(1)}, bf16[512,256]{1,0:T(8,128)(2,1)}, u32[]{:S(2)}) copy-start(bf16[512,256]{1,0:T(8,128)(2,1)} %keys_ref.9) | copy-start | bytes 786436
  0.7 11.1 %copy-start.1 = (bf16[512,256]{1,0:T(8,128)(2,1)S(1)}, bf16[512,256]{1,0:T(8,128)(2,1)}, u32[]{:S(2)}) copy-start(bf16[512,256]{1,0:T(8,128)(2,1)} %values_ref.9) | copy-start | bytes 786436
  5.8 13.1 %copy-start.11 = (bf16[256,768]{1,0:T(8,128)(2,1)S(1)}, bf16[256,768]{1,0:T(8,128)(2,1)}, u32[]{:S(2)}) copy-start(bf16[256,768]{1,0:T(8,128)(2,1)} %get-tuple-element.24) | copy-start | bytes 1179652
  5.8 13.1 %collective-permute-start = (bf16[256,768]{1,0:T(8,128)(2,1)}, bf16[256,768]{1,0:T(8,128)(2,1)S(1)}, u32[]{:S(2)}, u32[]{:S(2)}) collective-permute-start(bf16[256,768]{1,0:T(8,128)(2,1)} %get-tuple-element.25), channel_id=1, source_target_pairs={{0,4},{4,0},{8,12},{12,8},{16,20},{20,16},{24,28},{28,24},{1,5},{5... | collective-permute-start | bytes 1179656 | tf_op jit(solution)/shard_map/ppermute | solution.py:316
  8.8 12.4 %copy-start.10 = (bf16[256,768]{1,0:T(8,128)(2,1)S(1)}, bf16[256,768]{1,0:T(8,128)(2,1)}, u32[]{:S(2)}) copy-start(bf16[256,768]{1,0:T(8,128)(2,1)} %get-tuple-element.26) | copy-start | bytes 1179652
  8.9 17.7 %collective-permute-start.8 = (bf16[1536,128]{1,0:T(8,128)(2,1)S(1)}, bf16[1536,128]{1,0:T(8,128)(2,1)S(1)}, u32[]{:S(2)}, u32[]{:S(2)}) collective-permute-start(bf16[1536,128]{1,0:T(8,128)(2,1)S(1)} %shard_map.132), channel_id=1, source_target_pairs={{0,4},{4,0},{8,12},{12,8},{16,20},{20,16},{24,28},{28,24},{1,5},{5... | collective-permute-start | bytes 1179656 | tf_op jit(solution)/shard_map/ppermute | solution.py:316
  9.0 12.2 %collective-permute-start.4 = (bf16[256,768]{1,0:T(8,128)(2,1)}, bf16[256,768]{1,0:T(8,128)(2,1)S(1)}, u32[]{:S(2)}, u32[]{:S(2)}) collective-permute-start(bf16[256,768]{1,0:T(8,128)(2,1)} %get-tuple-element.27), channel_id=1, source_target_pairs={{0,8},{4,12},{8,0},{12,4},{16,24},{20,28},{24,16},{28,20},{1,9},{5... | collective-permute-start | bytes 1179656 | tf_op jit(solution)/shard_map/ppermute | solution.py:316
  19.1 8.3 %collective-permute-start.1 = (bf16[128,768]{1,0:T(8,128)(2,1)S(1)}, bf16[128,768]{1,0:T(8,128)(2,1)S(1)}, u32[]{:S(2)}, u32[]{:S(2)}) collective-permute-start(bf16[128,768]{1,0:T(8,128)(2,1)S(1)} %get-tuple-element.50), channel_id=1, source_target_pairs={{0,8},{4,12},{8,0},{12,4},{16,24},{20,28},{24,16},{28,20},{1,9},{5... | collective-permute-start | bytes 589832 | tf_op jit(solution)/shard_map/ppermute | solution.py:316
  21.3 10.7 %collective-permute-start.5 = (bf16[128,768]{1,0:T(8,128)(2,1)S(1)}, bf16[128,768]{1,0:T(8,128)(2,1)S(1)}, u32[]{:S(2)}, u32[]{:S(2)}) collective-permute-start(bf16[128,768]{1,0:T(8,128)(2,1)S(1)} %get-tuple-element.48), channel_id=1, source_target_pairs={{0,16},{4,20},{8,24},{12,28},{16,0},{20,4},{24,8},{28,12},{1,17},{... | collective-permute-start | bytes 589832 | tf_op jit(solution)/shard_map/ppermute | solution.py:316
  27.4 14.1 %collective-permute-start.2 = (bf16[64,768]{1,0:T(8,128)(2,1)S(1)}, bf16[64,768]{1,0:T(8,128)(2,1)S(1)}, u32[]{:S(2)}, u32[]{:S(2)}) collective-permute-start(bf16[64,768]{1,0:T(8,128)(2,1)S(1)} %get-tuple-element.54), channel_id=1, source_target_pairs={{0,16},{4,20},{8,24},{12,28},{16,0},{20,4},{24,8},{28,12},{1,17},{... | collective-permute-start | bytes 294920 | tf_op jit(solution)/shard_map/ppermute | solution.py:316
  32.1 13.5 %collective-permute-start.6 = (bf16[64,768]{1,0:T(8,128)(2,1)S(1)}, bf16[64,768]{1,0:T(8,128)(2,1)S(1)}, u32[]{:S(2)}, u32[]{:S(2)}) collective-permute-start(bf16[64,768]{1,0:T(8,128)(2,1)S(1)} %get-tuple-element.52), channel_id=1, source_target_pairs={{0,4},{4,0},{8,12},{12,8},{16,20},{20,16},{24,28},{28,24},{1,5},{5... | collective-permute-start | bytes 294920 | tf_op jit(solution)/shard_map/ppermute | solution.py:316
  33.7 17.6 %collective-permute-start.9 = (bf16[1024,128]{1,0:T(8,128)(2,1)S(1)}, bf16[1024,128]{1,0:T(8,128)(2,1)S(1)}, u32[]{:S(2)}, u32[]{:S(2)}) collective-permute-start(bf16[1024,128]{1,0:T(8,128)(2,1)S(1)} %get-tuple-element.30.high_ref), channel_id=1, source_target_pairs={{0,8},{4,12},{8,16},{12,20},{16,24},{20,28},{1,9},{5,13},{9,17},{1... | collective-permute-start | bytes 786440 | tf_op jit(solution)/shard_map/ppermute | solution.py:305
  37.8 13.5 %collective-permute-start.10 = (bf16[1024,128]{1,0:T(8,128)(2,1)S(1)}, bf16[1024,128]{1,0:T(8,128)(2,1)S(1)}, u32[]{:S(2)}, u32[]{:S(2)}) collective-permute-start(bf16[1024,128]{1,0:T(8,128)(2,1)S(1)} %get-tuple-element.31.low_ref), channel_id=1, source_target_pairs={{8,0},{12,4},{16,8},{20,12},{24,16},{28,20},{9,1},{13,5},{17,9},{2... | collective-permute-start | bytes 786440 | tf_op jit(solution)/shard_map/ppermute | solution.py:305
  39.1 12.2 %collective-permute-start.11 = (bf16[1024,256]{1,0:T(8,128)(2,1)}, bf16[1024,256]{1,0:T(8,128)(2,1)S(1)}, u32[]{:S(2)}, u32[]{:S(2)}) collective-permute-start(bf16[1024,256]{1,0:T(8,128)(2,1)} %constant_dynamic-update-slice_fusion), channel_id=1, source_target_pairs={{0,4},{4,8},{8,12},{12,16},{16,20},{20,24},{24,28},{1,5},{5,9},{9,... | collective-permute-start | bytes 1572872 | tf_op jit(solution)/shard_map/ppermute | solution.py:305
  41.5 7.1 %collective-permute-start.3 = (bf16[64,768]{1,0:T(8,128)(2,1)S(1)}, bf16[64,768]{1,0:T(8,128)(2,1)S(1)}, u32[]{:S(2)}, u32[]{:S(2)}) collective-permute-start(bf16[64,768]{1,0:T(8,128)(2,1)S(1)} %add_convert_fusion.3), channel_id=1, source_target_pairs={{0,16},{4,20},{8,24},{12,28},{16,0},{20,4},{24,8},{28,12},{1,17},{... | collective-permute-start | bytes 294920 | tf_op jit(solution)/shard_map/ppermute | solution.py:316
  45.6 5.7 %collective-permute-start.7 = (bf16[64,768]{1,0:T(8,128)(2,1)S(1)}, bf16[64,768]{1,0:T(8,128)(2,1)S(1)}, u32[]{:S(2)}, u32[]{:S(2)}) collective-permute-start(bf16[64,768]{1,0:T(8,128)(2,1)S(1)} %add_convert_fusion.2), channel_id=1, source_target_pairs={{0,4},{4,0},{8,12},{12,8},{16,20},{20,16},{24,28},{28,24},{1,5},{5... | collective-permute-start | bytes 294920 | tf_op jit(solution)/shard_map/ppermute | solution.py:316
  51.3 16.1 %collective-permute-start.12 = (bf16[128,768]{1,0:T(8,128)(2,1)S(1)}, bf16[128,768]{1,0:T(8,128)(2,1)S(1)}, u32[]{:S(2)}, u32[]{:S(2)}) collective-permute-start(bf16[128,768]{1,0:T(8,128)(2,1)S(1)} %pad_maximum_fusion.2), channel_id=1, source_target_pairs={{0,8},{4,12},{8,0},{12,4},{16,24},{20,28},{24,16},{28,20},{1,9},{5... | collective-permute-start | bytes 589832 | tf_op jit(solution)/shard_map/ppermute | solution.py:316
  59.0 9.7 %collective-permute-start.13 = (bf16[128,768]{1,0:T(8,128)(2,1)S(1)}, bf16[128,768]{1,0:T(8,128)(2,1)S(1)}, u32[]{:S(2)}, u32[]{:S(2)}) collective-permute-start(bf16[128,768]{1,0:T(8,128)(2,1)S(1)} %pad_maximum_fusion.3), channel_id=1, source_target_pairs={{0,16},{4,20},{8,24},{12,28},{16,0},{20,4},{24,8},{28,12},{1,17},{... | collective-permute-start | bytes 589832 | tf_op jit(solution)/shard_map/ppermute | solution.py:316
  67.3 7.2 %copy-start.7 = (bf16[512,128]{1,0:T(8,128)(2,1)}, bf16[512,128]{1,0:T(8,128)(2,1)S(1)}, u32[]{:S(2)}) copy-start(bf16[512,128]{1,0:T(8,128)(2,1)S(1)} %get-tuple-element.35.refs_5_) | copy-start | bytes 393220
  67.3 8.2 %collective-permute-start.16 = (bf16[512,128]{1,0:T(8,128)(2,1)S(1)}, bf16[512,128]{1,0:T(8,128)(2,1)S(1)}, u32[]{:S(2)}, u32[]{:S(2)}) collective-permute-start(bf16[512,128]{1,0:T(8,128)(2,1)S(1)} %get-tuple-element.38), channel_id=1, source_target_pairs={{0,4},{4,0},{8,12},{12,8},{16,20},{20,16},{24,28},{28,24},{1,5},{5... | collective-permute-start | bytes 393224 | tf_op jit(solution)/shard_map/ppermute | solution.py:316
  67.4 12.8 %copy-start.8 = (bf16[256,768]{1,0:T(8,128)(2,1)}, bf16[256,768]{1,0:T(8,128)(2,1)S(1)}, u32[]{:S(2)}) copy-start(bf16[256,768]{1,0:T(8,128)(2,1)S(1)} %pad_maximum_fusion.refs_0_) | copy-start | bytes 1179652
  68.7 11.5 %copy-start.9 = (bf16[256,768]{1,0:T(8,128)(2,1)}, bf16[256,768]{1,0:T(8,128)(2,1)S(1)}, u32[]{:S(2)}) copy-start(bf16[256,768]{1,0:T(8,128)(2,1)S(1)} %pad_maximum_fusion.1.refs_2_) | copy-start | bytes 1179652
  68.7 11.0 %collective-permute-start.14 = (bf16[256,768]{1,0:T(8,128)(2,1)S(1)}, bf16[256,768]{1,0:T(8,128)(2,1)S(1)}, u32[]{:S(2)}, u32[]{:S(2)}) collective-permute-start(bf16[256,768]{1,0:T(8,128)(2,1)S(1)} %pad_maximum_fusion.refs_0_), channel_id=1, source_target_pairs={{0,4},{4,0},{8,12},{12,8},{16,20},{20,16},{24,28},{28,24},{1,5},{5... | collective-permute-start | bytes 1179656 | tf_op jit(solution)/shard_map/ppermute | solution.py:316
  69.6 10.7 %collective-permute-start.15 = (bf16[256,768]{1,0:T(8,128)(2,1)S(1)}, bf16[256,768]{1,0:T(8,128)(2,1)S(1)}, u32[]{:S(2)}, u32[]{:S(2)}) collective-permute-start(bf16[256,768]{1,0:T(8,128)(2,1)S(1)} %pad_maximum_fusion.1.refs_2_), channel_id=1, source_target_pairs={{0,8},{4,12},{8,0},{12,4},{16,24},{20,28},{24,16},{28,20},{1,9},{5... | collective-permute-start | bytes 1179656 | tf_op jit(solution)/shard_map/ppermute | solution.py:316
  75.5 4.7 %copy-start.14 = (bf16[512,128]{1,0:T(8,128)(2,1)}, bf16[512,128]{1,0:T(8,128)(2,1)S(1)}, u32[]{:S(2)}) copy-start(bf16[512,128]{1,0:T(8,128)(2,1)S(1)} %collective-permute-done.16.refs_6_) | copy-start | bytes 393220
  75.5 12.5 %collective-permute-start.17 = (bf16[1024,256]{1,0:T(8,128)(2,1)}, bf16[1024,256]{1,0:T(8,128)(2,1)S(1)}, u32[]{:S(2)}, u32[]{:S(2)}) collective-permute-start(bf16[1024,256]{1,0:T(8,128)(2,1)} %constant_dynamic-update-slice_fusion), channel_id=1, source_target_pairs={{4,0},{8,4},{12,8},{16,12},{20,16},{24,20},{28,24},{5,1},{9,5},{13... | collective-permute-start | bytes 1572872 | tf_op jit(solution)/shard_map/ppermute | solution.py:305
  79.7 0.8 copy-start.12
  80.2 0.7 copy-start.13
  87.9 8.3 %copy-start.4 = (bf16[512,256]{1,0:T(8,128)(2,1)S(1)}, bf16[512,256]{1,0:T(8,128)(2,1)}, u32[]{:S(2)}) copy-start(bf16[512,256]{1,0:T(8,128)(2,1)} %queries_ref.7) | copy-start | bytes 786436
  87.9 8.3 %copy-start.5 = (bf16[512,256]{1,0:T(8,128)(2,1)S(1)}, bf16[512,256]{1,0:T(8,128)(2,1)}, u32[]{:S(2)}) copy-start(bf16[512,256]{1,0:T(8,128)(2,1)} %get-tuple-element.39.keep_ref) | copy-start | bytes 786436
  87.9 1.8 %collective-permute-start.19 = (bf16[512,256]{1,0:T(8,128)(2,1)}, bf16[512,256]{1,0:T(8,128)(2,1)S(1)}, u32[]{:S(2)}, u32[]{:S(2)}) collective-permute-start(bf16[512,256]{1,0:T(8,128)(2,1)} %get-tuple-element.44), channel_id=1, source_target_pairs={{0,1},{1,0},{2,3},{3,2},{4,5},{5,4},{6,7},{7,6},{8,9},{9,8},{10,11... | collective-permute-start | bytes 786440 | tf_op jit(solution)/shard_map/ppermute | solution.py:311
  88.0 3.9 %collective-permute-start.18 = (bf16[512,256]{1,0:T(8,128)(2,1)}, bf16[512,256]{1,0:T(8,128)(2,1)S(1)}, u32[]{:S(2)}, u32[]{:S(2)}) collective-permute-start(bf16[512,256]{1,0:T(8,128)(2,1)} %get-tuple-element.42), channel_id=1, source_target_pairs={{0,1},{1,0},{2,3},{3,2},{4,5},{5,4},{6,7},{7,6},{8,9},{9,8},{10,11... | collective-permute-start | bytes 786440 | tf_op jit(solution)/shard_map/ppermute | solution.py:311
  89.8 6.4 %collective-permute-start.21 = (bf16[256,256]{1,0:T(8,128)(2,1)S(1)}, bf16[256,256]{1,0:T(8,128)(2,1)S(1)}, u32[]{:S(2)}, u32[]{:S(2)}) collective-permute-start(bf16[256,256]{1,0:T(8,128)(2,1)S(1)} %get-tuple-element.46), channel_id=1, source_target_pairs={{0,2},{1,3},{2,0},{3,1},{4,6},{5,7},{6,4},{7,5},{8,10},{9,11},{10,... | collective-permute-start | bytes 393224 | tf_op jit(solution)/shard_map/ppermute | solution.py:311
  91.2 7.0 %collective-permute-start.20 = (bf16[256,256]{1,0:T(8,128)(2,1)S(1)}, bf16[256,256]{1,0:T(8,128)(2,1)S(1)}, u32[]{:S(2)}, u32[]{:S(2)}) collective-permute-start(bf16[256,256]{1,0:T(8,128)(2,1)S(1)} %get-tuple-element.47), channel_id=1, source_target_pairs={{0,2},{1,3},{2,0},{3,1},{4,6},{5,7},{6,4},{7,5},{8,10},{9,11},{10,... | collective-permute-start | bytes 393224 | tf_op jit(solution)/shard_map/ppermute | solution.py:311

commit v22 on v21

--- a/solution.py
+++ b/solution.py
@@ -57,49 +57,76 @@
     return slot
 
 
-def gradient_kernel(orders, place_ref, rates_ref, keys_ref, values_ref, weights_ref, *refs):
-    out_refs, chunk_refs = refs[:-2], refs[-2:]
+def gradient_kernel(orders, place_ref, rates_ref, keys_hbm, values_hbm, weights_hbm, *refs):
+    out_refs, chunk_refs = refs[:-7], refs[-7:-5]
+    keys_ref, values_ref, weights_ref, load_sems, store_sems = refs[-5:]
     place = place_ref[0, 0]
     rates = rates_ref[...]
-    keys = keys_ref[...]
-    values = values_ref[...]
-    hidden_size = chunk_refs[0].shape[0]
-    width = weights_ref.shape[2]
-    turn = pl.program_id(0)
-    step = weights_ref.shape[1]
+    hidden_size, width = weights_ref.shape[1:]
+    loads = [
+        pltpu.make_async_copy(source, target, load_sems.at[index])
+        for index, (source, target) in enumerate(
+            [
+                (keys_hbm, keys_ref),
+                (weights_hbm.at[0], weights_ref.at[0]),
+                (weights_hbm.at[1], weights_ref.at[1]),
+                (values_hbm, values_ref),
+                (weights_hbm.at[2], weights_ref.at[2]),
+            ]
+        )
+    ]
+    for load in loads:
+        load.start()
 
     def put(chunk, columns, product):
         order = orders[chunk]
-        block_rows = min(step, hidden_size >> len(order))
-        for start in range(0, step, block_rows):
-            row = turn * step + start
-            if order:
-                block = turn * (step // block_rows) + start // block_rows
-                row = slot_of(block ^ place, order) * block_rows
-            row = pl.multiple_of(row, block_rows)
-            chunk_refs[chunk][pl.ds(row, block_rows), columns] = product[start:start + block_rows]
-
+        block_rows = hidden_size >> len(order)
+        for block in range(1 << len(order)):
+            row = pl.multiple_of(slot_of(block ^ place, order) * block_rows, block_rows) if order else 0
+            chunk_refs[chunk][pl.ds(row, block_rows), columns] = product[
+                block * block_rows:(block + 1) * block_rows
+            ]
+
+    def stores_of(chunk):
+        halves = len(out_refs) // 2
+        half_rows = hidden_size // halves
+        stores = []
+        for half in reversed(range(halves)):
+            index = chunk * halves + half
+            stores.append(
+                pltpu.make_async_copy(
+                    chunk_refs[chunk].at[pl.ds(half * half_rows, half_rows), :],
+                    out_refs[index],
+                    store_sems.at[index],
+                )
+            )
+        for store in stores:
+            store.start()
+        return stores
+
+    loads[0].wait()
+    loads[1].wait()
+    keys = keys_ref[...]
     gate = dot_nt(weights_ref[0], keys) * INVERSE
-    up = dot_nt(weights_ref[1], keys) * INVERSE
     sigmoid = jax.nn.sigmoid(gate)
     silu = gate * sigmoid
+    loads[2].wait()
+    up = dot_nt(weights_ref[1], keys) * INVERSE
     hidden = (rates * silu * up).astype(BF16)
+    loads[3].wait()
+    values = values_ref[...]
+    put(1, slice(0, width), dot_nn(hidden, values).astype(BF16))
+    loads[4].wait()
     backward = rates * dot_nt(weights_ref[2], values)
-    d_gate = (backward * up * sigmoid * (1.0 + gate * (1.0 - sigmoid)) * INVERSE).astype(BF16)
     d_up = (backward * silu * INVERSE).astype(BF16)
     up_part = dot_nn(d_up, keys).astype(BF16)
+    put(1, slice(width, width + width // 2), up_part[:, width // 2:])
+    stores = stores_of(1)
+    put(0, slice(width, width + width // 2), up_part[:, :width // 2])
+    d_gate = (backward * up * sigmoid * (1.0 + gate * (1.0 - sigmoid)) * INVERSE).astype(BF16)
     put(0, slice(0, width), dot_nn(d_gate, keys).astype(BF16))
-    put(0, slice(width, width + width // 2), up_part[:, :width // 2])
-    put(1, slice(0, width), dot_nn(hidden, values).astype(BF16))
-    put(1, slice(width, width + width // 2), up_part[:, width // 2:])
-
-    @pl.when(turn == pl.num_programs(0) - 1)
-    def _():
-        halves = len(out_refs) // 2
-        half_rows = hidden_size // halves
-        for index, out_ref in enumerate(out_refs):
-            half = index % halves
-            out_ref[...] = chunk_refs[index // halves][half * half_rows:(half + 1) * half_rows, :]
+    for store in stores + stores_of(0):
+        store.wait()
 
 
 def attend_rows(edge_prev, edge_next, query_tile, keys_prev, keys_own, keys_next,
@@ -225,7 +252,7 @@
         pltpu.make_async_copy(source, target, sems.at[index])
         for index, (source, target) in enumerate(zip(sources, loaded))
     ]
-    for copy in copies:
+    for copy in copies[:-4]:
         copy.start()
     pieces, (weights_ref, keep_ref, other_ref, map_ref, output_ref) = loaded[:-5], loaded[-5:]
     place = place_ref[0, 0]
@@ -233,6 +260,8 @@
     hidden_size, width = weights_ref.shape[1:]
     for copy in copies[:-5]:
         copy.wait()
+    for copy in copies[-4:]:
+        copy.start()
     limit_norm = math.sqrt(FAST_HIDDEN * FAST_DIM) / 2.0
     step = 64
     square = jnp.zeros((1, pieces[0].shape[1]), F32)
@@ -386,20 +415,26 @@
     halves = 2 if halving else 1
     chunk_width = fast_width + fast_width // 2
     out_shapes = [shape((hidden_size // halves, chunk_width), BF16)] * (2 * halves)
-    whole = pl.BlockSpec(memory_space=pltpu.VMEM)
+    anywhere = pl.BlockSpec(memory_space=pl.ANY)
     gradients = pl.pallas_call(
         functools.partial(gradient_kernel, orders),
-        grid=(1,),
         out_shape=out_shapes,
         in_specs=[
             pl.BlockSpec(memory_space=pltpu.SMEM),
-            whole,
-            whole,
-            whole,
-            pl.BlockSpec((3, hidden_size, fast_width), lambda turn: (0, turn, 0)),
+            pl.BlockSpec(memory_space=pltpu.VMEM),
+            anywhere,
+            anywhere,
+            anywhere,
         ],
-        out_specs=[whole] * len(out_shapes),
-        scratch_shapes=[pltpu.VMEM((hidden_size, chunk_width), BF16)] * 2,
+        out_specs=[anywhere] * len(out_shapes),
+        scratch_shapes=[pltpu.VMEM((hidden_size, chunk_width), BF16)] * 2
+        + [
+            pltpu.VMEM(fast_keys.shape, BF16),
+            pltpu.VMEM(fast_values.shape, BF16),
+            pltpu.VMEM(weights.shape, BF16),
+            pltpu.SemaphoreType.DMA((5,)),
+            pltpu.SemaphoreType.DMA((len(out_shapes),)),
+        ],
         compiler_params=pltpu.CompilerParams(vmem_limit_bytes=VMEM_MOST),
         cost_estimate=pl.CostEstimate(flops=1000, bytes_accessed=1000, transcendentals=0),
     )(place, step_rates.reshape(1, rows), fast_keys, fast_values, weights)

time: 101 us -> 102 us (level)
  no operation moved by 1% of the time
where the time goes in v22:
time: 102 us
  starting transfers between devices  51.4 us (50%)
  waiting for transfers between devices  24.2 us (24%)
  Pallas kernels  20.7 us (20%)
  local copies, waits for them, and re-layouts  2.33 us (2%)
  other arithmetic  2.09 us (2%)
    ppermute x14, starting transfers between devices, seq_swap(): lax.ppermute(value, 'seq', [(i, i ^ step) for i in range(lax.axis_size('s...  39.5 us
    ppermute x14, waiting for transfers between devices, seq_swap(): lax.ppermute(value, 'seq', [(i, i ^ step) for i in range(lax.axis_size('s...  19.6 us
    pallas_call x6, Pallas kernels, call(): pl.pallas_call(body, out_shape=out_shapes, in_specs=in_specs, out_specs=j...  14.8 us
    ppermute x4, starting transfers between devices, seq_shift(): lax.ppermute(value, 'seq', [(i, i + step) for i in range(peers) if 0 <= i...  9.28 us
    pallas_call x1, Pallas kernels, local(): pl.pallas_call(functools.partial(gradient_kernel, orders), out_shape=out_...  5.83 us
    ppermute x4, waiting for transfers between devices, head_swap(): lax.ppermute(value, 'head', [(i, i ^ bit) for i in range(lax.axis_size('h...  4.56 us
    ppermute x4, starting transfers between devices, head_swap(): lax.ppermute(value, 'head', [(i, i ^ bit) for i in range(lax.axis_size('h...  2.65 us
  transfers between devices with their start and end apart: 22, of which 11 were waited for; matrix products, arithmetic and copies ran while one was open for 4% of the time, Pallas kernels for 12%

profile of v22, /device:TPU:0, one launch (start us, length us, event | category | flops | bytes accessed | tf_op | source)
XLA Modules:
  0.0 101.6 jit_solution(6886802221819093051)
XLA Ops:
  0.7 5.8 %shard_map.131 = (bf16[256,768]{1,0:T(8,128)(2,1)}, bf16[256,768]{1,0:T(8,128)(2,1)}, bf16[256,768]{1,0:T(8,128)(2,1)}, bf16[256,768]{1,0:T(8,128)(2,1)}) custom-call(s32[1,1]{1,0:T(1,128)} %bitcast.4.place_ref, f32[1,512]{1,0:T(1,128)} %bitcast.23, bf16[512,512]{1,0:T(8,128)(2,1)} %keys_hbm.1, bf16[512,512]{1,0:T(8,128)(2,1)} %values_hbm.1, ...), custom_call_target="tpu_custom_call" | custom-call | flops 1000 | bytes 1000 | tf_op jit(solution)/shard_map/pallas_call | solution.py:419
  6.5 3.0 %collective-permute-start = (bf16[256,768]{1,0:T(8,128)(2,1)}, bf16[256,768]{1,0:T(8,128)(2,1)S(1)}, u32[]{:S(2)}, u32[]{:S(2)}) collective-permute-start(bf16[256,768]{1,0:T(8,128)(2,1)} %get-tuple-element.25), channel_id=1, source_target_pairs={{0,4},{4,0},{8,12},{12,8},{16,20},{20,16},{24,28},{28,24},{1,5},{5... | collective-permute-start | bytes 1179656 | tf_op jit(solution)/shard_map/ppermute | solution.py:345
  9.6 0.1 shard_map.132
  9.7 0.1 collective-permute-start.8
  9.8 2.0 %collective-permute-start.4 = (bf16[256,768]{1,0:T(8,128)(2,1)}, bf16[256,768]{1,0:T(8,128)(2,1)S(1)}, u32[]{:S(2)}, u32[]{:S(2)}) collective-permute-start(bf16[256,768]{1,0:T(8,128)(2,1)} %get-tuple-element.27), channel_id=1, source_target_pairs={{0,8},{4,12},{8,0},{12,4},{16,24},{20,28},{24,16},{28,20},{1,9},{5... | collective-permute-start | bytes 1179656 | tf_op jit(solution)/shard_map/ppermute | solution.py:345
  11.8 0.7 constant_dynamic-update-slice_fusion.1
  12.5 0.7 constant_dynamic-update-slice_fusion
  13.3 6.5 %collective-permute-done = bf16[256,768]{1,0:T(8,128)(2,1)S(1)} collective-permute-done((bf16[256,768]{1,0:T(8,128)(2,1)}, bf16[256,768]{1,0:T(8,128)(2,1)S(1)}, u32[]{:S(2)}, u32[]{:S(2)}) %collective-permute-start) | collective-permute-done | bytes 393248 | tf_op jit(solution)/shard_map/ppermute | solution.py:345
  19.7 0.1 add_convert_fusion.1
  19.8 2.2 %collective-permute-start.1 = (bf16[128,768]{1,0:T(8,128)(2,1)S(1)}, bf16[128,768]{1,0:T(8,128)(2,1)S(1)}, u32[]{:S(2)}, u32[]{:S(2)}) collective-permute-start(bf16[128,768]{1,0:T(8,128)(2,1)S(1)} %get-tuple-element.50), channel_id=1, source_target_pairs={{0,8},{4,12},{8,0},{12,4},{16,24},{20,28},{24,16},{28,20},{1,9},{5... | collective-permute-start | bytes 589832 | tf_op jit(solution)/shard_map/ppermute | solution.py:345
  22.0 0.1 add_convert_fusion
  22.1 2.6 %collective-permute-start.5 = (bf16[128,768]{1,0:T(8,128)(2,1)S(1)}, bf16[128,768]{1,0:T(8,128)(2,1)S(1)}, u32[]{:S(2)}, u32[]{:S(2)}) collective-permute-start(bf16[128,768]{1,0:T(8,128)(2,1)S(1)} %get-tuple-element.48), channel_id=1, source_target_pairs={{0,16},{4,20},{8,24},{12,28},{16,0},{20,4},{24,8},{28,12},{1,17},{... | collective-permute-start | bytes 589832 | tf_op jit(solution)/shard_map/ppermute | solution.py:345
  24.7 2.6 %collective-permute-done.8.other_ref = bf16[1536,128]{1,0:T(8,128)(2,1)S(1)} collective-permute-done((bf16[1536,128]{1,0:T(8,128)(2,1)S(1)}, bf16[1536,128]{1,0:T(8,128)(2,1)S(1)}, u32[]{:S(2)}, u32[]{:S(2)}) %collective-permute-start.8) | collective-permute-done | bytes 393248 | tf_op jit(solution)/shard_map/ppermute | solution.py:345
  27.4 0.7 collective-permute-done.1
  28.2 2.1 %collective-permute-start.2 = (bf16[64,768]{1,0:T(8,128)(2,1)S(1)}, bf16[64,768]{1,0:T(8,128)(2,1)S(1)}, u32[]{:S(2)}, u32[]{:S(2)}) collective-permute-start(bf16[64,768]{1,0:T(8,128)(2,1)S(1)} %get-tuple-element.54), channel_id=1, source_target_pairs={{0,16},{4,20},{8,24},{12,28},{16,0},{20,4},{24,8},{28,12},{1,17},{... | collective-permute-start | bytes 294920 | tf_op jit(solution)/shard_map/ppermute | solution.py:345
  30.3 2.4 %collective-permute-done.5 = bf16[128,768]{1,0:T(8,128)(2,1)S(1)} collective-permute-done((bf16[128,768]{1,0:T(8,128)(2,1)S(1)}, bf16[128,768]{1,0:T(8,128)(2,1)S(1)}, u32[]{:S(2)}, u32[]{:S(2)}) %collective-permute-start.5) | collective-permute-done | bytes 196640 | tf_op jit(solution)/shard_map/ppermute | solution.py:345
  32.8 1.6 %collective-permute-start.6 = (bf16[64,768]{1,0:T(8,128)(2,1)S(1)}, bf16[64,768]{1,0:T(8,128)(2,1)S(1)}, u32[]{:S(2)}, u32[]{:S(2)}) collective-permute-start(bf16[64,768]{1,0:T(8,128)(2,1)S(1)} %get-tuple-element.52), channel_id=1, source_target_pairs={{0,4},{4,0},{8,12},{12,8},{16,20},{20,16},{24,28},{28,24},{1,5},{5... | collective-permute-start | bytes 294920 | tf_op jit(solution)/shard_map/ppermute | solution.py:345
  34.4 4.1 %collective-permute-start.9 = (bf16[1024,128]{1,0:T(8,128)(2,1)S(1)}, bf16[1024,128]{1,0:T(8,128)(2,1)S(1)}, u32[]{:S(2)}, u32[]{:S(2)}) collective-permute-start(bf16[1024,128]{1,0:T(8,128)(2,1)S(1)} %get-tuple-element.30.high_ref), channel_id=1, source_target_pairs={{0,8},{4,12},{8,16},{12,20},{16,24},{20,28},{1,9},{5,13},{9,17},{1... | collective-permute-start | bytes 786440 | tf_op jit(solution)/shard_map/ppermute | solution.py:334
  38.5 1.3 %collective-permute-start.10 = (bf16[1024,128]{1,0:T(8,128)(2,1)S(1)}, bf16[1024,128]{1,0:T(8,128)(2,1)S(1)}, u32[]{:S(2)}, u32[]{:S(2)}) collective-permute-start(bf16[1024,128]{1,0:T(8,128)(2,1)S(1)} %get-tuple-element.31.low_ref), channel_id=1, source_target_pairs={{8,0},{12,4},{16,8},{20,12},{24,16},{28,20},{9,1},{13,5},{17,9},{2... | collective-permute-start | bytes 786440 | tf_op jit(solution)/shard_map/ppermute | solution.py:334
  39.8 2.4 %collective-permute-start.11 = (bf16[1024,256]{1,0:T(8,128)(2,1)}, bf16[1024,256]{1,0:T(8,128)(2,1)S(1)}, u32[]{:S(2)}, u32[]{:S(2)}) collective-permute-start(bf16[1024,256]{1,0:T(8,128)(2,1)} %constant_dynamic-update-slice_fusion), channel_id=1, source_target_pairs={{0,4},{4,8},{8,12},{12,16},{16,20},{20,24},{24,28},{1,5},{5,9},{9,... | collective-permute-start | bytes 1572872 | tf_op jit(solution)/shard_map/ppermute | solution.py:334
  42.3 4.0 %collective-permute-start.3 = (bf16[64,768]{1,0:T(8,128)(2,1)S(1)}, bf16[64,768]{1,0:T(8,128)(2,1)S(1)}, u32[]{:S(2)}, u32[]{:S(2)}) collective-permute-start(bf16[64,768]{1,0:T(8,128)(2,1)S(1)} %add_convert_fusion.3), channel_id=1, source_target_pairs={{0,16},{4,20},{8,24},{12,28},{16,0},{20,4},{24,8},{28,12},{1,17},{... | collective-permute-start | bytes 294920 | tf_op jit(solution)/shard_map/ppermute | solution.py:345
  46.4 3.1 %collective-permute-start.7 = (bf16[64,768]{1,0:T(8,128)(2,1)S(1)}, bf16[64,768]{1,0:T(8,128)(2,1)S(1)}, u32[]{:S(2)}, u32[]{:S(2)}) collective-permute-start(bf16[64,768]{1,0:T(8,128)(2,1)S(1)} %add_convert_fusion.2), channel_id=1, source_target_pairs={{0,4},{4,0},{8,12},{12,8},{16,20},{20,16},{24,28},{28,24},{1,5},{5... | collective-permute-start | bytes 294920 | tf_op jit(solution)/shard_map/ppermute | solution.py:345
  49.5 2.6 %collective-permute-done.7 = bf16[64,768]{1,0:T(8,128)(2,1)S(1)} collective-permute-done((bf16[64,768]{1,0:T(8,128)(2,1)S(1)}, bf16[64,768]{1,0:T(8,128)(2,1)S(1)}, u32[]{:S(2)}, u32[]{:S(2)}) %collective-permute-start.7) | collective-permute-done | bytes 98336 | tf_op jit(solution)/shard_map/ppermute | solution.py:345
  52.1 7.5 %collective-permute-start.12 = (bf16[128,768]{1,0:T(8,128)(2,1)S(1)}, bf16[128,768]{1,0:T(8,128)(2,1)S(1)}, u32[]{:S(2)}, u32[]{:S(2)}) collective-permute-start(bf16[128,768]{1,0:T(8,128)(2,1)S(1)} %pad_maximum_fusion.2), channel_id=1, source_target_pairs={{0,8},{4,12},{8,0},{12,4},{16,24},{20,28},{24,16},{28,20},{1,9},{5... | collective-permute-start | bytes 589832 | tf_op jit(solution)/shard_map/ppermute | solution.py:345
  59.6 0.1 pad_maximum_fusion.4
  59.7 0.1 reshape.19.edge_ref
  59.8 5.3 %collective-permute-start.13 = (bf16[128,768]{1,0:T(8,128)(2,1)S(1)}, bf16[128,768]{1,0:T(8,128)(2,1)S(1)}, u32[]{:S(2)}, u32[]{:S(2)}) collective-permute-start(bf16[128,768]{1,0:T(8,128)(2,1)S(1)} %pad_maximum_fusion.3), channel_id=1, source_target_pairs={{0,16},{4,20},{8,24},{12,28},{16,0},{20,4},{24,8},{28,12},{1,17},{... | collective-permute-start | bytes 589832 | tf_op jit(solution)/shard_map/ppermute | solution.py:345
  65.1 3.0 %shard_map.134 = (bf16[512,128]{1,0:T(8,128)(2,1)S(1)}, bf16[512,128]{1,0:T(8,128)(2,1)S(1)}) custom-call(f32[2,2]{1,0:T(2,128)S(1)} %reshape.19.edge_ref, s32[1,1]{1,0:T(1,128)} %bitcast.5.side_ref, bf16[512,256]{1,0:T(8,128)(2,1)S(1)} %copy-done.6, bf16[1536,128]{1,0:T(8,128)(2,1)S(1)} %collective-permute-done.8.other_ref, ...), custom_call_target="tpu_custom_call" | custom-call | flops 805306368 | bytes 2097152 | tf_op jit(solution)/shard_map/pallas_call | solution.py:42
  68.1 0.1 collective-permute-start.16
  68.3 1.2 %collective-permute-done.13 = bf16[128,768]{1,0:T(8,128)(2,1)S(1)} collective-permute-done((bf16[128,768]{1,0:T(8,128)(2,1)S(1)}, bf16[128,768]{1,0:T(8,128)(2,1)S(1)}, u32[]{:S(2)}, u32[]{:S(2)}) %collective-permute-start.13) | collective-permute-done | bytes 196640 | tf_op jit(solution)/shard_map/ppermute | solution.py:345
  69.5 0.9 collective-permute-start.14
  70.4 4.8 %collective-permute-start.15 = (bf16[256,768]{1,0:T(8,128)(2,1)S(1)}, bf16[256,768]{1,0:T(8,128)(2,1)S(1)}, u32[]{:S(2)}, u32[]{:S(2)}) collective-permute-start(bf16[256,768]{1,0:T(8,128)(2,1)S(1)} %pad_maximum_fusion.1.refs_2_), channel_id=1, source_target_pairs={{0,8},{4,12},{8,0},{12,4},{16,24},{20,28},{24,16},{28,20},{1,9},{5... | collective-permute-start | bytes 1179656 | tf_op jit(solution)/shard_map/ppermute | solution.py:345
  75.2 1.1 %collective-permute-done.16.refs_6_ = bf16[512,128]{1,0:T(8,128)(2,1)S(1)} collective-permute-done((bf16[512,128]{1,0:T(8,128)(2,1)S(1)}, bf16[512,128]{1,0:T(8,128)(2,1)S(1)}, u32[]{:S(2)}, u32[]{:S(2)}) %collective-permute-start.16) | collective-permute-done | bytes 131104 | tf_op jit(solution)/shard_map/ppermute | solution.py:345
  76.3 1.5 %collective-permute-start.17 = (bf16[1024,256]{1,0:T(8,128)(2,1)}, bf16[1024,256]{1,0:T(8,128)(2,1)S(1)}, u32[]{:S(2)}, u32[]{:S(2)}) collective-permute-start(bf16[1024,256]{1,0:T(8,128)(2,1)} %constant_dynamic-update-slice_fusion), channel_id=1, source_target_pairs={{4,0},{8,4},{12,8},{16,12},{20,16},{24,20},{28,24},{5,1},{9,5},{13... | collective-permute-start | bytes 1572872 | tf_op jit(solution)/shard_map/ppermute | solution.py:334
  77.8 0.6 add_bitcast_fusion.places_ref
  78.4 2.1 %collective-permute-done.14.refs_1_ = bf16[256,768]{1,0:T(8,128)(2,1)S(1)} collective-permute-done((bf16[256,768]{1,0:T(8,128)(2,1)S(1)}, bf16[256,768]{1,0:T(8,128)(2,1)S(1)}, u32[]{:S(2)}, u32[]{:S(2)}) %collective-permute-start.14) | collective-permute-done | bytes 393248 | tf_op jit(solution)/shard_map/ppermute | solution.py:345
  80.5 0.4 collective-permute-done.15.refs_3_
  80.9 0.4 copy-done.12
  81.3 0.4 copy-done.13
  81.7 6.9 %shard_map.135 = (bf16[3,64,512]{2,1,0:T(8,128)(2,1)}, bf16[512,256]{1,0:T(8,128)(2,1)}, bf16[512,256]{1,0:T(8,128)(2,1)}, bf16[512,256]{1,0:T(8,128)(2,1)}, bf16[512,256]{1,0:T(8,128)(2,1)}) custom-call(s32[1,1]{1,0:T(1,128)} %bitcast.4.place_ref, s32[1,1]{1,0:T(1,128)} %bitcast.5.side_ref, s32[1,4]{1,0:T(1,128)} %add_bitcast_fusion.places_ref, ...), custom_call_target="tpu_custom_call" | custom-call | flops 1000 | bytes 1000 | tf_op jit(solution)/shard_map/pallas_call | solution.py:42
  88.7 0.5 collective-permute-start.18
  89.2 1.0 convert_element_type.95
  90.2 0.2 collective-permute-done.19
  90.5 1.6 %collective-permute-start.21 = (bf16[256,256]{1,0:T(8,128)(2,1)S(1)}, bf16[256,256]{1,0:T(8,128)(2,1)S(1)}, u32[]{:S(2)}, u32[]{:S(2)}) collective-permute-start(bf16[256,256]{1,0:T(8,128)(2,1)S(1)} %get-tuple-element.46), channel_id=1, source_target_pairs={{0,2},{1,3},{2,0},{3,1},{4,6},{5,7},{6,4},{7,5},{8,10},{9,11},{10,... | collective-permute-start | bytes 393224 | tf_op jit(solution)/shard_map/ppermute | solution.py:340
  92.1 0.5 collective-permute-start.20
  92.6 4.3 %collective-permute-done.21.far_ref = bf16[256,256]{1,0:T(8,128)(2,1)S(1)} collective-permute-done((bf16[256,256]{1,0:T(8,128)(2,1)S(1)}, bf16[256,256]{1,0:T(8,128)(2,1)S(1)}, u32[]{:S(2)}, u32[]{:S(2)}) %collective-permute-start.21) | collective-permute-done | bytes 131104 | tf_op jit(solution)/shard_map/ppermute | solution.py:340
  96.9 2.0 %shard_map.136.refs_0_ = bf16[256,256]{1,0:T(8,128)(2,1)S(1)} custom-call(f32[2,2]{1,0:T(2,128)S(1)} %reshape.19.edge_ref, bf16[512,256]{1,0:T(8,128)(2,1)S(1)} %copy-done.4, bf16[512,256]{1,0:T(8,128)(2,1)S(1)} %copy-done.5, bf16[512,256]{1,0:T(8,128)(2,1)S(1)} %collective-permute-done.18.near_ref, bf16[256,256]{1,0:T(8,128)(2,1)S(1)} %collective-permute-done.21.far_ref, ...), custom_call_target="tpu_custom_call" | custom-call | flops 402653184 | bytes 2097152 | tf_op jit(solution)/shard_map/pallas_call | solution.py:42
  98.9 2.7 %shard_map.137 = bf16[512,256]{1,0:T(8,128)(2,1)} custom-call(f32[2,2]{1,0:T(2,128)S(1)} %reshape.19.edge_ref, bf16[512,256]{1,0:T(8,128)(2,1)S(1)} %copy-done.4, bf16[512,256]{1,0:T(8,128)(2,1)S(1)} %copy-done.5, bf16[512,256]{1,0:T(8,128)(2,1)S(1)} %collective-permute-done.18.near_ref, bf16[256,256]{1,0:T(8,128)(2,1)S(1)} %collective-permute-done.20.far_ref, ...), custom_call_target="tpu_custom_call" | custom-call | flops 402653184 | bytes 2097152 | tf_op jit(solution)/shard_map/pallas_call | solution.py:42
  (50 shorter events, 0.5 us)
Async XLA Ops:
  0.6 8.9 %copy-start.3 = (bf16[512,256]{1,0:T(8,128)(2,1)S(1)}, bf16[512,256]{1,0:T(8,128)(2,1)}, u32[]{:S(2)}) copy-start(bf16[512,256]{1,0:T(8,128)(2,1)} %values_ref.5) | copy-start | bytes 786436
  0.6 8.9 %copy-start.2 = (bf16[512,256]{1,0:T(8,128)(2,1)S(1)}, bf16[512,256]{1,0:T(8,128)(2,1)}, u32[]{:S(2)}) copy-start(bf16[512,256]{1,0:T(8,128)(2,1)} %keys_ref.5) | copy-start | bytes 786436
  0.7 8.9 %copy-start.6 = (bf16[512,256]{1,0:T(8,128)(2,1)S(1)}, bf16[512,256]{1,0:T(8,128)(2,1)}, u32[]{:S(2)}) copy-start(bf16[512,256]{1,0:T(8,128)(2,1)} %queries_ref.5) | copy-start | bytes 786436
  0.7 11.1 %copy-start = (bf16[512,256]{1,0:T(8,128)(2,1)S(1)}, bf16[512,256]{1,0:T(8,128)(2,1)}, u32[]{:S(2)}) copy-start(bf16[512,256]{1,0:T(8,128)(2,1)} %keys_ref.7) | copy-start | bytes 786436
  0.7 11.9 %copy-start.1 = (bf16[512,256]{1,0:T(8,128)(2,1)S(1)}, bf16[512,256]{1,0:T(8,128)(2,1)}, u32[]{:S(2)}) copy-start(bf16[512,256]{1,0:T(8,128)(2,1)} %values_ref.7) | copy-start | bytes 786436
  6.5 13.2 %copy-start.11 = (bf16[256,768]{1,0:T(8,128)(2,1)S(1)}, bf16[256,768]{1,0:T(8,128)(2,1)}, u32[]{:S(2)}) copy-start(bf16[256,768]{1,0:T(8,128)(2,1)} %get-tuple-element.24) | copy-start | bytes 1179652
  6.5 13.2 %collective-permute-start = (bf16[256,768]{1,0:T(8,128)(2,1)}, bf16[256,768]{1,0:T(8,128)(2,1)S(1)}, u32[]{:S(2)}, u32[]{:S(2)}) collective-permute-start(bf16[256,768]{1,0:T(8,128)(2,1)} %get-tuple-element.25), channel_id=1, source_target_pairs={{0,4},{4,0},{8,12},{12,8},{16,20},{20,16},{24,28},{28,24},{1,5},{5... | collective-permute-start | bytes 1179656 | tf_op jit(solution)/shard_map/ppermute | solution.py:345
  9.6 12.4 %copy-start.10 = (bf16[256,768]{1,0:T(8,128)(2,1)S(1)}, bf16[256,768]{1,0:T(8,128)(2,1)}, u32[]{:S(2)}) copy-start(bf16[256,768]{1,0:T(8,128)(2,1)} %get-tuple-element.26) | copy-start | bytes 1179652
  9.7 17.7 %collective-permute-start.8 = (bf16[1536,128]{1,0:T(8,128)(2,1)S(1)}, bf16[1536,128]{1,0:T(8,128)(2,1)S(1)}, u32[]{:S(2)}, u32[]{:S(2)}) collective-permute-start(bf16[1536,128]{1,0:T(8,128)(2,1)S(1)} %shard_map.132), channel_id=1, source_target_pairs={{0,4},{4,0},{8,12},{12,8},{16,20},{20,16},{24,28},{28,24},{1,5},{5... | collective-permute-start | bytes 1179656 | tf_op jit(solution)/shard_map/ppermute | solution.py:345
  9.8 12.2 %collective-permute-start.4 = (bf16[256,768]{1,0:T(8,128)(2,1)}, bf16[256,768]{1,0:T(8,128)(2,1)S(1)}, u32[]{:S(2)}, u32[]{:S(2)}) collective-permute-start(bf16[256,768]{1,0:T(8,128)(2,1)} %get-tuple-element.27), channel_id=1, source_target_pairs={{0,8},{4,12},{8,0},{12,4},{16,24},{20,28},{24,16},{28,20},{1,9},{5... | collective-permute-start | bytes 1179656 | tf_op jit(solution)/shard_map/ppermute | solution.py:345
  19.8 8.3 %collective-permute-start.1 = (bf16[128,768]{1,0:T(8,128)(2,1)S(1)}, bf16[128,768]{1,0:T(8,128)(2,1)S(1)}, u32[]{:S(2)}, u32[]{:S(2)}) collective-permute-start(bf16[128,768]{1,0:T(8,128)(2,1)S(1)} %get-tuple-element.50), channel_id=1, source_target_pairs={{0,8},{4,12},{8,0},{12,4},{16,24},{20,28},{24,16},{28,20},{1,9},{5... | collective-permute-start | bytes 589832 | tf_op jit(solution)/shard_map/ppermute | solution.py:345
  22.1 10.7 %collective-permute-start.5 = (bf16[128,768]{1,0:T(8,128)(2,1)S(1)}, bf16[128,768]{1,0:T(8,128)(2,1)S(1)}, u32[]{:S(2)}, u32[]{:S(2)}) collective-permute-start(bf16[128,768]{1,0:T(8,128)(2,1)S(1)} %get-tuple-element.48), channel_id=1, source_target_pairs={{0,16},{4,20},{8,24},{12,28},{16,0},{20,4},{24,8},{28,12},{1,17},{... | collective-permute-start | bytes 589832 | tf_op jit(solution)/shard_map/ppermute | solution.py:345
  28.2 14.1 %collective-permute-start.2 = (bf16[64,768]{1,0:T(8,128)(2,1)S(1)}, bf16[64,768]{1,0:T(8,128)(2,1)S(1)}, u32[]{:S(2)}, u32[]{:S(2)}) collective-permute-start(bf16[64,768]{1,0:T(8,128)(2,1)S(1)} %get-tuple-element.54), channel_id=1, source_target_pairs={{0,16},{4,20},{8,24},{12,28},{16,0},{20,4},{24,8},{28,12},{1,17},{... | collective-permute-start | bytes 294920 | tf_op jit(solution)/shard_map/ppermute | solution.py:345
  32.8 13.6 %collective-permute-start.6 = (bf16[64,768]{1,0:T(8,128)(2,1)S(1)}, bf16[64,768]{1,0:T(8,128)(2,1)S(1)}, u32[]{:S(2)}, u32[]{:S(2)}) collective-permute-start(bf16[64,768]{1,0:T(8,128)(2,1)S(1)} %get-tuple-element.52), channel_id=1, source_target_pairs={{0,4},{4,0},{8,12},{12,8},{16,20},{20,16},{24,28},{28,24},{1,5},{5... | collective-permute-start | bytes 294920 | tf_op jit(solution)/shard_map/ppermute | solution.py:345
  34.4 17.6 %collective-permute-start.9 = (bf16[1024,128]{1,0:T(8,128)(2,1)S(1)}, bf16[1024,128]{1,0:T(8,128)(2,1)S(1)}, u32[]{:S(2)}, u32[]{:S(2)}) collective-permute-start(bf16[1024,128]{1,0:T(8,128)(2,1)S(1)} %get-tuple-element.30.high_ref), channel_id=1, source_target_pairs={{0,8},{4,12},{8,16},{12,20},{16,24},{20,28},{1,9},{5,13},{9,17},{1... | collective-permute-start | bytes 786440 | tf_op jit(solution)/shard_map/ppermute | solution.py:334
  38.5 13.5 %collective-permute-start.10 = (bf16[1024,128]{1,0:T(8,128)(2,1)S(1)}, bf16[1024,128]{1,0:T(8,128)(2,1)S(1)}, u32[]{:S(2)}, u32[]{:S(2)}) collective-permute-start(bf16[1024,128]{1,0:T(8,128)(2,1)S(1)} %get-tuple-element.31.low_ref), channel_id=1, source_target_pairs={{8,0},{12,4},{16,8},{20,12},{24,16},{28,20},{9,1},{13,5},{17,9},{2... | collective-permute-start | bytes 786440 | tf_op jit(solution)/shard_map/ppermute | solution.py:334
  39.8 12.2 %collective-permute-start.11 = (bf16[1024,256]{1,0:T(8,128)(2,1)}, bf16[1024,256]{1,0:T(8,128)(2,1)S(1)}, u32[]{:S(2)}, u32[]{:S(2)}) collective-permute-start(bf16[1024,256]{1,0:T(8,128)(2,1)} %constant_dynamic-update-slice_fusion), channel_id=1, source_target_pairs={{0,4},{4,8},{8,12},{12,16},{16,20},{20,24},{24,28},{1,5},{5,9},{9,... | collective-permute-start | bytes 1572872 | tf_op jit(solution)/shard_map/ppermute | solution.py:334
  42.3 7.1 %collective-permute-start.3 = (bf16[64,768]{1,0:T(8,128)(2,1)S(1)}, bf16[64,768]{1,0:T(8,128)(2,1)S(1)}, u32[]{:S(2)}, u32[]{:S(2)}) collective-permute-start(bf16[64,768]{1,0:T(8,128)(2,1)S(1)} %add_convert_fusion.3), channel_id=1, source_target_pairs={{0,16},{4,20},{8,24},{12,28},{16,0},{20,4},{24,8},{28,12},{1,17},{... | collective-permute-start | bytes 294920 | tf_op jit(solution)/shard_map/ppermute | solution.py:345
  46.4 5.7 %collective-permute-start.7 = (bf16[64,768]{1,0:T(8,128)(2,1)S(1)}, bf16[64,768]{1,0:T(8,128)(2,1)S(1)}, u32[]{:S(2)}, u32[]{:S(2)}) collective-permute-start(bf16[64,768]{1,0:T(8,128)(2,1)S(1)} %add_convert_fusion.2), channel_id=1, source_target_pairs={{0,4},{4,0},{8,12},{12,8},{16,20},{20,16},{24,28},{28,24},{1,5},{5... | collective-permute-start | bytes 294920 | tf_op jit(solution)/shard_map/ppermute | solution.py:345
  52.1 16.1 %collective-permute-start.12 = (bf16[128,768]{1,0:T(8,128)(2,1)S(1)}, bf16[128,768]{1,0:T(8,128)(2,1)S(1)}, u32[]{:S(2)}, u32[]{:S(2)}) collective-permute-start(bf16[128,768]{1,0:T(8,128)(2,1)S(1)} %pad_maximum_fusion.2), channel_id=1, source_target_pairs={{0,8},{4,12},{8,0},{12,4},{16,24},{20,28},{24,16},{28,20},{1,9},{5... | collective-permute-start | bytes 589832 | tf_op jit(solution)/shard_map/ppermute | solution.py:345
  59.8 9.6 %collective-permute-start.13 = (bf16[128,768]{1,0:T(8,128)(2,1)S(1)}, bf16[128,768]{1,0:T(8,128)(2,1)S(1)}, u32[]{:S(2)}, u32[]{:S(2)}) collective-permute-start(bf16[128,768]{1,0:T(8,128)(2,1)S(1)} %pad_maximum_fusion.3), channel_id=1, source_target_pairs={{0,16},{4,20},{8,24},{12,28},{16,0},{20,4},{24,8},{28,12},{1,17},{... | collective-permute-start | bytes 589832 | tf_op jit(solution)/shard_map/ppermute | solution.py:345
  68.1 7.0 %copy-start.7 = (bf16[512,128]{1,0:T(8,128)(2,1)}, bf16[512,128]{1,0:T(8,128)(2,1)S(1)}, u32[]{:S(2)}) copy-start(bf16[512,128]{1,0:T(8,128)(2,1)S(1)} %get-tuple-element.35.refs_5_) | copy-start | bytes 393220
  68.1 8.2 %collective-permute-start.16 = (bf16[512,128]{1,0:T(8,128)(2,1)S(1)}, bf16[512,128]{1,0:T(8,128)(2,1)S(1)}, u32[]{:S(2)}, u32[]{:S(2)}) collective-permute-start(bf16[512,128]{1,0:T(8,128)(2,1)S(1)} %get-tuple-element.38), channel_id=1, source_target_pairs={{0,4},{4,0},{8,12},{12,8},{16,20},{20,16},{24,28},{28,24},{1,5},{5... | collective-permute-start | bytes 393224 | tf_op jit(solution)/shard_map/ppermute | solution.py:345
  68.3 12.7 %copy-start.8 = (bf16[256,768]{1,0:T(8,128)(2,1)}, bf16[256,768]{1,0:T(8,128)(2,1)S(1)}, u32[]{:S(2)}) copy-start(bf16[256,768]{1,0:T(8,128)(2,1)S(1)} %pad_maximum_fusion.refs_0_) | copy-start | bytes 1179652
  69.5 11.5 %copy-start.9 = (bf16[256,768]{1,0:T(8,128)(2,1)}, bf16[256,768]{1,0:T(8,128)(2,1)S(1)}, u32[]{:S(2)}) copy-start(bf16[256,768]{1,0:T(8,128)(2,1)S(1)} %pad_maximum_fusion.1.refs_2_) | copy-start | bytes 1179652
  69.5 11.0 %collective-permute-start.14 = (bf16[256,768]{1,0:T(8,128)(2,1)S(1)}, bf16[256,768]{1,0:T(8,128)(2,1)S(1)}, u32[]{:S(2)}, u32[]{:S(2)}) collective-permute-start(bf16[256,768]{1,0:T(8,128)(2,1)S(1)} %pad_maximum_fusion.refs_0_), channel_id=1, source_target_pairs={{0,4},{4,0},{8,12},{12,8},{16,20},{20,16},{24,28},{28,24},{1,5},{5... | collective-permute-start | bytes 1179656 | tf_op jit(solution)/shard_map/ppermute | solution.py:345
  70.4 10.5 %collective-permute-start.15 = (bf16[256,768]{1,0:T(8,128)(2,1)S(1)}, bf16[256,768]{1,0:T(8,128)(2,1)S(1)}, u32[]{:S(2)}, u32[]{:S(2)}) collective-permute-start(bf16[256,768]{1,0:T(8,128)(2,1)S(1)} %pad_maximum_fusion.1.refs_2_), channel_id=1, source_target_pairs={{0,8},{4,12},{8,0},{12,4},{16,24},{20,28},{24,16},{28,20},{1,9},{5... | collective-permute-start | bytes 1179656 | tf_op jit(solution)/shard_map/ppermute | solution.py:345
  76.3 4.6 %copy-start.14 = (bf16[512,128]{1,0:T(8,128)(2,1)}, bf16[512,128]{1,0:T(8,128)(2,1)S(1)}, u32[]{:S(2)}) copy-start(bf16[512,128]{1,0:T(8,128)(2,1)S(1)} %collective-permute-done.16.refs_6_) | copy-start | bytes 393220
  76.3 12.4 %collective-permute-start.17 = (bf16[1024,256]{1,0:T(8,128)(2,1)}, bf16[1024,256]{1,0:T(8,128)(2,1)S(1)}, u32[]{:S(2)}, u32[]{:S(2)}) collective-permute-start(bf16[1024,256]{1,0:T(8,128)(2,1)} %constant_dynamic-update-slice_fusion), channel_id=1, source_target_pairs={{4,0},{8,4},{12,8},{16,12},{20,16},{24,20},{28,24},{5,1},{9,5},{13... | collective-permute-start | bytes 1572872 | tf_op jit(solution)/shard_map/ppermute | solution.py:334
  80.5 0.8 copy-start.12
  80.9 0.7 copy-start.13
  88.6 8.3 %copy-start.4 = (bf16[512,256]{1,0:T(8,128)(2,1)S(1)}, bf16[512,256]{1,0:T(8,128)(2,1)}, u32[]{:S(2)}) copy-start(bf16[512,256]{1,0:T(8,128)(2,1)} %queries_ref.7) | copy-start | bytes 786436
  88.6 8.3 %copy-start.5 = (bf16[512,256]{1,0:T(8,128)(2,1)S(1)}, bf16[512,256]{1,0:T(8,128)(2,1)}, u32[]{:S(2)}) copy-start(bf16[512,256]{1,0:T(8,128)(2,1)} %get-tuple-element.39.keep_ref) | copy-start | bytes 786436
  88.6 1.8 %collective-permute-start.19 = (bf16[512,256]{1,0:T(8,128)(2,1)}, bf16[512,256]{1,0:T(8,128)(2,1)S(1)}, u32[]{:S(2)}, u32[]{:S(2)}) collective-permute-start(bf16[512,256]{1,0:T(8,128)(2,1)} %get-tuple-element.44), channel_id=1, source_target_pairs={{0,1},{1,0},{2,3},{3,2},{4,5},{5,4},{6,7},{7,6},{8,9},{9,8},{10,11... | collective-permute-start | bytes 786440 | tf_op jit(solution)/shard_map/ppermute | solution.py:340
  88.7 3.9 %collective-permute-start.18 = (bf16[512,256]{1,0:T(8,128)(2,1)}, bf16[512,256]{1,0:T(8,128)(2,1)S(1)}, u32[]{:S(2)}, u32[]{:S(2)}) collective-permute-start(bf16[512,256]{1,0:T(8,128)(2,1)} %get-tuple-element.42), channel_id=1, source_target_pairs={{0,1},{1,0},{2,3},{3,2},{4,5},{5,4},{6,7},{7,6},{8,9},{9,8},{10,11... | collective-permute-start | bytes 786440 | tf_op jit(solution)/shard_map/ppermute | solution.py:340
  90.5 6.4 %collective-permute-start.21 = (bf16[256,256]{1,0:T(8,128)(2,1)S(1)}, bf16[256,256]{1,0:T(8,128)(2,1)S(1)}, u32[]{:S(2)}, u32[]{:S(2)}) collective-permute-start(bf16[256,256]{1,0:T(8,128)(2,1)S(1)} %get-tuple-element.46), channel_id=1, source_target_pairs={{0,2},{1,3},{2,0},{3,1},{4,6},{5,7},{6,4},{7,5},{8,10},{9,11},{10,... | collective-permute-start | bytes 393224 | tf_op jit(solution)/shard_map/ppermute | solution.py:340
  92.1 6.8 %collective-permute-start.20 = (bf16[256,256]{1,0:T(8,128)(2,1)S(1)}, bf16[256,256]{1,0:T(8,128)(2,1)S(1)}, u32[]{:S(2)}, u32[]{:S(2)}) collective-permute-start(bf16[256,256]{1,0:T(8,128)(2,1)S(1)} %get-tuple-element.47), channel_id=1, source_target_pairs={{0,2},{1,3},{2,0},{3,1},{4,6},{5,7},{6,4},{7,5},{8,10},{9,11},{10,... | collective-permute-start | bytes 393224 | tf_op jit(solution)/shard_map/ppermute | solution.py:340

commit v23 on v21

--- a/solution.py
+++ b/solution.py
@@ -469,7 +469,6 @@
             pltpu.VMEM(weights.shape, BF16),
             pltpu.SemaphoreType.DMA((len(operands),)),
         ],
-        limit=VMEM_MOST - 3 * 1024 * 1024,
     )
     far_near = head_swap(far_send, 1)
     far_keep = lax.optimization_barrier(far_keep.astype(F32))

time: 101 us -> 106 us (1.050)
  starting transfers between devices: 51.2 us -> 42.7 us
  local copies, waits for them, and re-layouts: 2.33 us -> 10.5 us
  waiting for transfers between devices: 24.3 us -> 28.1 us
  other arithmetic: 2.09 us -> 4.78 us
  Pallas kernels: 20 us -> 18.9 us
    unnamed x31 -> x45, local copies, waits for them, and re-layouts: 1.51 us -> 9.66 us
    ppermute x14, starting transfers between devices: 39.3 us -> 31.8 us  [seq_swap(): lax.ppermute(value, 'seq', [(i, i ^ step) for i in range(lax.axis_size('s...]
    concatenate x4, other arithmetic: 0.08 us -> 3.2 us  [doubling_step(): jnp.concatenate(parts)]
    ppermute x14, waiting for transfers between devices: 19.8 us -> 22.8 us  [seq_swap(): lax.ppermute(value, 'seq', [(i, i ^ step) for i in range(lax.axis_size('s...]
    pallas_call x6, Pallas kernels: 14.8 us -> 13.7 us  [call(): pl.pallas_call(body, out_shape=out_shapes, in_specs=in_specs, out_specs=j...]
  transfers between devices with their start and end apart: 22 -> 22, of which waited for: 11 -> 9; matrix products, arithmetic and copies ran while one was open for 4% -> 6% of each run, Pallas kernels for 12% -> 10%
where the time goes in v23:
time: 106 us
  starting transfers between devices  42.7 us (40%)
  waiting for transfers between devices  28.1 us (27%)
  Pallas kernels  18.9 us (18%)
  local copies, waits for them, and re-layouts  10.5 us (10%)
  other arithmetic  4.78 us (5%)
    ppermute x14, starting transfers between devices, seq_swap(): lax.ppermute(value, 'seq', [(i, i ^ step) for i in range(lax.axis_size('s...  31.8 us
    ppermute x14, waiting for transfers between devices, seq_swap(): lax.ppermute(value, 'seq', [(i, i ^ step) for i in range(lax.axis_size('s...  22.8 us
    pallas_call x6, Pallas kernels, call(): pl.pallas_call(body, out_shape=out_shapes, in_specs=in_specs, out_specs=j...  13.7 us
    unnamed x45, local copies, waits for them, and re-layouts  9.66 us
    ppermute x4, starting transfers between devices, seq_shift(): lax.ppermute(value, 'seq', [(i, i + step) for i in range(peers) if 0 <= i...  8.29 us
    ppermute x4, waiting for transfers between devices, head_swap(): lax.ppermute(value, 'head', [(i, i ^ bit) for i in range(lax.axis_size('h...  5.3 us
    pallas_call x1, Pallas kernels, local(): pl.pallas_call(functools.partial(gradient_kernel, orders), grid=(1,), out...  5.17 us
    concatenate x4, other arithmetic, doubling_step(): jnp.concatenate(parts)  3.2 us
  transfers between devices with their start and end apart: 22, of which 9 were waited for; matrix products, arithmetic and copies ran while one was open for 6% of the time, Pallas kernels for 10%

profile of v23, /device:TPU:0, one launch (start us, length us, event | category | flops | bytes accessed | tf_op | source)
XLA Modules:
  0.0 105.9 jit_solution(6046042191032914064)
XLA Ops:
  0.7 5.2 %shard_map.131 = (bf16[256,768]{1,0:T(8,128)(2,1)}, bf16[256,768]{1,0:T(8,128)(2,1)}, bf16[256,768]{1,0:T(8,128)(2,1)}, bf16[256,768]{1,0:T(8,128)(2,1)}) custom-call(s32[1,1]{1,0:T(1,128)} %bitcast.4.place_ref, f32[1,512]{1,0:T(1,128)} %bitcast.23, bf16[512,512]{1,0:T(8,128)(2,1)} %keys_ref.5, bf16[512,512]{1,0:T(8,128)(2,1)} %values_ref.5, ...), custom_call_target="tpu_custom_call" | custom-call | flops 1000 | bytes 1000 | tf_op jit(solution)/shard_map/pallas_call | solution.py:390
  5.9 3.0 %collective-permute-start = (bf16[256,768]{1,0:T(8,128)(2,1)}, bf16[256,768]{1,0:T(8,128)(2,1)}, u32[]{:S(2)}, u32[]{:S(2)}) collective-permute-start(bf16[256,768]{1,0:T(8,128)(2,1)} %get-tuple-element.25), channel_id=1, source_target_pairs={{0,4},{4,0},{8,12},{12,8},{16,20},{20,16},{24,28},{28,24},{1,5},{5... | collective-permute-start | bytes 1179656 | tf_op jit(solution)/shard_map/ppermute | solution.py:316
  9.0 2.1 %collective-permute-start.4 = (bf16[256,768]{1,0:T(8,128)(2,1)}, bf16[256,768]{1,0:T(8,128)(2,1)S(1)}, u32[]{:S(2)}, u32[]{:S(2)}) collective-permute-start(bf16[256,768]{1,0:T(8,128)(2,1)} %get-tuple-element.27), channel_id=1, source_target_pairs={{0,8},{4,12},{8,0},{12,4},{16,24},{20,28},{24,16},{28,20},{1,9},{5... | collective-permute-start | bytes 1179656 | tf_op jit(solution)/shard_map/ppermute | solution.py:316
  11.1 0.7 constant_dynamic-update-slice_fusion.1
  11.8 0.7 constant_dynamic-update-slice_fusion
  12.5 6.6 %collective-permute-done = bf16[256,768]{1,0:T(8,128)(2,1)} collective-permute-done((bf16[256,768]{1,0:T(8,128)(2,1)}, bf16[256,768]{1,0:T(8,128)(2,1)}, u32[]{:S(2)}, u32[]{:S(2)}) %collective-permute-start) | collective-permute-done | bytes 393248 | tf_op jit(solution)/shard_map/ppermute | solution.py:316
  19.1 1.1 %add_convert_fusion.1 = (bf16[128,768]{1,0:T(8,128)(2,1)S(1)}, f32[128,768]{1,0:T(8,128)S(1)}) fusion(bf16[256,768]{1,0:T(8,128)(2,1)} %collective-permute-done, bf16[256,768]{1,0:T(8,128)(2,1)S(1)} %copy-done.21), kind=kLoop, calls=%fused_computation.4 | loop fusion | flops 688128 | bytes 1376256 | tf_op jit(solution)/shard_map/convert_element_type | solution.py:332
  20.2 2.2 %collective-permute-start.1 = (bf16[128,768]{1,0:T(8,128)(2,1)S(1)}, bf16[128,768]{1,0:T(8,128)(2,1)S(1)}, u32[]{:S(2)}, u32[]{:S(2)}) collective-permute-start(bf16[128,768]{1,0:T(8,128)(2,1)S(1)} %get-tuple-element.50), channel_id=1, source_target_pairs={{0,8},{4,12},{8,0},{12,4},{16,24},{20,28},{24,16},{28,20},{1,9},{5... | collective-permute-start | bytes 589832 | tf_op jit(solution)/shard_map/ppermute | solution.py:316
  22.5 2.7 %collective-permute-start.5 = (bf16[128,768]{1,0:T(8,128)(2,1)S(1)}, bf16[128,768]{1,0:T(8,128)(2,1)S(1)}, u32[]{:S(2)}, u32[]{:S(2)}) collective-permute-start(bf16[128,768]{1,0:T(8,128)(2,1)S(1)} %get-tuple-element.48), channel_id=1, source_target_pairs={{0,16},{4,20},{8,24},{12,28},{16,0},{20,4},{24,8},{28,12},{1,17},{... | collective-permute-start | bytes 589832 | tf_op jit(solution)/shard_map/ppermute | solution.py:316
  25.2 1.4 %collective-permute-done.8.other_ref = bf16[1536,128]{1,0:T(8,128)(2,1)S(1)} collective-permute-done((bf16[1536,128]{1,0:T(8,128)(2,1)S(1)}, bf16[1536,128]{1,0:T(8,128)(2,1)S(1)}, u32[]{:S(2)}, u32[]{:S(2)}) %collective-permute-start.8) | collective-permute-done | bytes 393248 | tf_op jit(solution)/shard_map/ppermute | solution.py:316
  26.7 1.9 %collective-permute-done.1 = bf16[128,768]{1,0:T(8,128)(2,1)S(1)} collective-permute-done((bf16[128,768]{1,0:T(8,128)(2,1)S(1)}, bf16[128,768]{1,0:T(8,128)(2,1)S(1)}, u32[]{:S(2)}, u32[]{:S(2)}) %collective-permute-start.1) | collective-permute-done | bytes 196640 | tf_op jit(solution)/shard_map/ppermute | solution.py:316
  28.6 1.8 %collective-permute-start.2 = (bf16[64,768]{1,0:T(8,128)(2,1)S(1)}, bf16[64,768]{1,0:T(8,128)(2,1)S(1)}, u32[]{:S(2)}, u32[]{:S(2)}) collective-permute-start(bf16[64,768]{1,0:T(8,128)(2,1)S(1)} %get-tuple-element.54), channel_id=1, source_target_pairs={{0,16},{4,20},{8,24},{12,28},{16,0},{20,4},{24,8},{28,12},{1,17},{... | collective-permute-start | bytes 294920 | tf_op jit(solution)/shard_map/ppermute | solution.py:316
  30.4 3.0 %collective-permute-done.5 = bf16[128,768]{1,0:T(8,128)(2,1)S(1)} collective-permute-done((bf16[128,768]{1,0:T(8,128)(2,1)S(1)}, bf16[128,768]{1,0:T(8,128)(2,1)S(1)}, u32[]{:S(2)}, u32[]{:S(2)}) %collective-permute-start.5) | collective-permute-done | bytes 196640 | tf_op jit(solution)/shard_map/ppermute | solution.py:316
  33.4 1.7 %collective-permute-start.6 = (bf16[64,768]{1,0:T(8,128)(2,1)S(1)}, bf16[64,768]{1,0:T(8,128)(2,1)S(1)}, u32[]{:S(2)}, u32[]{:S(2)}) collective-permute-start(bf16[64,768]{1,0:T(8,128)(2,1)S(1)} %get-tuple-element.52), channel_id=1, source_target_pairs={{0,4},{4,0},{8,12},{12,8},{16,20},{20,16},{24,28},{28,24},{1,5},{5... | collective-permute-start | bytes 294920 | tf_op jit(solution)/shard_map/ppermute | solution.py:316
  35.1 3.1 %collective-permute-start.9 = (bf16[1024,128]{1,0:T(8,128)(2,1)S(1)}, bf16[1024,128]{1,0:T(8,128)(2,1)S(1)}, u32[]{:S(2)}, u32[]{:S(2)}) collective-permute-start(bf16[1024,128]{1,0:T(8,128)(2,1)S(1)} %get-tuple-element.30.high_ref), channel_id=1, source_target_pairs={{0,8},{4,12},{8,16},{12,20},{16,24},{20,28},{1,9},{5,13},{9,17},{1... | collective-permute-start | bytes 786440 | tf_op jit(solution)/shard_map/ppermute | solution.py:305
  38.2 1.3 %collective-permute-start.10 = (bf16[1024,128]{1,0:T(8,128)(2,1)S(1)}, bf16[1024,128]{1,0:T(8,128)(2,1)S(1)}, u32[]{:S(2)}, u32[]{:S(2)}) collective-permute-start(bf16[1024,128]{1,0:T(8,128)(2,1)S(1)} %get-tuple-element.31.low_ref), channel_id=1, source_target_pairs={{8,0},{12,4},{16,8},{20,12},{24,16},{28,20},{9,1},{13,5},{17,9},{2... | collective-permute-start | bytes 786440 | tf_op jit(solution)/shard_map/ppermute | solution.py:305
  39.5 2.4 %collective-permute-start.11 = (bf16[1024,256]{1,0:T(8,128)(2,1)}, bf16[1024,256]{1,0:T(8,128)(2,1)S(1)}, u32[]{:S(2)}, u32[]{:S(2)}) collective-permute-start(bf16[1024,256]{1,0:T(8,128)(2,1)} %constant_dynamic-update-slice_fusion), channel_id=1, source_target_pairs={{0,4},{4,8},{8,12},{12,16},{16,20},{20,24},{24,28},{1,5},{5,9},{9,... | collective-permute-start | bytes 1572872 | tf_op jit(solution)/shard_map/ppermute | solution.py:305
  41.9 4.3 %collective-permute-start.3 = (bf16[64,768]{1,0:T(8,128)(2,1)S(1)}, bf16[64,768]{1,0:T(8,128)(2,1)S(1)}, u32[]{:S(2)}, u32[]{:S(2)}) collective-permute-start(bf16[64,768]{1,0:T(8,128)(2,1)S(1)} %add_convert_fusion.3), channel_id=1, source_target_pairs={{0,16},{4,20},{8,24},{12,28},{16,0},{20,4},{24,8},{28,12},{1,17},{... | collective-permute-start | bytes 294920 | tf_op jit(solution)/shard_map/ppermute | solution.py:316
  46.3 3.1 %collective-permute-start.7 = (bf16[64,768]{1,0:T(8,128)(2,1)S(1)}, bf16[64,768]{1,0:T(8,128)(2,1)S(1)}, u32[]{:S(2)}, u32[]{:S(2)}) collective-permute-start(bf16[64,768]{1,0:T(8,128)(2,1)S(1)} %add_convert_fusion.2), channel_id=1, source_target_pairs={{0,4},{4,0},{8,12},{12,8},{16,20},{20,16},{24,28},{28,24},{1,5},{5... | collective-permute-start | bytes 294920 | tf_op jit(solution)/shard_map/ppermute | solution.py:316
  49.3 0.7 pad_maximum_fusion.2
  50.0 1.9 %collective-permute-done.7 = bf16[64,768]{1,0:T(8,128)(2,1)S(1)} collective-permute-done((bf16[64,768]{1,0:T(8,128)(2,1)S(1)}, bf16[64,768]{1,0:T(8,128)(2,1)S(1)}, u32[]{:S(2)}, u32[]{:S(2)}) %collective-permute-start.7) | collective-permute-done | bytes 98336 | tf_op jit(solution)/shard_map/ppermute | solution.py:316
  51.9 0.7 pad_maximum_fusion.3
  52.6 0.7 copy-done.15
  53.3 0.7 copy-done.17
  54.0 5.1 %collective-permute-start.12 = (bf16[128,768]{1,0:T(8,128)(2,1)}, bf16[128,768]{1,0:T(8,128)(2,1)}, u32[]{:S(2)}, u32[]{:S(2)}) collective-permute-start(bf16[128,768]{1,0:T(8,128)(2,1)} %pad_maximum_fusion.2), channel_id=1, source_target_pairs={{0,8},{4,12},{8,0},{12,4},{16,24},{20,28},{24,16},{28,20},{1,9},{5... | collective-permute-start | bytes 589832 | tf_op jit(solution)/shard_map/ppermute | solution.py:316
  59.3 2.0 %collective-permute-start.13 = (bf16[128,768]{1,0:T(8,128)(2,1)}, bf16[128,768]{1,0:T(8,128)(2,1)S(1)}, u32[]{:S(2)}, u32[]{:S(2)}) collective-permute-start(bf16[128,768]{1,0:T(8,128)(2,1)} %pad_maximum_fusion.3), channel_id=1, source_target_pairs={{0,16},{4,20},{8,24},{12,28},{16,0},{20,4},{24,8},{28,12},{1,17},{... | collective-permute-start | bytes 589832 | tf_op jit(solution)/shard_map/ppermute | solution.py:316
  61.3 0.9 copy-done.14
  62.2 0.9 copy-done.16
  63.2 0.9 copy-done.18
  64.1 3.1 %shard_map.134 = (bf16[512,128]{1,0:T(8,128)(2,1)S(1)}, bf16[512,128]{1,0:T(8,128)(2,1)S(1)}) custom-call(f32[2,2]{1,0:T(2,128)S(1)} %reshape.19.edge_ref, s32[1,1]{1,0:T(1,128)} %bitcast.5.side_ref, bf16[512,256]{1,0:T(8,128)(2,1)S(1)} %copy-done.8, bf16[1536,128]{1,0:T(8,128)(2,1)S(1)} %collective-permute-done.8.other_ref, ...), custom_call_target="tpu_custom_call" | custom-call | flops 805306368 | bytes 2097152 | tf_op jit(solution)/shard_map/pallas_call | solution.py:42
  67.2 3.7 %collective-permute-start.16 = (bf16[512,128]{1,0:T(8,128)(2,1)S(1)}, bf16[512,128]{1,0:T(8,128)(2,1)S(1)}, u32[]{:S(2)}, u32[]{:S(2)}) collective-permute-start(bf16[512,128]{1,0:T(8,128)(2,1)S(1)} %get-tuple-element.38), channel_id=1, source_target_pairs={{0,4},{4,0},{8,12},{12,8},{16,20},{20,16},{24,28},{28,24},{1,5},{5... | collective-permute-start | bytes 393224 | tf_op jit(solution)/shard_map/ppermute | solution.py:316
  70.9 1.0 pad_maximum_fusion.refs_0_
  72.0 0.8 pad_maximum_fusion.1.refs_2_
  72.9 5.3 %collective-permute-done.16.refs_6_ = bf16[512,128]{1,0:T(8,128)(2,1)S(1)} collective-permute-done((bf16[512,128]{1,0:T(8,128)(2,1)S(1)}, bf16[512,128]{1,0:T(8,128)(2,1)S(1)}, u32[]{:S(2)}, u32[]{:S(2)}) %collective-permute-start.16) | collective-permute-done | bytes 131104 | tf_op jit(solution)/shard_map/ppermute | solution.py:316
  78.2 0.7 copy-done.11
  78.9 1.5 %collective-permute-start.17 = (bf16[1024,256]{1,0:T(8,128)(2,1)}, bf16[1024,256]{1,0:T(8,128)(2,1)S(1)}, u32[]{:S(2)}, u32[]{:S(2)}) collective-permute-start(bf16[1024,256]{1,0:T(8,128)(2,1)} %constant_dynamic-update-slice_fusion), channel_id=1, source_target_pairs={{4,0},{8,4},{12,8},{16,12},{20,16},{24,20},{28,24},{5,1},{9,5},{13... | collective-permute-start | bytes 1572872 | tf_op jit(solution)/shard_map/ppermute | solution.py:305
  80.4 2.8 %collective-permute-done.14.refs_1_ = bf16[256,768]{1,0:T(8,128)(2,1)} collective-permute-done((bf16[256,768]{1,0:T(8,128)(2,1)S(1)}, bf16[256,768]{1,0:T(8,128)(2,1)}, u32[]{:S(2)}, u32[]{:S(2)}) %collective-permute-start.14) | collective-permute-done | bytes 393248 | tf_op jit(solution)/shard_map/ppermute | solution.py:316
  83.2 1.2 %copy-done.5 = bf16[512,1024]{1,0:T(8,128)(2,1)S(1)} copy-done((bf16[512,1024]{1,0:T(8,128)(2,1)S(1)}, bf16[512,1024]{1,0:T(8,128)(2,1)}, u32[]{:S(2)}) %copy-start.5) | copy-done | bytes 1048600
  84.4 0.9 copy-done.7
  85.4 0.9 copy-done.10
  86.3 0.9 copy-done.12
  87.2 5.8 %shard_map.135 = (bf16[3,64,512]{2,1,0:T(8,128)(2,1)}, bf16[512,256]{1,0:T(8,128)(2,1)S(1)}, bf16[512,256]{1,0:T(8,128)(2,1)S(1)}, bf16[512,256]{1,0:T(8,128)(2,1)S(1)}, bf16[512,256]{1,0:T(8,128)(2,1)S(1)}) custom-call(s32[1,1]{1,0:T(1,128)} %bitcast.4.place_ref, s32[1,1]{1,0:T(1,128)} %bitcast.5.side_ref, s32[1,4]{1,0:T(1,128)S(1)} %add_bitcast_fusion.places_ref, ...), custom_call_target="tpu_custom_call" | custom-call | flops 1000 | bytes 1000 | tf_op jit(solution)/shard_map/pallas_call | solution.py:42
  93.6 1.0 collective-permute-done.19
  94.7 1.4 %collective-permute-start.21 = (bf16[256,256]{1,0:T(8,128)(2,1)S(1)}, bf16[256,256]{1,0:T(8,128)(2,1)S(1)}, u32[]{:S(2)}, u32[]{:S(2)}) collective-permute-start(bf16[256,256]{1,0:T(8,128)(2,1)S(1)} %get-tuple-element.46), channel_id=1, source_target_pairs={{0,2},{1,3},{2,0},{3,1},{4,6},{5,7},{6,4},{7,5},{8,10},{9,11},{10,... | collective-permute-start | bytes 393224 | tf_op jit(solution)/shard_map/ppermute | solution.py:311
  96.1 0.7 collective-permute-start.20
  96.8 4.3 %collective-permute-done.21.far_ref = bf16[256,256]{1,0:T(8,128)(2,1)S(1)} collective-permute-done((bf16[256,256]{1,0:T(8,128)(2,1)S(1)}, bf16[256,256]{1,0:T(8,128)(2,1)S(1)}, u32[]{:S(2)}, u32[]{:S(2)}) %collective-permute-start.21) | collective-permute-done | bytes 131104 | tf_op jit(solution)/shard_map/ppermute | solution.py:311
  101.1 2.0 %shard_map.136.refs_0_ = bf16[256,256]{1,0:T(8,128)(2,1)S(1)} custom-call(f32[2,2]{1,0:T(2,128)S(1)} %reshape.19.edge_ref, bf16[512,256]{1,0:T(8,128)(2,1)S(1)} %copy-done.6, bf16[512,256]{1,0:T(8,128)(2,1)S(1)} %get-tuple-element.39.keep_ref, bf16[512,256]{1,0:T(8,128)(2,1)S(1)} %collective-permute-done.18.near_ref, ...), custom_call_target="tpu_custom_call" | custom-call | flops 402653184 | bytes 2097152 | tf_op jit(solution)/shard_map/pallas_call | solution.py:42
  103.1 2.7 %shard_map.137 = bf16[512,256]{1,0:T(8,128)(2,1)} custom-call(f32[2,2]{1,0:T(2,128)S(1)} %reshape.19.edge_ref, bf16[512,256]{1,0:T(8,128)(2,1)S(1)} %copy-done.6, bf16[512,256]{1,0:T(8,128)(2,1)S(1)} %get-tuple-element.39.keep_ref, bf16[512,256]{1,0:T(8,128)(2,1)S(1)} %collective-permute-done.18.near_ref, ...), custom_call_target="tpu_custom_call" | custom-call | flops 402653184 | bytes 2097152 | tf_op jit(solution)/shard_map/pallas_call | solution.py:42
  (64 shorter events, 1.6 us)
Async XLA Ops:
  0.6 8.2 %copy-start.4 = (bf16[512,256]{1,0:T(8,128)(2,1)S(1)}, bf16[512,256]{1,0:T(8,128)(2,1)}, u32[]{:S(2)}) copy-start(bf16[512,256]{1,0:T(8,128)(2,1)} %values_ref.7) | copy-start | bytes 786436
  0.6 8.2 %copy-start.3 = (bf16[512,256]{1,0:T(8,128)(2,1)S(1)}, bf16[512,256]{1,0:T(8,128)(2,1)}, u32[]{:S(2)}) copy-start(bf16[512,256]{1,0:T(8,128)(2,1)} %keys_ref.7) | copy-start | bytes 786436
  0.7 8.2 %copy-start.8 = (bf16[512,256]{1,0:T(8,128)(2,1)S(1)}, bf16[512,256]{1,0:T(8,128)(2,1)}, u32[]{:S(2)}) copy-start(bf16[512,256]{1,0:T(8,128)(2,1)} %queries_ref.5) | copy-start | bytes 786436
  0.7 10.4 %copy-start.1 = (bf16[512,256]{1,0:T(8,128)(2,1)S(1)}, bf16[512,256]{1,0:T(8,128)(2,1)}, u32[]{:S(2)}) copy-start(bf16[512,256]{1,0:T(8,128)(2,1)} %keys_ref.9) | copy-start | bytes 786436
  0.7 11.1 %copy-start.2 = (bf16[512,256]{1,0:T(8,128)(2,1)S(1)}, bf16[512,256]{1,0:T(8,128)(2,1)}, u32[]{:S(2)}) copy-start(bf16[512,256]{1,0:T(8,128)(2,1)} %values_ref.9) | copy-start | bytes 786436
  5.9 13.2 %copy-start.21 = (bf16[256,768]{1,0:T(8,128)(2,1)S(1)}, bf16[256,768]{1,0:T(8,128)(2,1)}, u32[]{:S(2)}) copy-start(bf16[256,768]{1,0:T(8,128)(2,1)} %get-tuple-element.24) | copy-start | bytes 1179652
  5.9 13.2 %collective-permute-start = (bf16[256,768]{1,0:T(8,128)(2,1)}, bf16[256,768]{1,0:T(8,128)(2,1)}, u32[]{:S(2)}, u32[]{:S(2)}) collective-permute-start(bf16[256,768]{1,0:T(8,128)(2,1)} %get-tuple-element.25), channel_id=1, source_target_pairs={{0,4},{4,0},{8,12},{12,8},{16,20},{20,16},{24,28},{28,24},{1,5},{5... | collective-permute-start | bytes 1179656 | tf_op jit(solution)/shard_map/ppermute | solution.py:316
  8.8 13.5 %copy-start.20 = (bf16[256,768]{1,0:T(8,128)(2,1)S(1)}, bf16[256,768]{1,0:T(8,128)(2,1)}, u32[]{:S(2)}) copy-start(bf16[256,768]{1,0:T(8,128)(2,1)} %get-tuple-element.26) | copy-start | bytes 1179652
  8.9 17.7 %collective-permute-start.8 = (bf16[1536,128]{1,0:T(8,128)(2,1)S(1)}, bf16[1536,128]{1,0:T(8,128)(2,1)S(1)}, u32[]{:S(2)}, u32[]{:S(2)}) collective-permute-start(bf16[1536,128]{1,0:T(8,128)(2,1)S(1)} %shard_map.132), channel_id=1, source_target_pairs={{0,4},{4,0},{8,12},{12,8},{16,20},{20,16},{24,28},{28,24},{1,5},{5... | collective-permute-start | bytes 1179656 | tf_op jit(solution)/shard_map/ppermute | solution.py:316
  9.0 13.4 %collective-permute-start.4 = (bf16[256,768]{1,0:T(8,128)(2,1)}, bf16[256,768]{1,0:T(8,128)(2,1)S(1)}, u32[]{:S(2)}, u32[]{:S(2)}) collective-permute-start(bf16[256,768]{1,0:T(8,128)(2,1)} %get-tuple-element.27), channel_id=1, source_target_pairs={{0,8},{4,12},{8,0},{12,4},{16,24},{20,28},{24,16},{28,20},{1,9},{5... | collective-permute-start | bytes 1179656 | tf_op jit(solution)/shard_map/ppermute | solution.py:316
  20.2 8.3 %collective-permute-start.1 = (bf16[128,768]{1,0:T(8,128)(2,1)S(1)}, bf16[128,768]{1,0:T(8,128)(2,1)S(1)}, u32[]{:S(2)}, u32[]{:S(2)}) collective-permute-start(bf16[128,768]{1,0:T(8,128)(2,1)S(1)} %get-tuple-element.50), channel_id=1, source_target_pairs={{0,8},{4,12},{8,0},{12,4},{16,24},{20,28},{24,16},{28,20},{1,9},{5... | collective-permute-start | bytes 589832 | tf_op jit(solution)/shard_map/ppermute | solution.py:316
  22.5 10.8 %collective-permute-start.5 = (bf16[128,768]{1,0:T(8,128)(2,1)S(1)}, bf16[128,768]{1,0:T(8,128)(2,1)S(1)}, u32[]{:S(2)}, u32[]{:S(2)}) collective-permute-start(bf16[128,768]{1,0:T(8,128)(2,1)S(1)} %get-tuple-element.48), channel_id=1, source_target_pairs={{0,16},{4,20},{8,24},{12,28},{16,0},{20,4},{24,8},{28,12},{1,17},{... | collective-permute-start | bytes 589832 | tf_op jit(solution)/shard_map/ppermute | solution.py:316
  26.7 26.0 %copy-start.13 = (bf16[1024,128]{1,0:T(8,128)(2,1)}, bf16[1024,128]{1,0:T(8,128)(2,1)S(1)}, u32[]{:S(2)}) copy-start(bf16[1024,128]{1,0:T(8,128)(2,1)S(1)} %get-tuple-element.30.high_ref) | copy-start | bytes 786436
  28.6 13.3 %collective-permute-start.2 = (bf16[64,768]{1,0:T(8,128)(2,1)S(1)}, bf16[64,768]{1,0:T(8,128)(2,1)S(1)}, u32[]{:S(2)}, u32[]{:S(2)}) collective-permute-start(bf16[64,768]{1,0:T(8,128)(2,1)S(1)} %get-tuple-element.54), channel_id=1, source_target_pairs={{0,16},{4,20},{8,24},{12,28},{16,0},{20,4},{24,8},{28,12},{1,17},{... | collective-permute-start | bytes 294920 | tf_op jit(solution)/shard_map/ppermute | solution.py:316
  33.4 12.9 %collective-permute-start.6 = (bf16[64,768]{1,0:T(8,128)(2,1)S(1)}, bf16[64,768]{1,0:T(8,128)(2,1)S(1)}, u32[]{:S(2)}, u32[]{:S(2)}) collective-permute-start(bf16[64,768]{1,0:T(8,128)(2,1)S(1)} %get-tuple-element.52), channel_id=1, source_target_pairs={{0,4},{4,0},{8,12},{12,8},{16,20},{20,16},{24,28},{28,24},{1,5},{5... | collective-permute-start | bytes 294920 | tf_op jit(solution)/shard_map/ppermute | solution.py:316
  35.1 17.6 %collective-permute-start.9 = (bf16[1024,128]{1,0:T(8,128)(2,1)S(1)}, bf16[1024,128]{1,0:T(8,128)(2,1)S(1)}, u32[]{:S(2)}, u32[]{:S(2)}) collective-permute-start(bf16[1024,128]{1,0:T(8,128)(2,1)S(1)} %get-tuple-element.30.high_ref), channel_id=1, source_target_pairs={{0,8},{4,12},{8,16},{12,20},{16,24},{20,28},{1,9},{5,13},{9,17},{1... | collective-permute-start | bytes 786440 | tf_op jit(solution)/shard_map/ppermute | solution.py:305
  38.2 15.1 %collective-permute-start.10 = (bf16[1024,128]{1,0:T(8,128)(2,1)S(1)}, bf16[1024,128]{1,0:T(8,128)(2,1)S(1)}, u32[]{:S(2)}, u32[]{:S(2)}) collective-permute-start(bf16[1024,128]{1,0:T(8,128)(2,1)S(1)} %get-tuple-element.31.low_ref), channel_id=1, source_target_pairs={{8,0},{12,4},{16,8},{20,12},{24,16},{28,20},{9,1},{13,5},{17,9},{2... | collective-permute-start | bytes 786440 | tf_op jit(solution)/shard_map/ppermute | solution.py:305
  39.5 14.5 %collective-permute-start.11 = (bf16[1024,256]{1,0:T(8,128)(2,1)}, bf16[1024,256]{1,0:T(8,128)(2,1)S(1)}, u32[]{:S(2)}, u32[]{:S(2)}) collective-permute-start(bf16[1024,256]{1,0:T(8,128)(2,1)} %constant_dynamic-update-slice_fusion), channel_id=1, source_target_pairs={{0,4},{4,8},{8,12},{12,16},{16,20},{20,24},{24,28},{1,5},{5,9},{9,... | collective-permute-start | bytes 1572872 | tf_op jit(solution)/shard_map/ppermute | solution.py:305
  41.9 7.4 %collective-permute-start.3 = (bf16[64,768]{1,0:T(8,128)(2,1)S(1)}, bf16[64,768]{1,0:T(8,128)(2,1)S(1)}, u32[]{:S(2)}, u32[]{:S(2)}) collective-permute-start(bf16[64,768]{1,0:T(8,128)(2,1)S(1)} %add_convert_fusion.3), channel_id=1, source_target_pairs={{0,16},{4,20},{8,24},{12,28},{16,0},{20,4},{24,8},{28,12},{1,17},{... | collective-permute-start | bytes 294920 | tf_op jit(solution)/shard_map/ppermute | solution.py:316
  46.3 5.7 %collective-permute-start.7 = (bf16[64,768]{1,0:T(8,128)(2,1)S(1)}, bf16[64,768]{1,0:T(8,128)(2,1)S(1)}, u32[]{:S(2)}, u32[]{:S(2)}) collective-permute-start(bf16[64,768]{1,0:T(8,128)(2,1)S(1)} %add_convert_fusion.2), channel_id=1, source_target_pairs={{0,4},{4,0},{8,12},{12,8},{16,20},{20,16},{24,28},{28,24},{1,5},{5... | collective-permute-start | bytes 294920 | tf_op jit(solution)/shard_map/ppermute | solution.py:316
  52.6 0.7 copy-start.15
  53.3 0.7 copy-start.17
  54.0 16.9 %collective-permute-start.12 = (bf16[128,768]{1,0:T(8,128)(2,1)}, bf16[128,768]{1,0:T(8,128)(2,1)}, u32[]{:S(2)}, u32[]{:S(2)}) collective-permute-start(bf16[128,768]{1,0:T(8,128)(2,1)} %pad_maximum_fusion.2), channel_id=1, source_target_pairs={{0,8},{4,12},{8,0},{12,4},{16,24},{20,28},{24,16},{28,20},{1,9},{5... | collective-permute-start | bytes 589832 | tf_op jit(solution)/shard_map/ppermute | solution.py:316
  59.3 23.9 %copy-start = (bf16[1,512,3,512]{3,1,2,0:T(8,128)(2,1)S(1)}, bf16[1,512,3,512]{3,1,2,0:T(8,128)(2,1)}, u32[]{:S(2)}) copy-start(bf16[1,512,3,512]{3,1,2,0:T(8,128)(2,1)} %param.19) | copy-start | bytes 4718596
  59.3 12.7 %collective-permute-start.13 = (bf16[128,768]{1,0:T(8,128)(2,1)}, bf16[128,768]{1,0:T(8,128)(2,1)S(1)}, u32[]{:S(2)}, u32[]{:S(2)}) collective-permute-start(bf16[128,768]{1,0:T(8,128)(2,1)} %pad_maximum_fusion.3), channel_id=1, source_target_pairs={{0,16},{4,20},{8,24},{12,28},{16,0},{20,4},{24,8},{28,12},{1,17},{... | collective-permute-start | bytes 589832 | tf_op jit(solution)/shard_map/ppermute | solution.py:316
  61.3 0.9 copy-start.14
  62.2 0.9 copy-start.16
  63.2 0.9 copy-start.18
  64.1 7.9 %copy-start.19 = (bf16[128,768]{1,0:T(8,128)(2,1)S(1)}, bf16[128,768]{1,0:T(8,128)(2,1)}, u32[]{:S(2)}) copy-start(bf16[128,768]{1,0:T(8,128)(2,1)} %pad_maximum_fusion.3) | copy-start | bytes 589828
  67.2 5.7 %copy-start.9 = (bf16[512,128]{1,0:T(8,128)(2,1)}, bf16[512,128]{1,0:T(8,128)(2,1)S(1)}, u32[]{:S(2)}) copy-start(bf16[512,128]{1,0:T(8,128)(2,1)S(1)} %get-tuple-element.35.refs_5_) | copy-start | bytes 393220
  67.2 11.0 %collective-permute-start.16 = (bf16[512,128]{1,0:T(8,128)(2,1)S(1)}, bf16[512,128]{1,0:T(8,128)(2,1)S(1)}, u32[]{:S(2)}, u32[]{:S(2)}) collective-permute-start(bf16[512,128]{1,0:T(8,128)(2,1)S(1)} %get-tuple-element.38), channel_id=1, source_target_pairs={{0,4},{4,0},{8,12},{12,8},{16,20},{20,16},{24,28},{28,24},{1,5},{5... | collective-permute-start | bytes 393224 | tf_op jit(solution)/shard_map/ppermute | solution.py:316
  72.8 10.4 %collective-permute-start.14 = (bf16[256,768]{1,0:T(8,128)(2,1)S(1)}, bf16[256,768]{1,0:T(8,128)(2,1)}, u32[]{:S(2)}, u32[]{:S(2)}) collective-permute-start(bf16[256,768]{1,0:T(8,128)(2,1)S(1)} %pad_maximum_fusion.refs_0_), channel_id=1, source_target_pairs={{0,4},{4,0},{8,12},{12,8},{16,20},{20,16},{24,28},{28,24},{1,5},{5... | collective-permute-start | bytes 1179656 | tf_op jit(solution)/shard_map/ppermute | solution.py:316
  72.8 10.4 %collective-permute-start.15 = (bf16[256,768]{1,0:T(8,128)(2,1)}, bf16[256,768]{1,0:T(8,128)(2,1)}, u32[]{:S(2)}, u32[]{:S(2)}) collective-permute-start(bf16[256,768]{1,0:T(8,128)(2,1)} %pad_maximum_fusion.1.refs_2_), channel_id=1, source_target_pairs={{0,8},{4,12},{8,0},{12,4},{16,24},{20,28},{24,16},{28,20},{1,9},{5... | collective-permute-start | bytes 1179656 | tf_op jit(solution)/shard_map/ppermute | solution.py:316
  78.2 0.7 copy-start.11
  78.9 14.2 %collective-permute-start.17 = (bf16[1024,256]{1,0:T(8,128)(2,1)}, bf16[1024,256]{1,0:T(8,128)(2,1)S(1)}, u32[]{:S(2)}, u32[]{:S(2)}) collective-permute-start(bf16[1024,256]{1,0:T(8,128)(2,1)} %constant_dynamic-update-slice_fusion), channel_id=1, source_target_pairs={{4,0},{8,4},{12,8},{16,12},{20,16},{24,20},{28,24},{5,1},{9,5},{13... | collective-permute-start | bytes 1572872 | tf_op jit(solution)/shard_map/ppermute | solution.py:305
  83.2 1.2 %copy-start.5 = (bf16[512,1024]{1,0:T(8,128)(2,1)S(1)}, bf16[512,1024]{1,0:T(8,128)(2,1)}, u32[]{:S(2)}) copy-start(bf16[512,1024]{1,0:T(8,128)(2,1)} %refs_8_.1) | copy-start | bytes 3145732
  84.4 0.9 copy-start.7
  85.4 0.9 copy-start.10
  86.3 0.9 copy-start.12
  93.0 8.1 %copy-start.6 = (bf16[512,256]{1,0:T(8,128)(2,1)S(1)}, bf16[512,256]{1,0:T(8,128)(2,1)}, u32[]{:S(2)}) copy-start(bf16[512,256]{1,0:T(8,128)(2,1)} %queries_ref.7) | copy-start | bytes 786436
  93.0 1.6 %collective-permute-start.19 = (bf16[512,256]{1,0:T(8,128)(2,1)S(1)}, bf16[512,256]{1,0:T(8,128)(2,1)S(1)}, u32[]{:S(2)}, u32[]{:S(2)}) collective-permute-start(bf16[512,256]{1,0:T(8,128)(2,1)S(1)} %get-tuple-element.44), channel_id=1, source_target_pairs={{0,1},{1,0},{2,3},{3,2},{4,5},{5,4},{6,7},{7,6},{8,9},{9,8},{10,11... | collective-permute-start | bytes 786440 | tf_op jit(solution)/shard_map/ppermute | solution.py:311
  93.1 3.7 %collective-permute-start.18 = (bf16[512,256]{1,0:T(8,128)(2,1)S(1)}, bf16[512,256]{1,0:T(8,128)(2,1)S(1)}, u32[]{:S(2)}, u32[]{:S(2)}) collective-permute-start(bf16[512,256]{1,0:T(8,128)(2,1)S(1)} %get-tuple-element.42), channel_id=1, source_target_pairs={{0,1},{1,0},{2,3},{3,2},{4,5},{5,4},{6,7},{7,6},{8,9},{9,8},{10,11... | collective-permute-start | bytes 786440 | tf_op jit(solution)/shard_map/ppermute | solution.py:311
  94.7 6.4 %collective-permute-start.21 = (bf16[256,256]{1,0:T(8,128)(2,1)S(1)}, bf16[256,256]{1,0:T(8,128)(2,1)S(1)}, u32[]{:S(2)}, u32[]{:S(2)}) collective-permute-start(bf16[256,256]{1,0:T(8,128)(2,1)S(1)} %get-tuple-element.46), channel_id=1, source_target_pairs={{0,2},{1,3},{2,0},{3,1},{4,6},{5,7},{6,4},{7,5},{8,10},{9,11},{10,... | collective-permute-start | bytes 393224 | tf_op jit(solution)/shard_map/ppermute | solution.py:311
  96.1 7.0 %collective-permute-start.20 = (bf16[256,256]{1,0:T(8,128)(2,1)S(1)}, bf16[256,256]{1,0:T(8,128)(2,1)S(1)}, u32[]{:S(2)}, u32[]{:S(2)}) collective-permute-start(bf16[256,256]{1,0:T(8,128)(2,1)S(1)} %get-tuple-element.47), channel_id=1, source_target_pairs={{0,2},{1,3},{2,0},{3,1},{4,6},{5,7},{6,4},{7,5},{8,10},{9,11},{10,... | collective-permute-start | bytes 393224 | tf_op jit(solution)/shard_map/ppermute | solution.py:311

commit v24 on v21

--- a/solution.py
+++ b/solution.py
@@ -235,12 +235,12 @@
         copy.wait()
     limit_norm = math.sqrt(FAST_HIDDEN * FAST_DIM) / 2.0
     step = 64
-    square = jnp.zeros((1, pieces[0].shape[1]), F32)
+    square = jnp.zeros((8, pieces[0].shape[1]), F32)
     for piece in pieces:
         for low in range(0, piece.shape[0], step):
             part = piece[low:low + step, :].astype(F32)
-            square = square + jnp.sum(part * part, axis=0, keepdims=True)
-    square = jnp.sum(square, axis=1, keepdims=True)
+            square = square + jnp.sum((part * part).reshape(step // 8, 8, -1), axis=0)
+    square = jnp.sum(jnp.sum(square, axis=0, keepdims=True), axis=1, keepdims=True)
     factor = jnp.minimum(1.0, limit_norm * lax.rsqrt(square + 1e-06))
     copies[-5].wait()
     per_chunk = len(pieces) // 2

time: 101 us -> 101 us (level)
  no operation moved by 1% of the time
where the time goes in v24:
time: 101 us
  starting transfers between devices  51.2 us (51%)
  waiting for transfers between devices  24.3 us (24%)
  Pallas kernels  20 us (20%)
  local copies, waits for them, and re-layouts  2.33 us (2%)
  other arithmetic  2.09 us (2%)
    ppermute x14, starting transfers between devices, seq_swap(): lax.ppermute(value, 'seq', [(i, i ^ step) for i in range(lax.axis_size('s...  39.3 us
    ppermute x14, waiting for transfers between devices, seq_swap(): lax.ppermute(value, 'seq', [(i, i ^ step) for i in range(lax.axis_size('s...  19.8 us
    pallas_call x6, Pallas kernels, call(): pl.pallas_call(body, out_shape=out_shapes, in_specs=in_specs, out_specs=j...  14.8 us
    ppermute x4, starting transfers between devices, seq_shift(): lax.ppermute(value, 'seq', [(i, i + step) for i in range(peers) if 0 <= i...  9.26 us
    pallas_call x1, Pallas kernels, local(): pl.pallas_call(functools.partial(gradient_kernel, orders), grid=(1,), out...  5.16 us
    ppermute x4, waiting for transfers between devices, head_swap(): lax.ppermute(value, 'head', [(i, i ^ bit) for i in range(lax.axis_size('h...  4.56 us
    ppermute x4, starting transfers between devices, head_swap(): lax.ppermute(value, 'head', [(i, i ^ bit) for i in range(lax.axis_size('h...  2.65 us
  transfers between devices with their start and end apart: 22, of which 11 were waited for; matrix products, arithmetic and copies ran while one was open for 4% of the time, Pallas kernels for 12%

profile of v24, /device:TPU:0, one launch (start us, length us, event | category | flops | bytes accessed | tf_op | source)
XLA Modules:
  0.0 100.9 jit_solution(11960230042776371920)
XLA Ops:
  0.7 5.2 %shard_map.131 = (bf16[256,768]{1,0:T(8,128)(2,1)}, bf16[256,768]{1,0:T(8,128)(2,1)}, bf16[256,768]{1,0:T(8,128)(2,1)}, bf16[256,768]{1,0:T(8,128)(2,1)}) custom-call(s32[1,1]{1,0:T(1,128)} %bitcast.4.place_ref, f32[1,512]{1,0:T(1,128)} %bitcast.23, bf16[512,512]{1,0:T(8,128)(2,1)} %keys_ref.5, bf16[512,512]{1,0:T(8,128)(2,1)} %values_ref.5, ...), custom_call_target="tpu_custom_call" | custom-call | flops 1000 | bytes 1000 | tf_op jit(solution)/shard_map/pallas_call | solution.py:390
  5.8 3.0 %collective-permute-start = (bf16[256,768]{1,0:T(8,128)(2,1)}, bf16[256,768]{1,0:T(8,128)(2,1)S(1)}, u32[]{:S(2)}, u32[]{:S(2)}) collective-permute-start(bf16[256,768]{1,0:T(8,128)(2,1)} %get-tuple-element.25), channel_id=1, source_target_pairs={{0,4},{4,0},{8,12},{12,8},{16,20},{20,16},{24,28},{28,24},{1,5},{5... | collective-permute-start | bytes 1179656 | tf_op jit(solution)/shard_map/ppermute | solution.py:316
  8.8 0.1 shard_map.132
  8.9 0.1 collective-permute-start.8
  9.0 2.1 %collective-permute-start.4 = (bf16[256,768]{1,0:T(8,128)(2,1)}, bf16[256,768]{1,0:T(8,128)(2,1)S(1)}, u32[]{:S(2)}, u32[]{:S(2)}) collective-permute-start(bf16[256,768]{1,0:T(8,128)(2,1)} %get-tuple-element.27), channel_id=1, source_target_pairs={{0,8},{4,12},{8,0},{12,4},{16,24},{20,28},{24,16},{28,20},{1,9},{5... | collective-permute-start | bytes 1179656 | tf_op jit(solution)/shard_map/ppermute | solution.py:316
  11.1 0.7 constant_dynamic-update-slice_fusion.1
  11.8 0.7 constant_dynamic-update-slice_fusion
  12.5 6.5 %collective-permute-done = bf16[256,768]{1,0:T(8,128)(2,1)S(1)} collective-permute-done((bf16[256,768]{1,0:T(8,128)(2,1)}, bf16[256,768]{1,0:T(8,128)(2,1)S(1)}, u32[]{:S(2)}, u32[]{:S(2)}) %collective-permute-start) | collective-permute-done | bytes 393248 | tf_op jit(solution)/shard_map/ppermute | solution.py:316
  19.0 0.1 add_convert_fusion.1
  19.1 2.2 %collective-permute-start.1 = (bf16[128,768]{1,0:T(8,128)(2,1)S(1)}, bf16[128,768]{1,0:T(8,128)(2,1)S(1)}, u32[]{:S(2)}, u32[]{:S(2)}) collective-permute-start(bf16[128,768]{1,0:T(8,128)(2,1)S(1)} %get-tuple-element.50), channel_id=1, source_target_pairs={{0,8},{4,12},{8,0},{12,4},{16,24},{20,28},{24,16},{28,20},{1,9},{5... | collective-permute-start | bytes 589832 | tf_op jit(solution)/shard_map/ppermute | solution.py:316
  21.2 0.1 add_convert_fusion
  21.3 2.7 %collective-permute-start.5 = (bf16[128,768]{1,0:T(8,128)(2,1)S(1)}, bf16[128,768]{1,0:T(8,128)(2,1)S(1)}, u32[]{:S(2)}, u32[]{:S(2)}) collective-permute-start(bf16[128,768]{1,0:T(8,128)(2,1)S(1)} %get-tuple-element.48), channel_id=1, source_target_pairs={{0,16},{4,20},{8,24},{12,28},{16,0},{20,4},{24,8},{28,12},{1,17},{... | collective-permute-start | bytes 589832 | tf_op jit(solution)/shard_map/ppermute | solution.py:316
  24.0 2.6 %collective-permute-done.8.other_ref = bf16[1536,128]{1,0:T(8,128)(2,1)S(1)} collective-permute-done((bf16[1536,128]{1,0:T(8,128)(2,1)S(1)}, bf16[1536,128]{1,0:T(8,128)(2,1)S(1)}, u32[]{:S(2)}, u32[]{:S(2)}) %collective-permute-start.8) | collective-permute-done | bytes 393248 | tf_op jit(solution)/shard_map/ppermute | solution.py:316
  26.7 0.7 collective-permute-done.1
  27.4 2.1 %collective-permute-start.2 = (bf16[64,768]{1,0:T(8,128)(2,1)S(1)}, bf16[64,768]{1,0:T(8,128)(2,1)S(1)}, u32[]{:S(2)}, u32[]{:S(2)}) collective-permute-start(bf16[64,768]{1,0:T(8,128)(2,1)S(1)} %get-tuple-element.54), channel_id=1, source_target_pairs={{0,16},{4,20},{8,24},{12,28},{16,0},{20,4},{24,8},{28,12},{1,17},{... | collective-permute-start | bytes 294920 | tf_op jit(solution)/shard_map/ppermute | solution.py:316
  29.6 2.5 %collective-permute-done.5 = bf16[128,768]{1,0:T(8,128)(2,1)S(1)} collective-permute-done((bf16[128,768]{1,0:T(8,128)(2,1)S(1)}, bf16[128,768]{1,0:T(8,128)(2,1)S(1)}, u32[]{:S(2)}, u32[]{:S(2)}) %collective-permute-start.5) | collective-permute-done | bytes 196640 | tf_op jit(solution)/shard_map/ppermute | solution.py:316
  32.1 1.6 %collective-permute-start.6 = (bf16[64,768]{1,0:T(8,128)(2,1)S(1)}, bf16[64,768]{1,0:T(8,128)(2,1)S(1)}, u32[]{:S(2)}, u32[]{:S(2)}) collective-permute-start(bf16[64,768]{1,0:T(8,128)(2,1)S(1)} %get-tuple-element.52), channel_id=1, source_target_pairs={{0,4},{4,0},{8,12},{12,8},{16,20},{20,16},{24,28},{28,24},{1,5},{5... | collective-permute-start | bytes 294920 | tf_op jit(solution)/shard_map/ppermute | solution.py:316
  33.7 4.1 %collective-permute-start.9 = (bf16[1024,128]{1,0:T(8,128)(2,1)S(1)}, bf16[1024,128]{1,0:T(8,128)(2,1)S(1)}, u32[]{:S(2)}, u32[]{:S(2)}) collective-permute-start(bf16[1024,128]{1,0:T(8,128)(2,1)S(1)} %get-tuple-element.30.high_ref), channel_id=1, source_target_pairs={{0,8},{4,12},{8,16},{12,20},{16,24},{20,28},{1,9},{5,13},{9,17},{1... | collective-permute-start | bytes 786440 | tf_op jit(solution)/shard_map/ppermute | solution.py:305
  37.8 1.3 %collective-permute-start.10 = (bf16[1024,128]{1,0:T(8,128)(2,1)S(1)}, bf16[1024,128]{1,0:T(8,128)(2,1)S(1)}, u32[]{:S(2)}, u32[]{:S(2)}) collective-permute-start(bf16[1024,128]{1,0:T(8,128)(2,1)S(1)} %get-tuple-element.31.low_ref), channel_id=1, source_target_pairs={{8,0},{12,4},{16,8},{20,12},{24,16},{28,20},{9,1},{13,5},{17,9},{2... | collective-permute-start | bytes 786440 | tf_op jit(solution)/shard_map/ppermute | solution.py:305
  39.1 2.4 %collective-permute-start.11 = (bf16[1024,256]{1,0:T(8,128)(2,1)}, bf16[1024,256]{1,0:T(8,128)(2,1)S(1)}, u32[]{:S(2)}, u32[]{:S(2)}) collective-permute-start(bf16[1024,256]{1,0:T(8,128)(2,1)} %constant_dynamic-update-slice_fusion), channel_id=1, source_target_pairs={{0,4},{4,8},{8,12},{12,16},{16,20},{20,24},{24,28},{1,5},{5,9},{9,... | collective-permute-start | bytes 1572872 | tf_op jit(solution)/shard_map/ppermute | solution.py:305
  41.5 4.0 %collective-permute-start.3 = (bf16[64,768]{1,0:T(8,128)(2,1)S(1)}, bf16[64,768]{1,0:T(8,128)(2,1)S(1)}, u32[]{:S(2)}, u32[]{:S(2)}) collective-permute-start(bf16[64,768]{1,0:T(8,128)(2,1)S(1)} %add_convert_fusion.3), channel_id=1, source_target_pairs={{0,16},{4,20},{8,24},{12,28},{16,0},{20,4},{24,8},{28,12},{1,17},{... | collective-permute-start | bytes 294920 | tf_op jit(solution)/shard_map/ppermute | solution.py:316
  45.6 3.1 %collective-permute-start.7 = (bf16[64,768]{1,0:T(8,128)(2,1)S(1)}, bf16[64,768]{1,0:T(8,128)(2,1)S(1)}, u32[]{:S(2)}, u32[]{:S(2)}) collective-permute-start(bf16[64,768]{1,0:T(8,128)(2,1)S(1)} %add_convert_fusion.2), channel_id=1, source_target_pairs={{0,4},{4,0},{8,12},{12,8},{16,20},{20,16},{24,28},{28,24},{1,5},{5... | collective-permute-start | bytes 294920 | tf_op jit(solution)/shard_map/ppermute | solution.py:316
  48.7 2.6 %collective-permute-done.7 = bf16[64,768]{1,0:T(8,128)(2,1)S(1)} collective-permute-done((bf16[64,768]{1,0:T(8,128)(2,1)S(1)}, bf16[64,768]{1,0:T(8,128)(2,1)S(1)}, u32[]{:S(2)}, u32[]{:S(2)}) %collective-permute-start.7) | collective-permute-done | bytes 98336 | tf_op jit(solution)/shard_map/ppermute | solution.py:316
  51.3 7.5 %collective-permute-start.12 = (bf16[128,768]{1,0:T(8,128)(2,1)S(1)}, bf16[128,768]{1,0:T(8,128)(2,1)S(1)}, u32[]{:S(2)}, u32[]{:S(2)}) collective-permute-start(bf16[128,768]{1,0:T(8,128)(2,1)S(1)} %pad_maximum_fusion.2), channel_id=1, source_target_pairs={{0,8},{4,12},{8,0},{12,4},{16,24},{20,28},{24,16},{28,20},{1,9},{5... | collective-permute-start | bytes 589832 | tf_op jit(solution)/shard_map/ppermute | solution.py:316
  58.9 0.1 pad_maximum_fusion.4
  58.9 0.1 reshape.19.edge_ref
  59.0 5.2 %collective-permute-start.13 = (bf16[128,768]{1,0:T(8,128)(2,1)S(1)}, bf16[128,768]{1,0:T(8,128)(2,1)S(1)}, u32[]{:S(2)}, u32[]{:S(2)}) collective-permute-start(bf16[128,768]{1,0:T(8,128)(2,1)S(1)} %pad_maximum_fusion.3), channel_id=1, source_target_pairs={{0,16},{4,20},{8,24},{12,28},{16,0},{20,4},{24,8},{28,12},{1,17},{... | collective-permute-start | bytes 589832 | tf_op jit(solution)/shard_map/ppermute | solution.py:316
  64.2 3.1 %shard_map.134 = (bf16[512,128]{1,0:T(8,128)(2,1)S(1)}, bf16[512,128]{1,0:T(8,128)(2,1)S(1)}) custom-call(f32[2,2]{1,0:T(2,128)S(1)} %reshape.19.edge_ref, s32[1,1]{1,0:T(1,128)} %bitcast.5.side_ref, bf16[512,256]{1,0:T(8,128)(2,1)S(1)} %copy-done.6, bf16[1536,128]{1,0:T(8,128)(2,1)S(1)} %collective-permute-done.8.other_ref, ...), custom_call_target="tpu_custom_call" | custom-call | flops 805306368 | bytes 2097152 | tf_op jit(solution)/shard_map/pallas_call | solution.py:42
  67.3 0.1 collective-permute-start.16
  67.4 1.3 %collective-permute-done.13 = bf16[128,768]{1,0:T(8,128)(2,1)S(1)} collective-permute-done((bf16[128,768]{1,0:T(8,128)(2,1)S(1)}, bf16[128,768]{1,0:T(8,128)(2,1)S(1)}, u32[]{:S(2)}, u32[]{:S(2)}) %collective-permute-start.13) | collective-permute-done | bytes 196640 | tf_op jit(solution)/shard_map/ppermute | solution.py:316
  68.7 0.8 collective-permute-start.14
  69.6 4.9 %collective-permute-start.15 = (bf16[256,768]{1,0:T(8,128)(2,1)S(1)}, bf16[256,768]{1,0:T(8,128)(2,1)S(1)}, u32[]{:S(2)}, u32[]{:S(2)}) collective-permute-start(bf16[256,768]{1,0:T(8,128)(2,1)S(1)} %pad_maximum_fusion.1.refs_2_), channel_id=1, source_target_pairs={{0,8},{4,12},{8,0},{12,4},{16,24},{20,28},{24,16},{28,20},{1,9},{5... | collective-permute-start | bytes 1179656 | tf_op jit(solution)/shard_map/ppermute | solution.py:316
  74.5 1.0 %collective-permute-done.16.refs_6_ = bf16[512,128]{1,0:T(8,128)(2,1)S(1)} collective-permute-done((bf16[512,128]{1,0:T(8,128)(2,1)S(1)}, bf16[512,128]{1,0:T(8,128)(2,1)S(1)}, u32[]{:S(2)}, u32[]{:S(2)}) %collective-permute-start.16) | collective-permute-done | bytes 131104 | tf_op jit(solution)/shard_map/ppermute | solution.py:316
  75.5 1.5 %collective-permute-start.17 = (bf16[1024,256]{1,0:T(8,128)(2,1)}, bf16[1024,256]{1,0:T(8,128)(2,1)S(1)}, u32[]{:S(2)}, u32[]{:S(2)}) collective-permute-start(bf16[1024,256]{1,0:T(8,128)(2,1)} %constant_dynamic-update-slice_fusion), channel_id=1, source_target_pairs={{4,0},{8,4},{12,8},{16,12},{20,16},{24,20},{28,24},{5,1},{9,5},{13... | collective-permute-start | bytes 1572872 | tf_op jit(solution)/shard_map/ppermute | solution.py:305
  77.0 0.6 add_bitcast_fusion.places_ref
  77.6 2.1 %collective-permute-done.14.refs_1_ = bf16[256,768]{1,0:T(8,128)(2,1)S(1)} collective-permute-done((bf16[256,768]{1,0:T(8,128)(2,1)S(1)}, bf16[256,768]{1,0:T(8,128)(2,1)S(1)}, u32[]{:S(2)}, u32[]{:S(2)}) %collective-permute-start.14) | collective-permute-done | bytes 393248 | tf_op jit(solution)/shard_map/ppermute | solution.py:316
  79.7 0.5 collective-permute-done.15.refs_3_
  80.2 0.2 copy-done.12
  80.5 0.5 copy-done.13
  81.0 6.9 %shard_map.135 = (bf16[3,64,512]{2,1,0:T(8,128)(2,1)}, bf16[512,256]{1,0:T(8,128)(2,1)}, bf16[512,256]{1,0:T(8,128)(2,1)}, bf16[512,256]{1,0:T(8,128)(2,1)}, bf16[512,256]{1,0:T(8,128)(2,1)}) custom-call(s32[1,1]{1,0:T(1,128)} %bitcast.4.place_ref, s32[1,1]{1,0:T(1,128)} %bitcast.5.side_ref, s32[1,4]{1,0:T(1,128)} %add_bitcast_fusion.places_ref, ...), custom_call_target="tpu_custom_call" | custom-call | flops 1000 | bytes 1000 | tf_op jit(solution)/shard_map/pallas_call | solution.py:42
  88.0 0.5 collective-permute-start.18
  88.5 1.0 convert_element_type.95
  89.5 0.2 collective-permute-done.19
  89.8 1.5 %collective-permute-start.21 = (bf16[256,256]{1,0:T(8,128)(2,1)S(1)}, bf16[256,256]{1,0:T(8,128)(2,1)S(1)}, u32[]{:S(2)}, u32[]{:S(2)}) collective-permute-start(bf16[256,256]{1,0:T(8,128)(2,1)S(1)} %get-tuple-element.46), channel_id=1, source_target_pairs={{0,2},{1,3},{2,0},{3,1},{4,6},{5,7},{6,4},{7,5},{8,10},{9,11},{10,... | collective-permute-start | bytes 393224 | tf_op jit(solution)/shard_map/ppermute | solution.py:311
  91.2 0.6 collective-permute-start.20
  91.9 4.3 %collective-permute-done.21.far_ref = bf16[256,256]{1,0:T(8,128)(2,1)S(1)} collective-permute-done((bf16[256,256]{1,0:T(8,128)(2,1)S(1)}, bf16[256,256]{1,0:T(8,128)(2,1)S(1)}, u32[]{:S(2)}, u32[]{:S(2)}) %collective-permute-start.21) | collective-permute-done | bytes 131104 | tf_op jit(solution)/shard_map/ppermute | solution.py:311
  96.2 2.0 %shard_map.136.refs_0_ = bf16[256,256]{1,0:T(8,128)(2,1)S(1)} custom-call(f32[2,2]{1,0:T(2,128)S(1)} %reshape.19.edge_ref, bf16[512,256]{1,0:T(8,128)(2,1)S(1)} %copy-done.4, bf16[512,256]{1,0:T(8,128)(2,1)S(1)} %copy-done.5, bf16[512,256]{1,0:T(8,128)(2,1)S(1)} %collective-permute-done.18.near_ref, bf16[256,256]{1,0:T(8,128)(2,1)S(1)} %collective-permute-done.21.far_ref, ...), custom_call_target="tpu_custom_call" | custom-call | flops 402653184 | bytes 2097152 | tf_op jit(solution)/shard_map/pallas_call | solution.py:42
  98.2 2.7 %shard_map.137 = bf16[512,256]{1,0:T(8,128)(2,1)} custom-call(f32[2,2]{1,0:T(2,128)S(1)} %reshape.19.edge_ref, bf16[512,256]{1,0:T(8,128)(2,1)S(1)} %copy-done.4, bf16[512,256]{1,0:T(8,128)(2,1)S(1)} %copy-done.5, bf16[512,256]{1,0:T(8,128)(2,1)S(1)} %collective-permute-done.18.near_ref, bf16[256,256]{1,0:T(8,128)(2,1)S(1)} %collective-permute-done.20.far_ref, ...), custom_call_target="tpu_custom_call" | custom-call | flops 402653184 | bytes 2097152 | tf_op jit(solution)/shard_map/pallas_call | solution.py:42
  (50 shorter events, 0.5 us)
Async XLA Ops:
  0.6 8.2 %copy-start.3 = (bf16[512,256]{1,0:T(8,128)(2,1)S(1)}, bf16[512,256]{1,0:T(8,128)(2,1)}, u32[]{:S(2)}) copy-start(bf16[512,256]{1,0:T(8,128)(2,1)} %values_ref.7) | copy-start | bytes 786436
  0.6 8.2 %copy-start.2 = (bf16[512,256]{1,0:T(8,128)(2,1)S(1)}, bf16[512,256]{1,0:T(8,128)(2,1)}, u32[]{:S(2)}) copy-start(bf16[512,256]{1,0:T(8,128)(2,1)} %keys_ref.7) | copy-start | bytes 786436
  0.7 8.2 %copy-start.6 = (bf16[512,256]{1,0:T(8,128)(2,1)S(1)}, bf16[512,256]{1,0:T(8,128)(2,1)}, u32[]{:S(2)}) copy-start(bf16[512,256]{1,0:T(8,128)(2,1)} %queries_ref.5) | copy-start | bytes 786436
  0.7 10.4 %copy-start = (bf16[512,256]{1,0:T(8,128)(2,1)S(1)}, bf16[512,256]{1,0:T(8,128)(2,1)}, u32[]{:S(2)}) copy-start(bf16[512,256]{1,0:T(8,128)(2,1)} %keys_ref.9) | copy-start | bytes 786436
  0.7 11.1 %copy-start.1 = (bf16[512,256]{1,0:T(8,128)(2,1)S(1)}, bf16[512,256]{1,0:T(8,128)(2,1)}, u32[]{:S(2)}) copy-start(bf16[512,256]{1,0:T(8,128)(2,1)} %values_ref.9) | copy-start | bytes 786436
  5.8 13.1 %copy-start.11 = (bf16[256,768]{1,0:T(8,128)(2,1)S(1)}, bf16[256,768]{1,0:T(8,128)(2,1)}, u32[]{:S(2)}) copy-start(bf16[256,768]{1,0:T(8,128)(2,1)} %get-tuple-element.24) | copy-start | bytes 1179652
  5.8 13.1 %collective-permute-start = (bf16[256,768]{1,0:T(8,128)(2,1)}, bf16[256,768]{1,0:T(8,128)(2,1)S(1)}, u32[]{:S(2)}, u32[]{:S(2)}) collective-permute-start(bf16[256,768]{1,0:T(8,128)(2,1)} %get-tuple-element.25), channel_id=1, source_target_pairs={{0,4},{4,0},{8,12},{12,8},{16,20},{20,16},{24,28},{28,24},{1,5},{5... | collective-permute-start | bytes 1179656 | tf_op jit(solution)/shard_map/ppermute | solution.py:316
  8.8 12.4 %copy-start.10 = (bf16[256,768]{1,0:T(8,128)(2,1)S(1)}, bf16[256,768]{1,0:T(8,128)(2,1)}, u32[]{:S(2)}) copy-start(bf16[256,768]{1,0:T(8,128)(2,1)} %get-tuple-element.26) | copy-start | bytes 1179652
  8.9 17.7 %collective-permute-start.8 = (bf16[1536,128]{1,0:T(8,128)(2,1)S(1)}, bf16[1536,128]{1,0:T(8,128)(2,1)S(1)}, u32[]{:S(2)}, u32[]{:S(2)}) collective-permute-start(bf16[1536,128]{1,0:T(8,128)(2,1)S(1)} %shard_map.132), channel_id=1, source_target_pairs={{0,4},{4,0},{8,12},{12,8},{16,20},{20,16},{24,28},{28,24},{1,5},{5... | collective-permute-start | bytes 1179656 | tf_op jit(solution)/shard_map/ppermute | solution.py:316
  9.0 12.2 %collective-permute-start.4 = (bf16[256,768]{1,0:T(8,128)(2,1)}, bf16[256,768]{1,0:T(8,128)(2,1)S(1)}, u32[]{:S(2)}, u32[]{:S(2)}) collective-permute-start(bf16[256,768]{1,0:T(8,128)(2,1)} %get-tuple-element.27), channel_id=1, source_target_pairs={{0,8},{4,12},{8,0},{12,4},{16,24},{20,28},{24,16},{28,20},{1,9},{5... | collective-permute-start | bytes 1179656 | tf_op jit(solution)/shard_map/ppermute | solution.py:316
  19.1 8.3 %collective-permute-start.1 = (bf16[128,768]{1,0:T(8,128)(2,1)S(1)}, bf16[128,768]{1,0:T(8,128)(2,1)S(1)}, u32[]{:S(2)}, u32[]{:S(2)}) collective-permute-start(bf16[128,768]{1,0:T(8,128)(2,1)S(1)} %get-tuple-element.50), channel_id=1, source_target_pairs={{0,8},{4,12},{8,0},{12,4},{16,24},{20,28},{24,16},{28,20},{1,9},{5... | collective-permute-start | bytes 589832 | tf_op jit(solution)/shard_map/ppermute | solution.py:316
  21.3 10.7 %collective-permute-start.5 = (bf16[128,768]{1,0:T(8,128)(2,1)S(1)}, bf16[128,768]{1,0:T(8,128)(2,1)S(1)}, u32[]{:S(2)}, u32[]{:S(2)}) collective-permute-start(bf16[128,768]{1,0:T(8,128)(2,1)S(1)} %get-tuple-element.48), channel_id=1, source_target_pairs={{0,16},{4,20},{8,24},{12,28},{16,0},{20,4},{24,8},{28,12},{1,17},{... | collective-permute-start | bytes 589832 | tf_op jit(solution)/shard_map/ppermute | solution.py:316
  27.4 14.1 %collective-permute-start.2 = (bf16[64,768]{1,0:T(8,128)(2,1)S(1)}, bf16[64,768]{1,0:T(8,128)(2,1)S(1)}, u32[]{:S(2)}, u32[]{:S(2)}) collective-permute-start(bf16[64,768]{1,0:T(8,128)(2,1)S(1)} %get-tuple-element.54), channel_id=1, source_target_pairs={{0,16},{4,20},{8,24},{12,28},{16,0},{20,4},{24,8},{28,12},{1,17},{... | collective-permute-start | bytes 294920 | tf_op jit(solution)/shard_map/ppermute | solution.py:316
  32.1 13.5 %collective-permute-start.6 = (bf16[64,768]{1,0:T(8,128)(2,1)S(1)}, bf16[64,768]{1,0:T(8,128)(2,1)S(1)}, u32[]{:S(2)}, u32[]{:S(2)}) collective-permute-start(bf16[64,768]{1,0:T(8,128)(2,1)S(1)} %get-tuple-element.52), channel_id=1, source_target_pairs={{0,4},{4,0},{8,12},{12,8},{16,20},{20,16},{24,28},{28,24},{1,5},{5... | collective-permute-start | bytes 294920 | tf_op jit(solution)/shard_map/ppermute | solution.py:316
  33.7 17.6 %collective-permute-start.9 = (bf16[1024,128]{1,0:T(8,128)(2,1)S(1)}, bf16[1024,128]{1,0:T(8,128)(2,1)S(1)}, u32[]{:S(2)}, u32[]{:S(2)}) collective-permute-start(bf16[1024,128]{1,0:T(8,128)(2,1)S(1)} %get-tuple-element.30.high_ref), channel_id=1, source_target_pairs={{0,8},{4,12},{8,16},{12,20},{16,24},{20,28},{1,9},{5,13},{9,17},{1... | collective-permute-start | bytes 786440 | tf_op jit(solution)/shard_map/ppermute | solution.py:305
  37.8 13.5 %collective-permute-start.10 = (bf16[1024,128]{1,0:T(8,128)(2,1)S(1)}, bf16[1024,128]{1,0:T(8,128)(2,1)S(1)}, u32[]{:S(2)}, u32[]{:S(2)}) collective-permute-start(bf16[1024,128]{1,0:T(8,128)(2,1)S(1)} %get-tuple-element.31.low_ref), channel_id=1, source_target_pairs={{8,0},{12,4},{16,8},{20,12},{24,16},{28,20},{9,1},{13,5},{17,9},{2... | collective-permute-start | bytes 786440 | tf_op jit(solution)/shard_map/ppermute | solution.py:305
  39.1 12.2 %collective-permute-start.11 = (bf16[1024,256]{1,0:T(8,128)(2,1)}, bf16[1024,256]{1,0:T(8,128)(2,1)S(1)}, u32[]{:S(2)}, u32[]{:S(2)}) collective-permute-start(bf16[1024,256]{1,0:T(8,128)(2,1)} %constant_dynamic-update-slice_fusion), channel_id=1, source_target_pairs={{0,4},{4,8},{8,12},{12,16},{16,20},{20,24},{24,28},{1,5},{5,9},{9,... | collective-permute-start | bytes 1572872 | tf_op jit(solution)/shard_map/ppermute | solution.py:305
  41.5 7.1 %collective-permute-start.3 = (bf16[64,768]{1,0:T(8,128)(2,1)S(1)}, bf16[64,768]{1,0:T(8,128)(2,1)S(1)}, u32[]{:S(2)}, u32[]{:S(2)}) collective-permute-start(bf16[64,768]{1,0:T(8,128)(2,1)S(1)} %add_convert_fusion.3), channel_id=1, source_target_pairs={{0,16},{4,20},{8,24},{12,28},{16,0},{20,4},{24,8},{28,12},{1,17},{... | collective-permute-start | bytes 294920 | tf_op jit(solution)/shard_map/ppermute | solution.py:316
  45.6 5.7 %collective-permute-start.7 = (bf16[64,768]{1,0:T(8,128)(2,1)S(1)}, bf16[64,768]{1,0:T(8,128)(2,1)S(1)}, u32[]{:S(2)}, u32[]{:S(2)}) collective-permute-start(bf16[64,768]{1,0:T(8,128)(2,1)S(1)} %add_convert_fusion.2), channel_id=1, source_target_pairs={{0,4},{4,0},{8,12},{12,8},{16,20},{20,16},{24,28},{28,24},{1,5},{5... | collective-permute-start | bytes 294920 | tf_op jit(solution)/shard_map/ppermute | solution.py:316
  51.3 16.1 %collective-permute-start.12 = (bf16[128,768]{1,0:T(8,128)(2,1)S(1)}, bf16[128,768]{1,0:T(8,128)(2,1)S(1)}, u32[]{:S(2)}, u32[]{:S(2)}) collective-permute-start(bf16[128,768]{1,0:T(8,128)(2,1)S(1)} %pad_maximum_fusion.2), channel_id=1, source_target_pairs={{0,8},{4,12},{8,0},{12,4},{16,24},{20,28},{24,16},{28,20},{1,9},{5... | collective-permute-start | bytes 589832 | tf_op jit(solution)/shard_map/ppermute | solution.py:316
  59.0 9.7 %collective-permute-start.13 = (bf16[128,768]{1,0:T(8,128)(2,1)S(1)}, bf16[128,768]{1,0:T(8,128)(2,1)S(1)}, u32[]{:S(2)}, u32[]{:S(2)}) collective-permute-start(bf16[128,768]{1,0:T(8,128)(2,1)S(1)} %pad_maximum_fusion.3), channel_id=1, source_target_pairs={{0,16},{4,20},{8,24},{12,28},{16,0},{20,4},{24,8},{28,12},{1,17},{... | collective-permute-start | bytes 589832 | tf_op jit(solution)/shard_map/ppermute | solution.py:316
  67.3 7.2 %copy-start.7 = (bf16[512,128]{1,0:T(8,128)(2,1)}, bf16[512,128]{1,0:T(8,128)(2,1)S(1)}, u32[]{:S(2)}) copy-start(bf16[512,128]{1,0:T(8,128)(2,1)S(1)} %get-tuple-element.35.refs_5_) | copy-start | bytes 393220
  67.3 8.2 %collective-permute-start.16 = (bf16[512,128]{1,0:T(8,128)(2,1)S(1)}, bf16[512,128]{1,0:T(8,128)(2,1)S(1)}, u32[]{:S(2)}, u32[]{:S(2)}) collective-permute-start(bf16[512,128]{1,0:T(8,128)(2,1)S(1)} %get-tuple-element.38), channel_id=1, source_target_pairs={{0,4},{4,0},{8,12},{12,8},{16,20},{20,16},{24,28},{28,24},{1,5},{5... | collective-permute-start | bytes 393224 | tf_op jit(solution)/shard_map/ppermute | solution.py:316
  67.4 12.8 %copy-start.8 = (bf16[256,768]{1,0:T(8,128)(2,1)}, bf16[256,768]{1,0:T(8,128)(2,1)S(1)}, u32[]{:S(2)}) copy-start(bf16[256,768]{1,0:T(8,128)(2,1)S(1)} %pad_maximum_fusion.refs_0_) | copy-start | bytes 1179652
  68.7 11.5 %copy-start.9 = (bf16[256,768]{1,0:T(8,128)(2,1)}, bf16[256,768]{1,0:T(8,128)(2,1)S(1)}, u32[]{:S(2)}) copy-start(bf16[256,768]{1,0:T(8,128)(2,1)S(1)} %pad_maximum_fusion.1.refs_2_) | copy-start | bytes 1179652
  68.7 11.0 %collective-permute-start.14 = (bf16[256,768]{1,0:T(8,128)(2,1)S(1)}, bf16[256,768]{1,0:T(8,128)(2,1)S(1)}, u32[]{:S(2)}, u32[]{:S(2)}) collective-permute-start(bf16[256,768]{1,0:T(8,128)(2,1)S(1)} %pad_maximum_fusion.refs_0_), channel_id=1, source_target_pairs={{0,4},{4,0},{8,12},{12,8},{16,20},{20,16},{24,28},{28,24},{1,5},{5... | collective-permute-start | bytes 1179656 | tf_op jit(solution)/shard_map/ppermute | solution.py:316
  69.6 10.7 %collective-permute-start.15 = (bf16[256,768]{1,0:T(8,128)(2,1)S(1)}, bf16[256,768]{1,0:T(8,128)(2,1)S(1)}, u32[]{:S(2)}, u32[]{:S(2)}) collective-permute-start(bf16[256,768]{1,0:T(8,128)(2,1)S(1)} %pad_maximum_fusion.1.refs_2_), channel_id=1, source_target_pairs={{0,8},{4,12},{8,0},{12,4},{16,24},{20,28},{24,16},{28,20},{1,9},{5... | collective-permute-start | bytes 1179656 | tf_op jit(solution)/shard_map/ppermute | solution.py:316
  75.5 4.7 %copy-start.14 = (bf16[512,128]{1,0:T(8,128)(2,1)}, bf16[512,128]{1,0:T(8,128)(2,1)S(1)}, u32[]{:S(2)}) copy-start(bf16[512,128]{1,0:T(8,128)(2,1)S(1)} %collective-permute-done.16.refs_6_) | copy-start | bytes 393220
  75.5 12.5 %collective-permute-start.17 = (bf16[1024,256]{1,0:T(8,128)(2,1)}, bf16[1024,256]{1,0:T(8,128)(2,1)S(1)}, u32[]{:S(2)}, u32[]{:S(2)}) collective-permute-start(bf16[1024,256]{1,0:T(8,128)(2,1)} %constant_dynamic-update-slice_fusion), channel_id=1, source_target_pairs={{4,0},{8,4},{12,8},{16,12},{20,16},{24,20},{28,24},{5,1},{9,5},{13... | collective-permute-start | bytes 1572872 | tf_op jit(solution)/shard_map/ppermute | solution.py:305
  79.7 0.8 copy-start.12
  80.2 0.7 copy-start.13
  87.9 8.3 %copy-start.4 = (bf16[512,256]{1,0:T(8,128)(2,1)S(1)}, bf16[512,256]{1,0:T(8,128)(2,1)}, u32[]{:S(2)}) copy-start(bf16[512,256]{1,0:T(8,128)(2,1)} %queries_ref.7) | copy-start | bytes 786436
  87.9 8.3 %copy-start.5 = (bf16[512,256]{1,0:T(8,128)(2,1)S(1)}, bf16[512,256]{1,0:T(8,128)(2,1)}, u32[]{:S(2)}) copy-start(bf16[512,256]{1,0:T(8,128)(2,1)} %get-tuple-element.39.keep_ref) | copy-start | bytes 786436
  87.9 1.8 %collective-permute-start.19 = (bf16[512,256]{1,0:T(8,128)(2,1)}, bf16[512,256]{1,0:T(8,128)(2,1)S(1)}, u32[]{:S(2)}, u32[]{:S(2)}) collective-permute-start(bf16[512,256]{1,0:T(8,128)(2,1)} %get-tuple-element.44), channel_id=1, source_target_pairs={{0,1},{1,0},{2,3},{3,2},{4,5},{5,4},{6,7},{7,6},{8,9},{9,8},{10,11... | collective-permute-start | bytes 786440 | tf_op jit(solution)/shard_map/ppermute | solution.py:311
  88.0 3.9 %collective-permute-start.18 = (bf16[512,256]{1,0:T(8,128)(2,1)}, bf16[512,256]{1,0:T(8,128)(2,1)S(1)}, u32[]{:S(2)}, u32[]{:S(2)}) collective-permute-start(bf16[512,256]{1,0:T(8,128)(2,1)} %get-tuple-element.42), channel_id=1, source_target_pairs={{0,1},{1,0},{2,3},{3,2},{4,5},{5,4},{6,7},{7,6},{8,9},{9,8},{10,11... | collective-permute-start | bytes 786440 | tf_op jit(solution)/shard_map/ppermute | solution.py:311
  89.8 6.4 %collective-permute-start.21 = (bf16[256,256]{1,0:T(8,128)(2,1)S(1)}, bf16[256,256]{1,0:T(8,128)(2,1)S(1)}, u32[]{:S(2)}, u32[]{:S(2)}) collective-permute-start(bf16[256,256]{1,0:T(8,128)(2,1)S(1)} %get-tuple-element.46), channel_id=1, source_target_pairs={{0,2},{1,3},{2,0},{3,1},{4,6},{5,7},{6,4},{7,5},{8,10},{9,11},{10,... | collective-permute-start | bytes 393224 | tf_op jit(solution)/shard_map/ppermute | solution.py:311
  91.2 7.0 %collective-permute-start.20 = (bf16[256,256]{1,0:T(8,128)(2,1)S(1)}, bf16[256,256]{1,0:T(8,128)(2,1)S(1)}, u32[]{:S(2)}, u32[]{:S(2)}) collective-permute-start(bf16[256,256]{1,0:T(8,128)(2,1)S(1)} %get-tuple-element.47), channel_id=1, source_target_pairs={{0,2},{1,3},{2,0},{3,1},{4,6},{5,7},{6,4},{7,5},{8,10},{9,11},{10,... | collective-permute-start | bytes 393224 | tf_op jit(solution)/shard_map/ppermute | solution.py:311
